TPU v7x, 32 devices: a whole 2x2x4 slice. The times are simulated.
32 devices in a mesh: section: 2 (over core), seq: 4 (over z), fsdp: 4 (over y, x).
Axes of the slice: x: 2, y: 2, z: 4, core: 2. Of those that a mesh axis runs over, the one named last changes fastest.
Arguments:
- inputs: bfloat16 [2, 4, 512, 2048], P(None, 'fsdp', 'seq'), may hold values from -6 to 6
- cotangent: bfloat16 [2, 4, 512, 2048], P(None, 'fsdp', 'seq'), may hold values from -6 to 6
- lengths: int32 [2, 4], P(None, 'fsdp'), may hold values from 257 to 512, as said below
- gain_in: bfloat16 [2, 2048], P('section', 'fsdp'), may hold values from 0.25 to 1.75
- w_in: bfloat16 [2, 2048, 8512], P('section', 'fsdp'), may hold values from -0.125 to 0.125
- conv_w: bfloat16 [2, 4, 4352], P('section', None, 'fsdp'), may hold values from -3 to 3
- conv_b: bfloat16 [2, 4352], P('section', 'fsdp'), may hold values from -3 to 3
- dt_bias: bfloat16 [2, 64], P('section', 'fsdp'), may hold values from -6 to -2
- a_log: bfloat16 [2, 64], P('section', 'fsdp'), may hold values from -6 to -1
- d_skip: bfloat16 [2, 64], P('section', 'fsdp'), may hold values from -3 to 3
- gain_out: bfloat16 [2, 4096], P('section', 'fsdp'), may hold values from 0.25 to 1.75
- w_out: bfloat16 [2, 4096, 2048], P('section', 'fsdp'), may hold values from -0.09375 to 0.09375
Outputs:
- layer_outputs: bfloat16 [2, 2, 4, 512, 2048], P('section', None, 'fsdp', 'seq')
- input_grads: float32 [2, 2, 4, 512, 2048], P('section', None, 'fsdp', 'seq')
- grad_gain_in: float32 [2, 2048], P('section', 'fsdp')
- grad_w_in: float32 [2, 2048, 8512], P('section', 'fsdp')
- grad_conv_w: float32 [2, 4, 4352], P('section', None, 'fsdp')
- grad_conv_b: float32 [2, 4352], P('section', 'fsdp')
- grad_dt_bias: float32 [2, 64], P('section', 'fsdp')
- grad_a_log: float32 [2, 64], P('section', 'fsdp')
- grad_d_skip: float32 [2, 64], P('section', 'fsdp')
- grad_gain_out: float32 [2, 4096], P('section', 'fsdp')
- grad_w_out: float32 [2, 4096, 2048], P('section', 'fsdp')
- act_rms: float32 [2, 2], P('section')
Inputs may be any that keep to these rules, and one draw needn't show every extreme that they name: `lengths`: each slot holds one sequence from position 0 and padding after it; in every slot column some micro-batch is full, 512 long.
All inputs are finite; a program needn't handle non-finite values.
Results may differ from a plain program's by a relative error of at most 0.008.
The roundings to bfloat16 on the way count: a program that leaves them out, or rounds other values in their place, can miss the bound.
Values may be sent and summed in bfloat16 or wider, within the bound.
No kernel may reach another device: no remote copies, remote signals or barrier semaphores. Data moves between devices by JAX's collectives and lax.ppermute only.
A program may use at most 512 MiB of HBM per device.

v0:
```python
import jax
import jax.numpy as jnp
from jax import lax
from jax.sharding import PartitionSpec as P

D = 2048
INNER = 4096
HEADS = 64
HEAD_DIM = 64
STATE = 128
KERNEL = 4
CHANNELS = 4352


norm_eps = 1e-05
highest = lax.Precision.HIGHEST


def carried_in(part, axis, combine, identity, reverse):
    count = lax.axis_size(axis)
    place = lax.axis_index(axis)
    ahead = count - 1 - place if reverse else place
    gathered = jax.tree.map(lambda a: lax.all_gather(a, axis), part)
    state = jax.tree.map(lambda a, e: jnp.zeros_like(a) + jnp.asarray(e, a.dtype), part, identity)

    def one(turn, state):
        source = count - 1 - turn if reverse else turn
        return combine(
            state, jax.tree.map(lambda a: lax.dynamic_index_in_dim(a, source, 0, False), gathered)
        )

    return lax.fori_loop(0, ahead, one, state)


def passed_along(value, axis, steps):
    count = lax.axis_size(axis)
    first, last = (max(0, -steps), min(count, count - steps))
    return lax.ppermute(value, axis, [(source, source + steps) for source in range(first, last)])


def rms_part(hidden, gain_vec):
    return (
        hidden * lax.rsqrt(jnp.mean(hidden * hidden, axis=-1, keepdims=True) + norm_eps) * gain_vec
    )


def conv_part(projected, edge_rows, conv_taps, conv_shift, dt_shift, decay_param):
    tokens_here = projected.shape[0]
    gate_z = projected[:, :INNER]
    conv_input = projected[:, INNER : INNER + CHANNELS]
    dt_input = projected[:, INNER + CHANNELS :]
    padded = jnp.concatenate([edge_rows, conv_input], axis=0)
    filtered = conv_shift[None, :] + sum(
        (
            conv_taps[tap_index][None, :] * padded[tap_index : tap_index + tokens_here]
            for tap_index in range(KERNEL)
        )
    )
    activated = jax.nn.silu(filtered)
    x_values = activated[:, :INNER]
    b_coeffs = activated[:, INNER : INNER + STATE]
    c_coeffs = activated[:, INNER + STATE :]
    dt_values = jax.nn.softplus(dt_input + dt_shift[None, :])
    decay_cum = jnp.cumsum(dt_values * (-jnp.exp(decay_param))[None, :], axis=0)
    return (gate_z, x_values, b_coeffs, c_coeffs, dt_values, decay_cum)


def mix_part(
    gate_z, x_values, b_coeffs, c_coeffs, dt_values, decay_cum, state_in, skip_gain, out_gain
):
    tokens_here = x_values.shape[0]
    match_scores = jnp.dot(c_coeffs, b_coeffs.T, precision=highest)
    causal_mask = (jnp.arange(tokens_here)[:, None] >= jnp.arange(tokens_here)[None, :])[None]
    cum_heads = decay_cum.T
    log_gaps = cum_heads[:, :, None] - cum_heads[:, None, :]
    decay_matrix = (
        jnp.where(causal_mask, jnp.exp(jnp.where(causal_mask, log_gaps, 0.0)), 0.0)
        * match_scores[None]
    )
    head_values = x_values.reshape(tokens_here, HEADS, HEAD_DIM)
    scaled_values = head_values * dt_values[:, :, None]
    within = jnp.einsum("hts,shp->thp", decay_matrix, scaled_values, precision=highest)
    carried = (
        jnp.einsum("tn,hpn->thp", c_coeffs, state_in, precision=highest)
        * jnp.exp(decay_cum)[:, :, None]
    )
    ssm_out = within + carried + skip_gain[None, :, None] * head_values
    gated_out = ssm_out.reshape(tokens_here, INNER) * jax.nn.silu(gate_z)
    return rms_part(gated_out, out_gain)


def state_part(x_values, b_coeffs, dt_values, decay_cum):
    final_log = decay_cum[-1]
    weighting = jnp.exp(final_log[None, :] - decay_cum) * dt_values
    head_values = x_values.reshape(-1, HEADS, HEAD_DIM) * weighting[:, :, None]
    return (jnp.exp(final_log), jnp.einsum("thp,tn->hpn", head_values, b_coeffs, precision=highest))


def pair_forward(earlier, later):
    return (earlier[0] * later[0], later[0][:, None, None] * earlier[1] + later[1])


def pair_reverse(earlier, later):
    return (earlier[0] * later[0], later[1] + later[0][:, None, None] * earlier[1])


def chain_forward(decay_total, state_local):
    identity = (jnp.ones_like(decay_total), jnp.zeros_like(state_local))
    state_in = carried_in((decay_total, state_local), "seq", pair_forward, identity, False)[1]
    log_table = jnp.zeros((1, decay_total.shape[0]), jnp.float32)
    return (state_in, log_table)


def chain_backward(decay_total, grad_state_in):
    identity = (jnp.ones_like(decay_total), jnp.zeros_like(grad_state_in))
    return carried_in((decay_total, grad_state_in), "seq", pair_reverse, identity, True)[1]


def small_params(weights):
    return tuple(
        (weight.astype(jnp.float32) for weight in (weights[2], weights[3], weights[4], weights[5]))
    )


def block_forward(hidden, valid, weights):
    tokens_here = hidden.shape[0]
    normed_in = rms_part(hidden, weights[0].astype(jnp.float32)).astype(jnp.bfloat16)
    projected = jnp.dot(normed_in, weights[1], preferred_element_type=jnp.float32)
    edge_rows = passed_along(
        projected[tokens_here - (KERNEL - 1) :, INNER : INNER + CHANNELS], "seq", 1
    )
    features = conv_part(projected, edge_rows, *small_params(weights))
    decay_total, state_local = state_part(features[1], features[2], features[4], features[5])
    state_in, log_table = chain_forward(decay_total, state_local)
    normed = mix_part(
        *features, state_in, weights[6].astype(jnp.float32), weights[7].astype(jnp.float32)
    )
    mixed = jnp.dot(normed.astype(jnp.bfloat16), weights[8], preferred_element_type=jnp.float32)
    result = valid * (hidden + mixed)
    return (result, mixed, (hidden, projected, edge_rows, state_in, decay_total, log_table))


def block_backward(grad_out, valid, saved, weights):
    hidden, projected, edge_rows, state_in, decay_total, log_table = saved
    tokens_here = hidden.shape[0]
    contract_rows = (((0,), (0,)), ((), ()))
    contract_cols = (((1,), (1,)), ((), ()))
    features, pull_conv = jax.vjp(conv_part, projected, edge_rows, *small_params(weights))
    normed, pull_mix = jax.vjp(
        mix_part,
        *features,
        state_in,
        weights[6].astype(jnp.float32),
        weights[7].astype(jnp.float32)
    )
    residual_grad = valid * grad_out
    mixed_low = residual_grad.astype(jnp.bfloat16)
    grad_w_out = lax.dot_general(
        normed.astype(jnp.bfloat16), mixed_low, contract_rows, preferred_element_type=jnp.float32
    )
    grad_normed = lax.dot_general(
        mixed_low, weights[8], contract_cols, preferred_element_type=jnp.float32
    )
    back_mix = pull_mix(grad_normed)
    carried_grad = chain_backward(decay_total, back_mix[6])
    grad_total = jnp.sum(carried_grad * state_in, axis=(1, 2))
    _, pull_state = jax.vjp(state_part, features[1], features[2], features[4], features[5])
    back_state = pull_state((grad_total, carried_grad))
    grad_features = (
        back_mix[0],
        back_mix[1] + back_state[0],
        back_mix[2] + back_state[1],
        back_mix[3],
        back_mix[4] + back_state[2],
        back_mix[5] + back_state[3],
    )
    back_conv = pull_conv(grad_features)
    edge_grad = passed_along(back_conv[1], "seq", -1)
    grad_proj = (
        back_conv[0].at[tokens_here - (KERNEL - 1) :, INNER : INNER + CHANNELS].add(edge_grad)
    )
    proj_low = grad_proj.astype(jnp.bfloat16)
    normed_in, pull_norm = jax.vjp(rms_part, hidden, weights[0].astype(jnp.float32))
    grad_w_in = lax.dot_general(
        normed_in.astype(jnp.bfloat16), proj_low, contract_rows, preferred_element_type=jnp.float32
    )
    grad_input = lax.dot_general(
        proj_low, weights[1], contract_cols, preferred_element_type=jnp.float32
    )
    grad_hidden, grad_gain_in = pull_norm(grad_input)
    pieces = (
        grad_gain_in,
        grad_w_in,
        back_conv[2],
        back_conv[3],
        back_conv[4],
        back_conv[5],
        back_mix[7],
        back_mix[8],
        grad_w_out,
    )
    return (residual_grad + grad_hidden, pieces)


def per_device(
    inputs,
    cotangent,
    lengths,
    gain_in,
    w_in,
    conv_w,
    conv_b,
    dt_bias,
    a_log,
    d_skip,
    gain_out,
    w_out,
):
    sections = lax.axis_size("section")
    section_id = lax.axis_index("section")
    micro = inputs.shape[0]
    tokens_here = inputs.shape[2]
    ticks = micro + sections - 1
    positions = lax.axis_index("seq") * tokens_here + jnp.arange(tokens_here, dtype=jnp.int32)
    weights = (
        lax.all_gather(gain_in[0], "fsdp", axis=0, tiled=True),
        lax.all_gather(w_in[0], "fsdp", axis=0, tiled=True),
        lax.all_gather(conv_w[0], "fsdp", axis=1, tiled=True),
        lax.all_gather(conv_b[0], "fsdp", axis=0, tiled=True),
        lax.all_gather(dt_bias[0], "fsdp", axis=0, tiled=True),
        lax.all_gather(a_log[0], "fsdp", axis=0, tiled=True),
        lax.all_gather(d_skip[0], "fsdp", axis=0, tiled=True),
        lax.all_gather(gain_out[0], "fsdp", axis=0, tiled=True),
        lax.all_gather(w_out[0], "fsdp", axis=0, tiled=True),
    )
    received = jnp.zeros((tokens_here, D), jnp.bfloat16)
    kept_list = []
    sent_list = []
    square_res = jnp.zeros((), jnp.float32)
    square_mix = jnp.zeros((), jnp.float32)
    valid_count = jnp.zeros((), jnp.float32)
    for tick_id in range(ticks):
        batch_id = tick_id - section_id
        active = (batch_id >= 0) & (batch_id < micro)
        clipped = jnp.clip(batch_id, 0, micro - 1)
        fresh_rows = lax.dynamic_index_in_dim(inputs, clipped, 0, keepdims=False)[0]
        hidden = jnp.where(section_id == 0, fresh_rows, received).astype(jnp.float32)
        length_now = lax.dynamic_index_in_dim(lengths, clipped, 0, keepdims=False)[0]
        valid = (positions < length_now).astype(jnp.float32)[:, None]
        result, mixed, saved = block_forward(hidden, valid, weights)
        sent_rows = result.astype(jnp.bfloat16)
        received = passed_along(sent_rows, "section", 1)
        active_f = active.astype(jnp.float32)
        square_res = square_res + active_f * jnp.sum(result * result)
        square_mix = square_mix + active_f * jnp.sum((valid * mixed) ** 2)
        valid_count = valid_count + active_f * jnp.sum(valid)
        kept_list.append((saved, valid))
        sent_list.append(sent_rows)
    square_res, square_mix, valid_count = lax.psum(
        (square_res, square_mix, valid_count), ("seq", "fsdp")
    )
    counted = valid_count * D
    act_rms = jnp.stack([jnp.sqrt(square_res / counted), jnp.sqrt(square_mix / counted)])[None]
    layer_out = lax.dynamic_slice_in_dim(jnp.stack(sent_list), section_id, micro, 0)
    weights = (
        lax.all_gather(gain_in[0], "fsdp", axis=0, tiled=True),
        lax.all_gather(w_in[0], "fsdp", axis=0, tiled=True),
        lax.all_gather(conv_w[0], "fsdp", axis=1, tiled=True),
        lax.all_gather(conv_b[0], "fsdp", axis=0, tiled=True),
        lax.all_gather(dt_bias[0], "fsdp", axis=0, tiled=True),
        lax.all_gather(a_log[0], "fsdp", axis=0, tiled=True),
        lax.all_gather(d_skip[0], "fsdp", axis=0, tiled=True),
        lax.all_gather(gain_out[0], "fsdp", axis=0, tiled=True),
        lax.all_gather(w_out[0], "fsdp", axis=0, tiled=True),
    )
    totals = tuple((jnp.zeros(weight.shape, jnp.float32) for weight in weights))
    returned = jnp.zeros((tokens_here, D), jnp.bfloat16)
    grad_list = []
    for tick_id in range(ticks):
        batch_id = micro - 1 - tick_id + (sections - 1 - section_id)
        active = (batch_id >= 0) & (batch_id < micro)
        clipped = jnp.clip(batch_id, 0, micro - 1)
        seed_rows = lax.dynamic_index_in_dim(cotangent, clipped, 0, keepdims=False)[0]
        grad_out = jnp.where(section_id == sections - 1, seed_rows, returned).astype(jnp.float32)
        saved, valid = kept_list[ticks - 1 - tick_id]
        grad_in, pieces = block_backward(grad_out, valid, saved, weights)
        returned = passed_along(grad_in.astype(jnp.bfloat16), "section", -1)
        totals = tuple(
            (
                running + jnp.where(active, piece_grad, 0.0)
                for running, piece_grad in zip(totals, pieces)
            )
        )
        grad_list.append(grad_in)
    in_grads = jnp.flip(
        lax.dynamic_slice_in_dim(jnp.stack(grad_list), sections - 1 - section_id, micro, 0), 0
    )
    (
        sum_gain_in,
        sum_w_in,
        sum_conv_w,
        sum_conv_b,
        sum_dt_bias,
        sum_a_log,
        sum_d_skip,
        sum_gain_out,
        sum_w_out,
    ) = totals
    owned = (
        lax.psum_scatter(sum_gain_in, "fsdp", scatter_dimension=0, tiled=True),
        lax.psum_scatter(sum_w_in, "fsdp", scatter_dimension=0, tiled=True),
        lax.psum_scatter(sum_conv_w, "fsdp", scatter_dimension=1, tiled=True),
        lax.psum_scatter(sum_conv_b, "fsdp", scatter_dimension=0, tiled=True),
        lax.psum_scatter(sum_dt_bias, "fsdp", scatter_dimension=0, tiled=True),
        lax.psum_scatter(sum_a_log, "fsdp", scatter_dimension=0, tiled=True),
        lax.psum_scatter(sum_d_skip, "fsdp", scatter_dimension=0, tiled=True),
        lax.psum_scatter(sum_gain_out, "fsdp", scatter_dimension=0, tiled=True),
        lax.psum_scatter(sum_w_out, "fsdp", scatter_dimension=0, tiled=True),
    )
    (
        own_gain_in,
        own_w_in,
        own_conv_w,
        own_conv_b,
        own_dt_bias,
        own_a_log,
        own_d_skip,
        own_gain_out,
        own_w_out,
    ) = owned
    summed = lax.psum(
        (
            own_gain_in,
            own_w_in,
            own_conv_w,
            own_conv_b,
            own_dt_bias,
            own_a_log,
            own_d_skip,
            own_gain_out,
            own_w_out,
        ),
        "seq",
    )
    return (
        layer_out[None, :, None],
        in_grads[None, :, None],
        summed[0][None],
        summed[1][None],
        summed[2][None],
        summed[3][None],
        summed[4][None],
        summed[5][None],
        summed[6][None],
        summed[7][None],
        summed[8][None],
        act_rms,
    )


def solution(mesh):
    in_specs = (
        P(None, "fsdp", "seq", None),
        P(None, "fsdp", "seq", None),
        P(None, "fsdp"),
        P("section", "fsdp"),
        P("section", "fsdp", None),
        P("section", None, "fsdp"),
        P("section", "fsdp"),
        P("section", "fsdp"),
        P("section", "fsdp"),
        P("section", "fsdp"),
        P("section", "fsdp"),
        P("section", "fsdp", None),
    )
    out_specs = (
        P("section", None, "fsdp", "seq", None),
        P("section", None, "fsdp", "seq", None),
        P("section", "fsdp"),
        P("section", "fsdp", None),
        P("section", None, "fsdp"),
        P("section", "fsdp"),
        P("section", "fsdp"),
        P("section", "fsdp"),
        P("section", "fsdp"),
        P("section", "fsdp"),
        P("section", "fsdp", None),
        P("section", None),
    )
    return jax.shard_map(
        per_device, mesh=mesh, in_specs=in_specs, out_specs=out_specs, check_vma=False
    )
```

profile of v0, /device:TPU:1, one launch (start us, length us, event | category | flops | bytes accessed | tf_op | source)
XLA Modules:
  0.0 3635.6 jit_solution(7088463664939890719)
XLA Ops:
  8.0 6.9 all-gather.2
  15.9 20.9 all-gather.1
  42.3 14.4 all-reduce.59
  57.5 90.0 %slice_reduce_fusion.3 = (f32[4352]{0:T(1024)S(1)}, f32[4352]{0:T(1024)S(1)}, f32[4352]{0:T(1024)S(1)}, f32[4352]{0:T(1024)S(1)}) fusion(f32[1,4,4352]{1,0,2:T(1,128)S(1)} %convert_element_type.211), kind=kLoop, calls=%fused_computation.113 | loop fusion | bytes 139264 | tf_op jit(solution)/shard_map/slice | solution.py:55
  147.6 179.0 %all-gather.27.cloned.1.call-done = bf16[1,2048,8512]{1,2,0:T(8,128)(2,1)} async-done(((bf16[1,512,8512]{1,2,0:T(8,128)(2,1)}), bf16[1,2048,8512]{1,2,0:T(8,128)(2,1)}) %all-gather.27.cloned.1.call-update) | async-done | bytes 34865168 | tf_op jit(solution)/shard_map/all_gather | solution.py:227
  326.6 15.1 fusion.10
  358.4 5.8 fusion.62
  374.2 6.1 all-gather.8
  385.9 7.2 all-gather.15
  394.2 128.5 %all-gather.29.cloned.1.call-done = f32[256,64,128]{2,1,0:T(8,128)} async-done(((f32[64,64,128]{2,1,0:T(8,128)}), f32[256,64,128]{2,1,0:T(8,128)}) %all-gather.29.cloned.1.call-update) | async-done | bytes 8388624 | tf_op jit(solution)/shard_map/all_gather | solution.py:23
  526.3 9.8 fusion.82
  542.5 137.5 %all-gather.31.cloned.1.call-done = bf16[1,4096,2048]{2,1,0:T(8,128)(2,1)} async-done(((bf16[1,1024,2048]{2,1,0:T(8,128)(2,1)}), bf16[1,4096,2048]{2,1,0:T(8,128)(2,1)}) %all-gather.31.cloned.1.call-update) | async-done | bytes 16777232 | tf_op jit(solution)/shard_map/all_gather | solution.py:234
  680.0 9.4 fusion.239
  693.5 15.1 fusion.8
  722.6 6.3 fusion.61
  742.9 7.0 all-gather.16
  751.0 135.9 %all-gather.33.cloned.1.call-done = f32[256,64,128]{2,1,0:T(8,128)} async-done(((f32[64,64,128]{2,1,0:T(8,128)}), f32[256,64,128]{2,1,0:T(8,128)}) %all-gather.33.cloned.1.call-update) | async-done | bytes 8388624 | tf_op jit(solution)/shard_map/all_gather | solution.py:23
  890.5 9.8 fusion.81
  905.8 10.0 fusion.241
  920.0 15.1 fusion.6
  947.5 5.8 fusion.60
  965.8 11.0 all-gather.17
  977.9 138.2 %all-gather.35.cloned.1.call-done = f32[256,64,128]{2,1,0:T(8,128)} async-done(((f32[64,64,128]{2,1,0:T(8,128)}), f32[256,64,128]{2,1,0:T(8,128)}) %all-gather.35.cloned.1.call-update) | async-done | bytes 8388624 | tf_op jit(solution)/shard_map/all_gather | solution.py:23
  1119.7 9.7 fusion.80
  1136.7 14.3 multiply_reduce_fusion.17
  1151.0 6.6 multiply_reduce_fusion.20
  1165.3 11.0 fusion.43
  1179.8 5.6 fusion.176
  1186.4 5.9 fusion.26
  1192.4 128.8 %all-gather.37.cloned.1.call-done = f32[256,64,128]{2,1,0:T(8,128)} async-done(((f32[64,64,128]{2,1,0:T(8,128)}), f32[256,64,128]{2,1,0:T(8,128)}) %all-gather.37.cloned.1.call-update) | async-done | bytes 8388624 | tf_op jit(solution)/shard_map/all_gather | solution.py:23
  1322.7 13.8 while.84
  1336.6 5.9 fusion.173
  1344.7 5.4 fusion.77
  1374.1 14.8 fusion.4
  1389.0 10.5 multiply_reduce_fusion.39
  1406.3 13.8 multiply_reduce_fusion.16
  1420.1 6.1 multiply_reduce_fusion.19
  1432.6 10.9 fusion.45
  1453.5 5.9 fusion.32
  1459.4 123.0 %all-gather.39.cloned.1.call-done = f32[256,64,128]{2,1,0:T(8,128)} async-done(((f32[64,64,128]{2,1,0:T(8,128)}), f32[256,64,128]{2,1,0:T(8,128)}) %all-gather.39.cloned.1.call-update) | async-done | bytes 8388624 | tf_op jit(solution)/shard_map/all_gather | solution.py:23
  1584.1 13.8 while.85
  1597.9 5.9 fusion.170
  1635.4 19.2 multiply_reduce_fusion.40
  1661.4 13.7 multiply_reduce_fusion.15
  1675.1 6.1 multiply_reduce_fusion.18
  1689.6 16.4 fusion.257
  1706.0 13.4 fusion.246
  1719.4 34.6 select_add_fusion.1
  1755.1 26.6 fusion.190
  1781.7 26.6 fusion.187
  1808.3 10.8 fusion.47
  1828.6 5.9 fusion.38
  1840.5 14.5 while.86
  1855.1 7.4 fusion.71
  1865.4 6.1 fusion.167
  1896.1 74.0 %select_add_fusion = f32[2048,8512]{0,1:T(8,128)} fusion(f32[2048,8512]{0,1:T(8,128)} %fusion.187, f32[2048,8512]{0,1:T(8,128)} %fusion.190, pred[]{:T(512)S(6)} %and.25, pred[]{:T(512)S(6)} %and.24, pred[]{:T(512)S(6)} %and.23, f32[128,8512]{1,0:T(8,128)} %scatter-add.14, f32[2048]{0:T(1024)S(1)} %bitcast.405, f32[128]{0:T(128)S(1)} %copy-done.100, ...), kind=kOutput, calls=%fused_computation.12 | convolution fusion | flops 4552302592 | bytes 214082048 | tf_op jit(solution)/shard_map/dot_general | solution.py:184
  1973.5 155.2 %reduce-scatter.8.cloned.1.call-done = f32[1024,2048]{1,0:T(8,128)} async-done(((f32[4096,2048]{1,0:T(8,128)}), f32[1024,2048]{1,0:T(8,128)}) %reduce-scatter.8.cloned.1.call-update) | async-done | bytes 8388624 | tf_op jit(solution)/shard_map/reduce_scatter | solution.py:318
  2128.7 582.7 %reduce-scatter.6.cloned.1.call-done = f32[512,8512]{0,1:T(8,128)} async-done(((f32[2048,8512]{0,1:T(8,128)}), f32[512,8512]{0,1:T(8,128)}) %reduce-scatter.6.cloned.1.call-update) | async-done | bytes 17432592 | tf_op jit(solution)/shard_map/reduce_scatter | solution.py:311
  2721.9 19.9 multiply_reduce_fusion.41
  2743.3 35.3 all-reduce.55
  2778.6 12.5 all-reduce.56
  2799.1 19.8 all-reduce.57
  2818.9 791.8 %all-reduce.62.cloned.1.call-done = (f32[1,512,8512]{1,2,0:T(8,128)}, f32[1,1024,2048]{2,1,0:T(8,128)}) async-done(((f32[1,512,8512]{1,2,0:T(8,128)}, f32[1,1024,2048]{2,1,0:T(8,128)}), (f32[1,512,8512]{1,2,0:T(8,128)}, f32[1,1024,2048]{2,1,0:T(8,128)})) %all-reduce.62.cloned.1.call-update) | async-done | bytes 25821200 | tf_op jit(solution)/shard_map/psum | solution.py:331
  3610.7 13.0 copy.760
  (726 shorter events, 345.3 us)
Async XLA Ops:
  7.2 319.4 %all-gather.27.cloned.1.call-start = ((), (), s32[]{:S(2)}) async-start(), calls=%async_computation.5 | async-start | bytes 43581440 | tf_op jit(solution)/shard_map/all_gather | solution.py:227
  7.9 514.8 %all-gather.29.cloned.1.call-start = ((), (), s32[]{:S(2)}) async-start(), calls=%async_computation.6 | async-start | bytes 10485760 | tf_op jit(solution)/shard_map/all_gather | solution.py:23
  56.7 90.9 %copy-start.201 = (bf16[64]{0:T(256)(128)(2,1)}, bf16[64]{0:T(256)(128)(2,1)S(1)}, u32[]{:S(2)}) copy-start(bf16[64]{0:T(256)(128)(2,1)S(1)} %get-tuple-element.687) | copy-start | bytes 388
  57.4 90.1 %copy-start.195 = (f32[128]{0:T(128)}, f32[128]{0:T(128)S(1)}, u32[]{:S(2)}) copy-start(f32[128]{0:T(128)S(1)} %fusion.212) | copy-start | bytes 1540
  57.4 269.2 %copy-start.99 = (f32[128]{0:T(128)}, f32[128]{0:T(128)S(1)}, u32[]{:S(2)}) copy-start(f32[128]{0:T(128)S(1)} %fusion.332) | copy-start | bytes 1540
  57.5 659.4 %copy-start.149 = (f32[64]{0:T(128)}, f32[64]{0:T(128)S(1)}, u32[]{:S(2)}) copy-start(f32[64]{0:T(128)S(1)} %fusion.328) | copy-start | bytes 772
  147.5 1472.8 %copy-start.85 = (f32[4352]{0:T(1024)}, f32[4352]{0:T(1024)S(1)}, u32[]{:S(2)}) copy-start(f32[4352]{0:T(1024)S(1)} %get-tuple-element.576) | copy-start | bytes 52228
  147.6 1472.8 %copy-start.87 = (f32[4352]{0:T(1024)}, f32[4352]{0:T(1024)S(1)}, u32[]{:S(2)}) copy-start(f32[4352]{0:T(1024)S(1)} %get-tuple-element.577) | copy-start | bytes 52228
  147.6 1472.8 %copy-start.89 = (f32[4352]{0:T(1024)}, f32[4352]{0:T(1024)S(1)}, u32[]{:S(2)}) copy-start(f32[4352]{0:T(1024)S(1)} %get-tuple-element.578) | copy-start | bytes 52228
  147.6 1472.8 %copy-start.91 = (f32[4352]{0:T(1024)}, f32[4352]{0:T(1024)S(1)}, u32[]{:S(2)}) copy-start(f32[4352]{0:T(1024)S(1)} %get-tuple-element.579) | copy-start | bytes 52228
  347.4 11.0 collective-permute-start
  352.0 30.2 copy-start.73
  373.4 306.6 %all-gather.31.cloned.1.call-start = ((), (), s32[]{:S(2)}) async-start(), calls=%async_computation.7 | async-start | bytes 20971520 | tf_op jit(solution)/shard_map/all_gather | solution.py:234
  374.1 512.9 %all-gather.33.cloned.1.call-start = ((), (), s32[]{:S(2)}) async-start(), calls=%async_computation.8 | async-start | bytes 10485760 | tf_op jit(solution)/shard_map/all_gather | solution.py:23
  374.2 516.3 %copy-start.175 = (f32[64]{0:T(128)}, f32[64]{0:T(128)S(1)}, u32[]{:S(2)}) copy-start(f32[64]{0:T(128)S(1)} %convert_element_type.220) | copy-start | bytes 772
  382.2 297.8 %copy-start.156 = (f32[128]{0:T(128)}, f32[128]{0:T(128)S(1)}, u32[]{:S(2)}) copy-start(f32[128]{0:T(128)S(1)} %get-tuple-element.695) | copy-start | bytes 1540
  382.2 144.0 %copy-start.161 = (pred[128,128]{1,0:T(8,128)(4,1)}, pred[128,128]{1,0:T(8,128)(4,1)S(1)}, u32[]{:S(2)}) copy-start(pred[128,128]{1,0:T(8,128)(4,1)S(1)} %iota_compare_fusion) | copy-start | bytes 49156
  382.3 143.9 %copy-start.143 = (f32[64,128]{1,0:T(8,128)}, f32[64,128]{1,0:T(8,128)S(1)}, u32[]{:S(2)}) copy-start(f32[64,128]{1,0:T(8,128)S(1)} %copy.612) | copy-start | bytes 98308
  382.4 143.8 %copy-start.101 = (f32[128,64]{0,1:T(8,128)}, f32[128,64]{0,1:T(8,128)S(1)}, u32[]{:S(2)}) copy-start(f32[128,64]{0,1:T(8,128)S(1)} %copy.615) | copy-start | bytes 98308
  384.0 142.2 %copy-start.113 = (f32[128,64]{0,1:T(8,128)}, f32[128,64]{0,1:T(8,128)S(1)}, u32[]{:S(2)}) copy-start(f32[128,64]{0,1:T(8,128)S(1)} %copy.611) | copy-start | bytes 98308
  394.2 132.0 %copy-start.132 = (f32[128,128]{1,0:T(8,128)}, f32[128,128]{1,0:T(8,128)S(1)}, u32[]{:S(2)}) copy-start(f32[128,128]{1,0:T(8,128)S(1)} %fusion.311) | copy-start | bytes 196612
  542.5 146.9 %copy-start.12 = (f32[128,4096]{1,0:T(8,128)}, f32[128,4096]{1,0:T(8,128)S(1)}, u32[]{:S(2)}) copy-start(f32[128,4096]{1,0:T(8,128)S(1)} %get-tuple-element.728) | copy-start | bytes 6291460
  542.5 146.8 %copy-start.197 = (f32[128]{0:T(128)}, f32[128]{0:T(128)S(1)}, u32[]{:S(2)}) copy-start(f32[128]{0:T(128)S(1)} %get-tuple-element.727) | copy-start | bytes 1540
  542.5 146.8 %copy-start.159 = (f32[128]{0:T(128)}, f32[128]{0:T(128)S(1)}, u32[]{:S(2)}) copy-start(f32[128]{0:T(128)S(1)} %fusion.333) | copy-start | bytes 1540
  689.3 3.8 collective-permute-start.1
  693.4 212.4 %copy-start.46 = (bf16[128,2048]{1,0:T(8,128)(2,1)}, bf16[128,2048]{1,0:T(8,128)(2,1)S(1)}, u32[]{:S(2)}) copy-start(bf16[128,2048]{1,0:T(8,128)(2,1)S(1)} %get-tuple-element.726) | copy-start | bytes 1572868
  713.6 9.0 collective-permute-start.2
  717.7 21.7 copy-start.75
  738.1 377.9 %all-gather.35.cloned.1.call-start = ((), (), s32[]{:S(2)}) async-start(), calls=%async_computation.9 | async-start | bytes 10485760 | tf_op jit(solution)/shard_map/all_gather | solution.py:23
  739.4 166.4 %copy-start.153 = (f32[128]{0:T(128)}, f32[128]{0:T(128)S(1)}, u32[]{:S(2)}) copy-start(f32[128]{0:T(128)S(1)} %get-tuple-element.693) | copy-start | bytes 1540
  739.5 151.0 %copy-start.145 = (f32[64,128]{1,0:T(8,128)}, f32[64,128]{1,0:T(8,128)S(1)}, u32[]{:S(2)}) copy-start(f32[64,128]{1,0:T(8,128)S(1)} %copy.623) | copy-start | bytes 98308
  741.0 149.4 %copy-start.115 = (f32[128,64]{0,1:T(8,128)}, f32[128,64]{0,1:T(8,128)S(1)}, u32[]{:S(2)}) copy-start(f32[128,64]{0,1:T(8,128)S(1)} %copy.622) | copy-start | bytes 98308
  751.0 139.5 %copy-start.134 = (f32[128,128]{1,0:T(8,128)}, f32[128,128]{1,0:T(8,128)S(1)}, u32[]{:S(2)}) copy-start(f32[128,128]{1,0:T(8,128)S(1)} %fusion.302) | copy-start | bytes 196612
  915.9 3.8 collective-permute-start.3
  920.0 479.5 %copy-start.53 = (bf16[128,2048]{1,0:T(8,128)(2,1)}, bf16[128,2048]{1,0:T(8,128)(2,1)S(1)}, u32[]{:S(2)}) copy-start(bf16[128,2048]{1,0:T(8,128)(2,1)S(1)} %get-tuple-element.720) | copy-start | bytes 1572868
  920.0 479.5 %copy-start.111 = (f32[128]{0:T(128)}, f32[128]{0:T(128)S(1)}, u32[]{:S(2)}) copy-start(f32[128]{0:T(128)S(1)} %fusion.336) | copy-start | bytes 1540
  940.1 7.4 collective-permute-start.4
  962.1 359.1 %all-gather.37.cloned.1.call-start = ((), (), s32[]{:S(2)}) async-start(), calls=%async_computation.10 | async-start | bytes 10485760 | tf_op jit(solution)/shard_map/all_gather | solution.py:23
  963.5 425.4 %copy-start.166 = (f32[128]{0:T(128)}, f32[128]{0:T(128)S(1)}, u32[]{:S(2)}) copy-start(f32[128]{0:T(128)S(1)} %get-tuple-element.691) | copy-start | bytes 1540
  977.9 187.4 %copy-start.136 = (f32[128,128]{1,0:T(8,128)}, f32[128,128]{1,0:T(8,128)S(1)}, u32[]{:S(2)}) copy-start(f32[128,128]{1,0:T(8,128)S(1)} %fusion.293) | copy-start | bytes 196612
  1136.7 252.2 %copy-start.147 = (f32[128]{0:T(128)}, f32[128]{0:T(128)S(1)}, u32[]{:S(2)}) copy-start(f32[128]{0:T(128)S(1)} %fusion.337) | copy-start | bytes 1540
  1165.2 417.2 %all-gather.39.cloned.1.call-start = ((), (), s32[]{:S(2)}) async-start(), calls=%async_computation.11 | async-start | bytes 10485760 | tf_op jit(solution)/shard_map/all_gather | solution.py:23
  1362.7 6.4 collective-permute-start.5
  1402.3 3.9 collective-permute-start.6
  1406.3 248.3 %copy-start.59 = (bf16[128,2048]{1,0:T(8,128)(2,1)}, bf16[128,2048]{1,0:T(8,128)(2,1)S(1)}, u32[]{:S(2)}) copy-start(bf16[128,2048]{1,0:T(8,128)(2,1)S(1)} %bitcast_select_fusion.1) | copy-start | bytes 1572868
  1432.5 406.5 %all-gather.41.cloned.1.call-start = ((), (), s32[]{:S(2)}) async-start(), calls=%async_computation.12 | async-start | bytes 10485760 | tf_op jit(solution)/shard_map/all_gather | solution.py:23
  1624.6 6.6 collective-permute-start.7
  1657.4 3.9 collective-permute-start.8
  1661.4 58.0 %copy-start.57 = (bf16[128,2048]{1,0:T(8,128)(2,1)}, bf16[128,2048]{1,0:T(8,128)(2,1)S(1)}, u32[]{:S(2)}) copy-start(bf16[128,2048]{1,0:T(8,128)(2,1)S(1)} %bitcast_select_fusion) | copy-start | bytes 1572868
  1689.0 439.7 %reduce-scatter.8.cloned.1.call-start = ((), (), s32[]{:S(2)}) async-start(), calls=%async_computation.4 | async-start | bytes 41943040 | tf_op jit(solution)/shard_map/reduce_scatter | solution.py:318
  1754.1 957.3 %reduce-scatter.6.cloned.1.call-start = ((), (), s32[]{:S(2)}) async-start(), calls=%async_computation.3 | async-start | bytes 87162880 | tf_op jit(solution)/shard_map/reduce_scatter | solution.py:311
  1781.7 26.6 copy-start.15
  1781.7 26.6 copy-start.114
  1781.7 26.6 copy-start.133
  1781.7 26.6 copy-start.144
  1781.7 26.6 copy-start.165
  1883.9 8.1 collective-permute-start.9
  1970.2 827.6 %reduce-scatter.10.cloned.1.call-start = ((), (), s32[]{:S(2)}) async-start(), calls=%async_computation.13 | async-start | bytes 2785280
  1973.5 1637.2 %all-reduce.62.cloned.1.call-start = ((), (), s32[]{:S(2)}) async-start(), calls=%async_computation.14 | async-start | bytes 51642368 | tf_op jit(solution)/shard_map/psum | solution.py:331
  2721.9 56.7 %copy-start.141 = (f32[2048]{0:T(1024)S(1)}, f32[2048]{0:T(1024)}, u32[]{:S(2)}) copy-start(f32[2048]{0:T(1024)} %get-tuple-element.601) | copy-start | bytes 24580
  2721.9 56.7 %copy-start.142 = (f32[2048]{0:T(1024)S(1)}, f32[2048]{0:T(1024)}, u32[]{:S(2)}) copy-start(f32[2048]{0:T(1024)} %get-tuple-element.603) | copy-start | bytes 24580
  2721.9 72.3 %copy-start.196 = (f32[128]{0:T(128)S(1)}, f32[128]{0:T(128)}, u32[]{:S(2)}) copy-start(f32[128]{0:T(128)} %copy-done.195) | copy-start | bytes 1540
  2721.9 72.3 %copy-start.58 = (bf16[128,2048]{1,0:T(8,128)(2,1)S(1)}, bf16[128,2048]{1,0:T(8,128)(2,1)}, u32[]{:S(2)}) copy-start(bf16[128,2048]{1,0:T(8,128)(2,1)} %copy-done.57) | copy-start | bytes 1572868
  2741.8 54.0 %copy-start.68 = (f32[128,2048]{1,0:T(8,128)S(1)}, f32[128,2048]{1,0:T(8,128)}, u32[]{:S(2)}) copy-start(f32[128,2048]{1,0:T(8,128)} %get-tuple-element.714) | copy-start | bytes 3145732
  (175 other events, 1072.0 us)
Sparse Core Ops, SparseCore 0:
  9.9 316.6 all-gather.26
  373.4 149.2 all-gather.28
  524.5 155.3 all-gather.30
  738.2 148.6 all-gather.32
  962.2 153.8 all-gather.34
  1165.4 155.7 all-gather.36
  1432.6 149.7 all-gather.38
  1689.1 149.7 all-gather.40
  1842.0 286.6 reduce-scatter.7
  2132.0 579.3 reduce-scatter.5
  2715.0 36.4 reduce-scatter.9
  2754.0 856.6 all-reduce.61
where the time goes:
time: 3640 us
  waiting for transfers between devices  2510 us (69%)
  matrix products  539 us (15%)
  local copies, waits for them, and re-layouts  231 us (6%)
  other arithmetic  157 us (4%)
  blocking collectives  141 us (4%)
    psum x1, waiting for transfers between devices, per_device(): lax.psum((own_gain_in, own_w_in, own_conv_w, own_conv_b, own_dt_bias, own...  792 us
    all_gather x6, waiting for transfers between devices, carried_in(): gathered = jax.tree.map(lambda a: lax.all_gather(a, axis), part)  659 us
    reduce_scatter x1, waiting for transfers between devices, per_device(): lax.psum_scatter(sum_w_in, 'fsdp', scatter_dimension=0, tiled=True)  583 us
    all_gather x1, waiting for transfers between devices, per_device(): lax.all_gather(w_in[0], 'fsdp', axis=0, tiled=True)  179 us
    reduce_scatter x1, waiting for transfers between devices, per_device(): lax.psum_scatter(sum_w_out, 'fsdp', scatter_dimension=0, tiled=True)  155 us
    all_gather x1, waiting for transfers between devices, per_device(): lax.all_gather(w_out[0], 'fsdp', axis=0, tiled=True)  137 us
    dot_general x3, matrix products, block_backward(): lax.dot_general(normed_in.astype(jnp.bfloat16), proj_low, contract_rows,...  127 us
    slice x1, local copies, waits for them, and re-layouts, conv_part(): conv_taps[tap_index][None, :] * padded[tap_index:tap_index + tokens_here]  90 us
  transfers between devices with their start and end apart: 22, of which 15 were waited for; matrix products, arithmetic and copies ran while one was open for 14% of the time, Pallas kernels for 0%

commit v1 on v0

v1 whole, which is shorter than its diff:
```python
import functools

import jax
import jax.numpy as jnp
from jax import lax
from jax.experimental import pallas as pl
from jax.experimental.pallas import tpu as pltpu
from jax.sharding import PartitionSpec as P

D = 2048
INNER = 4096
HEADS = 64
HEAD_DIM = 64
STATE = 128
KERNEL = 4
GROUP = 2 * STATE
CHANNELS = INNER + GROUP
LANES = 128
EPS = 1e-05
F32 = jnp.float32
BF16 = jnp.bfloat16
VMEM_BYTES = 48 * 1024 * 1024


def dot32(a, b, ca, cb):
    return lax.dot_general(
        a,
        b,
        (((ca,), (cb,)), ((), ())),
        precision=lax.Precision.HIGHEST,
        preferred_element_type=F32,
    )


def step_sizes(raw, hp, rows):
    shifted = raw + hp[0:1, :]
    dt = jnp.maximum(shifted, 0.0) + jnp.log1p(jnp.exp(-jnp.abs(shifted)))
    decay = dt * hp[1:2, :]
    row = lax.broadcasted_iota(jnp.int32, (rows, rows), 0)
    col = lax.broadcasted_iota(jnp.int32, (rows, rows), 1)
    lower = (row >= col).astype(F32)
    cum = dot32(lower, decay, 1, 0)
    cum_t = dot32(decay, lower, 0, 1)
    return shifted, dt, cum, cum_t, row, col, lower


def spread(v, table):
    hi = v.astype(BF16)
    rest = v - hi.astype(F32)
    mid = rest.astype(BF16)
    low = (rest - mid.astype(F32)).astype(BF16)
    one = lambda p: jnp.dot(p, table, preferred_element_type=F32)
    return one(hi) + one(mid) + one(low)


def forward_kernel(f_ref, pz, px, pbd, cw, hp, table, s0, e0, *rest, second):
    if second:
        dn, gain, y_ref, filt_ref, st_ref, fin_ref, stat_ref, state, xp, xw_s = rest
    else:
        y_ref, filt_ref, st_ref, fin_ref, stat_ref, state, xp, xw_s = rest
    i = pl.program_id(0)
    rows, width = px.shape

    @pl.when(i == 0)
    def _():
        state[...] = s0[...]
        xp[0:8, :] = e0[...]

    xp[8 : 8 + rows, :width] = px[...]
    xp[8 : 8 + rows, width:] = pbd[:, :GROUP]

    def conv_tile(lo):
        acc = cw[4:5, lo : lo + LANES]
        for k in range(KERNEL):
            acc = acc + cw[k : k + 1, lo : lo + LANES] * xp[5 + k : 5 + k + rows, lo : lo + LANES]
        filt_ref[:, lo : lo + LANES] = acc
        return acc * jax.nn.sigmoid(acc)

    b_c = conv_tile(width)
    c_c = conv_tile(width + STATE)
    _, dt, cum, cum_t, row, col, _ = step_sizes(pbd[:, GROUP:], hp, rows)
    last = cum[rows - 1 : rows, :]
    dt_e = spread(dt, table[...])
    ecum_e = spread(jnp.exp(cum), table[...])
    w_e = spread(jnp.exp(last - cum) * dt, table[...])
    last_e = spread(jnp.broadcast_to(jnp.exp(last), (8, last.shape[1])), table[...])
    skip_e = spread(jnp.broadcast_to(hp[2:3, :], (8, last.shape[1])), table[...])
    st_ref[0] = state[...]
    carried = dot32(c_c, state[...], 1, 0)
    scores = dot32(c_c, b_c, 1, 1)
    causal = row >= col
    lane = lax.broadcasted_iota(jnp.int32, (rows, LANES), 1)
    first = lane < HEAD_DIM
    ss = jnp.zeros((rows, LANES), F32)
    s2 = jnp.zeros((rows, LANES), F32)
    for j in range(width // LANES):
        lo = j * LANES
        here = slice(lo, lo + LANES)
        x = conv_tile(lo)
        xd = x * dt_e[:, here]
        parts = []
        for h in (2 * j, 2 * j + 1):
            gap = cum[:, h : h + 1] - cum_t[h : h + 1, :]
            m = jnp.exp(jnp.where(causal, gap, -1e30)) * scores
            parts.append(dot32(m, xd, 1, 0))
        y = (
            jnp.where(first, parts[0], parts[1])
            + carried[:, here] * ecum_e[:, here]
            + skip_e[0:1, here] * x
        )
        y_ref[:, here] = y
        xw_s[:, here] = x * w_e[:, here]
        z = pz[:, here]
        g = y * z * jax.nn.sigmoid(z)
        ss = ss + g * g
        if second:
            s2 = s2 + g * dn[:, here] * gain[0:1, here]
    state[...] = state[...] * last_e[0:1, :] + dot32(b_c, xw_s[...], 0, 0)
    fin_ref[...] = state[...]
    xp[0:8, :] = xp[rows : rows + 8, :]
    stat_ref[:, 0:1] = jnp.sum(ss, axis=1, keepdims=True)
    stat_ref[:, 1:2] = jnp.sum(s2, axis=1, keepdims=True)


def backward_kernel(
    f_ref,
    pz,
    px,
    pbd,
    y_ref,
    filt,
    dn,
    rc,
    st_in,
    st_out,
    cw,
    hp,
    table,
    gain,
    g0,
    e0,
    dz_ref,
    dx_ref,
    dbc_ref,
    ddt_ref,
    dgain_ref,
    dconv_ref,
    dhp_ref,
    gfin_ref,
    efin_ref,
    grad,
    dfp,
    both,
    xw_s,
    dyc_s,
    rowv,
):
    i = pl.program_id(0)
    rows, width = px.shape
    heads = hp.shape[1]

    @pl.when(i == 0)
    def _():
        grad[...] = g0[...]
        dfp[rows : rows + 8, :] = e0[...]
        dgain_ref[...] = jnp.zeros_like(dgain_ref)
        dconv_ref[...] = jnp.zeros_like(dconv_ref)
        dhp_ref[...] = jnp.zeros_like(dhp_ref)

    def silu_pair(v):
        s = jax.nn.sigmoid(v)
        a = v * s
        return a, s * (1.0 + v - a)

    b_c, b_d = silu_pair(filt[:, width : width + STATE])
    c_c, c_d = silu_pair(filt[:, width + STATE :])
    shifted, dt, cum, cum_t, row, col, lower = step_sizes(pbd[:, GROUP:], hp, rows)
    last = cum[rows - 1 : rows, :]
    tail = jnp.exp(last - cum)
    dt_e = spread(dt, table[...])
    ecum_e = spread(jnp.exp(cum), table[...])
    tail_e = spread(tail, table[...])
    last_e = spread(jnp.broadcast_to(jnp.exp(last), (8, heads)), table[...])
    skip_e = spread(jnp.broadcast_to(hp[2:3, :], (8, heads)), table[...])
    k_all = dot32(b_c, grad[...], 1, 0)
    scores_t = dot32(b_c, c_c, 1, 1)
    causal_t = row <= col
    lane = lax.broadcasted_iota(jnp.int32, (rows, LANES), 1)
    first = lane < HEAD_DIM
    dcb_t = jnp.zeros((rows, rows), F32)
    r = rc[:, 0:1]
    coef = rc[:, 1:2]
    rowv[0:1, :] = jnp.sum(grad[...] * st_out[0], axis=0, keepdims=True)
    for j in range(width // LANES):
        lo = j * LANES
        here = slice(lo, lo + LANES)
        z = pz[:, here]
        y = y_ref[:, here]
        sz, dsz = silu_pair(z)
        g = y * sz
        dnt = dn[:, here]
        dg = dnt * gain[0:1, here] * r - g * coef
        dgain_ref[0:1, here] += jnp.sum(dnt * g * r, axis=0, keepdims=True)
        dy = dg * sz
        dz_ref[:, here] = (dg * y * dsz).astype(BF16)
        x, xder = silu_pair(filt[:, here])
        xd = x * dt_e[:, here]
        parts = []
        for n, h in enumerate((2 * j, 2 * j + 1)):
            gap = cum_t[h : h + 1, :] - cum[:, h : h + 1]
            decay_t = jnp.exp(jnp.where(causal_t, gap, -1e30))
            parts.append(dot32(decay_t * scores_t, dy, 1, 0))
            keep = first if n == 0 else jnp.logical_not(first)
            dcb_t = dcb_t + decay_t * dot32(jnp.where(keep, xd, 0.0), dy, 1, 1)
        v = jnp.where(first, parts[0], parts[1]) + k_all[:, here] * tail_e[:, here]
        skip = skip_e[0:1, here]
        dx = dt_e[:, here] * v + skip * dy
        both[0:rows, here] = x * v
        both[rows : 2 * rows, here] = dy * (y - skip * x)
        rowv[1:2, here] = jnp.sum(dy * x, axis=0, keepdims=True)
        xw_s[:, here] = xd * tail_e[:, here]
        dyc_s[:, here] = dy * ecum_e[:, here]
        dfp[0:rows, here] = dx * xder
    dc = dot32(dcb_t, b_c, 0, 0) + dot32(dyc_s[...], st_in[0], 1, 1)
    db = dot32(dcb_t, c_c, 1, 0) + dot32(xw_s[...], grad[...], 1, 1)
    dfp[0:rows, width : width + STATE] = db * b_d
    dfp[0:rows, width + STATE :] = dc * c_d
    grad[...] = grad[...] * last_e[0:1, :] + dot32(c_c, dyc_s[...], 0, 0)
    gfin_ref[...] = grad[...]

    table32 = table[...].astype(F32)
    sums = dot32(both[...], table32, 1, 1)
    rsums = dot32(rowv[...], table32, 1, 1)
    ddt_x = sums[0:rows]
    dcum = sums[rows : 2 * rows] - dt * ddt_x
    upto = lax.broadcasted_iota(jnp.int32, (rows, heads), 0)
    dcum = dcum + jnp.where(upto == rows - 1, rsums[0:1, :], 0.0)
    ddecay = dot32(lower, dcum, 0, 0)
    ddt = ddt_x + hp[1:2, :] * ddecay
    draw = ddt * jax.nn.sigmoid(shifted)
    ddt_ref[...] = draw
    dhp_ref[0:1, :] += jnp.sum(draw, axis=0, keepdims=True)
    dhp_ref[1:2, :] += jnp.sum(ddecay * dt, axis=0, keepdims=True) * hp[1:2, :]
    dhp_ref[2:3, :] += rsums[1:2, :]

    for lo in range(0, width + GROUP, LANES):
        here = slice(lo, lo + LANES)
        src = px[:, here] if lo < width else pbd[:, lo - width : lo - width + LANES]
        total = jnp.zeros((rows, LANES), F32)
        for k in range(KERNEL):
            shift = KERNEL - 1 - k
            moved = dfp[shift : shift + rows, here]
            total = total + cw[k : k + 1, here] * moved
            dconv_ref[k : k + 1, here] += jnp.sum(src * moved, axis=0, keepdims=True)
        dconv_ref[4:5, here] += jnp.sum(dfp[0:rows, here], axis=0, keepdims=True)
        if lo < width:
            dx_ref[:, here] = total.astype(BF16)
        else:
            dbc_ref[:, lo - width : lo - width + LANES] = total
    dfp[rows : rows + 8, :] = dfp[0:8, :]
    efin_ref[...] = dfp[0:8, :]


def whole(shape):
    return pl.BlockSpec(shape, lambda i, f: (0,) * len(shape))


def run_forward(f, pz, px, pbd, cw, hp, table, s0, e0, extra, rows):
    total, width = px.shape
    heads = hp.shape[1]
    count = total // rows
    block = lambda w: pl.BlockSpec((rows, w), lambda i, f: (jnp.bitwise_xor(i, f[0]), 0))
    in_specs = [
        block(width),
        block(width),
        block(GROUP + heads),
        whole((8, width + GROUP)),
        whole((8, heads)),
        whole((heads, width)),
        whole((STATE, width)),
        whole((8, width + GROUP)),
    ]
    if extra:
        in_specs += [block(width), whole((1, width))]
    shape = jax.ShapeDtypeStruct
    return pl.pallas_call(
        functools.partial(forward_kernel, second=bool(extra)),
        grid_spec=pltpu.PrefetchScalarGridSpec(
            num_scalar_prefetch=1,
            grid=(count,),
            in_specs=in_specs,
            out_specs=[
                block(width),
                block(width + GROUP),
                pl.BlockSpec((1, STATE, width), lambda i, f: (i, 0, 0)),
                whole((STATE, width)),
                block(8),
            ],
            scratch_shapes=[
                pltpu.VMEM((STATE, width), F32),
                pltpu.VMEM((rows + 8, width + GROUP), F32),
                pltpu.VMEM((rows, width), F32),
            ],
        ),
        out_shape=[
            shape((total, width), F32),
            shape((total, width + GROUP), F32),
            shape((count, STATE, width), F32),
            shape((STATE, width), F32),
            shape((total, 8), F32),
        ],
        compiler_params=pltpu.CompilerParams(vmem_limit_bytes=VMEM_BYTES),
        name="scan_forward",
    )(f, pz, px, pbd, cw, hp, table, s0, e0, *extra)


def run_backward(f, pz, px, pbd, y, filt, dn, rc, states, cw, hp, table, gain, g0, e0, rows):
    total, width = px.shape
    heads = hp.shape[1]
    count = total // rows
    turn = lambda i: count - 1 - i
    block = lambda w: pl.BlockSpec((rows, w), lambda i, f: (jnp.bitwise_xor(turn(i), f[0]), 0))
    shape = jax.ShapeDtypeStruct
    return pl.pallas_call(
        backward_kernel,
        grid_spec=pltpu.PrefetchScalarGridSpec(
            num_scalar_prefetch=1,
            grid=(count,),
            in_specs=[
                block(width),
                block(width),
                block(GROUP + heads),
                block(width),
                block(width + GROUP),
                block(width),
                block(8),
                pl.BlockSpec((1, STATE, width), lambda i, f: (turn(i), 0, 0)),
                pl.BlockSpec((1, STATE, width), lambda i, f: (turn(i) + 1, 0, 0)),
                whole((8, width + GROUP)),
                whole((8, heads)),
                whole((heads, width)),
                whole((1, width)),
                whole((STATE, width)),
                whole((8, width + GROUP)),
            ],
            out_specs=[
                block(width),
                block(width),
                block(GROUP),
                block(heads),
                whole((8, width)),
                whole((8, width + GROUP)),
                whole((8, heads)),
                whole((STATE, width)),
                whole((8, width + GROUP)),
            ],
            scratch_shapes=[
                pltpu.VMEM((STATE, width), F32),
                pltpu.VMEM((rows + 8, width + GROUP), F32),
                pltpu.VMEM((2 * rows, width), F32),
                pltpu.VMEM((rows, width), F32),
                pltpu.VMEM((rows, width), F32),
                pltpu.VMEM((8, width), F32),
            ],
        ),
        out_shape=[
            shape((total, width), BF16),
            shape((total, width), BF16),
            shape((total, GROUP), F32),
            shape((total, heads), F32),
            shape((8, width), F32),
            shape((8, width + GROUP), F32),
            shape((8, heads), F32),
            shape((STATE, width), F32),
            shape((8, width + GROUP), F32),
        ],
        compiler_params=pltpu.CompilerParams(vmem_limit_bytes=VMEM_BYTES),
        name="scan_backward",
    )(f, pz, px, pbd, y, filt, dn, rc, states, states, cw, hp, table, gain, g0, e0)


def swap_section(v):
    return lax.ppermute(v, "section", [(0, 1), (1, 0)])


def move_fsdp(v, m):
    n = lax.axis_size("fsdp")
    return lax.ppermute(v, "fsdp", [(i, i ^ m) for i in range(n)])


def transpose_places(v):
    n, s = lax.axis_size("fsdp"), lax.axis_size("seq")
    pairs = [
        ((j * n + i) * n + k, (j * n + k) * n + i)
        for j in range(s // n)
        for i in range(n)
        for k in range(n)
    ]
    return lax.ppermute(v, ("seq", "fsdp"), pairs)


def gather_blocks(v):
    n = lax.axis_size("fsdp")
    return jnp.stack([v] + [move_fsdp(v, m) for m in range(1, n)])


def gather_in_order(v, f):
    n = lax.axis_size("fsdp")
    out = jnp.zeros((n,) + v.shape, v.dtype)
    for m in range(n):
        piece = v if m == 0 else move_fsdp(v, m)
        out = lax.dynamic_update_index_in_dim(out, piece, f ^ m, 0)
    return out


def scatter_sum(partial):
    n = lax.axis_size("fsdp")
    total = partial[0]
    for m in range(1, n):
        total = total + move_fsdp(partial[m].astype(BF16), m).astype(F32)
    return total


def sum_rows(v):
    n = lax.axis_size("fsdp")
    total = v
    for m in range(1, n):
        got = move_fsdp(v, m)
        total = total + jnp.stack([got[j ^ m] for j in range(n)])
    return total


def relay(total, local, reverse):
    n, s = lax.axis_size("fsdp"), lax.axis_size("seq")
    segments = s // n
    place = lax.axis_index("seq") // n
    own = lax.axis_index("seq") % n
    totals = lax.all_gather(total, "seq")
    locals_ = lax.all_gather(local, "seq")
    state = jnp.zeros_like(local)
    order = range(segments - 1, -1, -1) if reverse else range(segments)
    for j in order:
        use = (j > place) if reverse else (j < place)
        t = lax.dynamic_index_in_dim(totals, j * n + own, 0, False)
        v = lax.dynamic_index_in_dim(locals_, j * n + own, 0, False)
        state = jnp.where(use, t * state + v, state)
    return state


def next_segment(v, step):
    n, s = lax.axis_size("fsdp"), lax.axis_size("seq")
    pairs = [(k, k + step * n) for k in range(s) if 0 <= k + step * n < s]
    return lax.ppermute(v, "seq", pairs)


def dot_rows(a, b):
    return lax.dot_general(a, b, (((0,), (0,)), ((), ())), preferred_element_type=F32)


def dot_cols(a, b):
    return lax.dot_general(a, b, (((1,), (1,)), ((), ())), preferred_element_type=F32)


def normalised(h, gain):
    return h * lax.rsqrt(jnp.mean(h * h, axis=-1, keepdims=True) + EPS) * gain


def per_device(
    inputs,
    cotangent,
    lengths,
    gain_in,
    w_in,
    conv_w,
    conv_b,
    dt_bias,
    a_log,
    d_skip,
    gain_out,
    w_out,
):
    n = lax.axis_size("fsdp")
    nz = lax.axis_size("seq")
    segments = nz // n
    c = lax.axis_index("section")
    f = lax.axis_index("fsdp")
    place = lax.axis_index("seq")
    upper = c == 0
    rows = inputs.shape[2]
    width = INNER // n
    heads = HEADS // n
    share = D // n
    group = GROUP // n
    f1 = f.reshape(1).astype(jnp.int32)

    def pick(a, b):
        return jnp.where(upper, a, b)

    own_in = lax.dynamic_index_in_dim(inputs, c, 0, False)[0]
    own_ct = lax.dynamic_index_in_dim(cotangent, c, 0, False)[0]
    own_len = lax.dynamic_index_in_dim(lengths, c, 0, False)
    length = transpose_places(own_len)
    start = ((place // n) * n + f) * rows
    valid = (start + jnp.arange(rows, dtype=jnp.int32) < length[0]).astype(F32)[:, None]
    h0 = transpose_places(own_in)
    dout1 = transpose_places(own_ct).astype(F32)
    all_h0 = gather_blocks(h0).reshape(n * rows, D)

    pack = jnp.concatenate(
        [
            gain_in[0],
            conv_w[0].reshape(-1),
            conv_b[0],
            dt_bias[0],
            a_log[0],
            d_skip[0],
            gain_out[0],
        ]
    )
    mine = gather_in_order(pack, f)
    theirs = swap_section(mine)
    small = []
    for full in (pick(mine, theirs), pick(theirs, mine)):
        full = full.astype(F32)
        at = 0

        def take(size):
            nonlocal at
            at += size
            return full[:, at - size : at]

        per = CHANNELS // n
        gain = take(share).reshape(1, D)
        taps = take(KERNEL * per).reshape(n, KERNEL, per).transpose(1, 0, 2).reshape(KERNEL, -1)
        bias = take(per).reshape(1, CHANNELS)
        table = jnp.concatenate([taps, bias, jnp.zeros((3, CHANNELS), F32)])
        cw = jnp.concatenate(
            [lax.dynamic_slice_in_dim(table, f * width, width, 1), table[:, INNER:]], axis=1
        )
        own_heads = [
            lax.dynamic_index_in_dim(take(heads), f, 0, True) for _ in range(3)
        ]
        hp = jnp.concatenate(
            [own_heads[0], -jnp.exp(own_heads[1]), own_heads[2], jnp.zeros((5, heads), F32)]
        )
        gout = lax.dynamic_index_in_dim(take(width), f, 0, True)
        small.append((gain, cw, hp, gout))

    w = w_in[0]

    def columns(k):
        cut = lambda at, size: lax.dynamic_slice_in_dim(w, at, size, 1)
        return (
            cut(k * width, width),
            cut(INNER + k * width, width),
            jnp.concatenate(
                [w[:, 2 * INNER : 2 * INNER + GROUP], cut(2 * INNER + GROUP + k * heads, heads)],
                axis=1,
            ),
        )

    blocks = [columns(f ^ m) for m in range(n)]

    def fetch(layer, blocks):
        full = [jnp.zeros((n,) + b.shape, BF16) for b in blocks[0]]
        for m in range(n):
            for q in range(3):
                piece = blocks[m][q]
                if m:
                    pairs = [(layer * n + i, layer * n + (i ^ m)) for i in range(n)]
                    piece = lax.ppermute(piece, ("section", "fsdp"), pairs)
                other = lax.ppermute(piece, "section", [(layer, 1 - layer)])
                got = jnp.where(c == layer, piece, other)
                full[q] = lax.dynamic_update_index_in_dim(full[q], got, f ^ m, 0)
        return [v.reshape(D, v.shape[-1]) for v in full]

    w0 = fetch(0, blocks)
    blocks, _ = lax.optimization_barrier((blocks, w0))
    w1 = fetch(1, blocks)
    wo_mine = w_out[0]
    wo_other = swap_section(wo_mine)
    wo = (pick(wo_mine, wo_other), pick(wo_other, wo_mine))
    win = (w0, w1)

    expand = (
        jnp.arange(heads)[:, None] == jnp.arange(width)[None, :] // HEAD_DIM
    ).astype(BF16)
    zero_state = jnp.zeros((STATE, width), F32)
    zero_edge = jnp.zeros((8, width + GROUP), F32)

    def project(normed, layer):
        return [
            jnp.dot(normed, part, preferred_element_type=F32) for part in win[layer]
        ]

    def scan(proj, layer, extra):
        pz, px, pbd = proj
        _, cw, hp, _ = small[layer]
        args = (f1, pz, px, pbd, cw, hp, expand)
        if segments == 1:
            return run_forward(*args, zero_state, zero_edge, extra, rows)
        rear = lax.dynamic_slice_in_dim(
            jnp.concatenate([px, pbd[:, :GROUP]], axis=1), ((n - 1) ^ f) * rows + rows - 8, 8, 0
        )
        edge = next_segment(rear, 1)
        local = run_forward(*args, zero_state, edge, extra, rows)[3]
        decay = jax.nn.softplus(pbd[:, GROUP:] + hp[0:1]) * hp[1:2]
        total = jnp.repeat(jnp.exp(jnp.sum(decay, axis=0)), HEAD_DIM)[None, :]
        state = relay(total, local, False)
        return run_forward(*args, state, edge, extra, rows)

    def unscan(proj, fwd, dn, rc, layer):
        pz, px, pbd = proj
        y, filt, states, final = fwd[:4]
        _, cw, hp, gout = small[layer]
        states = jnp.concatenate([states, final[None]])
        args = (f1, pz, px, pbd, y, filt, dn, rc, states, cw, hp, expand, gout)
        if segments == 1:
            return run_backward(*args, zero_state, zero_edge, rows)
        local = run_backward(*args, zero_state, zero_edge, rows)[7]
        decay = jax.nn.softplus(pbd[:, GROUP:] + hp[0:1]) * hp[1:2]
        total = jnp.repeat(jnp.exp(jnp.sum(decay, axis=0)), HEAD_DIM)[None, :]
        grad = relay(total, local, True)
        edge = next_segment(run_backward(*args, grad, zero_edge, rows)[8], -1)
        return run_backward(*args, grad, edge, rows)

    def gated(pz, y, r, layer):
        g = y * jax.nn.silu(pz)
        return (g * r * small[layer][3]).astype(BF16)

    blockwise = lambda v: v.reshape(n, rows, v.shape[-1])

    normed_in0 = normalised(all_h0.astype(F32), small[0][0]).astype(BF16)
    proj0 = project(normed_in0, 0)
    fwd0 = scan(proj0, 0, ())
    stat0 = sum_rows(blockwise(fwd0[4][:, 0:1])).reshape(n * rows, 1)
    r0 = lax.rsqrt(stat0 / INNER + EPS)
    normed0 = gated(proj0[0], fwd0[0], r0, 0)
    mixed0 = scatter_sum(blockwise(jnp.dot(normed0, wo[0], preferred_element_type=F32)))
    out0 = valid * (h0.astype(F32) + mixed0)
    h1 = out0.astype(BF16)

    part1 = normalised(h1.astype(F32), small[1][0]).astype(BF16)
    normed_in1 = gather_blocks(part1).reshape(n * rows, D)
    proj1 = project(normed_in1, 1)
    dmixed1 = gather_blocks((valid * dout1).astype(BF16)).reshape(n * rows, D)
    dn1 = dot_cols(dmixed1, wo[1])
    fwd1 = scan(proj1, 1, (dn1, small[1][3]))
    stat1 = sum_rows(blockwise(fwd1[4][:, 0:2])).reshape(n * rows, 2)
    r1 = lax.rsqrt(stat1[:, 0:1] / INNER + EPS)
    normed1 = gated(proj1[0], fwd1[0], r1, 1)
    mixed1 = scatter_sum(blockwise(jnp.dot(normed1, wo[1], preferred_element_type=F32)))
    out1 = valid * (h1.astype(F32) + mixed1)
    last1 = out1.astype(BF16)

    def half_sums(a, b, parts):
        view = a.reshape(a.shape[0], parts, 2, -1)
        cut = lambda k: lax.dynamic_index_in_dim(view, k, 2, False).reshape(a.shape[0], -1)
        away = swap_section(dot_rows(cut(1 - c), b).astype(BF16))
        return (dot_rows(cut(c), b) + away.astype(F32)).astype(BF16)

    def over_seq(v, dim):
        piece = lax.psum_scatter(v, "seq", scatter_dimension=dim, tiled=True)
        return piece

    def back_layer(layer, dn, dmixed, rc, proj, fwd, normed, normed_in):
        gw_out = half_sums(normed, dmixed, 1)
        dz, dx, dbc, ddt, dgain, dconv, dhp, _, _ = unscan(proj, fwd, dn, rc, layer)
        wz, wx, wbd = win[layer]
        shares = blockwise(dbc)
        own_cols = lambda k: lax.dynamic_slice_in_dim(shares, k * group, group, 2)
        total = own_cols(f)
        for m in range(1, n):
            got = move_fsdp(own_cols(f ^ m), m)
            total = total + jnp.stack([got[j ^ m] for j in range(n)])
        dsmall = jnp.concatenate([total.reshape(n * rows, group), ddt], axis=1).astype(BF16)
        wsmall = jnp.concatenate(
            [lax.dynamic_slice_in_dim(wbd, f * group, group, 1), wbd[:, GROUP:]], axis=1
        )
        back = dot_cols(dz, wz) + dot_cols(dx, wx) + dot_cols(dsmall, wsmall)
        dnormed_in = scatter_sum(blockwise(back))
        dproj = jnp.concatenate([dz, dx, dsmall], axis=1)
        gw_in = half_sums(normed_in, dproj, n)
        return dnormed_in, gw_in, gw_out, (dgain[0], dconv[:5], dhp[:3])

    def back_norm(dout, dnormed_in, h, gain):
        h = h.astype(F32)
        r = lax.rsqrt(jnp.mean(h * h, axis=-1, keepdims=True) + EPS)
        u = dnormed_in * gain
        mean = jnp.mean(u * h, axis=-1, keepdims=True)
        dgain = jnp.sum(dnormed_in * h * r, axis=0)
        return valid * dout + r * u - h * (r * r * r) * mean, dgain

    def combine(layer, gw_in, gw_out):
        a = over_seq(gw_in.reshape(n, share // 2, -1), 1)
        b = over_seq(gw_out, 0)
        full = jnp.zeros_like(a)
        for m in range(n):
            piece = lax.dynamic_index_in_dim(a, f ^ m, 0, False)
            if m:
                piece = move_fsdp(piece, m)
            full = lax.dynamic_update_index_in_dim(full, piece, f ^ m, 0)
        return (
            lax.all_gather(full, "seq", axis=1, tiled=True),
            lax.all_gather(b, "seq", axis=0, tiled=True),
        )

    rc1 = jnp.concatenate(
        [r1, (r1 * r1 * r1 / INNER) * stat1[:, 1:2], jnp.zeros((n * rows, 6), F32)], axis=1
    )
    dnin1, gwi1, gwo1, smalls1 = back_layer(
        1, dn1, dmixed1, rc1, proj1, fwd1, normed1, normed_in1
    )
    grad1, dgin1 = back_norm(dout1, dnin1, h1, small[1][0])
    full1 = combine(1, gwi1, gwo1)

    dout0 = grad1.astype(BF16).astype(F32)
    dmixed0_own = (valid * dout0).astype(BF16)
    dmixed0 = gather_blocks(dmixed0_own).reshape(n * rows, D)
    along = jnp.sum(dmixed0_own.astype(F32) * mixed0, axis=-1, keepdims=True)
    along0 = gather_blocks(along).reshape(n * rows, 1)
    dn0 = dot_cols(dmixed0, wo[0])
    rc0 = jnp.concatenate(
        [r0, (r0 * r0 / INNER) * along0, jnp.zeros((n * rows, 6), F32)], axis=1
    )
    dnin0, gwi0, gwo0, smalls0 = back_layer(
        0, dn0, dmixed0, rc0, proj0, fwd0, normed0, normed_in0
    )
    grad0, dgin0 = back_norm(dout0, dnin0, h0, small[0][0])
    full0 = combine(0, gwi0, gwo0)

    def packed(dgin, smalls, out, mixed):
        dgain, dconv, dhp = smalls
        put = lambda v, size, at: lax.dynamic_update_slice(
            jnp.zeros(v.shape[:-1] + (size,), F32), v, (0,) * (v.ndim - 1) + (at,)
        )
        conv = put(dconv[:, :width], CHANNELS, f * width)
        conv = conv.at[:, INNER:].set(dconv[:, width:])
        sums = jnp.stack(
            [jnp.sum(out * out), jnp.sum((valid * mixed) ** 2), jnp.sum(valid)]
        )
        return jnp.concatenate(
            [
                dgin,
                conv.reshape(-1),
                put(dhp, HEADS, f * heads).reshape(-1),
                put(dgain, INNER, f * width),
                sums,
            ]
        )

    everyone = ("section", "seq", "fsdp")
    p1 = lax.psum(packed(dgin1, smalls1, out1, mixed1), everyone)
    p0 = lax.psum(packed(dgin0, smalls0, out0, mixed0), everyone)
    p = pick(p0, p1)
    at = 0

    def take(size):
        nonlocal at
        at += size
        return p[at - size : at]

    mine_of = lambda v, size: lax.dynamic_slice_in_dim(v, f * size, size, v.ndim - 1)
    o_gain_in = mine_of(take(D), share)
    o_conv = mine_of(take(5 * CHANNELS).reshape(5, CHANNELS), CHANNELS // n)
    o_heads = mine_of(take(3 * HEADS).reshape(3, HEADS), heads)
    o_gain_out = mine_of(take(INNER), width)
    sums = take(3)
    act_rms = jnp.sqrt(sums[:2] / (sums[2] * D))[None]

    def owned(a, b):
        own, away = pick(a, b), swap_section(pick(b, a))
        return pick(own, away), pick(away, own)

    lo_in, hi_in = owned(full0[0], full1[0])
    cols = jnp.concatenate([lo_in, hi_in], axis=1).astype(F32)
    side = lambda v: v.transpose(1, 0, 2).reshape(share, -1)
    g_w_in = jnp.concatenate(
        [
            side(cols[:, :, :width]),
            side(cols[:, :, width : 2 * width]),
            side(cols[:, :, 2 * width : 2 * width + group]),
            side(cols[:, :, 2 * width + group :]),
        ],
        axis=1,
    )
    lo_out, hi_out = owned(full0[1], full1[1])
    g_w_out = jnp.concatenate([lo_out, hi_out], axis=0).astype(F32)

    def returned(a, b):
        own, away = pick(a, b), pick(b, a)
        own = transpose_places(own)
        away = swap_section(transpose_places(away))
        return jnp.stack([pick(own, away), pick(away, own)])

    layer_out = returned(h1, last1)
    in_grads = returned(grad0, grad1)
    return (
        layer_out[None, :, None],
        in_grads[None, :, None],
        o_gain_in[None],
        g_w_in[None],
        o_conv[None, :4],
        o_conv[None, 4],
        o_heads[None, 0],
        o_heads[None, 1],
        o_heads[None, 2],
        o_gain_out[None],
        g_w_out[None],
        act_rms,
    )


def solution(mesh):
    in_specs = (
        P(None, "fsdp", "seq", None),
        P(None, "fsdp", "seq", None),
        P(None, "fsdp"),
        P("section", "fsdp"),
        P("section", "fsdp", None),
        P("section", None, "fsdp"),
        P("section", "fsdp"),
        P("section", "fsdp"),
        P("section", "fsdp"),
        P("section", "fsdp"),
        P("section", "fsdp"),
        P("section", "fsdp", None),
    )
    out_specs = (
        P("section", None, "fsdp", "seq", None),
        P("section", None, "fsdp", "seq", None),
        P("section", "fsdp"),
        P("section", "fsdp", None),
        P("section", None, "fsdp"),
        P("section", "fsdp"),
        P("section", "fsdp"),
        P("section", "fsdp"),
        P("section", "fsdp"),
        P("section", "fsdp"),
        P("section", "fsdp", None),
        P("section", None),
    )
    return jax.shard_map(
        per_device, mesh=mesh, in_specs=in_specs, out_specs=out_specs, check_vma=False
    )
```

time: 3640 us -> 1580 us (0.43)
  waiting for transfers between devices: 2510 us -> 571 us
  matrix products: 539 us -> 92.3 us
  starting transfers between devices: 22.3 us -> 267 us
  local copies, waits for them, and re-layouts: 231 us -> 375 us
  blocking collectives: 141 us -> 0 us
  Pallas kernels: 0 us -> 105 us
    reduce_scatter x2 -> x4, waiting for transfers between devices: 738 us -> 0.06 us  [over_seq(): piece = lax.psum_scatter(v, 'seq', scatter_dimension=dim, tiled=True)]
    psum x1, waiting for transfers between devices: 792 us -> 85.3 us  [per_device(): p0 = lax.psum(packed(dgin0, smalls0, out0, mixed0), everyone)]
    all_gather x8 -> x4, waiting for transfers between devices: 975 us -> 309 us  [the longest x2 178 us: combine(): lax.all_gather(full, 'seq', axis=1, tiled=True)]
    dot_general x54 -> x24, matrix products: 539 us -> 92.3 us  [the longest x8 31.9 us: dot_cols(): lax.dot_general(a, b, (((1,), (1,)), ((), ())), preferred_element_type=F32)]
    ppermute x10 -> x107, starting transfers between devices: 21.2 us -> 266 us  [the longest x48 127 us: move_fsdp(): return lax.ppermute(v, 'fsdp', [(i, i ^ m) for i in range(n)])]
    ppermute x10 -> x107, waiting for transfers between devices: 6.93 us -> 176 us  [the longest x48 98.2 us: move_fsdp(): return lax.ppermute(v, 'fsdp', [(i, i ^ m) for i in range(n)])]
    dynamic_update_slice x0 -> x26, local copies, waits for them, and re-layouts: none -> 168 us  [the longest x8 86.3 us: fetch(): full[q] = lax.dynamic_update_index_in_dim(full[q], got, f ^ m, 0)]
    pallas_call x0 -> x4, Pallas kernels: none -> 105 us  [the longest x2 71.5 us: run_backward(): pl.pallas_call(backward_kernel, grid_spec=pltpu.PrefetchScalarGridSpec(nu...]
  transfers between devices with their start and end apart: 22 -> 116, of which waited for: 15 -> 29; matrix products, arithmetic and copies ran while one was open for 14% -> 32% of each run, Pallas kernels for 0% -> 3%
where the time goes in v1:
time: 1580 us; the launch traced here: 1560 us
  waiting for transfers between devices  571 us (36%)
  local copies, waits for them, and re-layouts  375 us (24%)
  starting transfers between devices  267 us (17%)
  other arithmetic  128 us (8%)
  Pallas kernels  105 us (7%)
  matrix products  92.3 us (6%)
  between operations  19 us (1%)
    all_gather x2, waiting for transfers between devices, combine(): lax.all_gather(full, 'seq', axis=1, tiled=True)  178 us
    all_gather x2, waiting for transfers between devices, combine(): lax.all_gather(b, 'seq', axis=0, tiled=True)  131 us
    ppermute x48, starting transfers between devices, move_fsdp(): return lax.ppermute(v, 'fsdp', [(i, i ^ m) for i in range(n)])  127 us
    ppermute x48, waiting for transfers between devices, move_fsdp(): return lax.ppermute(v, 'fsdp', [(i, i ^ m) for i in range(n)])  98.2 us
    dynamic_update_slice x8, local copies, waits for them, and re-layouts, fetch(): full[q] = lax.dynamic_update_index_in_dim(full[q], got, f ^ m, 0)  86.3 us
    psum x1, waiting for transfers between devices, per_device(): p0 = lax.psum(packed(dgin0, smalls0, out0, mixed0), everyone)  85.3 us
    dynamic_update_slice x8, local copies, waits for them, and re-layouts, combine(): full = lax.dynamic_update_index_in_dim(full, piece, f ^ m, 0)  79.9 us
    pallas_call x2, Pallas kernels, run_backward(): pl.pallas_call(backward_kernel, grid_spec=pltpu.PrefetchScalarGridSpec(nu...  71.5 us
  transfers between devices with their start and end apart: 116, of which 29 were waited for; matrix products, arithmetic and copies ran while one was open for 32% of the time, Pallas kernels for 3%

profile of v1, /device:TPU:1, one launch (start us, length us, event | category | flops | bytes accessed | tf_op | source)
XLA Modules:
  0.0 1556.6 jit_solution(8217908224383149783)
XLA Ops:
  26.4 6.2 constant_dynamic-slice_fusion.34
  65.4 8.6 collective-permute-start.4
  83.5 14.0 collective-permute-done.27
  102.0 10.8 dynamic_update_slice.142
  125.8 10.8 dynamic_update_slice.143
  136.6 10.8 dynamic_update_slice.144
  147.4 10.8 dynamic_update_slice.145
  180.2 26.0 %collective-permute-start.33 = (bf16[1024,2048]{1,0:T(8,128)(2,1)}, bf16[1024,2048]{1,0:T(8,128)(2,1)}, u32[]{:S(2)}, u32[]{:S(2)}) collective-permute-start(bf16[1024,2048]{1,0:T(8,128)(2,1)} %bitcast.44), channel_id=1, source_target_pairs={{0,16},{16,0},{1,17},{17,1},{2,18},{18,2},{3,19},{19,3},{4,20},{20... | collective-permute-start | bytes 12582920 | tf_op jit(solution)/shard_map/ppermute | solution.py:383
  218.5 16.3 %scan_forward.2 = (f32[512,1024]{1,0:T(8,128)S(1)}, f32[512,1280]{1,0:T(8,128)}, f32[4,128,1024]{2,1,0:T(8,128)}, f32[128,1024]{1,0:T(8,128)S(1)}, f32[512,8]{1,0:T(8,128)}) custom-call(s32[1]{0:T(128)} %bitcast.3.f_ref, f32[512,1024]{1,0:T(8,128)} %fusion.115.pz, f32[512,1024]{1,0:T(8,128)} %fusion.116.px, f32[512,272]{1,0:T(8,128)S(1)} %fusion.117.pbd, ...), custom_call_target="tpu_custom_call" | custom-call | tf_op jit(solution)/shard_map/scan_forward/pallas_call | solution.py:286
  239.7 6.7 collective-permute-start.54
  273.4 10.8 dynamic_update_slice.154
  298.6 10.8 dynamic_update_slice.155
  309.4 10.8 dynamic_update_slice.156
  320.2 10.8 dynamic_update_slice.157
  349.1 5.8 fusion.111
  358.8 29.1 %collective-permute-done.48 = bf16[512,1024]{1,0:T(8,128)(2,1)S(1)} collective-permute-done((bf16[512,1024]{1,0:T(8,128)(2,1)S(1)}, bf16[512,1024]{1,0:T(8,128)(2,1)S(1)}, u32[]{:S(2)}, u32[]{:S(2)}) %collective-permute-start.48) | collective-permute-done | bytes 1048608 | tf_op jit(solution)/shard_map/ppermute | solution.py:571
  397.2 11.9 collective-permute-done.52
  416.7 15.9 %collective-permute-done.35 = bf16[128,2048]{1,0:T(8,128)(2,1)S(1)} collective-permute-done((bf16[128,2048]{1,0:T(8,128)(2,1)S(1)}, bf16[128,2048]{1,0:T(8,128)(2,1)S(1)}, u32[]{:S(2)}, u32[]{:S(2)}) %collective-permute-start.35) | collective-permute-done | bytes 524320 | tf_op jit(solution)/shard_map/ppermute | solution.py:388
  441.3 8.1 collective-permute-done.39
  466.4 6.7 fusion.3.rest_0_.dn
  473.1 17.0 %scan_forward.3 = (f32[512,1024]{1,0:T(8,128)S(1)}, f32[512,1280]{1,0:T(8,128)}, f32[4,128,1024]{2,1,0:T(8,128)}, f32[128,1024]{1,0:T(8,128)S(1)}, f32[512,8]{1,0:T(8,128)S(1)}) custom-call(s32[1]{0:T(128)} %bitcast.3.f_ref, f32[512,1024]{1,0:T(8,128)} %fusion.118.pz, f32[512,1024]{1,0:T(8,128)} %fusion.119.px, f32[512,272]{1,0:T(8,128)S(1)} %fusion.120.pbd, ...), custom_call_target="tpu_custom_call" | custom-call | tf_op jit(solution)/shard_map/scan_forward/pallas_call | solution.py:286
  499.2 8.7 constant_dynamic-slice_fusion.7
  509.6 5.8 copy.388
  517.9 35.8 %scan_backward.2 = (bf16[512,1024]{1,0:T(8,128)(2,1)S(1)}, bf16[512,1024]{1,0:T(8,128)(2,1)S(1)}, f32[512,256]{1,0:T(8,128)S(1)}, f32[512,16]{1,0:T(8,128)S(1)},...) custom-call(s32[1]{0:T(128)} %bitcast.3.f_ref, ...), custom_call_target="tpu_custom_call" | custom-call | tf_op jit(solution)/shard_map/scan_backward/pallas_call | solution.py:324
  570.3 6.6 convolution_convert_fusion
  576.9 6.7 fusion.113
  600.2 12.6 collective-permute-done.69
  615.1 6.6 reshape.656
  621.7 7.3 copy.359
  633.0 6.2 copy.387
  639.3 5.3 multiply_reduce_fusion.1
  645.1 6.9 add_convert_fusion
  652.0 6.3 copy.386
  671.1 6.6 collective-permute-done.82
  677.7 12.3 collective-permute-done.81
  692.6 8.0 fusion.dn
  700.6 35.7 %scan_backward.3 = (bf16[512,1024]{1,0:T(8,128)(2,1)S(1)}, bf16[512,1024]{1,0:T(8,128)(2,1)S(1)}, f32[512,256]{1,0:T(8,128)S(1)}, f32[512,16]{1,0:T(8,128)S(1)},...) custom-call(s32[1]{0:T(128)} %bitcast.3.f_ref, ...), custom_call_target="tpu_custom_call" | custom-call | tf_op jit(solution)/shard_map/scan_backward/pallas_call | solution.py:324
  742.3 6.6 collective-permute-done.88
  761.7 7.0 collective-permute-done.95
  773.4 6.3 copy.385
  816.3 10.0 dynamic_update_slice.168
  832.0 10.0 dynamic_update_slice.169
  842.0 10.0 dynamic_update_slice.170
  852.0 10.0 dynamic_update_slice.171
  868.6 10.0 dynamic_update_slice.164
  885.1 10.0 dynamic_update_slice.165
  895.1 10.0 dynamic_update_slice.166
  905.1 10.0 dynamic_update_slice.167
  919.8 5.4 collective-permute-start.72
  926.5 5.4 collective-permute-start.71
  949.1 18.1 %collective-permute-start.91 = (bf16[128,2048]{1,0:T(8,128)(2,1)}, bf16[128,2048]{1,0:T(8,128)(2,1)S(1)}, u32[]{:S(2)}, u32[]{:S(2)}) collective-permute-start(bf16[128,2048]{1,0:T(8,128)(2,1)} %get-tuple-element.245), channel_id=1, source_target_pairs={{0,3},{1,2},{2,1},{3,0},{4,7},{5,6},{6,5},{7,4},{8,11},{9,10},{10,... | collective-permute-start | bytes 1572872 | tf_op jit(solution)/shard_map/ppermute | solution.py:388
  967.2 55.5 %collective-permute-start.90 = (bf16[128,2048]{1,0:T(8,128)(2,1)}, bf16[128,2048]{1,0:T(8,128)(2,1)S(1)}, u32[]{:S(2)}, u32[]{:S(2)}) collective-permute-start(bf16[128,2048]{1,0:T(8,128)(2,1)} %get-tuple-element.246), channel_id=1, source_target_pairs={{0,2},{1,3},{2,0},{3,1},{4,6},{5,7},{6,4},{7,5},{8,10},{9,11},{10,... | collective-permute-start | bytes 1572872 | tf_op jit(solution)/shard_map/ppermute | solution.py:388
  1025.3 19.1 %collective-permute-done.90 = bf16[128,2048]{1,0:T(8,128)(2,1)S(1)} collective-permute-done((bf16[128,2048]{1,0:T(8,128)(2,1)}, bf16[128,2048]{1,0:T(8,128)(2,1)S(1)}, u32[]{:S(2)}, u32[]{:S(2)}) %collective-permute-start.90) | collective-permute-done | bytes 524320 | tf_op jit(solution)/shard_map/ppermute | solution.py:388
  1049.3 9.5 collective-permute-start.93
  1058.7 99.7 %all-gather.7.cloned.1.call-done = bf16[4,256,2128]{2,0,1:T(4,128)(2,1)} async-done(((bf16[4,64,2128]{2,0,1:T(4,128)(2,1)}), bf16[4,256,2128]{2,0,1:T(4,128)(2,1)}) %all-gather.7.cloned.1.call-update) | async-done | bytes 4358160 | tf_op jit(solution)/shard_map/all_gather | solution.py:704
  1158.5 8.2 copy.374
  1166.7 78.4 %all-gather.5.cloned.1.call-done = bf16[4,256,2128]{2,0,1:T(4,128)(2,1)} async-done(((bf16[4,64,2128]{2,0,1:T(4,128)(2,1)}), bf16[4,256,2128]{2,0,1:T(4,128)(2,1)}) %all-gather.5.cloned.1.call-update) | async-done | bytes 4358160 | tf_op jit(solution)/shard_map/all_gather | solution.py:704
  1245.1 8.3 copy.373
  1264.7 81.4 %all-gather.11.cloned.1.call-done = bf16[512,2048]{1,0:T(8,128)(2,1)} async-done(((bf16[128,2048]{1,0:T(8,128)(2,1)}), bf16[512,2048]{1,0:T(8,128)(2,1)}) %all-gather.11.cloned.1.call-update) | async-done | bytes 2097168 | tf_op jit(solution)/shard_map/all_gather | solution.py:705
  1346.1 49.3 %all-gather.9.cloned.1.call-done = bf16[512,2048]{1,0:T(8,128)(2,1)} async-done(((bf16[128,2048]{1,0:T(8,128)(2,1)}), bf16[512,2048]{1,0:T(8,128)(2,1)}) %all-gather.9.cloned.1.call-update) | async-done | bytes 2097168 | tf_op jit(solution)/shard_map/all_gather | solution.py:705
  1398.2 85.3 %all-reduce.3.cloned.1.call-done = (f32[28099]{0:T(1024)}, f32[28099]{0:T(1024)}) async-done(((f32[28099]{0:T(1024)}, f32[28099]{0:T(1024)}), (f32[28099]{0:T(1024)}, f32[28099]{0:T(1024)})) %all-reduce.3.cloned.1.call-update) | async-done | bytes 224808 | tf_op jit(solution)/shard_map/psum | solution.py:754
  1506.6 12.4 maximum_convert_fusion
  1519.1 6.9 fusion.90
  1526.0 23.0 %maximum_bitcast_fusion = f32[1,512,8512]{1,2,0:T(8,128)} fusion(f32[512,64]{0,1:T(8,128)S(1)} %bitcast.372, f32[512,256]{0,1:T(8,128)S(1)} %bitcast.339, f32[512,4096]{0,1:T(8,128)S(1)} %bitcast.307, f32[512,4096]{0,1:T(8,128)S(1)} %bitcast.306), kind=kLoop, calls=%fused_computation | loop fusion | flops 13074432 | bytes 34865152 | tf_op jit(solution)/shard_map/broadcast_in_dim | solution.py:802
  (681 shorter events, 436.0 us)
Async XLA Ops:
  8.0 801.7 %reduce-scatter.7.cloned.1.call-start = ((), (), s32[]{:S(2)}) async-start(), calls=%async_computation.6 | async-start | bytes 5570560 | tf_op jit(solution)/shard_map/reduce_scatter | solution.py:663
  13.2 37.2 %collective-permute-start.5 = (bf16[7024]{0:T(1024)(128)(2,1)S(1)}, bf16[7024]{0:T(1024)(128)(2,1)S(1)}, u32[]{:S(2)}, u32[]{:S(2)}) collective-permute-start(bf16[7024]{0:T(1024)(128)(2,1)S(1)} %concatenate.103), channel_id=1, source_target_pairs={{0,1},{1,0},{2,3},{3,2},{4,5},{5,4},{6,7},{7,6},{8,9},{9,8},{10,11... | collective-permute-start | bytes 42152 | tf_op jit(solution)/shard_map/ppermute | solution.py:388
  15.2 36.7 %collective-permute-start.6 = (bf16[7024]{0:T(1024)(128)(2,1)S(1)}, bf16[7024]{0:T(1024)(128)(2,1)S(1)}, u32[]{:S(2)}, u32[]{:S(2)}) collective-permute-start(bf16[7024]{0:T(1024)(128)(2,1)S(1)} %concatenate.103), channel_id=1, source_target_pairs={{0,2},{1,3},{2,0},{3,1},{4,6},{5,7},{6,4},{7,5},{8,10},{9,11},{10,... | collective-permute-start | bytes 42152 | tf_op jit(solution)/shard_map/ppermute | solution.py:388
  16.4 37.1 %collective-permute-start.7 = (bf16[7024]{0:T(1024)(128)(2,1)S(1)}, bf16[7024]{0:T(1024)(128)(2,1)S(1)}, u32[]{:S(2)}, u32[]{:S(2)}) collective-permute-start(bf16[7024]{0:T(1024)(128)(2,1)S(1)} %concatenate.103), channel_id=1, source_target_pairs={{0,3},{1,2},{2,1},{3,0},{4,7},{5,6},{6,5},{7,4},{8,11},{9,10},{10,... | collective-permute-start | bytes 42152 | tf_op jit(solution)/shard_map/ppermute | solution.py:388
  17.3 48.1 %collective-permute-start.1 = (bf16[128,2048]{1,0:T(8,128)(2,1)}, bf16[128,2048]{1,0:T(8,128)(2,1)S(1)}, u32[]{:S(2)}, u32[]{:S(2)}) collective-permute-start(bf16[128,2048]{1,0:T(8,128)(2,1)} %dynamic-slice_bitcast_fusion.1), channel_id=1, source_target_pairs={{0,0},{1,4},{2,8},{3,12},{4,1},{5,5},{6,9},{7,13},{8,2},{9,6},{10,... | collective-permute-start | bytes 1572872 | tf_op jit(solution)/shard_map/ppermute | solution.py:399
  20.2 35.9 %collective-permute-start = (s32[1]{0:T(128)}, s32[1]{0:T(128)}, u32[]{:S(2)}, u32[]{:S(2)}) collective-permute-start(s32[1]{0:T(128)} %bitcast), channel_id=1, source_target_pairs={{0,0},{1,4},{2,8},{3,12},{4,1},{5,5},{6,9},{7,13},{8,2},{9,6},{10,... | collective-permute-start | bytes 20 | tf_op jit(solution)/shard_map/ppermute | solution.py:399
  50.3 110.1 %collective-permute-start.9 = (bf16[512,1024]{1,0:T(8,128)(2,1)}, bf16[512,1024]{1,0:T(8,128)(2,1)}, u32[]{:S(2)}, u32[]{:S(2)}) collective-permute-start(bf16[512,1024]{1,0:T(8,128)(2,1)} %bitcast.12), channel_id=1, source_target_pairs={{0,16},{1,17},{2,18},{3,19},{4,20},{5,21},{6,22},{7,23},{8,24},{9,... | collective-permute-start | bytes 3145736 | tf_op jit(solution)/shard_map/ppermute | solution.py:572
  65.4 49.0 %collective-permute-start.4 = (bf16[128,2048]{1,0:T(8,128)(2,1)S(1)}, bf16[128,2048]{1,0:T(8,128)(2,1)S(1)}, u32[]{:S(2)}, u32[]{:S(2)}) collective-permute-start(bf16[128,2048]{1,0:T(8,128)(2,1)S(1)} %collective-permute-done.1), channel_id=1, source_target_pairs={{0,3},{1,2},{2,1},{3,0},{4,7},{5,6},{6,5},{7,4},{8,11},{9,10},{10,... | collective-permute-start | bytes 1572872 | tf_op jit(solution)/shard_map/ppermute | solution.py:388
  75.4 22.1 %collective-permute-start.27 = (bf16[512,272]{0,1:T(8,128)(2,1)S(1)}, bf16[512,272]{0,1:T(8,128)(2,1)S(1)}, u32[]{:S(2)}, u32[]{:S(2)}) collective-permute-start(bf16[512,272]{0,1:T(8,128)(2,1)S(1)} %collective-permute-done.26), channel_id=1, source_target_pairs={{0,16},{1,17},{2,18},{3,19},{4,20},{5,21},{6,22},{7,23},{8,24},{9,... | collective-permute-start | bytes 835592 | tf_op jit(solution)/shard_map/ppermute | solution.py:572
  76.8 36.0 %collective-permute-start.29 = (bf16[512,272]{0,1:T(8,128)(2,1)}, bf16[512,272]{0,1:T(8,128)(2,1)}, u32[]{:S(2)}, u32[]{:S(2)}) collective-permute-start(bf16[512,272]{0,1:T(8,128)(2,1)} %collective-permute-done.28), channel_id=1, source_target_pairs={{0,16},{1,17},{2,18},{3,19},{4,20},{5,21},{6,22},{7,23},{8,24},{9,... | collective-permute-start | bytes 835592 | tf_op jit(solution)/shard_map/ppermute | solution.py:572
  83.3 34.7 %collective-permute-start.3 = (bf16[128,2048]{1,0:T(8,128)(2,1)S(1)}, bf16[128,2048]{1,0:T(8,128)(2,1)S(1)}, u32[]{:S(2)}, u32[]{:S(2)}) collective-permute-start(bf16[128,2048]{1,0:T(8,128)(2,1)S(1)} %collective-permute-done.1), channel_id=1, source_target_pairs={{0,2},{1,3},{2,0},{3,1},{4,6},{5,7},{6,4},{7,5},{8,10},{9,11},{10,... | collective-permute-start | bytes 1572872 | tf_op jit(solution)/shard_map/ppermute | solution.py:388
  97.5 22.3 %collective-permute-start.2 = (bf16[128,2048]{1,0:T(8,128)(2,1)S(1)}, bf16[128,2048]{1,0:T(8,128)(2,1)S(1)}, u32[]{:S(2)}, u32[]{:S(2)}) collective-permute-start(bf16[128,2048]{1,0:T(8,128)(2,1)S(1)} %collective-permute-done.1), channel_id=1, source_target_pairs={{0,1},{1,0},{2,3},{3,2},{4,5},{5,4},{6,7},{7,6},{8,9},{9,8},{10,11... | collective-permute-start | bytes 1572872 | tf_op jit(solution)/shard_map/ppermute | solution.py:388
  112.8 49.1 %collective-permute-start.10 = (bf16[512,1024]{1,0:T(8,128)(2,1)}, bf16[512,1024]{1,0:T(8,128)(2,1)}, u32[]{:S(2)}, u32[]{:S(2)}) collective-permute-start(bf16[512,1024]{1,0:T(8,128)(2,1)} %bitcast.370), channel_id=1, source_target_pairs={{0,1},{1,0},{2,3},{3,2},{4,5},{5,4},{6,7},{7,6},{8,9},{9,8},{10,11... | collective-permute-start | bytes 3145736 | tf_op jit(solution)/shard_map/ppermute | solution.py:571
  114.4 48.2 %collective-permute-start.12 = (bf16[512,1024]{1,0:T(8,128)(2,1)}, bf16[512,1024]{1,0:T(8,128)(2,1)}, u32[]{:S(2)}, u32[]{:S(2)}) collective-permute-start(bf16[512,1024]{1,0:T(8,128)(2,1)} %bitcast.16), channel_id=1, source_target_pairs={{0,2},{1,3},{2,0},{3,1},{4,6},{5,7},{6,4},{7,5},{8,10},{9,11},{10,... | collective-permute-start | bytes 3145736 | tf_op jit(solution)/shard_map/ppermute | solution.py:571
  118.1 46.6 %collective-permute-start.14 = (bf16[512,1024]{1,0:T(8,128)(2,1)}, bf16[512,1024]{1,0:T(8,128)(2,1)}, u32[]{:S(2)}, u32[]{:S(2)}) collective-permute-start(bf16[512,1024]{1,0:T(8,128)(2,1)} %bitcast.18), channel_id=1, source_target_pairs={{0,3},{1,2},{2,1},{3,0},{4,7},{5,6},{6,5},{7,4},{8,11},{9,10},{10,... | collective-permute-start | bytes 3145736 | tf_op jit(solution)/shard_map/ppermute | solution.py:571
  119.8 45.9 %collective-permute-start.16 = (bf16[512,1024]{1,0:T(8,128)(2,1)S(1)}, bf16[512,1024]{1,0:T(8,128)(2,1)}, u32[]{:S(2)}, u32[]{:S(2)}) collective-permute-start(bf16[512,1024]{1,0:T(8,128)(2,1)S(1)} %bitcast.317), channel_id=1, source_target_pairs={{0,16},{1,17},{2,18},{3,19},{4,20},{5,21},{6,22},{7,23},{8,24},{9,... | collective-permute-start | bytes 3145736 | tf_op jit(solution)/shard_map/ppermute | solution.py:572
  165.7 40.5 %collective-permute-start.13 = (bf16[512,1024]{1,0:T(8,128)(2,1)}, bf16[512,1024]{1,0:T(8,128)(2,1)S(1)}, u32[]{:S(2)}, u32[]{:S(2)}) collective-permute-start(bf16[512,1024]{1,0:T(8,128)(2,1)} %collective-permute-done.12), channel_id=1, source_target_pairs={{0,16},{1,17},{2,18},{3,19},{4,20},{5,21},{6,22},{7,23},{8,24},{9,... | collective-permute-start | bytes 3145736 | tf_op jit(solution)/shard_map/ppermute | solution.py:572
  168.3 39.6 %collective-permute-start.15 = (bf16[512,1024]{1,0:T(8,128)(2,1)}, bf16[512,1024]{1,0:T(8,128)(2,1)S(1)}, u32[]{:S(2)}, u32[]{:S(2)}) collective-permute-start(bf16[512,1024]{1,0:T(8,128)(2,1)} %collective-permute-done.14), channel_id=1, source_target_pairs={{0,16},{1,17},{2,18},{3,19},{4,20},{5,21},{6,22},{7,23},{8,24},{9,... | collective-permute-start | bytes 3145736 | tf_op jit(solution)/shard_map/ppermute | solution.py:572
  172.1 36.2 %collective-permute-start.18 = (bf16[512,1024]{1,0:T(8,128)(2,1)S(1)}, bf16[512,1024]{1,0:T(8,128)(2,1)S(1)}, u32[]{:S(2)}, u32[]{:S(2)}) collective-permute-start(bf16[512,1024]{1,0:T(8,128)(2,1)S(1)} %collective-permute-done.17), channel_id=1, source_target_pairs={{0,16},{1,17},{2,18},{3,19},{4,20},{5,21},{6,22},{7,23},{8,24},{9,... | collective-permute-start | bytes 3145736 | tf_op jit(solution)/shard_map/ppermute | solution.py:572
  178.5 30.4 %collective-permute-start.20 = (bf16[512,1024]{1,0:T(8,128)(2,1)S(1)}, bf16[512,1024]{1,0:T(8,128)(2,1)S(1)}, u32[]{:S(2)}, u32[]{:S(2)}) collective-permute-start(bf16[512,1024]{1,0:T(8,128)(2,1)S(1)} %collective-permute-done.19), channel_id=1, source_target_pairs={{0,16},{1,17},{2,18},{3,19},{4,20},{5,21},{6,22},{7,23},{8,24},{9,... | collective-permute-start | bytes 3145736 | tf_op jit(solution)/shard_map/ppermute | solution.py:572
  180.2 167.5 %collective-permute-start.33 = (bf16[1024,2048]{1,0:T(8,128)(2,1)}, bf16[1024,2048]{1,0:T(8,128)(2,1)}, u32[]{:S(2)}, u32[]{:S(2)}) collective-permute-start(bf16[1024,2048]{1,0:T(8,128)(2,1)} %bitcast.44), channel_id=1, source_target_pairs={{0,16},{16,0},{1,17},{17,1},{2,18},{18,2},{3,19},{19,3},{4,20},{20... | collective-permute-start | bytes 12582920 | tf_op jit(solution)/shard_map/ppermute | solution.py:383
  239.7 28.3 %collective-permute-start.54 = (bf16[512,272]{0,1:T(8,128)(2,1)}, bf16[512,272]{0,1:T(8,128)(2,1)}, u32[]{:S(2)}, u32[]{:S(2)}) collective-permute-start(bf16[512,272]{0,1:T(8,128)(2,1)} %pad_maximum_fusion.5), channel_id=1, source_target_pairs={{16,0},{17,1},{18,2},{19,3},{20,4},{21,5},{22,6},{23,7},{24,8},{25... | collective-permute-start | bytes 835592 | tf_op jit(solution)/shard_map/ppermute | solution.py:572
  251.5 32.6 %collective-permute-start.59 = (bf16[512,272]{0,1:T(8,128)(2,1)}, bf16[512,272]{0,1:T(8,128)(2,1)}, u32[]{:S(2)}, u32[]{:S(2)}) collective-permute-start(bf16[512,272]{0,1:T(8,128)(2,1)} %get-tuple-element.85), channel_id=1, source_target_pairs={{16,19},{17,18},{18,17},{19,16},{20,23},{21,22},{22,21},{23,20},{2... | collective-permute-start | bytes 835592 | tf_op jit(solution)/shard_map/ppermute | solution.py:571
  260.7 26.5 %collective-permute-start.56 = (bf16[512,272]{0,1:T(8,128)(2,1)}, bf16[512,272]{0,1:T(8,128)(2,1)}, u32[]{:S(2)}, u32[]{:S(2)}) collective-permute-start(bf16[512,272]{0,1:T(8,128)(2,1)} %collective-permute-done.55), channel_id=1, source_target_pairs={{16,0},{17,1},{18,2},{19,3},{20,4},{21,5},{22,6},{23,7},{24,8},{25... | collective-permute-start | bytes 835592 | tf_op jit(solution)/shard_map/ppermute | solution.py:572
  262.7 26.8 %collective-permute-start.58 = (bf16[512,272]{0,1:T(8,128)(2,1)}, bf16[512,272]{0,1:T(8,128)(2,1)}, u32[]{:S(2)}, u32[]{:S(2)}) collective-permute-start(bf16[512,272]{0,1:T(8,128)(2,1)} %collective-permute-done.57), channel_id=1, source_target_pairs={{16,0},{17,1},{18,2},{19,3},{20,4},{21,5},{22,6},{23,7},{24,8},{25... | collective-permute-start | bytes 835592 | tf_op jit(solution)/shard_map/ppermute | solution.py:572
  268.0 65.9 %collective-permute-start.40 = (bf16[512,1024]{1,0:T(8,128)(2,1)}, bf16[512,1024]{1,0:T(8,128)(2,1)}, u32[]{:S(2)}, u32[]{:S(2)}) collective-permute-start(bf16[512,1024]{1,0:T(8,128)(2,1)} %bitcast.12), channel_id=1, source_target_pairs={{16,0},{17,1},{18,2},{19,3},{20,4},{21,5},{22,6},{23,7},{24,8},{25... | collective-permute-start | bytes 3145736 | tf_op jit(solution)/shard_map/ppermute | solution.py:572
  284.1 55.4 %collective-permute-start.41 = (bf16[512,1024]{1,0:T(8,128)(2,1)}, bf16[512,1024]{1,0:T(8,128)(2,1)}, u32[]{:S(2)}, u32[]{:S(2)}) collective-permute-start(bf16[512,1024]{1,0:T(8,128)(2,1)} %bitcast.371), channel_id=1, source_target_pairs={{16,17},{17,16},{18,19},{19,18},{20,21},{21,20},{22,23},{23,22},{2... | collective-permute-start | bytes 3145736 | tf_op jit(solution)/shard_map/ppermute | solution.py:571
  287.2 55.4 %collective-permute-start.47 = (bf16[512,1024]{1,0:T(8,128)(2,1)S(1)}, bf16[512,1024]{1,0:T(8,128)(2,1)}, u32[]{:S(2)}, u32[]{:S(2)}) collective-permute-start(bf16[512,1024]{1,0:T(8,128)(2,1)S(1)} %bitcast.318), channel_id=1, source_target_pairs={{16,0},{17,1},{18,2},{19,3},{20,4},{21,5},{22,6},{23,7},{24,8},{25... | collective-permute-start | bytes 3145736 | tf_op jit(solution)/shard_map/ppermute | solution.py:572
  294.5 50.5 %collective-permute-start.43 = (bf16[512,1024]{1,0:T(8,128)(2,1)}, bf16[512,1024]{1,0:T(8,128)(2,1)}, u32[]{:S(2)}, u32[]{:S(2)}) collective-permute-start(bf16[512,1024]{1,0:T(8,128)(2,1)} %bitcast.16), channel_id=1, source_target_pairs={{16,18},{17,19},{18,16},{19,17},{20,22},{21,23},{22,20},{23,21},{2... | collective-permute-start | bytes 3145736 | tf_op jit(solution)/shard_map/ppermute | solution.py:571
  339.6 48.3 %collective-permute-start.48 = (bf16[512,1024]{1,0:T(8,128)(2,1)S(1)}, bf16[512,1024]{1,0:T(8,128)(2,1)S(1)}, u32[]{:S(2)}, u32[]{:S(2)}) collective-permute-start(bf16[512,1024]{1,0:T(8,128)(2,1)S(1)} %bitcast.369), channel_id=1, source_target_pairs={{16,17},{17,16},{18,19},{19,18},{20,21},{21,20},{22,23},{23,22},{2... | collective-permute-start | bytes 3145736 | tf_op jit(solution)/shard_map/ppermute | solution.py:571
  345.8 44.0 %collective-permute-start.50 = (bf16[512,1024]{1,0:T(8,128)(2,1)S(1)}, bf16[512,1024]{1,0:T(8,128)(2,1)S(1)}, u32[]{:S(2)}, u32[]{:S(2)}) collective-permute-start(bf16[512,1024]{1,0:T(8,128)(2,1)S(1)} %bitcast.367), channel_id=1, source_target_pairs={{16,18},{17,19},{18,16},{19,17},{20,22},{21,23},{22,20},{23,21},{2... | collective-permute-start | bytes 3145736 | tf_op jit(solution)/shard_map/ppermute | solution.py:571
  347.7 43.5 %collective-permute-start.44 = (bf16[512,1024]{1,0:T(8,128)(2,1)}, bf16[512,1024]{1,0:T(8,128)(2,1)S(1)}, u32[]{:S(2)}, u32[]{:S(2)}) collective-permute-start(bf16[512,1024]{1,0:T(8,128)(2,1)} %collective-permute-done.43), channel_id=1, source_target_pairs={{16,0},{17,1},{18,2},{19,3},{20,4},{21,5},{22,6},{23,7},{24,8},{25... | collective-permute-start | bytes 3145736 | tf_op jit(solution)/shard_map/ppermute | solution.py:572
  355.0 59.4 %collective-permute-start.61 = (bf16[128,2048]{1,0:T(8,128)(2,1)S(1)}, bf16[128,2048]{1,0:T(8,128)(2,1)S(1)}, u32[]{:S(2)}, u32[]{:S(2)}) collective-permute-start(bf16[128,2048]{1,0:T(8,128)(2,1)S(1)} %copy-done.72), channel_id=1, source_target_pairs={{0,0},{1,4},{2,8},{3,12},{4,1},{5,5},{6,9},{7,13},{8,2},{9,6},{10,... | collective-permute-start | bytes 1572872 | tf_op jit(solution)/shard_map/ppermute | solution.py:399
  355.8 38.6 %collective-permute-start.46 = (bf16[512,1024]{1,0:T(8,128)(2,1)S(1)}, bf16[512,1024]{1,0:T(8,128)(2,1)S(1)}, u32[]{:S(2)}, u32[]{:S(2)}) collective-permute-start(bf16[512,1024]{1,0:T(8,128)(2,1)S(1)} %collective-permute-done.45), channel_id=1, source_target_pairs={{16,0},{17,1},{18,2},{19,3},{20,4},{21,5},{22,6},{23,7},{24,8},{25... | collective-permute-start | bytes 3145736 | tf_op jit(solution)/shard_map/ppermute | solution.py:572
  394.4 22.3 %collective-permute-start.36 = (bf16[128,2048]{1,0:T(8,128)(2,1)S(1)}, bf16[128,2048]{1,0:T(8,128)(2,1)S(1)}, u32[]{:S(2)}, u32[]{:S(2)}) collective-permute-start(bf16[128,2048]{1,0:T(8,128)(2,1)S(1)} %get-tuple-element.254), channel_id=1, source_target_pairs={{0,3},{1,2},{2,1},{3,0},{4,7},{5,6},{6,5},{7,4},{8,11},{9,10},{10,... | collective-permute-start | bytes 1572872 | tf_op jit(solution)/shard_map/ppermute | solution.py:388
  409.1 23.5 %collective-permute-start.35 = (bf16[128,2048]{1,0:T(8,128)(2,1)S(1)}, bf16[128,2048]{1,0:T(8,128)(2,1)S(1)}, u32[]{:S(2)}, u32[]{:S(2)}) collective-permute-start(bf16[128,2048]{1,0:T(8,128)(2,1)S(1)} %get-tuple-element.255), channel_id=1, source_target_pairs={{0,2},{1,3},{2,0},{3,1},{4,6},{5,7},{6,4},{7,5},{8,10},{9,11},{10,... | collective-permute-start | bytes 1572872 | tf_op jit(solution)/shard_map/ppermute | solution.py:388
  412.4 25.5 %collective-permute-start.53 = (bf16[512,1024]{1,0:T(8,128)(2,1)S(1)}, bf16[512,1024]{1,0:T(8,128)(2,1)S(1)}, u32[]{:S(2)}, u32[]{:S(2)}) collective-permute-start(bf16[512,1024]{1,0:T(8,128)(2,1)S(1)} %collective-permute-done.52), channel_id=1, source_target_pairs={{16,0},{17,1},{18,2},{19,3},{20,4},{21,5},{22,6},{23,7},{24,8},{25... | collective-permute-start | bytes 3145736 | tf_op jit(solution)/shard_map/ppermute | solution.py:572
  438.3 25.5 %collective-permute-start.64 = (bf16[128,2048]{1,0:T(8,128)(2,1)S(1)}, bf16[128,2048]{1,0:T(8,128)(2,1)S(1)}, u32[]{:S(2)}, u32[]{:S(2)}) collective-permute-start(bf16[128,2048]{1,0:T(8,128)(2,1)S(1)} %get-tuple-element.344), channel_id=1, source_target_pairs={{0,3},{1,2},{2,1},{3,0},{4,7},{5,6},{6,5},{7,4},{8,11},{9,10},{10,... | collective-permute-start | bytes 1572872 | tf_op jit(solution)/shard_map/ppermute | solution.py:388
  439.6 26.5 %collective-permute-start.63 = (bf16[128,2048]{1,0:T(8,128)(2,1)S(1)}, bf16[128,2048]{1,0:T(8,128)(2,1)S(1)}, u32[]{:S(2)}, u32[]{:S(2)}) collective-permute-start(bf16[128,2048]{1,0:T(8,128)(2,1)S(1)} %get-tuple-element.344), channel_id=1, source_target_pairs={{0,2},{1,3},{2,0},{3,1},{4,6},{5,7},{6,4},{7,5},{8,10},{9,11},{10,... | collective-permute-start | bytes 1572872 | tf_op jit(solution)/shard_map/ppermute | solution.py:388
  491.6 23.9 %collective-permute-start.67 = (f32[4,128,2]{1,0,2:T(4,128)S(1)}, f32[4,128,2]{1,0,2:T(4,128)S(1)}, u32[]{:S(2)}, u32[]{:S(2)}) collective-permute-start(f32[4,128,2]{1,0,2:T(4,128)S(1)} %copy.350), channel_id=1, source_target_pairs={{0,3},{1,2},{2,1},{3,0},{4,7},{5,6},{6,5},{7,4},{8,11},{9,10},{10,... | collective-permute-start | bytes 12296 | tf_op jit(solution)/shard_map/ppermute | solution.py:388
  576.9 68.2 %collective-permute-start.99 = (bf16[1024,2128]{0,1:T(8,128)(2,1)}, bf16[1024,2128]{0,1:T(8,128)(2,1)}, u32[]{:S(2)}, u32[]{:S(2)}) collective-permute-start(bf16[1024,2128]{0,1:T(8,128)(2,1)} %convolution_convert_fusion), channel_id=1, source_target_pairs={{0,16},{16,0},{1,17},{17,1},{2,18},{18,2},{3,19},{19,3},{4,20},{20... | collective-permute-start | bytes 13074440 | tf_op jit(solution)/shard_map/ppermute | solution.py:383
  586.3 26.5 %collective-permute-start.69 = (bf16[128,2048]{1,0:T(8,128)(2,1)S(1)}, bf16[128,2048]{1,0:T(8,128)(2,1)}, u32[]{:S(2)}, u32[]{:S(2)}) collective-permute-start(bf16[128,2048]{1,0:T(8,128)(2,1)S(1)} %get-tuple-element.249), channel_id=1, source_target_pairs={{0,2},{1,3},{2,0},{3,1},{4,6},{5,7},{6,4},{7,5},{8,10},{9,11},{10,... | collective-permute-start | bytes 1572872 | tf_op jit(solution)/shard_map/ppermute | solution.py:388
  587.2 52.0 %collective-permute-start.68 = (bf16[128,2048]{1,0:T(8,128)(2,1)}, bf16[128,2048]{1,0:T(8,128)(2,1)}, u32[]{:S(2)}, u32[]{:S(2)}) collective-permute-start(bf16[128,2048]{1,0:T(8,128)(2,1)} %get-tuple-element.247), channel_id=1, source_target_pairs={{0,1},{1,0},{2,3},{3,2},{4,5},{5,4},{6,7},{7,6},{8,9},{9,8},{10,11... | collective-permute-start | bytes 1572872 | tf_op jit(solution)/shard_map/ppermute | solution.py:388
  597.6 41.7 %collective-permute-start.79 = (bf16[128,2048]{1,0:T(8,128)(2,1)}, bf16[128,2048]{1,0:T(8,128)(2,1)}, u32[]{:S(2)}, u32[]{:S(2)}) collective-permute-start(bf16[128,2048]{1,0:T(8,128)(2,1)} %get-tuple-element.251), channel_id=1, source_target_pairs={{0,3},{1,2},{2,1},{3,0},{4,7},{5,6},{6,5},{7,4},{8,11},{9,10},{10,... | collective-permute-start | bytes 1572872 | tf_op jit(solution)/shard_map/ppermute | solution.py:388
  599.3 40.0 %collective-permute-start.78 = (bf16[128,2048]{1,0:T(8,128)(2,1)}, bf16[128,2048]{1,0:T(8,128)(2,1)}, u32[]{:S(2)}, u32[]{:S(2)}) collective-permute-start(bf16[128,2048]{1,0:T(8,128)(2,1)} %get-tuple-element.252), channel_id=1, source_target_pairs={{0,2},{1,3},{2,0},{3,1},{4,6},{5,7},{6,4},{7,5},{8,10},{9,11},{10,... | collective-permute-start | bytes 1572872 | tf_op jit(solution)/shard_map/ppermute | solution.py:388
  612.8 26.5 %collective-permute-start.77 = (bf16[128,2048]{1,0:T(8,128)(2,1)}, bf16[128,2048]{1,0:T(8,128)(2,1)}, u32[]{:S(2)}, u32[]{:S(2)}) collective-permute-start(bf16[128,2048]{1,0:T(8,128)(2,1)} %get-tuple-element.250), channel_id=1, source_target_pairs={{0,1},{1,0},{2,3},{3,2},{4,5},{5,4},{6,7},{7,6},{8,9},{9,8},{10,11... | collective-permute-start | bytes 1572872 | tf_op jit(solution)/shard_map/ppermute | solution.py:388
  658.3 203.8 %reduce-scatter.5.cloned.1.call-start = ((), (), s32[]{:S(2)}) async-start(), calls=%async_computation.4 | async-start | bytes 5570560 | tf_op jit(solution)/shard_map/reduce_scatter | solution.py:663
  779.7 137.6 %reduce-scatter.11.cloned.1.call-start = ((), (), s32[]{:S(2)}) async-start(), calls=%async_computation.10 | async-start | bytes 2621440 | tf_op jit(solution)/shard_map/reduce_scatter | solution.py:663
  794.5 228.2 %reduce-scatter.9.cloned.1.call-start = ((), (), s32[]{:S(2)}) async-start(), calls=%async_computation.8 | async-start | bytes 2621440 | tf_op jit(solution)/shard_map/reduce_scatter | solution.py:663
  809.6 348.8 %all-gather.7.cloned.1.call-start = ((), (), s32[]{:S(2)}) async-start(), calls=%async_computation.7 | async-start | bytes 5570560 | tf_op jit(solution)/shard_map/all_gather | solution.py:704
  862.0 383.1 %all-gather.5.cloned.1.call-start = ((), (), s32[]{:S(2)}) async-start(), calls=%async_computation.5 | async-start | bytes 5570560 | tf_op jit(solution)/shard_map/all_gather | solution.py:704
  915.2 431.0 %all-gather.11.cloned.1.call-start = ((), (), s32[]{:S(2)}) async-start(), calls=%async_computation.11 | async-start | bytes 2621440 | tf_op jit(solution)/shard_map/all_gather | solution.py:705
  917.3 478.1 %all-gather.9.cloned.1.call-start = ((), (), s32[]{:S(2)}) async-start(), calls=%async_computation.9 | async-start | bytes 2621440 | tf_op jit(solution)/shard_map/all_gather | solution.py:705
  926.5 97.5 %collective-permute-start.71 = (bf16[128,2048]{1,0:T(8,128)(2,1)}, bf16[128,2048]{1,0:T(8,128)(2,1)}, u32[]{:S(2)}, u32[]{:S(2)}) collective-permute-start(bf16[128,2048]{1,0:T(8,128)(2,1)} %get-tuple-element.256), channel_id=1, source_target_pairs={{0,0},{1,4},{2,8},{3,12},{4,1},{5,5},{6,9},{7,13},{8,2},{9,6},{10,... | collective-permute-start | bytes 1572872 | tf_op jit(solution)/shard_map/ppermute | solution.py:399
  934.6 89.5 %collective-permute-start.73 = (bf16[128,2048]{1,0:T(8,128)(2,1)}, bf16[128,2048]{1,0:T(8,128)(2,1)}, u32[]{:S(2)}, u32[]{:S(2)}) collective-permute-start(bf16[128,2048]{1,0:T(8,128)(2,1)} %collective-permute-done.72), channel_id=1, source_target_pairs={{0,16},{16,0},{1,17},{17,1},{2,18},{18,2},{3,19},{19,3},{4,20},{20... | collective-permute-start | bytes 1572872 | tf_op jit(solution)/shard_map/ppermute | solution.py:383
  949.1 76.3 %collective-permute-start.91 = (bf16[128,2048]{1,0:T(8,128)(2,1)}, bf16[128,2048]{1,0:T(8,128)(2,1)S(1)}, u32[]{:S(2)}, u32[]{:S(2)}) collective-permute-start(bf16[128,2048]{1,0:T(8,128)(2,1)} %get-tuple-element.245), channel_id=1, source_target_pairs={{0,3},{1,2},{2,1},{3,0},{4,7},{5,6},{6,5},{7,4},{8,11},{9,10},{10,... | collective-permute-start | bytes 1572872 | tf_op jit(solution)/shard_map/ppermute | solution.py:388
  967.2 77.3 %collective-permute-start.90 = (bf16[128,2048]{1,0:T(8,128)(2,1)}, bf16[128,2048]{1,0:T(8,128)(2,1)S(1)}, u32[]{:S(2)}, u32[]{:S(2)}) collective-permute-start(bf16[128,2048]{1,0:T(8,128)(2,1)} %get-tuple-element.246), channel_id=1, source_target_pairs={{0,2},{1,3},{2,0},{3,1},{4,6},{5,7},{6,4},{7,5},{8,10},{9,11},{10,... | collective-permute-start | bytes 1572872 | tf_op jit(solution)/shard_map/ppermute | solution.py:388
  1022.7 22.7 %collective-permute-start.89 = (bf16[128,2048]{1,0:T(8,128)(2,1)}, bf16[128,2048]{1,0:T(8,128)(2,1)}, u32[]{:S(2)}, u32[]{:S(2)}) collective-permute-start(bf16[128,2048]{1,0:T(8,128)(2,1)} %get-tuple-element.244), channel_id=1, source_target_pairs={{0,1},{1,0},{2,3},{3,2},{4,5},{5,4},{6,7},{7,6},{8,9},{9,8},{10,11... | collective-permute-start | bytes 1572872 | tf_op jit(solution)/shard_map/ppermute | solution.py:388
  1022.7 460.7 %all-reduce.3.cloned.1.call-start = ((), (), s32[]{:S(2)}) async-start(), calls=%async_computation.12 | async-start | bytes 458752 | tf_op jit(solution)/shard_map/psum | solution.py:754
  1049.3 215.3 %collective-permute-start.93 = (f32[128,2048]{1,0:T(8,128)}, f32[128,2048]{1,0:T(8,128)}, u32[]{:S(2)}, u32[]{:S(2)}) collective-permute-start(f32[128,2048]{1,0:T(8,128)} %get-tuple-element.237), channel_id=1, source_target_pairs={{0,0},{1,4},{2,8},{3,12},{4,1},{5,5},{6,9},{7,13},{8,2},{9,6},{10,... | collective-permute-start | bytes 3145736 | tf_op jit(solution)/shard_map/ppermute | solution.py:399
  1258.3 242.2 %collective-permute-start.103 = (bf16[4,256,2128]{1,2,0:T(8,128)(2,1)}, bf16[4,256,2128]{1,2,0:T(8,128)(2,1)}, u32[]{:S(2)}, u32[]{:S(2)}) collective-permute-start(bf16[4,256,2128]{1,2,0:T(8,128)(2,1)} %broadcast_select_fusion.2), channel_id=1, source_target_pairs={{0,16},{16,0},{1,17},{17,1},{2,18},{18,2},{3,19},{19,3},{4,20},{20... | collective-permute-start | bytes 13074440 | tf_op jit(solution)/shard_map/ppermute | solution.py:383
  1259.9 229.7 %collective-permute-start.92 = (f32[128,2048]{1,0:T(8,128)}, f32[128,2048]{1,0:T(8,128)S(1)}, u32[]{:S(2)}, u32[]{:S(2)}) collective-permute-start(f32[128,2048]{1,0:T(8,128)} %get-tuple-element.236), channel_id=1, source_target_pairs={{0,0},{1,4},{2,8},{3,12},{4,1},{5,5},{6,9},{7,13},{8,2},{9,6},{10,... | collective-permute-start | bytes 3145736 | tf_op jit(solution)/shard_map/ppermute | solution.py:399
  1264.6 225.0 %collective-permute-start.94 = (f32[128,2048]{1,0:T(8,128)}, f32[128,2048]{1,0:T(8,128)}, u32[]{:S(2)}, u32[]{:S(2)}) collective-permute-start(f32[128,2048]{1,0:T(8,128)} %collective-permute-done.93), channel_id=1, source_target_pairs={{0,16},{16,0},{1,17},{17,1},{2,18},{18,2},{3,19},{19,3},{4,20},{20... | collective-permute-start | bytes 3145736 | tf_op jit(solution)/shard_map/ppermute | solution.py:383
  1397.2 95.3 %collective-permute-start.106 = (bf16[512,2048]{1,0:T(8,128)(2,1)S(1)}, bf16[512,2048]{1,0:T(8,128)(2,1)}, u32[]{:S(2)}, u32[]{:S(2)}) collective-permute-start(bf16[512,2048]{1,0:T(8,128)(2,1)S(1)} %broadcast_select_fusion.6), channel_id=1, source_target_pairs={{0,16},{16,0},{1,17},{17,1},{2,18},{18,2},{3,19},{19,3},{4,20},{20... | collective-permute-start | bytes 6291464 | tf_op jit(solution)/shard_map/ppermute | solution.py:383
  (147 other events, 2220.4 us)
Sparse Core Ops, SparseCore 0:
  658.4 89.0 reduce-scatter.6
  779.8 81.4 reduce-scatter.4
  864.3 44.1 reduce-scatter.10
  910.7 99.9 reduce-scatter.8
  1012.1 146.3 all-gather.6
  1159.9 85.2 all-gather.4
  1246.7 99.3 all-gather.10
  1347.7 47.6 all-gather.8
Sparse Core Ops, SparseCore 1:
  1264.7 218.7 all-reduce.2

commit v2 on v1

--- a/solution.py
+++ b/solution.py
@@ -53,20 +53,20 @@
     return one(hi) + one(mid) + one(low)
 
 
-def forward_kernel(f_ref, pz, px, pbd, cw, hp, table, s0, e0, *rest, second):
+def forward_kernel(f_ref, pzx, pbd, cw, hp, table, s0, e0, *rest, second):
     if second:
         dn, gain, y_ref, filt_ref, st_ref, fin_ref, stat_ref, state, xp, xw_s = rest
     else:
         y_ref, filt_ref, st_ref, fin_ref, stat_ref, state, xp, xw_s = rest
     i = pl.program_id(0)
-    rows, width = px.shape
+    rows, width = y_ref.shape
 
     @pl.when(i == 0)
     def _():
         state[...] = s0[...]
         xp[0:8, :] = e0[...]
 
-    xp[8 : 8 + rows, :width] = px[...]
+    xp[8 : 8 + rows, :width] = pzx[:, width:]
     xp[8 : 8 + rows, width:] = pbd[:, :GROUP]
 
     def conv_tile(lo):
@@ -110,7 +110,7 @@
         )
         y_ref[:, here] = y
         xw_s[:, here] = x * w_e[:, here]
-        z = pz[:, here]
+        z = pzx[:, here]
         g = y * z * jax.nn.sigmoid(z)
         ss = ss + g * g
         if second:
@@ -118,14 +118,14 @@
     state[...] = state[...] * last_e[0:1, :] + dot32(b_c, xw_s[...], 0, 0)
     fin_ref[...] = state[...]
     xp[0:8, :] = xp[rows : rows + 8, :]
-    stat_ref[:, 0:1] = jnp.sum(ss, axis=1, keepdims=True)
-    stat_ref[:, 1:2] = jnp.sum(s2, axis=1, keepdims=True)
+    ones = jnp.ones((8, LANES), F32)
+    stat_ref[0, 0:1, :] = dot32(ones, ss, 1, 1)[0:1]
+    stat_ref[0, 1:2, :] = dot32(ones, s2, 1, 1)[0:1]
 
 
 def backward_kernel(
     f_ref,
-    pz,
-    px,
+    pzx,
     pbd,
     y_ref,
     filt,
@@ -139,8 +139,7 @@
     gain,
     g0,
     e0,
-    dz_ref,
-    dx_ref,
+    dzx_ref,
     dbc_ref,
     ddt_ref,
     dgain_ref,
@@ -156,7 +155,7 @@
     rowv,
 ):
     i = pl.program_id(0)
-    rows, width = px.shape
+    rows, width = y_ref.shape
     heads = hp.shape[1]
 
     @pl.when(i == 0)
@@ -188,13 +187,14 @@
     lane = lax.broadcasted_iota(jnp.int32, (rows, LANES), 1)
     first = lane < HEAD_DIM
     dcb_t = jnp.zeros((rows, rows), F32)
-    r = rc[:, 0:1]
-    coef = rc[:, 1:2]
+    rc_t = dot32((row == col).astype(F32), rc[0], 1, 1)
+    r = rc_t[:, 0:1]
+    coef = rc_t[:, 1:2]
     rowv[0:1, :] = jnp.sum(grad[...] * st_out[0], axis=0, keepdims=True)
     for j in range(width // LANES):
         lo = j * LANES
         here = slice(lo, lo + LANES)
-        z = pz[:, here]
+        z = pzx[:, here]
         y = y_ref[:, here]
         sz, dsz = silu_pair(z)
         g = y * sz
@@ -202,7 +202,7 @@
         dg = dnt * gain[0:1, here] * r - g * coef
         dgain_ref[0:1, here] += jnp.sum(dnt * g * r, axis=0, keepdims=True)
         dy = dg * sz
-        dz_ref[:, here] = (dg * y * dsz).astype(BF16)
+        dzx_ref[:, here] = (dg * y * dsz).astype(BF16)
         x, xder = silu_pair(filt[:, here])
         xd = x * dt_e[:, here]
         parts = []
@@ -245,7 +245,7 @@
 
     for lo in range(0, width + GROUP, LANES):
         here = slice(lo, lo + LANES)
-        src = px[:, here] if lo < width else pbd[:, lo - width : lo - width + LANES]
+        src = pzx[:, width + lo : width + lo + LANES] if lo < width else pbd[:, lo - width : lo - width + LANES]
         total = jnp.zeros((rows, LANES), F32)
         for k in range(KERNEL):
             shift = KERNEL - 1 - k
@@ -254,7 +254,7 @@
             dconv_ref[k : k + 1, here] += jnp.sum(src * moved, axis=0, keepdims=True)
         dconv_ref[4:5, here] += jnp.sum(dfp[0:rows, here], axis=0, keepdims=True)
         if lo < width:
-            dx_ref[:, here] = total.astype(BF16)
+            dzx_ref[:, width + lo : width + lo + LANES] = total.astype(BF16)
         else:
             dbc_ref[:, lo - width : lo - width + LANES] = total
     dfp[rows : rows + 8, :] = dfp[0:8, :]
@@ -265,14 +265,13 @@
     return pl.BlockSpec(shape, lambda i, f: (0,) * len(shape))
 
 
-def run_forward(f, pz, px, pbd, cw, hp, table, s0, e0, extra, rows):
-    total, width = px.shape
+def run_forward(f, pzx, pbd, cw, hp, table, s0, e0, extra, rows):
+    total, width = pzx.shape[0], pzx.shape[1] // 2
     heads = hp.shape[1]
     count = total // rows
     block = lambda w: pl.BlockSpec((rows, w), lambda i, f: (jnp.bitwise_xor(i, f[0]), 0))
     in_specs = [
-        block(width),
-        block(width),
+        block(2 * width),
         block(GROUP + heads),
         whole((8, width + GROUP)),
         whole((8, heads)),
@@ -294,7 +293,7 @@
                 block(width + GROUP),
                 pl.BlockSpec((1, STATE, width), lambda i, f: (i, 0, 0)),
                 whole((STATE, width)),
-                block(8),
+                pl.BlockSpec((1, 8, rows), lambda i, f: (jnp.bitwise_xor(i, f[0]), 0, 0)),
             ],
             scratch_shapes=[
                 pltpu.VMEM((STATE, width), F32),
@@ -307,15 +306,15 @@
             shape((total, width + GROUP), F32),
             shape((count, STATE, width), F32),
             shape((STATE, width), F32),
-            shape((total, 8), F32),
+            shape((count, 8, rows), F32),
         ],
         compiler_params=pltpu.CompilerParams(vmem_limit_bytes=VMEM_BYTES),
         name="scan_forward",
-    )(f, pz, px, pbd, cw, hp, table, s0, e0, *extra)
-
-
-def run_backward(f, pz, px, pbd, y, filt, dn, rc, states, cw, hp, table, gain, g0, e0, rows):
-    total, width = px.shape
+    )(f, pzx, pbd, cw, hp, table, s0, e0, *extra)
+
+
+def run_backward(f, pzx, pbd, y, filt, dn, rc, states, cw, hp, table, gain, g0, e0, rows):
+    total, width = pzx.shape[0], pzx.shape[1] // 2
     heads = hp.shape[1]
     count = total // rows
     turn = lambda i: count - 1 - i
@@ -327,13 +326,12 @@
             num_scalar_prefetch=1,
             grid=(count,),
             in_specs=[
-                block(width),
-                block(width),
+                block(2 * width),
                 block(GROUP + heads),
                 block(width),
                 block(width + GROUP),
                 block(width),
-                block(8),
+                pl.BlockSpec((1, 8, rows), lambda i, f: (jnp.bitwise_xor(turn(i), f[0]), 0, 0)),
                 pl.BlockSpec((1, STATE, width), lambda i, f: (turn(i), 0, 0)),
                 pl.BlockSpec((1, STATE, width), lambda i, f: (turn(i) + 1, 0, 0)),
                 whole((8, width + GROUP)),
@@ -344,8 +342,7 @@
                 whole((8, width + GROUP)),
             ],
             out_specs=[
-                block(width),
-                block(width),
+                block(2 * width),
                 block(GROUP),
                 block(heads),
                 whole((8, width)),
@@ -364,8 +361,7 @@
             ],
         ),
         out_shape=[
-            shape((total, width), BF16),
-            shape((total, width), BF16),
+            shape((total, 2 * width), BF16),
             shape((total, GROUP), F32),
             shape((total, heads), F32),
             shape((8, width), F32),
@@ -376,7 +372,58 @@
         ],
         compiler_params=pltpu.CompilerParams(vmem_limit_bytes=VMEM_BYTES),
         name="scan_backward",
-    )(f, pz, px, pbd, y, filt, dn, rc, states, states, cw, hp, table, gain, g0, e0)
+    )(f, pzx, pbd, y, filt, dn, rc, states, states, cw, hp, table, gain, g0, e0)
+
+
+def place_kernel(ids, *refs, plan, small):
+    out = refs[-1]
+    h, j = pl.program_id(0), pl.program_id(1)
+    core = ids[1]
+    for ref, (side, layer, first, size) in zip(refs, plan):
+
+        @pl.when((h == side) & (core == layer) & (j >= first) & (j < first + size))
+        def _():
+            v = ref[...]
+            out[...] = v.reshape(out.shape).astype(F32)
+
+    if small:
+
+        @pl.when(j == pl.num_programs(1) - 1)
+        def _():
+            v = refs[len(plan)]
+            out[:, : v.shape[2]] = v[0]
+
+
+def place_blocks(ids, chunks, small, out_shape, block, out_index, steps):
+    def step_of(side, layer, first, size, index):
+        def where(h, j, ids):
+            used = jnp.logical_and(h == side, ids[1] == layer)
+            return index(jnp.where(used, jnp.clip(j - first, 0, size - 1), 0))
+
+        return where
+
+    in_specs = [
+        pl.BlockSpec(shape, step_of(side, layer, first, size, index))
+        for _, side, layer, first, size, shape, index in chunks
+    ]
+    args = [c[0] for c in chunks]
+    if small is not None:
+        in_specs.append(pl.BlockSpec((1,) + small.shape[1:], lambda h, j, ids: (h, 0, 0)))
+        args.append(small)
+    return pl.pallas_call(
+        functools.partial(
+            place_kernel, plan=tuple(c[1:5] for c in chunks), small=small is not None
+        ),
+        grid_spec=pltpu.PrefetchScalarGridSpec(
+            num_scalar_prefetch=1,
+            grid=(2, steps),
+            in_specs=in_specs,
+            out_specs=pl.BlockSpec(block, out_index),
+        ),
+        out_shape=jax.ShapeDtypeStruct(out_shape, F32),
+        compiler_params=pltpu.CompilerParams(vmem_limit_bytes=VMEM_BYTES),
+        name="place_gradient",
+    )(ids, *args)
 
 
 def swap_section(v):
@@ -399,25 +446,60 @@
     return lax.ppermute(v, ("seq", "fsdp"), pairs)
 
 
-def gather_blocks(v):
+def to_local(v):
+    n, f, c = lax.axis_size("fsdp"), lax.axis_index("fsdp"), lax.axis_index("section")
+    size = v.shape[-1] // (2 * n)
+    return jnp.concatenate(
+        [
+            lax.dynamic_slice_in_dim(v, ((f ^ m) * 2 + (c ^ t)) * size, size, v.ndim - 1)
+            for t in range(2)
+            for m in range(n)
+        ],
+        axis=-1,
+    )
+
+
+def to_natural(v):
+    n, f, c = lax.axis_size("fsdp"), lax.axis_index("fsdp"), lax.axis_index("section")
+    size = v.shape[-1] // (2 * n)
+    return jnp.concatenate(
+        [
+            lax.dynamic_slice_in_dim(v, ((c ^ h) * n + (f ^ k)) * size, size, v.ndim - 1)
+            for k in range(n)
+            for h in range(2)
+        ],
+        axis=-1,
+    )
+
+
+def reorder(v, m):
+    n = lax.axis_size("fsdp")
+    size = v.shape[-1] // (2 * n)
+    return jnp.concatenate(
+        [
+            v[..., (t * n + (j ^ m)) * size : (t * n + (j ^ m) + 1) * size]
+            for t in range(2)
+            for j in range(n)
+        ],
+        axis=-1,
+    )
+
+
+def gather_plain(v):
     n = lax.axis_size("fsdp")
     return jnp.stack([v] + [move_fsdp(v, m) for m in range(1, n)])
 
 
-def gather_in_order(v, f):
+def gather_rows(v):
     n = lax.axis_size("fsdp")
-    out = jnp.zeros((n,) + v.shape, v.dtype)
-    for m in range(n):
-        piece = v if m == 0 else move_fsdp(v, m)
-        out = lax.dynamic_update_index_in_dim(out, piece, f ^ m, 0)
-    return out
+    return jnp.concatenate([v] + [reorder(move_fsdp(v, m), m) for m in range(1, n)])
 
 
 def scatter_sum(partial):
     n = lax.axis_size("fsdp")
     total = partial[0]
     for m in range(1, n):
-        total = total + move_fsdp(partial[m].astype(BF16), m).astype(F32)
+        total = total + reorder(move_fsdp(partial[m].astype(BF16), m), m).astype(F32)
     return total
 
 
@@ -427,6 +509,22 @@
     for m in range(1, n):
         got = move_fsdp(v, m)
         total = total + jnp.stack([got[j ^ m] for j in range(n)])
+    return total
+
+
+def seq_sum(v):
+    s = lax.axis_size("seq")
+    place = lax.axis_index("seq")
+    half = s // 2
+    add = lambda a, b: (a.astype(F32) + b.astype(F32)).astype(BF16)
+    total = v
+    for j in range(half - 1):
+        pairs = [(j, j + 1), (s - 1 - j, s - 2 - j)]
+        total = add(total, lax.ppermute(total, "seq", pairs))
+    total = add(total, lax.ppermute(total, "seq", [(half - 1, half), (half, half - 1)]))
+    for j in reversed(range(half - 1)):
+        got = lax.ppermute(total, "seq", [(j + 1, j), (s - 2 - j, s - 1 - j)])
+        total = jnp.where((place == j) | (place == s - 1 - j), got, total)
     return total
 
 
@@ -490,34 +588,69 @@
     width = INNER // n
     heads = HEADS // n
     share = D // n
+    half = share // 2
     group = GROUP // n
+    pairs_of = n // 2
     f1 = f.reshape(1).astype(jnp.int32)
+    ids = jnp.stack([f, c]).astype(jnp.int32)
 
     def pick(a, b):
         return jnp.where(upper, a, b)
+
+    w = w_in[0]
+    kept = lax.dynamic_slice_in_dim(w, c * half, half, 0)
+    other = swap_section(lax.dynamic_slice_in_dim(w, (1 - c) * half, half, 0))
+
+    def columns(v, k):
+        cut = lambda at, size: lax.dynamic_slice_in_dim(v, at, size, 1)
+        return (
+            jnp.concatenate([cut(k * width, width), cut(INNER + k * width, width)], axis=1),
+            jnp.concatenate(
+                [v[:, 2 * INNER : 2 * INNER + GROUP], cut(2 * INNER + GROUP + k * heads, heads)],
+                axis=1,
+            ),
+        )
+
+    def cut_blocks(layer):
+        return [
+            [
+                jnp.where(c == layer, a, b)
+                for a, b in zip(columns(kept, f ^ m), columns(other, f ^ m))
+            ]
+            for m in range(n)
+        ]
+
+    def fetch(blocks):
+        got = [
+            [b if m == 0 else move_fsdp(b, m) for b in blocks[m]] for m in range(n)
+        ]
+        across = [[swap_section(b) for b in pieces] for pieces in got]
+        full = [
+            jnp.concatenate([p[q] for p in got] + [p[q] for p in across]) for q in range(2)
+        ]
+        return full, got
 
     own_in = lax.dynamic_index_in_dim(inputs, c, 0, False)[0]
     own_ct = lax.dynamic_index_in_dim(cotangent, c, 0, False)[0]
     own_len = lax.dynamic_index_in_dim(lengths, c, 0, False)
+    h0 = to_local(transpose_places(own_in))
     length = transpose_places(own_len)
     start = ((place // n) * n + f) * rows
     valid = (start + jnp.arange(rows, dtype=jnp.int32) < length[0]).astype(F32)[:, None]
-    h0 = transpose_places(own_in)
-    dout1 = transpose_places(own_ct).astype(F32)
-    all_h0 = gather_blocks(h0).reshape(n * rows, D)
+    all_h0 = gather_rows(h0)
 
     pack = jnp.concatenate(
         [
             gain_in[0],
-            conv_w[0].reshape(-1),
-            conv_b[0],
             dt_bias[0],
             a_log[0],
             d_skip[0],
             gain_out[0],
+            conv_w[0].reshape(-1),
+            conv_b[0],
         ]
     )
-    mine = gather_in_order(pack, f)
+    mine = gather_plain(pack)
     theirs = swap_section(mine)
     small = []
     for full in (pick(mine, theirs), pick(theirs, mine)):
@@ -529,58 +662,35 @@
             at += size
             return full[:, at - size : at]
 
+        halves = take(share).reshape(n, 2, half)
+        gain = pick(halves, halves[:, ::-1]).transpose(1, 0, 2).reshape(1, D)
+        hp = [take(heads)[0:1] for _ in range(3)]
+        hp = jnp.concatenate([hp[0], -jnp.exp(hp[1]), hp[2], jnp.zeros((5, heads), F32)])
+        gout = take(width)[0:1]
+        rest = full[:, at:]
+        rest = jnp.concatenate(
+            [lax.dynamic_index_in_dim(rest, f ^ k, 0, True) for k in range(n)]
+        )
         per = CHANNELS // n
-        gain = take(share).reshape(1, D)
-        taps = take(KERNEL * per).reshape(n, KERNEL, per).transpose(1, 0, 2).reshape(KERNEL, -1)
-        bias = take(per).reshape(1, CHANNELS)
-        table = jnp.concatenate([taps, bias, jnp.zeros((3, CHANNELS), F32)])
+        taps = rest[:, : KERNEL * per].reshape(n, KERNEL, per).transpose(1, 0, 2)
+        bias = rest[:, KERNEL * per :].reshape(1, CHANNELS)
+        table = jnp.concatenate(
+            [taps.reshape(KERNEL, CHANNELS), bias, jnp.zeros((3, CHANNELS), F32)]
+        )
         cw = jnp.concatenate(
             [lax.dynamic_slice_in_dim(table, f * width, width, 1), table[:, INNER:]], axis=1
         )
-        own_heads = [
-            lax.dynamic_index_in_dim(take(heads), f, 0, True) for _ in range(3)
-        ]
-        hp = jnp.concatenate(
-            [own_heads[0], -jnp.exp(own_heads[1]), own_heads[2], jnp.zeros((5, heads), F32)]
-        )
-        gout = lax.dynamic_index_in_dim(take(width), f, 0, True)
         small.append((gain, cw, hp, gout))
 
-    w = w_in[0]
-
-    def columns(k):
-        cut = lambda at, size: lax.dynamic_slice_in_dim(w, at, size, 1)
-        return (
-            cut(k * width, width),
-            cut(INNER + k * width, width),
-            jnp.concatenate(
-                [w[:, 2 * INNER : 2 * INNER + GROUP], cut(2 * INNER + GROUP + k * heads, heads)],
-                axis=1,
-            ),
-        )
-
-    blocks = [columns(f ^ m) for m in range(n)]
-
-    def fetch(layer, blocks):
-        full = [jnp.zeros((n,) + b.shape, BF16) for b in blocks[0]]
-        for m in range(n):
-            for q in range(3):
-                piece = blocks[m][q]
-                if m:
-                    pairs = [(layer * n + i, layer * n + (i ^ m)) for i in range(n)]
-                    piece = lax.ppermute(piece, ("section", "fsdp"), pairs)
-                other = lax.ppermute(piece, "section", [(layer, 1 - layer)])
-                got = jnp.where(c == layer, piece, other)
-                full[q] = lax.dynamic_update_index_in_dim(full[q], got, f ^ m, 0)
-        return [v.reshape(D, v.shape[-1]) for v in full]
-
-    w0 = fetch(0, blocks)
-    blocks, _ = lax.optimization_barrier((blocks, w0))
-    w1 = fetch(1, blocks)
-    wo_mine = w_out[0]
+    w0, came = fetch(cut_blocks(0))
+    blocks1, own_ct, wo_mine, _ = lax.optimization_barrier(
+        (cut_blocks(1), own_ct, w_out[0], came)
+    )
     wo_other = swap_section(wo_mine)
-    wo = (pick(wo_mine, wo_other), pick(wo_other, wo_mine))
+    wo = (to_local(pick(wo_mine, wo_other)), to_local(pick(wo_other, wo_mine)))
+    w1, _ = fetch(blocks1)
     win = (w0, w1)
+    dout1 = to_local(transpose_places(own_ct)).astype(F32)
 
     expand = (
         jnp.arange(heads)[:, None] == jnp.arange(width)[None, :] // HEAD_DIM
@@ -589,84 +699,99 @@
     zero_edge = jnp.zeros((8, width + GROUP), F32)
 
     def project(normed, layer):
-        return [
-            jnp.dot(normed, part, preferred_element_type=F32) for part in win[layer]
-        ]
+        return [jnp.dot(normed, part, preferred_element_type=F32) for part in win[layer]]
+
+    def decay_of(pbd, hp):
+        decay = jax.nn.softplus(pbd[:, GROUP:] + hp[0:1]) * hp[1:2]
+        return jnp.repeat(jnp.exp(jnp.sum(decay, axis=0)), HEAD_DIM)[None, :]
 
     def scan(proj, layer, extra):
-        pz, px, pbd = proj
+        pzx, pbd = proj
         _, cw, hp, _ = small[layer]
-        args = (f1, pz, px, pbd, cw, hp, expand)
+        args = (f1, pzx, pbd, cw, hp, expand)
         if segments == 1:
             return run_forward(*args, zero_state, zero_edge, extra, rows)
         rear = lax.dynamic_slice_in_dim(
-            jnp.concatenate([px, pbd[:, :GROUP]], axis=1), ((n - 1) ^ f) * rows + rows - 8, 8, 0
+            jnp.concatenate([pzx[:, width:], pbd[:, :GROUP]], axis=1),
+            ((n - 1) ^ f) * rows + rows - 8,
+            8,
+            0,
         )
         edge = next_segment(rear, 1)
         local = run_forward(*args, zero_state, edge, extra, rows)[3]
-        decay = jax.nn.softplus(pbd[:, GROUP:] + hp[0:1]) * hp[1:2]
-        total = jnp.repeat(jnp.exp(jnp.sum(decay, axis=0)), HEAD_DIM)[None, :]
-        state = relay(total, local, False)
+        state = relay(decay_of(pbd, hp), local, False)
         return run_forward(*args, state, edge, extra, rows)
 
     def unscan(proj, fwd, dn, rc, layer):
-        pz, px, pbd = proj
+        pzx, pbd = proj
         y, filt, states, final = fwd[:4]
         _, cw, hp, gout = small[layer]
         states = jnp.concatenate([states, final[None]])
-        args = (f1, pz, px, pbd, y, filt, dn, rc, states, cw, hp, expand, gout)
+        args = (f1, pzx, pbd, y, filt, dn, rc, states, cw, hp, expand, gout)
         if segments == 1:
             return run_backward(*args, zero_state, zero_edge, rows)
-        local = run_backward(*args, zero_state, zero_edge, rows)[7]
-        decay = jax.nn.softplus(pbd[:, GROUP:] + hp[0:1]) * hp[1:2]
-        total = jnp.repeat(jnp.exp(jnp.sum(decay, axis=0)), HEAD_DIM)[None, :]
-        grad = relay(total, local, True)
-        edge = next_segment(run_backward(*args, grad, zero_edge, rows)[8], -1)
+        local = run_backward(*args, zero_state, zero_edge, rows)[6]
+        grad = relay(decay_of(pbd, hp), local, True)
+        edge = next_segment(run_backward(*args, grad, zero_edge, rows)[7], -1)
         return run_backward(*args, grad, edge, rows)
 
-    def gated(pz, y, r, layer):
-        g = y * jax.nn.silu(pz)
-        return (g * r * small[layer][3]).astype(BF16)
+    def gated(pzx, y, r, layer):
+        g = y * jax.nn.silu(pzx[:, :width])
+        return (g * r.reshape(-1, 1) * small[layer][3]).astype(BF16)
 
     blockwise = lambda v: v.reshape(n, rows, v.shape[-1])
 
     normed_in0 = normalised(all_h0.astype(F32), small[0][0]).astype(BF16)
     proj0 = project(normed_in0, 0)
     fwd0 = scan(proj0, 0, ())
-    stat0 = sum_rows(blockwise(fwd0[4][:, 0:1])).reshape(n * rows, 1)
-    r0 = lax.rsqrt(stat0 / INNER + EPS)
+    stat0 = sum_rows(fwd0[4])
+    r0 = lax.rsqrt(stat0[:, 0] / INNER + EPS)
     normed0 = gated(proj0[0], fwd0[0], r0, 0)
     mixed0 = scatter_sum(blockwise(jnp.dot(normed0, wo[0], preferred_element_type=F32)))
     out0 = valid * (h0.astype(F32) + mixed0)
     h1 = out0.astype(BF16)
 
     part1 = normalised(h1.astype(F32), small[1][0]).astype(BF16)
-    normed_in1 = gather_blocks(part1).reshape(n * rows, D)
+    normed_in1 = gather_rows(part1)
     proj1 = project(normed_in1, 1)
-    dmixed1 = gather_blocks((valid * dout1).astype(BF16)).reshape(n * rows, D)
+    dmixed1 = gather_rows((valid * dout1).astype(BF16))
     dn1 = dot_cols(dmixed1, wo[1])
     fwd1 = scan(proj1, 1, (dn1, small[1][3]))
-    stat1 = sum_rows(blockwise(fwd1[4][:, 0:2])).reshape(n * rows, 2)
-    r1 = lax.rsqrt(stat1[:, 0:1] / INNER + EPS)
+    stat1 = sum_rows(fwd1[4])
+    r1 = lax.rsqrt(stat1[:, 0] / INNER + EPS)
     normed1 = gated(proj1[0], fwd1[0], r1, 1)
     mixed1 = scatter_sum(blockwise(jnp.dot(normed1, wo[1], preferred_element_type=F32)))
     out1 = valid * (h1.astype(F32) + mixed1)
     last1 = out1.astype(BF16)
 
-    def half_sums(a, b, parts):
-        view = a.reshape(a.shape[0], parts, 2, -1)
-        cut = lambda k: lax.dynamic_index_in_dim(view, k, 2, False).reshape(a.shape[0], -1)
-        away = swap_section(dot_rows(cut(1 - c), b).astype(BF16))
-        return (dot_rows(cut(c), b) + away.astype(F32)).astype(BF16)
-
-    def over_seq(v, dim):
-        piece = lax.psum_scatter(v, "seq", scatter_dimension=dim, tiled=True)
-        return piece
+    def half_sum(own, away):
+        away = swap_section(dot_rows(*away).astype(BF16))
+        return (dot_rows(*own) + away.astype(F32)).astype(BF16)
+
+    def grads_in(normed_in, part):
+        total = half_sum((normed_in[:, : D // 2], part), (normed_in[:, D // 2 :], part))
+        total = total.reshape(n, half, -1)
+        pieces = [total[0]] + [move_fsdp(total[m], m) for m in range(1, n)]
+        return pieces
+
+    def pair_up(pieces):
+        return [
+            seq_sum(jnp.stack(pieces[2 * k : 2 * k + 2])) for k in range(pairs_of)
+        ]
+
+    def grads_out(normed, dmixed):
+        size = D // 2 // pairs_of
+        result = []
+        for k in range(pairs_of):
+            own = dmixed[:, k * size : (k + 1) * size]
+            away = dmixed[:, D // 2 + k * size : D // 2 + (k + 1) * size]
+            result.append(seq_sum(half_sum((normed, own), (normed, away))))
+        return result
 
     def back_layer(layer, dn, dmixed, rc, proj, fwd, normed, normed_in):
-        gw_out = half_sums(normed, dmixed, 1)
-        dz, dx, dbc, ddt, dgain, dconv, dhp, _, _ = unscan(proj, fwd, dn, rc, layer)
-        wz, wx, wbd = win[layer]
+        gw_out = grads_out(normed, dmixed)
+        dzx, dbc, ddt, dgain, dconv, dhp, _, _ = unscan(proj, fwd, dn, rc, layer)
+        wzx, wbd = win[layer]
         shares = blockwise(dbc)
         own_cols = lambda k: lax.dynamic_slice_in_dim(shares, k * group, group, 2)
         total = own_cols(f)
@@ -677,10 +802,12 @@
         wsmall = jnp.concatenate(
             [lax.dynamic_slice_in_dim(wbd, f * group, group, 1), wbd[:, GROUP:]], axis=1
         )
-        back = dot_cols(dz, wz) + dot_cols(dx, wx) + dot_cols(dsmall, wsmall)
+        back = dot_cols(dzx, wzx) + dot_cols(dsmall, wsmall)
         dnormed_in = scatter_sum(blockwise(back))
-        dproj = jnp.concatenate([dz, dx, dsmall], axis=1)
-        gw_in = half_sums(normed_in, dproj, n)
+        gz = grads_in(normed_in, dzx[:, :width])
+        gx = grads_in(normed_in, dzx[:, width:])
+        gs = grads_in(normed_in, dsmall)
+        gw_in = pair_up(gz) + pair_up(gx) + [seq_sum(jnp.stack(gs))]
         return dnormed_in, gw_in, gw_out, (dgain[0], dconv[:5], dhp[:3])
 
     def back_norm(dout, dnormed_in, h, gain):
@@ -691,43 +818,26 @@
         dgain = jnp.sum(dnormed_in * h * r, axis=0)
         return valid * dout + r * u - h * (r * r * r) * mean, dgain
 
-    def combine(layer, gw_in, gw_out):
-        a = over_seq(gw_in.reshape(n, share // 2, -1), 1)
-        b = over_seq(gw_out, 0)
-        full = jnp.zeros_like(a)
-        for m in range(n):
-            piece = lax.dynamic_index_in_dim(a, f ^ m, 0, False)
-            if m:
-                piece = move_fsdp(piece, m)
-            full = lax.dynamic_update_index_in_dim(full, piece, f ^ m, 0)
-        return (
-            lax.all_gather(full, "seq", axis=1, tiled=True),
-            lax.all_gather(b, "seq", axis=0, tiled=True),
-        )
-
-    rc1 = jnp.concatenate(
-        [r1, (r1 * r1 * r1 / INNER) * stat1[:, 1:2], jnp.zeros((n * rows, 6), F32)], axis=1
-    )
+    def scales(r, coef):
+        rest = jnp.zeros((n, 6, rows), F32)
+        return jnp.concatenate([r[:, None], coef[:, None], rest], axis=1)
+
+    rc1 = scales(r1, (r1 * r1 * r1 / INNER) * stat1[:, 1])
     dnin1, gwi1, gwo1, smalls1 = back_layer(
         1, dn1, dmixed1, rc1, proj1, fwd1, normed1, normed_in1
     )
     grad1, dgin1 = back_norm(dout1, dnin1, h1, small[1][0])
-    full1 = combine(1, gwi1, gwo1)
 
     dout0 = grad1.astype(BF16).astype(F32)
     dmixed0_own = (valid * dout0).astype(BF16)
-    dmixed0 = gather_blocks(dmixed0_own).reshape(n * rows, D)
-    along = jnp.sum(dmixed0_own.astype(F32) * mixed0, axis=-1, keepdims=True)
-    along0 = gather_blocks(along).reshape(n * rows, 1)
+    dmixed0 = gather_rows(dmixed0_own)
+    along0 = gather_plain(jnp.sum(dmixed0_own.astype(F32) * mixed0, axis=-1))
     dn0 = dot_cols(dmixed0, wo[0])
-    rc0 = jnp.concatenate(
-        [r0, (r0 * r0 / INNER) * along0, jnp.zeros((n * rows, 6), F32)], axis=1
-    )
+    rc0 = scales(r0, (r0 * r0 / INNER) * along0)
     dnin0, gwi0, gwo0, smalls0 = back_layer(
         0, dn0, dmixed0, rc0, proj0, fwd0, normed0, normed_in0
     )
     grad0, dgin0 = back_norm(dout0, dnin0, h0, small[0][0])
-    full0 = combine(0, gwi0, gwo0)
 
     def packed(dgin, smalls, out, mixed):
         dgain, dconv, dhp = smalls
@@ -741,7 +851,7 @@
         )
         return jnp.concatenate(
             [
-                dgin,
+                to_natural(dgin),
                 conv.reshape(-1),
                 put(dhp, HEADS, f * heads).reshape(-1),
                 put(dgain, INNER, f * width),
@@ -750,8 +860,9 @@
         )
 
     everyone = ("section", "seq", "fsdp")
-    p1 = lax.psum(packed(dgin1, smalls1, out1, mixed1), everyone)
-    p0 = lax.psum(packed(dgin0, smalls0, out0, mixed0), everyone)
+    p1 = packed(dgin1, smalls1, out1, mixed1)
+    p0 = packed(dgin0, smalls0, out0, mixed0)
+    p0, p1 = lax.psum((p0, p1), everyone)
     p = pick(p0, p1)
     at = 0
 
@@ -768,29 +879,72 @@
     sums = take(3)
     act_rms = jnp.sqrt(sums[:2] / (sums[2] * D))[None]
 
-    def owned(a, b):
-        own, away = pick(a, b), swap_section(pick(b, a))
-        return pick(own, away), pick(away, own)
-
-    lo_in, hi_in = owned(full0[0], full1[0])
-    cols = jnp.concatenate([lo_in, hi_in], axis=1).astype(F32)
-    side = lambda v: v.transpose(1, 0, 2).reshape(share, -1)
-    g_w_in = jnp.concatenate(
+    def hand_over(v, layer):
+        return lax.ppermute(v, "section", [(1 - layer, layer)])
+
+    away1 = [hand_over(v, 1) for v in gwi1 + gwo1]
+    away0 = [hand_over(v, 0) for v in gwi0 + gwo0]
+    in_count = len(gwi1)
+    own = (gwi0 + gwo0, gwi1 + gwo1)
+    away = (away0, away1)
+
+    def small_columns(v):
+        v = v.astype(F32)
+        by_place = [lax.dynamic_index_in_dim(v, f ^ k, 0, False) for k in range(n)]
+        return jnp.concatenate(
+            [b[:, :group] for b in by_place] + [b[:, group:] for b in by_place], axis=1
+        )
+
+    at_small = in_count - 1
+    small_in = jnp.stack(
         [
-            side(cols[:, :, :width]),
-            side(cols[:, :, width : 2 * width]),
-            side(cols[:, :, 2 * width : 2 * width + group]),
-            side(cols[:, :, 2 * width + group :]),
-        ],
-        axis=1,
-    )
-    lo_out, hi_out = owned(full0[1], full1[1])
-    g_w_out = jnp.concatenate([lo_out, hi_out], axis=0).astype(F32)
+            small_columns(pick(own[0][at_small], own[1][at_small])),
+            small_columns(pick(away0[at_small], away1[at_small])),
+        ]
+    )
+    side_row = lambda h, ids: jnp.where(h == 0, ids[1], 1 - ids[1])
+    chunks_in = [
+        (src[side][layer][k], side, layer, 2 * k, 2, (1, half, width), lambda i: (i, 0, 0))
+        for src in ((own, away),)
+        for side in range(2)
+        for layer in range(2)
+        for k in range(at_small)
+    ]
+    g_w_in = place_blocks(
+        ids,
+        chunks_in,
+        small_in,
+        (share, 2 * INNER + GROUP + HEADS),
+        (half, width),
+        lambda h, j, ids: (
+            side_row(h, ids),
+            jnp.where(
+                j < 2 * n, (j // n) * n + jnp.bitwise_xor(j % n, ids[0]), 2 * n
+            ),
+        ),
+        2 * n + 1,
+    )
+    chunks_out = [
+        (src[side][layer][in_count + k], side, layer, 2 * k, 2, (width, half), lambda i: (0, i))
+        for src in ((own, away),)
+        for side in range(2)
+        for layer in range(2)
+        for k in range(pairs_of)
+    ]
+    g_w_out = place_blocks(
+        ids,
+        chunks_out,
+        None,
+        (width, D),
+        (width, half),
+        lambda h, j, ids: (0, jnp.bitwise_xor(j, ids[0]) * 2 + side_row(h, ids)),
+        n,
+    )
 
     def returned(a, b):
         own, away = pick(a, b), pick(b, a)
-        own = transpose_places(own)
-        away = swap_section(transpose_places(away))
+        own = transpose_places(to_natural(own))
+        away = swap_section(transpose_places(to_natural(away)))
         return jnp.stack([pick(own, away), pick(away, own)])
 
     layer_out = returned(h1, last1)

time: 1580 us -> 1680 us (1.063)
  local copies, waits for them, and re-layouts: 375 us -> 144 us
  starting transfers between devices: 267 us -> 473 us
  waiting for transfers between devices: 571 us -> 704 us
  other arithmetic: 128 us -> 90.5 us
  Pallas kernels: 105 us -> 129 us
    all_gather x4 -> x0, waiting for transfers between devices: 309 us -> none  [the longest x2 178 us: combine(): lax.all_gather(full, 'seq', axis=1, tiled=True)]
    ppermute x42 -> x56, waiting for transfers between devices: 63.4 us -> 329 us  [the longest x14 207 us: seq_sum(): got = lax.ppermute(total, 'seq', [(j + 1, j), (s - 2 - j, s - 1 - j)])]
    ppermute x42 -> x56, starting transfers between devices: 74.6 us -> 256 us  [the longest x14 140 us: seq_sum(): total = add(total, lax.ppermute(total, 'seq', pairs))]
    dynamic_update_slice x20 -> x0, local copies, waits for them, and re-layouts: 167 us -> none  [the longest x8 86.3 us: fetch(): full[q] = lax.dynamic_update_index_in_dim(full[q], got, f ^ m, 0)]
    ppermute x48 -> x72, waiting for transfers between devices: 98.2 us -> 251 us  [move_fsdp(): return lax.ppermute(v, 'fsdp', [(i, i ^ m) for i in range(n)])]
    psum x1, waiting for transfers between devices: 85.3 us -> 119 us  [per_device(): p0, p1 = lax.psum((p0, p1), everyone)]
    broadcast_in_dim x8 -> x0, other arithmetic: 30 us -> none  [the longest x1 23 us: per_device(): g_w_in[None]]
    unnamed x197 -> x437, local copies, waits for them, and re-layouts: 30.4 us -> 57.4 us
  transfers between devices with their start and end apart: 116 -> 167, of which waited for: 29 -> 57; matrix products, arithmetic and copies ran while one was open for 32% -> 16% of each run, Pallas kernels for 3% -> 4%
where the time goes in v2:
time: 1680 us; the launch traced here: 1650 us
  waiting for transfers between devices  704 us (42%)
  starting transfers between devices  473 us (28%)
  local copies, waits for them, and re-layouts  144 us (9%)
  Pallas kernels  129 us (8%)
  matrix products  91.3 us (5%)
  other arithmetic  90.5 us (5%)
  between operations  19.5 us (1%)
    ppermute x72, waiting for transfers between devices, move_fsdp(): return lax.ppermute(v, 'fsdp', [(i, i ^ m) for i in range(n)])  251 us
    ppermute x14, waiting for transfers between devices, seq_sum(): got = lax.ppermute(total, 'seq', [(j + 1, j), (s - 2 - j, s - 1 - j)])  207 us
    ppermute x72, starting transfers between devices, move_fsdp(): return lax.ppermute(v, 'fsdp', [(i, i ^ m) for i in range(n)])  151 us
    ppermute x14, starting transfers between devices, seq_sum(): total = add(total, lax.ppermute(total, 'seq', pairs))  140 us
    ppermute x14, waiting for transfers between devices, seq_sum(): total = add(total, lax.ppermute(total, 'seq', pairs))  122 us
    psum x1, waiting for transfers between devices, per_device(): p0, p1 = lax.psum((p0, p1), everyone)  119 us
    ppermute x14, starting transfers between devices, hand_over(): return lax.ppermute(v, 'section', [(1 - layer, layer)])  86.3 us
    pallas_call x2, Pallas kernels, run_backward(): pl.pallas_call(backward_kernel, grid_spec=pltpu.PrefetchScalarGridSpec(nu...  69.3 us
  transfers between devices with their start and end apart: 167, of which 57 were waited for; matrix products, arithmetic and copies ran while one was open for 16% of the time, Pallas kernels for 4%

profile of v2, /device:TPU:1, one launch (start us, length us, event | category | flops | bytes accessed | tf_op | source)
XLA Modules:
  0.0 1650.3 jit_solution(12173756018044505604)
XLA Ops:
  15.8 6.1 dynamic-slice_bitcast_fusion
  28.7 6.9 dynamic-slice_bitcast_fusion.4
  81.1 14.5 collective-permute-done.17
  99.8 27.5 %collective-permute-done.18 = bf16[256,272]{0,1:T(8,128)(2,1)S(1)} collective-permute-done((bf16[256,272]{0,1:T(8,128)(2,1)S(1)}, bf16[256,272]{0,1:T(8,128)(2,1)S(1)}, u32[]{:S(2)}, u32[]{:S(2)}) %collective-permute-start.18) | collective-permute-done | bytes 139296 | tf_op jit(solution)/shard_map/ppermute | solution.py:435
  159.9 8.3 collective-permute-start.34
  169.9 7.8 collective-permute-start.4
  177.7 28.0 %collective-permute-start.3 = (bf16[128,2048]{1,0:T(8,128)(2,1)S(1)}, bf16[128,2048]{1,0:T(8,128)(2,1)S(1)}, u32[]{:S(2)}, u32[]{:S(2)}) collective-permute-start(bf16[128,2048]{1,0:T(8,128)(2,1)S(1)} %constant_dynamic-update-slice_fusion), channel_id=1, source_target_pairs={{0,2},{1,3},{2,0},{3,1},{4,6},{5,7},{6,4},{7,5},{8,10},{9,11},{10,... | collective-permute-start | bytes 1572872 | tf_op jit(solution)/shard_map/ppermute | solution.py:435
  205.9 19.4 %collective-permute-done.4 = bf16[128,2048]{1,0:T(8,128)(2,1)S(1)} collective-permute-done((bf16[128,2048]{1,0:T(8,128)(2,1)S(1)}, bf16[128,2048]{1,0:T(8,128)(2,1)S(1)}, u32[]{:S(2)}, u32[]{:S(2)}) %collective-permute-start.4) | collective-permute-done | bytes 524320 | tf_op jit(solution)/shard_map/ppermute | solution.py:435
  227.6 10.6 collective-permute-done.2
  251.1 9.7 fusion.184.pzx
  262.1 16.1 scan_forward.2
  283.6 9.8 collective-permute-done.35
  318.1 9.5 collective-permute-done.30
  327.7 11.4 collective-permute-done.29
  346.1 9.5 collective-permute-done.33
  355.8 11.0 collective-permute-done.32
  372.3 10.5 fusion.186.pzx
  383.0 6.3 collective-permute-done.50
  400.0 17.2 %scan_forward.3 = (f32[512,1024]{1,0:T(8,128)S(1)}, f32[512,1280]{1,0:T(8,128)}, f32[4,128,1024]{2,1,0:T(8,128)S(1)}, f32[128,1024]{1,0:T(8,128)S(1)}, f32[4,8,128]{2,1,0:T(8,128)S(1)}) custom-call(s32[1]{0:T(128)} %bitcast.3.f_ref, f32[512,2048]{1,0:T(8,128)} %fusion.186.pzx, f32[512,272]{1,0:T(8,128)S(1)} %fusion.187.pbd, ...), custom_call_target="tpu_custom_call" | custom-call | tf_op jit(solution)/shard_map/scan_forward/pallas_call | solution.py:285
  421.9 34.6 %scan_backward.2 = (bf16[512,2048]{1,0:T(8,128)(2,1)S(1)}, f32[512,256]{1,0:T(8,128)S(1)}, f32[512,16]{1,0:T(8,128)S(1)}, f32[8,1024]{1,0:T(8,128)S(1)}, f32[8,1...) custom-call(s32[1]{0:T(128)} %bitcast.3.f_ref, f32[512,2048]{1,0:T(8,128)} %fusion.186.pzx, ...), custom_call_target="tpu_custom_call" | custom-call | tf_op jit(solution)/shard_map/scan_backward/pallas_call | solution.py:323
  487.0 18.6 %collective-permute-start.137 = (bf16[1024,80]{0,1:T(8,128)(2,1)S(1)}, bf16[1024,80]{0,1:T(8,128)(2,1)S(1)}, u32[]{:S(2)}, u32[]{:S(2)}) collective-permute-start(bf16[1024,80]{0,1:T(8,128)(2,1)S(1)} %convolution_convert_fusion.8), channel_id=1, source_target_pairs={{0,16},{16,0},{1,17},{17,1},{2,18},{18,2},{3,19},{19,3},{4,20},{20... | collective-permute-start | bytes 491528 | tf_op jit(solution)/shard_map/ppermute | solution.py:430
  510.8 6.9 fusion.181
  542.3 12.6 collective-permute-done.65
  593.7 8.5 collective-permute-done.68
  602.2 8.9 collective-permute-done.67
  620.3 34.7 %scan_backward.3 = (bf16[512,2048]{1,0:T(8,128)(2,1)S(1)}, f32[512,256]{1,0:T(8,128)S(1)}, f32[512,16]{1,0:T(8,128)S(1)}, f32[8,1024]{1,0:T(8,128)S(1)}, f32[8,1...) custom-call(s32[1]{0:T(128)} %bitcast.3.f_ref, f32[512,2048]{1,0:T(8,128)} %fusion.184.pzx, ...), custom_call_target="tpu_custom_call" | custom-call | tf_op jit(solution)/shard_map/scan_backward/pallas_call | solution.py:323
  669.1 9.1 collective-permute-done.74
  688.0 6.9 fusion.183
  697.2 15.0 collective-permute-start.134
  718.4 21.4 %collective-permute-start.77 = (bf16[128,2048]{1,0:T(8,128)(2,1)S(1)}, bf16[128,2048]{1,0:T(8,128)(2,1)S(1)}, u32[]{:S(2)}, u32[]{:S(2)}) collective-permute-start(bf16[128,2048]{1,0:T(8,128)(2,1)S(1)} %get-tuple-element.209), channel_id=1, source_target_pairs={{0,2},{1,3},{2,0},{3,1},{4,6},{5,7},{6,4},{7,5},{8,10},{9,11},{10,... | collective-permute-start | bytes 1572872 | tf_op jit(solution)/shard_map/ppermute | solution.py:435
  741.0 11.6 collective-permute-start.76
  752.7 8.5 collective-permute-done.77
  777.3 119.4 %all-reduce.3.cloned.1.call-done = (f32[28099]{0:T(1024)}, f32[28099]{0:T(1024)}) async-done(((f32[28099]{0:T(1024)}, f32[28099]{0:T(1024)}), (f32[28099]{0:T(1024)}, f32[28099]{0:T(1024)})) %all-reduce.3.cloned.1.call-update) | async-done | bytes 224808 | tf_op jit(solution)/shard_map/psum | solution.py:865
  904.1 5.7 collective-permute-done.136
  939.0 10.9 collective-permute-done.108
  961.0 11.4 collective-permute-done.118
  973.8 10.0 collective-permute-done.117
  986.9 16.2 collective-permute-start.104
  1010.9 16.4 collective-permute-done.151
  1029.2 20.5 %collective-permute-done.104 = bf16[2,256,1024]{2,1,0:T(8,128)(2,1)S(1)} collective-permute-done((bf16[2,256,1024]{2,1,0:T(8,128)(2,1)S(1)}, bf16[2,256,1024]{2,1,0:T(8,128)(2,1)S(1)}, u32[]{:S(2)}, u32[]{:S(2)}) %collective-permute-start.104) | collective-permute-done | bytes 1048608 | tf_op jit(solution)/shard_map/ppermute | solution.py:523
  1050.1 22.1 %collective-permute-done.109 = bf16[2,256,1024]{2,1,0:T(8,128)(2,1)S(1)} collective-permute-done((bf16[2,256,1024]{2,1,0:T(8,128)(2,1)S(1)}, bf16[2,256,1024]{2,1,0:T(8,128)(2,1)S(1)}, u32[]{:S(2)}, u32[]{:S(2)}) %collective-permute-start.109) | collective-permute-done | bytes 1048608 | tf_op jit(solution)/shard_map/ppermute | solution.py:523
  1073.8 20.9 %collective-permute-done.114 = bf16[2,256,1024]{2,1,0:T(8,128)(2,1)S(1)} collective-permute-done((bf16[2,256,1024]{2,1,0:T(8,128)(2,1)S(1)}, bf16[2,256,1024]{2,1,0:T(8,128)(2,1)S(1)}, u32[]{:S(2)}, u32[]{:S(2)}) %collective-permute-start.114) | collective-permute-done | bytes 1048608 | tf_op jit(solution)/shard_map/ppermute | solution.py:523
  1095.4 21.7 %collective-permute-done.119 = bf16[2,256,1024]{2,1,0:T(8,128)(2,1)S(1)} collective-permute-done((bf16[2,256,1024]{2,1,0:T(8,128)(2,1)S(1)}, bf16[2,256,1024]{2,1,0:T(8,128)(2,1)S(1)}, u32[]{:S(2)}, u32[]{:S(2)}) %collective-permute-start.119) | collective-permute-done | bytes 1048608 | tf_op jit(solution)/shard_map/ppermute | solution.py:523
  1127.7 10.6 collective-permute-done.98
  1143.4 11.2 collective-permute-start.84
  1154.6 39.3 %collective-permute-start.89 = (bf16[2,256,1024]{2,1,0:T(8,128)(2,1)S(1)}, bf16[2,256,1024]{2,1,0:T(8,128)(2,1)S(1)}, u32[]{:S(2)}, u32[]{:S(2)}) collective-permute-start(bf16[2,256,1024]{2,1,0:T(8,128)(2,1)S(1)} %pad_maximum_fusion.15), channel_id=1, source_target_pairs={{0,4},{12,8},{1,5},{13,9},{2,6},{14,10},{3,7},{15,11},{16,20},{28,... | collective-permute-start | bytes 3145736 | tf_op jit(solution)/shard_map/ppermute | solution.py:523
  1193.9 22.5 %collective-permute-start.94 = (bf16[2,256,1024]{2,1,0:T(8,128)(2,1)S(1)}, bf16[2,256,1024]{2,1,0:T(8,128)(2,1)S(1)}, u32[]{:S(2)}, u32[]{:S(2)}) collective-permute-start(bf16[2,256,1024]{2,1,0:T(8,128)(2,1)S(1)} %pad_maximum_fusion.16), channel_id=1, source_target_pairs={{0,4},{12,8},{1,5},{13,9},{2,6},{14,10},{3,7},{15,11},{16,20},{28,... | collective-permute-start | bytes 3145736 | tf_op jit(solution)/shard_map/ppermute | solution.py:523
  1216.4 22.5 %collective-permute-start.99 = (bf16[2,256,1024]{2,1,0:T(8,128)(2,1)S(1)}, bf16[2,256,1024]{2,1,0:T(8,128)(2,1)S(1)}, u32[]{:S(2)}, u32[]{:S(2)}) collective-permute-start(bf16[2,256,1024]{2,1,0:T(8,128)(2,1)S(1)} %pad_maximum_fusion.17), channel_id=1, source_target_pairs={{0,4},{12,8},{1,5},{13,9},{2,6},{14,10},{3,7},{15,11},{16,20},{28,... | collective-permute-start | bytes 3145736 | tf_op jit(solution)/shard_map/ppermute | solution.py:523
  1244.9 13.7 collective-permute-done.99
  1261.6 11.7 collective-permute-start.81
  1274.7 74.2 %collective-permute-done.149 = bf16[1024,512]{1,0:T(8,128)(2,1)S(1)} collective-permute-done((bf16[1024,512]{1,0:T(8,128)(2,1)S(1)}, bf16[1024,512]{1,0:T(8,128)(2,1)S(1)}, u32[]{:S(2)}, u32[]{:S(2)}) %collective-permute-start.149) | collective-permute-done | bytes 1048608 | tf_op jit(solution)/shard_map/ppermute | solution.py:526
  1349.7 21.7 %collective-permute-done.153 = bf16[1024,512]{1,0:T(8,128)(2,1)S(1)} collective-permute-done((bf16[1024,512]{1,0:T(8,128)(2,1)S(1)}, bf16[1024,512]{1,0:T(8,128)(2,1)S(1)}, u32[]{:S(2)}, u32[]{:S(2)}) %collective-permute-start.153) | collective-permute-done | bytes 1048608 | tf_op jit(solution)/shard_map/ppermute | solution.py:526
  1384.4 6.3 collective-permute-done.106
  1392.1 18.6 %collective-permute-done.111 = bf16[2,256,1024]{2,1,0:T(8,128)(2,1)S(1)} collective-permute-done((bf16[2,256,1024]{2,1,0:T(8,128)(2,1)S(1)}, bf16[2,256,1024]{2,1,0:T(8,128)(2,1)S(1)}, u32[]{:S(2)}, u32[]{:S(2)}) %collective-permute-start.111) | collective-permute-done | bytes 1048608 | tf_op jit(solution)/shard_map/ppermute | solution.py:526
  1412.0 21.2 %collective-permute-done.116 = bf16[2,256,1024]{2,1,0:T(8,128)(2,1)S(1)} collective-permute-done((bf16[2,256,1024]{2,1,0:T(8,128)(2,1)S(1)}, bf16[2,256,1024]{2,1,0:T(8,128)(2,1)S(1)}, u32[]{:S(2)}, u32[]{:S(2)}) %collective-permute-start.116) | collective-permute-done | bytes 1048608 | tf_op jit(solution)/shard_map/ppermute | solution.py:526
  1434.5 23.1 %collective-permute-done.121 = bf16[2,256,1024]{2,1,0:T(8,128)(2,1)S(1)} collective-permute-done((bf16[2,256,1024]{2,1,0:T(8,128)(2,1)S(1)}, bf16[2,256,1024]{2,1,0:T(8,128)(2,1)S(1)}, u32[]{:S(2)}, u32[]{:S(2)}) %collective-permute-start.121) | collective-permute-done | bytes 1048608 | tf_op jit(solution)/shard_map/ppermute | solution.py:526
  1460.7 30.0 %collective-permute-start.162 = (bf16[1024,512]{1,0:T(8,128)(2,1)S(1)}, bf16[1024,512]{1,0:T(8,128)(2,1)S(1)}, u32[]{:S(2)}, u32[]{:S(2)}) collective-permute-start(bf16[1024,512]{1,0:T(8,128)(2,1)S(1)} %broadcast_select_fusion.5.refs_0_), channel_id=1, source_target_pairs={{16,0},{17,1},{18,2},{19,3},{20,4},{21,5},{22,6},{23,7},{24,8},{25... | collective-permute-start | bytes 3145736 | tf_op jit(solution)/shard_map/ppermute | solution.py:883
  1490.7 19.4 %collective-permute-start.163 = (bf16[1024,512]{1,0:T(8,128)(2,1)S(1)}, bf16[1024,512]{1,0:T(8,128)(2,1)S(1)}, u32[]{:S(2)}, u32[]{:S(2)}) collective-permute-start(bf16[1024,512]{1,0:T(8,128)(2,1)S(1)} %broadcast_select_fusion.4.refs_1_), channel_id=1, source_target_pairs={{16,0},{17,1},{18,2},{19,3},{20,4},{21,5},{22,6},{23,7},{24,8},{25... | collective-permute-start | bytes 3145736 | tf_op jit(solution)/shard_map/ppermute | solution.py:883
  1511.4 13.6 collective-permute-done.96
  1526.3 21.2 %collective-permute-done.101 = bf16[2,256,1024]{2,1,0:T(8,128)(2,1)S(1)} collective-permute-done((bf16[2,256,1024]{2,1,0:T(8,128)(2,1)S(1)}, bf16[2,256,1024]{2,1,0:T(8,128)(2,1)S(1)}, u32[]{:S(2)}, u32[]{:S(2)}) %collective-permute-start.101) | collective-permute-done | bytes 1048608 | tf_op jit(solution)/shard_map/ppermute | solution.py:526
  1555.4 18.2 %collective-permute-start.122 = (bf16[2,256,1024]{2,1,0:T(8,128)(2,1)}, bf16[2,256,1024]{2,1,0:T(8,128)(2,1)}, u32[]{:S(2)}, u32[]{:S(2)}) collective-permute-start(bf16[2,256,1024]{2,1,0:T(8,128)(2,1)} %broadcast_select_fusion.13.refs_0_), channel_id=1, source_target_pairs={{16,0},{17,1},{18,2},{19,3},{20,4},{21,5},{22,6},{23,7},{24,8},{25... | collective-permute-start | bytes 3145736 | tf_op jit(solution)/shard_map/ppermute | solution.py:883
  1598.7 8.3 place_gradient.3
  1607.1 18.2 %place_gradient.2 = f32[512,8512]{1,0:T(8,128)} custom-call(s32[2]{0:T(128)S(1)} %pad_add_fusion.ids, bf16[2,256,1024]{2,1,0:T(8,128)(2,1)} %broadcast_select_fusion.13.refs_0_, bf16[2,256,1024]{2,1,0:T(8,128)(2,1)} %broadcast_select_fusion.12.refs_1_, bf16[2,256,1024]{2,1,0:T(8,128)(2,1)} %broadcast_select_fusion.11.refs_2_, ...), custom_call_target="tpu_custom_call" | custom-call | tf_op jit(solution)/shard_map/place_gradient/pallas_call | solution.py:413
  1625.3 18.0 %copy.61 = f32[1,512,8512]{1,2,0:T(8,128)} copy(f32[1,512,8512]{2,1,0:T(8,128)} %bitcast.184) | data formatting | bytes 34865152
  (1030 shorter events, 474.9 us)
Async XLA Ops:
  7.2 889.5 %all-reduce.3.cloned.1.call-start = ((), (), s32[]{:S(2)}) async-start(), calls=%async_computation | async-start | bytes 458752 | tf_op jit(solution)/shard_map/psum | solution.py:865
  21.8 40.1 %collective-permute-start.9 = (bf16[256,8512]{0,1:T(8,128)(2,1)}, bf16[256,8512]{0,1:T(8,128)(2,1)}, u32[]{:S(2)}, u32[]{:S(2)}) collective-permute-start(bf16[256,8512]{0,1:T(8,128)(2,1)} %get-tuple-element.164), channel_id=1, source_target_pairs={{0,16},{16,0},{1,17},{17,1},{2,18},{18,2},{3,19},{19,3},{4,20},{20... | collective-permute-start | bytes 13074440 | tf_op jit(solution)/shard_map/ppermute | solution.py:430
  65.9 67.2 %collective-permute-start.10 = (bf16[256,2048]{0,1:T(8,128)(2,1)S(1)}, bf16[256,2048]{0,1:T(8,128)(2,1)S(1)}, u32[]{:S(2)}, u32[]{:S(2)}) collective-permute-start(bf16[256,2048]{0,1:T(8,128)(2,1)S(1)} %get-tuple-element.224), channel_id=1, source_target_pairs={{0,1},{1,0},{2,3},{3,2},{4,5},{5,4},{6,7},{7,6},{8,9},{9,8},{10,11... | collective-permute-start | bytes 3145736 | tf_op jit(solution)/shard_map/ppermute | solution.py:435
  72.4 60.6 %collective-permute-start.11 = (bf16[256,2048]{0,1:T(8,128)(2,1)S(1)}, bf16[256,2048]{0,1:T(8,128)(2,1)S(1)}, u32[]{:S(2)}, u32[]{:S(2)}) collective-permute-start(bf16[256,2048]{0,1:T(8,128)(2,1)S(1)} %get-tuple-element.222), channel_id=1, source_target_pairs={{0,2},{1,3},{2,0},{3,1},{4,6},{5,7},{6,4},{7,5},{8,10},{9,11},{10,... | collective-permute-start | bytes 3145736 | tf_op jit(solution)/shard_map/ppermute | solution.py:435
  75.6 51.7 %collective-permute-start.18 = (bf16[256,272]{0,1:T(8,128)(2,1)S(1)}, bf16[256,272]{0,1:T(8,128)(2,1)S(1)}, u32[]{:S(2)}, u32[]{:S(2)}) collective-permute-start(bf16[256,272]{0,1:T(8,128)(2,1)S(1)} %get-tuple-element.279), channel_id=1, source_target_pairs={{0,2},{1,3},{2,0},{3,1},{4,6},{5,7},{6,4},{7,5},{8,10},{9,11},{10,... | collective-permute-start | bytes 417800 | tf_op jit(solution)/shard_map/ppermute | solution.py:435
  77.1 56.0 %collective-permute-start.12 = (bf16[256,2048]{0,1:T(8,128)(2,1)S(1)}, bf16[256,2048]{0,1:T(8,128)(2,1)S(1)}, u32[]{:S(2)}, u32[]{:S(2)}) collective-permute-start(bf16[256,2048]{0,1:T(8,128)(2,1)S(1)} %get-tuple-element.220), channel_id=1, source_target_pairs={{0,3},{1,2},{2,1},{3,0},{4,7},{5,6},{6,5},{7,4},{8,11},{9,10},{10,... | collective-permute-start | bytes 3145736 | tf_op jit(solution)/shard_map/ppermute | solution.py:435
  130.5 39.1 %collective-permute-start.1 = (bf16[128,2048]{1,0:T(8,128)(2,1)S(1)}, bf16[128,2048]{1,0:T(8,128)(2,1)S(1)}, u32[]{:S(2)}, u32[]{:S(2)}) collective-permute-start(bf16[128,2048]{1,0:T(8,128)(2,1)S(1)} %copy-done.65), channel_id=1, source_target_pairs={{0,0},{1,4},{2,8},{3,12},{4,1},{5,5},{6,9},{7,13},{8,2},{9,6},{10,... | collective-permute-start | bytes 1572872 | tf_op jit(solution)/shard_map/ppermute | solution.py:446
  145.2 155.4 %collective-permute-start.37 = (bf16[256,2048]{0,1:T(8,128)(2,1)S(1)}, bf16[256,2048]{0,1:T(8,128)(2,1)S(1)}, u32[]{:S(2)}, u32[]{:S(2)}) collective-permute-start(bf16[256,2048]{0,1:T(8,128)(2,1)S(1)} %get-tuple-element.71), channel_id=1, source_target_pairs={{0,16},{16,0},{1,17},{17,1},{2,18},{18,2},{3,19},{19,3},{4,20},{20... | collective-permute-start | bytes 3145736 | tf_op jit(solution)/shard_map/ppermute | solution.py:430
  159.0 146.9 %collective-permute-start.27 = (bf16[1024,2048]{1,0:T(8,128)(2,1)S(1)}, bf16[1024,2048]{1,0:T(8,128)(2,1)}, u32[]{:S(2)}, u32[]{:S(2)}) collective-permute-start(bf16[1024,2048]{1,0:T(8,128)(2,1)S(1)} %bitcast.222), channel_id=1, source_target_pairs={{0,16},{16,0},{1,17},{17,1},{2,18},{18,2},{3,19},{19,3},{4,20},{20... | collective-permute-start | bytes 12582920 | tf_op jit(solution)/shard_map/ppermute | solution.py:430
  159.9 120.2 %collective-permute-start.34 = (bf16[256,2048]{0,1:T(8,128)(2,1)}, bf16[256,2048]{0,1:T(8,128)(2,1)}, u32[]{:S(2)}, u32[]{:S(2)}) collective-permute-start(bf16[256,2048]{0,1:T(8,128)(2,1)} %get-tuple-element.72), channel_id=1, source_target_pairs={{0,1},{1,0},{2,3},{3,2},{4,5},{5,4},{6,7},{7,6},{8,9},{9,8},{10,11... | collective-permute-start | bytes 3145736 | tf_op jit(solution)/shard_map/ppermute | solution.py:435
  169.9 55.4 %collective-permute-start.4 = (bf16[128,2048]{1,0:T(8,128)(2,1)S(1)}, bf16[128,2048]{1,0:T(8,128)(2,1)S(1)}, u32[]{:S(2)}, u32[]{:S(2)}) collective-permute-start(bf16[128,2048]{1,0:T(8,128)(2,1)S(1)} %constant_dynamic-update-slice_fusion), channel_id=1, source_target_pairs={{0,3},{1,2},{2,1},{3,0},{4,7},{5,6},{6,5},{7,4},{8,11},{9,10},{10,... | collective-permute-start | bytes 1572872 | tf_op jit(solution)/shard_map/ppermute | solution.py:435
  177.7 49.4 %collective-permute-start.3 = (bf16[128,2048]{1,0:T(8,128)(2,1)S(1)}, bf16[128,2048]{1,0:T(8,128)(2,1)S(1)}, u32[]{:S(2)}, u32[]{:S(2)}) collective-permute-start(bf16[128,2048]{1,0:T(8,128)(2,1)S(1)} %constant_dynamic-update-slice_fusion), channel_id=1, source_target_pairs={{0,2},{1,3},{2,0},{3,1},{4,6},{5,7},{6,4},{7,5},{8,10},{9,11},{10,... | collective-permute-start | bytes 1572872 | tf_op jit(solution)/shard_map/ppermute | solution.py:435
  245.2 48.1 %collective-permute-start.35 = (bf16[256,2048]{0,1:T(8,128)(2,1)}, bf16[256,2048]{0,1:T(8,128)(2,1)}, u32[]{:S(2)}, u32[]{:S(2)}) collective-permute-start(bf16[256,2048]{0,1:T(8,128)(2,1)} %get-tuple-element.73), channel_id=1, source_target_pairs={{0,2},{1,3},{2,0},{3,1},{4,6},{5,7},{6,4},{7,5},{8,10},{9,11},{10,... | collective-permute-start | bytes 3145736 | tf_op jit(solution)/shard_map/ppermute | solution.py:435
  248.8 48.0 %collective-permute-start.36 = (bf16[256,2048]{0,1:T(8,128)(2,1)}, bf16[256,2048]{0,1:T(8,128)(2,1)}, u32[]{:S(2)}, u32[]{:S(2)}) collective-permute-start(bf16[256,2048]{0,1:T(8,128)(2,1)} %get-tuple-element.74), channel_id=1, source_target_pairs={{0,3},{1,2},{2,1},{3,0},{4,7},{5,6},{6,5},{7,4},{8,11},{9,10},{10,... | collective-permute-start | bytes 3145736 | tf_op jit(solution)/shard_map/ppermute | solution.py:435
  344.8 38.1 %collective-permute-start.51 = (bf16[128,2048]{1,0:T(8,128)(2,1)S(1)}, bf16[128,2048]{1,0:T(8,128)(2,1)S(1)}, u32[]{:S(2)}, u32[]{:S(2)}) collective-permute-start(bf16[128,2048]{1,0:T(8,128)(2,1)S(1)} %get-tuple-element.375), channel_id=1, source_target_pairs={{0,3},{1,2},{2,1},{3,0},{4,7},{5,6},{6,5},{7,4},{8,11},{9,10},{10,... | collective-permute-start | bytes 1572872 | tf_op jit(solution)/shard_map/ppermute | solution.py:435
  344.8 44.5 %collective-permute-start.50 = (bf16[128,2048]{1,0:T(8,128)(2,1)S(1)}, bf16[128,2048]{1,0:T(8,128)(2,1)S(1)}, u32[]{:S(2)}, u32[]{:S(2)}) collective-permute-start(bf16[128,2048]{1,0:T(8,128)(2,1)S(1)} %get-tuple-element.375), channel_id=1, source_target_pairs={{0,2},{1,3},{2,0},{3,1},{4,6},{5,7},{6,4},{7,5},{8,10},{9,11},{10,... | collective-permute-start | bytes 1572872 | tf_op jit(solution)/shard_map/ppermute | solution.py:435
  355.6 35.0 %collective-permute-start.49 = (bf16[128,2048]{1,0:T(8,128)(2,1)S(1)}, bf16[128,2048]{1,0:T(8,128)(2,1)S(1)}, u32[]{:S(2)}, u32[]{:S(2)}) collective-permute-start(bf16[128,2048]{1,0:T(8,128)(2,1)S(1)} %get-tuple-element.375), channel_id=1, source_target_pairs={{0,1},{1,0},{2,3},{3,2},{4,5},{5,4},{6,7},{7,6},{8,9},{9,8},{10,11... | collective-permute-start | bytes 1572872 | tf_op jit(solution)/shard_map/ppermute | solution.py:435
  477.0 49.0 %collective-permute-start.57 = (bf16[128,2048]{1,0:T(8,128)(2,1)}, bf16[128,2048]{1,0:T(8,128)(2,1)}, u32[]{:S(2)}, u32[]{:S(2)}) collective-permute-start(bf16[128,2048]{1,0:T(8,128)(2,1)} %get-tuple-element.211), channel_id=1, source_target_pairs={{0,3},{1,2},{2,1},{3,0},{4,7},{5,6},{6,5},{7,4},{8,11},{9,10},{10,... | collective-permute-start | bytes 1572872 | tf_op jit(solution)/shard_map/ppermute | solution.py:435
  478.6 56.7 %collective-permute-start.56 = (bf16[128,2048]{1,0:T(8,128)(2,1)}, bf16[128,2048]{1,0:T(8,128)(2,1)}, u32[]{:S(2)}, u32[]{:S(2)}) collective-permute-start(bf16[128,2048]{1,0:T(8,128)(2,1)} %get-tuple-element.212), channel_id=1, source_target_pairs={{0,2},{1,3},{2,0},{3,1},{4,6},{5,7},{6,4},{7,5},{8,10},{9,11},{10,... | collective-permute-start | bytes 1572872 | tf_op jit(solution)/shard_map/ppermute | solution.py:435
  518.4 63.1 %collective-permute-start.154 = (bf16[1024,512]{1,0:T(8,128)(2,1)}, bf16[1024,512]{1,0:T(8,128)(2,1)}, u32[]{:S(2)}, u32[]{:S(2)}) collective-permute-start(bf16[1024,512]{1,0:T(8,128)(2,1)} %convolution_convert_fusion.5), channel_id=1, source_target_pairs={{0,16},{16,0},{1,17},{17,1},{2,18},{18,2},{3,19},{19,3},{4,20},{20... | collective-permute-start | bytes 3145736 | tf_op jit(solution)/shard_map/ppermute | solution.py:430
  524.7 60.4 %collective-permute-start.158 = (bf16[1024,512]{1,0:T(8,128)(2,1)}, bf16[1024,512]{1,0:T(8,128)(2,1)}, u32[]{:S(2)}, u32[]{:S(2)}) collective-permute-start(bf16[1024,512]{1,0:T(8,128)(2,1)} %convolution_convert_fusion.4), channel_id=1, source_target_pairs={{0,16},{16,0},{1,17},{17,1},{2,18},{18,2},{3,19},{19,3},{4,20},{20... | collective-permute-start | bytes 3145736 | tf_op jit(solution)/shard_map/ppermute | solution.py:430
  574.1 346.7 %collective-permute-start.102 = (bf16[1024,1024]{1,0:T(8,128)(2,1)}, bf16[1024,1024]{1,0:T(8,128)(2,1)}, u32[]{:S(2)}, u32[]{:S(2)}) collective-permute-start(bf16[1024,1024]{1,0:T(8,128)(2,1)} %convolution_convert_fusion.1), channel_id=1, source_target_pairs={{0,16},{16,0},{1,17},{17,1},{2,18},{18,2},{3,19},{19,3},{4,20},{20... | collective-permute-start | bytes 6291464 | tf_op jit(solution)/shard_map/ppermute | solution.py:430
  585.1 109.8 %collective-permute-start.59 = (bf16[128,2048]{1,0:T(8,128)(2,1)}, bf16[128,2048]{1,0:T(8,128)(2,1)}, u32[]{:S(2)}, u32[]{:S(2)}) collective-permute-start(bf16[128,2048]{1,0:T(8,128)(2,1)} %constant_dynamic-update-slice_fusion.136), channel_id=1, source_target_pairs={{0,0},{1,4},{2,8},{3,12},{4,1},{5,5},{6,9},{7,13},{8,2},{9,6},{10,... | collective-permute-start | bytes 1572872 | tf_op jit(solution)/shard_map/ppermute | solution.py:446
  694.9 230.5 %collective-permute-start.112 = (bf16[1024,1024]{1,0:T(8,128)(2,1)}, bf16[1024,1024]{1,0:T(8,128)(2,1)}, u32[]{:S(2)}, u32[]{:S(2)}) collective-permute-start(bf16[1024,1024]{1,0:T(8,128)(2,1)} %convolution_convert_fusion), channel_id=1, source_target_pairs={{0,16},{16,0},{1,17},{17,1},{2,18},{18,2},{3,19},{19,3},{4,20},{20... | collective-permute-start | bytes 6291464 | tf_op jit(solution)/shard_map/ppermute | solution.py:430
  715.3 187.1 %collective-permute-start.143 = (bf16[4,256,80]{1,2,0:T(8,128)(2,1)S(1)}, bf16[4,256,80]{1,2,0:T(8,128)(2,1)}, u32[]{:S(2)}, u32[]{:S(2)}) collective-permute-start(bf16[4,256,80]{1,2,0:T(8,128)(2,1)S(1)} %copy-done.59), channel_id=1, source_target_pairs={{4,0},{8,12},{5,1},{9,13},{6,2},{10,14},{7,3},{11,15},{20,16},{24,... | collective-permute-start | bytes 491528 | tf_op jit(solution)/shard_map/ppermute | solution.py:526
  718.4 42.8 %collective-permute-start.77 = (bf16[128,2048]{1,0:T(8,128)(2,1)S(1)}, bf16[128,2048]{1,0:T(8,128)(2,1)S(1)}, u32[]{:S(2)}, u32[]{:S(2)}) collective-permute-start(bf16[128,2048]{1,0:T(8,128)(2,1)S(1)} %get-tuple-element.209), channel_id=1, source_target_pairs={{0,2},{1,3},{2,0},{3,1},{4,6},{5,7},{6,4},{7,5},{8,10},{9,11},{10,... | collective-permute-start | bytes 1572872 | tf_op jit(solution)/shard_map/ppermute | solution.py:435
  761.2 153.2 %collective-permute-start.155 = (bf16[1024,512]{1,0:T(8,128)(2,1)}, bf16[1024,512]{1,0:T(8,128)(2,1)}, u32[]{:S(2)}, u32[]{:S(2)}) collective-permute-start(bf16[1024,512]{1,0:T(8,128)(2,1)} %add_convert_fusion.9), channel_id=1, source_target_pairs={{0,4},{12,8},{1,5},{13,9},{2,6},{14,10},{3,7},{15,11},{16,20},{28,... | collective-permute-start | bytes 3145736 | tf_op jit(solution)/shard_map/ppermute | solution.py:523
  773.5 142.9 %collective-permute-start.159 = (bf16[1024,512]{1,0:T(8,128)(2,1)}, bf16[1024,512]{1,0:T(8,128)(2,1)}, u32[]{:S(2)}, u32[]{:S(2)}) collective-permute-start(bf16[1024,512]{1,0:T(8,128)(2,1)} %add_convert_fusion.6), channel_id=1, source_target_pairs={{0,4},{12,8},{1,5},{13,9},{2,6},{14,10},{3,7},{15,11},{16,20},{28,... | collective-permute-start | bytes 3145736 | tf_op jit(solution)/shard_map/ppermute | solution.py:523
  931.2 72.2 %collective-permute-start.82 = (bf16[1024,1024]{1,0:T(8,128)(2,1)S(1)}, bf16[1024,1024]{1,0:T(8,128)(2,1)S(1)}, u32[]{:S(2)}, u32[]{:S(2)}) collective-permute-start(bf16[1024,1024]{1,0:T(8,128)(2,1)S(1)} %copy-done.119), channel_id=1, source_target_pairs={{0,16},{16,0},{1,17},{17,1},{2,18},{18,2},{3,19},{19,3},{4,20},{20... | collective-permute-start | bytes 6291464 | tf_op jit(solution)/shard_map/ppermute | solution.py:430
  937.8 34.6 %collective-permute-start.118 = (bf16[256,1024]{1,0:T(8,128)(2,1)S(1)}, bf16[256,1024]{1,0:T(8,128)(2,1)S(1)}, u32[]{:S(2)}, u32[]{:S(2)}) collective-permute-start(bf16[256,1024]{1,0:T(8,128)(2,1)S(1)} %get-tuple-element.190), channel_id=1, source_target_pairs={{0,3},{1,2},{2,1},{3,0},{4,7},{5,6},{6,5},{7,4},{8,11},{9,10},{10,... | collective-permute-start | bytes 1572872 | tf_op jit(solution)/shard_map/ppermute | solution.py:435
  949.9 56.2 %collective-permute-start.92 = (bf16[1024,1024]{1,0:T(8,128)(2,1)S(1)}, bf16[1024,1024]{1,0:T(8,128)(2,1)S(1)}, u32[]{:S(2)}, u32[]{:S(2)}) collective-permute-start(bf16[1024,1024]{1,0:T(8,128)(2,1)S(1)} %copy-done.118), channel_id=1, source_target_pairs={{0,16},{16,0},{1,17},{17,1},{2,18},{18,2},{3,19},{19,3},{4,20},{20... | collective-permute-start | bytes 6291464 | tf_op jit(solution)/shard_map/ppermute | solution.py:430
  985.2 42.0 %collective-permute-start.151 = (bf16[1024,512]{1,0:T(8,128)(2,1)S(1)}, bf16[1024,512]{1,0:T(8,128)(2,1)S(1)}, u32[]{:S(2)}, u32[]{:S(2)}) collective-permute-start(bf16[1024,512]{1,0:T(8,128)(2,1)S(1)} %add_convert_fusion.12), channel_id=1, source_target_pairs={{0,4},{12,8},{1,5},{13,9},{2,6},{14,10},{3,7},{15,11},{16,20},{28,... | collective-permute-start | bytes 3145736 | tf_op jit(solution)/shard_map/ppermute | solution.py:523
  986.9 62.8 %collective-permute-start.104 = (bf16[2,256,1024]{2,1,0:T(8,128)(2,1)S(1)}, bf16[2,256,1024]{2,1,0:T(8,128)(2,1)S(1)}, u32[]{:S(2)}, u32[]{:S(2)}) collective-permute-start(bf16[2,256,1024]{2,1,0:T(8,128)(2,1)S(1)} %pad_maximum_fusion.18), channel_id=1, source_target_pairs={{0,4},{12,8},{1,5},{13,9},{2,6},{14,10},{3,7},{15,11},{16,20},{28,... | collective-permute-start | bytes 3145736 | tf_op jit(solution)/shard_map/ppermute | solution.py:523
  1003.4 68.8 %collective-permute-start.109 = (bf16[2,256,1024]{2,1,0:T(8,128)(2,1)S(1)}, bf16[2,256,1024]{2,1,0:T(8,128)(2,1)S(1)}, u32[]{:S(2)}, u32[]{:S(2)}) collective-permute-start(bf16[2,256,1024]{2,1,0:T(8,128)(2,1)S(1)} %pad_maximum_fusion.19), channel_id=1, source_target_pairs={{0,4},{12,8},{1,5},{13,9},{2,6},{14,10},{3,7},{15,11},{16,20},{28,... | collective-permute-start | bytes 3145736 | tf_op jit(solution)/shard_map/ppermute | solution.py:523
  1006.1 88.5 %collective-permute-start.114 = (bf16[2,256,1024]{2,1,0:T(8,128)(2,1)S(1)}, bf16[2,256,1024]{2,1,0:T(8,128)(2,1)S(1)}, u32[]{:S(2)}, u32[]{:S(2)}) collective-permute-start(bf16[2,256,1024]{2,1,0:T(8,128)(2,1)S(1)} %pad_maximum_fusion.20), channel_id=1, source_target_pairs={{0,4},{12,8},{1,5},{13,9},{2,6},{14,10},{3,7},{15,11},{16,20},{28,... | collective-permute-start | bytes 3145736 | tf_op jit(solution)/shard_map/ppermute | solution.py:523
  1009.3 107.9 %collective-permute-start.119 = (bf16[2,256,1024]{2,1,0:T(8,128)(2,1)S(1)}, bf16[2,256,1024]{2,1,0:T(8,128)(2,1)S(1)}, u32[]{:S(2)}, u32[]{:S(2)}) collective-permute-start(bf16[2,256,1024]{2,1,0:T(8,128)(2,1)S(1)} %pad_maximum_fusion.21), channel_id=1, source_target_pairs={{0,4},{12,8},{1,5},{13,9},{2,6},{14,10},{3,7},{15,11},{16,20},{28,... | collective-permute-start | bytes 3145736 | tf_op jit(solution)/shard_map/ppermute | solution.py:523
  1027.3 112.4 %collective-permute-start.157 = (bf16[1024,512]{1,0:T(8,128)(2,1)S(1)}, bf16[1024,512]{1,0:T(8,128)(2,1)S(1)}, u32[]{:S(2)}, u32[]{:S(2)}) collective-permute-start(bf16[1024,512]{1,0:T(8,128)(2,1)S(1)} %add_convert_fusion.7), channel_id=1, source_target_pairs={{4,0},{8,12},{5,1},{9,13},{6,2},{10,14},{7,3},{11,15},{20,16},{24,... | collective-permute-start | bytes 3145736 | tf_op jit(solution)/shard_map/ppermute | solution.py:526
  1049.7 67.7 %collective-permute-start.83 = (bf16[256,1024]{1,0:T(8,128)(2,1)S(1)}, bf16[256,1024]{1,0:T(8,128)(2,1)S(1)}, u32[]{:S(2)}, u32[]{:S(2)}) collective-permute-start(bf16[256,1024]{1,0:T(8,128)(2,1)S(1)} %get-tuple-element.203), channel_id=1, source_target_pairs={{0,1},{1,0},{2,3},{3,2},{4,5},{5,4},{6,7},{7,6},{8,9},{9,8},{10,11... | collective-permute-start | bytes 1572872 | tf_op jit(solution)/shard_map/ppermute | solution.py:435
  1072.2 46.4 %collective-permute-start.88 = (bf16[256,1024]{1,0:T(8,128)(2,1)S(1)}, bf16[256,1024]{1,0:T(8,128)(2,1)S(1)}, u32[]{:S(2)}, u32[]{:S(2)}) collective-permute-start(bf16[256,1024]{1,0:T(8,128)(2,1)S(1)} %get-tuple-element.202), channel_id=1, source_target_pairs={{0,3},{1,2},{2,1},{3,0},{4,7},{5,6},{6,5},{7,4},{8,11},{9,10},{10,... | collective-permute-start | bytes 1572872 | tf_op jit(solution)/shard_map/ppermute | solution.py:435
  1139.0 54.9 %collective-permute-start.105 = (bf16[2,256,1024]{2,1,0:T(8,128)(2,1)S(1)}, bf16[2,256,1024]{2,1,0:T(8,128)(2,1)S(1)}, u32[]{:S(2)}, u32[]{:S(2)}) collective-permute-start(bf16[2,256,1024]{2,1,0:T(8,128)(2,1)S(1)} %add_convert_fusion.23), channel_id=1, source_target_pairs={{4,8},{8,4},{5,9},{9,5},{6,10},{10,6},{7,11},{11,7},{20,24},{24,20... | collective-permute-start | bytes 3145736 | tf_op jit(solution)/shard_map/ppermute | solution.py:524
  1139.7 76.7 %collective-permute-start.110 = (bf16[2,256,1024]{2,1,0:T(8,128)(2,1)S(1)}, bf16[2,256,1024]{2,1,0:T(8,128)(2,1)S(1)}, u32[]{:S(2)}, u32[]{:S(2)}) collective-permute-start(bf16[2,256,1024]{2,1,0:T(8,128)(2,1)S(1)} %add_convert_fusion.21), channel_id=1, source_target_pairs={{4,8},{8,4},{5,9},{9,5},{6,10},{10,6},{7,11},{11,7},{20,24},{24,20... | collective-permute-start | bytes 3145736 | tf_op jit(solution)/shard_map/ppermute | solution.py:524
  1142.6 98.2 %collective-permute-start.79 = (f32[128,2048]{1,0:T(8,128)S(1)}, f32[128,2048]{1,0:T(8,128)S(1)}, u32[]{:S(2)}, u32[]{:S(2)}) collective-permute-start(f32[128,2048]{1,0:T(8,128)S(1)} %copy-done.105), channel_id=1, source_target_pairs={{0,0},{1,4},{2,8},{3,12},{4,1},{5,5},{6,9},{7,13},{8,2},{9,6},{10,... | collective-permute-start | bytes 3145736 | tf_op jit(solution)/shard_map/ppermute | solution.py:446
  1143.4 98.7 %collective-permute-start.84 = (bf16[2,256,1024]{2,1,0:T(8,128)(2,1)S(1)}, bf16[2,256,1024]{2,1,0:T(8,128)(2,1)S(1)}, u32[]{:S(2)}, u32[]{:S(2)}) collective-permute-start(bf16[2,256,1024]{2,1,0:T(8,128)(2,1)S(1)} %pad_maximum_fusion.14), channel_id=1, source_target_pairs={{0,4},{12,8},{1,5},{13,9},{2,6},{14,10},{3,7},{15,11},{16,20},{28,... | collective-permute-start | bytes 3145736 | tf_op jit(solution)/shard_map/ppermute | solution.py:523
  1154.6 88.2 %collective-permute-start.89 = (bf16[2,256,1024]{2,1,0:T(8,128)(2,1)S(1)}, bf16[2,256,1024]{2,1,0:T(8,128)(2,1)S(1)}, u32[]{:S(2)}, u32[]{:S(2)}) collective-permute-start(bf16[2,256,1024]{2,1,0:T(8,128)(2,1)S(1)} %pad_maximum_fusion.15), channel_id=1, source_target_pairs={{0,4},{12,8},{1,5},{13,9},{2,6},{14,10},{3,7},{15,11},{16,20},{28,... | collective-permute-start | bytes 3145736 | tf_op jit(solution)/shard_map/ppermute | solution.py:523
  1193.9 49.6 %collective-permute-start.94 = (bf16[2,256,1024]{2,1,0:T(8,128)(2,1)S(1)}, bf16[2,256,1024]{2,1,0:T(8,128)(2,1)S(1)}, u32[]{:S(2)}, u32[]{:S(2)}) collective-permute-start(bf16[2,256,1024]{2,1,0:T(8,128)(2,1)S(1)} %pad_maximum_fusion.16), channel_id=1, source_target_pairs={{0,4},{12,8},{1,5},{13,9},{2,6},{14,10},{3,7},{15,11},{16,20},{28,... | collective-permute-start | bytes 3145736 | tf_op jit(solution)/shard_map/ppermute | solution.py:523
  1216.4 42.2 %collective-permute-start.99 = (bf16[2,256,1024]{2,1,0:T(8,128)(2,1)S(1)}, bf16[2,256,1024]{2,1,0:T(8,128)(2,1)S(1)}, u32[]{:S(2)}, u32[]{:S(2)}) collective-permute-start(bf16[2,256,1024]{2,1,0:T(8,128)(2,1)S(1)} %pad_maximum_fusion.17), channel_id=1, source_target_pairs={{0,4},{12,8},{1,5},{13,9},{2,6},{14,10},{3,7},{15,11},{16,20},{28,... | collective-permute-start | bytes 3145736 | tf_op jit(solution)/shard_map/ppermute | solution.py:523
  1243.6 105.4 %collective-permute-start.149 = (bf16[1024,512]{1,0:T(8,128)(2,1)S(1)}, bf16[1024,512]{1,0:T(8,128)(2,1)S(1)}, u32[]{:S(2)}, u32[]{:S(2)}) collective-permute-start(bf16[1024,512]{1,0:T(8,128)(2,1)S(1)} %add_convert_fusion.13), channel_id=1, source_target_pairs={{4,0},{8,12},{5,1},{9,13},{6,2},{10,14},{7,3},{11,15},{20,16},{24,... | collective-permute-start | bytes 3145736 | tf_op jit(solution)/shard_map/ppermute | solution.py:526
  1258.5 112.9 %collective-permute-start.153 = (bf16[1024,512]{1,0:T(8,128)(2,1)S(1)}, bf16[1024,512]{1,0:T(8,128)(2,1)S(1)}, u32[]{:S(2)}, u32[]{:S(2)}) collective-permute-start(bf16[1024,512]{1,0:T(8,128)(2,1)S(1)} %add_convert_fusion.10), channel_id=1, source_target_pairs={{4,0},{8,12},{5,1},{9,13},{6,2},{10,14},{7,3},{11,15},{20,16},{24,... | collective-permute-start | bytes 3145736 | tf_op jit(solution)/shard_map/ppermute | solution.py:526
  1261.6 112.2 %collective-permute-start.81 = (f32[128,2048]{1,0:T(8,128)S(1)}, f32[128,2048]{1,0:T(8,128)S(1)}, u32[]{:S(2)}, u32[]{:S(2)}) collective-permute-start(f32[128,2048]{1,0:T(8,128)S(1)} %collective-permute-done.80), channel_id=1, source_target_pairs={{0,16},{16,0},{1,17},{17,1},{2,18},{18,2},{3,19},{19,3},{4,20},{20... | collective-permute-start | bytes 3145736 | tf_op jit(solution)/shard_map/ppermute | solution.py:430
  1273.3 102.0 %collective-permute-start.85 = (bf16[2,256,1024]{2,1,0:T(8,128)(2,1)S(1)}, bf16[2,256,1024]{2,1,0:T(8,128)(2,1)S(1)}, u32[]{:S(2)}, u32[]{:S(2)}) collective-permute-start(bf16[2,256,1024]{2,1,0:T(8,128)(2,1)S(1)} %add_convert_fusion.31), channel_id=1, source_target_pairs={{4,8},{8,4},{5,9},{9,5},{6,10},{10,6},{7,11},{11,7},{20,24},{24,20... | collective-permute-start | bytes 3145736 | tf_op jit(solution)/shard_map/ppermute | solution.py:524
  1274.0 102.5 %collective-permute-start.90 = (bf16[2,256,1024]{2,1,0:T(8,128)(2,1)S(1)}, bf16[2,256,1024]{2,1,0:T(8,128)(2,1)S(1)}, u32[]{:S(2)}, u32[]{:S(2)}) collective-permute-start(bf16[2,256,1024]{2,1,0:T(8,128)(2,1)S(1)} %add_convert_fusion.29), channel_id=1, source_target_pairs={{4,8},{8,4},{5,9},{9,5},{6,10},{10,6},{7,11},{11,7},{20,24},{24,20... | collective-permute-start | bytes 3145736 | tf_op jit(solution)/shard_map/ppermute | solution.py:524
  1377.8 55.3 %collective-permute-start.116 = (bf16[2,256,1024]{2,1,0:T(8,128)(2,1)S(1)}, bf16[2,256,1024]{2,1,0:T(8,128)(2,1)S(1)}, u32[]{:S(2)}, u32[]{:S(2)}) collective-permute-start(bf16[2,256,1024]{2,1,0:T(8,128)(2,1)S(1)} %add_convert_fusion.18), channel_id=1, source_target_pairs={{4,0},{8,12},{5,1},{9,13},{6,2},{10,14},{7,3},{11,15},{20,16},{24,... | collective-permute-start | bytes 3145736 | tf_op jit(solution)/shard_map/ppermute | solution.py:526
  1379.2 78.4 %collective-permute-start.121 = (bf16[2,256,1024]{2,1,0:T(8,128)(2,1)S(1)}, bf16[2,256,1024]{2,1,0:T(8,128)(2,1)S(1)}, u32[]{:S(2)}, u32[]{:S(2)}) collective-permute-start(bf16[2,256,1024]{2,1,0:T(8,128)(2,1)S(1)} %add_convert_fusion.16), channel_id=1, source_target_pairs={{4,0},{8,12},{5,1},{9,13},{6,2},{10,14},{7,3},{11,15},{20,16},{24,... | collective-permute-start | bytes 3145736 | tf_op jit(solution)/shard_map/ppermute | solution.py:526
  1383.1 77.5 %collective-permute-start.165 = (bf16[1024,512]{1,0:T(8,128)(2,1)S(1)}, bf16[1024,512]{1,0:T(8,128)(2,1)}, u32[]{:S(2)}, u32[]{:S(2)}) collective-permute-start(bf16[1024,512]{1,0:T(8,128)(2,1)S(1)} %broadcast_select_fusion.2.refs_3_), channel_id=1, source_target_pairs={{0,16},{1,17},{2,18},{3,19},{4,20},{5,21},{6,22},{7,23},{8,24},{9,... | collective-permute-start | bytes 3145736 | tf_op jit(solution)/shard_map/ppermute | solution.py:883
  1390.8 99.9 %collective-permute-start.86 = (bf16[2,256,1024]{2,1,0:T(8,128)(2,1)S(1)}, bf16[2,256,1024]{2,1,0:T(8,128)(2,1)S(1)}, u32[]{:S(2)}, u32[]{:S(2)}) collective-permute-start(bf16[2,256,1024]{2,1,0:T(8,128)(2,1)S(1)} %add_convert_fusion.30), channel_id=1, source_target_pairs={{4,0},{8,12},{5,1},{9,13},{6,2},{10,14},{7,3},{11,15},{20,16},{24,... | collective-permute-start | bytes 3145736 | tf_op jit(solution)/shard_map/ppermute | solution.py:526
  1410.7 99.4 %collective-permute-start.91 = (bf16[2,256,1024]{2,1,0:T(8,128)(2,1)S(1)}, bf16[2,256,1024]{2,1,0:T(8,128)(2,1)S(1)}, u32[]{:S(2)}, u32[]{:S(2)}) collective-permute-start(bf16[2,256,1024]{2,1,0:T(8,128)(2,1)S(1)} %add_convert_fusion.28), channel_id=1, source_target_pairs={{4,0},{8,12},{5,1},{9,13},{6,2},{10,14},{7,3},{11,15},{20,16},{24,... | collective-permute-start | bytes 3145736 | tf_op jit(solution)/shard_map/ppermute | solution.py:526
  1433.2 91.8 %collective-permute-start.96 = (bf16[2,256,1024]{2,1,0:T(8,128)(2,1)S(1)}, bf16[2,256,1024]{2,1,0:T(8,128)(2,1)S(1)}, u32[]{:S(2)}, u32[]{:S(2)}) collective-permute-start(bf16[2,256,1024]{2,1,0:T(8,128)(2,1)S(1)} %add_convert_fusion.26), channel_id=1, source_target_pairs={{4,0},{8,12},{5,1},{9,13},{6,2},{10,14},{7,3},{11,15},{20,16},{24,... | collective-permute-start | bytes 3145736 | tf_op jit(solution)/shard_map/ppermute | solution.py:526
  1457.6 89.9 %collective-permute-start.101 = (bf16[2,256,1024]{2,1,0:T(8,128)(2,1)S(1)}, bf16[2,256,1024]{2,1,0:T(8,128)(2,1)S(1)}, u32[]{:S(2)}, u32[]{:S(2)}) collective-permute-start(bf16[2,256,1024]{2,1,0:T(8,128)(2,1)S(1)} %add_convert_fusion.24), channel_id=1, source_target_pairs={{4,0},{8,12},{5,1},{9,13},{6,2},{10,14},{7,3},{11,15},{20,16},{24,... | collective-permute-start | bytes 3145736 | tf_op jit(solution)/shard_map/ppermute | solution.py:526
  1460.7 92.5 %collective-permute-start.162 = (bf16[1024,512]{1,0:T(8,128)(2,1)S(1)}, bf16[1024,512]{1,0:T(8,128)(2,1)S(1)}, u32[]{:S(2)}, u32[]{:S(2)}) collective-permute-start(bf16[1024,512]{1,0:T(8,128)(2,1)S(1)} %broadcast_select_fusion.5.refs_0_), channel_id=1, source_target_pairs={{16,0},{17,1},{18,2},{19,3},{20,4},{21,5},{22,6},{23,7},{24,8},{25... | collective-permute-start | bytes 3145736 | tf_op jit(solution)/shard_map/ppermute | solution.py:883
  1490.7 64.7 %collective-permute-start.163 = (bf16[1024,512]{1,0:T(8,128)(2,1)S(1)}, bf16[1024,512]{1,0:T(8,128)(2,1)S(1)}, u32[]{:S(2)}, u32[]{:S(2)}) collective-permute-start(bf16[1024,512]{1,0:T(8,128)(2,1)S(1)} %broadcast_select_fusion.4.refs_1_), channel_id=1, source_target_pairs={{16,0},{17,1},{18,2},{19,3},{20,4},{21,5},{22,6},{23,7},{24,8},{25... | collective-permute-start | bytes 3145736 | tf_op jit(solution)/shard_map/ppermute | solution.py:883
  1510.1 63.5 %collective-permute-start.126 = (bf16[2,256,1024]{2,1,0:T(8,128)(2,1)S(1)}, bf16[2,256,1024]{2,1,0:T(8,128)(2,1)S(1)}, u32[]{:S(2)}, u32[]{:S(2)}) collective-permute-start(bf16[2,256,1024]{2,1,0:T(8,128)(2,1)S(1)} %broadcast_select_fusion.9.refs_4_), channel_id=1, source_target_pairs={{0,16},{1,17},{2,18},{3,19},{4,20},{5,21},{6,22},{7,23},{8,24},{9,... | collective-permute-start | bytes 3145736 | tf_op jit(solution)/shard_map/ppermute | solution.py:883
  1525.0 50.9 %collective-permute-start.127 = (bf16[2,256,1024]{2,1,0:T(8,128)(2,1)S(1)}, bf16[2,256,1024]{2,1,0:T(8,128)(2,1)S(1)}, u32[]{:S(2)}, u32[]{:S(2)}) collective-permute-start(bf16[2,256,1024]{2,1,0:T(8,128)(2,1)S(1)} %broadcast_select_fusion.8.refs_5_), channel_id=1, source_target_pairs={{0,16},{1,17},{2,18},{3,19},{4,20},{5,21},{6,22},{7,23},{8,24},{9,... | collective-permute-start | bytes 3145736 | tf_op jit(solution)/shard_map/ppermute | solution.py:883
  1554.1 52.9 %collective-permute-start.129 = (bf16[2,256,1024]{2,1,0:T(8,128)(2,1)}, bf16[2,256,1024]{2,1,0:T(8,128)(2,1)}, u32[]{:S(2)}, u32[]{:S(2)}) collective-permute-start(bf16[2,256,1024]{2,1,0:T(8,128)(2,1)} %broadcast_select_fusion.6.refs_7_), channel_id=1, source_target_pairs={{0,16},{1,17},{2,18},{3,19},{4,20},{5,21},{6,22},{7,23},{8,24},{9,... | collective-permute-start | bytes 3145736 | tf_op jit(solution)/shard_map/ppermute | solution.py:883
  1555.4 51.6 %collective-permute-start.122 = (bf16[2,256,1024]{2,1,0:T(8,128)(2,1)}, bf16[2,256,1024]{2,1,0:T(8,128)(2,1)}, u32[]{:S(2)}, u32[]{:S(2)}) collective-permute-start(bf16[2,256,1024]{2,1,0:T(8,128)(2,1)} %broadcast_select_fusion.13.refs_0_), channel_id=1, source_target_pairs={{16,0},{17,1},{18,2},{19,3},{20,4},{21,5},{22,6},{23,7},{24,8},{25... | collective-permute-start | bytes 3145736 | tf_op jit(solution)/shard_map/ppermute | solution.py:883
  (224 other events, 3674.7 us)
Sparse Core Ops, SparseCore 0:
  772.0 124.6 all-reduce.2

commit v3 on v2

v3 whole, which is shorter than its diff:
```python
import functools

import jax
import jax.numpy as jnp
from jax import lax
from jax.experimental import pallas as pl
from jax.experimental.pallas import tpu as pltpu
from jax.sharding import PartitionSpec as P

D = 2048
INNER = 4096
HEADS = 64
HEAD_DIM = 64
STATE = 128
KERNEL = 4
GROUP = 2 * STATE
CHANNELS = INNER + GROUP
LANES = 128
EPS = 1e-05
F32 = jnp.float32
BF16 = jnp.bfloat16
VMEM_BYTES = 48 * 1024 * 1024


def split(v):
    hi = v.astype(BF16)
    return hi, (v - hi.astype(F32)).astype(BF16)


def dot32(a, b, ca, cb):
    (ah, al), (bh, bl) = (v if isinstance(v, tuple) else split(v) for v in (a, b))
    one = lambda p, q: lax.dot_general(
        p, q, (((ca,), (cb,)), ((), ())), preferred_element_type=F32
    )
    return one(ah, bh) + (one(ah, bl) + one(al, bh))


def step_sizes(raw, hp, rows):
    shifted = raw + hp[0:1, :]
    dt = jnp.maximum(shifted, 0.0) + jnp.log1p(jnp.exp(-jnp.abs(shifted)))
    decay = dt * hp[1:2, :]
    row = lax.broadcasted_iota(jnp.int32, (rows, rows), 0)
    col = lax.broadcasted_iota(jnp.int32, (rows, rows), 1)
    lower = (row >= col).astype(F32)
    cum = dot32(lower, decay, 1, 0)
    cum_t = dot32(decay, lower, 0, 1)
    return shifted, dt, cum, cum_t, row, col, lower


def pair_lanes(v, j, first):
    return jnp.where(first, v[:, 2 * j : 2 * j + 1], v[:, 2 * j + 1 : 2 * j + 2])


def head_sums(v, table):
    hi, low = split(v)
    one = lambda p: lax.dot_general(
        p, table, (((1,), (1,)), ((), ())), preferred_element_type=F32
    )
    return one(hi) + one(low)


def forward_kernel(f_ref, proj, cw, hp, table, s0, e0, *rest, second):
    if second:
        dn, gain, y_ref, filt_ref, st_ref, stat_ref, state, xp, xw_s, last_s = rest
    else:
        y_ref, filt_ref, st_ref, stat_ref, state, xp, xw_s, last_s = rest
    i = pl.program_id(0)
    rows, width = y_ref.shape

    @pl.when(i == 0)
    def _():
        state[...] = s0[...]
        xp[0:8, :] = e0[...]

    xp[8 : 8 + rows, :] = proj[:, width : 2 * width + GROUP]

    def conv_tile(lo):
        acc = cw[4:5, lo : lo + LANES]
        for k in range(KERNEL):
            acc = acc + cw[k : k + 1, lo : lo + LANES] * xp[5 + k : 5 + k + rows, lo : lo + LANES]
        filt_ref[:, lo : lo + LANES] = acc
        return acc * jax.nn.sigmoid(acc)

    b_c = conv_tile(width)
    c_c = conv_tile(width + STATE)
    _, dt, cum, cum_t, row, col, _ = step_sizes(proj[:, 2 * width + GROUP :], hp, rows)
    last = cum[rows - 1 : rows, :]
    ecum = jnp.exp(cum)
    weight = jnp.exp(last - cum) * dt
    elast = jnp.exp(last)
    b_c, c_c = split(b_c), split(c_c)
    carried = dot32(c_c, state[...], 1, 0)
    scores = dot32(c_c, b_c, 1, 1)
    causal = row >= col
    lane = lax.broadcasted_iota(jnp.int32, (rows, LANES), 1)
    first = lane < HEAD_DIM
    ss = jnp.zeros((rows, LANES), F32)
    s2 = jnp.zeros((rows, LANES), F32)
    for j in range(width // LANES):
        lo = j * LANES
        here = slice(lo, lo + LANES)
        x = conv_tile(lo)
        xd = x * pair_lanes(dt, j, first)
        m = []
        for h in (2 * j, 2 * j + 1):
            gap = cum[:, h : h + 1] - cum_t[h : h + 1, :]
            m.append(jnp.exp(jnp.where(causal, gap, -1e30)) * scores)
        xd2 = jnp.concatenate([jnp.where(first, xd, 0.0), jnp.where(first, 0.0, xd)])
        y = (
            dot32(jnp.concatenate(m, axis=1), xd2, 1, 0)
            + carried[:, here] * pair_lanes(ecum, j, first)
            + pair_lanes(hp[2:3, :], j, first[0:1]) * x
        )
        y_ref[:, here] = y
        xw_s[:, here] = x * pair_lanes(weight, j, first)
        last_s[0:1, here] = pair_lanes(elast, j, first[0:1])
        z = proj[:, here]
        g = y * z * jax.nn.sigmoid(z)
        ss = ss + g * g
        if second:
            s2 = s2 + g * dn[:, here] * gain[0:1, here]
    state[...] = state[...] * last_s[0:1, :] + dot32(b_c, xw_s[...], 0, 0)
    st_ref[0] = state[...]
    xp[0:8, :] = xp[rows : rows + 8, :]
    ones = jnp.ones((8, LANES), F32)
    stat_ref[0, 0:1, :] = dot32(ones, ss, 1, 1)[0:1]
    stat_ref[0, 1:2, :] = dot32(ones, s2, 1, 1)[0:1]


def backward_kernel(
    f_ref,
    proj,
    y_ref,
    filt,
    dn,
    rc,
    st_before,
    st_out,
    s0,
    cw,
    hp,
    table,
    gain,
    g0,
    e0,
    dproj,
    dbc_ref,
    dgain_ref,
    dconv_ref,
    dhp_ref,
    gfin_ref,
    efin_ref,
    grad,
    dfp,
    both,
    xw_s,
    dyc_s,
    rowv,
):
    i = pl.program_id(0)
    rows, width = y_ref.shape
    heads = hp.shape[1]

    @pl.when(i == 0)
    def _():
        grad[...] = g0[...]
        dfp[rows : rows + 8, :] = e0[...]
        dgain_ref[...] = jnp.zeros_like(dgain_ref)
        dconv_ref[...] = jnp.zeros_like(dconv_ref)
        dhp_ref[...] = jnp.zeros_like(dhp_ref)

    def silu_pair(v):
        s = jax.nn.sigmoid(v)
        a = v * s
        return a, s * (1.0 + v - a)

    b_c, b_d = silu_pair(filt[:, width : width + STATE])
    c_c, c_d = silu_pair(filt[:, width + STATE :])
    shifted, dt, cum, cum_t, row, col, lower = step_sizes(proj[:, 2 * width + GROUP :], hp, rows)
    last = cum[rows - 1 : rows, :]
    tail = jnp.exp(last - cum)
    ecum = jnp.exp(cum)
    elast = jnp.exp(last)
    b_c, c_c = split(b_c), split(c_c)
    grad_p = split(grad[...])
    k_all = dot32(b_c, grad_p, 1, 0)
    scores_t = dot32(b_c, c_c, 1, 1)
    causal_t = row <= col
    lane = lax.broadcasted_iota(jnp.int32, (rows, LANES), 1)
    first = lane < HEAD_DIM
    dcb_t = jnp.zeros((rows, rows), F32)
    rc_t = dot32((row == col).astype(F32), rc[0], 1, 1)
    r = rc_t[:, 0:1]
    coef = rc_t[:, 1:2]
    rowv[0:1, :] = jnp.sum(grad[...] * st_out[0], axis=0, keepdims=True)
    for j in range(width // LANES):
        lo = j * LANES
        here = slice(lo, lo + LANES)
        z = proj[:, here]
        y = y_ref[:, here]
        sz, dsz = silu_pair(z)
        g = y * sz
        dnt = dn[:, here]
        dg = dnt * gain[0:1, here] * r - g * coef
        dgain_ref[0:1, here] += jnp.sum(dnt * g * r, axis=0, keepdims=True)
        dy = dg * sz
        dproj[:, here] = (dg * y * dsz).astype(BF16)
        x, xder = silu_pair(filt[:, here])
        dt_e = pair_lanes(dt, j, first)
        tail_e = pair_lanes(tail, j, first)
        xd = x * dt_e
        dy2 = split(jnp.concatenate([jnp.where(first, dy, 0.0), jnp.where(first, 0.0, dy)]))
        decays = []
        for h in (2 * j, 2 * j + 1):
            gap = cum_t[h : h + 1, :] - cum[:, h : h + 1]
            decays.append(jnp.exp(jnp.where(causal_t, gap, -1e30)))
        m = jnp.concatenate([d * scores_t for d in decays], axis=1)
        dm = dot32(xd, dy2, 1, 1)
        dcb_t = dcb_t + (decays[0] * dm[:, :rows] + decays[1] * dm[:, rows:])
        v = dot32(m, dy2, 1, 0) + k_all[:, here] * tail_e
        skip = pair_lanes(hp[2:3, :], j, first[0:1])
        dx = dt_e * v + skip * dy
        both[0:rows, here] = x * v
        both[rows : 2 * rows, here] = dy * (y - skip * x)
        rowv[1:2, here] = jnp.sum(dy * x, axis=0, keepdims=True)
        rowv[2:3, here] = pair_lanes(elast, j, first[0:1])
        xw_s[:, here] = xd * tail_e
        dyc_s[:, here] = dy * pair_lanes(ecum, j, first)
        dfp[0:rows, here] = dx * xder
    dcb_t = split(dcb_t)
    dyc = split(dyc_s[...])
    st_in = jnp.where(i == pl.num_programs(0) - 1, s0[...], st_before[0])
    dc = dot32(dcb_t, b_c, 0, 0) + dot32(dyc, st_in, 1, 1)
    db = dot32(dcb_t, c_c, 1, 0) + dot32(xw_s[...], grad_p, 1, 1)
    dfp[0:rows, width : width + STATE] = db * b_d
    dfp[0:rows, width + STATE :] = dc * c_d
    grad[...] = grad[...] * rowv[2:3, :] + dot32(c_c, dyc, 0, 0)
    gfin_ref[...] = grad[...]

    sums = head_sums(both[...], table[...])
    rsums = head_sums(rowv[...], table[...])
    ddt_x = sums[0:rows]
    dcum = sums[rows : 2 * rows] - dt * ddt_x
    upto = lax.broadcasted_iota(jnp.int32, (rows, heads), 0)
    dcum = dcum + jnp.where(upto == rows - 1, rsums[0:1, :], 0.0)
    ddecay = dot32(lower, dcum, 0, 0)
    ddt = ddt_x + hp[1:2, :] * ddecay
    draw = ddt * jax.nn.sigmoid(shifted)
    dproj[:, 2 * width + GROUP :] = draw.astype(BF16)
    dhp_ref[0:1, :] += jnp.sum(draw, axis=0, keepdims=True)
    dhp_ref[1:2, :] += jnp.sum(ddecay * dt, axis=0, keepdims=True) * hp[1:2, :]
    dhp_ref[2:3, :] += rsums[1:2, :]

    for lo in range(0, width + GROUP, LANES):
        here = slice(lo, lo + LANES)
        src = proj[:, width + lo : width + lo + LANES]
        total = jnp.zeros((rows, LANES), F32)
        for k in range(KERNEL):
            shift = KERNEL - 1 - k
            moved = dfp[shift : shift + rows, here]
            total = total + cw[k : k + 1, here] * moved
            dconv_ref[k : k + 1, here] += jnp.sum(src * moved, axis=0, keepdims=True)
        dconv_ref[4:5, here] += jnp.sum(dfp[0:rows, here], axis=0, keepdims=True)
        out = slice(width + lo, width + lo + LANES)
        if lo < width:
            dproj[:, out] = total.astype(BF16)
        else:
            dproj[:, out] = jnp.zeros((rows, LANES), BF16)
            dbc_ref[:, lo - width : lo - width + LANES] = total
    dfp[rows : rows + 8, :] = dfp[0:8, :]
    efin_ref[...] = dfp[0:8, :]


def whole(shape):
    return pl.BlockSpec(shape, lambda i, f: (0,) * len(shape))


def run_forward(f, proj, cw, hp, table, s0, e0, extra, rows):
    total, (heads, width) = proj.shape[0], table.shape
    count = total // rows
    block = lambda w: pl.BlockSpec((rows, w), lambda i, f: (jnp.bitwise_xor(i, f[0]), 0))
    in_specs = [
        block(proj.shape[1]),
        whole((8, width + GROUP)),
        whole((8, heads)),
        whole((heads, width)),
        whole((STATE, width)),
        whole((8, width + GROUP)),
    ]
    if extra:
        in_specs += [block(width), whole((1, width))]
    shape = jax.ShapeDtypeStruct
    return pl.pallas_call(
        functools.partial(forward_kernel, second=bool(extra)),
        grid_spec=pltpu.PrefetchScalarGridSpec(
            num_scalar_prefetch=1,
            grid=(count,),
            in_specs=in_specs,
            out_specs=[
                block(width),
                block(width + GROUP),
                pl.BlockSpec((1, STATE, width), lambda i, f: (i, 0, 0)),
                pl.BlockSpec((1, 8, rows), lambda i, f: (jnp.bitwise_xor(i, f[0]), 0, 0)),
            ],
            scratch_shapes=[
                pltpu.VMEM((STATE, width), F32),
                pltpu.VMEM((rows + 8, width + GROUP), F32),
                pltpu.VMEM((rows, width), F32),
                pltpu.VMEM((8, width), F32),
            ],
        ),
        out_shape=[
            shape((total, width), F32),
            shape((total, width + GROUP), F32),
            shape((count, STATE, width), F32),
            shape((count, 8, rows), F32),
        ],
        compiler_params=pltpu.CompilerParams(vmem_limit_bytes=VMEM_BYTES),
        name="scan_forward",
    )(f, proj, cw, hp, table, s0, e0, *extra)


def run_backward(f, proj, y, filt, dn, rc, states, s0, cw, hp, table, gain, g0, e0, rows):
    total, (heads, width) = proj.shape[0], table.shape
    count = total // rows
    turn = lambda i: count - 1 - i
    block = lambda w: pl.BlockSpec((rows, w), lambda i, f: (jnp.bitwise_xor(turn(i), f[0]), 0))
    shape = jax.ShapeDtypeStruct
    return pl.pallas_call(
        backward_kernel,
        grid_spec=pltpu.PrefetchScalarGridSpec(
            num_scalar_prefetch=1,
            grid=(count,),
            in_specs=[
                block(proj.shape[1]),
                block(width),
                block(width + GROUP),
                block(width),
                pl.BlockSpec((1, 8, rows), lambda i, f: (jnp.bitwise_xor(turn(i), f[0]), 0, 0)),
                pl.BlockSpec((1, STATE, width), lambda i, f: (jnp.maximum(turn(i) - 1, 0), 0, 0)),
                pl.BlockSpec((1, STATE, width), lambda i, f: (turn(i), 0, 0)),
                whole((STATE, width)),
                whole((8, width + GROUP)),
                whole((8, heads)),
                whole((heads, width)),
                whole((1, width)),
                whole((STATE, width)),
                whole((8, width + GROUP)),
            ],
            out_specs=[
                block(proj.shape[1]),
                block(GROUP),
                whole((8, width)),
                whole((8, width + GROUP)),
                whole((8, heads)),
                whole((STATE, width)),
                whole((8, width + GROUP)),
            ],
            scratch_shapes=[
                pltpu.VMEM((STATE, width), F32),
                pltpu.VMEM((rows + 8, width + GROUP), F32),
                pltpu.VMEM((2 * rows, width), F32),
                pltpu.VMEM((rows, width), F32),
                pltpu.VMEM((rows, width), F32),
                pltpu.VMEM((8, width), F32),
            ],
        ),
        out_shape=[
            shape(proj.shape, BF16),
            shape((total, GROUP), F32),
            shape((8, width), F32),
            shape((8, width + GROUP), F32),
            shape((8, heads), F32),
            shape((STATE, width), F32),
            shape((8, width + GROUP), F32),
        ],
        compiler_params=pltpu.CompilerParams(vmem_limit_bytes=VMEM_BYTES),
        name="scan_backward",
    )(f, proj, y, filt, dn, rc, states, states, s0, cw, hp, table, gain, g0, e0)


def place_kernel(ids, *refs, plan, small):
    out = refs[-1]
    h, j = pl.program_id(0), pl.program_id(1)
    core = ids[1]
    for ref, (side, layer, first, size) in zip(refs, plan):

        @pl.when((h == side) & (core == layer) & (j >= first) & (j < first + size))
        def _():
            v = ref[...]
            out[...] = v.reshape(out.shape).astype(F32)

    if small:

        @pl.when(j == pl.num_programs(1) - 1)
        def _():
            v = refs[len(plan)]
            out[: v.shape[1], :] = v[0]


def place_blocks(ids, chunks, small, out_shape, block, out_index, steps):
    def step_of(side, layer, first, size, index):
        def where(h, j, ids):
            used = jnp.logical_and(h == side, ids[1] == layer)
            return index(jnp.where(used, jnp.clip(j - first, 0, size - 1), 0))

        return where

    in_specs = [
        pl.BlockSpec(shape, step_of(side, layer, first, size, index))
        for _, side, layer, first, size, shape, index in chunks
    ]
    args = [c[0] for c in chunks]
    if small is not None:
        in_specs.append(pl.BlockSpec((1,) + small.shape[1:], lambda h, j, ids: (h, 0, 0)))
        args.append(small)
    return pl.pallas_call(
        functools.partial(
            place_kernel, plan=tuple(c[1:5] for c in chunks), small=small is not None
        ),
        grid_spec=pltpu.PrefetchScalarGridSpec(
            num_scalar_prefetch=1,
            grid=(2, steps),
            in_specs=in_specs,
            out_specs=pl.BlockSpec(block, out_index),
        ),
        out_shape=jax.ShapeDtypeStruct(out_shape, F32),
        compiler_params=pltpu.CompilerParams(vmem_limit_bytes=VMEM_BYTES),
        name="place_gradient",
    )(ids, *args)


def swap_section(v):
    return lax.ppermute(v, "section", [(0, 1), (1, 0)])


def move_fsdp(v, m):
    n = lax.axis_size("fsdp")
    return lax.ppermute(v, "fsdp", [(i, i ^ m) for i in range(n)])


def move_in_group(v, m):
    n, s = lax.axis_size("fsdp"), lax.axis_size("seq")
    return lax.ppermute(v, "seq", [(k, k // n * n + (k % n ^ m)) for k in range(s)])


def at(v, k):
    return lax.dynamic_index_in_dim(v, k, 0, False)


def exchange(pieces, move):
    return jnp.stack([p if m == 0 else move(p, m) for m, p in enumerate(pieces)])


def trade_places(v):
    n, f = lax.axis_size("fsdp"), lax.axis_index("fsdp")
    i = lax.axis_index("seq") % n
    size = v.shape[-1] // n
    cut = lambda k: lax.dynamic_slice_in_dim(v, k * size, size, 1)
    v = exchange([cut(f ^ m) for m in range(n)], move_fsdp)
    v = exchange([at(v, f ^ i ^ m) for m in range(n)], move_in_group)
    v = exchange([at(v, f ^ i ^ m) for m in range(n)], move_fsdp)
    return jnp.concatenate([at(v, f ^ k) for k in range(n)], axis=1)


def to_local(v):
    n, f, c = lax.axis_size("fsdp"), lax.axis_index("fsdp"), lax.axis_index("section")
    size = v.shape[-1] // (2 * n)
    cut = lambda k: lax.dynamic_slice_in_dim(v, k * size, size, v.ndim - 1)
    return [
        jnp.concatenate([cut((f ^ m) * 2 + (c ^ t)) for m in range(n)], axis=-1)
        for t in range(2)
    ]


def to_natural(pair):
    n, f, c = lax.axis_size("fsdp"), lax.axis_index("fsdp"), lax.axis_index("section")
    v = jnp.concatenate(pair, axis=-1)
    size = v.shape[-1] // (2 * n)
    cut = lambda k: lax.dynamic_slice_in_dim(v, k * size, size, v.ndim - 1)
    return jnp.concatenate(
        [cut((c ^ h) * n + (f ^ k)) for k in range(n) for h in range(2)], axis=-1
    )


def reorder(v, m):
    n = lax.axis_size("fsdp")
    size = v.shape[-1] // n
    return jnp.concatenate(
        [v[..., (j ^ m) * size : ((j ^ m) + 1) * size] for j in range(n)], axis=-1
    )


def gather_rows(v):
    n = lax.axis_size("fsdp")
    return jnp.concatenate([v] + [move_fsdp(v, m) for m in range(1, n)])


def gather_local(pair):
    n = lax.axis_size("fsdp")
    joint = jnp.concatenate(pair, axis=-1)
    came = [joint] + [move_fsdp(joint, m) for m in range(1, n)]
    size = joint.shape[-1] // 2
    return [
        jnp.concatenate(
            [reorder(v[:, t * size : (t + 1) * size], m) for m, v in enumerate(came)]
        )
        for t in range(2)
    ]


def scatter_sum(partial, local):
    n = lax.axis_size("fsdp")
    size = partial.shape[-1] // 2
    total = partial[0]
    for m in range(1, n):
        got = move_fsdp(partial[m].astype(BF16), m)
        if local:
            got = jnp.concatenate([reorder(got[:, :size], m), reorder(got[:, size:], m)], axis=-1)
        total = total + got.astype(F32)
    return total


def sum_rows(v):
    n = lax.axis_size("fsdp")
    total = v
    for m in range(1, n):
        got = move_fsdp(v, m)
        total = total + jnp.stack([got[j ^ m] for j in range(n)])
    return total


def sum_everywhere(v):
    n, s = lax.axis_size("fsdp"), lax.axis_size("seq")
    v = v + swap_section(v)
    m = 1
    while m < n:
        v = v + move_fsdp(v, m)
        m *= 2
    m = 1
    while m < s:
        v = v + lax.ppermute(v, "seq", [(k, k ^ m) for k in range(s)])
        m *= 2
    return v


class SeqSums:
    def __init__(self):
        s = lax.axis_size("seq")
        half = s // 2
        self.pairs = [[(j, j + 1), (s - 1 - j, s - 2 - j)] for j in range(half - 1)]
        self.pairs.append([(half - 1, half), (half, half - 1)])
        self.inward = half
        self.pairs += [[(j + 1, j), (s - 2 - j, s - 1 - j)] for j in reversed(range(half - 1))]
        self.values, self.phase, self.moving = [], [], []

    def add(self, values):
        first = len(self.values)
        self.values += values
        self.phase += [0] * len(values)
        return list(range(first, len(self.values)))

    def begin(self, chosen=None):
        place = lax.axis_index("seq")
        for k in range(len(self.values)) if chosen is None else chosen:
            step = self.phase[k]
            if step == len(self.pairs):
                continue
            v = self.values[k]
            got = lax.ppermute(v, "seq", self.pairs[step])
            if step < self.inward:
                v = (v.astype(F32) + got.astype(F32)).astype(BF16)
            else:
                here = functools.reduce(
                    jnp.logical_or, [place == to for _, to in self.pairs[step]]
                )
                v = jnp.where(here, got, v)
            self.moving.append((k, v))
            self.phase[k] = step + 1

    def end(self, work):
        moved = [v for _, v in self.moving]
        work, moved, rest = lax.optimization_barrier(
            (work, moved, [v for v, p in zip(self.values, self.phase) if p == 0])
        )
        for (k, _), v in zip(self.moving, moved):
            self.values[k] = v
        fresh = [k for k, p in enumerate(self.phase) if p == 0]
        for k, v in zip(fresh, rest):
            self.values[k] = v
        self.moving = []
        return work

    def busy(self):
        return any(p < len(self.pairs) for p in self.phase)


def relay(total, local, reverse):
    n, s = lax.axis_size("fsdp"), lax.axis_size("seq")
    segments = s // n
    place = lax.axis_index("seq") // n
    own = lax.axis_index("seq") % n
    totals = lax.all_gather(total, "seq")
    locals_ = lax.all_gather(local, "seq")
    state = jnp.zeros_like(local)
    order = range(segments - 1, -1, -1) if reverse else range(segments)
    for j in order:
        use = (j > place) if reverse else (j < place)
        t = lax.dynamic_index_in_dim(totals, j * n + own, 0, False)
        v = lax.dynamic_index_in_dim(locals_, j * n + own, 0, False)
        state = jnp.where(use, t * state + v, state)
    return state


def next_segment(v, step):
    n, s = lax.axis_size("fsdp"), lax.axis_size("seq")
    pairs = [(k, k + step * n) for k in range(s) if 0 <= k + step * n < s]
    return lax.ppermute(v, "seq", pairs)


def dot_rows(a, b):
    return lax.dot_general(a, b, (((0,), (0,)), ((), ())), preferred_element_type=F32)


def dot_cols(a, b):
    return lax.dot_general(a, b, (((1,), (1,)), ((), ())), preferred_element_type=F32)


def normalised(h, gain):
    return h * lax.rsqrt(jnp.mean(h * h, axis=-1, keepdims=True) + EPS) * gain


def per_device(
    inputs,
    cotangent,
    lengths,
    gain_in,
    w_in,
    conv_w,
    conv_b,
    dt_bias,
    a_log,
    d_skip,
    gain_out,
    w_out,
):
    n = lax.axis_size("fsdp")
    nz = lax.axis_size("seq")
    segments = nz // n
    c = lax.axis_index("section")
    f = lax.axis_index("fsdp")
    place = lax.axis_index("seq")
    upper = c == 0
    even = place % 2 == 0
    rows = inputs.shape[2]
    width = INNER // n
    heads = HEADS // n
    share = D // n
    half = share // 2
    group = GROUP // n
    pairs_of = n // 2
    f1 = f.reshape(1).astype(jnp.int32)
    ids = jnp.stack([f, c]).astype(jnp.int32)
    tie = lax.optimization_barrier

    def pick(a, b):
        return jnp.where(upper, a, b)

    h0 = trade_places(at(inputs, c)[0])

    pack = jnp.concatenate(
        [
            gain_in[0],
            dt_bias[0],
            a_log[0],
            d_skip[0],
            gain_out[0],
            conv_w[0].reshape(-1),
            conv_b[0],
        ]
    )
    mine = exchange([pack] * n, move_fsdp)

    w = w_in[0].T

    def cut_pieces(side):
        cut = lambda at_row, size: lax.dynamic_slice(w, (at_row, side * half), (size, half))
        first = jnp.where(even, 0, INNER)
        return jnp.stack(
            [
                jnp.concatenate(
                    [
                        cut(first + (f ^ m) * width, width),
                        cut(2 * INNER, GROUP),
                        cut(2 * INNER + GROUP + (f ^ m) * heads, heads),
                    ]
                )
                for m in range(n)
            ]
        )

    kept = cut_pieces(c)
    other = swap_section(cut_pieces(1 - c))

    def neighbour(v):
        return lax.ppermute(v, "seq", [(k, k ^ 1) for k in range(nz)])

    def arrange(came, traded):
        zs = [jnp.where(even, a[:width], b) for a, b in zip(came, traded)]
        xs = [jnp.where(even, b, a[:width]) for a, b in zip(came, traded)]
        rest = [a[width:] for a in came]
        return jnp.concatenate([jnp.concatenate(v, axis=1) for v in (zs, xs, rest)])

    first = jnp.where(upper, kept, other)
    came = [first[0]] + [move_fsdp(first[m], m) for m in range(1, n)]
    traded = [neighbour(v[:width]) for v in came]
    h0_local = gather_local(to_local(h0))
    mine, came, traded, h0_local = tie((mine, came, traded, h0_local))
    w0_own = arrange(came, traded)
    w0 = (w0_own, swap_section(w0_own))

    second, own_ct, wo_mine, own_len, _ = tie(
        (jnp.where(upper, other, kept), at(cotangent, c)[0], w_out[0], at(lengths, c), w0_own)
    )
    wo_other = swap_section(wo_mine)
    wo = (pick(wo_mine, wo_other), pick(wo_other, wo_mine))
    came = [second[0]] + [move_fsdp(second[m], m) for m in range(1, n)]
    came_half = jnp.stack([v[:width] for v in came])
    w1_own = arrange(came, neighbour(came_half))
    w1 = (w1_own, swap_section(w1_own))
    win = (w0, w1)
    slot_pairs = [
        ((j * n + i) * n + k, (j * n + k) * n + i)
        for j in range(segments)
        for i in range(n)
        for k in range(n)
    ]
    length = lax.ppermute(own_len, ("seq", "fsdp"), slot_pairs)
    start = ((place // n) * n + f) * rows
    valid = (start + jnp.arange(rows, dtype=jnp.int32) < length[0]).astype(F32)[:, None]
    dout1 = trade_places(own_ct).astype(F32)

    theirs = swap_section(mine)
    small = []
    for full in (pick(mine, theirs), pick(theirs, mine)):
        full = full.astype(F32)
        used = 0

        def take(size):
            nonlocal used
            used += size
            return full[:, used - size : used]

        gain = take(share)
        hp = [take(heads)[0:1] for _ in range(3)]
        hp = jnp.concatenate([hp[0], -jnp.exp(hp[1]), hp[2], jnp.zeros((5, heads), F32)])
        gout = take(width)[0:1]
        rest = jnp.stack([at(full[:, used:], f ^ k) for k in range(n)])
        gain = jnp.concatenate([at(gain, f ^ k) for k in range(n)])[None]
        per = CHANNELS // n
        taps = rest[:, : KERNEL * per].reshape(n, KERNEL, per).transpose(1, 0, 2)
        bias = rest[:, KERNEL * per :].reshape(1, CHANNELS)
        table = jnp.concatenate(
            [taps.reshape(KERNEL, CHANNELS), bias, jnp.zeros((3, CHANNELS), F32)]
        )
        cw = jnp.concatenate(
            [lax.dynamic_slice_in_dim(table, f * width, width, 1), table[:, INNER:]], axis=1
        )
        small.append((gain, cw, hp, gout))

    expand = (
        jnp.arange(heads)[:, None] == jnp.arange(width)[None, :] // HEAD_DIM
    ).astype(BF16)
    zero_state = jnp.zeros((STATE, width), F32)
    zero_edge = jnp.zeros((8, width + GROUP), F32)

    def project(normed, layer):
        return dot_cols(normed[0], win[layer][0]) + dot_cols(normed[1], win[layer][1])

    def decay_of(proj, hp):
        decay = jax.nn.softplus(proj[:, 2 * width + GROUP :] + hp[0:1]) * hp[1:2]
        return jnp.repeat(jnp.exp(jnp.sum(decay, axis=0)), HEAD_DIM)[None, :]

    def scan(proj, layer, extra):
        _, cw, hp, _ = small[layer]
        args = (f1, proj, cw, hp, expand)
        if segments == 1:
            return run_forward(*args, zero_state, zero_edge, extra, rows), zero_state
        rear = lax.dynamic_slice_in_dim(
            proj[:, width : 2 * width + GROUP], ((n - 1) ^ f) * rows + rows - 8, 8, 0
        )
        edge = next_segment(rear, 1)
        local = run_forward(*args, zero_state, edge, extra, rows)[2][-1]
        state = relay(decay_of(proj, hp), local, False)
        return run_forward(*args, state, edge, extra, rows), state

    def unscan(proj, fwd, dn, rc, layer):
        (y, filt, states, _), state = fwd
        _, cw, hp, gout = small[layer]
        args = (f1, proj, y, filt, dn, rc, states, state, cw, hp, expand, gout)
        if segments == 1:
            return run_backward(*args, zero_state, zero_edge, rows)[:5]
        local = run_backward(*args, zero_state, zero_edge, rows)[5]
        grad = relay(decay_of(proj, hp), local, True)
        edge = next_segment(run_backward(*args, grad, zero_edge, rows)[6], -1)
        return run_backward(*args, grad, edge, rows)[:5]

    def gated(proj, y, r, layer):
        g = y * jax.nn.silu(proj[:, :width])
        return (g * r.reshape(-1, 1) * small[layer][3]).astype(BF16)

    blockwise = lambda v: v.reshape(n, rows, v.shape[-1])

    both = jnp.concatenate(h0_local, axis=1).astype(F32)
    gain0 = jnp.concatenate(to_local(small[0][0]), axis=1)
    normed_in0 = normalised(both, gain0).astype(BF16)
    normed_in0 = (normed_in0[:, : D // 2], normed_in0[:, D // 2 :])
    proj0 = project(normed_in0, 0)
    fwd0 = scan(proj0, 0, ())
    stat0 = sum_rows(fwd0[0][3])
    r0 = lax.rsqrt(stat0[:, 0] / INNER + EPS)
    normed0 = gated(proj0, fwd0[0][0], r0, 0)
    mixed0 = scatter_sum(
        blockwise(jnp.dot(normed0, wo[0], preferred_element_type=F32)), False
    )
    out0 = valid * (h0.astype(F32) + mixed0)
    h1 = out0.astype(BF16)

    part1 = normalised(h1.astype(F32), small[1][0]).astype(BF16)
    normed_in1 = gather_local(to_local(part1))
    dmixed1 = gather_rows((valid * dout1).astype(BF16))
    dn1 = dot_cols(dmixed1, wo[1])
    proj1 = project(normed_in1, 1)
    fwd1 = scan(proj1, 1, (dn1, small[1][3]))
    stat1 = sum_rows(fwd1[0][3])
    r1 = lax.rsqrt(stat1[:, 0] / INNER + EPS)
    normed1 = gated(proj1, fwd1[0][0], r1, 1)

    sums = SeqSums()

    def half_sum(own, away):
        away = swap_section(dot_rows(*away).astype(BF16))
        return (dot_rows(*own) + away.astype(F32)).astype(BF16)

    def grads_in(part, normed_in):
        total = half_sum((part, normed_in[0]), (part, normed_in[1]))
        pieces = [total[:, m * half : (m + 1) * half] for m in range(n)]
        return [pieces[0]] + [move_fsdp(pieces[m], m) for m in range(1, n)]

    def pair_up(pieces):
        return [jnp.stack(pieces[2 * k : 2 * k + 2]) for k in range(pairs_of)]

    def grads_out(normed, dmixed):
        size = D // 2
        cut = lambda k: lax.dynamic_slice_in_dim(normed, k * (width // 2), width // 2, 1)
        own, away = cut(c), cut(1 - c)
        parts = [dmixed[:, k * size : (k + 1) * size] for k in range(2)]
        return [half_sum((own, v), (away, v)) for v in parts]

    def group_sum(dbc):
        shares = blockwise(dbc)
        own_cols = lambda k: lax.dynamic_slice_in_dim(shares, k * group, group, 2)
        total = own_cols(f)
        for m in range(1, n):
            got = move_fsdp(own_cols(f ^ m), m)
            total = total + jnp.stack([got[j ^ m] for j in range(n)])
        return total.reshape(n * rows, group).astype(BF16)

    def back_in(dproj, dgroup, layer):
        out = []
        for part in win[layer]:
            mine = lax.dynamic_slice_in_dim(part, 2 * width + f * group, group, 0)
            out.append(
                jnp.dot(dproj, part, preferred_element_type=F32)
                + jnp.dot(dgroup, mine, preferred_element_type=F32)
            )
        return scatter_sum(blockwise(jnp.concatenate(out, axis=1)), True)

    def back_norm(dout, dnormed_in, h, gain):
        dnormed_in = to_natural([dnormed_in])
        h = h.astype(F32)
        r = lax.rsqrt(jnp.mean(h * h, axis=-1, keepdims=True) + EPS)
        u = dnormed_in * gain
        mean = jnp.mean(u * h, axis=-1, keepdims=True)
        dgain = jnp.sum(dnormed_in * h * r, axis=0)
        return valid * dout + r * u - h * (r * r * r) * mean, dgain

    def scales(r, coef):
        rest = jnp.zeros((n, 6, rows), F32)
        return jnp.concatenate([r[:, None], coef[:, None], rest], axis=1)

    rc1 = scales(r1, (r1 * r1 * r1 / INNER) * stat1[:, 1])
    go1 = sums.add(grads_out(normed1, dmixed1))
    rc1, normed1 = sums.end((rc1, normed1))

    sums.begin()
    d1 = unscan(proj1, fwd1, dn1, rc1, 1)
    d1 = sums.end(d1)

    sums.begin()
    dproj1, dbc1 = d1[:2]
    dgroup1 = group_sum(dbc1)
    dnin1 = back_in(dproj1, dgroup1, 1)
    gz = pair_up(grads_in(dproj1[:, :width], normed_in1))
    dnin1, dgroup1, gz, normed1 = sums.end((dnin1, dgroup1, gz, normed1))
    gz1 = sums.add(gz)

    sums.begin()
    grad1, dgin1 = back_norm(dout1, dnin1, h1, small[1][0])
    dout0 = grad1.astype(BF16).astype(F32)
    dmixed0_own = (valid * dout0).astype(BF16)
    dmixed0 = gather_rows(dmixed0_own)
    along0 = exchange([jnp.sum(dmixed0_own.astype(F32) * mixed0, axis=-1)] * n, move_fsdp)
    rc0 = scales(r0, (r0 * r0 / INNER) * along0)
    dn0 = dot_cols(dmixed0, wo[0])
    gx = pair_up(grads_in(dproj1[:, width : 2 * width], normed_in1))
    dsmall1 = jnp.concatenate([dgroup1, dproj1[:, 2 * width + GROUP :]], axis=1)
    gs = jnp.stack(grads_in(dsmall1, normed_in1))
    grad1, dgin1, dmixed0, rc0, dn0, gx, gs = sums.end(
        (grad1, dgin1, dmixed0, rc0, dn0, gx, gs)
    )
    gx1 = sums.add(gx)
    gs1 = sums.add([gs])

    sums.begin()
    d0 = unscan(proj0, fwd0, dn0, rc0, 0)
    go = grads_out(normed0, dmixed0)
    d0, go = sums.end((d0, go))
    go0 = sums.add(go)

    sums.begin()
    dproj0, dbc0 = d0[:2]
    gz = pair_up(grads_in(dproj0[:, :width], normed_in0))
    dgroup0 = group_sum(dbc0)
    dnin0 = back_in(dproj0, dgroup0, 0)
    gz, dgroup0, dnin0 = sums.end((gz, dgroup0, dnin0))
    gz0 = sums.add(gz)

    sums.begin()
    gx = pair_up(grads_in(dproj0[:, width : 2 * width], normed_in0))
    dsmall0 = jnp.concatenate([dgroup0, dproj0[:, 2 * width + GROUP :]], axis=1)
    gs = jnp.stack(grads_in(dsmall0, normed_in0))
    grad0, dgin0 = back_norm(dout0, dnin0, h0, small[0][0])
    gx, gs, grad0, dgin0 = sums.end((gx, gs, grad0, dgin0))
    gx0 = sums.add(gx)
    gs0 = sums.add([gs])

    sums.begin()
    mixed1 = scatter_sum(
        blockwise(jnp.dot(normed1, wo[1], preferred_element_type=F32)), False
    )
    out1 = valid * (h1.astype(F32) + mixed1)
    last1 = out1.astype(BF16)
    back = trade_places(jnp.concatenate([h1, last1, grad0.astype(BF16), grad1.astype(BF16)]))
    back, out1, mixed1 = sums.end((back, out1, mixed1))

    sums.begin()
    smalls1 = (d1[2][0], d1[3][:5], d1[4][:3])
    smalls0 = (d0[2][0], d0[3][:5], d0[4][:3])

    def packed(dgin, smalls, out, mixed):
        dgain, dconv, dhp = smalls
        put = lambda v, size, at_lane: lax.dynamic_update_slice(
            jnp.zeros(v.shape[:-1] + (size,), F32), v, (0,) * (v.ndim - 1) + (at_lane,)
        )
        conv = put(dconv[:, :width], CHANNELS, f * width)
        conv = conv.at[:, INNER:].set(dconv[:, width:])
        totals = jnp.stack(
            [jnp.sum(out * out), jnp.sum((valid * mixed) ** 2), jnp.sum(valid)]
        )
        return jnp.concatenate(
            [
                dgin,
                conv.reshape(-1),
                put(dhp, HEADS, f * heads).reshape(-1),
                put(dgain, INNER, f * width),
                totals,
            ]
        )

    p = sum_everywhere(
        jnp.stack([packed(dgin0, smalls0, out0, mixed0), packed(dgin1, smalls1, out1, mixed1)])
    )
    p = sums.end(pick(p[0], p[1]))
    while sums.busy():
        sums.begin()
        p = sums.end(p)

    used = 0

    def part(size):
        nonlocal used
        used += size
        return p[used - size : used]

    mine_of = lambda v, size: lax.dynamic_slice_in_dim(v, f * size, size, v.ndim - 1)
    o_gain_in = mine_of(part(D), share)
    o_conv = mine_of(part(5 * CHANNELS).reshape(5, CHANNELS), CHANNELS // n)
    o_heads = mine_of(part(3 * HEADS).reshape(3, HEADS), heads)
    o_gain_out = mine_of(part(INNER), width)
    totals = part(3)
    act_rms = jnp.sqrt(totals[:2] / (totals[2] * D))[None]

    def hand_over(v, layer):
        return lax.ppermute(v, "section", [(1 - layer, layer)])

    own = [[sums.values[k] for k in ks] for ks in (gz0 + gx0 + gs0 + go0, gz1 + gx1 + gs1 + go1)]
    away = [[hand_over(v, layer) for v in own[layer]] for layer in range(2)]
    held = (own, away)
    at_small = 2 * pairs_of

    def small_rows(v):
        v = v.astype(F32)
        by_place = [at(v, f ^ k) for k in range(n)]
        return jnp.concatenate([b[:group] for b in by_place] + [b[group:] for b in by_place])

    small_in = jnp.stack(
        [small_rows(pick(side[0][at_small], side[1][at_small])) for side in held]
    )
    turned = lambda h, ids: jnp.where(h == 0, ids[1], 1 - ids[1])
    chunks_in = [
        (held[side][layer][k], side, layer, 2 * k, 2, (1, width, half), lambda i: (i, 0, 0))
        for side in range(2)
        for layer in range(2)
        for k in range(at_small)
    ]
    g_w_in = place_blocks(
        ids,
        chunks_in,
        small_in,
        (2 * INNER + GROUP + HEADS, share),
        (width, half),
        lambda h, j, ids: (
            jnp.where(j < 2 * n, (j // n) * n + jnp.bitwise_xor(j % n, ids[0]), 2 * n),
            turned(h, ids),
        ),
        2 * n + 1,
    )
    chunks_out = [
        (
            held[side][layer][at_small + 1 + k],
            side,
            layer,
            k,
            1,
            (width // 2, D // 2),
            lambda i: (0, 0),
        )
        for side in range(2)
        for layer in range(2)
        for k in range(2)
    ]
    g_w_out = place_blocks(
        ids,
        chunks_out,
        None,
        (width, D),
        (width // 2, D // 2),
        lambda h, j, ids: (turned(h, ids), j),
        2,
    )

    back = back.reshape(2, 2, rows, D)
    kept_back = pick(back[:, 0], back[:, 1])
    other_back = swap_section(pick(back[:, 1], back[:, 0]))
    both_back = jnp.stack(
        [pick(kept_back, other_back), pick(other_back, kept_back)], axis=1
    )
    return (
        both_back[0][None, :, None],
        both_back[1].astype(F32)[None, :, None],
        o_gain_in[None],
        g_w_in.T[None],
        o_conv[None, :4],
        o_conv[None, 4],
        o_heads[None, 0],
        o_heads[None, 1],
        o_heads[None, 2],
        o_gain_out[None],
        g_w_out[None],
        act_rms,
    )


def solution(mesh):
    in_specs = (
        P(None, "fsdp", "seq", None),
        P(None, "fsdp", "seq", None),
        P(None, "fsdp"),
        P("section", "fsdp"),
        P("section", "fsdp", None),
        P("section", None, "fsdp"),
        P("section", "fsdp"),
        P("section", "fsdp"),
        P("section", "fsdp"),
        P("section", "fsdp"),
        P("section", "fsdp"),
        P("section", "fsdp", None),
    )
    out_specs = (
        P("section", None, "fsdp", "seq", None),
        P("section", None, "fsdp", "seq", None),
        P("section", "fsdp"),
        P("section", "fsdp", None),
        P("section", None, "fsdp"),
        P("section", "fsdp"),
        P("section", "fsdp"),
        P("section", "fsdp"),
        P("section", "fsdp"),
        P("section", "fsdp"),
        P("section", "fsdp", None),
        P("section", None),
    )
    return jax.shard_map(
        per_device, mesh=mesh, in_specs=in_specs, out_specs=out_specs, check_vma=False
    )
```

time: 1680 us -> 1360 us (0.81); the launches traced: 1650 us -> 1360 us
  starting transfers between devices: 473 us -> 302 us
  waiting for transfers between devices: 704 us -> 555 us
  other arithmetic: 90.5 us -> 207 us
  local copies, waits for them, and re-layouts: 144 us -> 85.2 us
  Pallas kernels: 129 us -> 90.2 us
  matrix products: 91.3 us -> 112 us
    psum x1 -> x0, waiting for transfers between devices: 119 us -> none  [per_device(): p0, p1 = lax.psum((p0, p1), everyone)]
    concatenate x7 -> x12, other arithmetic: 21.5 us -> 105 us  [the longest x2 81.2 us: arrange(): return jnp.concatenate([jnp.concatenate(v, axis=1) for v in (zs, xs, rest)])]
    ppermute x72 -> x86, starting transfers between devices: 151 us -> 89.4 us  [move_fsdp(): return lax.ppermute(v, 'fsdp', [(i, i ^ m) for i in range(n)])]
    ppermute x14, starting transfers between devices: 86.3 us -> 27.6 us  [hand_over(): return lax.ppermute(v, 'section', [(1 - layer, layer)])]
    ppermute x49 -> x59, starting transfers between devices: 180 us -> 122 us  [the longest x42 71.1 us: begin(): got = lax.ppermute(v, 'seq', self.pairs[step])]
    unnamed x437 -> x325, local copies, waits for them, and re-layouts: 57.4 us -> 16.9 us
    ppermute x49 -> x59, waiting for transfers between devices: 329 us -> 299 us  [the longest x42 197 us: begin(): got = lax.ppermute(v, 'seq', self.pairs[step])]
    pallas_call x2, Pallas kernels: 69.3 us -> 43.5 us  [run_backward(): pl.pallas_call(backward_kernel, grid_spec=pltpu.PrefetchScalarGridSpec(nu...]
  transfers between devices with their start and end apart: 167 -> 176, of which waited for: 57 -> 66; matrix products, arithmetic and copies ran while one was open for 16% -> 23% of each run, Pallas kernels for 4% -> 4%
where the time goes in v3:
time: 1360 us
  waiting for transfers between devices  555 us (41%)
  starting transfers between devices  302 us (22%)
  other arithmetic  207 us (15%)
  matrix products  112 us (8%)
  Pallas kernels  90.2 us (7%)
  local copies, waits for them, and re-layouts  85.2 us (6%)
    ppermute x86, waiting for transfers between devices, move_fsdp(): return lax.ppermute(v, 'fsdp', [(i, i ^ m) for i in range(n)])  253 us
    ppermute x42, waiting for transfers between devices, begin(): got = lax.ppermute(v, 'seq', self.pairs[step])  197 us
    ppermute x86, starting transfers between devices, move_fsdp(): return lax.ppermute(v, 'fsdp', [(i, i ^ m) for i in range(n)])  89.4 us
    concatenate x2, other arithmetic, arrange(): return jnp.concatenate([jnp.concatenate(v, axis=1) for v in (zs, xs, rest)])  81.2 us
    ppermute x9, waiting for transfers between devices, move_in_group(): lax.ppermute(v, 'seq', [(k, k // n * n + (k % n ^ m)) for k in range(s)])  76.7 us
    ppermute x42, starting transfers between devices, begin(): got = lax.ppermute(v, 'seq', self.pairs[step])  71.1 us
    ppermute x17, starting transfers between devices, swap_section(): return lax.ppermute(v, 'section', [(0, 1), (1, 0)])  63.3 us
    pallas_call x2, Pallas kernels, run_backward(): pl.pallas_call(backward_kernel, grid_spec=pltpu.PrefetchScalarGridSpec(nu...  43.5 us
  transfers between devices with their start and end apart: 176, of which 66 were waited for; matrix products, arithmetic and copies ran while one was open for 23% of the time, Pallas kernels for 4%

profile of v3, /device:TPU:1, one launch (start us, length us, event | category | flops | bytes accessed | tf_op | source)
XLA Modules:
  0.0 1357.1 jit_solution(15218741179355724902)
XLA Ops:
  29.9 7.8 collective-permute-start
  49.2 9.5 collective-permute-done.20
  64.0 7.2 collective-permute-done.22
  71.4 14.0 %collective-permute-done.6 = bf16[1296,256]{1,0:T(8,128)(2,1)S(1)} collective-permute-done((bf16[1296,256]{1,0:T(8,128)(2,1)S(1)}, bf16[1296,256]{1,0:T(8,128)(2,1)S(1)}, u32[]{:S(2)}, u32[]{:S(2)}) %collective-permute-start.6) | collective-permute-done | bytes 663584 | tf_op jit(solution)/shard_map/ppermute | solution.py:439
  85.5 12.9 collective-permute-done.4
  101.2 6.6 maximum_maximum_fusion.3
  107.8 6.6 maximum_maximum_fusion.2
  114.4 9.3 collective-permute-done.9
  124.9 40.6 %maximum_maximum_fusion = bf16[2320,1024]{1,0:T(8,128)(2,1)} fusion(bf16[272,256]{1,0:T(8,128)(2,1)S(1)} %slice.1159, bf16[272,256]{1,0:T(8,128)(2,1)S(1)} %slice.1158, bf16[272,256]{1,0:T(8,128)(2,1)S(1)} %slice-done.1, bf16[272,256]{1,0:T(8,128)(2,1)S(1)} %slice.1156, bf16[1024,256]{1,0:T(8,128)(2,1)S(1)} %get-tuple-element.430, ...), kind=kLoop, calls=%fused_computation.10 | loop fusion | flops 57016320 | bytes 9502720 | tf_op jit(solution)/shard_map/concatenate | solution.py:712
  202.5 7.5 collective-permute-done.37
  214.7 5.9 fusion.82
  230.4 35.6 %collective-permute-done.44 = bf16[128,512]{1,0:T(8,128)(2,1)S(1)} collective-permute-done((bf16[128,512]{1,0:T(8,128)(2,1)S(1)}, bf16[128,512]{1,0:T(8,128)(2,1)S(1)}, u32[]{:S(2)}, u32[]{:S(2)}) %collective-permute-start.44) | collective-permute-done | bytes 131104 | tf_op jit(solution)/shard_map/ppermute | solution.py:444
  278.9 7.1 convolution_add_fusion.1.proj
  286.1 11.2 scan_forward.2
  316.4 40.6 %maximum_maximum_fusion.1 = bf16[2320,1024]{1,0:T(8,128)(2,1)} fusion(bf16[272,256]{1,0:T(8,128)(2,1)S(1)} %slice-done, bf16[272,256]{1,0:T(8,128)(2,1)S(1)} %slice.1473, bf16[272,256]{1,0:T(8,128)(2,1)S(1)} %slice.1472, bf16[272,256]{1,0:T(8,128)(2,1)S(1)} %copy-done.74, bf16[1024,256]{1,0:T(8,128)(2,1)S(1)} %get-tuple-element.418, ...), kind=kLoop, calls=%fused_computation.11 | loop fusion | flops 57016320 | bytes 9502720 | tf_op jit(solution)/shard_map/concatenate | solution.py:712
  376.2 7.7 collective-permute-done.33
  385.2 11.8 collective-permute-done.34
  398.1 6.8 maximum_maximum_fusion.5
  406.4 13.0 collective-permute-done.51
  423.2 5.2 fusion.221
  428.5 14.6 %convolution_add_fusion.proj = f32[512,2320]{1,0:T(8,128)} fusion(f32[512,2320]{1,0:T(8,128)S(1)} %fusion.221, bf16[2320,1024]{1,0:T(8,128)(2,1)} %maximum_maximum_fusion.1, bf16[128,256]{1,0:T(8,128)(2,1)S(1)} %get-tuple-element.488, bf16[128,256]{1,0:T(8,128)(2,1)S(1)} %get-tuple-element.489, bf16[128,256]{1,0:T(8,128)(2,1)S(1)} %get-tuple-element.490, ...), kind=kOutput, calls=%fused_computation.8 | convolution fusion | flops 2448564224 | bytes 15302656 | tf_op jit(solution)/shard_map/dot_general | solution.py:626
  443.1 11.9 scan_forward.3
  484.1 21.7 %scan_backward.2 = (bf16[512,2320]{1,0:T(8,128)(2,1)}, f32[512,256]{1,0:T(8,128)S(1)}, f32[8,1024]{1,0:T(8,128)S(1)}, f32[8,1280]{1,0:T(8,128)S(1)}, f32[8,16]{1...) custom-call(s32[1]{0:T(128)} %bitcast.81.f_ref, f32[512,2320]{1,0:T(8,128)} %convolution_add_fusion.proj, ...), custom_call_target="tpu_custom_call" | custom-call | tf_op jit(solution)/shard_map/scan_backward/pallas_call | solution.py:329
  507.8 16.8 %collective-permute-done.58 = bf16[512,1024]{1,0:T(8,128)(2,1)} collective-permute-done((bf16[512,1024]{1,0:T(8,128)(2,1)}, bf16[512,1024]{1,0:T(8,128)(2,1)}, u32[]{:S(2)}, u32[]{:S(2)}) %collective-permute-start.58) | collective-permute-done | bytes 1048608 | tf_op jit(solution)/shard_map/ppermute | solution.py:570
  532.8 7.3 collective-permute-done.61
  562.4 5.1 collective-permute-done.63
  569.4 9.5 collective-permute-done.65
  579.8 10.0 collective-permute-done.64
  591.9 7.6 add_convert_fusion.3
  602.3 7.8 add_convert_fusion.2
  612.8 11.5 collective-permute-done.68
  626.0 7.0 collective-permute-start.92
  638.5 6.9 collective-permute-done.83
  653.8 9.9 collective-permute-done.72
  664.7 10.8 collective-permute-done.74
  690.7 17.6 %collective-permute-done.90 = bf16[512,1024]{1,0:T(8,128)(2,1)S(1)} collective-permute-done((bf16[512,1024]{1,0:T(8,128)(2,1)S(1)}, bf16[512,1024]{1,0:T(8,128)(2,1)S(1)}, u32[]{:S(2)}, u32[]{:S(2)}) %collective-permute-start.90) | collective-permute-done | bytes 1048608 | tf_op jit(solution)/shard_map/ppermute | solution.py:570
  715.8 15.0 %collective-permute-done.89 = bf16[512,1024]{1,0:T(8,128)(2,1)S(1)} collective-permute-done((bf16[512,1024]{1,0:T(8,128)(2,1)S(1)}, bf16[512,1024]{1,0:T(8,128)(2,1)S(1)}, u32[]{:S(2)}, u32[]{:S(2)}) %collective-permute-start.89) | collective-permute-done | bytes 1048608 | tf_op jit(solution)/shard_map/ppermute | solution.py:570
  740.1 21.8 %scan_backward.3 = (bf16[512,2320]{1,0:T(8,128)(2,1)}, f32[512,256]{1,0:T(8,128)S(1)}, f32[8,1024]{1,0:T(8,128)S(1)}, f32[8,1280]{1,0:T(8,128)S(1)}, f32[8,16]{1...) custom-call(s32[1]{0:T(128)} %bitcast.81.f_ref, f32[512,2320]{1,0:T(8,128)} %convolution_add_fusion.1.proj, ...), custom_call_target="tpu_custom_call" | custom-call | tf_op jit(solution)/shard_map/scan_backward/pallas_call | solution.py:329
  770.9 6.3 collective-permute-done.97
  789.1 5.7 collective-permute-done.109
  810.9 5.9 collective-permute-start.120
  820.4 8.3 collective-permute-done.113
  829.6 13.2 collective-permute-done.112
  849.0 7.2 collective-permute-done.119
  857.7 6.5 collective-permute-start.100
  865.2 10.2 collective-permute-done.115
  876.5 21.4 %collective-permute-done.114 = bf16[2,1024,256]{2,1,0:T(8,128)(2,1)S(1)} collective-permute-done((bf16[2,1024,256]{2,1,0:T(8,128)(2,1)S(1)}, bf16[2,1024,256]{2,1,0:T(8,128)(2,1)S(1)}, u32[]{:S(2)}, u32[]{:S(2)}) %collective-permute-start.114) | collective-permute-done | bytes 1048608 | tf_op jit(solution)/shard_map/ppermute | solution.py:570
  906.5 18.2 %collective-permute-done.106 = bf16[1024,256]{1,0:T(8,128)(2,1)S(1)} collective-permute-done((bf16[1024,256]{1,0:T(8,128)(2,1)S(1)}, bf16[1024,256]{1,0:T(8,128)(2,1)S(1)}, u32[]{:S(2)}, u32[]{:S(2)}) %collective-permute-start.106) | collective-permute-done | bytes 524320 | tf_op jit(solution)/shard_map/ppermute | solution.py:439
  931.9 15.3 %collective-permute-done.102 = bf16[1024,256]{1,0:T(8,128)(2,1)S(1)} collective-permute-done((bf16[1024,256]{1,0:T(8,128)(2,1)S(1)}, bf16[1024,256]{1,0:T(8,128)(2,1)S(1)}, u32[]{:S(2)}, u32[]{:S(2)}) %collective-permute-start.102) | collective-permute-done | bytes 524320 | tf_op jit(solution)/shard_map/ppermute | solution.py:439
  974.6 9.9 collective-permute-done.126
  985.6 21.3 %collective-permute-done.125 = bf16[2,1024,256]{2,1,0:T(8,128)(2,1)S(1)} collective-permute-done((bf16[2,1024,256]{2,1,0:T(8,128)(2,1)S(1)}, bf16[2,1024,256]{2,1,0:T(8,128)(2,1)S(1)}, u32[]{:S(2)}, u32[]{:S(2)}) %collective-permute-start.125) | collective-permute-done | bytes 1048608 | tf_op jit(solution)/shard_map/ppermute | solution.py:570
  1020.0 8.9 collective-permute-done.134
  1057.2 24.2 %collective-permute-done.136 = bf16[512,512]{1,0:T(8,128)(2,1)S(1)} collective-permute-done((bf16[512,512]{1,0:T(8,128)(2,1)}, bf16[512,512]{1,0:T(8,128)(2,1)S(1)}, u32[]{:S(2)}, u32[]{:S(2)}) %collective-permute-start.136) | collective-permute-done | bytes 524320 | tf_op jit(solution)/shard_map/ppermute | solution.py:444
  1082.7 12.2 collective-permute-done.137
  1107.0 5.0 collective-permute-done.142
  1113.1 19.9 %collective-permute-done.141 = bf16[512,1024]{1,0:T(8,128)(2,1)S(1)} collective-permute-done((bf16[512,1024]{1,0:T(8,128)(2,1)S(1)}, bf16[512,1024]{1,0:T(8,128)(2,1)S(1)}, u32[]{:S(2)}, u32[]{:S(2)}) %collective-permute-start.141) | collective-permute-done | bytes 1048608 | tf_op jit(solution)/shard_map/ppermute | solution.py:570
  1140.5 13.5 collective-permute-start.149
  1172.4 35.3 %collective-permute-start.152 = (f32[2,28099]{1,0:T(2,128)S(1)}, f32[2,28099]{1,0:T(2,128)S(1)}, u32[]{:S(2)}, u32[]{:S(2)}) collective-permute-start(f32[2,28099]{1,0:T(2,128)S(1)} %add.913), channel_id=1, source_target_pairs={{0,4},{4,0},{8,12},{12,8},{1,5},{5,1},{9,13},{13,9},{2,6},{6,2},{1... | collective-permute-start | bytes 674384 | tf_op jit(solution)/shard_map/ppermute | solution.py:542
  1208.7 10.3 collective-permute-done.152
  1231.3 5.8 collective-permute-done.153
  1248.7 6.1 place_gradient.3
  1258.0 36.9 %collective-permute-done.161 = bf16[4,80,256]{2,1,0:T(8,128)(2,1)S(1)} collective-permute-done((bf16[4,80,256]{2,1,0:T(8,128)(2,1)S(1)}, bf16[4,80,256]{2,1,0:T(8,128)(2,1)S(1)}, u32[]{:S(2)}, u32[]{:S(2)}) %collective-permute-start.161) | collective-permute-done | bytes 163872 | tf_op jit(solution)/shard_map/ppermute | solution.py:570
  1301.8 5.4 collective-permute-start.170
  1339.0 17.6 %place_gradient.2 = f32[8512,512]{1,0:T(8,128)} custom-call(s32[2]{0:T(128)S(1)} %pad_add_fusion.ids, bf16[2,1024,256]{2,1,0:T(8,128)(2,1)S(1)} %copy-done.12, bf16[2,1024,256]{2,1,0:T(8,128)(2,1)S(1)} %copy-done.10, bf16[2,1024,256]{2,1,0:T(8,128)(2,1)S(1)} %copy-done.15, bf16[2,1024,256]{2,1,0:T(8,128)(2,1)S(1)} %copy-done.14, ...), custom_call_target="tpu_custom_call" | custom-call | tf_op jit(solution)/shard_map/place_gradient/pallas_call | solution.py:417
  (957 shorter events, 520.9 us)
Async XLA Ops:
  62.0 36.4 %collective-permute-start.4 = (bf16[1296,256]{1,0:T(8,128)(2,1)S(1)}, bf16[1296,256]{1,0:T(8,128)(2,1)S(1)}, u32[]{:S(2)}, u32[]{:S(2)}) collective-permute-start(bf16[1296,256]{1,0:T(8,128)(2,1)S(1)} %get-tuple-element.371), channel_id=1, source_target_pairs={{0,1},{1,0},{2,3},{3,2},{4,5},{5,4},{6,7},{7,6},{8,9},{9,8},{10,11... | collective-permute-start | bytes 1990664 | tf_op jit(solution)/shard_map/ppermute | solution.py:439
  64.0 37.1 %collective-permute-start.5 = (bf16[1296,256]{1,0:T(8,128)(2,1)S(1)}, bf16[1296,256]{1,0:T(8,128)(2,1)S(1)}, u32[]{:S(2)}, u32[]{:S(2)}) collective-permute-start(bf16[1296,256]{1,0:T(8,128)(2,1)S(1)} %get-tuple-element.370), channel_id=1, source_target_pairs={{0,2},{1,3},{2,0},{3,1},{4,6},{5,7},{6,4},{7,5},{8,10},{9,11},{10,... | collective-permute-start | bytes 1990664 | tf_op jit(solution)/shard_map/ppermute | solution.py:439
  71.3 43.1 %collective-permute-start.7 = (bf16[1024,256]{1,0:T(8,128)(2,1)S(1)}, bf16[1024,256]{1,0:T(8,128)(2,1)S(1)}, u32[]{:S(2)}, u32[]{:S(2)}) collective-permute-start(bf16[1024,256]{1,0:T(8,128)(2,1)S(1)} %slice_bitcast_fusion.14), channel_id=1, source_target_pairs={{0,4},{4,0},{8,12},{12,8},{1,5},{5,1},{9,13},{13,9},{2,6},{6,2},{1... | collective-permute-start | bytes 1572872 | tf_op jit(solution)/shard_map/ppermute | solution.py:706
  165.5 113.3 %collective-permute-start.25 = (bf16[2320,1024]{1,0:T(8,128)(2,1)}, bf16[2320,1024]{1,0:T(8,128)(2,1)}, u32[]{:S(2)}, u32[]{:S(2)}) collective-permute-start(bf16[2320,1024]{1,0:T(8,128)(2,1)} %maximum_maximum_fusion), channel_id=1, source_target_pairs={{0,16},{16,0},{1,17},{17,1},{2,18},{18,2},{3,19},{19,3},{4,20},{20... | collective-permute-start | bytes 14254088 | tf_op jit(solution)/shard_map/ppermute | solution.py:434
  173.3 47.3 %collective-permute-start.41 = (bf16[128,512]{1,0:T(8,128)(2,1)}, bf16[128,512]{1,0:T(8,128)(2,1)}, u32[]{:S(2)}, u32[]{:S(2)}) collective-permute-start(bf16[128,512]{1,0:T(8,128)(2,1)} %get-tuple-element.470), channel_id=1, source_target_pairs={{0,1},{1,0},{2,3},{3,2},{4,5},{5,4},{6,7},{7,6},{8,9},{9,8},{10,11... | collective-permute-start | bytes 393224 | tf_op jit(solution)/shard_map/ppermute | solution.py:439
  210.0 98.5 %collective-permute-start.29 = (bf16[1024,2048]{1,0:T(8,128)(2,1)}, bf16[1024,2048]{1,0:T(8,128)(2,1)}, u32[]{:S(2)}, u32[]{:S(2)}) collective-permute-start(bf16[1024,2048]{1,0:T(8,128)(2,1)} %bitcast.542), channel_id=1, source_target_pairs={{0,16},{16,0},{1,17},{17,1},{2,18},{18,2},{3,19},{19,3},{4,20},{20... | collective-permute-start | bytes 12582920 | tf_op jit(solution)/shard_map/ppermute | solution.py:434
  213.1 64.3 %collective-permute-start.39 = (bf16[4,1024,256]{2,1,0:T(8,128)(2,1)S(1)}, bf16[4,1024,256]{2,1,0:T(8,128)(2,1)S(1)}, u32[]{:S(2)}, u32[]{:S(2)}) collective-permute-start(bf16[4,1024,256]{2,1,0:T(8,128)(2,1)S(1)} %pad_maximum_fusion.5), channel_id=1, source_target_pairs={{0,4},{4,0},{8,12},{12,8},{1,5},{5,1},{9,13},{13,9},{2,6},{6,2},{1... | collective-permute-start | bytes 6291464 | tf_op jit(solution)/shard_map/ppermute | solution.py:706
  227.4 38.6 %collective-permute-start.44 = (bf16[128,512]{1,0:T(8,128)(2,1)S(1)}, bf16[128,512]{1,0:T(8,128)(2,1)S(1)}, u32[]{:S(2)}, u32[]{:S(2)}) collective-permute-start(bf16[128,512]{1,0:T(8,128)(2,1)S(1)} %get-tuple-element.466), channel_id=1, source_target_pairs={{0,4},{4,0},{8,12},{12,8},{1,5},{5,1},{9,13},{13,9},{2,6},{6,2},{1... | collective-permute-start | bytes 393224 | tf_op jit(solution)/shard_map/ppermute | solution.py:444
  228.9 41.2 %collective-permute-start.45 = (bf16[128,512]{1,0:T(8,128)(2,1)S(1)}, bf16[128,512]{1,0:T(8,128)(2,1)S(1)}, u32[]{:S(2)}, u32[]{:S(2)}) collective-permute-start(bf16[128,512]{1,0:T(8,128)(2,1)S(1)} %get-tuple-element.465), channel_id=1, source_target_pairs={{0,8},{4,12},{8,0},{12,4},{1,9},{5,13},{9,1},{13,5},{2,10},{6,14},... | collective-permute-start | bytes 393224 | tf_op jit(solution)/shard_map/ppermute | solution.py:444
  272.9 43.4 %collective-permute-start.47 = (bf16[128,512]{1,0:T(8,128)(2,1)S(1)}, bf16[128,512]{1,0:T(8,128)(2,1)S(1)}, u32[]{:S(2)}, u32[]{:S(2)}) collective-permute-start(bf16[128,512]{1,0:T(8,128)(2,1)S(1)} %get-tuple-element.462), channel_id=1, source_target_pairs={{0,1},{1,0},{2,3},{3,2},{4,5},{5,4},{6,7},{7,6},{8,9},{9,8},{10,11... | collective-permute-start | bytes 393224 | tf_op jit(solution)/shard_map/ppermute | solution.py:439
  273.3 83.7 %collective-permute-start.48 = (bf16[128,512]{1,0:T(8,128)(2,1)}, bf16[128,512]{1,0:T(8,128)(2,1)}, u32[]{:S(2)}, u32[]{:S(2)}) collective-permute-start(bf16[128,512]{1,0:T(8,128)(2,1)} %get-tuple-element.461), channel_id=1, source_target_pairs={{0,2},{1,3},{2,0},{3,1},{4,6},{5,7},{6,4},{7,5},{8,10},{9,11},{10,... | collective-permute-start | bytes 393224 | tf_op jit(solution)/shard_map/ppermute | solution.py:439
  277.4 84.2 %collective-permute-start.49 = (bf16[128,512]{1,0:T(8,128)(2,1)S(1)}, bf16[128,512]{1,0:T(8,128)(2,1)S(1)}, u32[]{:S(2)}, u32[]{:S(2)}) collective-permute-start(bf16[128,512]{1,0:T(8,128)(2,1)S(1)} %get-tuple-element.460), channel_id=1, source_target_pairs={{0,3},{1,2},{2,1},{3,0},{4,7},{5,6},{6,5},{7,4},{8,11},{9,10},{10,... | collective-permute-start | bytes 393224 | tf_op jit(solution)/shard_map/ppermute | solution.py:439
  313.7 48.9 %collective-permute-start.30 = (bf16[128,2048]{1,0:T(8,128)(2,1)S(1)}, bf16[128,2048]{1,0:T(8,128)(2,1)S(1)}, u32[]{:S(2)}, u32[]{:S(2)}) collective-permute-start(bf16[128,2048]{1,0:T(8,128)(2,1)S(1)} %get-tuple-element.420), channel_id=1, source_target_pairs={{0,1},{1,0},{2,3},{3,2},{4,5},{5,4},{6,7},{7,6},{8,9},{9,8},{10,11... | collective-permute-start | bytes 1572872 | tf_op jit(solution)/shard_map/ppermute | solution.py:439
  314.8 47.8 %collective-permute-start.31 = (bf16[128,2048]{1,0:T(8,128)(2,1)S(1)}, bf16[128,2048]{1,0:T(8,128)(2,1)S(1)}, u32[]{:S(2)}, u32[]{:S(2)}) collective-permute-start(bf16[128,2048]{1,0:T(8,128)(2,1)S(1)} %get-tuple-element.422), channel_id=1, source_target_pairs={{0,2},{1,3},{2,0},{3,1},{4,6},{5,7},{6,4},{7,5},{8,10},{9,11},{10,... | collective-permute-start | bytes 1572872 | tf_op jit(solution)/shard_map/ppermute | solution.py:439
  316.2 46.4 %collective-permute-start.32 = (bf16[128,2048]{1,0:T(8,128)(2,1)S(1)}, bf16[128,2048]{1,0:T(8,128)(2,1)S(1)}, u32[]{:S(2)}, u32[]{:S(2)}) collective-permute-start(bf16[128,2048]{1,0:T(8,128)(2,1)S(1)} %get-tuple-element.421), channel_id=1, source_target_pairs={{0,3},{1,2},{2,1},{3,0},{4,7},{5,6},{6,5},{7,4},{8,11},{9,10},{10,... | collective-permute-start | bytes 1572872 | tf_op jit(solution)/shard_map/ppermute | solution.py:439
  357.0 66.2 %collective-permute-start.40 = (bf16[2320,1024]{1,0:T(8,128)(2,1)}, bf16[2320,1024]{1,0:T(8,128)(2,1)}, u32[]{:S(2)}, u32[]{:S(2)}) collective-permute-start(bf16[2320,1024]{1,0:T(8,128)(2,1)} %maximum_maximum_fusion.1), channel_id=1, source_target_pairs={{0,16},{16,0},{1,17},{17,1},{2,18},{18,2},{3,19},{19,3},{4,20},{20... | collective-permute-start | bytes 14254088 | tf_op jit(solution)/shard_map/ppermute | solution.py:434
  383.9 35.5 %collective-permute-start.51 = (bf16[128,2048]{1,0:T(8,128)(2,1)S(1)}, bf16[128,2048]{1,0:T(8,128)(2,1)S(1)}, u32[]{:S(2)}, u32[]{:S(2)}) collective-permute-start(bf16[128,2048]{1,0:T(8,128)(2,1)S(1)} %get-tuple-element.618), channel_id=1, source_target_pairs={{0,2},{1,3},{2,0},{3,1},{4,6},{5,7},{6,4},{7,5},{8,10},{9,11},{10,... | collective-permute-start | bytes 1572872 | tf_op jit(solution)/shard_map/ppermute | solution.py:439
  480.3 44.3 %collective-permute-start.58 = (bf16[512,1024]{1,0:T(8,128)(2,1)}, bf16[512,1024]{1,0:T(8,128)(2,1)}, u32[]{:S(2)}, u32[]{:S(2)}) collective-permute-start(bf16[512,1024]{1,0:T(8,128)(2,1)} %add_convert_fusion.31), channel_id=1, source_target_pairs={{0,4},{12,8},{1,5},{13,9},{2,6},{14,10},{3,7},{15,11},{16,20},{28,... | collective-permute-start | bytes 3145736 | tf_op jit(solution)/shard_map/ppermute | solution.py:570
  528.4 61.7 %collective-permute-start.71 = (bf16[512,1024]{1,0:T(8,128)(2,1)S(1)}, bf16[512,1024]{1,0:T(8,128)(2,1)S(1)}, u32[]{:S(2)}, u32[]{:S(2)}) collective-permute-start(bf16[512,1024]{1,0:T(8,128)(2,1)S(1)} %add_convert_fusion.28), channel_id=1, source_target_pairs={{4,8},{8,4},{5,9},{9,5},{6,10},{10,6},{7,11},{11,7},{20,24},{24,20... | collective-permute-start | bytes 3145736 | tf_op jit(solution)/shard_map/ppermute | solution.py:570
  529.2 61.6 %collective-permute-start.70 = (bf16[512,1024]{1,0:T(8,128)(2,1)S(1)}, bf16[512,1024]{1,0:T(8,128)(2,1)S(1)}, u32[]{:S(2)}, u32[]{:S(2)}) collective-permute-start(bf16[512,1024]{1,0:T(8,128)(2,1)S(1)} %add_convert_fusion.29), channel_id=1, source_target_pairs={{4,8},{8,4},{5,9},{9,5},{6,10},{10,6},{7,11},{11,7},{20,24},{24,20... | collective-permute-start | bytes 3145736 | tf_op jit(solution)/shard_map/ppermute | solution.py:570
  558.7 32.4 %collective-permute-start.66 = (bf16[1024,1024]{1,0:T(8,128)(2,1)S(1)}, bf16[1024,1024]{1,0:T(8,128)(2,1)S(1)}, u32[]{:S(2)}, u32[]{:S(2)}) collective-permute-start(bf16[1024,1024]{1,0:T(8,128)(2,1)S(1)} %convolution_convert_fusion.3), channel_id=1, source_target_pairs={{0,16},{16,0},{1,17},{17,1},{2,18},{18,2},{3,19},{19,3},{4,20},{20... | collective-permute-start | bytes 6291464 | tf_op jit(solution)/shard_map/ppermute | solution.py:434
  562.4 39.9 %collective-permute-start.81 = (bf16[1024,1024]{1,0:T(8,128)(2,1)S(1)}, bf16[1024,1024]{1,0:T(8,128)(2,1)S(1)}, u32[]{:S(2)}, u32[]{:S(2)}) collective-permute-start(bf16[1024,1024]{1,0:T(8,128)(2,1)S(1)} %convolution_convert_fusion.2), channel_id=1, source_target_pairs={{0,16},{16,0},{1,17},{17,1},{2,18},{18,2},{3,19},{19,3},{4,20},{20... | collective-permute-start | bytes 6291464 | tf_op jit(solution)/shard_map/ppermute | solution.py:434
  610.2 35.2 %collective-permute-start.83 = (bf16[1024,256]{1,0:T(8,128)(2,1)S(1)}, bf16[1024,256]{1,0:T(8,128)(2,1)S(1)}, u32[]{:S(2)}, u32[]{:S(2)}) collective-permute-start(bf16[1024,256]{1,0:T(8,128)(2,1)S(1)} %get-tuple-element.405), channel_id=1, source_target_pairs={{0,2},{1,3},{2,0},{3,1},{4,6},{5,7},{6,4},{7,5},{8,10},{9,11},{10,... | collective-permute-start | bytes 1572872 | tf_op jit(solution)/shard_map/ppermute | solution.py:439
  611.1 39.2 %collective-permute-start.84 = (bf16[1024,256]{1,0:T(8,128)(2,1)S(1)}, bf16[1024,256]{1,0:T(8,128)(2,1)S(1)}, u32[]{:S(2)}, u32[]{:S(2)}) collective-permute-start(bf16[1024,256]{1,0:T(8,128)(2,1)S(1)} %get-tuple-element.406), channel_id=1, source_target_pairs={{0,3},{1,2},{2,1},{3,0},{4,7},{5,6},{6,5},{7,4},{8,11},{9,10},{10,... | collective-permute-start | bytes 1572872 | tf_op jit(solution)/shard_map/ppermute | solution.py:439
  626.0 61.6 %collective-permute-start.92 = (bf16[2,1024,256]{2,1,0:T(8,128)(2,1)S(1)}, bf16[2,1024,256]{2,1,0:T(8,128)(2,1)S(1)}, u32[]{:S(2)}, u32[]{:S(2)}) collective-permute-start(bf16[2,1024,256]{2,1,0:T(8,128)(2,1)S(1)} %pad_maximum_fusion.23), channel_id=1, source_target_pairs={{0,4},{12,8},{1,5},{13,9},{2,6},{14,10},{3,7},{15,11},{16,20},{28,... | collective-permute-start | bytes 3145736 | tf_op jit(solution)/shard_map/ppermute | solution.py:570
  633.0 55.7 %collective-permute-start.91 = (bf16[2,1024,256]{2,1,0:T(8,128)(2,1)S(1)}, bf16[2,1024,256]{2,1,0:T(8,128)(2,1)S(1)}, u32[]{:S(2)}, u32[]{:S(2)}) collective-permute-start(bf16[2,1024,256]{2,1,0:T(8,128)(2,1)S(1)} %pad_maximum_fusion.22), channel_id=1, source_target_pairs={{0,4},{12,8},{1,5},{13,9},{2,6},{14,10},{3,7},{15,11},{16,20},{28,... | collective-permute-start | bytes 3145736 | tf_op jit(solution)/shard_map/ppermute | solution.py:570
  685.6 45.3 %collective-permute-start.89 = (bf16[512,1024]{1,0:T(8,128)(2,1)S(1)}, bf16[512,1024]{1,0:T(8,128)(2,1)S(1)}, u32[]{:S(2)}, u32[]{:S(2)}) collective-permute-start(bf16[512,1024]{1,0:T(8,128)(2,1)S(1)} %add_convert_fusion.27), channel_id=1, source_target_pairs={{4,0},{8,12},{5,1},{9,13},{6,2},{10,14},{7,3},{11,15},{20,16},{24,... | collective-permute-start | bytes 3145736 | tf_op jit(solution)/shard_map/ppermute | solution.py:570
  730.9 38.4 %collective-permute-start.98 = (bf16[2,1024,256]{2,1,0:T(8,128)(2,1)S(1)}, bf16[2,1024,256]{2,1,0:T(8,128)(2,1)}, u32[]{:S(2)}, u32[]{:S(2)}) collective-permute-start(bf16[2,1024,256]{2,1,0:T(8,128)(2,1)S(1)} %pad_maximum_fusion.25), channel_id=1, source_target_pairs={{0,4},{12,8},{1,5},{13,9},{2,6},{14,10},{3,7},{15,11},{16,20},{28,... | collective-permute-start | bytes 3145736 | tf_op jit(solution)/shard_map/ppermute | solution.py:570
  734.6 42.6 %collective-permute-start.97 = (bf16[2,1024,256]{2,1,0:T(8,128)(2,1)S(1)}, bf16[2,1024,256]{2,1,0:T(8,128)(2,1)}, u32[]{:S(2)}, u32[]{:S(2)}) collective-permute-start(bf16[2,1024,256]{2,1,0:T(8,128)(2,1)S(1)} %pad_maximum_fusion.24), channel_id=1, source_target_pairs={{0,4},{12,8},{1,5},{13,9},{2,6},{14,10},{3,7},{15,11},{16,20},{28,... | collective-permute-start | bytes 3145736 | tf_op jit(solution)/shard_map/ppermute | solution.py:570
  736.8 41.9 %collective-permute-start.96 = (bf16[2,1024,256]{2,1,0:T(8,128)(2,1)S(1)}, bf16[2,1024,256]{2,1,0:T(8,128)(2,1)}, u32[]{:S(2)}, u32[]{:S(2)}) collective-permute-start(bf16[2,1024,256]{2,1,0:T(8,128)(2,1)S(1)} %add_convert_fusion.24), channel_id=1, source_target_pairs={{4,8},{8,4},{5,9},{9,5},{6,10},{10,6},{7,11},{11,7},{20,24},{24,20... | collective-permute-start | bytes 3145736 | tf_op jit(solution)/shard_map/ppermute | solution.py:570
  738.4 41.8 %collective-permute-start.95 = (bf16[2,1024,256]{2,1,0:T(8,128)(2,1)S(1)}, bf16[2,1024,256]{2,1,0:T(8,128)(2,1)}, u32[]{:S(2)}, u32[]{:S(2)}) collective-permute-start(bf16[2,1024,256]{2,1,0:T(8,128)(2,1)S(1)} %add_convert_fusion.25), channel_id=1, source_target_pairs={{4,8},{8,4},{5,9},{9,5},{6,10},{10,6},{7,11},{11,7},{20,24},{24,20... | collective-permute-start | bytes 3145736 | tf_op jit(solution)/shard_map/ppermute | solution.py:570
  783.3 35.6 %collective-permute-start.118 = (bf16[4,80,256]{2,1,0:T(8,128)(2,1)S(1)}, bf16[4,80,256]{2,1,0:T(8,128)(2,1)S(1)}, u32[]{:S(2)}, u32[]{:S(2)}) collective-permute-start(bf16[4,80,256]{2,1,0:T(8,128)(2,1)S(1)} %add_convert_fusion.35), channel_id=1, source_target_pairs={{4,8},{8,4},{5,9},{9,5},{6,10},{10,6},{7,11},{11,7},{20,24},{24,20... | collective-permute-start | bytes 491528 | tf_op jit(solution)/shard_map/ppermute | solution.py:570
  810.9 36.3 %collective-permute-start.120 = (bf16[512,1024]{1,0:T(8,128)(2,1)S(1)}, bf16[512,1024]{1,0:T(8,128)(2,1)S(1)}, u32[]{:S(2)}, u32[]{:S(2)}) collective-permute-start(bf16[512,1024]{1,0:T(8,128)(2,1)S(1)} %add_convert_fusion.22), channel_id=1, source_target_pairs={{0,4},{12,8},{1,5},{13,9},{2,6},{14,10},{3,7},{15,11},{16,20},{28,... | collective-permute-start | bytes 3145736 | tf_op jit(solution)/shard_map/ppermute | solution.py:570
  816.8 39.3 %collective-permute-start.119 = (bf16[512,1024]{1,0:T(8,128)(2,1)S(1)}, bf16[512,1024]{1,0:T(8,128)(2,1)S(1)}, u32[]{:S(2)}, u32[]{:S(2)}) collective-permute-start(bf16[512,1024]{1,0:T(8,128)(2,1)S(1)} %add_convert_fusion.23), channel_id=1, source_target_pairs={{0,4},{12,8},{1,5},{13,9},{2,6},{14,10},{3,7},{15,11},{16,20},{28,... | collective-permute-start | bytes 3145736 | tf_op jit(solution)/shard_map/ppermute | solution.py:570
  818.2 39.5 %collective-permute-start.117 = (bf16[2,1024,256]{2,1,0:T(8,128)(2,1)S(1)}, bf16[2,1024,256]{2,1,0:T(8,128)(2,1)S(1)}, u32[]{:S(2)}, u32[]{:S(2)}) collective-permute-start(bf16[2,1024,256]{2,1,0:T(8,128)(2,1)S(1)} %add_convert_fusion.18), channel_id=1, source_target_pairs={{4,8},{8,4},{5,9},{9,5},{6,10},{10,6},{7,11},{11,7},{20,24},{24,20... | collective-permute-start | bytes 3145736 | tf_op jit(solution)/shard_map/ppermute | solution.py:570
  819.0 45.9 %collective-permute-start.116 = (bf16[2,1024,256]{2,1,0:T(8,128)(2,1)S(1)}, bf16[2,1024,256]{2,1,0:T(8,128)(2,1)S(1)}, u32[]{:S(2)}, u32[]{:S(2)}) collective-permute-start(bf16[2,1024,256]{2,1,0:T(8,128)(2,1)S(1)} %add_convert_fusion.19), channel_id=1, source_target_pairs={{4,8},{8,4},{5,9},{9,5},{6,10},{10,6},{7,11},{11,7},{20,24},{24,20... | collective-permute-start | bytes 3145736 | tf_op jit(solution)/shard_map/ppermute | solution.py:570
  842.8 56.2 %collective-permute-start.104 = (bf16[1024,1024]{1,0:T(8,128)(2,1)S(1)}, bf16[1024,1024]{1,0:T(8,128)(2,1)S(1)}, u32[]{:S(2)}, u32[]{:S(2)}) collective-permute-start(bf16[1024,1024]{1,0:T(8,128)(2,1)S(1)} %convolution_convert_fusion), channel_id=1, source_target_pairs={{0,16},{16,0},{1,17},{17,1},{2,18},{18,2},{3,19},{19,3},{4,20},{20... | collective-permute-start | bytes 6291464 | tf_op jit(solution)/shard_map/ppermute | solution.py:434
  856.2 41.7 %collective-permute-start.114 = (bf16[2,1024,256]{2,1,0:T(8,128)(2,1)S(1)}, bf16[2,1024,256]{2,1,0:T(8,128)(2,1)S(1)}, u32[]{:S(2)}, u32[]{:S(2)}) collective-permute-start(bf16[2,1024,256]{2,1,0:T(8,128)(2,1)S(1)} %add_convert_fusion.21), channel_id=1, source_target_pairs={{4,0},{8,12},{5,1},{9,13},{6,2},{10,14},{7,3},{11,15},{20,16},{24,... | collective-permute-start | bytes 3145736 | tf_op jit(solution)/shard_map/ppermute | solution.py:570
  857.7 45.5 %collective-permute-start.100 = (bf16[1024,1024]{1,0:T(8,128)(2,1)S(1)}, bf16[1024,1024]{1,0:T(8,128)(2,1)S(1)}, u32[]{:S(2)}, u32[]{:S(2)}) collective-permute-start(bf16[1024,1024]{1,0:T(8,128)(2,1)S(1)} %convolution_convert_fusion.1), channel_id=1, source_target_pairs={{0,16},{16,0},{1,17},{17,1},{2,18},{18,2},{3,19},{19,3},{4,20},{20... | collective-permute-start | bytes 6291464 | tf_op jit(solution)/shard_map/ppermute | solution.py:434
  904.7 42.5 %collective-permute-start.102 = (bf16[1024,256]{1,0:T(8,128)(2,1)S(1)}, bf16[1024,256]{1,0:T(8,128)(2,1)S(1)}, u32[]{:S(2)}, u32[]{:S(2)}) collective-permute-start(bf16[1024,256]{1,0:T(8,128)(2,1)S(1)} %get-tuple-element.401), channel_id=1, source_target_pairs={{0,2},{1,3},{2,0},{3,1},{4,6},{5,7},{6,4},{7,5},{8,10},{9,11},{10,... | collective-permute-start | bytes 1572872 | tf_op jit(solution)/shard_map/ppermute | solution.py:439
  905.5 43.0 %collective-permute-start.103 = (bf16[1024,256]{1,0:T(8,128)(2,1)S(1)}, bf16[1024,256]{1,0:T(8,128)(2,1)S(1)}, u32[]{:S(2)}, u32[]{:S(2)}) collective-permute-start(bf16[1024,256]{1,0:T(8,128)(2,1)S(1)} %get-tuple-element.402), channel_id=1, source_target_pairs={{0,3},{1,2},{2,1},{3,0},{4,7},{5,6},{6,5},{7,4},{8,11},{9,10},{10,... | collective-permute-start | bytes 1572872 | tf_op jit(solution)/shard_map/ppermute | solution.py:439
  925.7 39.2 %collective-permute-start.131 = (bf16[2,1024,256]{2,1,0:T(8,128)(2,1)S(1)}, bf16[2,1024,256]{2,1,0:T(8,128)(2,1)S(1)}, u32[]{:S(2)}, u32[]{:S(2)}) collective-permute-start(bf16[2,1024,256]{2,1,0:T(8,128)(2,1)S(1)} %pad_maximum_fusion.29), channel_id=1, source_target_pairs={{0,4},{12,8},{1,5},{13,9},{2,6},{14,10},{3,7},{15,11},{16,20},{28,... | collective-permute-start | bytes 3145736 | tf_op jit(solution)/shard_map/ppermute | solution.py:570
  965.0 42.0 %collective-permute-start.125 = (bf16[2,1024,256]{2,1,0:T(8,128)(2,1)S(1)}, bf16[2,1024,256]{2,1,0:T(8,128)(2,1)S(1)}, u32[]{:S(2)}, u32[]{:S(2)}) collective-permute-start(bf16[2,1024,256]{2,1,0:T(8,128)(2,1)S(1)} %add_convert_fusion.17), channel_id=1, source_target_pairs={{4,0},{8,12},{5,1},{9,13},{6,2},{10,14},{7,3},{11,15},{20,16},{24,... | collective-permute-start | bytes 3145736 | tf_op jit(solution)/shard_map/ppermute | solution.py:570
  1012.4 37.8 %collective-permute-start.146 = (bf16[2,1024,256]{2,1,0:T(8,128)(2,1)}, bf16[2,1024,256]{2,1,0:T(8,128)(2,1)}, u32[]{:S(2)}, u32[]{:S(2)}) collective-permute-start(bf16[2,1024,256]{2,1,0:T(8,128)(2,1)} %pad_maximum_fusion.27), channel_id=1, source_target_pairs={{0,4},{12,8},{1,5},{13,9},{2,6},{14,10},{3,7},{15,11},{16,20},{28,... | collective-permute-start | bytes 3145736 | tf_op jit(solution)/shard_map/ppermute | solution.py:570
  1037.4 60.3 %collective-permute-start.145 = (bf16[2,1024,256]{2,1,0:T(8,128)(2,1)}, bf16[2,1024,256]{2,1,0:T(8,128)(2,1)}, u32[]{:S(2)}, u32[]{:S(2)}) collective-permute-start(bf16[2,1024,256]{2,1,0:T(8,128)(2,1)} %pad_maximum_fusion.26), channel_id=1, source_target_pairs={{0,4},{12,8},{1,5},{13,9},{2,6},{14,10},{3,7},{15,11},{16,20},{28,... | collective-permute-start | bytes 3145736 | tf_op jit(solution)/shard_map/ppermute | solution.py:570
  1041.7 59.4 %collective-permute-start.144 = (bf16[2,1024,256]{2,1,0:T(8,128)(2,1)}, bf16[2,1024,256]{2,1,0:T(8,128)(2,1)}, u32[]{:S(2)}, u32[]{:S(2)}) collective-permute-start(bf16[2,1024,256]{2,1,0:T(8,128)(2,1)} %add_convert_fusion.10), channel_id=1, source_target_pairs={{4,8},{8,4},{5,9},{9,5},{6,10},{10,6},{7,11},{11,7},{20,24},{24,20... | collective-permute-start | bytes 3145736 | tf_op jit(solution)/shard_map/ppermute | solution.py:570
  1047.7 33.7 %collective-permute-start.136 = (bf16[512,512]{1,0:T(8,128)(2,1)}, bf16[512,512]{1,0:T(8,128)(2,1)S(1)}, u32[]{:S(2)}, u32[]{:S(2)}) collective-permute-start(bf16[512,512]{1,0:T(8,128)(2,1)} %get-tuple-element.385), channel_id=1, source_target_pairs={{0,8},{4,12},{8,0},{12,4},{1,9},{5,13},{9,1},{13,5},{2,10},{6,14},... | collective-permute-start | bytes 1572872 | tf_op jit(solution)/shard_map/ppermute | solution.py:444
  1050.3 44.6 %collective-permute-start.137 = (bf16[512,512]{1,0:T(8,128)(2,1)}, bf16[512,512]{1,0:T(8,128)(2,1)S(1)}, u32[]{:S(2)}, u32[]{:S(2)}) collective-permute-start(bf16[512,512]{1,0:T(8,128)(2,1)} %get-tuple-element.384), channel_id=1, source_target_pairs={{0,12},{4,8},{8,4},{12,0},{1,13},{5,9},{9,5},{13,1},{2,14},{6,10},... | collective-permute-start | bytes 1572872 | tf_op jit(solution)/shard_map/ppermute | solution.py:444
  1053.7 50.7 %collective-permute-start.143 = (bf16[2,1024,256]{2,1,0:T(8,128)(2,1)S(1)}, bf16[2,1024,256]{2,1,0:T(8,128)(2,1)S(1)}, u32[]{:S(2)}, u32[]{:S(2)}) collective-permute-start(bf16[2,1024,256]{2,1,0:T(8,128)(2,1)S(1)} %add_convert_fusion.11), channel_id=1, source_target_pairs={{4,8},{8,4},{5,9},{9,5},{6,10},{10,6},{7,11},{11,7},{20,24},{24,20... | collective-permute-start | bytes 3145736 | tf_op jit(solution)/shard_map/ppermute | solution.py:570
  1094.9 38.1 %collective-permute-start.141 = (bf16[512,1024]{1,0:T(8,128)(2,1)S(1)}, bf16[512,1024]{1,0:T(8,128)(2,1)S(1)}, u32[]{:S(2)}, u32[]{:S(2)}) collective-permute-start(bf16[512,1024]{1,0:T(8,128)(2,1)S(1)} %copy-done.33), channel_id=1, source_target_pairs={{4,0},{8,12},{5,1},{9,13},{6,2},{10,14},{7,3},{11,15},{20,16},{24,... | collective-permute-start | bytes 3145736 | tf_op jit(solution)/shard_map/ppermute | solution.py:570
  1097.7 36.5 %collective-permute-start.138 = (bf16[512,512]{1,0:T(8,128)(2,1)S(1)}, bf16[512,512]{1,0:T(8,128)(2,1)S(1)}, u32[]{:S(2)}, u32[]{:S(2)}) collective-permute-start(bf16[512,512]{1,0:T(8,128)(2,1)S(1)} %get-tuple-element.382), channel_id=1, source_target_pairs={{0,1},{1,0},{2,3},{3,2},{4,5},{5,4},{6,7},{7,6},{8,9},{9,8},{10,11... | collective-permute-start | bytes 1572872 | tf_op jit(solution)/shard_map/ppermute | solution.py:439
  1101.1 33.0 %collective-permute-start.139 = (bf16[512,512]{1,0:T(8,128)(2,1)S(1)}, bf16[512,512]{1,0:T(8,128)(2,1)S(1)}, u32[]{:S(2)}, u32[]{:S(2)}) collective-permute-start(bf16[512,512]{1,0:T(8,128)(2,1)S(1)} %get-tuple-element.381), channel_id=1, source_target_pairs={{0,2},{1,3},{2,0},{3,1},{4,6},{5,7},{6,4},{7,5},{8,10},{9,11},{10,... | collective-permute-start | bytes 1572872 | tf_op jit(solution)/shard_map/ppermute | solution.py:439
  1156.1 64.2 %collective-permute-start.157 = (bf16[2,1024,256]{2,1,0:T(8,128)(2,1)S(1)}, bf16[2,1024,256]{2,1,0:T(8,128)(2,1)}, u32[]{:S(2)}, u32[]{:S(2)}) collective-permute-start(bf16[2,1024,256]{2,1,0:T(8,128)(2,1)S(1)} %copy-done.31), channel_id=1, source_target_pairs={{4,8},{8,4},{5,9},{9,5},{6,10},{10,6},{7,11},{11,7},{20,24},{24,20... | collective-permute-start | bytes 3145736 | tf_op jit(solution)/shard_map/ppermute | solution.py:570
  1163.2 61.4 %collective-permute-start.156 = (bf16[2,1024,256]{2,1,0:T(8,128)(2,1)}, bf16[2,1024,256]{2,1,0:T(8,128)(2,1)}, u32[]{:S(2)}, u32[]{:S(2)}) collective-permute-start(bf16[2,1024,256]{2,1,0:T(8,128)(2,1)} %add_convert_fusion.7), channel_id=1, source_target_pairs={{4,8},{8,4},{5,9},{9,5},{6,10},{10,6},{7,11},{11,7},{20,24},{24,20... | collective-permute-start | bytes 3145736 | tf_op jit(solution)/shard_map/ppermute | solution.py:570
  1165.6 61.0 %collective-permute-start.155 = (bf16[2,1024,256]{2,1,0:T(8,128)(2,1)}, bf16[2,1024,256]{2,1,0:T(8,128)(2,1)S(1)}, u32[]{:S(2)}, u32[]{:S(2)}) collective-permute-start(bf16[2,1024,256]{2,1,0:T(8,128)(2,1)} %add_convert_fusion.8), channel_id=1, source_target_pairs={{4,0},{8,12},{5,1},{9,13},{6,2},{10,14},{7,3},{11,15},{20,16},{24,... | collective-permute-start | bytes 3145736 | tf_op jit(solution)/shard_map/ppermute | solution.py:570
  1168.4 59.7 %collective-permute-start.154 = (bf16[2,1024,256]{2,1,0:T(8,128)(2,1)}, bf16[2,1024,256]{2,1,0:T(8,128)(2,1)S(1)}, u32[]{:S(2)}, u32[]{:S(2)}) collective-permute-start(bf16[2,1024,256]{2,1,0:T(8,128)(2,1)} %add_convert_fusion.9), channel_id=1, source_target_pairs={{4,0},{8,12},{5,1},{9,13},{6,2},{10,14},{7,3},{11,15},{20,16},{24,... | collective-permute-start | bytes 3145736 | tf_op jit(solution)/shard_map/ppermute | solution.py:570
  1172.4 46.5 %collective-permute-start.152 = (f32[2,28099]{1,0:T(2,128)S(1)}, f32[2,28099]{1,0:T(2,128)S(1)}, u32[]{:S(2)}, u32[]{:S(2)}) collective-permute-start(f32[2,28099]{1,0:T(2,128)S(1)} %add.913), channel_id=1, source_target_pairs={{0,4},{4,0},{8,12},{12,8},{1,5},{5,1},{9,13},{13,9},{2,6},{6,2},{1... | collective-permute-start | bytes 674384 | tf_op jit(solution)/shard_map/ppermute | solution.py:542
  1242.2 54.6 %collective-permute-start.160 = (bf16[2,1024,256]{2,1,0:T(8,128)(2,1)S(1)}, bf16[2,1024,256]{2,1,0:T(8,128)(2,1)}, u32[]{:S(2)}, u32[]{:S(2)}) collective-permute-start(bf16[2,1024,256]{2,1,0:T(8,128)(2,1)S(1)} %add_convert_fusion.4), channel_id=1, source_target_pairs={{4,0},{8,12},{5,1},{9,13},{6,2},{10,14},{7,3},{11,15},{20,16},{24,... | collective-permute-start | bytes 3145736 | tf_op jit(solution)/shard_map/ppermute | solution.py:570
  1243.5 56.0 %collective-permute-start.159 = (bf16[2,1024,256]{2,1,0:T(8,128)(2,1)S(1)}, bf16[2,1024,256]{2,1,0:T(8,128)(2,1)S(1)}, u32[]{:S(2)}, u32[]{:S(2)}) collective-permute-start(bf16[2,1024,256]{2,1,0:T(8,128)(2,1)S(1)} %add_convert_fusion.5), channel_id=1, source_target_pairs={{4,0},{8,12},{5,1},{9,13},{6,2},{10,14},{7,3},{11,15},{20,16},{24,... | collective-permute-start | bytes 3145736 | tf_op jit(solution)/shard_map/ppermute | solution.py:570
  1245.1 79.7 %collective-permute-start.166 = (bf16[2,1024,256]{2,1,0:T(8,128)(2,1)}, bf16[2,1024,256]{2,1,0:T(8,128)(2,1)}, u32[]{:S(2)}, u32[]{:S(2)}) collective-permute-start(bf16[2,1024,256]{2,1,0:T(8,128)(2,1)} %broadcast_select_fusion.15.refs_4_), channel_id=1, source_target_pairs={{0,16},{1,17},{2,18},{3,19},{4,20},{5,21},{6,22},{7,23},{8,24},{9,... | collective-permute-start | bytes 3145736 | tf_op jit(solution)/shard_map/ppermute | solution.py:1005
  1246.4 80.0 %collective-permute-start.167 = (bf16[2,1024,256]{2,1,0:T(8,128)(2,1)}, bf16[2,1024,256]{2,1,0:T(8,128)(2,1)}, u32[]{:S(2)}, u32[]{:S(2)}) collective-permute-start(bf16[2,1024,256]{2,1,0:T(8,128)(2,1)} %broadcast_select_fusion.14.refs_5_), channel_id=1, source_target_pairs={{0,16},{1,17},{2,18},{3,19},{4,20},{5,21},{6,22},{7,23},{8,24},{9,... | collective-permute-start | bytes 3145736 | tf_op jit(solution)/shard_map/ppermute | solution.py:1005
  1254.8 40.0 %collective-permute-start.161 = (bf16[4,80,256]{2,1,0:T(8,128)(2,1)S(1)}, bf16[4,80,256]{2,1,0:T(8,128)(2,1)S(1)}, u32[]{:S(2)}, u32[]{:S(2)}) collective-permute-start(bf16[4,80,256]{2,1,0:T(8,128)(2,1)S(1)} %add_convert_fusion.32), channel_id=1, source_target_pairs={{4,0},{8,12},{5,1},{9,13},{6,2},{10,14},{7,3},{11,15},{20,16},{24,... | collective-permute-start | bytes 491528 | tf_op jit(solution)/shard_map/ppermute | solution.py:570
  1294.8 34.8 %collective-permute-start.171 = (bf16[4,80,256]{2,1,0:T(8,128)(2,1)}, bf16[4,80,256]{2,1,0:T(8,128)(2,1)}, u32[]{:S(2)}, u32[]{:S(2)}) collective-permute-start(bf16[4,80,256]{2,1,0:T(8,128)(2,1)} %broadcast_select_fusion.36), channel_id=1, source_target_pairs={{0,16},{1,17},{2,18},{3,19},{4,20},{5,21},{6,22},{7,23},{8,24},{9,... | collective-permute-start | bytes 491528 | tf_op jit(solution)/shard_map/ppermute | solution.py:1005
  1296.8 34.2 %collective-permute-start.168 = (bf16[2,1024,256]{2,1,0:T(8,128)(2,1)}, bf16[2,1024,256]{2,1,0:T(8,128)(2,1)}, u32[]{:S(2)}, u32[]{:S(2)}) collective-permute-start(bf16[2,1024,256]{2,1,0:T(8,128)(2,1)} %broadcast_select_fusion.13.refs_6_), channel_id=1, source_target_pairs={{0,16},{1,17},{2,18},{3,19},{4,20},{5,21},{6,22},{7,23},{8,24},{9,... | collective-permute-start | bytes 3145736 | tf_op jit(solution)/shard_map/ppermute | solution.py:1005
  (238 other events, 5146.1 us)

commit v4 on v3

v4 whole, which is shorter than its diff:
```python
import functools

import jax
import jax.numpy as jnp
from jax import lax
from jax.experimental import pallas as pl
from jax.experimental.pallas import tpu as pltpu
from jax.sharding import PartitionSpec as P

D = 2048
INNER = 4096
HEADS = 64
HEAD_DIM = 64
STATE = 128
KERNEL = 4
GROUP = 2 * STATE
CHANNELS = INNER + GROUP
LANES = 128
EPS = 1e-05
F32 = jnp.float32
BF16 = jnp.bfloat16
VMEM_BYTES = 48 * 1024 * 1024


def split(v):
    hi = v.astype(BF16)
    return hi, (v - hi.astype(F32)).astype(BF16)


def dot32(a, b, ca, cb):
    (ah, al), (bh, bl) = (v if isinstance(v, tuple) else split(v) for v in (a, b))
    one = lambda p, q: lax.dot_general(
        p, q, (((ca,), (cb,)), ((), ())), preferred_element_type=F32
    )
    return one(ah, bh) + (one(ah, bl) + one(al, bh))


def step_sizes(raw, hp, rows):
    shifted = raw + hp[0:1, :]
    dt = jnp.maximum(shifted, 0.0) + jnp.log1p(jnp.exp(-jnp.abs(shifted)))
    decay = dt * hp[1:2, :]
    row = lax.broadcasted_iota(jnp.int32, (rows, rows), 0)
    col = lax.broadcasted_iota(jnp.int32, (rows, rows), 1)
    lower = (row >= col).astype(F32)
    cum = dot32(lower, decay, 1, 0)
    cum_t = dot32(decay, lower, 0, 1)
    return shifted, dt, cum, cum_t, row, col, lower


def pair_lanes(v, j, first):
    return jnp.where(first, v[:, 2 * j : 2 * j + 1], v[:, 2 * j + 1 : 2 * j + 2])


def head_sums(v, table):
    hi, low = split(v)
    one = lambda p: lax.dot_general(
        p, table, (((1,), (1,)), ((), ())), preferred_element_type=F32
    )
    return one(hi) + one(low)


def forward_kernel(proj, cw, hp, s0, e0, y_ref, filt_ref, st_ref, state, xp, xw_s, last_s):
    i = pl.program_id(0)
    rows, width = y_ref.shape

    @pl.when(i == 0)
    def _():
        state[...] = s0[...]
        xp[0:8, :] = e0[...]

    xp[8 : 8 + rows, :] = proj[:, : width + GROUP]

    def conv_tile(lo):
        acc = cw[4:5, lo : lo + LANES]
        for k in range(KERNEL):
            acc = acc + cw[k : k + 1, lo : lo + LANES] * xp[5 + k : 5 + k + rows, lo : lo + LANES]
        filt_ref[:, lo : lo + LANES] = acc
        return acc * jax.nn.sigmoid(acc)

    b_c = conv_tile(width)
    c_c = conv_tile(width + STATE)
    _, dt, cum, cum_t, row, col, _ = step_sizes(proj[:, width + GROUP :], hp, rows)
    last = cum[rows - 1 : rows, :]
    ecum = jnp.exp(cum)
    weight = jnp.exp(last - cum) * dt
    elast = jnp.exp(last)
    b_c, c_c = split(b_c), split(c_c)
    carried = dot32(c_c, state[...], 1, 0)
    scores = dot32(c_c, b_c, 1, 1)
    causal = row >= col
    lane = lax.broadcasted_iota(jnp.int32, (rows, LANES), 1)
    first = lane < HEAD_DIM
    for j in range(width // LANES):
        lo = j * LANES
        here = slice(lo, lo + LANES)
        x = conv_tile(lo)
        xd = x * pair_lanes(dt, j, first)
        m = []
        for h in (2 * j, 2 * j + 1):
            gap = cum[:, h : h + 1] - cum_t[h : h + 1, :]
            m.append(jnp.exp(jnp.where(causal, gap, -1e30)) * scores)
        xd2 = jnp.concatenate([jnp.where(first, xd, 0.0), jnp.where(first, 0.0, xd)])
        y = (
            dot32(jnp.concatenate(m, axis=1), xd2, 1, 0)
            + carried[:, here] * pair_lanes(ecum, j, first)
            + pair_lanes(hp[2:3, :], j, first[0:1]) * x
        )
        y_ref[:, here] = y
        xw_s[:, here] = x * pair_lanes(weight, j, first)
        last_s[0:1, here] = pair_lanes(elast, j, first[0:1])
    state[...] = state[...] * last_s[0:1, :] + dot32(b_c, xw_s[...], 0, 0)
    st_ref[0] = state[...]
    xp[0:8, :] = xp[rows : rows + 8, :]


def backward_kernel(
    pz,
    proj,
    y_ref,
    filt,
    dn,
    rc,
    st_before,
    st_out,
    s0,
    cw,
    hp,
    table,
    gain,
    g0,
    e0,
    dz_ref,
    dproj,
    dbc_ref,
    dgain_ref,
    dconv_ref,
    dhp_ref,
    gfin_ref,
    efin_ref,
    grad,
    dfp,
    both,
    xw_s,
    dyc_s,
    rowv,
):
    i = pl.program_id(0)
    rows, width = y_ref.shape
    heads = hp.shape[1]

    @pl.when(i == 0)
    def _():
        grad[...] = g0[...]
        dfp[rows : rows + 8, :] = e0[...]
        dgain_ref[...] = jnp.zeros_like(dgain_ref)
        dconv_ref[...] = jnp.zeros_like(dconv_ref)
        dhp_ref[...] = jnp.zeros_like(dhp_ref)

    def silu_pair(v):
        s = jax.nn.sigmoid(v)
        a = v * s
        return a, s * (1.0 + v - a)

    b_c, b_d = silu_pair(filt[:, width : width + STATE])
    c_c, c_d = silu_pair(filt[:, width + STATE :])
    shifted, dt, cum, cum_t, row, col, lower = step_sizes(proj[:, width + GROUP :], hp, rows)
    last = cum[rows - 1 : rows, :]
    tail = jnp.exp(last - cum)
    ecum = jnp.exp(cum)
    elast = jnp.exp(last)
    b_c, c_c = split(b_c), split(c_c)
    grad_p = split(grad[...])
    k_all = dot32(b_c, grad_p, 1, 0)
    scores_t = dot32(b_c, c_c, 1, 1)
    causal_t = row <= col
    lane = lax.broadcasted_iota(jnp.int32, (rows, LANES), 1)
    first = lane < HEAD_DIM
    dcb_t = jnp.zeros((rows, rows), F32)
    rc_t = dot32((row == col).astype(F32), rc[0], 1, 1)
    r = rc_t[:, 0:1]
    coef = rc_t[:, 1:2]
    rowv[0:1, :] = jnp.sum(grad[...] * st_out[0], axis=0, keepdims=True)
    for j in range(width // LANES):
        lo = j * LANES
        here = slice(lo, lo + LANES)
        z = pz[:, here]
        y = y_ref[:, here]
        sz, dsz = silu_pair(z)
        g = y * sz
        dnt = dn[:, here]
        dg = dnt * gain[0:1, here] * r - g * coef
        dgain_ref[0:1, here] += jnp.sum(dnt * g * r, axis=0, keepdims=True)
        dy = dg * sz
        dz_ref[:, here] = (dg * y * dsz).astype(BF16)
        x, xder = silu_pair(filt[:, here])
        dt_e = pair_lanes(dt, j, first)
        tail_e = pair_lanes(tail, j, first)
        xd = x * dt_e
        dy2 = split(jnp.concatenate([jnp.where(first, dy, 0.0), jnp.where(first, 0.0, dy)]))
        decays = []
        for h in (2 * j, 2 * j + 1):
            gap = cum_t[h : h + 1, :] - cum[:, h : h + 1]
            decays.append(jnp.exp(jnp.where(causal_t, gap, -1e30)))
        m = jnp.concatenate([d * scores_t for d in decays], axis=1)
        dm = dot32(xd, dy2, 1, 1)
        dcb_t = dcb_t + (decays[0] * dm[:, :rows] + decays[1] * dm[:, rows:])
        v = dot32(m, dy2, 1, 0) + k_all[:, here] * tail_e
        skip = pair_lanes(hp[2:3, :], j, first[0:1])
        dx = dt_e * v + skip * dy
        both[0:rows, here] = x * v
        both[rows : 2 * rows, here] = dy * (y - skip * x)
        rowv[1:2, here] = jnp.sum(dy * x, axis=0, keepdims=True)
        rowv[2:3, here] = pair_lanes(elast, j, first[0:1])
        xw_s[:, here] = xd * tail_e
        dyc_s[:, here] = dy * pair_lanes(ecum, j, first)
        dfp[0:rows, here] = dx * xder
    dcb_t = split(dcb_t)
    dyc = split(dyc_s[...])
    st_in = jnp.where(i == pl.num_programs(0) - 1, s0[...], st_before[0])
    dc = dot32(dcb_t, b_c, 0, 0) + dot32(dyc, st_in, 1, 1)
    db = dot32(dcb_t, c_c, 1, 0) + dot32(xw_s[...], grad_p, 1, 1)
    dfp[0:rows, width : width + STATE] = db * b_d
    dfp[0:rows, width + STATE :] = dc * c_d
    grad[...] = grad[...] * rowv[2:3, :] + dot32(c_c, dyc, 0, 0)
    gfin_ref[...] = grad[...]

    sums = head_sums(both[...], table[...])
    rsums = head_sums(rowv[...], table[...])
    ddt_x = sums[0:rows]
    dcum = sums[rows : 2 * rows] - dt * ddt_x
    upto = lax.broadcasted_iota(jnp.int32, (rows, heads), 0)
    dcum = dcum + jnp.where(upto == rows - 1, rsums[0:1, :], 0.0)
    ddecay = dot32(lower, dcum, 0, 0)
    ddt = ddt_x + hp[1:2, :] * ddecay
    draw = ddt * jax.nn.sigmoid(shifted)
    dproj[:, width + GROUP :] = draw.astype(BF16)
    dhp_ref[0:1, :] += jnp.sum(draw, axis=0, keepdims=True)
    dhp_ref[1:2, :] += jnp.sum(ddecay * dt, axis=0, keepdims=True) * hp[1:2, :]
    dhp_ref[2:3, :] += rsums[1:2, :]

    for lo in range(0, width + GROUP, LANES):
        here = slice(lo, lo + LANES)
        src = proj[:, here]
        total = jnp.zeros((rows, LANES), F32)
        for k in range(KERNEL):
            shift = KERNEL - 1 - k
            moved = dfp[shift : shift + rows, here]
            total = total + cw[k : k + 1, here] * moved
            dconv_ref[k : k + 1, here] += jnp.sum(src * moved, axis=0, keepdims=True)
        dconv_ref[4:5, here] += jnp.sum(dfp[0:rows, here], axis=0, keepdims=True)
        if lo < width:
            dproj[:, here] = total.astype(BF16)
        else:
            dproj[:, here] = jnp.zeros((rows, LANES), BF16)
            share = dbc_ref.shape[2]
            for k in range(LANES // share):
                dbc_ref[(lo - width) // share + k] = total[:, k * share : (k + 1) * share]
    dfp[rows : rows + 8, :] = dfp[0:8, :]
    efin_ref[...] = dfp[0:8, :]


def whole(shape):
    return pl.BlockSpec(shape, lambda i: (0,) * len(shape))


def run_forward(proj, cw, hp, s0, e0, rows):
    total, width = proj.shape[0], s0.shape[1]
    count = total // rows
    block = lambda w: pl.BlockSpec((rows, w), lambda i: (i, 0))
    shape = jax.ShapeDtypeStruct
    return pl.pallas_call(
        forward_kernel,
        grid=(count,),
        in_specs=[block(proj.shape[1])] + [whole(v.shape) for v in (cw, hp, s0, e0)],
        out_specs=[
            block(width),
            block(width + GROUP),
            pl.BlockSpec((1, STATE, width), lambda i: (i, 0, 0)),
        ],
        scratch_shapes=[
            pltpu.VMEM((STATE, width), F32),
            pltpu.VMEM((rows + 8, width + GROUP), F32),
            pltpu.VMEM((rows, width), F32),
            pltpu.VMEM((8, width), F32),
        ],
        out_shape=[
            shape((total, width), F32),
            shape((total, width + GROUP), F32),
            shape((count, STATE, width), F32),
        ],
        compiler_params=pltpu.CompilerParams(vmem_limit_bytes=VMEM_BYTES),
        name="scan_forward",
    )(proj, cw, hp, s0, e0)


def run_backward(pz, proj, y, filt, dn, rc, states, s0, cw, hp, table, gain, g0, e0, rows, places):
    total, (heads, width) = proj.shape[0], table.shape
    count = total // rows
    turn = lambda i: count - 1 - i
    block = lambda w: pl.BlockSpec((rows, w), lambda i: (turn(i), 0))
    shape = jax.ShapeDtypeStruct
    share = GROUP // places
    return pl.pallas_call(
        backward_kernel,
        grid=(count,),
        in_specs=[
            block(width),
            block(proj.shape[1]),
            block(width),
            block(width + GROUP),
            block(width),
            pl.BlockSpec((1, 8, rows), lambda i: (turn(i), 0, 0)),
            pl.BlockSpec((1, STATE, width), lambda i: (jnp.maximum(turn(i) - 1, 0), 0, 0)),
            pl.BlockSpec((1, STATE, width), lambda i: (turn(i), 0, 0)),
        ]
        + [whole(v.shape) for v in (s0, cw, hp, table, gain, g0, e0)],
        out_specs=[
            block(width),
            block(proj.shape[1]),
            pl.BlockSpec((places, rows, share), lambda i: (0, turn(i), 0)),
            whole((8, width)),
            whole((8, width + GROUP)),
            whole((8, heads)),
            whole((STATE, width)),
            whole((8, width + GROUP)),
        ],
        scratch_shapes=[
            pltpu.VMEM((STATE, width), F32),
            pltpu.VMEM((rows + 8, width + GROUP), F32),
            pltpu.VMEM((2 * rows, width), F32),
            pltpu.VMEM((rows, width), F32),
            pltpu.VMEM((rows, width), F32),
            pltpu.VMEM((8, width), F32),
        ],
        out_shape=[
            shape((total, width), BF16),
            shape(proj.shape, BF16),
            shape((places, total, share), F32),
            shape((8, width), F32),
            shape((8, width + GROUP), F32),
            shape((8, heads), F32),
            shape((STATE, width), F32),
            shape((8, width + GROUP), F32),
        ],
        compiler_params=pltpu.CompilerParams(vmem_limit_bytes=VMEM_BYTES),
        name="scan_backward",
    )(pz, proj, y, filt, dn, rc, states, states, s0, cw, hp, table, gain, g0, e0)


def bring(step, pieces, buffers, sems, own):
    for near, far, buffer, sem in zip(*pieces, buffers, sems):
        to, done = buffer.at[step % 2], sem.at[step % 2]

        @pl.when(own)
        def _():
            pltpu.make_async_copy(near[step], to, done).start()

        @pl.when(jnp.logical_not(own))
        def _():
            pltpu.make_async_copy(far[step], to, done).start()


def arrived(step, pieces, buffers, sems):
    for near, buffer, sem in zip(pieces[0], buffers, sems):
        pltpu.make_async_copy(near[step], buffer.at[step % 2], sem.at[step % 2]).wait()
    return [buffer.at[step % 2] for buffer in buffers]


def project_kernel(ids, normed, *refs, layer, n):
    near, far = [refs[0:n]], [refs[n : 2 * n]]
    out, buffer, sem = refs[2 * n :]
    pieces = (near, far)
    own = ids[1] == layer
    columns = out.shape[1]
    share = buffer.shape[2]
    bring(0, pieces, [buffer], [sem], own)
    for m in range(n):
        if m + 1 < n:
            bring(m + 1, pieces, [buffer], [sem], own)
        (w,) = arrived(m, pieces, [buffer], [sem])
        from_place = pl.multiple_of(jnp.bitwise_xor(ids[0], m) * share, share)
        a = normed[:, pl.ds(from_place, share)]
        for lo in range(0, columns, 256):
            here = slice(lo, min(lo + 256, columns))
            v = lax.dot_general(
                a, w[here, :], (((1,), (1,)), ((), ())), preferred_element_type=F32
            )
            out[:, here] = v if m == 0 else out[:, here] + v


def project(ids, normed, near, far, layer):
    n = len(near)
    columns, share = near[0].shape
    rows = normed.shape[0]
    vmem = pl.BlockSpec(memory_space=pltpu.VMEM)
    return pl.pallas_call(
        functools.partial(project_kernel, layer=layer, n=n),
        in_specs=[pl.BlockSpec(memory_space=pltpu.SMEM), vmem]
        + [pl.BlockSpec(memory_space=pl.ANY)] * (2 * n),
        out_specs=vmem,
        scratch_shapes=[
            pltpu.VMEM((2, columns, share), BF16),
            pltpu.SemaphoreType.DMA((2,)),
        ],
        out_shape=jax.ShapeDtypeStruct((rows, columns), F32),
        compiler_params=pltpu.CompilerParams(vmem_limit_bytes=VMEM_BYTES),
        cost_estimate=pl.CostEstimate(
            flops=2 * rows * columns * share * n,
            bytes_accessed=columns * share * n * 2 + rows * columns * 4,
            transcendentals=0,
        ),
        name="project",
    )(ids, normed, *near, *far)


def back_kernel(ids, dz, dx, *refs, layer, n):
    near = (refs[0:n], refs[n : 2 * n])
    far = (refs[2 * n : 3 * n], refs[3 * n : 4 * n])
    out, zbuf, xbuf, zsem, xsem = refs[4 * n :]
    pieces = (near, far)
    own = ids[1] == layer
    share = zbuf.shape[2]
    args = ([zbuf, xbuf], [zsem, xsem])
    bring(0, pieces, *args, own)
    for m in range(n):
        if m + 1 < n:
            bring(m + 1, pieces, *args, own)
        wz, wx = arrived(m, pieces, *args)
        for lo in range(0, share, 256):
            here = slice(lo, lo + 256)
            v = jnp.dot(dz[...], wz[:, here], preferred_element_type=F32) + jnp.dot(
                dx[...], wx[:, here], preferred_element_type=F32
            )
            at_lane = pl.multiple_of(jnp.bitwise_xor(ids[0], m) * share + lo, 256)
            out[:, pl.ds(at_lane, 256)] = v.astype(BF16)


def project_back(ids, dz, dx, near, far, layer):
    n = len(near[0])
    share = near[0][0].shape[1]
    rows = dz.shape[0]
    columns = dz.shape[1] + dx.shape[1]
    vmem = pl.BlockSpec(memory_space=pltpu.VMEM)
    return pl.pallas_call(
        functools.partial(back_kernel, layer=layer, n=n),
        in_specs=[pl.BlockSpec(memory_space=pltpu.SMEM), vmem, vmem]
        + [pl.BlockSpec(memory_space=pl.ANY)] * (4 * n),
        out_specs=vmem,
        scratch_shapes=[
            pltpu.VMEM((2, dz.shape[1], share), BF16),
            pltpu.VMEM((2, dx.shape[1], share), BF16),
            pltpu.SemaphoreType.DMA((2,)),
            pltpu.SemaphoreType.DMA((2,)),
        ],
        out_shape=jax.ShapeDtypeStruct((rows, n * share), BF16),
        compiler_params=pltpu.CompilerParams(vmem_limit_bytes=VMEM_BYTES),
        cost_estimate=pl.CostEstimate(
            flops=2 * rows * columns * share * n,
            bytes_accessed=columns * share * n * 2 + rows * n * share * 2,
            transcendentals=0,
        ),
        name="project_back",
    )(ids, dz, dx, *near[0], *near[1], *far[0], *far[1])


def place_kernel(ids, *refs, plan, small):
    out = refs[-1]
    h, j = pl.program_id(0), pl.program_id(1)
    for ref, (side, layer, first, size, turned) in zip(refs, plan):

        @pl.when((h == side) & (ids[1] == layer) & (j >= first) & (j < first + size))
        def _():
            v = (ref[0] if turned else ref[...]).astype(F32)
            out[...] = v.T if turned else v

    if small:

        @pl.when(j == pl.num_programs(1) - 1)
        def _():
            v = refs[len(plan)]
            out[: v.shape[1], :] = v[0]


def place_blocks(ids, chunks, small, out_shape, block, out_index, steps):
    def step_of(side, layer, first, size, index):
        def where(h, j, ids):
            used = jnp.logical_and(h == side, ids[1] == layer)
            return index(jnp.where(used, jnp.clip(j - first, 0, size - 1), 0))

        return where

    in_specs = [
        pl.BlockSpec(shape, step_of(side, layer, first, size, index))
        for _, side, layer, first, size, _, shape, index in chunks
    ]
    args = [c[0] for c in chunks]
    if small is not None:
        in_specs.append(pl.BlockSpec((1,) + small.shape[1:], lambda h, j, ids: (h, 0, 0)))
        args.append(small)
    return pl.pallas_call(
        functools.partial(
            place_kernel, plan=tuple(c[1:6] for c in chunks), small=small is not None
        ),
        grid_spec=pltpu.PrefetchScalarGridSpec(
            num_scalar_prefetch=1,
            grid=(2, steps),
            in_specs=in_specs,
            out_specs=pl.BlockSpec(block, out_index),
        ),
        out_shape=jax.ShapeDtypeStruct(out_shape, F32),
        compiler_params=pltpu.CompilerParams(vmem_limit_bytes=VMEM_BYTES),
        name="place_gradient",
    )(ids, *args)


def swap_section(v):
    return lax.ppermute(v, "section", [(0, 1), (1, 0)])


def at(v, k):
    return lax.dynamic_index_in_dim(v, k, 0, False)


def exchange(v):
    return lax.all_to_all(v, "fsdp", 0, 0, tiled=True)


def to_all(v):
    n = lax.axis_size("fsdp")
    return exchange(jnp.broadcast_to(v[None], (n,) + v.shape))


def gather_rows(v):
    return to_all(v).reshape(-1, v.shape[-1])


def scatter_sum(partial):
    n = lax.axis_size("fsdp")
    got = exchange(partial.reshape(n, -1, partial.shape[-1]))
    return jnp.sum(got.astype(F32), axis=0)


def trade_places(v):
    n, s = lax.axis_size("fsdp"), lax.axis_size("seq")
    rows, size = v.shape[0], v.shape[1] // n
    groups = [[j * n + i for i in range(n)] for j in range(s // n)]
    v = v.reshape(rows, n, size).transpose(1, 0, 2)
    v = lax.all_to_all(exchange(v), "seq", 0, 0, axis_index_groups=groups, tiled=True)
    return exchange(v).transpose(1, 0, 2).reshape(rows, n * size)


def sum_everywhere(v):
    n, s = lax.axis_size("fsdp"), lax.axis_size("seq")
    v = v + swap_section(v)
    m = 1
    while m < n:
        v = v + lax.ppermute(v, "fsdp", [(k, k ^ m) for k in range(n)])
        m *= 2
    m = 1
    while m < s:
        v = v + lax.ppermute(v, "seq", [(k, k ^ m) for k in range(s)])
        m *= 2
    return v


class SeqSums:
    def __init__(self):
        s = lax.axis_size("seq")
        half = s // 2
        self.pairs = [[(j, j + 1), (s - 1 - j, s - 2 - j)] for j in range(half - 1)]
        self.pairs.append([(half - 1, half), (half, half - 1)])
        self.inward = half
        self.pairs += [[(j + 1, j), (s - 2 - j, s - 1 - j)] for j in reversed(range(half - 1))]
        self.values, self.phase, self.moving = [], [], []

    def add(self, values):
        first = len(self.values)
        self.values += values
        self.phase += [0] * len(values)
        return list(range(first, len(self.values)))

    def begin(self):
        place = lax.axis_index("seq")
        taken = set()
        for k, step in enumerate(self.phase):
            if step == len(self.pairs) or step in taken:
                continue
            taken.add(step)
            v = self.values[k]
            got = lax.ppermute(v, "seq", self.pairs[step])
            if step < self.inward:
                v = (v.astype(F32) + got.astype(F32)).astype(BF16)
            else:
                here = functools.reduce(
                    jnp.logical_or, [place == to for _, to in self.pairs[step]]
                )
                v = jnp.where(here, got, v)
            self.moving.append((k, v))
            self.phase[k] = step + 1

    def end(self, work):
        moved = [v for _, v in self.moving]
        still = [k for k, p in enumerate(self.phase) if p == 0]
        work, moved, rest = lax.optimization_barrier(
            (work, moved, [self.values[k] for k in still])
        )
        for (k, _), v in zip(self.moving, moved):
            self.values[k] = v
        for k, v in zip(still, rest):
            self.values[k] = v
        self.moving = []
        return work

    def done(self, ks):
        return all(self.phase[k] == len(self.pairs) for k in ks)


def relay(total, local, reverse):
    n, s = lax.axis_size("fsdp"), lax.axis_size("seq")
    segments = s // n
    place = lax.axis_index("seq") // n
    own = lax.axis_index("seq") % n
    totals = lax.all_gather(total, "seq")
    locals_ = lax.all_gather(local, "seq")
    state = jnp.zeros_like(local)
    order = range(segments - 1, -1, -1) if reverse else range(segments)
    for j in order:
        use = (j > place) if reverse else (j < place)
        t = lax.dynamic_index_in_dim(totals, j * n + own, 0, False)
        v = lax.dynamic_index_in_dim(locals_, j * n + own, 0, False)
        state = jnp.where(use, t * state + v, state)
    return state


def next_segment(v, step):
    n, s = lax.axis_size("fsdp"), lax.axis_size("seq")
    pairs = [(k, k + step * n) for k in range(s) if 0 <= k + step * n < s]
    return lax.ppermute(v, "seq", pairs)


def dot_rows(a, b):
    return lax.dot_general(a, b, (((0,), (0,)), ((), ())), preferred_element_type=F32)


def dot_cols(a, b):
    return lax.dot_general(a, b, (((1,), (1,)), ((), ())), preferred_element_type=F32)


def normalised(h, gain):
    return h * lax.rsqrt(jnp.mean(h * h, axis=-1, keepdims=True) + EPS) * gain


def per_device(
    inputs,
    cotangent,
    lengths,
    gain_in,
    w_in,
    conv_w,
    conv_b,
    dt_bias,
    a_log,
    d_skip,
    gain_out,
    w_out,
):
    n = lax.axis_size("fsdp")
    nz = lax.axis_size("seq")
    segments = nz // n
    c = lax.axis_index("section")
    f = lax.axis_index("fsdp")
    place = lax.axis_index("seq")
    upper = c == 0
    rows = inputs.shape[2]
    width = INNER // n
    heads = HEADS // n
    share = D // n
    half = share // 2
    group = GROUP // n
    ids = jnp.stack([f, c]).astype(jnp.int32)
    tie = lax.optimization_barrier

    def pick(a, b):
        return jnp.where(upper, a, b)

    h0 = trade_places(at(inputs, c)[0])

    w = w_in[0].T

    def cut(first, size):
        return lax.dynamic_slice_in_dim(w, first, size, 0)

    def piece_z(m):
        return cut((f ^ m) * width, width)

    def piece_x(m):
        return jnp.concatenate(
            [
                cut(INNER + (f ^ m) * width, width),
                w[2 * INNER : 2 * INNER + GROUP],
                cut(2 * INNER + GROUP + (f ^ m) * heads, heads),
            ]
        )

    def fetch(pieces, layer):
        pairs = lambda m: [(layer * n + i, layer * n + (i ^ m)) for i in range(n)]
        near = [
            v if m == 0 else lax.ppermute(v, ("section", "fsdp"), pairs(m))
            for m, v in enumerate(pieces)
        ]
        return near, [lax.ppermute(v, "section", [(layer, 1 - layer)]) for v in near]

    pieces_x = [piece_x(m) for m in range(n)]
    pieces_z = [piece_z(m) for m in range(n)]
    near_x0, far_x0 = fetch(pieces_x, 0)
    all_h0 = gather_rows(h0)
    pieces_z0, near_x0, all_h0 = tie((pieces_z, near_x0, all_h0))
    near_z0, far_z0 = fetch(pieces_z0, 0)

    pack = jnp.concatenate(
        [
            gain_in[0],
            dt_bias[0],
            a_log[0],
            d_skip[0],
            gain_out[0],
            conv_w[0].reshape(-1),
            conv_b[0],
        ]
    )
    mine = to_all(pack)
    theirs = swap_section(mine)
    small = []
    for full in (pick(mine, theirs), pick(theirs, mine)):
        full = full.astype(F32)
        used = 0

        def take(size):
            nonlocal used
            used += size
            return full[:, used - size : used]

        gain = take(share).reshape(1, D)
        hp = [at(take(heads), f)[None] for _ in range(3)]
        hp = jnp.concatenate([hp[0], -jnp.exp(hp[1]), hp[2], jnp.zeros((5, heads), F32)])
        gout = at(take(width), f)[None]
        per = CHANNELS // n
        taps = take(KERNEL * per).reshape(n, KERNEL, per).transpose(1, 0, 2)
        bias = take(per).reshape(1, CHANNELS)
        table = jnp.concatenate(
            [taps.reshape(KERNEL, CHANNELS), bias, jnp.zeros((3, CHANNELS), F32)]
        )
        cw = jnp.concatenate(
            [lax.dynamic_slice_in_dim(table, f * width, width, 1), table[:, INNER:]], axis=1
        )
        small.append((gain, cw, hp, gout))

    pieces_x1, pieces_z1, own_ct, wo_mine, own_len, near_z0 = tie(
        (pieces_x, pieces_z, at(cotangent, c)[0], w_out[0], at(lengths, c), near_z0)
    )
    wo_other = swap_section(wo_mine)
    wo = (pick(wo_mine, wo_other), pick(wo_other, wo_mine))
    near_x1, far_x1 = fetch(pieces_x1, 1)
    near_z1, far_z1 = fetch(pieces_z1, 1)
    win = ((near_z0, far_z0, near_x0, far_x0), (near_z1, far_z1, near_x1, far_x1))
    slot_pairs = [
        ((j * n + i) * n + k, (j * n + k) * n + i)
        for j in range(segments)
        for i in range(n)
        for k in range(n)
    ]
    length = lax.ppermute(own_len, ("seq", "fsdp"), slot_pairs)
    start = ((place // n) * n + f) * rows
    valid = (start + jnp.arange(rows, dtype=jnp.int32) < length[0]).astype(F32)[:, None]
    dout1 = trade_places(own_ct).astype(F32)

    expand = (
        jnp.arange(heads)[:, None] == jnp.arange(width)[None, :] // HEAD_DIM
    ).astype(BF16)
    zero_state = jnp.zeros((STATE, width), F32)
    zero_edge = jnp.zeros((8, width + GROUP), F32)

    def project_x(normed, layer):
        return project(ids, normed, win[layer][2], win[layer][3], layer)

    def project_z(normed, layer):
        return project(ids, normed, win[layer][0], win[layer][1], layer)

    def decay_of(px, hp):
        decay = jax.nn.softplus(px[:, width + GROUP :] + hp[0:1]) * hp[1:2]
        return jnp.repeat(jnp.exp(jnp.sum(decay, axis=0)), HEAD_DIM)[None, :]

    def scan(px, layer):
        _, cw, hp, _ = small[layer]
        args = (px, cw, hp)
        if segments == 1:
            return run_forward(*args, zero_state, zero_edge, rows), zero_state
        edge = next_segment(px[-8:, : width + GROUP], 1)
        local = run_forward(*args, zero_state, edge, rows)[2][-1]
        state = relay(decay_of(px, hp), local, False)
        return run_forward(*args, state, edge, rows), state

    def unscan(pz, px, fwd, dn, rc, layer):
        (y, filt, states), state = fwd
        _, cw, hp, gout = small[layer]
        args = (pz, px, y, filt, dn, rc, states, state, cw, hp, expand, gout)
        if segments == 1:
            return run_backward(*args, zero_state, zero_edge, rows, n)[:6]
        local = run_backward(*args, zero_state, zero_edge, rows, n)[6]
        grad = relay(decay_of(px, hp), local, True)
        edge = next_segment(run_backward(*args, grad, zero_edge, rows, n)[7], -1)
        return run_backward(*args, grad, edge, rows, n)[:6]

    def gate(pz, y):
        return y * jax.nn.silu(pz)

    def gated(pz, y, r, layer):
        return (gate(pz, y) * r[:, None] * small[layer][3]).astype(BF16)

    def sum_of_shares(v):
        return jnp.sum(to_all(v), axis=0)

    normed_in0 = normalised(all_h0.astype(F32), small[0][0]).astype(BF16)
    px0 = project_x(normed_in0, 0)
    fwd0 = scan(px0, 0)
    pz0 = project_z(normed_in0, 0)
    g0 = gate(pz0, fwd0[0][0])
    stat0 = sum_of_shares(jnp.sum(g0 * g0, axis=1).reshape(n, rows)).reshape(-1)
    r0 = lax.rsqrt(stat0 / INNER + EPS)
    normed0 = gated(pz0, fwd0[0][0], r0, 0)
    mixed0 = scatter_sum(jnp.dot(normed0, wo[0], preferred_element_type=F32).astype(BF16))
    out0 = valid * (h0.astype(F32) + mixed0)
    h1 = out0.astype(BF16)

    normed_in1 = gather_rows(normalised(h1.astype(F32), small[1][0]).astype(BF16))
    px1 = project_x(normed_in1, 1)
    dmixed1 = gather_rows((valid * dout1).astype(BF16))
    dn1 = dot_cols(dmixed1, wo[1])
    fwd1 = scan(px1, 1)
    pz1 = project_z(normed_in1, 1)
    g1 = gate(pz1, fwd1[0][0])
    stat1 = sum_of_shares(
        jnp.stack(
            [
                jnp.sum(g1 * g1, axis=1).reshape(n, rows),
                jnp.sum(g1 * dn1 * small[1][3], axis=1).reshape(n, rows),
            ]
        )
    ).reshape(2, -1)
    r1 = lax.rsqrt(stat1[0] / INNER + EPS)
    normed1 = gated(pz1, fwd1[0][0], r1, 1)

    sums = SeqSums()

    def halves(v):
        v = v.reshape(v.shape[0], n, 2, half)
        return [
            pick(v[:, :, t], v[:, :, 1 - t]).reshape(v.shape[0], n * half) for t in range(2)
        ]

    def half_sums(own, away, parts):
        sizes = [p.shape[1] for p in parts]
        other = swap_section(dot_rows(away, jnp.concatenate(parts, axis=1)).astype(BF16))
        result, first = [], 0
        for p, size in zip(parts, sizes):
            share_of = other[:, first : first + size].astype(F32)
            result.append((dot_rows(own, p) + share_of).astype(BF16))
            first += size
        return result

    def grads_in(kept, parts):
        return [v.reshape(n, half, -1) for v in half_sums(*kept, parts)]

    def grads_out(normed, dmixed):
        part = lambda k: lax.dynamic_slice_in_dim(normed, k * (width // 2), width // 2, 1)
        return half_sums(part(c), part(1 - c), [dmixed[:, : D // 2], dmixed[:, D // 2 :]])

    def with_group(dxs, dbc):
        total = jnp.sum(exchange(dbc), axis=0).astype(BF16)
        column = jnp.arange(GROUP)[None, :] // group
        own = jnp.where(column == f, jnp.concatenate([total] * n, axis=1), 0)
        full = lax.dynamic_update_slice(dxs, own.astype(BF16), (0, width))
        late = jnp.concatenate(
            [dxs[:, width // 2 : width], total, dxs[:, width + GROUP :]], axis=1
        )
        return full, late

    def back_in(dz, full, layer):
        near_z, far_z, near_x, far_x = win[layer]
        return project_back(ids, dz, full, (near_z, near_x), (far_z, far_x), layer)

    def back_norm(dout, dnormed_in, h, gain):
        h = h.astype(F32)
        r = lax.rsqrt(jnp.mean(h * h, axis=-1, keepdims=True) + EPS)
        u = dnormed_in * gain
        mean = jnp.mean(u * h, axis=-1, keepdims=True)
        dgain = jnp.sum(dnormed_in * h * r, axis=0)
        return valid * dout + r * u - h * (r * r * r) * mean, dgain

    def scales(r, coef):
        top = jnp.stack([r.reshape(n, rows), coef.reshape(n, rows)], axis=1)
        return jnp.concatenate([top, jnp.zeros((n, 6, rows), F32)], axis=1)

    rc1 = scales(r1, (r1 * r1 * r1 / INNER) * stat1[1])
    kept0, kept1 = halves(normed_in0), halves(normed_in1)
    go1 = sums.add(grads_out(normed1, dmixed1))
    rc1, normed1, h1 = sums.end((rc1, normed1, h1))

    sums.begin()
    mixed1 = scatter_sum(jnp.dot(normed1, wo[1], preferred_element_type=F32).astype(BF16))
    d1 = unscan(pz1, px1, fwd1, dn1, rc1, 1)
    out1 = valid * (h1.astype(F32) + mixed1)
    d1, out1, mixed1 = sums.end((d1, out1, mixed1))

    sums.begin()
    full1, late1 = with_group(d1[1], d1[2])
    back1 = back_in(d1[0], full1, 1)
    gz = grads_in(kept1, [d1[0][:, : width // 2], d1[0][:, width // 2 :]])
    back1, late1, gz = sums.end((back1, late1, gz))
    gz1 = sums.add(gz)

    sums.begin()
    dnin1 = scatter_sum(back1)
    gx = grads_in(kept1, [d1[1][:, : width // 2], late1])
    dnin1, gx = sums.end((dnin1, gx))
    gx1 = sums.add(gx)

    sums.begin()
    grad1, dgin1 = back_norm(dout1, dnin1, h1, small[1][0])
    dout0 = grad1.astype(BF16).astype(F32)
    dmixed0_own = (valid * dout0).astype(BF16)
    dmixed0 = gather_rows(dmixed0_own)
    along0 = to_all(jnp.sum(dmixed0_own.astype(F32) * mixed0, axis=-1)).reshape(-1)
    rc0 = scales(r0, (r0 * r0 / INNER) * along0)
    grad1, dgin1, dmixed0, rc0 = sums.end((grad1, dgin1, dmixed0, rc0))

    sums.begin()
    dn0 = dot_cols(dmixed0, wo[0])
    d0 = unscan(pz0, px0, fwd0, dn0, rc0, 0)
    d0 = sums.end(d0)

    sums.begin()
    go = grads_out(normed0, dmixed0)
    full0, late0 = with_group(d0[1], d0[2])
    gz = [exchange(v) for v in grads_in(kept0, [d0[0][:, : width // 2], d0[0][:, width // 2 :]])]
    go, full0, late0, gz = sums.end((go, full0, late0, gz))
    go0 = sums.add(go)
    gz0 = sums.add(gz)

    sums.begin()
    dnin0 = scatter_sum(back_in(d0[0], full0, 0))
    gx = grads_in(kept0, [d0[1][:, : width // 2], late0])
    dnin0, gx = sums.end((dnin0, gx))

    sums.begin()
    gx = [exchange(v) for v in gx]
    grad0, dgin0 = back_norm(dout0, dnin0, h0, small[0][0])
    gx, grad0, dgin0 = sums.end((gx, grad0, dgin0))
    gx0 = sums.add(gx)

    sums.begin()
    back = trade_places(
        jnp.concatenate([h1, out1.astype(BF16), grad0.astype(BF16), grad1.astype(BF16)])
    )
    back = sums.end(back)

    sums.begin()
    smalls1 = (d1[3][0], d1[4][:5], d1[5][:3])
    smalls0 = (d0[3][0], d0[4][:5], d0[5][:3])

    def packed(dgin, smalls, out, mixed):
        dgain, dconv, dhp = smalls
        put = lambda v, size, at_lane: lax.dynamic_update_slice(
            jnp.zeros(v.shape[:-1] + (size,), F32), v, (0,) * (v.ndim - 1) + (at_lane,)
        )
        conv = put(dconv[:, :width], CHANNELS, f * width)
        conv = conv.at[:, INNER:].set(dconv[:, width:])
        totals = jnp.stack(
            [jnp.sum(out * out), jnp.sum((valid * mixed) ** 2), jnp.sum(valid)]
        )
        return jnp.concatenate(
            [
                dgin,
                conv.reshape(-1),
                put(dhp, HEADS, f * heads).reshape(-1),
                put(dgain, INNER, f * width),
                totals,
            ]
        )

    p = sum_everywhere(
        jnp.stack([packed(dgin0, smalls0, out0, mixed0), packed(dgin1, smalls1, out1, mixed1)])
    )
    p = sums.end(pick(p[0], p[1]))

    def hand_over(v, layer):
        return lax.ppermute(v, "section", [(1 - layer, layer)])

    names = {"own": {}, "away": {}}
    order = [(k, 1, "in") for k in gz1 + gx1] + [(k, 1, "out") for k in go1]
    order += [(k, 0, "in") for k in gz0 + gx0] + [(k, 0, "out") for k in go0]
    while order:
        sums.begin()
        ready = [e for e in order if e[0] not in [k for k, _ in sums.moving]]
        ready = [e for e in ready if sums.done([e[0]])][:3]
        fresh = []
        for k, layer, kind in ready:
            v = sums.values[k]
            v = exchange(v) if (layer, kind) == (1, "in") else v
            fresh.append((v, hand_over(v, layer)))
        fresh, p = sums.end((fresh, p))
        for (k, layer, kind), (v, other) in zip(ready, fresh):
            names["own"][k], names["away"][k] = v, other
        order = [e for e in order if e not in ready]

    used = 0

    def part(size):
        nonlocal used
        used += size
        return p[used - size : used]

    mine_of = lambda v, size: lax.dynamic_slice_in_dim(v, f * size, size, v.ndim - 1)
    o_gain_in = mine_of(part(D), share)
    o_conv = mine_of(part(5 * CHANNELS).reshape(5, CHANNELS), CHANNELS // n)
    o_heads = mine_of(part(3 * HEADS).reshape(3, HEADS), heads)
    o_gain_out = mine_of(part(INNER), width)
    totals = part(3)
    act_rms = jnp.sqrt(totals[:2] / (totals[2] * D))[None]

    sides = ("own", "away")
    part_width = width // 2
    by_layer = (gz0 + gx0, gz1 + gx1)

    def small_rows(v):
        v = v[:, :, part_width:].astype(F32).transpose(0, 2, 1)
        return jnp.concatenate(
            [v[:, :group].reshape(GROUP, half), v[:, group:].reshape(HEADS, half)]
        )

    small_in = jnp.stack(
        [
            small_rows(pick(names[side][by_layer[0][3]], names[side][by_layer[1][3]]))
            for side in sides
        ]
    )
    turned = lambda h, ids: jnp.where(h == 0, ids[1], 1 - ids[1])
    chunks_in = [
        (
            names[side][by_layer[layer][k]],
            s,
            layer,
            n * k,
            n,
            True,
            (1, half, part_width),
            lambda i: (i, 0, 0),
        )
        for s, side in enumerate(sides)
        for layer in range(2)
        for k in range(4)
    ]
    g_w_in = place_blocks(
        ids,
        chunks_in,
        small_in,
        (2 * INNER + GROUP + HEADS, share),
        (part_width, half),
        lambda h, j, ids: (
            jnp.where(
                j < 4 * n, j // (2 * n) * 2 * n + (j % n) * 2 + j // n % 2, 4 * n
            ),
            turned(h, ids),
        ),
        4 * n + 1,
    )
    chunks_out = [
        (
            names[side][(go0, go1)[layer][k]],
            s,
            layer,
            k,
            1,
            False,
            (width // 2, D // 2),
            lambda i: (0, 0),
        )
        for s, side in enumerate(sides)
        for layer in range(2)
        for k in range(2)
    ]
    g_w_out = place_blocks(
        ids,
        chunks_out,
        None,
        (width, D),
        (width // 2, D // 2),
        lambda h, j, ids: (turned(h, ids), j),
        2,
    )

    back = back.reshape(2, 2, rows, D)
    kept_back = pick(back[:, 0], back[:, 1])
    other_back = swap_section(pick(back[:, 1], back[:, 0]))
    both_back = jnp.stack(
        [pick(kept_back, other_back), pick(other_back, kept_back)], axis=1
    )
    return (
        both_back[0][None, :, None],
        both_back[1].astype(F32)[None, :, None],
        o_gain_in[None],
        g_w_in.T[None],
        o_conv[None, :4],
        o_conv[None, 4],
        o_heads[None, 0],
        o_heads[None, 1],
        o_heads[None, 2],
        o_gain_out[None],
        g_w_out[None],
        act_rms,
    )


def solution(mesh):
    in_specs = (
        P(None, "fsdp", "seq", None),
        P(None, "fsdp", "seq", None),
        P(None, "fsdp"),
        P("section", "fsdp"),
        P("section", "fsdp", None),
        P("section", None, "fsdp"),
        P("section", "fsdp"),
        P("section", "fsdp"),
        P("section", "fsdp"),
        P("section", "fsdp"),
        P("section", "fsdp"),
        P("section", "fsdp", None),
    )
    out_specs = (
        P("section", None, "fsdp", "seq", None),
        P("section", None, "fsdp", "seq", None),
        P("section", "fsdp"),
        P("section", "fsdp", None),
        P("section", None, "fsdp"),
        P("section", "fsdp"),
        P("section", "fsdp"),
        P("section", "fsdp"),
        P("section", "fsdp"),
        P("section", "fsdp"),
        P("section", "fsdp", None),
        P("section", None),
    )
    return jax.shard_map(
        per_device, mesh=mesh, in_specs=in_specs, out_specs=out_specs, check_vma=False
    )
```

time: 1360 us -> 1310 us (0.963)
  waiting for transfers between devices: 555 us -> 302 us
  local copies, waits for them, and re-layouts: 85.2 us -> 169 us
  starting transfers between devices: 302 us -> 385 us
  Pallas kernels: 90.2 us -> 146 us
  matrix products: 112 us -> 83.6 us
  other arithmetic: 207 us -> 182 us
  blocking collectives: 0 us -> 23.4 us
    ppermute x100 -> x30, waiting for transfers between devices: 339 us -> 55.2 us  [the longest x12 45.6 us: fetch(): lax.ppermute(v, ('section', 'fsdp'), pairs(m))]
    all_to_all x0 -> x28, waiting for transfers between devices: none -> 148 us  [the longest x25 101 us: exchange(): return lax.all_to_all(v, 'fsdp', 0, 0, tiled=True)]
    ppermute x42 -> x36, waiting for transfers between devices: 197 us -> 74 us  [begin(): got = lax.ppermute(v, 'seq', self.pairs[step])]
    all_to_all x0 -> x28, starting transfers between devices: none -> 118 us  [the longest x25 105 us: exchange(): return lax.all_to_all(v, 'fsdp', 0, 0, tiled=True)]
    concatenate x14 -> x6, other arithmetic: 105 us -> 8.42 us  [the longest x1 3.62 us: piece_x(): jnp.concatenate([cut(INNER + (f ^ m) * width, width), w[2 * INNER:2 * INN...]
    pallas_call x6 -> x12, Pallas kernels: 90.2 us -> 146 us  [the longest x2 40.6 us: run_backward(): pl.pallas_call(backward_kernel, grid=(count,), in_specs=[block(width), bl...]
    ppermute x100 -> x30, starting transfers between devices: 103 us -> 57.5 us  [the longest x16 27.6 us: fetch(): lax.ppermute(v, 'section', [(layer, 1 - layer)])]
    ppermute x42 -> x36, starting transfers between devices: 71.1 us -> 112 us  [begin(): got = lax.ppermute(v, 'seq', self.pairs[step])]
  transfers between devices with their start and end apart: 176 -> 119, of which waited for: 66 -> 35; matrix products, arithmetic and copies ran while one was open for 23% -> 24% of each run, Pallas kernels for 4% -> 9%
where the time goes in v4:
time: 1310 us; the launch traced here: 1290 us
  starting transfers between devices  385 us (29%)
  waiting for transfers between devices  302 us (23%)
  other arithmetic  182 us (14%)
  local copies, waits for them, and re-layouts  169 us (13%)
  Pallas kernels  146 us (11%)
  matrix products  83.6 us (6%)
  blocking collectives  23.4 us (2%)
    ppermute x36, starting transfers between devices, begin(): got = lax.ppermute(v, 'seq', self.pairs[step])  112 us
    all_to_all x25, starting transfers between devices, exchange(): return lax.all_to_all(v, 'fsdp', 0, 0, tiled=True)  105 us
    all_to_all x25, waiting for transfers between devices, exchange(): return lax.all_to_all(v, 'fsdp', 0, 0, tiled=True)  101 us
    ppermute x36, waiting for transfers between devices, begin(): got = lax.ppermute(v, 'seq', self.pairs[step])  74 us
    convert_element_type x24, other arithmetic, begin(): v = (v.astype(F32) + got.astype(F32)).astype(BF16)  62.9 us
    dot_general x18, matrix products, dot_rows(): lax.dot_general(a, b, (((0,), (0,)), ((), ())), preferred_element_type=F32)  58.5 us
    ppermute x10, starting transfers between devices, swap_section(): return lax.ppermute(v, 'section', [(0, 1), (1, 0)])  49.1 us
    all_to_all x3, waiting for transfers between devices, trade_places(): lax.all_to_all(exchange(v), 'seq', 0, 0, axis_index_groups=groups, tiled=...  47.4 us
  transfers between devices with their start and end apart: 119, of which 35 were waited for; matrix products, arithmetic and copies ran while one was open for 24% of the time, Pallas kernels for 9%

profile of v4, /device:TPU:1, one launch (start us, length us, event | category | flops | bytes accessed | tf_op | source)
XLA Modules:
  0.0 1293.9 jit_solution(16775221929318802400)
XLA Ops:
  16.0 9.1 all_to_all.160
  25.1 4.6 all-to-all-start.1
  31.5 6.5 dynamic-slice_bitcast_fusion.4
  55.2 9.9 collective-permute-start.7
  77.5 32.7 %all-to-all-done.3 = bf16[4,128,2048]{2,1,0:T(8,128)(2,1)} async-done(((bf16[4,128,2048]{2,1,0:T(8,128)(2,1)}), bf16[4,128,2048]{2,1,0:T(8,128)(2,1)}, u32[]{:S(2)}, u32[]{:S(2)}) %all-to-all-start.3) | async-done | bytes 2097184 | tf_op jit(solution)/shard_map/all_to_all | solution.py:525
  115.4 27.8 %collective-permute-start.16 = (bf16[1024,2048]{1,0:T(8,128)(2,1)}, bf16[1024,2048]{1,0:T(8,128)(2,1)}, u32[]{:S(2)}, u32[]{:S(2)}) collective-permute-start(bf16[1024,2048]{1,0:T(8,128)(2,1)} %bitcast.296), channel_id=1, source_target_pairs={{0,16},{16,0},{1,17},{17,1},{2,18},{18,2},{3,19},{19,3},{4,20},{20... | collective-permute-start | bytes 12582920 | tf_op jit(solution)/shard_map/ppermute | solution.py:517
  165.6 8.9 project.4.proj
  174.5 10.7 scan_forward.2
  194.1 7.4 project.5.pz
  205.0 7.2 all_to_all.161
  219.3 11.1 all-to-all-done.9
  234.6 6.2 convolution_convert_fusion.3
  290.1 4.8 collective-permute-start.20
  294.9 4.7 collective-permute-done.17.refs_1_.refs_5_
  302.0 7.7 collective-permute-done.18.refs_2_.refs_6_
  314.0 26.2 %collective-permute-done.19.refs_3_.refs_7_ = bf16[1296,512]{1,0:T(8,128)(2,1)} collective-permute-done((bf16[1296,512]{1,0:T(8,128)(2,1)}, bf16[1296,512]{1,0:T(8,128)(2,1)}, u32[]{:S(2)}, u32[]{:S(2)}) %collective-permute-start.19) | collective-permute-done | bytes 1327136 | tf_op jit(solution)/shard_map/ppermute | solution.py:708
  349.7 6.9 collective-permute-done.26.refs_3_
  362.2 7.7 project.6.proj
  369.9 10.6 scan_forward.3
  385.4 6.7 project.7.pz
  393.1 8.7 multiply_reduce_fusion.1
  415.4 4.5 reshape_reshape.3
  437.4 7.9 broadcast_select_fusion.3
  445.2 5.8 copy.269
  451.0 20.3 %scan_backward.2 = (bf16[512,1024]{1,0:T(8,128)(2,1)S(1)}, bf16[512,1296]{1,0:T(8,128)(2,1)S(1)}, f32[4,512,64]{2,1,0:T(8,128)S(1)}, f32[8,1024]{1,0:T(8,128)S(1...) custom-call(f32[512,1024]{1,0:T(8,128)} %project.7.pz, ...), custom_call_target="tpu_custom_call" | custom-call | tf_op jit(solution)/shard_map/scan_backward/pallas_call | solution.py:303
  492.6 5.8 copy.268
  508.7 10.3 project_back.2
  540.1 5.8 collective-permute-start.39
  554.6 12.9 collective-permute-done.39
  570.2 6.5 collective-permute-done.37
  604.0 7.2 all_to_all.162
  621.7 6.7 collective-permute-start.42
  633.4 14.1 %collective-permute-done.42 = bf16[4,256,512]{2,1,0:T(8,128)(2,1)S(1)} collective-permute-done((bf16[4,256,512]{2,1,0:T(8,128)(2,1)}, bf16[4,256,512]{2,1,0:T(8,128)(2,1)S(1)}, u32[]{:S(2)}, u32[]{:S(2)}) %collective-permute-start.42) | collective-permute-done | bytes 1048608 | tf_op jit(solution)/shard_map/ppermute | solution.py:590
  650.1 7.7 broadcast_select_fusion.1
  657.8 5.8 copy.275
  664.4 6.7 collective-permute-start.45
  671.0 6.5 fusion.3.dn
  677.5 20.3 %scan_backward.3 = (bf16[512,1024]{1,0:T(8,128)(2,1)S(1)}, bf16[512,1296]{1,0:T(8,128)(2,1)S(1)}, f32[4,512,64]{2,1,0:T(8,128)S(1)}, f32[8,1024]{1,0:T(8,128)S(1...) custom-call(f32[512,1024]{1,0:T(8,128)} %project.5.pz, ...), custom_call_target="tpu_custom_call" | custom-call | tf_op jit(solution)/shard_map/scan_backward/pallas_call | solution.py:303
  708.6 5.2 collective-permute-start.47
  723.9 5.8 copy.274
  736.2 7.4 collective-permute-start.50
  751.1 4.7 all-to-all-start.19
  793.5 6.0 collective-permute-start.54
  799.4 10.6 project_back.3
  829.9 9.4 all-to-all-done.21
  855.6 4.5 all-to-all-start.22
  863.0 16.6 %collective-permute-start.57 = (bf16[512,1024]{1,0:T(8,128)(2,1)}, bf16[512,1024]{1,0:T(8,128)(2,1)}, u32[]{:S(2)}, u32[]{:S(2)}) collective-permute-start(bf16[512,1024]{1,0:T(8,128)(2,1)} %add_convert_fusion.20), channel_id=1, source_target_pairs={{0,4},{12,8},{1,5},{13,9},{2,6},{14,10},{3,7},{15,11},{16,20},{28,... | collective-permute-start | bytes 3145736 | tf_op jit(solution)/shard_map/ppermute | solution.py:590
  892.2 8.1 collective-permute-done.57
  925.8 18.9 %all-to-all-done.24 = bf16[4,512,512]{2,1,0:T(8,128)(2,1)} async-done(((bf16[4,512,512]{2,1,0:T(8,128)(2,1)}), bf16[4,512,512]{2,1,0:T(8,128)(2,1)}, u32[]{:S(2)}, u32[]{:S(2)}) %all-to-all-start.24) | async-done | bytes 2097184 | tf_op jit(solution)/shard_map/all_to_all | solution.py:525
  954.5 8.8 collective-permute-start.60
  963.3 33.6 %all-to-all-done.25 = bf16[4,512,512]{2,1,0:T(8,128)(2,1)} async-done(((bf16[4,512,512]{2,1,0:T(8,128)(2,1)}), bf16[4,512,512]{2,1,0:T(8,128)(2,1)}, u32[]{:S(2)}, u32[]{:S(2)}) %all-to-all-start.25) | async-done | bytes 2097184 | tf_op jit(solution)/shard_map/all_to_all | solution.py:548
  1013.1 11.7 all-to-all-done.26
  1042.8 11.3 collective-permute-done.68
  1055.3 13.5 %collective-permute-done.69 = f32[2,28099]{1,0:T(2,128)S(1)} collective-permute-done((f32[2,28099]{1,0:T(2,128)S(1)}, f32[2,28099]{1,0:T(2,128)S(1)}, u32[]{:S(2)}, u32[]{:S(2)}) %collective-permute-start.69) | collective-permute-done | bytes 224824 | tf_op jit(solution)/shard_map/ppermute | solution.py:561
  1079.4 7.9 all-to-all-done.28.refs_5_
  1093.3 5.4 collective-permute-start.75
  1122.7 7.2 collective-permute-start.82
  1132.5 10.7 collective-permute-done.80
  1162.7 9.0 collective-permute-start.84
  1189.6 10.0 collective-permute-start.88
  1204.4 12.7 collective-permute-done.89
  1224.5 10.9 collective-permute-start.90
  1245.3 6.4 place_gradient.3
  1267.7 26.0 %place_gradient.2 = f32[8512,512]{1,0:T(8,128)} custom-call(s32[2]{0:T(128)S(1)} %pad_add_fusion.ids, bf16[4,256,512]{2,1,0:T(8,128)(2,1)S(1)} %copy-done.13, bf16[4,256,512]{2,1,0:T(8,128)(2,1)S(1)} %copy-done.15, bf16[4,256,512]{2,1,0:T(8,128)(2,1)S(1)} %copy-done.16, bf16[4,256,592]{2,1,0:T(8,128)(2,1)} %broadcast_select_fusion.10.refs_3_, ...), custom_call_target="tpu_custom_call" | custom-call | tf_op jit(solution)/shard_map/place_gradient/pallas_call | solution.py:500
  (624 shorter events, 627.5 us)
Async XLA Ops:
  40.6 27.3 %all-to-all-start.2 = ((bf16[4,128,512]{2,1,0:T(8,128)(2,1)}), bf16[4,128,512]{2,1,0:T(8,128)(2,1)S(1)}, u32[]{:S(2)}, u32[]{:S(2)}) async-start(bf16[4,128,512]{2,1,0:T(8,128)(2,1)} %all-to-all-done.1), calls=%async_computation.2 | async-start | bytes 1048576 | tf_op jit(solution)/shard_map/all_to_all | solution.py:525
  47.8 29.7 %collective-permute-start = (bf16[1296,512]{1,0:T(8,128)(2,1)}, bf16[1296,512]{1,0:T(8,128)(2,1)}, u32[]{:S(2)}, u32[]{:S(2)}) collective-permute-start(bf16[1296,512]{1,0:T(8,128)(2,1)} %get-tuple-element.221), channel_id=1, source_target_pairs={{0,1},{1,0},{2,3},{3,2},{4,5},{5,4},{6,7},{7,6},{8,9},{9,8},{10,11... | collective-permute-start | bytes 3981320 | tf_op jit(solution)/shard_map/ppermute | solution.py:708
  49.5 28.0 %collective-permute-start.1 = (bf16[1296,512]{1,0:T(8,128)(2,1)}, bf16[1296,512]{1,0:T(8,128)(2,1)}, u32[]{:S(2)}, u32[]{:S(2)}) collective-permute-start(bf16[1296,512]{1,0:T(8,128)(2,1)} %get-tuple-element.222), channel_id=1, source_target_pairs={{0,2},{1,3},{2,0},{3,1},{4,6},{5,7},{6,4},{7,5},{8,10},{9,11},{10,... | collective-permute-start | bytes 3981320 | tf_op jit(solution)/shard_map/ppermute | solution.py:708
  52.9 94.4 %collective-permute-start.8 = (bf16[1296,512]{1,0:T(8,128)(2,1)S(1)}, bf16[1296,512]{1,0:T(8,128)(2,1)}, u32[]{:S(2)}, u32[]{:S(2)}) collective-permute-start(bf16[1296,512]{1,0:T(8,128)(2,1)S(1)} %get-tuple-element.220.refs_0_.refs_4_), channel_id=1, source_target_pairs={{0,16},{1,17},{2,18},{3,19},{4,20},{5,21},{6,22},{7,23},{8,24},{9,... | collective-permute-start | bytes 3981320 | tf_op jit(solution)/shard_map/ppermute | solution.py:711
  71.8 38.4 %all-to-all-start.3 = ((bf16[4,128,2048]{2,1,0:T(8,128)(2,1)}), bf16[4,128,2048]{2,1,0:T(8,128)(2,1)}, u32[]{:S(2)}, u32[]{:S(2)}) async-start(bf16[4,128,2048]{2,1,0:T(8,128)(2,1)} %broadcast_in_dim.53), calls=%async_computation.3 | async-start | bytes 4194304 | tf_op jit(solution)/shard_map/all_to_all | solution.py:525
  115.4 119.2 %collective-permute-start.16 = (bf16[1024,2048]{1,0:T(8,128)(2,1)}, bf16[1024,2048]{1,0:T(8,128)(2,1)}, u32[]{:S(2)}, u32[]{:S(2)}) collective-permute-start(bf16[1024,2048]{1,0:T(8,128)(2,1)} %bitcast.296), channel_id=1, source_target_pairs={{0,16},{16,0},{1,17},{17,1},{2,18},{18,2},{3,19},{19,3},{4,20},{20... | collective-permute-start | bytes 12582920 | tf_op jit(solution)/shard_map/ppermute | solution.py:517
  147.3 46.8 %collective-permute-start.12 = (bf16[1024,512]{1,0:T(8,128)(2,1)S(1)}, bf16[1024,512]{1,0:T(8,128)(2,1)}, u32[]{:S(2)}, u32[]{:S(2)}) collective-permute-start(bf16[1024,512]{1,0:T(8,128)(2,1)S(1)} %get-tuple-element.225.refs_0_), channel_id=1, source_target_pairs={{0,16},{1,17},{2,18},{3,19},{4,20},{5,21},{6,22},{7,23},{8,24},{9,... | collective-permute-start | bytes 3145736 | tf_op jit(solution)/shard_map/ppermute | solution.py:711
  151.9 42.2 %collective-permute-start.13 = (bf16[1024,512]{1,0:T(8,128)(2,1)}, bf16[1024,512]{1,0:T(8,128)(2,1)}, u32[]{:S(2)}, u32[]{:S(2)}) collective-permute-start(bf16[1024,512]{1,0:T(8,128)(2,1)} %collective-permute-done.3.refs_1_), channel_id=1, source_target_pairs={{0,16},{1,17},{2,18},{3,19},{4,20},{5,21},{6,22},{7,23},{8,24},{9,... | collective-permute-start | bytes 3145736 | tf_op jit(solution)/shard_map/ppermute | solution.py:711
  155.3 38.8 %collective-permute-start.14 = (bf16[1024,512]{1,0:T(8,128)(2,1)}, bf16[1024,512]{1,0:T(8,128)(2,1)}, u32[]{:S(2)}, u32[]{:S(2)}) collective-permute-start(bf16[1024,512]{1,0:T(8,128)(2,1)} %collective-permute-done.4.refs_2_), channel_id=1, source_target_pairs={{0,16},{1,17},{2,18},{3,19},{4,20},{5,21},{6,22},{7,23},{8,24},{9,... | collective-permute-start | bytes 3145736 | tf_op jit(solution)/shard_map/ppermute | solution.py:711
  158.7 35.4 %collective-permute-start.15 = (bf16[1024,512]{1,0:T(8,128)(2,1)}, bf16[1024,512]{1,0:T(8,128)(2,1)}, u32[]{:S(2)}, u32[]{:S(2)}) collective-permute-start(bf16[1024,512]{1,0:T(8,128)(2,1)} %collective-permute-done.5.refs_3_), channel_id=1, source_target_pairs={{0,16},{1,17},{2,18},{3,19},{4,20},{5,21},{6,22},{7,23},{8,24},{9,... | collective-permute-start | bytes 3145736 | tf_op jit(solution)/shard_map/ppermute | solution.py:711
  241.2 28.8 %all-to-all-start.6 = ((bf16[4,128,2048]{2,1,0:T(8,128)(2,1)}), bf16[4,128,2048]{2,1,0:T(8,128)(2,1)}, u32[]{:S(2)}, u32[]{:S(2)}) async-start(bf16[4,128,2048]{2,1,0:T(8,128)(2,1)} %bitcast.247), calls=%async_computation.6 | async-start | bytes 4194304 | tf_op jit(solution)/shard_map/all_to_all | solution.py:525
  247.6 42.5 %collective-permute-start.24 = (bf16[1024,512]{1,0:T(8,128)(2,1)}, bf16[1024,512]{1,0:T(8,128)(2,1)}, u32[]{:S(2)}, u32[]{:S(2)}) collective-permute-start(bf16[1024,512]{1,0:T(8,128)(2,1)} %get-tuple-element.226), channel_id=1, source_target_pairs={{16,17},{17,16},{18,19},{19,18},{20,21},{21,20},{22,23},{23,22},{2... | collective-permute-start | bytes 3145736 | tf_op jit(solution)/shard_map/ppermute | solution.py:708
  251.0 61.1 %collective-permute-start.25 = (bf16[1024,512]{1,0:T(8,128)(2,1)}, bf16[1024,512]{1,0:T(8,128)(2,1)}, u32[]{:S(2)}, u32[]{:S(2)}) collective-permute-start(bf16[1024,512]{1,0:T(8,128)(2,1)} %get-tuple-element.227), channel_id=1, source_target_pairs={{16,18},{17,19},{18,16},{19,17},{20,22},{21,23},{22,20},{23,21},{2... | collective-permute-start | bytes 3145736 | tf_op jit(solution)/shard_map/ppermute | solution.py:708
  254.1 45.6 %collective-permute-start.17 = (bf16[1296,512]{1,0:T(8,128)(2,1)}, bf16[1296,512]{1,0:T(8,128)(2,1)}, u32[]{:S(2)}, u32[]{:S(2)}) collective-permute-start(bf16[1296,512]{1,0:T(8,128)(2,1)} %get-tuple-element.221), channel_id=1, source_target_pairs={{16,17},{17,16},{18,19},{19,18},{20,21},{21,20},{22,23},{23,22},{2... | collective-permute-start | bytes 3981320 | tf_op jit(solution)/shard_map/ppermute | solution.py:708
  256.3 53.4 %collective-permute-start.18 = (bf16[1296,512]{1,0:T(8,128)(2,1)}, bf16[1296,512]{1,0:T(8,128)(2,1)}, u32[]{:S(2)}, u32[]{:S(2)}) collective-permute-start(bf16[1296,512]{1,0:T(8,128)(2,1)} %get-tuple-element.222), channel_id=1, source_target_pairs={{16,18},{17,19},{18,16},{19,17},{20,22},{21,23},{22,20},{23,21},{2... | collective-permute-start | bytes 3981320 | tf_op jit(solution)/shard_map/ppermute | solution.py:708
  281.4 61.2 %all-to-all-start.7 = ((bf16[4,128,2048]{2,1,0:T(8,128)(2,1)}), bf16[4,128,2048]{2,1,0:T(8,128)(2,1)}, u32[]{:S(2)}, u32[]{:S(2)}) async-start(bf16[4,128,2048]{2,1,0:T(8,128)(2,1)} %broadcast_in_dim.59), calls=%async_computation.7 | async-start | bytes 4194304 | tf_op jit(solution)/shard_map/all_to_all | solution.py:525
  285.8 54.4 %collective-permute-start.19 = (bf16[1296,512]{1,0:T(8,128)(2,1)}, bf16[1296,512]{1,0:T(8,128)(2,1)}, u32[]{:S(2)}, u32[]{:S(2)}) collective-permute-start(bf16[1296,512]{1,0:T(8,128)(2,1)} %get-tuple-element.223), channel_id=1, source_target_pairs={{16,19},{17,18},{18,17},{19,16},{20,23},{21,22},{22,21},{23,20},{2... | collective-permute-start | bytes 3981320 | tf_op jit(solution)/shard_map/ppermute | solution.py:708
  290.1 67.8 %collective-permute-start.20 = (bf16[1296,512]{1,0:T(8,128)(2,1)S(1)}, bf16[1296,512]{1,0:T(8,128)(2,1)}, u32[]{:S(2)}, u32[]{:S(2)}) collective-permute-start(bf16[1296,512]{1,0:T(8,128)(2,1)S(1)} %get-tuple-element.220.refs_0_.refs_4_), channel_id=1, source_target_pairs={{16,0},{17,1},{18,2},{19,3},{20,4},{21,5},{22,6},{23,7},{24,8},{25... | collective-permute-start | bytes 3981320 | tf_op jit(solution)/shard_map/ppermute | solution.py:711
  299.6 59.7 %collective-permute-start.21 = (bf16[1296,512]{1,0:T(8,128)(2,1)}, bf16[1296,512]{1,0:T(8,128)(2,1)}, u32[]{:S(2)}, u32[]{:S(2)}) collective-permute-start(bf16[1296,512]{1,0:T(8,128)(2,1)} %collective-permute-done.17.refs_1_.refs_5_), channel_id=1, source_target_pairs={{16,0},{17,1},{18,2},{19,3},{20,4},{21,5},{22,6},{23,7},{24,8},{25... | collective-permute-start | bytes 3981320 | tf_op jit(solution)/shard_map/ppermute | solution.py:711
  309.7 51.0 %collective-permute-start.22 = (bf16[1296,512]{1,0:T(8,128)(2,1)}, bf16[1296,512]{1,0:T(8,128)(2,1)}, u32[]{:S(2)}, u32[]{:S(2)}) collective-permute-start(bf16[1296,512]{1,0:T(8,128)(2,1)} %collective-permute-done.18.refs_2_.refs_6_), channel_id=1, source_target_pairs={{16,0},{17,1},{18,2},{19,3},{20,4},{21,5},{22,6},{23,7},{24,8},{25... | collective-permute-start | bytes 3981320 | tf_op jit(solution)/shard_map/ppermute | solution.py:711
  312.1 44.5 %collective-permute-start.26 = (bf16[1024,512]{1,0:T(8,128)(2,1)}, bf16[1024,512]{1,0:T(8,128)(2,1)}, u32[]{:S(2)}, u32[]{:S(2)}) collective-permute-start(bf16[1024,512]{1,0:T(8,128)(2,1)} %get-tuple-element.228), channel_id=1, source_target_pairs={{16,19},{17,18},{18,17},{19,16},{20,23},{21,22},{22,21},{23,20},{2... | collective-permute-start | bytes 3145736 | tf_op jit(solution)/shard_map/ppermute | solution.py:708
  345.2 47.9 %all-to-all-start.11 = ((bf16[4,128,2048]{2,1,0:T(8,128)(2,1)}), bf16[4,128,2048]{2,1,0:T(8,128)(2,1)}, u32[]{:S(2)}, u32[]{:S(2)}) async-start(bf16[4,128,2048]{2,1,0:T(8,128)(2,1)} %broadcast_in_dim.60), calls=%async_computation.11 | async-start | bytes 4194304 | tf_op jit(solution)/shard_map/all_to_all | solution.py:525
  430.5 45.9 %all-to-all-start.13 = ((bf16[4,128,2048]{2,1,0:T(8,128)(2,1)}), bf16[4,128,2048]{2,1,0:T(8,128)(2,1)}, u32[]{:S(2)}, u32[]{:S(2)}) async-start(bf16[4,128,2048]{2,1,0:T(8,128)(2,1)} %bitcast.248), calls=%async_computation.13 | async-start | bytes 4194304 | tf_op jit(solution)/shard_map/all_to_all | solution.py:525
  434.9 38.5 %collective-permute-start.32 = (bf16[512,1024]{1,0:T(8,128)(2,1)}, bf16[512,1024]{1,0:T(8,128)(2,1)}, u32[]{:S(2)}, u32[]{:S(2)}) collective-permute-start(bf16[512,1024]{1,0:T(8,128)(2,1)} %add_convert_fusion.35), channel_id=1, source_target_pairs={{0,4},{12,8},{1,5},{13,9},{2,6},{14,10},{3,7},{15,11},{16,20},{28,... | collective-permute-start | bytes 3145736 | tf_op jit(solution)/shard_map/ppermute | solution.py:590
  483.4 45.7 %collective-permute-start.33 = (bf16[1024,1024]{1,0:T(8,128)(2,1)}, bf16[1024,1024]{1,0:T(8,128)(2,1)}, u32[]{:S(2)}, u32[]{:S(2)}) collective-permute-start(bf16[1024,1024]{1,0:T(8,128)(2,1)} %convolution_convert_fusion.7), channel_id=1, source_target_pairs={{0,16},{16,0},{1,17},{17,1},{2,18},{18,2},{3,19},{19,3},{4,20},{20... | collective-permute-start | bytes 6291464 | tf_op jit(solution)/shard_map/ppermute | solution.py:517
  537.9 44.2 %collective-permute-start.36 = (bf16[1024,1104]{0,1:T(8,128)(2,1)}, bf16[1024,1104]{0,1:T(8,128)(2,1)}, u32[]{:S(2)}, u32[]{:S(2)}) collective-permute-start(bf16[1024,1104]{0,1:T(8,128)(2,1)} %convolution_convert_fusion.1), channel_id=1, source_target_pairs={{0,16},{16,0},{1,17},{17,1},{2,18},{18,2},{3,19},{19,3},{4,20},{20... | collective-permute-start | bytes 6782984 | tf_op jit(solution)/shard_map/ppermute | solution.py:517
  540.1 27.4 %collective-permute-start.39 = (bf16[4,256,512]{2,1,0:T(8,128)(2,1)}, bf16[4,256,512]{2,1,0:T(8,128)(2,1)}, u32[]{:S(2)}, u32[]{:S(2)}) collective-permute-start(bf16[4,256,512]{2,1,0:T(8,128)(2,1)} %bitcast.67), channel_id=1, source_target_pairs={{0,4},{12,8},{1,5},{13,9},{2,6},{14,10},{3,7},{15,11},{16,20},{28,... | collective-permute-start | bytes 3145736 | tf_op jit(solution)/shard_map/ppermute | solution.py:590
  545.9 33.1 %all-to-all-start.15 = ((bf16[4,128,2048]{2,1,0:T(8,128)(2,1)}), bf16[4,128,2048]{2,1,0:T(8,128)(2,1)}, u32[]{:S(2)}, u32[]{:S(2)}) async-start(bf16[4,128,2048]{2,1,0:T(8,128)(2,1)} %bitcast.239), calls=%async_computation.15 | async-start | bytes 4194304 | tf_op jit(solution)/shard_map/all_to_all | solution.py:525
  595.6 32.9 %collective-permute-start.40 = (bf16[512,1024]{1,0:T(8,128)(2,1)}, bf16[512,1024]{1,0:T(8,128)(2,1)}, u32[]{:S(2)}, u32[]{:S(2)}) collective-permute-start(bf16[512,1024]{1,0:T(8,128)(2,1)} %add_convert_fusion.27), channel_id=1, source_target_pairs={{4,0},{8,12},{5,1},{9,13},{6,2},{10,14},{7,3},{11,15},{20,16},{24,... | collective-permute-start | bytes 3145736 | tf_op jit(solution)/shard_map/ppermute | solution.py:590
  598.7 32.2 %collective-permute-start.41 = (bf16[4,256,512]{2,1,0:T(8,128)(2,1)}, bf16[4,256,512]{2,1,0:T(8,128)(2,1)}, u32[]{:S(2)}, u32[]{:S(2)}) collective-permute-start(bf16[4,256,512]{2,1,0:T(8,128)(2,1)} %add_convert_fusion.26), channel_id=1, source_target_pairs={{4,8},{8,4},{5,9},{9,5},{6,10},{10,6},{7,11},{11,7},{20,24},{24,20... | collective-permute-start | bytes 3145736 | tf_op jit(solution)/shard_map/ppermute | solution.py:590
  612.7 36.1 %all-to-all-start.16 = ((bf16[4,128,2048]{2,1,0:T(8,128)(2,1)}), bf16[4,128,2048]{2,1,0:T(8,128)(2,1)}, u32[]{:S(2)}, u32[]{:S(2)}) async-start(bf16[4,128,2048]{2,1,0:T(8,128)(2,1)} %broadcast_in_dim.64), calls=%async_computation.16 | async-start | bytes 4194304 | tf_op jit(solution)/shard_map/all_to_all | solution.py:525
  648.8 49.0 %collective-permute-start.43 = (bf16[4,256,512]{2,1,0:T(8,128)(2,1)}, bf16[4,256,512]{2,1,0:T(8,128)(2,1)}, u32[]{:S(2)}, u32[]{:S(2)}) collective-permute-start(bf16[4,256,512]{2,1,0:T(8,128)(2,1)} %add_convert_fusion.25), channel_id=1, source_target_pairs={{4,0},{8,12},{5,1},{9,13},{6,2},{10,14},{7,3},{11,15},{20,16},{24,... | collective-permute-start | bytes 3145736 | tf_op jit(solution)/shard_map/ppermute | solution.py:590
  663.6 37.3 %collective-permute-start.44 = (bf16[4,256,512]{2,1,0:T(8,128)(2,1)}, bf16[4,256,512]{2,1,0:T(8,128)(2,1)S(1)}, u32[]{:S(2)}, u32[]{:S(2)}) collective-permute-start(bf16[4,256,512]{2,1,0:T(8,128)(2,1)} %add_convert_fusion.24), channel_id=1, source_target_pairs={{4,8},{8,4},{5,9},{9,5},{6,10},{10,6},{7,11},{11,7},{20,24},{24,20... | collective-permute-start | bytes 3145736 | tf_op jit(solution)/shard_map/ppermute | solution.py:590
  664.4 39.1 %collective-permute-start.45 = (bf16[4,256,512]{2,1,0:T(8,128)(2,1)}, bf16[4,256,512]{2,1,0:T(8,128)(2,1)S(1)}, u32[]{:S(2)}, u32[]{:S(2)}) collective-permute-start(bf16[4,256,512]{2,1,0:T(8,128)(2,1)} %bitcast.70), channel_id=1, source_target_pairs={{0,4},{12,8},{1,5},{13,9},{2,6},{14,10},{3,7},{15,11},{16,20},{28,... | collective-permute-start | bytes 3145736 | tf_op jit(solution)/shard_map/ppermute | solution.py:590
  708.6 39.2 %collective-permute-start.47 = (bf16[1024,1024]{1,0:T(8,128)(2,1)}, bf16[1024,1024]{1,0:T(8,128)(2,1)}, u32[]{:S(2)}, u32[]{:S(2)}) collective-permute-start(bf16[1024,1024]{1,0:T(8,128)(2,1)} %convolution_convert_fusion.6), channel_id=1, source_target_pairs={{0,16},{16,0},{1,17},{17,1},{2,18},{18,2},{3,19},{19,3},{4,20},{20... | collective-permute-start | bytes 6291464 | tf_op jit(solution)/shard_map/ppermute | solution.py:517
  717.9 37.9 %collective-permute-start.46 = (bf16[512,2048]{1,0:T(8,128)(2,1)}, bf16[512,2048]{1,0:T(8,128)(2,1)}, u32[]{:S(2)}, u32[]{:S(2)}) collective-permute-start(bf16[512,2048]{1,0:T(8,128)(2,1)} %convolution_convert_fusion.4), channel_id=1, source_target_pairs={{0,16},{16,0},{1,17},{17,1},{2,18},{18,2},{3,19},{19,3},{4,20},{20... | collective-permute-start | bytes 6291464 | tf_op jit(solution)/shard_map/ppermute | solution.py:517
  730.8 42.4 %collective-permute-start.48 = (bf16[4,256,512]{2,1,0:T(8,128)(2,1)}, bf16[4,256,512]{2,1,0:T(8,128)(2,1)}, u32[]{:S(2)}, u32[]{:S(2)}) collective-permute-start(bf16[4,256,512]{2,1,0:T(8,128)(2,1)} %add_convert_fusion.23), channel_id=1, source_target_pairs={{4,0},{8,12},{5,1},{9,13},{6,2},{10,14},{7,3},{11,15},{20,16},{24,... | collective-permute-start | bytes 3145736 | tf_op jit(solution)/shard_map/ppermute | solution.py:590
  732.1 43.5 %collective-permute-start.49 = (bf16[4,256,512]{2,1,0:T(8,128)(2,1)}, bf16[4,256,512]{2,1,0:T(8,128)(2,1)}, u32[]{:S(2)}, u32[]{:S(2)}) collective-permute-start(bf16[4,256,512]{2,1,0:T(8,128)(2,1)} %add_convert_fusion.22), channel_id=1, source_target_pairs={{4,8},{8,4},{5,9},{9,5},{6,10},{10,6},{7,11},{11,7},{20,24},{24,20... | collective-permute-start | bytes 3145736 | tf_op jit(solution)/shard_map/ppermute | solution.py:590
  736.2 42.2 %collective-permute-start.50 = (bf16[4,256,592]{1,2,0:T(8,128)(2,1)}, bf16[4,256,592]{1,2,0:T(8,128)(2,1)}, u32[]{:S(2)}, u32[]{:S(2)}) collective-permute-start(bf16[4,256,592]{1,2,0:T(8,128)(2,1)} %copy.276), channel_id=1, source_target_pairs={{0,4},{12,8},{1,5},{13,9},{2,6},{14,10},{3,7},{15,11},{16,20},{28,... | collective-permute-start | bytes 3637256 | tf_op jit(solution)/shard_map/ppermute | solution.py:590
  790.7 51.6 %collective-permute-start.51 = (bf16[1024,1104]{0,1:T(8,128)(2,1)}, bf16[1024,1104]{0,1:T(8,128)(2,1)}, u32[]{:S(2)}, u32[]{:S(2)}) collective-permute-start(bf16[1024,1104]{0,1:T(8,128)(2,1)} %convolution_convert_fusion), channel_id=1, source_target_pairs={{0,16},{16,0},{1,17},{17,1},{2,18},{18,2},{3,19},{19,3},{4,20},{20... | collective-permute-start | bytes 6782984 | tf_op jit(solution)/shard_map/ppermute | solution.py:517
  793.5 28.0 %collective-permute-start.54 = (bf16[512,1024]{1,0:T(8,128)(2,1)}, bf16[512,1024]{1,0:T(8,128)(2,1)}, u32[]{:S(2)}, u32[]{:S(2)}) collective-permute-start(bf16[512,1024]{1,0:T(8,128)(2,1)} %add_convert_fusion.21), channel_id=1, source_target_pairs={{0,4},{12,8},{1,5},{13,9},{2,6},{14,10},{3,7},{15,11},{16,20},{28,... | collective-permute-start | bytes 3145736 | tf_op jit(solution)/shard_map/ppermute | solution.py:590
  810.0 29.2 %all-to-all-start.21 = ((bf16[4,128,2048]{2,1,0:T(8,128)(2,1)}), bf16[4,128,2048]{2,1,0:T(8,128)(2,1)}, u32[]{:S(2)}, u32[]{:S(2)}) async-start(bf16[4,128,2048]{2,1,0:T(8,128)(2,1)} %bitcast.240), calls=%async_computation.21 | async-start | bytes 4194304 | tf_op jit(solution)/shard_map/all_to_all | solution.py:525
  852.2 37.0 %collective-permute-start.56 = (bf16[512,1024]{1,0:T(8,128)(2,1)}, bf16[512,1024]{1,0:T(8,128)(2,1)}, u32[]{:S(2)}, u32[]{:S(2)}) collective-permute-start(bf16[512,1024]{1,0:T(8,128)(2,1)} %add_convert_fusion.15), channel_id=1, source_target_pairs={{4,8},{8,4},{5,9},{9,5},{6,10},{10,6},{7,11},{11,7},{20,24},{24,20... | collective-permute-start | bytes 3145736 | tf_op jit(solution)/shard_map/ppermute | solution.py:590
  855.6 29.3 %all-to-all-start.22 = ((bf16[4,256,512]{2,1,0:T(8,128)(2,1)}), bf16[4,256,512]{2,1,0:T(8,128)(2,1)}, u32[]{:S(2)}, u32[]{:S(2)}) async-start(bf16[4,256,512]{2,1,0:T(8,128)(2,1)} %bitcast.267), calls=%async_computation.22 | async-start | bytes 2097152 | tf_op jit(solution)/shard_map/all_to_all | solution.py:525
  861.6 41.3 %collective-permute-start.55 = (bf16[4,256,592]{1,2,0:T(8,128)(2,1)}, bf16[4,256,592]{1,2,0:T(8,128)(2,1)}, u32[]{:S(2)}, u32[]{:S(2)}) collective-permute-start(bf16[4,256,592]{1,2,0:T(8,128)(2,1)} %copy.282), channel_id=1, source_target_pairs={{4,0},{8,12},{5,1},{9,13},{6,2},{10,14},{7,3},{11,15},{20,16},{24,... | collective-permute-start | bytes 3637256 | tf_op jit(solution)/shard_map/ppermute | solution.py:590
  863.0 37.3 %collective-permute-start.57 = (bf16[512,1024]{1,0:T(8,128)(2,1)}, bf16[512,1024]{1,0:T(8,128)(2,1)}, u32[]{:S(2)}, u32[]{:S(2)}) collective-permute-start(bf16[512,1024]{1,0:T(8,128)(2,1)} %add_convert_fusion.20), channel_id=1, source_target_pairs={{0,4},{12,8},{1,5},{13,9},{2,6},{14,10},{3,7},{15,11},{16,20},{28,... | collective-permute-start | bytes 3145736 | tf_op jit(solution)/shard_map/ppermute | solution.py:590
  915.9 28.8 %all-to-all-start.24 = ((bf16[4,512,512]{2,1,0:T(8,128)(2,1)}), bf16[4,512,512]{2,1,0:T(8,128)(2,1)}, u32[]{:S(2)}, u32[]{:S(2)}) async-start(bf16[4,512,512]{2,1,0:T(8,128)(2,1)} %copy.285), calls=%async_computation.24 | async-start | bytes 4194304 | tf_op jit(solution)/shard_map/all_to_all | solution.py:525
  944.7 52.3 %all-to-all-start.25 = ((bf16[4,512,512]{2,1,0:T(8,128)(2,1)}), bf16[4,512,512]{2,1,0:T(8,128)(2,1)}, u32[]{:S(2)}, u32[]{:S(2)}) async-start(bf16[4,512,512]{2,1,0:T(8,128)(2,1)} %all-to-all-done.24), calls=%async_computation.25 | async-start | bytes 4194304 | tf_op jit(solution)/shard_map/all_to_all | solution.py:548
  950.1 50.5 %collective-permute-start.65 = (f32[2,28099]{1,0:T(2,128)}, f32[2,28099]{1,0:T(2,128)}, u32[]{:S(2)}, u32[]{:S(2)}) collective-permute-start(f32[2,28099]{1,0:T(2,128)} %pad_maximum_fusion.9), channel_id=1, source_target_pairs={{0,16},{16,0},{1,17},{17,1},{2,18},{18,2},{3,19},{19,3},{4,20},{20... | collective-permute-start | bytes 674384 | tf_op jit(solution)/shard_map/ppermute | solution.py:517
  951.6 54.8 %collective-permute-start.58 = (bf16[512,1024]{1,0:T(8,128)(2,1)}, bf16[512,1024]{1,0:T(8,128)(2,1)}, u32[]{:S(2)}, u32[]{:S(2)}) collective-permute-start(bf16[512,1024]{1,0:T(8,128)(2,1)} %add_convert_fusion.14), channel_id=1, source_target_pairs={{4,0},{8,12},{5,1},{9,13},{6,2},{10,14},{7,3},{11,15},{20,16},{24,... | collective-permute-start | bytes 3145736 | tf_op jit(solution)/shard_map/ppermute | solution.py:590
  952.9 55.8 %collective-permute-start.59 = (bf16[512,1024]{1,0:T(8,128)(2,1)S(1)}, bf16[512,1024]{1,0:T(8,128)(2,1)}, u32[]{:S(2)}, u32[]{:S(2)}) collective-permute-start(bf16[512,1024]{1,0:T(8,128)(2,1)S(1)} %copy-done.46), channel_id=1, source_target_pairs={{4,8},{8,4},{5,9},{9,5},{6,10},{10,6},{7,11},{11,7},{20,24},{24,20... | collective-permute-start | bytes 3145736 | tf_op jit(solution)/shard_map/ppermute | solution.py:590
  954.5 56.8 %collective-permute-start.60 = (bf16[4,256,512]{2,1,0:T(8,128)(2,1)}, bf16[4,256,512]{2,1,0:T(8,128)(2,1)}, u32[]{:S(2)}, u32[]{:S(2)}) collective-permute-start(bf16[4,256,512]{2,1,0:T(8,128)(2,1)} %all-to-all-done.19), channel_id=1, source_target_pairs={{0,4},{12,8},{1,5},{13,9},{2,6},{14,10},{3,7},{15,11},{16,20},{28,... | collective-permute-start | bytes 3145736 | tf_op jit(solution)/shard_map/ppermute | solution.py:590
  997.0 27.9 %all-to-all-start.26 = ((bf16[4,512,512]{2,1,0:T(8,128)(2,1)}), bf16[4,512,512]{2,1,0:T(8,128)(2,1)S(1)}, u32[]{:S(2)}, u32[]{:S(2)}) async-start(bf16[4,512,512]{2,1,0:T(8,128)(2,1)} %all-to-all-done.25), calls=%async_computation.26 | async-start | bytes 4194304 | tf_op jit(solution)/shard_map/all_to_all | solution.py:525
  1026.5 42.8 %collective-permute-start.70 = (bf16[512,1024]{1,0:T(8,128)(2,1)}, bf16[512,1024]{1,0:T(8,128)(2,1)S(1)}, u32[]{:S(2)}, u32[]{:S(2)}) collective-permute-start(bf16[512,1024]{1,0:T(8,128)(2,1)} %add_convert_fusion.12), channel_id=1, source_target_pairs={{4,0},{8,12},{5,1},{9,13},{6,2},{10,14},{7,3},{11,15},{20,16},{24,... | collective-permute-start | bytes 3145736 | tf_op jit(solution)/shard_map/ppermute | solution.py:590
  1030.4 44.3 %collective-permute-start.71 = (bf16[4,256,512]{2,1,0:T(8,128)(2,1)S(1)}, bf16[4,256,512]{2,1,0:T(8,128)(2,1)}, u32[]{:S(2)}, u32[]{:S(2)}) collective-permute-start(bf16[4,256,512]{2,1,0:T(8,128)(2,1)S(1)} %add_convert_fusion.11), channel_id=1, source_target_pairs={{4,8},{8,4},{5,9},{9,5},{6,10},{10,6},{7,11},{11,7},{20,24},{24,20... | collective-permute-start | bytes 3145736 | tf_op jit(solution)/shard_map/ppermute | solution.py:590
  1036.3 34.0 %all-to-all-start.27 = ((bf16[4,256,512]{2,1,0:T(8,128)(2,1)}), bf16[4,256,512]{2,1,0:T(8,128)(2,1)S(1)}, u32[]{:S(2)}, u32[]{:S(2)}) async-start(bf16[4,256,512]{2,1,0:T(8,128)(2,1)} %broadcast_select_fusion.17), calls=%async_computation.27 | async-start | bytes 2097152 | tf_op jit(solution)/shard_map/all_to_all | solution.py:525
  1039.9 36.3 %collective-permute-start.72 = (bf16[4,256,512]{2,1,0:T(8,128)(2,1)}, bf16[4,256,512]{2,1,0:T(8,128)(2,1)}, u32[]{:S(2)}, u32[]{:S(2)}) collective-permute-start(bf16[4,256,512]{2,1,0:T(8,128)(2,1)} %all-to-all-done.20), channel_id=1, source_target_pairs={{0,4},{12,8},{1,5},{13,9},{2,6},{14,10},{3,7},{15,11},{16,20},{28,... | collective-permute-start | bytes 3145736 | tf_op jit(solution)/shard_map/ppermute | solution.py:590
  1121.8 27.4 %collective-permute-start.81 = (bf16[4,256,512]{2,1,0:T(8,128)(2,1)}, bf16[4,256,512]{2,1,0:T(8,128)(2,1)S(1)}, u32[]{:S(2)}, u32[]{:S(2)}) collective-permute-start(bf16[4,256,512]{2,1,0:T(8,128)(2,1)} %add_convert_fusion.7), channel_id=1, source_target_pairs={{4,8},{8,4},{5,9},{9,5},{6,10},{10,6},{7,11},{11,7},{20,24},{24,20... | collective-permute-start | bytes 3145736 | tf_op jit(solution)/shard_map/ppermute | solution.py:590
  1122.7 28.9 %collective-permute-start.82 = (bf16[4,256,592]{1,2,0:T(8,128)(2,1)}, bf16[4,256,592]{1,2,0:T(8,128)(2,1)}, u32[]{:S(2)}, u32[]{:S(2)}) collective-permute-start(bf16[4,256,592]{1,2,0:T(8,128)(2,1)} %all-to-all-done.23), channel_id=1, source_target_pairs={{0,4},{12,8},{1,5},{13,9},{2,6},{14,10},{3,7},{15,11},{16,20},{28,... | collective-permute-start | bytes 3637256 | tf_op jit(solution)/shard_map/ppermute | solution.py:590
  1129.9 27.3 %collective-permute-start.77 = (bf16[4,256,592]{1,2,0:T(8,128)(2,1)}, bf16[4,256,592]{1,2,0:T(8,128)(2,1)}, u32[]{:S(2)}, u32[]{:S(2)}) collective-permute-start(bf16[4,256,592]{1,2,0:T(8,128)(2,1)} %all-to-all-done.30), channel_id=1, source_target_pairs={{0,16},{1,17},{2,18},{3,19},{4,20},{5,21},{6,22},{7,23},{8,24},{9,... | collective-permute-start | bytes 3637256 | tf_op jit(solution)/shard_map/ppermute | solution.py:997
  1188.3 28.8 %collective-permute-start.89 = (bf16[4,256,592]{1,2,0:T(8,128)(2,1)}, bf16[4,256,592]{1,2,0:T(8,128)(2,1)}, u32[]{:S(2)}, u32[]{:S(2)}) collective-permute-start(bf16[4,256,592]{1,2,0:T(8,128)(2,1)} %copy.296), channel_id=1, source_target_pairs={{4,0},{8,12},{5,1},{9,13},{6,2},{10,14},{7,3},{11,15},{20,16},{24,... | collective-permute-start | bytes 3637256 | tf_op jit(solution)/shard_map/ppermute | solution.py:590
  1189.6 32.5 %collective-permute-start.88 = (bf16[512,1024]{1,0:T(8,128)(2,1)}, bf16[512,1024]{1,0:T(8,128)(2,1)}, u32[]{:S(2)}, u32[]{:S(2)}) collective-permute-start(bf16[512,1024]{1,0:T(8,128)(2,1)} %broadcast_select_fusion.18.refs_1_), channel_id=1, source_target_pairs={{16,0},{17,1},{18,2},{19,3},{20,4},{21,5},{22,6},{23,7},{24,8},{25... | collective-permute-start | bytes 3145736 | tf_op jit(solution)/shard_map/ppermute | solution.py:997
  1204.4 31.0 %collective-permute-start.61 = (bf16[2,128,2048]{2,1,0:T(8,128)(2,1)}, bf16[2,128,2048]{2,1,0:T(8,128)(2,1)}, u32[]{:S(2)}, u32[]{:S(2)}) collective-permute-start(bf16[2,128,2048]{2,1,0:T(8,128)(2,1)} %fusion.24), channel_id=1, source_target_pairs={{0,16},{16,0},{1,17},{17,1},{2,18},{18,2},{3,19},{19,3},{4,20},{20... | collective-permute-start | bytes 3145736 | tf_op jit(solution)/shard_map/ppermute | solution.py:517
  1224.5 27.3 %collective-permute-start.90 = (bf16[4,256,592]{1,2,0:T(8,128)(2,1)}, bf16[4,256,592]{1,2,0:T(8,128)(2,1)}, u32[]{:S(2)}, u32[]{:S(2)}) collective-permute-start(bf16[4,256,592]{1,2,0:T(8,128)(2,1)} %copy.298), channel_id=1, source_target_pairs={{16,0},{17,1},{18,2},{19,3},{20,4},{21,5},{22,6},{23,7},{24,8},{25... | collective-permute-start | bytes 3637256 | tf_op jit(solution)/shard_map/ppermute | solution.py:997
  (130 other events, 2122.3 us)

commit v5 on v4

--- a/solution.py
+++ b/solution.py
@@ -463,54 +463,88 @@
     )(ids, dz, dx, *near[0], *near[1], *far[0], *far[1])
 
 
-def place_kernel(ids, *refs, plan, small):
-    out = refs[-1]
-    h, j = pl.program_id(0), pl.program_id(1)
-    for ref, (side, layer, first, size, turned) in zip(refs, plan):
-
-        @pl.when((h == side) & (ids[1] == layer) & (j >= first) & (j < first + size))
-        def _():
-            v = (ref[0] if turned else ref[...]).astype(F32)
-            out[...] = v.T if turned else v
-
-    if small:
-
-        @pl.when(j == pl.num_programs(1) - 1)
-        def _():
-            v = refs[len(plan)]
-            out[: v.shape[1], :] = v[0]
-
-
-def place_blocks(ids, chunks, small, out_shape, block, out_index, steps):
-    def step_of(side, layer, first, size, index):
-        def where(h, j, ids):
-            used = jnp.logical_and(h == side, ids[1] == layer)
-            return index(jnp.where(used, jnp.clip(j - first, 0, size - 1), 0))
-
-        return where
-
-    in_specs = [
-        pl.BlockSpec(shape, step_of(side, layer, first, size, index))
-        for _, side, layer, first, size, _, shape, index in chunks
-    ]
-    args = [c[0] for c in chunks]
-    if small is not None:
-        in_specs.append(pl.BlockSpec((1,) + small.shape[1:], lambda h, j, ids: (h, 0, 0)))
-        args.append(small)
+def place_kernel(ids, *refs, plan, count, rows_of_small):
+    small = refs[count]
+    out, eye, pieces, blocks, in_sem, out_sem = refs[-6:]
+    core = ids[1]
+    size, share = blocks.shape[1:]
+
+    def fetch(k):
+        for layer in range(2):
+
+            @pl.when(core == layer)
+            def _():
+                src = refs[plan[k][layer]]
+                pltpu.make_async_copy(
+                    src.at[:, :, pl.ds(0, size)], pieces.at[k % 2], in_sem.at[k % 2]
+                ).start()
+
+    def send(step, first, count):
+        return pltpu.make_async_copy(
+            blocks.at[step % 2, pl.ds(0, count)],
+            out.at[pl.ds(first, count)],
+            out_sem.at[step % 2],
+        )
+
+    eye[...] = (
+        lax.broadcasted_iota(jnp.int32, eye.shape, 0)
+        == lax.broadcasted_iota(jnp.int32, eye.shape, 1)
+    ).astype(BF16)
+    fetch(0)
+    sent = []
+    for k, (_, _, side, firsts) in enumerate(plan):
+        if k + 1 < len(plan):
+            fetch(k + 1)
+        pltpu.make_async_copy(pieces.at[k % 2], pieces.at[k % 2], in_sem.at[k % 2]).wait()
+        shift = jnp.where(side == 0, core, 1 - core) * (2 * size)
+        for p, first in enumerate(firsts):
+            step = len(sent)
+            if step >= 2:
+                sent[step - 2].wait()
+            blocks[step % 2] = lax.dot_general(
+                pieces[k % 2, p],
+                eye[...],
+                (((0,), (0,)), ((), ())),
+                preferred_element_type=F32,
+            )
+            sent.append(send(step, pl.multiple_of(first + shift, 8), size))
+            sent[-1].start()
+    if rows_of_small:
+        step = len(sent)
+        sent[step - 2].wait()
+        first, count = rows_of_small
+        sent.append(
+            pltpu.make_async_copy(small, out.at[pl.ds(first, count)], out_sem.at[step % 2])
+        )
+        sent[-1].start()
+    sent[-2].wait()
+    sent[-1].wait()
+
+
+def place_in(ids, arrays, plan, small, rows_of_small, before, shape, size):
+    places, share, _ = arrays[0].shape
+    any_space = pl.BlockSpec(memory_space=pl.ANY)
     return pl.pallas_call(
         functools.partial(
-            place_kernel, plan=tuple(c[1:6] for c in chunks), small=small is not None
+            place_kernel, plan=plan, count=len(arrays), rows_of_small=rows_of_small
         ),
-        grid_spec=pltpu.PrefetchScalarGridSpec(
-            num_scalar_prefetch=1,
-            grid=(2, steps),
-            in_specs=in_specs,
-            out_specs=pl.BlockSpec(block, out_index),
-        ),
-        out_shape=jax.ShapeDtypeStruct(out_shape, F32),
+        in_specs=[pl.BlockSpec(memory_space=pltpu.SMEM)]
+        + [any_space] * len(arrays)
+        + [pl.BlockSpec(memory_space=pltpu.VMEM)]
+        + [any_space] * len(before),
+        out_specs=any_space,
+        scratch_shapes=[
+            pltpu.VMEM((share, share), BF16),
+            pltpu.VMEM((2, places, share, size), BF16),
+            pltpu.VMEM((2, size, share), F32),
+            pltpu.SemaphoreType.DMA((2,)),
+            pltpu.SemaphoreType.DMA((2,)),
+        ],
+        out_shape=jax.ShapeDtypeStruct(shape, F32),
+        input_output_aliases={len(arrays) + 2: 0} if before else {},
         compiler_params=pltpu.CompilerParams(vmem_limit_bytes=VMEM_BYTES),
-        name="place_gradient",
-    )(ids, *args)
+        name="place_in",
+    )(ids, *arrays, small, *before)
 
 
 def swap_section(v):
@@ -540,27 +574,29 @@
     return jnp.sum(got.astype(F32), axis=0)
 
 
-def trade_places(v):
+def in_group(v):
     n, s = lax.axis_size("fsdp"), lax.axis_size("seq")
-    rows, size = v.shape[0], v.shape[1] // n
     groups = [[j * n + i for i in range(n)] for j in range(s // n)]
-    v = v.reshape(rows, n, size).transpose(1, 0, 2)
-    v = lax.all_to_all(exchange(v), "seq", 0, 0, axis_index_groups=groups, tiled=True)
-    return exchange(v).transpose(1, 0, 2).reshape(rows, n * size)
-
-
-def sum_everywhere(v):
-    n, s = lax.axis_size("fsdp"), lax.axis_size("seq")
-    v = v + swap_section(v)
-    m = 1
-    while m < n:
-        v = v + lax.ppermute(v, "fsdp", [(k, k ^ m) for k in range(n)])
-        m *= 2
-    m = 1
-    while m < s:
-        v = v + lax.ppermute(v, "seq", [(k, k ^ m) for k in range(s)])
-        m *= 2
-    return v
+    return lax.all_to_all(v, "seq", 0, 0, axis_index_groups=groups, tiled=True)
+
+
+def quarters(v):
+    n = lax.axis_size("fsdp")
+    return v.reshape(v.shape[0], n, -1).transpose(1, 0, 2)
+
+
+def joined(v):
+    return v.transpose(1, 0, 2).reshape(v.shape[1], -1)
+
+
+def move_fsdp(v, m):
+    n = lax.axis_size("fsdp")
+    return lax.ppermute(v, "fsdp", [(k, k ^ m) for k in range(n)])
+
+
+def move_seq(v, m):
+    s = lax.axis_size("seq")
+    return lax.ppermute(v, "seq", [(k, k ^ m) for k in range(s)])
 
 
 class SeqSums:
@@ -683,8 +719,6 @@
     def pick(a, b):
         return jnp.where(upper, a, b)
 
-    h0 = trade_places(at(inputs, c)[0])
-
     w = w_in[0].T
 
     def cut(first, size):
@@ -710,12 +744,17 @@
         ]
         return near, [lax.ppermute(v, "section", [(layer, 1 - layer)]) for v in near]
 
+    def whole_slot(v):
+        return joined(to_all(v.reshape(n * rows, share)))
+
     pieces_x = [piece_x(m) for m in range(n)]
-    pieces_z = [piece_z(m) for m in range(n)]
     near_x0, far_x0 = fetch(pieces_x, 0)
-    all_h0 = gather_rows(h0)
-    pieces_z0, near_x0, all_h0 = tie((pieces_z, near_x0, all_h0))
-    near_z0, far_z0 = fetch(pieces_z0, 0)
+    part_h0 = in_group(exchange(quarters(at(inputs, c)[0])))
+    near_x0, part_h0 = tie((near_x0, part_h0))
+    far_x0 = [lax.ppermute(v, "section", [(0, 1)]) for v in near_x0]
+    all_h0 = whole_slot(part_h0)
+    pieces_z, _ = tie(([piece_z(m) for m in range(n)], part_h0))
+    near_z0, far_z0 = fetch(pieces_z, 0)
 
     pack = jnp.concatenate(
         [
@@ -755,25 +794,7 @@
         )
         small.append((gain, cw, hp, gout))
 
-    pieces_x1, pieces_z1, own_ct, wo_mine, own_len, near_z0 = tie(
-        (pieces_x, pieces_z, at(cotangent, c)[0], w_out[0], at(lengths, c), near_z0)
-    )
-    wo_other = swap_section(wo_mine)
-    wo = (pick(wo_mine, wo_other), pick(wo_other, wo_mine))
-    near_x1, far_x1 = fetch(pieces_x1, 1)
-    near_z1, far_z1 = fetch(pieces_z1, 1)
-    win = ((near_z0, far_z0, near_x0, far_x0), (near_z1, far_z1, near_x1, far_x1))
-    slot_pairs = [
-        ((j * n + i) * n + k, (j * n + k) * n + i)
-        for j in range(segments)
-        for i in range(n)
-        for k in range(n)
-    ]
-    length = lax.ppermute(own_len, ("seq", "fsdp"), slot_pairs)
-    start = ((place // n) * n + f) * rows
-    valid = (start + jnp.arange(rows, dtype=jnp.int32) < length[0]).astype(F32)[:, None]
-    dout1 = trade_places(own_ct).astype(F32)
-
+    win = [(near_z0, far_z0, near_x0, far_x0), None]
     expand = (
         jnp.arange(heads)[:, None] == jnp.arange(width)[None, :] // HEAD_DIM
     ).astype(BF16)
@@ -822,21 +843,51 @@
 
     normed_in0 = normalised(all_h0.astype(F32), small[0][0]).astype(BF16)
     px0 = project_x(normed_in0, 0)
+    px0, pieces_x1, pieces_z1, own_ct, wo_mine, own_len = tie(
+        (px0, pieces_x, pieces_z, at(cotangent, c)[0], w_out[0], at(lengths, c))
+    )
+    near_x1, far_x1 = fetch(pieces_x1, 1)
+    wo_other = swap_section(wo_mine)
+    wo = (pick(wo_mine, wo_other), pick(wo_other, wo_mine))
+    slot_pairs = [
+        ((j * n + i) * n + k, (j * n + k) * n + i)
+        for j in range(segments)
+        for i in range(n)
+        for k in range(n)
+    ]
+    length = lax.ppermute(own_len, ("seq", "fsdp"), slot_pairs)
+    first_row = (place // n) * n * rows
+    all_valid = first_row + jnp.arange(n * rows, dtype=jnp.int32) < length[0]
+    all_valid = all_valid.astype(F32)[:, None]
+    own_rows = lambda v: lax.dynamic_slice_in_dim(v, f * rows, rows, 0)
+    valid = own_rows(all_valid)
+    h0 = own_rows(all_h0)
     fwd0 = scan(px0, 0)
     pz0 = project_z(normed_in0, 0)
     g0 = gate(pz0, fwd0[0][0])
     stat0 = sum_of_shares(jnp.sum(g0 * g0, axis=1).reshape(n, rows)).reshape(-1)
     r0 = lax.rsqrt(stat0 / INNER + EPS)
     normed0 = gated(pz0, fwd0[0][0], r0, 0)
+    part_ct = in_group(exchange(quarters(own_ct)))
+    normed0, wo, near_x1, part_ct = tie((normed0, wo, near_x1, part_ct))
+    far_x1 = [lax.ppermute(v, "section", [(1, 0)]) for v in near_x1]
     mixed0 = scatter_sum(jnp.dot(normed0, wo[0], preferred_element_type=F32).astype(BF16))
     out0 = valid * (h0.astype(F32) + mixed0)
     h1 = out0.astype(BF16)
 
     normed_in1 = gather_rows(normalised(h1.astype(F32), small[1][0]).astype(BF16))
+    normed_in1, far_x1, part_ct, pieces_z1 = tie((normed_in1, far_x1, part_ct, pieces_z1))
+    near_z1, far_z1 = fetch(pieces_z1, 1)
+    win[1] = (near_z1, far_z1, near_x1, far_x1)
     px1 = project_x(normed_in1, 1)
-    dmixed1 = gather_rows((valid * dout1).astype(BF16))
+    all_ct = whole_slot(part_ct)
+    fwd1 = scan(px1, 1)
+    fwd1, all_ct, near_z1 = tie((fwd1, all_ct, near_z1))
+    far_z1 = [lax.ppermute(v, "section", [(1, 0)]) for v in near_z1]
+    win[1] = (near_z1, far_z1, near_x1, far_x1)
+    dout1 = own_rows(all_ct).astype(F32)
+    dmixed1 = (all_valid * all_ct.astype(F32)).astype(BF16)
     dn1 = dot_cols(dmixed1, wo[1])
-    fwd1 = scan(px1, 1)
     pz1 = project_z(normed_in1, 1)
     g1 = gate(pz1, fwd1[0][0])
     stat1 = sum_of_shares(
@@ -850,40 +901,43 @@
     r1 = lax.rsqrt(stat1[0] / INNER + EPS)
     normed1 = gated(pz1, fwd1[0][0], r1, 1)
 
-    sums = SeqSums()
-
-    def halves(v):
-        v = v.reshape(v.shape[0], n, 2, half)
-        return [
-            pick(v[:, :, t], v[:, :, 1 - t]).reshape(v.shape[0], n * half) for t in range(2)
-        ]
-
-    def half_sums(own, away, parts):
-        sizes = [p.shape[1] for p in parts]
-        other = swap_section(dot_rows(away, jnp.concatenate(parts, axis=1)).astype(BF16))
-        result, first = [], 0
-        for p, size in zip(parts, sizes):
-            share_of = other[:, first : first + size].astype(F32)
-            result.append((dot_rows(own, p) + share_of).astype(BF16))
-            first += size
+    part_width = width // 4
+
+    def cut_half(v, k):
+        size = v.shape[1] // 2
+        return lax.dynamic_slice_in_dim(v, k * size, size, 1)
+
+    def half_of(parts, k):
+        return jnp.concatenate([cut_half(v, k) for v in parts], axis=1)
+
+    def away_in(normed_in, parts):
+        return swap_section(dot_rows(normed_in, half_of(parts, 1 - c)).astype(BF16))
+
+    def own_in_pieces(normed_in, parts, away):
+        own = half_of(parts, c)
+        result = []
+        for cols in (slice(0, part_width), slice(part_width, own.shape[1])):
+            total = dot_rows(normed_in, own[:, cols]) + away[:, cols].astype(F32)
+            result.append(total.astype(BF16).reshape(n, share, -1))
         return result
 
-    def grads_in(kept, parts):
-        return [v.reshape(n, half, -1) for v in half_sums(*kept, parts)]
-
-    def grads_out(normed, dmixed):
-        part = lambda k: lax.dynamic_slice_in_dim(normed, k * (width // 2), width // 2, 1)
-        return half_sums(part(c), part(1 - c), [dmixed[:, : D // 2], dmixed[:, D // 2 :]])
+    def away_out(normed, dmixed):
+        return swap_section(dot_rows(cut_half(normed, 1 - c), dmixed).astype(BF16))
+
+    def own_out_pieces(normed, dmixed, away):
+        own = cut_half(normed, c)
+        result = []
+        for cols in (slice(0, D // 2), slice(D // 2, D)):
+            total = dot_rows(own, dmixed[:, cols]) + away[:, cols].astype(F32)
+            result.append(total.astype(BF16))
+        return result
 
     def with_group(dxs, dbc):
         total = jnp.sum(exchange(dbc), axis=0).astype(BF16)
         column = jnp.arange(GROUP)[None, :] // group
         own = jnp.where(column == f, jnp.concatenate([total] * n, axis=1), 0)
         full = lax.dynamic_update_slice(dxs, own.astype(BF16), (0, width))
-        late = jnp.concatenate(
-            [dxs[:, width // 2 : width], total, dxs[:, width + GROUP :]], axis=1
-        )
-        return full, late
+        return full, [dxs[:, :width], total, dxs[:, width + GROUP :]]
 
     def back_in(dz, full, layer):
         near_z, far_z, near_x, far_x = win[layer]
@@ -901,75 +955,8 @@
         top = jnp.stack([r.reshape(n, rows), coef.reshape(n, rows)], axis=1)
         return jnp.concatenate([top, jnp.zeros((n, 6, rows), F32)], axis=1)
 
-    rc1 = scales(r1, (r1 * r1 * r1 / INNER) * stat1[1])
-    kept0, kept1 = halves(normed_in0), halves(normed_in1)
-    go1 = sums.add(grads_out(normed1, dmixed1))
-    rc1, normed1, h1 = sums.end((rc1, normed1, h1))
-
-    sums.begin()
-    mixed1 = scatter_sum(jnp.dot(normed1, wo[1], preferred_element_type=F32).astype(BF16))
-    d1 = unscan(pz1, px1, fwd1, dn1, rc1, 1)
-    out1 = valid * (h1.astype(F32) + mixed1)
-    d1, out1, mixed1 = sums.end((d1, out1, mixed1))
-
-    sums.begin()
-    full1, late1 = with_group(d1[1], d1[2])
-    back1 = back_in(d1[0], full1, 1)
-    gz = grads_in(kept1, [d1[0][:, : width // 2], d1[0][:, width // 2 :]])
-    back1, late1, gz = sums.end((back1, late1, gz))
-    gz1 = sums.add(gz)
-
-    sums.begin()
-    dnin1 = scatter_sum(back1)
-    gx = grads_in(kept1, [d1[1][:, : width // 2], late1])
-    dnin1, gx = sums.end((dnin1, gx))
-    gx1 = sums.add(gx)
-
-    sums.begin()
-    grad1, dgin1 = back_norm(dout1, dnin1, h1, small[1][0])
-    dout0 = grad1.astype(BF16).astype(F32)
-    dmixed0_own = (valid * dout0).astype(BF16)
-    dmixed0 = gather_rows(dmixed0_own)
-    along0 = to_all(jnp.sum(dmixed0_own.astype(F32) * mixed0, axis=-1)).reshape(-1)
-    rc0 = scales(r0, (r0 * r0 / INNER) * along0)
-    grad1, dgin1, dmixed0, rc0 = sums.end((grad1, dgin1, dmixed0, rc0))
-
-    sums.begin()
-    dn0 = dot_cols(dmixed0, wo[0])
-    d0 = unscan(pz0, px0, fwd0, dn0, rc0, 0)
-    d0 = sums.end(d0)
-
-    sums.begin()
-    go = grads_out(normed0, dmixed0)
-    full0, late0 = with_group(d0[1], d0[2])
-    gz = [exchange(v) for v in grads_in(kept0, [d0[0][:, : width // 2], d0[0][:, width // 2 :]])]
-    go, full0, late0, gz = sums.end((go, full0, late0, gz))
-    go0 = sums.add(go)
-    gz0 = sums.add(gz)
-
-    sums.begin()
-    dnin0 = scatter_sum(back_in(d0[0], full0, 0))
-    gx = grads_in(kept0, [d0[1][:, : width // 2], late0])
-    dnin0, gx = sums.end((dnin0, gx))
-
-    sums.begin()
-    gx = [exchange(v) for v in gx]
-    grad0, dgin0 = back_norm(dout0, dnin0, h0, small[0][0])
-    gx, grad0, dgin0 = sums.end((gx, grad0, dgin0))
-    gx0 = sums.add(gx)
-
-    sums.begin()
-    back = trade_places(
-        jnp.concatenate([h1, out1.astype(BF16), grad0.astype(BF16), grad1.astype(BF16)])
-    )
-    back = sums.end(back)
-
-    sums.begin()
-    smalls1 = (d1[3][0], d1[4][:5], d1[5][:3])
-    smalls0 = (d0[3][0], d0[4][:5], d0[5][:3])
-
-    def packed(dgin, smalls, out, mixed):
-        dgain, dconv, dhp = smalls
+    def packed(dgin, d, out, mixed):
+        dgain, dconv, dhp = d[3][0], d[4][:5], d[5][:3]
         put = lambda v, size, at_lane: lax.dynamic_update_slice(
             jnp.zeros(v.shape[:-1] + (size,), F32), v, (0,) * (v.ndim - 1) + (at_lane,)
         )
@@ -988,30 +975,109 @@
             ]
         )
 
-    p = sum_everywhere(
-        jnp.stack([packed(dgin0, smalls0, out0, mixed0), packed(dgin1, smalls1, out1, mixed1)])
-    )
-    p = sums.end(pick(p[0], p[1]))
-
     def hand_over(v, layer):
         return lax.ppermute(v, "section", [(1 - layer, layer)])
 
+    sums = SeqSums()
+    rc1 = scales(r1, (r1 * r1 * r1 / INNER) * stat1[1])
+    away = away_out(normed1, dmixed1)
+    go1 = sums.add(own_out_pieces(normed1, dmixed1, away))
+    rc1, normed1, dn1 = sums.end((rc1, normed1, dn1))
+
+    sums.begin()
+    d1 = unscan(pz1, px1, fwd1, dn1, rc1, 1)
+    mixed1 = scatter_sum(jnp.dot(normed1, wo[1], preferred_element_type=F32).astype(BF16))
+    d1, mixed1 = sums.end((d1, mixed1))
+
+    sums.begin()
+    away = away_in(normed_in1, [d1[0]])
+    full1, xs1 = with_group(d1[1], d1[2])
+    back1 = back_in(d1[0], full1, 1)
+    back1, xs1, away, full1 = sums.end((back1, xs1, away, full1))
+
+    sums.begin()
+    dnin1 = scatter_sum(back1)
+    gz = own_in_pieces(normed_in1, [d1[0]], away)
+    away = away_in(normed_in1, xs1)
+    dnin1, gz, away = sums.end((dnin1, gz, away))
+    gz1 = sums.add(gz)
+
+    sums.begin()
+    grad1, dgin1 = back_norm(dout1, dnin1, h1, small[1][0])
+    dout0 = grad1.astype(BF16).astype(F32)
+    dmixed0_own = (valid * dout0).astype(BF16)
+    dmixed0 = gather_rows(dmixed0_own)
+    along0 = to_all(jnp.sum(dmixed0_own.astype(F32) * mixed0, axis=-1)).reshape(-1)
+    rc0 = scales(r0, (r0 * r0 / INNER) * along0)
+    gx = own_in_pieces(normed_in1, xs1, away)
+    out1 = valid * (h1.astype(F32) + mixed1)
+    grad1, dgin1, dmixed0, rc0, gx, out1 = sums.end((grad1, dgin1, dmixed0, rc0, gx, out1))
+    gx1 = sums.add(gx)
+
+    sums.begin()
+    dn0 = dot_cols(dmixed0, wo[0])
+    d0 = unscan(pz0, px0, fwd0, dn0, rc0, 0)
+    d0 = sums.end(d0)
+
+    sums.begin()
+    away_z = away_in(normed_in0, [d0[0]])
+    away_o = away_out(normed0, dmixed0)
+    full0, xs0 = with_group(d0[1], d0[2])
+    gz = own_in_pieces(normed_in0, [d0[0]], away_z)
+    go = own_out_pieces(normed0, dmixed0, away_o)
+    full0, xs0, gz, go = sums.end((full0, xs0, gz, go))
+    go0 = sums.add(go)
+
+    sums.begin()
+    away = away_in(normed_in0, xs0)
+    gz = [exchange(v) for v in gz]
+    gx = own_in_pieces(normed_in0, xs0, away)
+    gz, gx, full0 = sums.end((gz, gx, full0))
+    gz0 = sums.add(gz)
+
+    sums.begin()
+    gx = [exchange(v) for v in gx]
+    back0 = back_in(d0[0], full0, 0)
+    gx, back0 = sums.end((gx, back0))
+    gx0 = sums.add(gx)
+
+    sums.begin()
+    dnin0 = scatter_sum(back0)
+    grad0, dgin0 = back_norm(dout0, dnin0, h0, small[0][0])
+    p = jnp.stack([packed(dgin0, d0, out0, mixed0), packed(dgin1, d1, out1, mixed1)])
+    p = p + swap_section(p)
+    p, grad0, grad1, h1, out1 = sums.end((p, grad0, grad1, h1, out1))
+
     names = {"own": {}, "away": {}}
-    order = [(k, 1, "in") for k in gz1 + gx1] + [(k, 1, "out") for k in go1]
-    order += [(k, 0, "in") for k in gz0 + gx0] + [(k, 0, "out") for k in go0]
+    order = [(k, 1, "out") for k in go1] + [(k, 1, "in") for k in gz1 + gx1]
+    order += [(k, 0, "out") for k in go0] + [(k, 0, "in") for k in gz0 + gx0]
+    back = jnp.concatenate([h1, out1.astype(BF16), grad0.astype(BF16), grad1.astype(BF16)])
+    back_steps = [lambda v: exchange(quarters(v)), in_group, lambda v: joined(exchange(v))]
+    p_steps = [lambda v, m=m: move_fsdp(v, m) for m in (1 << j for j in range(n.bit_length() - 1))]
+    p_steps += [lambda v, m=m: move_seq(v, m) for m in (1 << j for j in range(nz.bit_length() - 1))]
+    exchanged = set()
     while order:
         sums.begin()
-        ready = [e for e in order if e[0] not in [k for k, _ in sums.moving]]
-        ready = [e for e in ready if sums.done([e[0]])][:3]
-        fresh = []
-        for k, layer, kind in ready:
-            v = sums.values[k]
-            v = exchange(v) if (layer, kind) == (1, "in") else v
-            fresh.append((v, hand_over(v, layer)))
-        fresh, p = sums.end((fresh, p))
-        for (k, layer, kind), (v, other) in zip(ready, fresh):
-            names["own"][k], names["away"][k] = v, other
-        order = [e for e in order if e not in ready]
+        moving = [k for k, _ in sums.moving]
+        ready = [e for e in order if e[0] not in moving and sums.done([e[0]])]
+        turn = [e for e in ready if e[1:] == (1, "in") and e[0] not in exchanged][:2]
+        if back_steps:
+            back = back_steps.pop(0)(back)
+            turn = turn[:1]
+        if p_steps:
+            p = p + p_steps.pop(0)(p)
+        swapped = {e[0]: exchange(sums.values[e[0]]) for e in turn}
+        final = [e for e in ready if e[1:] != (1, "in") or e[0] in exchanged][:2]
+        fresh = {e[0]: hand_over(sums.values[e[0]], e[1]) for e in final}
+        kept = {e[0]: sums.values[e[0]] for e in final}
+        swapped, fresh, kept, back, p = sums.end((swapped, fresh, kept, back, p))
+        for k, v in swapped.items():
+            sums.values[k] = v
+            exchanged.add(k)
+        for k in fresh:
+            names["own"][k], names["away"][k] = kept[k], fresh[k]
+        order = [e for e in order if e not in final]
+    p = pick(p[0], p[1])
 
     used = 0
 
@@ -1029,75 +1095,41 @@
     act_rms = jnp.sqrt(totals[:2] / (totals[2] * D))[None]
 
     sides = ("own", "away")
-    part_width = width // 2
-    by_layer = (gz0 + gx0, gz1 + gx1)
-
-    def small_rows(v):
-        v = v[:, :, part_width:].astype(F32).transpose(0, 2, 1)
-        return jnp.concatenate(
-            [v[:, :group].reshape(GROUP, half), v[:, group:].reshape(HEADS, half)]
-        )
-
-    small_in = jnp.stack(
+    held = [
+        [[names[side][k] for k in ks] for ks in (gz0 + gx0 + go0, gz1 + gx1 + go1)]
+        for side in sides
+    ]
+
+    def both_halves(a, b):
+        return jnp.stack([pick(a, b), pick(b, a)], axis=1)
+
+    narrow = [pick(side[0][3], side[1][3])[:, :, part_width:] for side in held]
+    narrow = both_halves(*[v.astype(F32).transpose(0, 2, 1) for v in narrow])
+    small_in = jnp.concatenate(
         [
-            small_rows(pick(names[side][by_layer[0][3]], names[side][by_layer[1][3]]))
-            for side in sides
+            narrow[:, :, : group // 2].reshape(GROUP, share),
+            narrow[:, :, group // 2 :].reshape(HEADS, share),
         ]
     )
-    turned = lambda h, ids: jnp.where(h == 0, ids[1], 1 - ids[1])
-    chunks_in = [
-        (
-            names[side][by_layer[layer][k]],
-            s,
-            layer,
-            n * k,
-            n,
-            True,
-            (1, half, part_width),
-            lambda i: (i, 0, 0),
-        )
-        for s, side in enumerate(sides)
-        for layer in range(2)
-        for k in range(4)
+    g_w_in = []
+    shape_in = (2 * INNER + GROUP + HEADS, share)
+    for ks, rows_of_small in (((0, 1), None), ((2, 3), (2 * INNER, GROUP + HEADS))):
+        arrays, plan = [], []
+        for k in ks:
+            for s in range(2):
+                arrays += [held[s][0][k], held[s][1][k]]
+                base = k // 2 * INNER + k % 2 * part_width
+                firsts = tuple(base + q * width for q in range(n))
+                plan.append((len(arrays) - 2, len(arrays) - 1, s, firsts))
+        g_w_in = [
+            place_in(
+                ids, arrays, tuple(plan), small_in, rows_of_small, g_w_in, shape_in, part_width
+            )
+        ]
+    halves_out = [
+        jnp.concatenate([pick(side[0][k], side[1][k]) for k in (4, 5)], axis=1) for side in held
     ]
-    g_w_in = place_blocks(
-        ids,
-        chunks_in,
-        small_in,
-        (2 * INNER + GROUP + HEADS, share),
-        (part_width, half),
-        lambda h, j, ids: (
-            jnp.where(
-                j < 4 * n, j // (2 * n) * 2 * n + (j % n) * 2 + j // n % 2, 4 * n
-            ),
-            turned(h, ids),
-        ),
-        4 * n + 1,
-    )
-    chunks_out = [
-        (
-            names[side][(go0, go1)[layer][k]],
-            s,
-            layer,
-            k,
-            1,
-            False,
-            (width // 2, D // 2),
-            lambda i: (0, 0),
-        )
-        for s, side in enumerate(sides)
-        for layer in range(2)
-        for k in range(2)
-    ]
-    g_w_out = place_blocks(
-        ids,
-        chunks_out,
-        None,
-        (width, D),
-        (width // 2, D // 2),
-        lambda h, j, ids: (turned(h, ids), j),
-        2,
-    )
+    g_w_out = both_halves(*[v[None] for v in halves_out]).reshape(width, D).astype(F32)
 
     back = back.reshape(2, 2, rows, D)
     kept_back = pick(back[:, 0], back[:, 1])
@@ -1109,7 +1141,7 @@
         both_back[0][None, :, None],
         both_back[1].astype(F32)[None, :, None],
         o_gain_in[None],
-        g_w_in.T[None],
+        g_w_in[0].T[None],
         o_conv[None, :4],
         o_conv[None, 4],
         o_heads[None, 0],

time: 1310 us -> 1260 us (0.962)
  starting transfers between devices: 385 us -> 333 us
  waiting for transfers between devices: 302 us -> 342 us
  local copies, waits for them, and re-layouts: 169 us -> 148 us
    ppermute x36, waiting for transfers between devices: 74 us -> 138 us  [begin(): got = lax.ppermute(v, 'seq', self.pairs[step])]
    ppermute x4 -> x16, waiting for transfers between devices: 26.8 us -> 79.7 us  [the longest x2 52.8 us: move_seq(): return lax.ppermute(v, 'seq', [(k, k ^ m) for k in range(s)])]
    all_to_all x3, waiting for transfers between devices: 47.4 us -> 0.01 us  [in_group(): return lax.all_to_all(v, 'seq', 0, 0, axis_index_groups=groups, tiled=True)]
    ppermute x10, starting transfers between devices: 49.1 us -> 20.4 us  [swap_section(): return lax.ppermute(v, 'section', [(0, 1), (1, 0)])]
    select_n x4 -> x0, local copies, waits for them, and re-layouts: 23.3 us -> none  [pick(): return jnp.where(upper, a, b)]
    ppermute x16 -> x4, starting transfers between devices: 27.6 us -> 5.16 us  [fetch(): lax.ppermute(v, 'section', [(layer, 1 - layer)])]
    all_to_all x25, waiting for transfers between devices: 101 us -> 79.7 us  [exchange(): return lax.all_to_all(v, 'fsdp', 0, 0, tiled=True)]
    ppermute x4 -> x16, starting transfers between devices: 4.95 us -> 23.8 us  [the longest x4 8.36 us: per_device(): far_x1 = [lax.ppermute(v, 'section', [(1, 0)]) for v in near_x1]]
  transfers between devices with their start and end apart: 119 -> 119, of which waited for: 35 -> 35; matrix products, arithmetic and copies ran while one was open for 24% -> 23% of each run, Pallas kernels for 9% -> 10%
where the time goes in v5:
time: 1260 us; the launch traced here: 1250 us
  waiting for transfers between devices  342 us (27%)
  starting transfers between devices  333 us (26%)
  other arithmetic  177 us (14%)
  local copies, waits for them, and re-layouts  148 us (12%)
  Pallas kernels  134 us (11%)
  matrix products  84 us (7%)
  blocking collectives  23.7 us (2%)
    ppermute x36, waiting for transfers between devices, begin(): got = lax.ppermute(v, 'seq', self.pairs[step])  138 us
    all_to_all x25, starting transfers between devices, exchange(): return lax.all_to_all(v, 'fsdp', 0, 0, tiled=True)  106 us
    ppermute x36, starting transfers between devices, begin(): got = lax.ppermute(v, 'seq', self.pairs[step])  100 us
    all_to_all x25, waiting for transfers between devices, exchange(): return lax.all_to_all(v, 'fsdp', 0, 0, tiled=True)  79.7 us
    convert_element_type x24, other arithmetic, begin(): v = (v.astype(F32) + got.astype(F32)).astype(BF16)  65.1 us
    dot_general x18, matrix products, dot_rows(): lax.dot_general(a, b, (((0,), (0,)), ((), ())), preferred_element_type=F32)  62 us
    ppermute x2, waiting for transfers between devices, move_seq(): return lax.ppermute(v, 'seq', [(k, k ^ m) for k in range(s)])  52.8 us
    pallas_call x2, Pallas kernels, run_backward(): pl.pallas_call(backward_kernel, grid=(count,), in_specs=[block(width), bl...  40.6 us
  transfers between devices with their start and end apart: 119, of which 35 were waited for; matrix products, arithmetic and copies ran while one was open for 23% of the time, Pallas kernels for 10%

profile of v5, /device:TPU:1, one launch (start us, length us, event | category | flops | bytes accessed | tf_op | source)
XLA Modules:
  0.0 1245.1 jit_solution(17065516985121851949)
XLA Ops:
  3.2 5.6 dynamic-slice_bitcast_fusion
  28.4 23.7 %all_to_all.150 = bf16[4,128,512]{1,2,0:T(8,128)(2,1)} all-to-all(bf16[4,128,512]{1,2,0:T(8,128)(2,1)S(1)} %bitcast.250), channel_id=1, replica_groups=mesh['section'=2,'seq'=4,'fsdp'=4] {'fsdp'}, dimensions={0} | all-to-all | bytes 1048576 | tf_op jit(solution)/shard_map/all_to_all | solution.py:559
  52.1 4.6 all-to-all-start.1
  58.8 12.0 collective-permute-start.3
  77.0 4.4 all-to-all-start.2
  86.8 19.1 %all-to-all-done.2 = bf16[4,512,512]{2,1,0:T(8,128)(2,1)} async-done(((bf16[4,512,512]{2,1,0:T(8,128)(2,1)}), bf16[4,512,512]{2,1,0:T(8,128)(2,1)}, u32[]{:S(2)}, u32[]{:S(2)}) %all-to-all-start.2) | async-done | bytes 2097184 | tf_op jit(solution)/shard_map/all_to_all | solution.py:559
  112.5 8.7 project.5.proj
  138.8 10.6 scan_forward.2
  150.7 8.3 collective-permute-done.8.refs_5_.refs_9_
  161.3 7.2 project.4.pz
  184.3 4.8 all-to-all-start.6
  192.6 5.8 broadcast_select_fusion
  198.5 14.0 %collective-permute-done.18.refs_2_.refs_6_ = bf16[1296,512]{1,0:T(8,128)(2,1)} collective-permute-done((bf16[1296,512]{1,0:T(8,128)(2,1)}, bf16[1296,512]{1,0:T(8,128)(2,1)}, u32[]{:S(2)}, u32[]{:S(2)}) %collective-permute-start.18) | collective-permute-done | bytes 1327136 | tf_op jit(solution)/shard_map/ppermute | solution.py:742
  212.4 6.2 convolution_convert_fusion.3
  218.6 4.4 all-to-all-start.7
  226.1 21.6 %all-to-all-done.7 = bf16[4,128,2048]{2,1,0:T(8,128)(2,1)} async-done(((bf16[4,128,2048]{2,1,0:T(8,128)(2,1)}), bf16[4,128,2048]{2,1,0:T(8,128)(2,1)}, u32[]{:S(2)}, u32[]{:S(2)}) %all-to-all-start.7) | async-done | bytes 2097184 | tf_op jit(solution)/shard_map/all_to_all | solution.py:559
  255.3 4.5 all-to-all-start.8
  271.6 12.5 %all-to-all-done.8 = bf16[4,128,2048]{2,1,0:T(8,128)(2,1)} async-done(((bf16[4,128,2048]{2,1,0:T(8,128)(2,1)}), bf16[4,128,2048]{2,1,0:T(8,128)(2,1)}, u32[]{:S(2)}, u32[]{:S(2)}) %all-to-all-start.8) | async-done | bytes 2097184 | tf_op jit(solution)/shard_map/all_to_all | solution.py:559
  288.7 4.5 all-to-all-start.9
  303.0 7.8 project.6.proj
  310.9 10.6 scan_forward.3
  329.6 12.1 collective-permute-done.26.refs_3_
  351.4 7.4 project.7.pz
  358.9 6.8 multiply_reduce_fusion.2
  393.1 4.5 all-to-all-start.11
  397.6 4.5 collective-permute-start.32
  405.0 20.3 %scan_backward.2 = (bf16[512,1024]{1,0:T(8,128)(2,1)S(1)}, bf16[512,1296]{1,0:T(8,128)(2,1)S(1)}, f32[4,512,64]{2,1,0:T(8,128)S(1)}, f32[8,1024]{1,0:T(8,128)S(1...) custom-call(f32[512,1024]{1,0:T(8,128)} %project.7.pz, ...), custom_call_target="tpu_custom_call" | custom-call | tf_op jit(solution)/shard_map/scan_backward/pallas_call | solution.py:303
  458.7 10.5 project_back.2
  484.5 4.6 all-to-all-start.13
  500.6 17.0 %collective-permute-done.37 = bf16[512,1024]{1,0:T(8,128)(2,1)} collective-permute-done((bf16[512,1024]{1,0:T(8,128)(2,1)}, bf16[512,1024]{1,0:T(8,128)(2,1)}, u32[]{:S(2)}, u32[]{:S(2)}) %collective-permute-start.37) | collective-permute-done | bytes 1048608 | tf_op jit(solution)/shard_map/ppermute | solution.py:626
  536.8 4.8 all-to-all-start.14
  561.0 5.0 all-to-all-done.14
  566.0 5.3 collective-permute-start.42
  578.1 5.3 fusion.126.dn
  583.4 20.2 %scan_backward.3 = (bf16[512,1024]{1,0:T(8,128)(2,1)S(1)}, bf16[512,1296]{1,0:T(8,128)(2,1)S(1)}, f32[4,512,64]{2,1,0:T(8,128)S(1)}, f32[8,1024]{1,0:T(8,128)S(1...) custom-call(f32[512,1024]{1,0:T(8,128)} %project.4.pz, ...), custom_call_target="tpu_custom_call" | custom-call | tf_op jit(solution)/shard_map/scan_backward/pallas_call | solution.py:303
  611.9 4.6 all-to-all-start.16
  641.1 4.8 collective-permute-done.47
  674.2 6.0 collective-permute-start.51
  686.9 10.5 collective-permute-done.49
  699.8 5.5 collective-permute-done.51
  726.1 5.4 collective-permute-start.54
  743.2 10.6 project_back.3
  768.3 4.8 all-to-all-done.20
  773.1 7.4 collective-permute-start.58
  785.1 4.6 all-to-all-start.21
  794.4 6.4 collective-permute-done.58
  806.6 5.8 collective-permute-done.56
  837.9 4.6 all-to-all-start.26
  850.9 21.8 %collective-permute-done.61 = f32[2,28099]{1,0:T(2,128)S(1)} collective-permute-done((f32[2,28099]{1,0:T(2,128)S(1)}, f32[2,28099]{1,0:T(2,128)S(1)}, u32[]{:S(2)}, u32[]{:S(2)}) %collective-permute-start.61) | collective-permute-done | bytes 224824 | tf_op jit(solution)/shard_map/ppermute | solution.py:594
  887.2 5.4 all-to-all-done.24.refs_5_
  892.5 4.4 all-to-all-start.27
  907.7 5.7 collective-permute-start.66
  914.2 38.1 %collective-permute-done.70 = bf16[4,512,256]{2,1,0:T(8,128)(2,1)S(1)} collective-permute-done((bf16[4,512,256]{2,1,0:T(8,128)(2,1)}, bf16[4,512,256]{2,1,0:T(8,128)(2,1)S(1)}, u32[]{:S(2)}, u32[]{:S(2)}) %collective-permute-start.70) | collective-permute-done | bytes 1048608 | tf_op jit(solution)/shard_map/ppermute | solution.py:626
  962.8 17.8 %collective-permute-start.76 = (bf16[4,512,256]{2,1,0:T(8,128)(2,1)}, bf16[4,512,256]{2,1,0:T(8,128)(2,1)}, u32[]{:S(2)}, u32[]{:S(2)}) collective-permute-start(bf16[4,512,256]{2,1,0:T(8,128)(2,1)} %copy-done.88), channel_id=1, source_target_pairs={{0,4},{12,8},{1,5},{13,9},{2,6},{14,10},{3,7},{15,11},{16,20},{28,... | collective-permute-start | bytes 3145736 | tf_op jit(solution)/shard_map/ppermute | solution.py:626
  988.0 24.2 %collective-permute-done.73 = f32[2,28099]{1,0:T(2,128)S(1)} collective-permute-done((f32[2,28099]{1,0:T(2,128)S(1)}, f32[2,28099]{1,0:T(2,128)S(1)}, u32[]{:S(2)}, u32[]{:S(2)}) %collective-permute-start.73) | collective-permute-done | bytes 224824 | tf_op jit(solution)/shard_map/ppermute | solution.py:599
  1012.1 5.6 collective-permute-start.72
  1038.3 6.0 collective-permute-start.82
  1045.6 28.6 %collective-permute-done.79 = f32[2,28099]{1,0:T(2,128)S(1)} collective-permute-done((f32[2,28099]{1,0:T(2,128)S(1)}, f32[2,28099]{1,0:T(2,128)S(1)}, u32[]{:S(2)}, u32[]{:S(2)}) %collective-permute-start.79) | collective-permute-done | bytes 224824 | tf_op jit(solution)/shard_map/ppermute | solution.py:599
  1107.9 5.0 collective-permute-start.84
  1112.9 14.6 %collective-permute-done.85 = bf16[4,512,256]{2,1,0:T(8,128)(2,1)} collective-permute-done((bf16[4,512,256]{2,1,0:T(8,128)(2,1)}, bf16[4,512,256]{2,1,0:T(8,128)(2,1)}, u32[]{:S(2)}, u32[]{:S(2)}) %collective-permute-start.85) | collective-permute-done | bytes 1048608 | tf_op jit(solution)/shard_map/ppermute | solution.py:626
  1148.6 26.3 %collective-permute-done.88 = bf16[4,512,296]{1,2,0:T(8,128)(2,1)} collective-permute-done((bf16[4,512,296]{1,2,0:T(8,128)(2,1)}, bf16[4,512,296]{1,2,0:T(8,128)(2,1)}, u32[]{:S(2)}, u32[]{:S(2)}) %collective-permute-start.88) | collective-permute-done | bytes 1212448 | tf_op jit(solution)/shard_map/ppermute | solution.py:626
  1189.6 4.7 bitcast_convert_fusion
  1217.8 10.0 place_in.2.refs_9_
  1227.8 10.5 place_in.3
  (748 shorter events, 602.2 us)
Async XLA Ops:
  11.0 62.5 %collective-permute-start = (bf16[1296,512]{1,0:T(8,128)(2,1)}, bf16[1296,512]{1,0:T(8,128)(2,1)}, u32[]{:S(2)}, u32[]{:S(2)}) collective-permute-start(bf16[1296,512]{1,0:T(8,128)(2,1)} %get-tuple-element.270), channel_id=1, source_target_pairs={{0,1},{1,0},{2,3},{3,2},{4,5},{5,4},{6,7},{7,6},{8,9},{9,8},{10,11... | collective-permute-start | bytes 3981320 | tf_op jit(solution)/shard_map/ppermute | solution.py:742
  12.8 60.7 %collective-permute-start.1 = (bf16[1296,512]{1,0:T(8,128)(2,1)}, bf16[1296,512]{1,0:T(8,128)(2,1)}, u32[]{:S(2)}, u32[]{:S(2)}) collective-permute-start(bf16[1296,512]{1,0:T(8,128)(2,1)} %get-tuple-element.271), channel_id=1, source_target_pairs={{0,2},{1,3},{2,0},{3,1},{4,6},{5,7},{6,4},{7,5},{8,10},{9,11},{10,... | collective-permute-start | bytes 3981320 | tf_op jit(solution)/shard_map/ppermute | solution.py:742
  14.5 59.0 %collective-permute-start.2 = (bf16[1296,512]{1,0:T(8,128)(2,1)}, bf16[1296,512]{1,0:T(8,128)(2,1)}, u32[]{:S(2)}, u32[]{:S(2)}) collective-permute-start(bf16[1296,512]{1,0:T(8,128)(2,1)} %get-tuple-element.272), channel_id=1, source_target_pairs={{0,3},{1,2},{2,1},{3,0},{4,7},{5,6},{6,5},{7,4},{8,11},{9,10},{10,... | collective-permute-start | bytes 3981320 | tf_op jit(solution)/shard_map/ppermute | solution.py:742
  58.8 27.9 %collective-permute-start.3 = (bf16[4,7024]{1,0:T(4,128)(2,1)S(1)}, bf16[4,7024]{1,0:T(4,128)(2,1)S(1)}, u32[]{:S(2)}, u32[]{:S(2)}) collective-permute-start(bf16[4,7024]{1,0:T(4,128)(2,1)S(1)} %bitcast.264), channel_id=1, source_target_pairs={{0,16},{16,0},{1,17},{17,1},{2,18},{18,2},{3,19},{19,3},{4,20},{20... | collective-permute-start | bytes 168584 | tf_op jit(solution)/shard_map/ppermute | solution.py:551
  77.0 28.8 %all-to-all-start.2 = ((bf16[4,512,512]{2,1,0:T(8,128)(2,1)}), bf16[4,512,512]{2,1,0:T(8,128)(2,1)}, u32[]{:S(2)}, u32[]{:S(2)}) async-start(bf16[4,512,512]{2,1,0:T(8,128)(2,1)} %broadcast_in_dim.47), calls=%async_computation.2 | async-start | bytes 4194304 | tf_op jit(solution)/shard_map/all_to_all | solution.py:559
  81.5 31.0 %collective-permute-start.11 = (bf16[1296,512]{1,0:T(8,128)(2,1)S(1)}, bf16[1296,512]{1,0:T(8,128)(2,1)}, u32[]{:S(2)}, u32[]{:S(2)}) collective-permute-start(bf16[1296,512]{1,0:T(8,128)(2,1)S(1)} %get-tuple-element.276.refs_0_.refs_4_), channel_id=1, source_target_pairs={{0,16},{1,17},{2,18},{3,19},{4,20},{5,21},{6,22},{7,23},{8,24},{9,... | collective-permute-start | bytes 3981320 | tf_op jit(solution)/shard_map/ppermute | solution.py:754
  82.8 29.7 %collective-permute-start.12 = (bf16[1296,512]{1,0:T(8,128)(2,1)}, bf16[1296,512]{1,0:T(8,128)(2,1)}, u32[]{:S(2)}, u32[]{:S(2)}) collective-permute-start(bf16[1296,512]{1,0:T(8,128)(2,1)} %collective-permute-done.refs_1_.refs_5_), channel_id=1, source_target_pairs={{0,16},{1,17},{2,18},{3,19},{4,20},{5,21},{6,22},{7,23},{8,24},{9,... | collective-permute-start | bytes 3981320 | tf_op jit(solution)/shard_map/ppermute | solution.py:754
  84.1 28.4 %collective-permute-start.13 = (bf16[1296,512]{1,0:T(8,128)(2,1)}, bf16[1296,512]{1,0:T(8,128)(2,1)}, u32[]{:S(2)}, u32[]{:S(2)}) collective-permute-start(bf16[1296,512]{1,0:T(8,128)(2,1)} %collective-permute-done.1.refs_2_.refs_6_), channel_id=1, source_target_pairs={{0,16},{1,17},{2,18},{3,19},{4,20},{5,21},{6,22},{7,23},{8,24},{9,... | collective-permute-start | bytes 3981320 | tf_op jit(solution)/shard_map/ppermute | solution.py:754
  121.2 71.4 %collective-permute-start.16 = (bf16[1024,2048]{1,0:T(8,128)(2,1)}, bf16[1024,2048]{1,0:T(8,128)(2,1)}, u32[]{:S(2)}, u32[]{:S(2)}) collective-permute-start(bf16[1024,2048]{1,0:T(8,128)(2,1)} %bitcast.36), channel_id=1, source_target_pairs={{0,16},{16,0},{1,17},{17,1},{2,18},{18,2},{3,19},{19,3},{4,20},{20... | collective-permute-start | bytes 12582920 | tf_op jit(solution)/shard_map/ppermute | solution.py:551
  131.5 27.6 %collective-permute-start.8 = (bf16[1024,512]{1,0:T(8,128)(2,1)}, bf16[1024,512]{1,0:T(8,128)(2,1)}, u32[]{:S(2)}, u32[]{:S(2)}) collective-permute-start(bf16[1024,512]{1,0:T(8,128)(2,1)} %collective-permute-done.4.refs_1_), channel_id=1, source_target_pairs={{0,16},{1,17},{2,18},{3,19},{4,20},{5,21},{6,22},{7,23},{8,24},{9,... | collective-permute-start | bytes 3145736 | tf_op jit(solution)/shard_map/ppermute | solution.py:745
  132.8 28.5 %collective-permute-start.9 = (bf16[1024,512]{1,0:T(8,128)(2,1)}, bf16[1024,512]{1,0:T(8,128)(2,1)}, u32[]{:S(2)}, u32[]{:S(2)}) collective-permute-start(bf16[1024,512]{1,0:T(8,128)(2,1)} %collective-permute-done.5.refs_2_), channel_id=1, source_target_pairs={{0,16},{1,17},{2,18},{3,19},{4,20},{5,21},{6,22},{7,23},{8,24},{9,... | collective-permute-start | bytes 3145736 | tf_op jit(solution)/shard_map/ppermute | solution.py:745
  134.4 37.7 %all-to-all-start.5 = ((bf16[4,128,512]{1,2,0:T(8,128)(2,1)}), bf16[4,128,512]{1,2,0:T(8,128)(2,1)}, u32[]{:S(2)}, u32[]{:S(2)}) async-start(bf16[4,128,512]{1,2,0:T(8,128)(2,1)} %bitcast.44), calls=%async_computation.5 | async-start | bytes 1048576 | tf_op jit(solution)/shard_map/all_to_all | solution.py:559
  179.3 33.2 %collective-permute-start.18 = (bf16[1296,512]{1,0:T(8,128)(2,1)}, bf16[1296,512]{1,0:T(8,128)(2,1)}, u32[]{:S(2)}, u32[]{:S(2)}) collective-permute-start(bf16[1296,512]{1,0:T(8,128)(2,1)} %get-tuple-element.271), channel_id=1, source_target_pairs={{16,18},{17,19},{18,16},{19,17},{20,22},{21,23},{22,20},{23,21},{2... | collective-permute-start | bytes 3981320 | tf_op jit(solution)/shard_map/ppermute | solution.py:742
  182.4 30.1 %collective-permute-start.19 = (bf16[1296,512]{1,0:T(8,128)(2,1)}, bf16[1296,512]{1,0:T(8,128)(2,1)}, u32[]{:S(2)}, u32[]{:S(2)}) collective-permute-start(bf16[1296,512]{1,0:T(8,128)(2,1)} %get-tuple-element.272), channel_id=1, source_target_pairs={{16,19},{17,18},{18,17},{19,16},{20,23},{21,22},{22,21},{23,20},{2... | collective-permute-start | bytes 3981320 | tf_op jit(solution)/shard_map/ppermute | solution.py:742
  218.6 29.1 %all-to-all-start.7 = ((bf16[4,128,2048]{2,1,0:T(8,128)(2,1)}), bf16[4,128,2048]{2,1,0:T(8,128)(2,1)}, u32[]{:S(2)}, u32[]{:S(2)}) async-start(bf16[4,128,2048]{2,1,0:T(8,128)(2,1)} %bitcast.247), calls=%async_computation.7 | async-start | bytes 4194304 | tf_op jit(solution)/shard_map/all_to_all | solution.py:559
  255.3 28.8 %all-to-all-start.8 = ((bf16[4,128,2048]{2,1,0:T(8,128)(2,1)}), bf16[4,128,2048]{2,1,0:T(8,128)(2,1)}, u32[]{:S(2)}, u32[]{:S(2)}) async-start(bf16[4,128,2048]{2,1,0:T(8,128)(2,1)} %broadcast_in_dim.53), calls=%async_computation.8 | async-start | bytes 4194304 | tf_op jit(solution)/shard_map/all_to_all | solution.py:559
  288.7 35.5 %all-to-all-start.9 = ((bf16[4,512,512]{2,1,0:T(8,128)(2,1)}), bf16[4,512,512]{2,1,0:T(8,128)(2,1)}, u32[]{:S(2)}, u32[]{:S(2)}) async-start(bf16[4,512,512]{2,1,0:T(8,128)(2,1)} %broadcast_in_dim.55), calls=%async_computation.9 | async-start | bytes 4194304 | tf_op jit(solution)/shard_map/all_to_all | solution.py:559
  293.2 36.4 %collective-permute-start.24 = (bf16[1024,512]{1,0:T(8,128)(2,1)}, bf16[1024,512]{1,0:T(8,128)(2,1)}, u32[]{:S(2)}, u32[]{:S(2)}) collective-permute-start(bf16[1024,512]{1,0:T(8,128)(2,1)} %get-tuple-element.295), channel_id=1, source_target_pairs={{16,17},{17,16},{18,19},{19,18},{20,21},{21,20},{22,23},{23,22},{2... | collective-permute-start | bytes 3145736 | tf_op jit(solution)/shard_map/ppermute | solution.py:742
  296.5 33.1 %collective-permute-start.25 = (bf16[1024,512]{1,0:T(8,128)(2,1)}, bf16[1024,512]{1,0:T(8,128)(2,1)}, u32[]{:S(2)}, u32[]{:S(2)}) collective-permute-start(bf16[1024,512]{1,0:T(8,128)(2,1)} %get-tuple-element.296), channel_id=1, source_target_pairs={{16,18},{17,19},{18,16},{19,17},{20,22},{21,23},{22,20},{23,21},{2... | collective-permute-start | bytes 3145736 | tf_op jit(solution)/shard_map/ppermute | solution.py:742
  299.6 42.1 %collective-permute-start.26 = (bf16[1024,512]{1,0:T(8,128)(2,1)}, bf16[1024,512]{1,0:T(8,128)(2,1)}, u32[]{:S(2)}, u32[]{:S(2)}) collective-permute-start(bf16[1024,512]{1,0:T(8,128)(2,1)} %get-tuple-element.297), channel_id=1, source_target_pairs={{16,19},{17,18},{18,17},{19,16},{20,23},{21,22},{22,21},{23,20},{2... | collective-permute-start | bytes 3145736 | tf_op jit(solution)/shard_map/ppermute | solution.py:742
  393.1 38.6 %all-to-all-start.11 = ((bf16[4,128,2048]{2,1,0:T(8,128)(2,1)}), bf16[4,128,2048]{2,1,0:T(8,128)(2,1)}, u32[]{:S(2)}, u32[]{:S(2)}) async-start(bf16[4,128,2048]{2,1,0:T(8,128)(2,1)} %bitcast.248), calls=%async_computation.11 | async-start | bytes 4194304 | tf_op jit(solution)/shard_map/all_to_all | solution.py:559
  397.6 31.5 %collective-permute-start.32 = (bf16[512,1024]{1,0:T(8,128)(2,1)}, bf16[512,1024]{1,0:T(8,128)(2,1)S(1)}, u32[]{:S(2)}, u32[]{:S(2)}) collective-permute-start(bf16[512,1024]{1,0:T(8,128)(2,1)} %add_convert_fusion.31), channel_id=1, source_target_pairs={{0,4},{12,8},{1,5},{13,9},{2,6},{14,10},{3,7},{15,11},{16,20},{28,... | collective-permute-start | bytes 3145736 | tf_op jit(solution)/shard_map/ppermute | solution.py:626
  439.1 36.9 %collective-permute-start.33 = (bf16[2048,512]{1,0:T(8,128)(2,1)}, bf16[2048,512]{1,0:T(8,128)(2,1)}, u32[]{:S(2)}, u32[]{:S(2)}) collective-permute-start(bf16[2048,512]{1,0:T(8,128)(2,1)} %convolution_convert_fusion.6), channel_id=1, source_target_pairs={{0,16},{16,0},{1,17},{17,1},{2,18},{18,2},{3,19},{19,3},{4,20},{20... | collective-permute-start | bytes 6291464 | tf_op jit(solution)/shard_map/ppermute | solution.py:551
  482.1 40.1 %collective-permute-start.36 = (bf16[2048,552]{0,1:T(8,128)(2,1)}, bf16[2048,552]{0,1:T(8,128)(2,1)}, u32[]{:S(2)}, u32[]{:S(2)}) collective-permute-start(bf16[2048,552]{0,1:T(8,128)(2,1)} %convolution_convert_fusion.1), channel_id=1, source_target_pairs={{0,16},{16,0},{1,17},{17,1},{2,18},{18,2},{3,19},{19,3},{4,20},{20... | collective-permute-start | bytes 6782984 | tf_op jit(solution)/shard_map/ppermute | solution.py:551
  484.5 35.5 %all-to-all-start.13 = ((bf16[4,128,2048]{2,1,0:T(8,128)(2,1)}), bf16[4,128,2048]{2,1,0:T(8,128)(2,1)}, u32[]{:S(2)}, u32[]{:S(2)}) async-start(bf16[4,128,2048]{2,1,0:T(8,128)(2,1)} %bitcast.242), calls=%async_computation.13 | async-start | bytes 4194304 | tf_op jit(solution)/shard_map/all_to_all | solution.py:559
  489.1 28.5 %collective-permute-start.37 = (bf16[512,1024]{1,0:T(8,128)(2,1)}, bf16[512,1024]{1,0:T(8,128)(2,1)}, u32[]{:S(2)}, u32[]{:S(2)}) collective-permute-start(bf16[512,1024]{1,0:T(8,128)(2,1)} %add_convert_fusion.28), channel_id=1, source_target_pairs={{4,0},{8,12},{5,1},{9,13},{6,2},{10,14},{7,3},{11,15},{20,16},{24,... | collective-permute-start | bytes 3145736 | tf_op jit(solution)/shard_map/ppermute | solution.py:626
  536.8 29.3 %all-to-all-start.14 = ((bf16[4,128,2048]{2,1,0:T(8,128)(2,1)}), bf16[4,128,2048]{2,1,0:T(8,128)(2,1)}, u32[]{:S(2)}, u32[]{:S(2)}) async-start(bf16[4,128,2048]{2,1,0:T(8,128)(2,1)} %broadcast_in_dim.59), calls=%async_computation.14 | async-start | bytes 4194304 | tf_op jit(solution)/shard_map/all_to_all | solution.py:559
  566.0 37.6 %collective-permute-start.42 = (bf16[4,512,256]{2,1,0:T(8,128)(2,1)}, bf16[4,512,256]{2,1,0:T(8,128)(2,1)S(1)}, u32[]{:S(2)}, u32[]{:S(2)}) collective-permute-start(bf16[4,512,256]{2,1,0:T(8,128)(2,1)} %bitcast.59), channel_id=1, source_target_pairs={{0,4},{12,8},{1,5},{13,9},{2,6},{14,10},{3,7},{15,11},{16,20},{28,... | collective-permute-start | bytes 3145736 | tf_op jit(solution)/shard_map/ppermute | solution.py:626
  571.3 35.6 %collective-permute-start.41 = (bf16[4,512,256]{2,1,0:T(8,128)(2,1)}, bf16[4,512,256]{2,1,0:T(8,128)(2,1)S(1)}, u32[]{:S(2)}, u32[]{:S(2)}) collective-permute-start(bf16[4,512,256]{2,1,0:T(8,128)(2,1)} %add_convert_fusion.25), channel_id=1, source_target_pairs={{4,8},{8,4},{5,9},{9,5},{6,10},{10,6},{7,11},{11,7},{20,24},{24,20... | collective-permute-start | bytes 3145736 | tf_op jit(solution)/shard_map/ppermute | solution.py:626
  576.3 57.6 %collective-permute-start.44 = (bf16[512,2048]{1,0:T(8,128)(2,1)}, bf16[512,2048]{1,0:T(8,128)(2,1)}, u32[]{:S(2)}, u32[]{:S(2)}) collective-permute-start(bf16[512,2048]{1,0:T(8,128)(2,1)} %convolution_convert_fusion.4), channel_id=1, source_target_pairs={{0,16},{16,0},{1,17},{17,1},{2,18},{18,2},{3,19},{19,3},{4,20},{20... | collective-permute-start | bytes 6291464 | tf_op jit(solution)/shard_map/ppermute | solution.py:551
  620.7 35.8 %collective-permute-start.43 = (bf16[2048,512]{1,0:T(8,128)(2,1)}, bf16[2048,512]{1,0:T(8,128)(2,1)}, u32[]{:S(2)}, u32[]{:S(2)}) collective-permute-start(bf16[2048,512]{1,0:T(8,128)(2,1)} %convolution_convert_fusion.5), channel_id=1, source_target_pairs={{0,16},{16,0},{1,17},{17,1},{2,18},{18,2},{3,19},{19,3},{4,20},{20... | collective-permute-start | bytes 6291464 | tf_op jit(solution)/shard_map/ppermute | solution.py:551
  667.3 48.3 %collective-permute-start.48 = (bf16[2048,552]{0,1:T(8,128)(2,1)}, bf16[2048,552]{0,1:T(8,128)(2,1)}, u32[]{:S(2)}, u32[]{:S(2)}) collective-permute-start(bf16[2048,552]{0,1:T(8,128)(2,1)} %convolution_convert_fusion), channel_id=1, source_target_pairs={{0,16},{16,0},{1,17},{17,1},{2,18},{18,2},{3,19},{19,3},{4,20},{20... | collective-permute-start | bytes 6782984 | tf_op jit(solution)/shard_map/ppermute | solution.py:551
  674.2 31.0 %collective-permute-start.51 = (bf16[4,512,296]{1,2,0:T(8,128)(2,1)}, bf16[4,512,296]{1,2,0:T(8,128)(2,1)}, u32[]{:S(2)}, u32[]{:S(2)}) collective-permute-start(bf16[4,512,296]{1,2,0:T(8,128)(2,1)} %copy.251), channel_id=1, source_target_pairs={{0,4},{12,8},{1,5},{13,9},{2,6},{14,10},{3,7},{15,11},{16,20},{28,... | collective-permute-start | bytes 3637256 | tf_op jit(solution)/shard_map/ppermute | solution.py:626
  726.1 32.1 %collective-permute-start.54 = (bf16[512,1024]{1,0:T(8,128)(2,1)}, bf16[512,1024]{1,0:T(8,128)(2,1)}, u32[]{:S(2)}, u32[]{:S(2)}) collective-permute-start(bf16[512,1024]{1,0:T(8,128)(2,1)} %add_convert_fusion.20), channel_id=1, source_target_pairs={{0,4},{12,8},{1,5},{13,9},{2,6},{14,10},{3,7},{15,11},{16,20},{28,... | collective-permute-start | bytes 3145736 | tf_op jit(solution)/shard_map/ppermute | solution.py:626
  773.1 27.7 %collective-permute-start.58 = (bf16[512,1024]{1,0:T(8,128)(2,1)}, bf16[512,1024]{1,0:T(8,128)(2,1)}, u32[]{:S(2)}, u32[]{:S(2)}) collective-permute-start(bf16[512,1024]{1,0:T(8,128)(2,1)} %add_convert_fusion.19), channel_id=1, source_target_pairs={{0,4},{12,8},{1,5},{13,9},{2,6},{14,10},{3,7},{15,11},{16,20},{28,... | collective-permute-start | bytes 3145736 | tf_op jit(solution)/shard_map/ppermute | solution.py:626
  783.8 28.6 %collective-permute-start.56 = (bf16[4,512,296]{1,2,0:T(8,128)(2,1)}, bf16[4,512,296]{1,2,0:T(8,128)(2,1)}, u32[]{:S(2)}, u32[]{:S(2)}) collective-permute-start(bf16[4,512,296]{1,2,0:T(8,128)(2,1)} %copy.256), channel_id=1, source_target_pairs={{4,0},{8,12},{5,1},{9,13},{6,2},{10,14},{7,3},{11,15},{20,16},{24,... | collective-permute-start | bytes 3637256 | tf_op jit(solution)/shard_map/ppermute | solution.py:626
  785.1 32.5 %all-to-all-start.21 = ((bf16[4,128,2048]{2,1,0:T(8,128)(2,1)}), bf16[4,128,2048]{2,1,0:T(8,128)(2,1)}, u32[]{:S(2)}, u32[]{:S(2)}) async-start(bf16[4,128,2048]{2,1,0:T(8,128)(2,1)} %bitcast.241), calls=%async_computation.21 | async-start | bytes 4194304 | tf_op jit(solution)/shard_map/all_to_all | solution.py:559
  837.9 37.2 %all-to-all-start.26 = ((bf16[4,512,512]{2,1,0:T(8,128)(2,1)}), bf16[4,512,512]{2,1,0:T(8,128)(2,1)}, u32[]{:S(2)}, u32[]{:S(2)}) async-start(bf16[4,512,512]{2,1,0:T(8,128)(2,1)} %bitcast.243), calls=%async_computation.26 | async-start | bytes 4194304 | tf_op jit(solution)/shard_map/all_to_all | solution.py:559
  842.5 36.9 %collective-permute-start.64 = (bf16[4,512,256]{2,1,0:T(8,128)(2,1)}, bf16[4,512,256]{2,1,0:T(8,128)(2,1)}, u32[]{:S(2)}, u32[]{:S(2)}) collective-permute-start(bf16[4,512,256]{2,1,0:T(8,128)(2,1)} %all-to-all-done.17), channel_id=1, source_target_pairs={{0,4},{12,8},{1,5},{13,9},{2,6},{14,10},{3,7},{15,11},{16,20},{28,... | collective-permute-start | bytes 3145736 | tf_op jit(solution)/shard_map/ppermute | solution.py:626
  844.9 37.2 %collective-permute-start.63 = (bf16[512,1024]{1,0:T(8,128)(2,1)S(1)}, bf16[512,1024]{1,0:T(8,128)(2,1)}, u32[]{:S(2)}, u32[]{:S(2)}) collective-permute-start(bf16[512,1024]{1,0:T(8,128)(2,1)S(1)} %copy-done.83), channel_id=1, source_target_pairs={{4,8},{8,4},{5,9},{9,5},{6,10},{10,6},{7,11},{11,7},{20,24},{24,20... | collective-permute-start | bytes 3145736 | tf_op jit(solution)/shard_map/ppermute | solution.py:626
  846.6 38.3 %collective-permute-start.62 = (bf16[512,1024]{1,0:T(8,128)(2,1)}, bf16[512,1024]{1,0:T(8,128)(2,1)}, u32[]{:S(2)}, u32[]{:S(2)}) collective-permute-start(bf16[512,1024]{1,0:T(8,128)(2,1)} %add_convert_fusion.13), channel_id=1, source_target_pairs={{4,0},{8,12},{5,1},{9,13},{6,2},{10,14},{7,3},{11,15},{20,16},{24,... | collective-permute-start | bytes 3145736 | tf_op jit(solution)/shard_map/ppermute | solution.py:626
  849.6 37.6 %collective-permute-start.59 = (bf16[512,1024]{1,0:T(8,128)(2,1)S(1)}, bf16[512,1024]{1,0:T(8,128)(2,1)}, u32[]{:S(2)}, u32[]{:S(2)}) collective-permute-start(bf16[512,1024]{1,0:T(8,128)(2,1)S(1)} %copy-done.86), channel_id=1, source_target_pairs={{0,16},{1,17},{2,18},{3,19},{4,20},{5,21},{6,22},{7,23},{8,24},{9,... | collective-permute-start | bytes 3145736 | tf_op jit(solution)/shard_map/ppermute | solution.py:979
  892.5 64.9 %all-to-all-start.27 = ((bf16[4,512,512]{2,1,0:T(8,128)(2,1)}), bf16[4,512,512]{2,1,0:T(8,128)(2,1)}, u32[]{:S(2)}, u32[]{:S(2)}) async-start(bf16[4,512,512]{2,1,0:T(8,128)(2,1)} %all-to-all-done.26), calls=%async_computation.27 | async-start | bytes 4194304 | tf_op jit(solution)/shard_map/all_to_all | solution.py:580
  897.0 55.3 %collective-permute-start.70 = (bf16[4,512,256]{2,1,0:T(8,128)(2,1)}, bf16[4,512,256]{2,1,0:T(8,128)(2,1)S(1)}, u32[]{:S(2)}, u32[]{:S(2)}) collective-permute-start(bf16[4,512,256]{2,1,0:T(8,128)(2,1)} %all-to-all-done.18), channel_id=1, source_target_pairs={{0,4},{12,8},{1,5},{13,9},{2,6},{14,10},{3,7},{15,11},{16,20},{28,... | collective-permute-start | bytes 3145736 | tf_op jit(solution)/shard_map/ppermute | solution.py:626
  900.4 53.4 %collective-permute-start.69 = (bf16[4,512,256]{2,1,0:T(8,128)(2,1)}, bf16[4,512,256]{2,1,0:T(8,128)(2,1)S(1)}, u32[]{:S(2)}, u32[]{:S(2)}) collective-permute-start(bf16[4,512,256]{2,1,0:T(8,128)(2,1)} %add_convert_fusion.10), channel_id=1, source_target_pairs={{4,8},{8,4},{5,9},{9,5},{6,10},{10,6},{7,11},{11,7},{20,24},{24,20... | collective-permute-start | bytes 3145736 | tf_op jit(solution)/shard_map/ppermute | solution.py:626
  901.1 55.2 %collective-permute-start.68 = (bf16[512,1024]{1,0:T(8,128)(2,1)}, bf16[512,1024]{1,0:T(8,128)(2,1)S(1)}, u32[]{:S(2)}, u32[]{:S(2)}) collective-permute-start(bf16[512,1024]{1,0:T(8,128)(2,1)} %add_convert_fusion.11), channel_id=1, source_target_pairs={{4,0},{8,12},{5,1},{9,13},{6,2},{10,14},{7,3},{11,15},{20,16},{24,... | collective-permute-start | bytes 3145736 | tf_op jit(solution)/shard_map/ppermute | solution.py:626
  902.5 54.9 %collective-permute-start.65 = (bf16[4,512,256]{2,1,0:T(8,128)(2,1)S(1)}, bf16[4,512,256]{2,1,0:T(8,128)(2,1)S(1)}, u32[]{:S(2)}, u32[]{:S(2)}) collective-permute-start(bf16[4,512,256]{2,1,0:T(8,128)(2,1)S(1)} %all-to-all-done.25.refs_1_), channel_id=1, source_target_pairs={{0,16},{1,17},{2,18},{3,19},{4,20},{5,21},{6,22},{7,23},{8,24},{9,... | collective-permute-start | bytes 3145736 | tf_op jit(solution)/shard_map/ppermute | solution.py:979
  907.7 49.7 %collective-permute-start.66 = (bf16[512,1024]{1,0:T(8,128)(2,1)}, bf16[512,1024]{1,0:T(8,128)(2,1)}, u32[]{:S(2)}, u32[]{:S(2)}) collective-permute-start(bf16[512,1024]{1,0:T(8,128)(2,1)} %broadcast_select_fusion.13), channel_id=1, source_target_pairs={{16,0},{17,1},{18,2},{19,3},{20,4},{21,5},{22,6},{23,7},{24,8},{25... | collective-permute-start | bytes 3145736 | tf_op jit(solution)/shard_map/ppermute | solution.py:979
  958.4 60.4 %all-to-all-start.28 = ((bf16[4,512,512]{2,1,0:T(8,128)(2,1)}), bf16[4,512,512]{2,1,0:T(8,128)(2,1)}, u32[]{:S(2)}, u32[]{:S(2)}) async-start(bf16[4,512,512]{2,1,0:T(8,128)(2,1)} %all-to-all-done.27), calls=%async_computation.28 | async-start | bytes 4194304 | tf_op jit(solution)/shard_map/all_to_all | solution.py:559
  962.8 59.5 %collective-permute-start.76 = (bf16[4,512,256]{2,1,0:T(8,128)(2,1)}, bf16[4,512,256]{2,1,0:T(8,128)(2,1)}, u32[]{:S(2)}, u32[]{:S(2)}) collective-permute-start(bf16[4,512,256]{2,1,0:T(8,128)(2,1)} %copy-done.88), channel_id=1, source_target_pairs={{0,4},{12,8},{1,5},{13,9},{2,6},{14,10},{3,7},{15,11},{16,20},{28,... | collective-permute-start | bytes 3145736 | tf_op jit(solution)/shard_map/ppermute | solution.py:626
  980.7 44.4 %collective-permute-start.75 = (bf16[4,512,256]{2,1,0:T(8,128)(2,1)S(1)}, bf16[4,512,256]{2,1,0:T(8,128)(2,1)}, u32[]{:S(2)}, u32[]{:S(2)}) collective-permute-start(bf16[4,512,256]{2,1,0:T(8,128)(2,1)S(1)} %add_convert_fusion.8), channel_id=1, source_target_pairs={{4,8},{8,4},{5,9},{9,5},{6,10},{10,6},{7,11},{11,7},{20,24},{24,20... | collective-permute-start | bytes 3145736 | tf_op jit(solution)/shard_map/ppermute | solution.py:626
  982.3 45.3 %collective-permute-start.74 = (bf16[4,512,256]{2,1,0:T(8,128)(2,1)}, bf16[4,512,256]{2,1,0:T(8,128)(2,1)}, u32[]{:S(2)}, u32[]{:S(2)}) collective-permute-start(bf16[4,512,256]{2,1,0:T(8,128)(2,1)} %add_convert_fusion.9), channel_id=1, source_target_pairs={{4,0},{8,12},{5,1},{9,13},{6,2},{10,14},{7,3},{11,15},{20,16},{24,... | collective-permute-start | bytes 3145736 | tf_op jit(solution)/shard_map/ppermute | solution.py:626
  983.6 28.5 %collective-permute-start.73 = (f32[2,28099]{1,0:T(2,128)S(1)}, f32[2,28099]{1,0:T(2,128)S(1)}, u32[]{:S(2)}, u32[]{:S(2)}) collective-permute-start(f32[2,28099]{1,0:T(2,128)S(1)} %copy-done.108), channel_id=1, source_target_pairs={{0,4},{4,0},{8,12},{12,8},{1,5},{5,1},{9,13},{13,9},{2,6},{6,2},{1... | collective-permute-start | bytes 674384 | tf_op jit(solution)/shard_map/ppermute | solution.py:599
  986.7 48.7 %collective-permute-start.71 = (bf16[4,512,256]{2,1,0:T(8,128)(2,1)}, bf16[4,512,256]{2,1,0:T(8,128)(2,1)}, u32[]{:S(2)}, u32[]{:S(2)}) collective-permute-start(bf16[4,512,256]{2,1,0:T(8,128)(2,1)} %all-to-all-done.24.refs_5_), channel_id=1, source_target_pairs={{0,16},{1,17},{2,18},{3,19},{4,20},{5,21},{6,22},{7,23},{8,24},{9,... | collective-permute-start | bytes 3145736 | tf_op jit(solution)/shard_map/ppermute | solution.py:979
  1035.4 54.5 %collective-permute-start.81 = (bf16[4,512,256]{2,1,0:T(8,128)(2,1)}, bf16[4,512,256]{2,1,0:T(8,128)(2,1)}, u32[]{:S(2)}, u32[]{:S(2)}) collective-permute-start(bf16[4,512,256]{2,1,0:T(8,128)(2,1)} %add_convert_fusion.6), channel_id=1, source_target_pairs={{4,8},{8,4},{5,9},{9,5},{6,10},{10,6},{7,11},{11,7},{20,24},{24,20... | collective-permute-start | bytes 3145736 | tf_op jit(solution)/shard_map/ppermute | solution.py:626
  1037.1 55.6 %collective-permute-start.80 = (bf16[4,512,256]{2,1,0:T(8,128)(2,1)}, bf16[4,512,256]{2,1,0:T(8,128)(2,1)}, u32[]{:S(2)}, u32[]{:S(2)}) collective-permute-start(bf16[4,512,256]{2,1,0:T(8,128)(2,1)} %add_convert_fusion.7), channel_id=1, source_target_pairs={{4,0},{8,12},{5,1},{9,13},{6,2},{10,14},{7,3},{11,15},{20,16},{24,... | collective-permute-start | bytes 3145736 | tf_op jit(solution)/shard_map/ppermute | solution.py:626
  1038.3 56.7 %collective-permute-start.82 = (bf16[4,512,296]{1,2,0:T(8,128)(2,1)}, bf16[4,512,296]{1,2,0:T(8,128)(2,1)}, u32[]{:S(2)}, u32[]{:S(2)}) collective-permute-start(bf16[4,512,296]{1,2,0:T(8,128)(2,1)} %all-to-all-done.20), channel_id=1, source_target_pairs={{0,4},{12,8},{1,5},{13,9},{2,6},{14,10},{3,7},{15,11},{16,20},{28,... | collective-permute-start | bytes 3637256 | tf_op jit(solution)/shard_map/ppermute | solution.py:626
  1044.3 29.9 %collective-permute-start.79 = (f32[2,28099]{1,0:T(2,128)S(1)}, f32[2,28099]{1,0:T(2,128)S(1)}, u32[]{:S(2)}, u32[]{:S(2)}) collective-permute-start(f32[2,28099]{1,0:T(2,128)S(1)} %add.479), channel_id=1, source_target_pairs={{0,8},{4,12},{8,0},{12,4},{1,9},{5,13},{9,1},{13,5},{2,10},{6,14},... | collective-permute-start | bytes 674384 | tf_op jit(solution)/shard_map/ppermute | solution.py:599
  1044.4 56.6 %collective-permute-start.77 = (bf16[4,512,256]{2,1,0:T(8,128)(2,1)S(1)}, bf16[4,512,256]{2,1,0:T(8,128)(2,1)}, u32[]{:S(2)}, u32[]{:S(2)}) collective-permute-start(bf16[4,512,256]{2,1,0:T(8,128)(2,1)S(1)} %all-to-all-done.23.refs_1_), channel_id=1, source_target_pairs={{0,16},{1,17},{2,18},{3,19},{4,20},{5,21},{6,22},{7,23},{8,24},{9,... | collective-permute-start | bytes 3145736 | tf_op jit(solution)/shard_map/ppermute | solution.py:979
  1106.6 29.2 %collective-permute-start.83 = (bf16[4,512,296]{1,2,0:T(8,128)(2,1)}, bf16[4,512,296]{1,2,0:T(8,128)(2,1)}, u32[]{:S(2)}, u32[]{:S(2)}) collective-permute-start(bf16[4,512,296]{1,2,0:T(8,128)(2,1)} %all-to-all-done.22), channel_id=1, source_target_pairs={{0,16},{1,17},{2,18},{3,19},{4,20},{5,21},{6,22},{7,23},{8,24},{9,... | collective-permute-start | bytes 3637256 | tf_op jit(solution)/shard_map/ppermute | solution.py:979
  1107.9 27.9 %collective-permute-start.84 = (bf16[4,512,256]{2,1,0:T(8,128)(2,1)S(1)}, bf16[4,512,256]{2,1,0:T(8,128)(2,1)}, u32[]{:S(2)}, u32[]{:S(2)}) collective-permute-start(bf16[4,512,256]{2,1,0:T(8,128)(2,1)S(1)} %copy-done.11), channel_id=1, source_target_pairs={{16,0},{17,1},{18,2},{19,3},{20,4},{21,5},{22,6},{23,7},{24,8},{25... | collective-permute-start | bytes 3145736 | tf_op jit(solution)/shard_map/ppermute | solution.py:979
  1138.3 36.6 %collective-permute-start.88 = (bf16[4,512,296]{1,2,0:T(8,128)(2,1)}, bf16[4,512,296]{1,2,0:T(8,128)(2,1)}, u32[]{:S(2)}, u32[]{:S(2)}) collective-permute-start(bf16[4,512,296]{1,2,0:T(8,128)(2,1)} %copy.265), channel_id=1, source_target_pairs={{4,0},{8,12},{5,1},{9,13},{6,2},{10,14},{7,3},{11,15},{20,16},{24,... | collective-permute-start | bytes 3637256 | tf_op jit(solution)/shard_map/ppermute | solution.py:626
  1139.6 40.6 %collective-permute-start.87 = (bf16[4,512,256]{2,1,0:T(8,128)(2,1)S(1)}, bf16[4,512,256]{2,1,0:T(8,128)(2,1)}, u32[]{:S(2)}, u32[]{:S(2)}) collective-permute-start(bf16[4,512,256]{2,1,0:T(8,128)(2,1)S(1)} %copy-done.13), channel_id=1, source_target_pairs={{16,0},{17,1},{18,2},{19,3},{20,4},{21,5},{22,6},{23,7},{24,8},{25... | collective-permute-start | bytes 3145736 | tf_op jit(solution)/shard_map/ppermute | solution.py:979
  1211.7 29.7 %collective-permute-start.90 = (bf16[2,128,2048]{2,1,0:T(8,128)(2,1)}, bf16[2,128,2048]{2,1,0:T(8,128)(2,1)}, u32[]{:S(2)}, u32[]{:S(2)}) collective-permute-start(bf16[2,128,2048]{2,1,0:T(8,128)(2,1)} %fusion.10), channel_id=1, source_target_pairs={{0,16},{16,0},{1,17},{17,1},{2,18},{18,2},{3,19},{19,3},{4,20},{20... | collective-permute-start | bytes 3145736 | tf_op jit(solution)/shard_map/ppermute | solution.py:551
  (197 other events, 2806.1 us)

commit v6 on v5

--- a/solution.py
+++ b/solution.py
@@ -476,7 +476,7 @@
             def _():
                 src = refs[plan[k][layer]]
                 pltpu.make_async_copy(
-                    src.at[:, :, pl.ds(0, size)], pieces.at[k % 2], in_sem.at[k % 2]
+                    src.at[:, pl.ds(0, share)], pieces.at[k % 2], in_sem.at[k % 2]
                 ).start()
 
     def send(step, first, count):
@@ -522,7 +522,7 @@
 
 
 def place_in(ids, arrays, plan, small, rows_of_small, before, shape, size):
-    places, share, _ = arrays[0].shape
+    places, share = arrays[0].shape[0], shape[1]
     any_space = pl.BlockSpec(memory_space=pl.ANY)
     return pl.pallas_call(
         functools.partial(
@@ -607,7 +607,8 @@
         self.pairs.append([(half - 1, half), (half, half - 1)])
         self.inward = half
         self.pairs += [[(j + 1, j), (s - 2 - j, s - 1 - j)] for j in reversed(range(half - 1))]
-        self.values, self.phase, self.moving = [], [], []
+        self.values, self.phase = [], []
+        self.came, self.moving, self.fresh = [], [], []
 
     def add(self, values):
         first = len(self.values)
@@ -617,13 +618,8 @@
 
     def begin(self):
         place = lax.axis_index("seq")
-        taken = set()
-        for k, step in enumerate(self.phase):
-            if step == len(self.pairs) or step in taken:
-                continue
-            taken.add(step)
-            v = self.values[k]
-            got = lax.ppermute(v, "seq", self.pairs[step])
+        for k, got in self.came:
+            step, v = self.phase[k] - 1, self.values[k]
             if step < self.inward:
                 v = (v.astype(F32) + got.astype(F32)).astype(BF16)
             else:
@@ -631,24 +627,37 @@
                     jnp.logical_or, [place == to for _, to in self.pairs[step]]
                 )
                 v = jnp.where(here, got, v)
-            self.moving.append((k, v))
+            self.fresh.append((k, v))
+        taken = set()
+        waiting = [k for k, _ in self.came]
+        for k, step in enumerate(self.phase):
+            if step == len(self.pairs) or step in taken or k in waiting:
+                continue
+            taken.add(step)
+            self.moving.append((k, lax.ppermute(self.values[k], "seq", self.pairs[step])))
             self.phase[k] = step + 1
 
     def end(self, work):
-        moved = [v for _, v in self.moving]
         still = [k for k, p in enumerate(self.phase) if p == 0]
-        work, moved, rest = lax.optimization_barrier(
-            (work, moved, [self.values[k] for k in still])
+        work, fresh, came, rest = lax.optimization_barrier(
+            (
+                work,
+                [v for _, v in self.fresh],
+                [v for _, v in self.moving],
+                [self.values[k] for k in still],
+            )
         )
-        for (k, _), v in zip(self.moving, moved):
+        for (k, _), v in zip(self.fresh, fresh):
             self.values[k] = v
         for k, v in zip(still, rest):
             self.values[k] = v
-        self.moving = []
+        self.came = [(k, v) for (k, _), v in zip(self.moving, came)]
+        self.moving, self.fresh = [], []
         return work
 
-    def done(self, ks):
-        return all(self.phase[k] == len(self.pairs) for k in ks)
+    def done(self, k):
+        busy = [j for j, _ in self.came + self.moving + self.fresh]
+        return self.phase[k] == len(self.pairs) and k not in busy
 
 
 def relay(total, local, reverse):
@@ -747,15 +756,6 @@
     def whole_slot(v):
         return joined(to_all(v.reshape(n * rows, share)))
 
-    pieces_x = [piece_x(m) for m in range(n)]
-    near_x0, far_x0 = fetch(pieces_x, 0)
-    part_h0 = in_group(exchange(quarters(at(inputs, c)[0])))
-    near_x0, part_h0 = tie((near_x0, part_h0))
-    far_x0 = [lax.ppermute(v, "section", [(0, 1)]) for v in near_x0]
-    all_h0 = whole_slot(part_h0)
-    pieces_z, _ = tie(([piece_z(m) for m in range(n)], part_h0))
-    near_z0, far_z0 = fetch(pieces_z, 0)
-
     pack = jnp.concatenate(
         [
             gain_in[0],
@@ -767,7 +767,17 @@
             conv_b[0],
         ]
     )
-    mine = to_all(pack)
+    mine, part_h0, pieces_x = tie(
+        (to_all(pack), exchange(quarters(at(inputs, c)[0])), [piece_x(m) for m in range(n)])
+    )
+    near_x0, far_x0 = fetch(pieces_x, 0)
+    part_h0 = in_group(part_h0)
+    near_x0, part_h0 = tie((near_x0, part_h0))
+    far_x0 = [lax.ppermute(v, "section", [(0, 1)]) for v in near_x0]
+    all_h0 = whole_slot(part_h0)
+    pieces_z, all_h0 = tie(([piece_z(m) for m in range(n)], all_h0))
+    near_z0, far_z0 = fetch(pieces_z, 0)
+
     theirs = swap_section(mine)
     small = []
     for full in (pick(mine, theirs), pick(theirs, mine)):
@@ -843,9 +853,11 @@
 
     normed_in0 = normalised(all_h0.astype(F32), small[0][0]).astype(BF16)
     px0 = project_x(normed_in0, 0)
-    px0, pieces_x1, pieces_z1, own_ct, wo_mine, own_len = tie(
-        (px0, pieces_x, pieces_z, at(cotangent, c)[0], w_out[0], at(lengths, c))
+    px0, near_z0, pieces_x1, pieces_z1, own_ct, wo_mine, own_len = tie(
+        (px0, near_z0, pieces_x, pieces_z, at(cotangent, c)[0], w_out[0], at(lengths, c))
     )
+    far_z0 = [lax.ppermute(v, "section", [(0, 1)]) for v in near_z0]
+    win[0] = (near_z0, far_z0, near_x0, far_x0)
     near_x1, far_x1 = fetch(pieces_x1, 1)
     wo_other = swap_section(wo_mine)
     wo = (pick(wo_mine, wo_other), pick(wo_other, wo_mine))
@@ -865,26 +877,27 @@
     fwd0 = scan(px0, 0)
     pz0 = project_z(normed_in0, 0)
     g0 = gate(pz0, fwd0[0][0])
-    stat0 = sum_of_shares(jnp.sum(g0 * g0, axis=1).reshape(n, rows)).reshape(-1)
+    stat0, near_x1, pieces_z1 = tie((jnp.sum(g0 * g0, axis=1), near_x1, pieces_z1))
+    near_z1, far_z1 = fetch(pieces_z1, 1)
+    stat0 = sum_of_shares(stat0.reshape(n, rows)).reshape(-1)
     r0 = lax.rsqrt(stat0 / INNER + EPS)
     normed0 = gated(pz0, fwd0[0][0], r0, 0)
     part_ct = in_group(exchange(quarters(own_ct)))
-    normed0, wo, near_x1, part_ct = tie((normed0, wo, near_x1, part_ct))
+    normed0, wo, part_ct = tie((normed0, wo, part_ct))
     far_x1 = [lax.ppermute(v, "section", [(1, 0)]) for v in near_x1]
     mixed0 = scatter_sum(jnp.dot(normed0, wo[0], preferred_element_type=F32).astype(BF16))
     out0 = valid * (h0.astype(F32) + mixed0)
     h1 = out0.astype(BF16)
 
+    h1, near_z1 = tie((h1, near_z1))
+    far_z1 = [lax.ppermute(v, "section", [(1, 0)]) for v in near_z1]
+    win[1] = (near_z1, far_z1, near_x1, far_x1)
     normed_in1 = gather_rows(normalised(h1.astype(F32), small[1][0]).astype(BF16))
-    normed_in1, far_x1, part_ct, pieces_z1 = tie((normed_in1, far_x1, part_ct, pieces_z1))
-    near_z1, far_z1 = fetch(pieces_z1, 1)
-    win[1] = (near_z1, far_z1, near_x1, far_x1)
+    normed_in1, far_x1, part_ct = tie((normed_in1, far_x1, part_ct))
     px1 = project_x(normed_in1, 1)
     all_ct = whole_slot(part_ct)
     fwd1 = scan(px1, 1)
-    fwd1, all_ct, near_z1 = tie((fwd1, all_ct, near_z1))
-    far_z1 = [lax.ppermute(v, "section", [(1, 0)]) for v in near_z1]
-    win[1] = (near_z1, far_z1, near_x1, far_x1)
+    fwd1, all_ct = tie((fwd1, all_ct))
     dout1 = own_rows(all_ct).astype(F32)
     dmixed1 = (all_valid * all_ct.astype(F32)).astype(BF16)
     dn1 = dot_cols(dmixed1, wo[1])
@@ -907,18 +920,26 @@
         size = v.shape[1] // 2
         return lax.dynamic_slice_in_dim(v, k * size, size, 1)
 
-    def half_of(parts, k):
+    def narrow_of(parts, k):
         return jnp.concatenate([cut_half(v, k) for v in parts], axis=1)
 
-    def away_in(normed_in, parts):
-        return swap_section(dot_rows(normed_in, half_of(parts, 1 - c)).astype(BF16))
-
-    def own_in_pieces(normed_in, parts, away):
-        own = half_of(parts, c)
+    def away_in(normed_in, part, narrow=()):
+        away = [dot_rows(normed_in, cut_half(part, 1 - c)).astype(BF16)]
+        if narrow:
+            away.append(dot_rows(narrow_of(narrow, 1 - c), normed_in).astype(BF16))
+        return [swap_section(v) for v in away]
+
+    def own_in_pieces(normed_in, part, away, narrow=()):
+        own = cut_half(part, c)
         result = []
-        for cols in (slice(0, part_width), slice(part_width, own.shape[1])):
-            total = dot_rows(normed_in, own[:, cols]) + away[:, cols].astype(F32)
+        for cols in (slice(0, part_width), slice(part_width, 2 * part_width)):
+            total = dot_rows(normed_in, own[:, cols]) + away[0][:, cols].astype(F32)
             result.append(total.astype(BF16).reshape(n, share, -1))
+        if narrow:
+            total = dot_rows(narrow_of(narrow, c), normed_in) + away[1].astype(F32)
+            rest = total.astype(BF16).reshape(-1, n, share).transpose(1, 0, 2)
+            rest = rest.reshape(n, -1, part_width)
+            result[1] = jnp.concatenate([result[1], rest], axis=1)
         return result
 
     def away_out(normed, dmixed):
@@ -937,7 +958,7 @@
         column = jnp.arange(GROUP)[None, :] // group
         own = jnp.where(column == f, jnp.concatenate([total] * n, axis=1), 0)
         full = lax.dynamic_update_slice(dxs, own.astype(BF16), (0, width))
-        return full, [dxs[:, :width], total, dxs[:, width + GROUP :]]
+        return full, (dxs[:, :width], [total, dxs[:, width + GROUP :]])
 
     def back_in(dz, full, layer):
         near_z, far_z, near_x, far_x = win[layer]
@@ -990,15 +1011,15 @@
     d1, mixed1 = sums.end((d1, mixed1))
 
     sums.begin()
-    away = away_in(normed_in1, [d1[0]])
+    away = away_in(normed_in1, d1[0])
     full1, xs1 = with_group(d1[1], d1[2])
     back1 = back_in(d1[0], full1, 1)
     back1, xs1, away, full1 = sums.end((back1, xs1, away, full1))
 
     sums.begin()
     dnin1 = scatter_sum(back1)
-    gz = own_in_pieces(normed_in1, [d1[0]], away)
-    away = away_in(normed_in1, xs1)
+    gz = own_in_pieces(normed_in1, d1[0], away)
+    away = away_in(normed_in1, *xs1)
     dnin1, gz, away = sums.end((dnin1, gz, away))
     gz1 = sums.add(gz)
 
@@ -1009,7 +1030,7 @@
     dmixed0 = gather_rows(dmixed0_own)
     along0 = to_all(jnp.sum(dmixed0_own.astype(F32) * mixed0, axis=-1)).reshape(-1)
     rc0 = scales(r0, (r0 * r0 / INNER) * along0)
-    gx = own_in_pieces(normed_in1, xs1, away)
+    gx = own_in_pieces(normed_in1, xs1[0], away, xs1[1])
     out1 = valid * (h1.astype(F32) + mixed1)
     grad1, dgin1, dmixed0, rc0, gx, out1 = sums.end((grad1, dgin1, dmixed0, rc0, gx, out1))
     gx1 = sums.add(gx)
@@ -1020,18 +1041,18 @@
     d0 = sums.end(d0)
 
     sums.begin()
-    away_z = away_in(normed_in0, [d0[0]])
+    away_z = away_in(normed_in0, d0[0])
     away_o = away_out(normed0, dmixed0)
     full0, xs0 = with_group(d0[1], d0[2])
-    gz = own_in_pieces(normed_in0, [d0[0]], away_z)
+    gz = own_in_pieces(normed_in0, d0[0], away_z)
     go = own_out_pieces(normed0, dmixed0, away_o)
     full0, xs0, gz, go = sums.end((full0, xs0, gz, go))
     go0 = sums.add(go)
 
     sums.begin()
-    away = away_in(normed_in0, xs0)
+    away = away_in(normed_in0, *xs0)
     gz = [exchange(v) for v in gz]
-    gx = own_in_pieces(normed_in0, xs0, away)
+    gx = own_in_pieces(normed_in0, xs0[0], away, xs0[1])
     gz, gx, full0 = sums.end((gz, gx, full0))
     gz0 = sums.add(gz)
 
@@ -1058,8 +1079,7 @@
     exchanged = set()
     while order:
         sums.begin()
-        moving = [k for k, _ in sums.moving]
-        ready = [e for e in order if e[0] not in moving and sums.done([e[0]])]
+        ready = [e for e in order if sums.done(e[0])]
         turn = [e for e in ready if e[1:] == (1, "in") and e[0] not in exchanged][:2]
         if back_steps:
             back = back_steps.pop(0)(back)
@@ -1103,8 +1123,8 @@
     def both_halves(a, b):
         return jnp.stack([pick(a, b), pick(b, a)], axis=1)
 
-    narrow = [pick(side[0][3], side[1][3])[:, :, part_width:] for side in held]
-    narrow = both_halves(*[v.astype(F32).transpose(0, 2, 1) for v in narrow])
+    narrow = [pick(side[0][3], side[1][3])[:, share:] for side in held]
+    narrow = both_halves(*[v.astype(F32).reshape(n, -1, share) for v in narrow])
     small_in = jnp.concatenate(
         [
             narrow[:, :, : group // 2].reshape(GROUP, share),

time: 1260 us -> 1200 us (0.952)
  local copies, waits for them, and re-layouts: 148 us -> 100 us
  other arithmetic: 177 us -> 149 us
  starting transfers between devices: 333 us -> 358 us
    optimization_barrier x15 -> x3, local copies, waits for them, and re-layouts: 36.1 us -> 6.76 us  [the longest x2 4.7 us: end(): lax.optimization_barrier((work, [v for _, v in self.fresh], [v for _, v i...]
    ppermute x2, waiting for transfers between devices: 52.8 us -> 24.7 us  [move_seq(): return lax.ppermute(v, 'seq', [(k, k ^ m) for k in range(s)])]
    ppermute x10 -> x12, starting transfers between devices: 20.4 us -> 39.4 us  [swap_section(): return lax.ppermute(v, 'section', [(0, 1), (1, 0)])]
    ppermute x40, starting transfers between devices: 105 us -> 121 us  [the longest x36 116 us: begin(): lax.ppermute(self.values[k], 'seq', self.pairs[step])]
    ppermute x6 -> x0, local copies, waits for them, and re-layouts: 15.1 us -> none  [begin(): got = lax.ppermute(v, 'seq', self.pairs[step])]
    unnamed x291 -> x262, local copies, waits for them, and re-layouts: 30.3 us -> 35.8 us
    dot_general x18 -> x22, matrix products: 62 us -> 66.8 us  [dot_rows(): lax.dot_general(a, b, (((0,), (0,)), ((), ())), preferred_element_type=F32)]
  transfers between devices with their start and end apart: 119 -> 121, of which waited for: 35 -> 41; matrix products, arithmetic and copies ran while one was open for 23% -> 20% of each run, Pallas kernels for 10% -> 11%
where the time goes in v6:
time: 1200 us; the launch traced here: 1190 us
  starting transfers between devices  358 us (30%)
  waiting for transfers between devices  341 us (28%)
  other arithmetic  149 us (12%)
  Pallas kernels  134 us (11%)
  local copies, waits for them, and re-layouts  100 us (8%)
  matrix products  86.7 us (7%)
  blocking collectives  15.5 us (1%)
    ppermute x36, waiting for transfers between devices, begin(): lax.ppermute(self.values[k], 'seq', self.pairs[step])  155 us
    ppermute x36, starting transfers between devices, begin(): lax.ppermute(self.values[k], 'seq', self.pairs[step])  116 us
    all_to_all x25, starting transfers between devices, exchange(): return lax.all_to_all(v, 'fsdp', 0, 0, tiled=True)  103 us
    all_to_all x25, waiting for transfers between devices, exchange(): return lax.all_to_all(v, 'fsdp', 0, 0, tiled=True)  90.6 us
    dot_general x22, matrix products, dot_rows(): lax.dot_general(a, b, (((0,), (0,)), ((), ())), preferred_element_type=F32)  66.8 us
    convert_element_type x24, other arithmetic, begin(): v = (v.astype(F32) + got.astype(F32)).astype(BF16)  61.4 us
    pallas_call x2, Pallas kernels, run_backward(): pl.pallas_call(backward_kernel, grid=(count,), in_specs=[block(width), bl...  40.6 us
    ppermute x12, starting transfers between devices, swap_section(): return lax.ppermute(v, 'section', [(0, 1), (1, 0)])  39.4 us
  transfers between devices with their start and end apart: 121, of which 41 were waited for; matrix products, arithmetic and copies ran while one was open for 20% of the time, Pallas kernels for 11%

profile of v6, /device:TPU:1, one launch (start us, length us, event | category | flops | bytes accessed | tf_op | source)
XLA Modules:
  0.0 1189.1 jit_solution(1210332453287044038)
XLA Ops:
  12.4 6.5 dynamic-slice_bitcast_fusion
  38.1 4.6 all-to-all-start.2
  44.6 6.2 collective-permute-start.3
  57.1 4.5 all-to-all-start.3
  66.9 16.1 %all-to-all-done.3 = bf16[4,512,512]{2,1,0:T(8,128)(2,1)} async-done(((bf16[4,512,512]{2,1,0:T(8,128)(2,1)}), bf16[4,512,512]{2,1,0:T(8,128)(2,1)}, u32[]{:S(2)}, u32[]{:S(2)}) %all-to-all-start.3) | async-done | bytes 2097184 | tf_op jit(solution)/shard_map/all_to_all | solution.py:559
  86.6 4.9 collective-permute-done.4.refs_4_.refs_12_
  98.8 8.7 project.4.proj
  107.5 26.1 %collective-permute-start.19 = (bf16[1024,2048]{1,0:T(8,128)(2,1)}, bf16[1024,2048]{1,0:T(8,128)(2,1)}, u32[]{:S(2)}, u32[]{:S(2)}) collective-permute-start(bf16[1024,2048]{1,0:T(8,128)(2,1)} %bitcast.36), channel_id=1, source_target_pairs={{0,16},{16,0},{1,17},{17,1},{2,18},{18,2},{3,19},{19,3},{4,20},{20... | collective-permute-start | bytes 12582920 | tf_op jit(solution)/shard_map/ppermute | solution.py:551
  157.2 10.7 scan_forward.2
  169.3 7.4 project.5.pz
  193.5 4.6 all-to-all-start.6
  201.0 5.8 broadcast_select_fusion
  207.4 6.2 convolution_convert_fusion.1
  213.6 4.5 all-to-all-start.7
  229.7 8.5 all-to-all-done.7
  242.0 7.4 collective-permute-done.20.refs_1_
  249.4 21.1 %collective-permute-done.22.refs_3_ = bf16[1024,512]{1,0:T(8,128)(2,1)} collective-permute-done((bf16[1024,512]{1,0:T(8,128)(2,1)}, bf16[1024,512]{1,0:T(8,128)(2,1)}, u32[]{:S(2)}, u32[]{:S(2)}) %collective-permute-start.22) | collective-permute-done | bytes 1048608 | tf_op jit(solution)/shard_map/ppermute | solution.py:751
  295.5 4.5 all-to-all-start.9
  305.5 7.7 project.6.proj
  313.3 10.6 scan_forward.3
  329.0 6.6 project.7.pz
  342.5 4.7 multiply_reduce_fusion.1
  375.0 4.5 all-to-all-start.11
  382.4 20.3 %scan_backward.2 = (bf16[512,1024]{1,0:T(8,128)(2,1)S(1)}, bf16[512,1296]{1,0:T(8,128)(2,1)S(1)}, f32[4,512,64]{2,1,0:T(8,128)S(1)}, f32[8,1024]{1,0:T(8,128)S(1...) custom-call(f32[512,1024]{1,0:T(8,128)} %project.7.pz, ...), custom_call_target="tpu_custom_call" | custom-call | tf_op jit(solution)/shard_map/scan_backward/pallas_call | solution.py:303
  431.2 10.4 project_back.2
  449.0 4.6 all-to-all-start.13
  468.9 9.7 all-to-all-done.13
  491.8 9.9 collective-permute-start.39
  503.3 4.5 all-to-all-start.14
  521.8 10.4 all-to-all-done.14
  544.3 5.3 fusion.132.dn
  549.6 20.4 %scan_backward.3 = (bf16[512,1024]{1,0:T(8,128)(2,1)S(1)}, bf16[512,1296]{1,0:T(8,128)(2,1)S(1)}, f32[4,512,64]{2,1,0:T(8,128)S(1)}, f32[8,1024]{1,0:T(8,128)S(1...) custom-call(f32[512,1024]{1,0:T(8,128)} %project.5.pz, ...), custom_call_target="tpu_custom_call" | custom-call | tf_op jit(solution)/shard_map/scan_backward/pallas_call | solution.py:303
  592.5 6.9 collective-permute-start.46
  629.1 5.2 collective-permute-start.50
  662.8 6.9 all-to-all-done.18
  677.0 7.9 collective-permute-start.53
  696.5 10.8 project_back.3
  708.3 4.5 all-to-all-start.21
  717.8 7.8 collective-permute-start.57
  757.6 10.9 all-to-all-done.22.refs_1_
  768.5 4.6 all-to-all-start.23
  779.2 22.9 %collective-permute-done.60 = f32[2,28099]{1,0:T(2,128)S(1)} collective-permute-done((f32[2,28099]{1,0:T(2,128)S(1)}, f32[2,28099]{1,0:T(2,128)S(1)}, u32[]{:S(2)}, u32[]{:S(2)}) %collective-permute-start.60) | collective-permute-done | bytes 224824 | tf_op jit(solution)/shard_map/ppermute | solution.py:594
  802.1 5.5 collective-permute-start.63
  819.2 8.4 collective-permute-done.63
  827.7 15.5 %all_to_all.150.refs_5_ = bf16[4,512,256]{2,1,0:T(8,128)(2,1)} all-to-all(bf16[4,512,256]{2,1,0:T(8,128)(2,1)} %broadcast_select_fusion.10), channel_id=1, replica_groups=mesh['section'=2,'seq'=4,'fsdp'=4] {'fsdp'}, dimensions={0} | all-to-all | bytes 2097152 | tf_op jit(solution)/shard_map/all_to_all | solution.py:559
  843.2 4.6 all-to-all-start.25
  852.2 8.9 collective-permute-start.68
  868.0 32.5 %collective-permute-done.68 = bf16[4,512,256]{2,1,0:T(8,128)(2,1)} collective-permute-done((bf16[4,512,256]{2,1,0:T(8,128)(2,1)}, bf16[4,512,256]{2,1,0:T(8,128)(2,1)}, u32[]{:S(2)}, u32[]{:S(2)}) %collective-permute-start.68) | collective-permute-done | bytes 1048608 | tf_op jit(solution)/shard_map/ppermute | solution.py:637
  900.5 9.4 collective-permute-done.66
  910.0 4.5 all-to-all-start.27
  918.7 14.2 %collective-permute-start.73 = (bf16[4,512,256]{2,1,0:T(8,128)(2,1)}, bf16[4,512,256]{2,1,0:T(8,128)(2,1)}, u32[]{:S(2)}, u32[]{:S(2)}) collective-permute-start(bf16[4,512,256]{2,1,0:T(8,128)(2,1)} %all-to-all-done.19), channel_id=1, source_target_pairs={{0,4},{12,8},{1,5},{13,9},{2,6},{14,10},{3,7},{15,11},{16,20},{28,... | collective-permute-start | bytes 3145736 | tf_op jit(solution)/shard_map/ppermute | solution.py:637
  932.9 5.9 all-to-all-done.27
  950.2 7.0 collective-permute-done.70
  962.3 6.2 collective-permute-start.78
  972.7 4.6 collective-permute-start.75
  989.5 17.7 %collective-permute-done.75 = f32[2,28099]{1,0:T(2,128)} collective-permute-done((f32[2,28099]{1,0:T(2,128)S(1)}, f32[2,28099]{1,0:T(2,128)}, u32[]{:S(2)}, u32[]{:S(2)}) %collective-permute-start.75) | collective-permute-done | bytes 224824 | tf_op jit(solution)/shard_map/ppermute | solution.py:599
  1009.8 6.1 collective-permute-start.80
  1023.3 19.4 %collective-permute-done.81 = bf16[4,512,256]{2,1,0:T(8,128)(2,1)S(1)} collective-permute-done((bf16[4,512,256]{2,1,0:T(8,128)(2,1)}, bf16[4,512,256]{2,1,0:T(8,128)(2,1)S(1)}, u32[]{:S(2)}, u32[]{:S(2)}) %collective-permute-start.81) | collective-permute-done | bytes 1048608 | tf_op jit(solution)/shard_map/ppermute | solution.py:637
  1048.1 27.7 %collective-permute-done.84 = bf16[4,512,256]{2,1,0:T(8,128)(2,1)S(1)} collective-permute-done((bf16[4,512,256]{2,1,0:T(8,128)(2,1)S(1)}, bf16[4,512,256]{2,1,0:T(8,128)(2,1)S(1)}, u32[]{:S(2)}, u32[]{:S(2)}) %collective-permute-start.84) | collective-permute-done | bytes 1048608 | tf_op jit(solution)/shard_map/ppermute | solution.py:637
  1081.8 22.8 %collective-permute-done.87 = bf16[4,512,256]{2,1,0:T(8,128)(2,1)S(1)} collective-permute-done((bf16[4,512,256]{2,1,0:T(8,128)(2,1)S(1)}, bf16[4,512,256]{2,1,0:T(8,128)(2,1)S(1)}, u32[]{:S(2)}, u32[]{:S(2)}) %collective-permute-start.87) | collective-permute-done | bytes 1048608 | tf_op jit(solution)/shard_map/ppermute | solution.py:637
  1111.8 23.8 %collective-permute-done.89 = bf16[4,592,256]{2,1,0:T(8,128)(2,1)} collective-permute-done((bf16[4,592,256]{2,1,0:T(8,128)(2,1)}, bf16[4,592,256]{2,1,0:T(8,128)(2,1)}, u32[]{:S(2)}, u32[]{:S(2)}) %collective-permute-start.89) | collective-permute-done | bytes 1212448 | tf_op jit(solution)/shard_map/ppermute | solution.py:637
  1145.2 4.7 bitcast_convert_fusion
  1161.7 10.0 place_in.2.refs_9_
  1171.8 10.5 place_in.3
  (718 shorter events, 538.7 us)
Async XLA Ops:
  61.6 29.9 %collective-permute-start.4 = (bf16[1296,512]{1,0:T(8,128)(2,1)S(1)}, bf16[1296,512]{1,0:T(8,128)(2,1)}, u32[]{:S(2)}, u32[]{:S(2)}) collective-permute-start(bf16[1296,512]{1,0:T(8,128)(2,1)S(1)} %get-tuple-element.349.refs_0_.refs_4_), channel_id=1, source_target_pairs={{0,16},{1,17},{2,18},{3,19},{4,20},{5,21},{6,22},{7,23},{8,24},{9,... | collective-permute-start | bytes 3981320 | tf_op jit(solution)/shard_map/ppermute | solution.py:776
  62.9 31.2 %collective-permute-start.5 = (bf16[1296,512]{1,0:T(8,128)(2,1)}, bf16[1296,512]{1,0:T(8,128)(2,1)}, u32[]{:S(2)}, u32[]{:S(2)}) collective-permute-start(bf16[1296,512]{1,0:T(8,128)(2,1)} %collective-permute-done.refs_1_.refs_5_), channel_id=1, source_target_pairs={{0,16},{1,17},{2,18},{3,19},{4,20},{5,21},{6,22},{7,23},{8,24},{9,... | collective-permute-start | bytes 3981320 | tf_op jit(solution)/shard_map/ppermute | solution.py:776
  64.2 33.9 %collective-permute-start.6 = (bf16[1296,512]{1,0:T(8,128)(2,1)}, bf16[1296,512]{1,0:T(8,128)(2,1)}, u32[]{:S(2)}, u32[]{:S(2)}) collective-permute-start(bf16[1296,512]{1,0:T(8,128)(2,1)} %collective-permute-done.1.refs_2_.refs_6_), channel_id=1, source_target_pairs={{0,16},{1,17},{2,18},{3,19},{4,20},{5,21},{6,22},{7,23},{8,24},{9,... | collective-permute-start | bytes 3981320 | tf_op jit(solution)/shard_map/ppermute | solution.py:776
  65.5 33.3 %collective-permute-start.7 = (bf16[1296,512]{1,0:T(8,128)(2,1)}, bf16[1296,512]{1,0:T(8,128)(2,1)}, u32[]{:S(2)}, u32[]{:S(2)}) collective-permute-start(bf16[1296,512]{1,0:T(8,128)(2,1)} %collective-permute-done.2.refs_3_.refs_7_), channel_id=1, source_target_pairs={{0,16},{1,17},{2,18},{3,19},{4,20},{5,21},{6,22},{7,23},{8,24},{9,... | collective-permute-start | bytes 3981320 | tf_op jit(solution)/shard_map/ppermute | solution.py:776
  107.5 93.5 %collective-permute-start.19 = (bf16[1024,2048]{1,0:T(8,128)(2,1)}, bf16[1024,2048]{1,0:T(8,128)(2,1)}, u32[]{:S(2)}, u32[]{:S(2)}) collective-permute-start(bf16[1024,2048]{1,0:T(8,128)(2,1)} %bitcast.36), channel_id=1, source_target_pairs={{0,16},{16,0},{1,17},{17,1},{2,18},{18,2},{3,19},{19,3},{4,20},{20... | collective-permute-start | bytes 12582920 | tf_op jit(solution)/shard_map/ppermute | solution.py:551
  139.1 30.2 %collective-permute-start.14 = (bf16[1024,512]{1,0:T(8,128)(2,1)}, bf16[1024,512]{1,0:T(8,128)(2,1)}, u32[]{:S(2)}, u32[]{:S(2)}) collective-permute-start(bf16[1024,512]{1,0:T(8,128)(2,1)} %collective-permute-done.10.refs_3_), channel_id=1, source_target_pairs={{0,16},{1,17},{2,18},{3,19},{4,20},{5,21},{6,22},{7,23},{8,24},{9,... | collective-permute-start | bytes 3145736 | tf_op jit(solution)/shard_map/ppermute | solution.py:859
  144.3 35.9 %collective-permute-start.16 = (bf16[1296,512]{1,0:T(8,128)(2,1)}, bf16[1296,512]{1,0:T(8,128)(2,1)}, u32[]{:S(2)}, u32[]{:S(2)}) collective-permute-start(bf16[1296,512]{1,0:T(8,128)(2,1)} %get-tuple-element.332), channel_id=1, source_target_pairs={{16,17},{17,16},{18,19},{19,18},{20,21},{21,20},{22,23},{23,22},{2... | collective-permute-start | bytes 3981320 | tf_op jit(solution)/shard_map/ppermute | solution.py:751
  147.3 37.3 %collective-permute-start.17 = (bf16[1296,512]{1,0:T(8,128)(2,1)}, bf16[1296,512]{1,0:T(8,128)(2,1)}, u32[]{:S(2)}, u32[]{:S(2)}) collective-permute-start(bf16[1296,512]{1,0:T(8,128)(2,1)} %get-tuple-element.333), channel_id=1, source_target_pairs={{16,18},{17,19},{18,16},{19,17},{20,22},{21,23},{22,20},{23,21},{2... | collective-permute-start | bytes 3981320 | tf_op jit(solution)/shard_map/ppermute | solution.py:751
  149.5 35.0 %collective-permute-start.18 = (bf16[1296,512]{1,0:T(8,128)(2,1)}, bf16[1296,512]{1,0:T(8,128)(2,1)}, u32[]{:S(2)}, u32[]{:S(2)}) collective-permute-start(bf16[1296,512]{1,0:T(8,128)(2,1)} %get-tuple-element.334), channel_id=1, source_target_pairs={{16,19},{17,18},{18,17},{19,16},{20,23},{21,22},{22,21},{23,20},{2... | collective-permute-start | bytes 3981320 | tf_op jit(solution)/shard_map/ppermute | solution.py:751
  152.8 33.3 %all-to-all-start.5 = ((bf16[4,128,512]{1,2,0:T(8,128)(2,1)}), bf16[4,128,512]{1,2,0:T(8,128)(2,1)}, u32[]{:S(2)}, u32[]{:S(2)}) async-start(bf16[4,128,512]{1,2,0:T(8,128)(2,1)} %bitcast.44), calls=%async_computation.5 | async-start | bytes 1048576 | tf_op jit(solution)/shard_map/all_to_all | solution.py:559
  218.0 31.4 %collective-permute-start.20 = (bf16[1024,512]{1,0:T(8,128)(2,1)}, bf16[1024,512]{1,0:T(8,128)(2,1)}, u32[]{:S(2)}, u32[]{:S(2)}) collective-permute-start(bf16[1024,512]{1,0:T(8,128)(2,1)} %get-tuple-element.345), channel_id=1, source_target_pairs={{16,17},{17,16},{18,19},{19,18},{20,21},{21,20},{22,23},{23,22},{2... | collective-permute-start | bytes 3145736 | tf_op jit(solution)/shard_map/ppermute | solution.py:751
  221.3 28.1 %collective-permute-start.21 = (bf16[1024,512]{1,0:T(8,128)(2,1)}, bf16[1024,512]{1,0:T(8,128)(2,1)}, u32[]{:S(2)}, u32[]{:S(2)}) collective-permute-start(bf16[1024,512]{1,0:T(8,128)(2,1)} %get-tuple-element.346), channel_id=1, source_target_pairs={{16,18},{17,19},{18,16},{19,17},{20,22},{21,23},{22,20},{23,21},{2... | collective-permute-start | bytes 3145736 | tf_op jit(solution)/shard_map/ppermute | solution.py:751
  224.5 46.0 %collective-permute-start.22 = (bf16[1024,512]{1,0:T(8,128)(2,1)}, bf16[1024,512]{1,0:T(8,128)(2,1)}, u32[]{:S(2)}, u32[]{:S(2)}) collective-permute-start(bf16[1024,512]{1,0:T(8,128)(2,1)} %get-tuple-element.347), channel_id=1, source_target_pairs={{16,19},{17,18},{18,17},{19,16},{20,23},{21,22},{22,21},{23,20},{2... | collective-permute-start | bytes 3145736 | tf_op jit(solution)/shard_map/ppermute | solution.py:751
  295.5 41.1 %all-to-all-start.9 = ((bf16[4,512,512]{2,1,0:T(8,128)(2,1)}), bf16[4,512,512]{2,1,0:T(8,128)(2,1)}, u32[]{:S(2)}, u32[]{:S(2)}) async-start(bf16[4,512,512]{2,1,0:T(8,128)(2,1)} %broadcast_in_dim.55), calls=%async_computation.9 | async-start | bytes 4194304 | tf_op jit(solution)/shard_map/all_to_all | solution.py:559
  299.9 26.7 %collective-permute-start.27 = (bf16[1024,512]{1,0:T(8,128)(2,1)S(1)}, bf16[1024,512]{1,0:T(8,128)(2,1)S(1)}, u32[]{:S(2)}, u32[]{:S(2)}) collective-permute-start(bf16[1024,512]{1,0:T(8,128)(2,1)S(1)} %get-tuple-element.360.refs_0_), channel_id=1, source_target_pairs={{16,0},{17,1},{18,2},{19,3},{20,4},{21,5},{22,6},{23,7},{24,8},{25... | collective-permute-start | bytes 3145736 | tf_op jit(solution)/shard_map/ppermute | solution.py:893
  375.0 29.7 %all-to-all-start.11 = ((bf16[4,128,2048]{2,1,0:T(8,128)(2,1)}), bf16[4,128,2048]{2,1,0:T(8,128)(2,1)}, u32[]{:S(2)}, u32[]{:S(2)}) async-start(bf16[4,128,2048]{2,1,0:T(8,128)(2,1)} %bitcast.258), calls=%async_computation.11 | async-start | bytes 4194304 | tf_op jit(solution)/shard_map/all_to_all | solution.py:559
  379.4 28.3 %collective-permute-start.32 = (bf16[512,1024]{1,0:T(8,128)(2,1)}, bf16[512,1024]{1,0:T(8,128)(2,1)}, u32[]{:S(2)}, u32[]{:S(2)}) collective-permute-start(bf16[512,1024]{1,0:T(8,128)(2,1)} %add_convert_fusion.27), channel_id=1, source_target_pairs={{0,4},{12,8},{1,5},{13,9},{2,6},{14,10},{3,7},{15,11},{16,20},{28,... | collective-permute-start | bytes 3145736 | tf_op jit(solution)/shard_map/ppermute | solution.py:637
  412.0 32.0 %collective-permute-start.33 = (bf16[2048,512]{1,0:T(8,128)(2,1)}, bf16[2048,512]{1,0:T(8,128)(2,1)}, u32[]{:S(2)}, u32[]{:S(2)}) collective-permute-start(bf16[2048,512]{1,0:T(8,128)(2,1)} %convolution_convert_fusion.6), channel_id=1, source_target_pairs={{0,16},{16,0},{1,17},{17,1},{2,18},{18,2},{3,19},{19,3},{4,20},{20... | collective-permute-start | bytes 6291464 | tf_op jit(solution)/shard_map/ppermute | solution.py:551
  448.2 32.7 %collective-permute-start.35 = (bf16[2048,512]{1,0:T(8,128)(2,1)}, bf16[2048,512]{1,0:T(8,128)(2,1)}, u32[]{:S(2)}, u32[]{:S(2)}) collective-permute-start(bf16[2048,512]{1,0:T(8,128)(2,1)} %convolution_convert_fusion.5), channel_id=1, source_target_pairs={{0,16},{16,0},{1,17},{17,1},{2,18},{18,2},{3,19},{19,3},{4,20},{20... | collective-permute-start | bytes 6291464 | tf_op jit(solution)/shard_map/ppermute | solution.py:551
  449.0 29.7 %all-to-all-start.13 = ((bf16[4,128,2048]{2,1,0:T(8,128)(2,1)}), bf16[4,128,2048]{2,1,0:T(8,128)(2,1)}, u32[]{:S(2)}, u32[]{:S(2)}) async-start(bf16[4,128,2048]{2,1,0:T(8,128)(2,1)} %bitcast.248), calls=%async_computation.13 | async-start | bytes 4194304 | tf_op jit(solution)/shard_map/all_to_all | solution.py:559
  490.1 28.5 %collective-permute-start.38 = (bf16[512,1024]{1,0:T(8,128)(2,1)}, bf16[512,1024]{1,0:T(8,128)(2,1)}, u32[]{:S(2)}, u32[]{:S(2)}) collective-permute-start(bf16[512,1024]{1,0:T(8,128)(2,1)} %add_convert_fusion.24), channel_id=1, source_target_pairs={{4,8},{8,4},{5,9},{9,5},{6,10},{10,6},{7,11},{11,7},{20,24},{24,20... | collective-permute-start | bytes 3145736 | tf_op jit(solution)/shard_map/ppermute | solution.py:637
  491.8 30.0 %collective-permute-start.39 = (bf16[4,512,256]{2,1,0:T(8,128)(2,1)}, bf16[4,512,256]{2,1,0:T(8,128)(2,1)}, u32[]{:S(2)}, u32[]{:S(2)}) collective-permute-start(bf16[4,512,256]{2,1,0:T(8,128)(2,1)} %bitcast.260), channel_id=1, source_target_pairs={{0,4},{12,8},{1,5},{13,9},{2,6},{14,10},{3,7},{15,11},{16,20},{28,... | collective-permute-start | bytes 3145736 | tf_op jit(solution)/shard_map/ppermute | solution.py:637
  503.3 28.9 %all-to-all-start.14 = ((bf16[4,128,2048]{2,1,0:T(8,128)(2,1)}), bf16[4,128,2048]{2,1,0:T(8,128)(2,1)}, u32[]{:S(2)}, u32[]{:S(2)}) async-start(bf16[4,128,2048]{2,1,0:T(8,128)(2,1)} %broadcast_in_dim.59), calls=%async_computation.14 | async-start | bytes 4194304 | tf_op jit(solution)/shard_map/all_to_all | solution.py:559
  532.1 44.2 %collective-permute-start.40 = (bf16[512,1024]{1,0:T(8,128)(2,1)}, bf16[512,1024]{1,0:T(8,128)(2,1)S(1)}, u32[]{:S(2)}, u32[]{:S(2)}) collective-permute-start(bf16[512,1024]{1,0:T(8,128)(2,1)} %add_convert_fusion.23), channel_id=1, source_target_pairs={{4,0},{8,12},{5,1},{9,13},{6,2},{10,14},{7,3},{11,15},{20,16},{24,... | collective-permute-start | bytes 3145736 | tf_op jit(solution)/shard_map/ppermute | solution.py:637
  533.7 42.7 %collective-permute-start.41 = (bf16[4,512,256]{2,1,0:T(8,128)(2,1)}, bf16[4,512,256]{2,1,0:T(8,128)(2,1)S(1)}, u32[]{:S(2)}, u32[]{:S(2)}) collective-permute-start(bf16[4,512,256]{2,1,0:T(8,128)(2,1)} %bitcast.59), channel_id=1, source_target_pairs={{0,4},{12,8},{1,5},{13,9},{2,6},{14,10},{3,7},{15,11},{16,20},{28,... | collective-permute-start | bytes 3145736 | tf_op jit(solution)/shard_map/ppermute | solution.py:637
  542.2 58.7 %collective-permute-start.43 = (bf16[512,2048]{1,0:T(8,128)(2,1)}, bf16[512,2048]{1,0:T(8,128)(2,1)}, u32[]{:S(2)}, u32[]{:S(2)}) collective-permute-start(bf16[512,2048]{1,0:T(8,128)(2,1)} %convolution_convert_fusion.3), channel_id=1, source_target_pairs={{0,16},{16,0},{1,17},{17,1},{2,18},{18,2},{3,19},{19,3},{4,20},{20... | collective-permute-start | bytes 6291464 | tf_op jit(solution)/shard_map/ppermute | solution.py:551
  579.0 29.4 %collective-permute-start.42 = (bf16[2048,512]{1,0:T(8,128)(2,1)}, bf16[2048,512]{1,0:T(8,128)(2,1)}, u32[]{:S(2)}, u32[]{:S(2)}) collective-permute-start(bf16[2048,512]{1,0:T(8,128)(2,1)} %convolution_convert_fusion.4), channel_id=1, source_target_pairs={{0,16},{16,0},{1,17},{17,1},{2,18},{18,2},{3,19},{19,3},{4,20},{20... | collective-permute-start | bytes 6291464 | tf_op jit(solution)/shard_map/ppermute | solution.py:551
  592.5 27.2 %collective-permute-start.46 = (bf16[4,512,256]{2,1,0:T(8,128)(2,1)}, bf16[4,512,256]{2,1,0:T(8,128)(2,1)}, u32[]{:S(2)}, u32[]{:S(2)}) collective-permute-start(bf16[4,512,256]{2,1,0:T(8,128)(2,1)} %bitcast.62), channel_id=1, source_target_pairs={{0,4},{12,8},{1,5},{13,9},{2,6},{14,10},{3,7},{15,11},{16,20},{28,... | collective-permute-start | bytes 3145736 | tf_op jit(solution)/shard_map/ppermute | solution.py:637
  622.3 34.2 %collective-permute-start.47 = (bf16[2048,512]{1,0:T(8,128)(2,1)}, bf16[2048,512]{1,0:T(8,128)(2,1)}, u32[]{:S(2)}, u32[]{:S(2)}) collective-permute-start(bf16[2048,512]{1,0:T(8,128)(2,1)} %convolution_convert_fusion.2), channel_id=1, source_target_pairs={{0,16},{16,0},{1,17},{17,1},{2,18},{18,2},{3,19},{19,3},{4,20},{20... | collective-permute-start | bytes 6291464 | tf_op jit(solution)/shard_map/ppermute | solution.py:551
  629.1 40.6 %collective-permute-start.50 = (bf16[4,592,256]{2,1,0:T(8,128)(2,1)}, bf16[4,592,256]{2,1,0:T(8,128)(2,1)}, u32[]{:S(2)}, u32[]{:S(2)}) collective-permute-start(bf16[4,592,256]{2,1,0:T(8,128)(2,1)} %pad_maximum_fusion.8), channel_id=1, source_target_pairs={{0,4},{12,8},{1,5},{13,9},{2,6},{14,10},{3,7},{15,11},{16,20},{28,... | collective-permute-start | bytes 3637256 | tf_op jit(solution)/shard_map/ppermute | solution.py:637
  674.0 33.3 %collective-permute-start.51 = (bf16[4,512,256]{2,1,0:T(8,128)(2,1)}, bf16[4,512,256]{2,1,0:T(8,128)(2,1)}, u32[]{:S(2)}, u32[]{:S(2)}) collective-permute-start(bf16[4,512,256]{2,1,0:T(8,128)(2,1)} %add_convert_fusion.17), channel_id=1, source_target_pairs={{4,0},{8,12},{5,1},{9,13},{6,2},{10,14},{7,3},{11,15},{20,16},{24,... | collective-permute-start | bytes 3145736 | tf_op jit(solution)/shard_map/ppermute | solution.py:637
  675.3 32.0 %collective-permute-start.52 = (bf16[4,512,256]{2,1,0:T(8,128)(2,1)}, bf16[4,512,256]{2,1,0:T(8,128)(2,1)}, u32[]{:S(2)}, u32[]{:S(2)}) collective-permute-start(bf16[4,512,256]{2,1,0:T(8,128)(2,1)} %add_convert_fusion.16), channel_id=1, source_target_pairs={{4,8},{8,4},{5,9},{9,5},{6,10},{10,6},{7,11},{11,7},{20,24},{24,20... | collective-permute-start | bytes 3145736 | tf_op jit(solution)/shard_map/ppermute | solution.py:637
  677.0 30.4 %collective-permute-start.53 = (bf16[512,1024]{1,0:T(8,128)(2,1)}, bf16[512,1024]{1,0:T(8,128)(2,1)}, u32[]{:S(2)}, u32[]{:S(2)}) collective-permute-start(bf16[512,1024]{1,0:T(8,128)(2,1)} %add_convert_fusion.20), channel_id=1, source_target_pairs={{0,4},{12,8},{1,5},{13,9},{2,6},{14,10},{3,7},{15,11},{16,20},{28,... | collective-permute-start | bytes 3145736 | tf_op jit(solution)/shard_map/ppermute | solution.py:637
  708.3 28.8 %all-to-all-start.21 = ((bf16[4,128,2048]{2,1,0:T(8,128)(2,1)}), bf16[4,128,2048]{2,1,0:T(8,128)(2,1)}, u32[]{:S(2)}, u32[]{:S(2)}) async-start(bf16[4,128,2048]{2,1,0:T(8,128)(2,1)} %bitcast.249), calls=%async_computation.21 | async-start | bytes 4194304 | tf_op jit(solution)/shard_map/all_to_all | solution.py:559
  714.8 36.3 %collective-permute-start.56 = (bf16[4,592,256]{2,1,0:T(8,128)(2,1)}, bf16[4,592,256]{2,1,0:T(8,128)(2,1)}, u32[]{:S(2)}, u32[]{:S(2)}) collective-permute-start(bf16[4,592,256]{2,1,0:T(8,128)(2,1)} %add_convert_fusion.3), channel_id=1, source_target_pairs={{4,8},{8,4},{5,9},{9,5},{6,10},{10,6},{7,11},{11,7},{20,24},{24,20... | collective-permute-start | bytes 3637256 | tf_op jit(solution)/shard_map/ppermute | solution.py:637
  716.5 34.5 %collective-permute-start.55 = (bf16[4,512,256]{2,1,0:T(8,128)(2,1)}, bf16[4,512,256]{2,1,0:T(8,128)(2,1)}, u32[]{:S(2)}, u32[]{:S(2)}) collective-permute-start(bf16[4,512,256]{2,1,0:T(8,128)(2,1)} %add_convert_fusion.15), channel_id=1, source_target_pairs={{4,0},{8,12},{5,1},{9,13},{6,2},{10,14},{7,3},{11,15},{20,16},{24,... | collective-permute-start | bytes 3145736 | tf_op jit(solution)/shard_map/ppermute | solution.py:637
  717.8 33.3 %collective-permute-start.57 = (bf16[512,1024]{1,0:T(8,128)(2,1)}, bf16[512,1024]{1,0:T(8,128)(2,1)}, u32[]{:S(2)}, u32[]{:S(2)}) collective-permute-start(bf16[512,1024]{1,0:T(8,128)(2,1)} %add_convert_fusion.19), channel_id=1, source_target_pairs={{0,4},{12,8},{1,5},{13,9},{2,6},{14,10},{3,7},{15,11},{16,20},{28,... | collective-permute-start | bytes 3145736 | tf_op jit(solution)/shard_map/ppermute | solution.py:637
  768.5 59.1 %all-to-all-start.23 = ((bf16[4,512,512]{2,1,0:T(8,128)(2,1)}), bf16[4,512,512]{2,1,0:T(8,128)(2,1)}, u32[]{:S(2)}, u32[]{:S(2)}) async-start(bf16[4,512,512]{2,1,0:T(8,128)(2,1)} %bitcast.228), calls=%async_computation.23 | async-start | bytes 4194304 | tf_op jit(solution)/shard_map/all_to_all | solution.py:559
  773.1 28.9 %collective-permute-start.60 = (f32[2,28099]{1,0:T(2,128)S(1)}, f32[2,28099]{1,0:T(2,128)S(1)}, u32[]{:S(2)}, u32[]{:S(2)}) collective-permute-start(f32[2,28099]{1,0:T(2,128)S(1)} %fusion.125), channel_id=1, source_target_pairs={{0,1},{1,0},{2,3},{3,2},{4,5},{5,4},{6,7},{7,6},{8,9},{9,8},{10,11... | collective-permute-start | bytes 674384 | tf_op jit(solution)/shard_map/ppermute | solution.py:594
  774.5 42.1 %collective-permute-start.58 = (bf16[512,1024]{1,0:T(8,128)(2,1)S(1)}, bf16[512,1024]{1,0:T(8,128)(2,1)S(1)}, u32[]{:S(2)}, u32[]{:S(2)}) collective-permute-start(bf16[512,1024]{1,0:T(8,128)(2,1)S(1)} %copy-done.76), channel_id=1, source_target_pairs={{0,16},{1,17},{2,18},{3,19},{4,20},{5,21},{6,22},{7,23},{8,24},{9,... | collective-permute-start | bytes 3145736 | tf_op jit(solution)/shard_map/ppermute | solution.py:1000
  775.8 40.8 %collective-permute-start.59 = (bf16[512,1024]{1,0:T(8,128)(2,1)}, bf16[512,1024]{1,0:T(8,128)(2,1)S(1)}, u32[]{:S(2)}, u32[]{:S(2)}) collective-permute-start(bf16[512,1024]{1,0:T(8,128)(2,1)} %broadcast_select_fusion.14), channel_id=1, source_target_pairs={{0,16},{1,17},{2,18},{3,19},{4,20},{5,21},{6,22},{7,23},{8,24},{9,... | collective-permute-start | bytes 3145736 | tf_op jit(solution)/shard_map/ppermute | solution.py:1000
  777.1 39.5 %collective-permute-start.61 = (bf16[4,512,256]{2,1,0:T(8,128)(2,1)}, bf16[4,512,256]{2,1,0:T(8,128)(2,1)S(1)}, u32[]{:S(2)}, u32[]{:S(2)}) collective-permute-start(bf16[4,512,256]{2,1,0:T(8,128)(2,1)} %add_convert_fusion.14), channel_id=1, source_target_pairs={{4,0},{8,12},{5,1},{9,13},{6,2},{10,14},{7,3},{11,15},{20,16},{24,... | collective-permute-start | bytes 3145736 | tf_op jit(solution)/shard_map/ppermute | solution.py:637
  778.4 38.2 %collective-permute-start.62 = (bf16[512,1024]{1,0:T(8,128)(2,1)S(1)}, bf16[512,1024]{1,0:T(8,128)(2,1)S(1)}, u32[]{:S(2)}, u32[]{:S(2)}) collective-permute-start(bf16[512,1024]{1,0:T(8,128)(2,1)S(1)} %copy-done.73), channel_id=1, source_target_pairs={{4,8},{8,4},{5,9},{9,5},{6,10},{10,6},{7,11},{11,7},{20,24},{24,20... | collective-permute-start | bytes 3145736 | tf_op jit(solution)/shard_map/ppermute | solution.py:637
  843.2 66.8 %all-to-all-start.25 = ((bf16[4,512,512]{2,1,0:T(8,128)(2,1)}), bf16[4,512,512]{2,1,0:T(8,128)(2,1)}, u32[]{:S(2)}, u32[]{:S(2)}) async-start(bf16[4,512,512]{2,1,0:T(8,128)(2,1)} %all-to-all-done.23), calls=%async_computation.25 | async-start | bytes 4194304 | tf_op jit(solution)/shard_map/all_to_all | solution.py:580
  847.8 62.1 %collective-permute-start.66 = (bf16[4,592,256]{2,1,0:T(8,128)(2,1)}, bf16[4,592,256]{2,1,0:T(8,128)(2,1)}, u32[]{:S(2)}, u32[]{:S(2)}) collective-permute-start(bf16[4,592,256]{2,1,0:T(8,128)(2,1)} %add_convert_fusion.2), channel_id=1, source_target_pairs={{4,0},{8,12},{5,1},{9,13},{6,2},{10,14},{7,3},{11,15},{20,16},{24,... | collective-permute-start | bytes 3637256 | tf_op jit(solution)/shard_map/ppermute | solution.py:637
  852.2 48.3 %collective-permute-start.68 = (bf16[4,512,256]{2,1,0:T(8,128)(2,1)}, bf16[4,512,256]{2,1,0:T(8,128)(2,1)}, u32[]{:S(2)}, u32[]{:S(2)}) collective-permute-start(bf16[4,512,256]{2,1,0:T(8,128)(2,1)} %all-to-all-done.18), channel_id=1, source_target_pairs={{0,4},{12,8},{1,5},{13,9},{2,6},{14,10},{3,7},{15,11},{16,20},{28,... | collective-permute-start | bytes 3145736 | tf_op jit(solution)/shard_map/ppermute | solution.py:637
  910.0 28.8 %all-to-all-start.27 = ((bf16[4,512,512]{2,1,0:T(8,128)(2,1)}), bf16[4,512,512]{2,1,0:T(8,128)(2,1)}, u32[]{:S(2)}, u32[]{:S(2)}) async-start(bf16[4,512,512]{2,1,0:T(8,128)(2,1)} %all-to-all-done.25), calls=%async_computation.27 | async-start | bytes 4194304 | tf_op jit(solution)/shard_map/all_to_all | solution.py:559
  914.4 47.8 %collective-permute-start.69 = (bf16[4,512,256]{2,1,0:T(8,128)(2,1)}, bf16[4,512,256]{2,1,0:T(8,128)(2,1)}, u32[]{:S(2)}, u32[]{:S(2)}) collective-permute-start(bf16[4,512,256]{2,1,0:T(8,128)(2,1)} %all_to_all.150.refs_5_), channel_id=1, source_target_pairs={{0,16},{1,17},{2,18},{3,19},{4,20},{5,21},{6,22},{7,23},{8,24},{9,... | collective-permute-start | bytes 3145736 | tf_op jit(solution)/shard_map/ppermute | solution.py:1000
  915.7 46.5 %collective-permute-start.71 = (bf16[512,1024]{1,0:T(8,128)(2,1)}, bf16[512,1024]{1,0:T(8,128)(2,1)}, u32[]{:S(2)}, u32[]{:S(2)}) collective-permute-start(bf16[512,1024]{1,0:T(8,128)(2,1)} %add_convert_fusion.11), channel_id=1, source_target_pairs={{4,0},{8,12},{5,1},{9,13},{6,2},{10,14},{7,3},{11,15},{20,16},{24,... | collective-permute-start | bytes 3145736 | tf_op jit(solution)/shard_map/ppermute | solution.py:637
  917.0 45.2 %collective-permute-start.72 = (bf16[4,512,256]{2,1,0:T(8,128)(2,1)}, bf16[4,512,256]{2,1,0:T(8,128)(2,1)}, u32[]{:S(2)}, u32[]{:S(2)}) collective-permute-start(bf16[4,512,256]{2,1,0:T(8,128)(2,1)} %add_convert_fusion.10), channel_id=1, source_target_pairs={{4,8},{8,4},{5,9},{9,5},{6,10},{10,6},{7,11},{11,7},{20,24},{24,20... | collective-permute-start | bytes 3145736 | tf_op jit(solution)/shard_map/ppermute | solution.py:637
  918.7 43.6 %collective-permute-start.73 = (bf16[4,512,256]{2,1,0:T(8,128)(2,1)}, bf16[4,512,256]{2,1,0:T(8,128)(2,1)}, u32[]{:S(2)}, u32[]{:S(2)}) collective-permute-start(bf16[4,512,256]{2,1,0:T(8,128)(2,1)} %all-to-all-done.19), channel_id=1, source_target_pairs={{0,4},{12,8},{1,5},{13,9},{2,6},{14,10},{3,7},{15,11},{16,20},{28,... | collective-permute-start | bytes 3145736 | tf_op jit(solution)/shard_map/ppermute | solution.py:637
  962.3 46.1 %collective-permute-start.78 = (bf16[4,592,256]{2,1,0:T(8,128)(2,1)}, bf16[4,592,256]{2,1,0:T(8,128)(2,1)}, u32[]{:S(2)}, u32[]{:S(2)}) collective-permute-start(bf16[4,592,256]{2,1,0:T(8,128)(2,1)} %copy-done.61), channel_id=1, source_target_pairs={{0,4},{12,8},{1,5},{13,9},{2,6},{14,10},{3,7},{15,11},{16,20},{28,... | collective-permute-start | bytes 3637256 | tf_op jit(solution)/shard_map/ppermute | solution.py:637
  968.5 39.8 %collective-permute-start.74 = (bf16[4,512,256]{2,1,0:T(8,128)(2,1)S(1)}, bf16[4,512,256]{2,1,0:T(8,128)(2,1)S(1)}, u32[]{:S(2)}, u32[]{:S(2)}) collective-permute-start(bf16[4,512,256]{2,1,0:T(8,128)(2,1)S(1)} %all-to-all-done.26.refs_1_), channel_id=1, source_target_pairs={{0,16},{1,17},{2,18},{3,19},{4,20},{5,21},{6,22},{7,23},{8,24},{9,... | collective-permute-start | bytes 3145736 | tf_op jit(solution)/shard_map/ppermute | solution.py:1000
  969.8 38.6 %collective-permute-start.76 = (bf16[512,1024]{1,0:T(8,128)(2,1)}, bf16[512,1024]{1,0:T(8,128)(2,1)}, u32[]{:S(2)}, u32[]{:S(2)}) collective-permute-start(bf16[512,1024]{1,0:T(8,128)(2,1)} %add_convert_fusion.9), channel_id=1, source_target_pairs={{4,0},{8,12},{5,1},{9,13},{6,2},{10,14},{7,3},{11,15},{20,16},{24,... | collective-permute-start | bytes 3145736 | tf_op jit(solution)/shard_map/ppermute | solution.py:637
  971.1 37.3 %collective-permute-start.77 = (bf16[4,512,256]{2,1,0:T(8,128)(2,1)}, bf16[4,512,256]{2,1,0:T(8,128)(2,1)}, u32[]{:S(2)}, u32[]{:S(2)}) collective-permute-start(bf16[4,512,256]{2,1,0:T(8,128)(2,1)} %add_convert_fusion.8), channel_id=1, source_target_pairs={{4,8},{8,4},{5,9},{9,5},{6,10},{10,6},{7,11},{11,7},{20,24},{24,20... | collective-permute-start | bytes 3145736 | tf_op jit(solution)/shard_map/ppermute | solution.py:637
  972.7 34.5 %collective-permute-start.75 = (f32[2,28099]{1,0:T(2,128)S(1)}, f32[2,28099]{1,0:T(2,128)}, u32[]{:S(2)}, u32[]{:S(2)}) collective-permute-start(f32[2,28099]{1,0:T(2,128)S(1)} %copy-done.119), channel_id=1, source_target_pairs={{0,8},{4,12},{8,0},{12,4},{1,9},{5,13},{9,1},{13,5},{2,10},{6,14},... | collective-permute-start | bytes 674384 | tf_op jit(solution)/shard_map/ppermute | solution.py:599
  977.3 31.0 %all-to-all-start.28 = ((bf16[4,592,256]{2,1,0:T(8,128)(2,1)}), bf16[4,592,256]{2,1,0:T(8,128)(2,1)}, u32[]{:S(2)}, u32[]{:S(2)}) async-start(bf16[4,592,256]{2,1,0:T(8,128)(2,1)} %broadcast_select_fusion.5), calls=%async_computation.28 | async-start | bytes 2424832 | tf_op jit(solution)/shard_map/all_to_all | solution.py:559
  1008.4 34.4 %collective-permute-start.79 = (bf16[4,592,256]{2,1,0:T(8,128)(2,1)}, bf16[4,592,256]{2,1,0:T(8,128)(2,1)S(1)}, u32[]{:S(2)}, u32[]{:S(2)}) collective-permute-start(bf16[4,592,256]{2,1,0:T(8,128)(2,1)} %all-to-all-done.28.refs_5_), channel_id=1, source_target_pairs={{0,16},{1,17},{2,18},{3,19},{4,20},{5,21},{6,22},{7,23},{8,24},{9,... | collective-permute-start | bytes 3637256 | tf_op jit(solution)/shard_map/ppermute | solution.py:1000
  1015.9 26.8 %collective-permute-start.81 = (bf16[4,512,256]{2,1,0:T(8,128)(2,1)}, bf16[4,512,256]{2,1,0:T(8,128)(2,1)S(1)}, u32[]{:S(2)}, u32[]{:S(2)}) collective-permute-start(bf16[4,512,256]{2,1,0:T(8,128)(2,1)} %add_convert_fusion.7), channel_id=1, source_target_pairs={{4,0},{8,12},{5,1},{9,13},{6,2},{10,14},{7,3},{11,15},{20,16},{24,... | collective-permute-start | bytes 3145736 | tf_op jit(solution)/shard_map/ppermute | solution.py:637
  1042.7 33.0 %collective-permute-start.85 = (bf16[4,592,256]{2,1,0:T(8,128)(2,1)S(1)}, bf16[4,592,256]{2,1,0:T(8,128)(2,1)S(1)}, u32[]{:S(2)}, u32[]{:S(2)}) collective-permute-start(bf16[4,592,256]{2,1,0:T(8,128)(2,1)S(1)} %add_convert_fusion.1), channel_id=1, source_target_pairs={{4,8},{8,4},{5,9},{9,5},{6,10},{10,6},{7,11},{11,7},{20,24},{24,20... | collective-permute-start | bytes 3637256 | tf_op jit(solution)/shard_map/ppermute | solution.py:637
  1045.9 29.9 %collective-permute-start.84 = (bf16[4,512,256]{2,1,0:T(8,128)(2,1)S(1)}, bf16[4,512,256]{2,1,0:T(8,128)(2,1)S(1)}, u32[]{:S(2)}, u32[]{:S(2)}) collective-permute-start(bf16[4,512,256]{2,1,0:T(8,128)(2,1)S(1)} %add_convert_fusion.5), channel_id=1, source_target_pairs={{4,0},{8,12},{5,1},{9,13},{6,2},{10,14},{7,3},{11,15},{20,16},{24,... | collective-permute-start | bytes 3145736 | tf_op jit(solution)/shard_map/ppermute | solution.py:637
  1078.0 26.6 %collective-permute-start.87 = (bf16[4,512,256]{2,1,0:T(8,128)(2,1)S(1)}, bf16[4,512,256]{2,1,0:T(8,128)(2,1)S(1)}, u32[]{:S(2)}, u32[]{:S(2)}) collective-permute-start(bf16[4,512,256]{2,1,0:T(8,128)(2,1)S(1)} %add_convert_fusion.4), channel_id=1, source_target_pairs={{4,0},{8,12},{5,1},{9,13},{6,2},{10,14},{7,3},{11,15},{20,16},{24,... | collective-permute-start | bytes 3145736 | tf_op jit(solution)/shard_map/ppermute | solution.py:637
  1105.6 30.1 %collective-permute-start.89 = (bf16[4,592,256]{2,1,0:T(8,128)(2,1)}, bf16[4,592,256]{2,1,0:T(8,128)(2,1)}, u32[]{:S(2)}, u32[]{:S(2)}) collective-permute-start(bf16[4,592,256]{2,1,0:T(8,128)(2,1)} %add_convert_fusion), channel_id=1, source_target_pairs={{4,0},{8,12},{5,1},{9,13},{6,2},{10,14},{7,3},{11,15},{20,16},{24,... | collective-permute-start | bytes 3637256 | tf_op jit(solution)/shard_map/ppermute | solution.py:637
  1154.3 31.0 %collective-permute-start.92 = (bf16[2,128,2048]{2,1,0:T(8,128)(2,1)}, bf16[2,128,2048]{2,1,0:T(8,128)(2,1)}, u32[]{:S(2)}, u32[]{:S(2)}) collective-permute-start(bf16[2,128,2048]{2,1,0:T(8,128)(2,1)} %fusion.16), channel_id=1, source_target_pairs={{0,16},{16,0},{1,17},{17,1},{2,18},{18,2},{3,19},{19,3},{4,20},{20... | collective-permute-start | bytes 3145736 | tf_op jit(solution)/shard_map/ppermute | solution.py:551
  (185 other events, 2433.7 us)

commit v7 on v6

--- a/solution.py
+++ b/solution.py
@@ -432,10 +432,10 @@
                 dx[...], wx[:, here], preferred_element_type=F32
             )
             at_lane = pl.multiple_of(jnp.bitwise_xor(ids[0], m) * share + lo, 256)
-            out[:, pl.ds(at_lane, 256)] = v.astype(BF16)
-
-
-def project_back(ids, dz, dx, near, far, layer):
+            out[:, pl.ds(at_lane, 256)] = v.astype(out.dtype)
+
+
+def project_back(ids, dz, dx, near, far, layer, kind):
     n = len(near[0])
     share = near[0][0].shape[1]
     rows = dz.shape[0]
@@ -452,7 +452,7 @@
             pltpu.SemaphoreType.DMA((2,)),
             pltpu.SemaphoreType.DMA((2,)),
         ],
-        out_shape=jax.ShapeDtypeStruct((rows, n * share), BF16),
+        out_shape=jax.ShapeDtypeStruct((rows, n * share), kind),
         compiler_params=pltpu.CompilerParams(vmem_limit_bytes=VMEM_BYTES),
         cost_estimate=pl.CostEstimate(
             flops=2 * rows * columns * share * n,
@@ -496,7 +496,7 @@
         if k + 1 < len(plan):
             fetch(k + 1)
         pltpu.make_async_copy(pieces.at[k % 2], pieces.at[k % 2], in_sem.at[k % 2]).wait()
-        shift = jnp.where(side == 0, core, 1 - core) * (2 * size)
+        shift = jnp.where(side == 0, core, 1 - core) * size
         for p, first in enumerate(firsts):
             step = len(sent)
             if step >= 2:
@@ -547,6 +547,33 @@
     )(ids, *arrays, small, *before)
 
 
+def combine_kernel(flags, *refs, adds):
+    count = len(adds)
+    for k, add in enumerate(adds):
+        v, got, out = refs[2 * k], refs[2 * k + 1], refs[2 * count + k]
+        if add:
+            out[...] = (v[...].astype(F32) + got[...].astype(F32)).astype(BF16)
+        else:
+            out[...] = jnp.where(flags[k] == 1, got[...], v[...])
+
+
+def combine(items, flags):
+    steps = 8
+    shapes = [v.shape for v, _, _ in items]
+    flat = [(v.reshape(-1, v.shape[-1]), g.reshape(-1, g.shape[-1])) for v, g, _ in items]
+    spec = lambda v: pl.BlockSpec((v.shape[0] // steps, v.shape[1]), lambda i: (i, 0))
+    out = pl.pallas_call(
+        functools.partial(combine_kernel, adds=tuple(add for _, _, add in items)),
+        grid=(steps,),
+        in_specs=[pl.BlockSpec(memory_space=pltpu.SMEM)] + [spec(v) for p in flat for v in p],
+        out_specs=[spec(v) for v, _ in flat],
+        out_shape=[jax.ShapeDtypeStruct(v.shape, BF16) for v, _ in flat],
+        compiler_params=pltpu.CompilerParams(vmem_limit_bytes=VMEM_BYTES),
+        name="combine",
+    )(flags, *[v for p in flat for v in p])
+    return [v.reshape(shape) for v, shape in zip(out, shapes)]
+
+
 def swap_section(v):
     return lax.ppermute(v, "section", [(0, 1), (1, 0)])
 
@@ -607,57 +634,46 @@
         self.pairs.append([(half - 1, half), (half, half - 1)])
         self.inward = half
         self.pairs += [[(j + 1, j), (s - 2 - j, s - 1 - j)] for j in reversed(range(half - 1))]
-        self.values, self.phase = [], []
-        self.came, self.moving, self.fresh = [], [], []
-
-    def add(self, values):
-        first = len(self.values)
-        self.values += values
-        self.phase += [0] * len(values)
-        return list(range(first, len(self.values)))
+        self.values, self.phase, self.moving = [], [], []
+
+    def add(self, value):
+        self.values.append(value)
+        self.phase.append(0)
+        return len(self.values) - 1
 
     def begin(self):
-        place = lax.axis_index("seq")
-        for k, got in self.came:
-            step, v = self.phase[k] - 1, self.values[k]
-            if step < self.inward:
-                v = (v.astype(F32) + got.astype(F32)).astype(BF16)
-            else:
-                here = functools.reduce(
-                    jnp.logical_or, [place == to for _, to in self.pairs[step]]
-                )
-                v = jnp.where(here, got, v)
-            self.fresh.append((k, v))
         taken = set()
-        waiting = [k for k, _ in self.came]
         for k, step in enumerate(self.phase):
-            if step == len(self.pairs) or step in taken or k in waiting:
+            if step == len(self.pairs) or step in taken:
                 continue
             taken.add(step)
             self.moving.append((k, lax.ppermute(self.values[k], "seq", self.pairs[step])))
+
+    def end(self, work):
+        place = lax.axis_index("seq")
+        items, flags = [], []
+        for k, got in self.moving:
+            step = self.phase[k]
+            items.append((self.values[k], got, step < self.inward))
+            here = [place == to for _, to in self.pairs[step]]
+            flags.append(functools.reduce(jnp.logical_or, here))
             self.phase[k] = step + 1
-
-    def end(self, work):
+        moved = combine(items, jnp.stack(flags).astype(jnp.int32)) if items else []
         still = [k for k, p in enumerate(self.phase) if p == 0]
-        work, fresh, came, rest = lax.optimization_barrier(
-            (
-                work,
-                [v for _, v in self.fresh],
-                [v for _, v in self.moving],
-                [self.values[k] for k in still],
-            )
+        work, moved, rest = lax.optimization_barrier(
+            (work, moved, [self.values[k] for k in still])
         )
-        for (k, _), v in zip(self.fresh, fresh):
+        for (k, _), v in zip(self.moving, moved):
             self.values[k] = v
         for k, v in zip(still, rest):
             self.values[k] = v
-        self.came = [(k, v) for (k, _), v in zip(self.moving, came)]
-        self.moving, self.fresh = [], []
+        self.moving = []
         return work
 
-    def done(self, k):
-        busy = [j for j, _ in self.came + self.moving + self.fresh]
-        return self.phase[k] == len(self.pairs) and k not in busy
+    def finish(self, chunks):
+        while any(self.phase[k] < len(self.pairs) for k in chunks):
+            self.begin()
+            self.end(())
 
 
 def relay(total, local, reverse):
@@ -774,8 +790,8 @@
     part_h0 = in_group(part_h0)
     near_x0, part_h0 = tie((near_x0, part_h0))
     far_x0 = [lax.ppermute(v, "section", [(0, 1)]) for v in near_x0]
+    pieces_z, part_h0 = tie(([piece_z(m) for m in range(n)], part_h0))
     all_h0 = whole_slot(part_h0)
-    pieces_z, all_h0 = tie(([piece_z(m) for m in range(n)], all_h0))
     near_z0, far_z0 = fetch(pieces_z, 0)
 
     theirs = swap_section(mine)
@@ -853,11 +869,9 @@
 
     normed_in0 = normalised(all_h0.astype(F32), small[0][0]).astype(BF16)
     px0 = project_x(normed_in0, 0)
-    px0, near_z0, pieces_x1, pieces_z1, own_ct, wo_mine, own_len = tie(
-        (px0, near_z0, pieces_x, pieces_z, at(cotangent, c)[0], w_out[0], at(lengths, c))
+    px0, pieces_x1, pieces_z1, own_ct, wo_mine, own_len = tie(
+        (px0, pieces_x, pieces_z, at(cotangent, c)[0], w_out[0], at(lengths, c))
     )
-    far_z0 = [lax.ppermute(v, "section", [(0, 1)]) for v in near_z0]
-    win[0] = (near_z0, far_z0, near_x0, far_x0)
     near_x1, far_x1 = fetch(pieces_x1, 1)
     wo_other = swap_section(wo_mine)
     wo = (pick(wo_mine, wo_other), pick(wo_other, wo_mine))
@@ -874,7 +888,9 @@
     own_rows = lambda v: lax.dynamic_slice_in_dim(v, f * rows, rows, 0)
     valid = own_rows(all_valid)
     h0 = own_rows(all_h0)
-    fwd0 = scan(px0, 0)
+    fwd0, near_z0 = tie((scan(px0, 0), near_z0))
+    far_z0 = [lax.ppermute(v, "section", [(0, 1)]) for v in near_z0]
+    win[0] = (near_z0, far_z0, near_x0, far_x0)
     pz0 = project_z(normed_in0, 0)
     g0 = gate(pz0, fwd0[0][0])
     stat0, near_x1, pieces_z1 = tie((jnp.sum(g0 * g0, axis=1), near_x1, pieces_z1))
@@ -885,15 +901,14 @@
     part_ct = in_group(exchange(quarters(own_ct)))
     normed0, wo, part_ct = tie((normed0, wo, part_ct))
     far_x1 = [lax.ppermute(v, "section", [(1, 0)]) for v in near_x1]
-    mixed0 = scatter_sum(jnp.dot(normed0, wo[0], preferred_element_type=F32).astype(BF16))
+    mixed0 = scatter_sum(jnp.dot(normed0, wo[0], preferred_element_type=F32))
     out0 = valid * (h0.astype(F32) + mixed0)
     h1 = out0.astype(BF16)
 
-    h1, near_z1 = tie((h1, near_z1))
+    normed_in1 = gather_rows(normalised(h1.astype(F32), small[1][0]).astype(BF16))
+    normed_in1, far_x1, part_ct, near_z1 = tie((normed_in1, far_x1, part_ct, near_z1))
     far_z1 = [lax.ppermute(v, "section", [(1, 0)]) for v in near_z1]
     win[1] = (near_z1, far_z1, near_x1, far_x1)
-    normed_in1 = gather_rows(normalised(h1.astype(F32), small[1][0]).astype(BF16))
-    normed_in1, far_x1, part_ct = tie((normed_in1, far_x1, part_ct))
     px1 = project_x(normed_in1, 1)
     all_ct = whole_slot(part_ct)
     fwd1 = scan(px1, 1)
@@ -914,7 +929,7 @@
     r1 = lax.rsqrt(stat1[0] / INNER + EPS)
     normed1 = gated(pz1, fwd1[0][0], r1, 1)
 
-    part_width = width // 4
+    part_width = width // 2
 
     def cut_half(v, k):
         size = v.shape[1] // 2
@@ -929,29 +944,21 @@
             away.append(dot_rows(narrow_of(narrow, 1 - c), normed_in).astype(BF16))
         return [swap_section(v) for v in away]
 
-    def own_in_pieces(normed_in, part, away, narrow=()):
-        own = cut_half(part, c)
-        result = []
-        for cols in (slice(0, part_width), slice(part_width, 2 * part_width)):
-            total = dot_rows(normed_in, own[:, cols]) + away[0][:, cols].astype(F32)
-            result.append(total.astype(BF16).reshape(n, share, -1))
+    def own_in_piece(normed_in, part, away, narrow=()):
+        total = dot_rows(normed_in, cut_half(part, c)) + away[0].astype(F32)
+        result = total.astype(BF16).reshape(n, share, -1)
         if narrow:
-            total = dot_rows(narrow_of(narrow, c), normed_in) + away[1].astype(F32)
-            rest = total.astype(BF16).reshape(-1, n, share).transpose(1, 0, 2)
-            rest = rest.reshape(n, -1, part_width)
-            result[1] = jnp.concatenate([result[1], rest], axis=1)
+            total = (dot_rows(narrow_of(narrow, c), normed_in) + away[1].astype(F32)).astype(BF16)
+            fill = jnp.zeros((-total.shape[0] % 64, D), BF16)
+            rest = jnp.concatenate([total, fill]).reshape(-1, n, share).transpose(1, 0, 2)
+            result = jnp.concatenate([result, rest], axis=1)
         return result
 
     def away_out(normed, dmixed):
         return swap_section(dot_rows(cut_half(normed, 1 - c), dmixed).astype(BF16))
 
-    def own_out_pieces(normed, dmixed, away):
-        own = cut_half(normed, c)
-        result = []
-        for cols in (slice(0, D // 2), slice(D // 2, D)):
-            total = dot_rows(own, dmixed[:, cols]) + away[:, cols].astype(F32)
-            result.append(total.astype(BF16))
-        return result
+    def own_out_piece(normed, dmixed, away):
+        return (dot_rows(cut_half(normed, c), dmixed) + away.astype(F32)).astype(BF16)
 
     def with_group(dxs, dbc):
         total = jnp.sum(exchange(dbc), axis=0).astype(BF16)
@@ -960,9 +967,9 @@
         full = lax.dynamic_update_slice(dxs, own.astype(BF16), (0, width))
         return full, (dxs[:, :width], [total, dxs[:, width + GROUP :]])
 
-    def back_in(dz, full, layer):
+    def back_in(dz, full, layer, kind):
         near_z, far_z, near_x, far_x = win[layer]
-        return project_back(ids, dz, full, (near_z, near_x), (far_z, far_x), layer)
+        return project_back(ids, dz, full, (near_z, near_x), (far_z, far_x), layer, kind)
 
     def back_norm(dout, dnormed_in, h, gain):
         h = h.astype(F32)
@@ -1002,7 +1009,7 @@
     sums = SeqSums()
     rc1 = scales(r1, (r1 * r1 * r1 / INNER) * stat1[1])
     away = away_out(normed1, dmixed1)
-    go1 = sums.add(own_out_pieces(normed1, dmixed1, away))
+    o1 = sums.add(own_out_piece(normed1, dmixed1, away))
     rc1, normed1, dn1 = sums.end((rc1, normed1, dn1))
 
     sums.begin()
@@ -1013,15 +1020,17 @@
     sums.begin()
     away = away_in(normed_in1, d1[0])
     full1, xs1 = with_group(d1[1], d1[2])
-    back1 = back_in(d1[0], full1, 1)
-    back1, xs1, away, full1 = sums.end((back1, xs1, away, full1))
+    back1 = back_in(d1[0], full1, 1, F32)
+    gz = own_in_piece(normed_in1, d1[0], away)
+    back1, xs1, full1, gz = sums.end((back1, xs1, full1, gz))
+    z1 = sums.add(gz)
 
     sums.begin()
     dnin1 = scatter_sum(back1)
-    gz = own_in_pieces(normed_in1, d1[0], away)
     away = away_in(normed_in1, *xs1)
-    dnin1, gz, away = sums.end((dnin1, gz, away))
-    gz1 = sums.add(gz)
+    gx = own_in_piece(normed_in1, xs1[0], away, xs1[1])
+    dnin1, gx = sums.end((dnin1, gx))
+    x1 = sums.add(gx)
 
     sums.begin()
     grad1, dgin1 = back_norm(dout1, dnin1, h1, small[1][0])
@@ -1030,74 +1039,80 @@
     dmixed0 = gather_rows(dmixed0_own)
     along0 = to_all(jnp.sum(dmixed0_own.astype(F32) * mixed0, axis=-1)).reshape(-1)
     rc0 = scales(r0, (r0 * r0 / INNER) * along0)
-    gx = own_in_pieces(normed_in1, xs1[0], away, xs1[1])
     out1 = valid * (h1.astype(F32) + mixed1)
-    grad1, dgin1, dmixed0, rc0, gx, out1 = sums.end((grad1, dgin1, dmixed0, rc0, gx, out1))
-    gx1 = sums.add(gx)
+    grad1, dgin1, dmixed0, rc0, out1 = sums.end((grad1, dgin1, dmixed0, rc0, out1))
 
     sums.begin()
+    back_h = exchange(quarters(jnp.concatenate([h1, out1.astype(BF16)])))
     dn0 = dot_cols(dmixed0, wo[0])
     d0 = unscan(pz0, px0, fwd0, dn0, rc0, 0)
-    d0 = sums.end(d0)
+    go = own_out_piece(normed0, dmixed0, away_out(normed0, dmixed0))
+    d0, go, back_h = sums.end((d0, go, back_h))
+    o0 = sums.add(go)
 
     sums.begin()
-    away_z = away_in(normed_in0, d0[0])
-    away_o = away_out(normed0, dmixed0)
+    back_h = in_group(back_h)
+    away = away_in(normed_in0, d0[0])
     full0, xs0 = with_group(d0[1], d0[2])
-    gz = own_in_pieces(normed_in0, d0[0], away_z)
-    go = own_out_pieces(normed0, dmixed0, away_o)
-    full0, xs0, gz, go = sums.end((full0, xs0, gz, go))
-    go0 = sums.add(go)
+    gz = own_in_piece(normed_in0, d0[0], away)
+    away = away_in(normed_in0, *xs0)
+    gx = own_in_piece(normed_in0, xs0[0], away, xs0[1])
+    full0, gz, gx, back_h = sums.end((full0, gz, gx, back_h))
+    z0 = sums.add(gz)
 
     sums.begin()
-    away = away_in(normed_in0, *xs0)
-    gz = [exchange(v) for v in gz]
-    gx = own_in_pieces(normed_in0, xs0[0], away, xs0[1])
-    gz, gx, full0 = sums.end((gz, gx, full0))
-    gz0 = sums.add(gz)
-
-    sums.begin()
-    gx = [exchange(v) for v in gx]
-    back0 = back_in(d0[0], full0, 0)
-    gx, back0 = sums.end((gx, back0))
-    gx0 = sums.add(gx)
-
+    gx = exchange(gx)
+    back0 = back_in(d0[0], full0, 0, BF16)
+    back_h = joined(exchange(back_h))
+    gx, back0, back_h = sums.end((gx, back0, back_h))
+    x0 = sums.add(gx)
+
+    def hand_over(v, layer):
+        return lax.ppermute(v, "section", [(1 - layer, layer)])
+
+    sums.finish([o1, z1])
     sums.begin()
     dnin0 = scatter_sum(back0)
+    own_z1 = exchange(sums.values[z1])
+    own_o1 = sums.values[o1]
+    away_o1 = hand_over(own_o1, 1)
+    dnin0, own_z1, own_o1, away_o1 = sums.end((dnin0, own_z1, own_o1, away_o1))
+
+    sums.finish([x1, o0])
+    sums.begin()
+    own_x1 = exchange(sums.values[x1])
+    away_z1 = hand_over(own_z1, 1)
+    own_o0 = sums.values[o0]
+    away_o0 = hand_over(own_o0, 0)
     grad0, dgin0 = back_norm(dout0, dnin0, h0, small[0][0])
+    back_g = exchange(quarters(jnp.concatenate([grad0.astype(BF16), grad1.astype(BF16)])))
     p = jnp.stack([packed(dgin0, d0, out0, mixed0), packed(dgin1, d1, out1, mixed1)])
     p = p + swap_section(p)
-    p, grad0, grad1, h1, out1 = sums.end((p, grad0, grad1, h1, out1))
-
-    names = {"own": {}, "away": {}}
-    order = [(k, 1, "out") for k in go1] + [(k, 1, "in") for k in gz1 + gx1]
-    order += [(k, 0, "out") for k in go0] + [(k, 0, "in") for k in gz0 + gx0]
-    back = jnp.concatenate([h1, out1.astype(BF16), grad0.astype(BF16), grad1.astype(BF16)])
-    back_steps = [lambda v: exchange(quarters(v)), in_group, lambda v: joined(exchange(v))]
-    p_steps = [lambda v, m=m: move_fsdp(v, m) for m in (1 << j for j in range(n.bit_length() - 1))]
-    p_steps += [lambda v, m=m: move_seq(v, m) for m in (1 << j for j in range(nz.bit_length() - 1))]
-    exchanged = set()
-    while order:
-        sums.begin()
-        ready = [e for e in order if sums.done(e[0])]
-        turn = [e for e in ready if e[1:] == (1, "in") and e[0] not in exchanged][:2]
-        if back_steps:
-            back = back_steps.pop(0)(back)
-            turn = turn[:1]
-        if p_steps:
-            p = p + p_steps.pop(0)(p)
-        swapped = {e[0]: exchange(sums.values[e[0]]) for e in turn}
-        final = [e for e in ready if e[1:] != (1, "in") or e[0] in exchanged][:2]
-        fresh = {e[0]: hand_over(sums.values[e[0]], e[1]) for e in final}
-        kept = {e[0]: sums.values[e[0]] for e in final}
-        swapped, fresh, kept, back, p = sums.end((swapped, fresh, kept, back, p))
-        for k, v in swapped.items():
-            sums.values[k] = v
-            exchanged.add(k)
-        for k in fresh:
-            names["own"][k], names["away"][k] = kept[k], fresh[k]
-        order = [e for e in order if e not in final]
+    p, back_g, own_x1, own_z1, away_z1, own_o0, away_o0 = sums.end(
+        (p, back_g, own_x1, own_z1, away_z1, own_o0, away_o0)
+    )
+
+    sums.finish([z0])
+    sums.begin()
+    back_g = in_group(back_g)
+    own_z0 = exchange(sums.values[z0])
+    away_x1 = hand_over(own_x1, 1)
+    m = 1
+    while m < n:
+        p = p + move_fsdp(p, m)
+        m *= 2
+    p, back_g, own_z0, own_x1, away_x1 = sums.end((p, back_g, own_z0, own_x1, away_x1))
+    sums.finish([x0])
+    away_z0 = hand_over(own_z0, 0)
+    own_x0 = sums.values[x0]
+    away_x0 = hand_over(own_x0, 0)
+    back_g = joined(exchange(back_g))
+    m = 1
+    while m < nz:
+        p = p + move_seq(p, m)
+        m *= 2
     p = pick(p[0], p[1])
+    back = jnp.concatenate([back_h, back_g])
 
     used = 0
 
@@ -1114,42 +1129,38 @@
     totals = part(3)
     act_rms = jnp.sqrt(totals[:2] / (totals[2] * D))[None]
 
-    sides = ("own", "away")
     held = [
-        [[names[side][k] for k in ks] for ks in (gz0 + gx0 + go0, gz1 + gx1 + go1)]
-        for side in sides
+        [(own_z0, own_x0, own_o0), (own_z1, own_x1, own_o1)],
+        [(away_z0, away_x0, away_o0), (away_z1, away_x1, away_o1)],
     ]
 
     def both_halves(a, b):
         return jnp.stack([pick(a, b), pick(b, a)], axis=1)
 
-    narrow = [pick(side[0][3], side[1][3])[:, share:] for side in held]
-    narrow = both_halves(*[v.astype(F32).reshape(n, -1, share) for v in narrow])
+    rows_of = GROUP // n // 2, HEADS // n // 2
+    narrow = [pick(side[0][1], side[1][1])[:, share : share + sum(rows_of)] for side in held]
+    narrow = both_halves(*[v.astype(F32) for v in narrow])
     small_in = jnp.concatenate(
         [
-            narrow[:, :, : group // 2].reshape(GROUP, share),
-            narrow[:, :, group // 2 :].reshape(HEADS, share),
+            narrow[:, :, : rows_of[0]].reshape(GROUP, share),
+            narrow[:, :, rows_of[0] :].reshape(HEADS, share),
         ]
     )
     g_w_in = []
     shape_in = (2 * INNER + GROUP + HEADS, share)
-    for ks, rows_of_small in (((0, 1), None), ((2, 3), (2 * INNER, GROUP + HEADS))):
+    for k, rows_of_small in ((0, None), (1, (2 * INNER, GROUP + HEADS))):
         arrays, plan = [], []
-        for k in ks:
-            for s in range(2):
-                arrays += [held[s][0][k], held[s][1][k]]
-                base = k // 2 * INNER + k % 2 * part_width
-                firsts = tuple(base + q * width for q in range(n))
-                plan.append((len(arrays) - 2, len(arrays) - 1, s, firsts))
+        for s in range(2):
+            arrays += [held[s][0][k], held[s][1][k]]
+            firsts = tuple(k * INNER + q * width for q in range(n))
+            plan.append((len(arrays) - 2, len(arrays) - 1, s, firsts))
         g_w_in = [
             place_in(
                 ids, arrays, tuple(plan), small_in, rows_of_small, g_w_in, shape_in, part_width
             )
         ]
-    halves_out = [
-        jnp.concatenate([pick(side[0][k], side[1][k]) for k in (4, 5)], axis=1) for side in held
-    ]
-    g_w_out = both_halves(*[v[None] for v in halves_out]).reshape(width, D).astype(F32)
+    halves_out = [pick(side[0][2], side[1][2]) for side in held]
+    g_w_out = jnp.concatenate([pick(*halves_out), pick(*halves_out[::-1])]).astype(F32)
 
     back = back.reshape(2, 2, rows, D)
     kept_back = pick(back[:, 0], back[:, 1])

time: 1200 us -> 1210 us (level)
  waiting for transfers between devices: 341 us -> 422 us
  other arithmetic: 149 us -> 77.2 us
  Pallas kernels: 134 us -> 197 us
  starting transfers between devices: 358 us -> 299 us
    pallas_call x0 -> x10, Pallas kernels: none -> 67.6 us  [combine(): pl.pallas_call(functools.partial(combine_kernel, adds=tuple((add for _, _...]
    convert_element_type x27 -> x6, other arithmetic: 66.6 us -> 6.97 us  [the longest x1 4.28 us: per_device(): jnp.concatenate([pick(*halves_out), pick(*halves_out[::-1])]).astype(F32)]
    ppermute x36 -> x18, starting transfers between devices: 116 us -> 68.9 us  [begin(): lax.ppermute(self.values[k], 'seq', self.pairs[step])]
    all_to_all x3 -> x4, waiting for transfers between devices: 0.56 us -> 41 us  [in_group(): return lax.all_to_all(v, 'seq', 0, 0, axis_index_groups=groups, tiled=True)]
    ppermute x36 -> x18, waiting for transfers between devices: 155 us -> 182 us  [begin(): lax.ppermute(self.values[k], 'seq', self.pairs[step])]
    ppermute x2, waiting for transfers between devices: 24.7 us -> 4.37 us  [move_seq(): return lax.ppermute(v, 'seq', [(k, k ^ m) for k in range(s)])]
    select_n x12 -> x0, other arithmetic: 18.8 us -> none  [begin(): v = jnp.where(here, got, v)]
    ppermute x12, starting transfers between devices: 39.4 us -> 24.5 us  [swap_section(): return lax.ppermute(v, 'section', [(0, 1), (1, 0)])]
  transfers between devices with their start and end apart: 121 -> 96, of which waited for: 41 -> 41; matrix products, arithmetic and copies ran while one was open for 20% -> 14% of each run, Pallas kernels for 11% -> 13%
where the time goes in v7:
time: 1210 us; the launch traced here: 1200 us
  waiting for transfers between devices  422 us (35%)
  starting transfers between devices  299 us (25%)
  Pallas kernels  197 us (16%)
  local copies, waits for them, and re-layouts  110 us (9%)
  matrix products  80.8 us (7%)
  other arithmetic  77.2 us (6%)
    ppermute x18, waiting for transfers between devices, begin(): lax.ppermute(self.values[k], 'seq', self.pairs[step])  182 us
    all_to_all x23, starting transfers between devices, exchange(): return lax.all_to_all(v, 'fsdp', 0, 0, tiled=True)  96.8 us
    all_to_all x23, waiting for transfers between devices, exchange(): return lax.all_to_all(v, 'fsdp', 0, 0, tiled=True)  96.4 us
    ppermute x18, starting transfers between devices, begin(): lax.ppermute(self.values[k], 'seq', self.pairs[step])  68.9 us
    pallas_call x10, Pallas kernels, combine(): pl.pallas_call(functools.partial(combine_kernel, adds=tuple((add for _, _...  67.6 us
    dot_general x16, matrix products, dot_rows(): lax.dot_general(a, b, (((0,), (0,)), ((), ())), preferred_element_type=F32)  56.9 us
    unnamed x184, local copies, waits for them, and re-layouts  47.3 us
    all_to_all x4, waiting for transfers between devices, in_group(): return lax.all_to_all(v, 'seq', 0, 0, axis_index_groups=groups, tiled=True)  41 us
  transfers between devices with their start and end apart: 96, of which 41 were waited for; matrix products, arithmetic and copies ran while one was open for 14% of the time, Pallas kernels for 13%

profile of v7, /device:TPU:1, one launch (start us, length us, event | category | flops | bytes accessed | tf_op | source)
XLA Modules:
  0.0 1195.7 jit_solution(11516839904513644118)
XLA Ops:
  13.5 6.5 dynamic-slice_bitcast_fusion
  49.5 7.0 all-to-all-done.2
  70.1 21.6 %all-to-all-done.3 = bf16[4,512,512]{2,1,0:T(8,128)(2,1)} async-done(((bf16[4,512,512]{2,1,0:T(8,128)(2,1)}), bf16[4,512,512]{2,1,0:T(8,128)(2,1)}, u32[]{:S(2)}, u32[]{:S(2)}) %all-to-all-start.3) | async-done | bytes 2097184 | tf_op jit(solution)/shard_map/all_to_all | solution.py:586
  107.8 8.8 project.4.proj
  116.5 9.6 collective-permute-start.19
  130.0 10.6 scan_forward.2
  150.5 10.4 collective-permute-done.11.refs_4_.refs_8_
  178.4 6.7 project.5.pz
  188.6 12.8 %collective-permute-done.17.refs_2_.refs_6_ = bf16[1296,512]{1,0:T(8,128)(2,1)} collective-permute-done((bf16[1296,512]{1,0:T(8,128)(2,1)}, bf16[1296,512]{1,0:T(8,128)(2,1)}, u32[]{:S(2)}, u32[]{:S(2)}) %collective-permute-start.17) | collective-permute-done | bytes 1327136 | tf_op jit(solution)/shard_map/ppermute | solution.py:767
  210.2 5.8 all-to-all-start.6
  218.9 5.8 broadcast_select_fusion
  224.7 5.2 all-to-all-done.6
  229.9 6.9 fusion.117
  236.8 4.9 all-to-all-start.7
  244.8 6.7 collective-permute-start.24
  251.5 5.8 collective-permute-start.25
  257.3 32.1 %all-to-all-done.7 = f32[4,128,2048]{2,1,0:T(8,128)} async-done(((f32[4,128,2048]{2,1,0:T(8,128)}), f32[4,128,2048]{2,1,0:T(8,128)}, u32[]{:S(2)}, u32[]{:S(2)}) %all-to-all-start.7) | async-done | bytes 4194336 | tf_op jit(solution)/shard_map/all_to_all | solution.py:586
  314.8 24.8 %collective-permute-done.26.refs_3_ = bf16[1024,512]{1,0:T(8,128)(2,1)S(1)} collective-permute-done((bf16[1024,512]{1,0:T(8,128)(2,1)}, bf16[1024,512]{1,0:T(8,128)(2,1)S(1)}, u32[]{:S(2)}, u32[]{:S(2)}) %collective-permute-start.26) | collective-permute-done | bytes 1048608 | tf_op jit(solution)/shard_map/ppermute | solution.py:767
  358.7 7.7 project.6.proj
  366.4 10.7 scan_forward.3
  382.2 6.3 project.7.pz
  392.3 6.9 multiply_reduce_fusion.2
  416.6 4.9 add_convert_fusion.5.refs_0_
  432.4 20.4 %scan_backward.2 = (bf16[512,1024]{1,0:T(8,128)(2,1)S(1)}, bf16[512,1296]{1,0:T(8,128)(2,1)S(1)}, f32[4,512,64]{2,1,0:T(8,128)S(1)}, f32[8,1024]{1,0:T(8,128)S(1...) custom-call(f32[512,1024]{1,0:T(8,128)} %project.7.pz, ...), custom_call_target="tpu_custom_call" | custom-call | tf_op jit(solution)/shard_map/scan_backward/pallas_call | solution.py:303
  460.3 7.9 collective-permute-done.32.refs_1_
  468.3 6.2 combine.10.refs_0_
  489.7 6.5 all-to-all-done.12
  501.1 11.1 project_back.2
  512.3 4.9 add_convert_fusion.4
  523.1 5.0 all-to-all-start.13
  529.6 18.5 %collective-permute-start.38 = (bf16[4,512,512]{2,1,0:T(8,128)(2,1)}, bf16[4,512,512]{2,1,0:T(8,128)(2,1)}, u32[]{:S(2)}, u32[]{:S(2)}) collective-permute-start(bf16[4,512,512]{2,1,0:T(8,128)(2,1)} %bitcast.307), channel_id=1, source_target_pairs={{0,4},{12,8},{1,5},{13,9},{2,6},{14,10},{3,7},{15,11},{16,20},{28,... | collective-permute-start | bytes 6291464 | tf_op jit(solution)/shard_map/ppermute | solution.py:650
  560.4 28.7 %collective-permute-done.37.refs_1_ = bf16[512,2048]{1,0:T(8,128)(2,1)} collective-permute-done((bf16[512,2048]{1,0:T(8,128)(2,1)}, bf16[512,2048]{1,0:T(8,128)(2,1)}, u32[]{:S(2)}, u32[]{:S(2)}) %collective-permute-start.37) | collective-permute-done | bytes 2097184 | tf_op jit(solution)/shard_map/ppermute | solution.py:650
  591.2 6.9 combine.12
  609.8 5.9 collective-permute-start.40
  621.0 6.5 all_to_all.145
  633.7 29.4 %collective-permute-done.40 = bf16[4,576,512]{2,1,0:T(8,128)(2,1)} collective-permute-done((bf16[4,576,512]{2,1,0:T(8,128)(2,1)}, bf16[4,576,512]{2,1,0:T(8,128)(2,1)}, u32[]{:S(2)}, u32[]{:S(2)}) %collective-permute-start.40) | collective-permute-done | bytes 2359328 | tf_op jit(solution)/shard_map/ppermute | solution.py:650
  664.7 7.3 combine.13
  689.1 6.5 fusion.118.dn
  695.6 20.4 %scan_backward.3 = (bf16[512,1024]{1,0:T(8,128)(2,1)S(1)}, bf16[512,1296]{1,0:T(8,128)(2,1)S(1)}, f32[4,512,64]{2,1,0:T(8,128)S(1)}, f32[8,1024]{1,0:T(8,128)S(1...) custom-call(f32[512,1024]{1,0:T(8,128)} %project.5.pz, ...), custom_call_target="tpu_custom_call" | custom-call | tf_op jit(solution)/shard_map/scan_backward/pallas_call | solution.py:303
  716.1 5.6 add_convert_fusion.2.refs_2_
  721.7 10.2 collective-permute-done.42
  731.9 7.2 combine.14
  755.1 9.4 collective-permute-start.48
  787.6 20.4 %collective-permute-done.48.refs_3_ = bf16[512,2048]{1,0:T(8,128)(2,1)} collective-permute-done((bf16[512,2048]{1,0:T(8,128)(2,1)}, bf16[512,2048]{1,0:T(8,128)(2,1)}, u32[]{:S(2)}, u32[]{:S(2)}) %collective-permute-start.48) | collective-permute-done | bytes 2097184 | tf_op jit(solution)/shard_map/ppermute | solution.py:650
  811.6 6.6 combine.15
  819.6 5.2 all-to-all-done.18
  831.2 6.6 collective-permute-start.50
  847.9 10.7 project_back.3
  861.0 18.9 %collective-permute-done.50 = bf16[4,512,512]{2,1,0:T(8,128)(2,1)} collective-permute-done((bf16[4,512,512]{2,1,0:T(8,128)(2,1)}, bf16[4,512,512]{2,1,0:T(8,128)(2,1)}, u32[]{:S(2)}, u32[]{:S(2)}) %collective-permute-start.50) | collective-permute-done | bytes 2097184 | tf_op jit(solution)/shard_map/ppermute | solution.py:650
  879.9 7.6 combine.16
  891.1 5.5 collective-permute-start.54
  901.2 14.3 %all-to-all-done.21 = bf16[4,128,2048]{2,1,0:T(8,128)(2,1)S(1)} async-done(((bf16[4,128,2048]{2,1,0:T(8,128)(2,1)}), bf16[4,128,2048]{2,1,0:T(8,128)(2,1)S(1)}, u32[]{:S(2)}, u32[]{:S(2)}) %all-to-all-start.21) | async-done | bytes 2097184 | tf_op jit(solution)/shard_map/all_to_all | solution.py:586
  925.3 17.4 %collective-permute-done.52.refs_1_ = bf16[512,2048]{1,0:T(8,128)(2,1)} collective-permute-done((bf16[512,2048]{1,0:T(8,128)(2,1)}, bf16[512,2048]{1,0:T(8,128)(2,1)}, u32[]{:S(2)}, u32[]{:S(2)}) %collective-permute-start.52) | collective-permute-done | bytes 2097184 | tf_op jit(solution)/shard_map/ppermute | solution.py:650
  943.1 9.2 combine.17
  952.4 5.0 all-to-all-start.24
  974.7 5.6 collective-permute-start.57
  990.1 40.7 %collective-permute-done.58 = bf16[4,512,512]{2,1,0:T(8,128)(2,1)} collective-permute-done((bf16[4,512,512]{2,1,0:T(8,128)(2,1)}, bf16[4,512,512]{2,1,0:T(8,128)(2,1)}, u32[]{:S(2)}, u32[]{:S(2)}) %collective-permute-start.58) | collective-permute-done | bytes 2097184 | tf_op jit(solution)/shard_map/ppermute | solution.py:650
  1030.7 7.7 combine.18
  1038.4 12.8 %all-to-all-start.25 = ((bf16[4,256,512]{2,1,0:T(8,128)(2,1)}), bf16[4,256,512]{2,1,0:T(8,128)(2,1)}, u32[]{:S(2)}, u32[]{:S(2)}) async-start(bf16[4,256,512]{2,1,0:T(8,128)(2,1)} %all-to-all-done.23), calls=%async_computation.25 | async-start | bytes 2097152 | tf_op jit(solution)/shard_map/all_to_all | solution.py:607
  1053.8 23.6 %all-to-all-done.25 = bf16[4,256,512]{2,1,0:T(8,128)(2,1)} async-done(((bf16[4,256,512]{2,1,0:T(8,128)(2,1)}), bf16[4,256,512]{2,1,0:T(8,128)(2,1)}, u32[]{:S(2)}, u32[]{:S(2)}) %all-to-all-start.25) | async-done | bytes 1048608 | tf_op jit(solution)/shard_map/all_to_all | solution.py:607
  1083.6 28.4 %collective-permute-done.60 = f32[2,28099]{1,0:T(2,128)S(1)} collective-permute-done((f32[2,28099]{1,0:T(2,128)S(1)}, f32[2,28099]{1,0:T(2,128)S(1)}, u32[]{:S(2)}, u32[]{:S(2)}) %collective-permute-start.60) | collective-permute-done | bytes 224824 | tf_op jit(solution)/shard_map/ppermute | solution.py:621
  1113.4 5.1 collective-permute-done.61
  1179.4 7.0 place_in.2.refs_5_
  1186.4 8.8 place_in.3
  (557 shorter events, 471.9 us)
Async XLA Ops:
  60.0 31.6 %all-to-all-start.3 = ((bf16[4,512,512]{2,1,0:T(8,128)(2,1)}), bf16[4,512,512]{2,1,0:T(8,128)(2,1)}, u32[]{:S(2)}, u32[]{:S(2)}) async-start(bf16[4,512,512]{2,1,0:T(8,128)(2,1)} %broadcast_in_dim.48), calls=%async_computation.3 | async-start | bytes 4194304 | tf_op jit(solution)/shard_map/all_to_all | solution.py:586
  64.7 35.7 %collective-permute-start.4 = (bf16[1296,512]{1,0:T(8,128)(2,1)S(1)}, bf16[1296,512]{1,0:T(8,128)(2,1)}, u32[]{:S(2)}, u32[]{:S(2)}) collective-permute-start(bf16[1296,512]{1,0:T(8,128)(2,1)S(1)} %get-tuple-element.245.refs_0_.refs_4_), channel_id=1, source_target_pairs={{0,16},{1,17},{2,18},{3,19},{4,20},{5,21},{6,22},{7,23},{8,24},{9,... | collective-permute-start | bytes 3981320 | tf_op jit(solution)/shard_map/ppermute | solution.py:792
  66.0 37.0 %collective-permute-start.5 = (bf16[1296,512]{1,0:T(8,128)(2,1)}, bf16[1296,512]{1,0:T(8,128)(2,1)}, u32[]{:S(2)}, u32[]{:S(2)}) collective-permute-start(bf16[1296,512]{1,0:T(8,128)(2,1)} %collective-permute-done.refs_1_.refs_5_), channel_id=1, source_target_pairs={{0,16},{1,17},{2,18},{3,19},{4,20},{5,21},{6,22},{7,23},{8,24},{9,... | collective-permute-start | bytes 3981320 | tf_op jit(solution)/shard_map/ppermute | solution.py:792
  67.3 38.0 %collective-permute-start.6 = (bf16[1296,512]{1,0:T(8,128)(2,1)}, bf16[1296,512]{1,0:T(8,128)(2,1)}, u32[]{:S(2)}, u32[]{:S(2)}) collective-permute-start(bf16[1296,512]{1,0:T(8,128)(2,1)} %collective-permute-done.1.refs_2_.refs_6_), channel_id=1, source_target_pairs={{0,16},{1,17},{2,18},{3,19},{4,20},{5,21},{6,22},{7,23},{8,24},{9,... | collective-permute-start | bytes 3981320 | tf_op jit(solution)/shard_map/ppermute | solution.py:792
  68.6 39.2 %collective-permute-start.7 = (bf16[1296,512]{1,0:T(8,128)(2,1)}, bf16[1296,512]{1,0:T(8,128)(2,1)}, u32[]{:S(2)}, u32[]{:S(2)}) collective-permute-start(bf16[1296,512]{1,0:T(8,128)(2,1)} %collective-permute-done.2.refs_3_.refs_7_), channel_id=1, source_target_pairs={{0,16},{1,17},{2,18},{3,19},{4,20},{5,21},{6,22},{7,23},{8,24},{9,... | collective-permute-start | bytes 3981320 | tf_op jit(solution)/shard_map/ppermute | solution.py:792
  116.5 102.3 %collective-permute-start.19 = (bf16[1024,2048]{1,0:T(8,128)(2,1)}, bf16[1024,2048]{1,0:T(8,128)(2,1)}, u32[]{:S(2)}, u32[]{:S(2)}) collective-permute-start(bf16[1024,2048]{1,0:T(8,128)(2,1)} %bitcast.36), channel_id=1, source_target_pairs={{0,16},{16,0},{1,17},{17,1},{2,18},{18,2},{3,19},{19,3},{4,20},{20... | collective-permute-start | bytes 12582920 | tf_op jit(solution)/shard_map/ppermute | solution.py:578
  161.9 26.8 %collective-permute-start.16 = (bf16[1296,512]{1,0:T(8,128)(2,1)}, bf16[1296,512]{1,0:T(8,128)(2,1)}, u32[]{:S(2)}, u32[]{:S(2)}) collective-permute-start(bf16[1296,512]{1,0:T(8,128)(2,1)} %get-tuple-element.233), channel_id=1, source_target_pairs={{16,17},{17,16},{18,19},{19,18},{20,21},{21,20},{22,23},{23,22},{2... | collective-permute-start | bytes 3981320 | tf_op jit(solution)/shard_map/ppermute | solution.py:767
  164.1 37.3 %collective-permute-start.17 = (bf16[1296,512]{1,0:T(8,128)(2,1)}, bf16[1296,512]{1,0:T(8,128)(2,1)}, u32[]{:S(2)}, u32[]{:S(2)}) collective-permute-start(bf16[1296,512]{1,0:T(8,128)(2,1)} %get-tuple-element.234), channel_id=1, source_target_pairs={{16,18},{17,19},{18,16},{19,17},{20,22},{21,23},{22,20},{23,21},{2... | collective-permute-start | bytes 3981320 | tf_op jit(solution)/shard_map/ppermute | solution.py:767
  167.3 34.1 %collective-permute-start.18 = (bf16[1296,512]{1,0:T(8,128)(2,1)}, bf16[1296,512]{1,0:T(8,128)(2,1)}, u32[]{:S(2)}, u32[]{:S(2)}) collective-permute-start(bf16[1296,512]{1,0:T(8,128)(2,1)} %get-tuple-element.235), channel_id=1, source_target_pairs={{16,19},{17,18},{18,17},{19,16},{20,23},{21,22},{22,21},{23,20},{2... | collective-permute-start | bytes 3981320 | tf_op jit(solution)/shard_map/ppermute | solution.py:767
  170.4 32.4 %all-to-all-start.5 = ((bf16[4,128,512]{1,2,0:T(8,128)(2,1)}), bf16[4,128,512]{1,2,0:T(8,128)(2,1)}, u32[]{:S(2)}, u32[]{:S(2)}) async-start(bf16[4,128,512]{1,2,0:T(8,128)(2,1)} %bitcast.305), calls=%async_computation.5 | async-start | bytes 1048576 | tf_op jit(solution)/shard_map/all_to_all | solution.py:586
  236.8 52.6 %all-to-all-start.7 = ((f32[4,128,2048]{2,1,0:T(8,128)}), f32[4,128,2048]{2,1,0:T(8,128)}, u32[]{:S(2)}, u32[]{:S(2)}) async-start(f32[4,128,2048]{2,1,0:T(8,128)} %bitcast.288), calls=%async_computation.7 | async-start | bytes 8388608 | tf_op jit(solution)/shard_map/all_to_all | solution.py:586
  244.8 63.1 %collective-permute-start.24 = (bf16[1024,512]{1,0:T(8,128)(2,1)}, bf16[1024,512]{1,0:T(8,128)(2,1)}, u32[]{:S(2)}, u32[]{:S(2)}) collective-permute-start(bf16[1024,512]{1,0:T(8,128)(2,1)} %get-tuple-element.251), channel_id=1, source_target_pairs={{16,17},{17,16},{18,19},{19,18},{20,21},{21,20},{22,23},{23,22},{2... | collective-permute-start | bytes 3145736 | tf_op jit(solution)/shard_map/ppermute | solution.py:767
  251.5 58.7 %collective-permute-start.25 = (bf16[1024,512]{1,0:T(8,128)(2,1)}, bf16[1024,512]{1,0:T(8,128)(2,1)}, u32[]{:S(2)}, u32[]{:S(2)}) collective-permute-start(bf16[1024,512]{1,0:T(8,128)(2,1)} %get-tuple-element.252), channel_id=1, source_target_pairs={{16,18},{17,19},{18,16},{19,17},{20,22},{21,23},{22,20},{23,21},{2... | collective-permute-start | bytes 3145736 | tf_op jit(solution)/shard_map/ppermute | solution.py:767
  297.8 46.0 %all-to-all-start.8 = ((bf16[4,128,2048]{2,1,0:T(8,128)(2,1)}), bf16[4,128,2048]{2,1,0:T(8,128)(2,1)}, u32[]{:S(2)}, u32[]{:S(2)}) async-start(bf16[4,128,2048]{2,1,0:T(8,128)(2,1)} %broadcast_in_dim.53), calls=%async_computation.8 | async-start | bytes 4194304 | tf_op jit(solution)/shard_map/all_to_all | solution.py:586
  302.3 37.2 %collective-permute-start.20 = (bf16[1296,512]{1,0:T(8,128)(2,1)S(1)}, bf16[1296,512]{1,0:T(8,128)(2,1)S(1)}, u32[]{:S(2)}, u32[]{:S(2)}) collective-permute-start(bf16[1296,512]{1,0:T(8,128)(2,1)S(1)} %get-tuple-element.245.refs_0_.refs_4_), channel_id=1, source_target_pairs={{16,0},{17,1},{18,2},{19,3},{20,4},{21,5},{22,6},{23,7},{24,8},{25... | collective-permute-start | bytes 3981320 | tf_op jit(solution)/shard_map/ppermute | solution.py:903
  305.1 35.5 %collective-permute-start.21 = (bf16[1296,512]{1,0:T(8,128)(2,1)}, bf16[1296,512]{1,0:T(8,128)(2,1)S(1)}, u32[]{:S(2)}, u32[]{:S(2)}) collective-permute-start(bf16[1296,512]{1,0:T(8,128)(2,1)} %collective-permute-done.16.refs_1_.refs_5_), channel_id=1, source_target_pairs={{16,0},{17,1},{18,2},{19,3},{20,4},{21,5},{22,6},{23,7},{24,8},{25... | collective-permute-start | bytes 3981320 | tf_op jit(solution)/shard_map/ppermute | solution.py:903
  306.5 35.2 %collective-permute-start.22 = (bf16[1296,512]{1,0:T(8,128)(2,1)}, bf16[1296,512]{1,0:T(8,128)(2,1)S(1)}, u32[]{:S(2)}, u32[]{:S(2)}) collective-permute-start(bf16[1296,512]{1,0:T(8,128)(2,1)} %collective-permute-done.17.refs_2_.refs_6_), channel_id=1, source_target_pairs={{16,0},{17,1},{18,2},{19,3},{20,4},{21,5},{22,6},{23,7},{24,8},{25... | collective-permute-start | bytes 3981320 | tf_op jit(solution)/shard_map/ppermute | solution.py:903
  307.9 36.0 %collective-permute-start.23 = (bf16[1296,512]{1,0:T(8,128)(2,1)}, bf16[1296,512]{1,0:T(8,128)(2,1)}, u32[]{:S(2)}, u32[]{:S(2)}) collective-permute-start(bf16[1296,512]{1,0:T(8,128)(2,1)} %collective-permute-done.18.refs_3_.refs_7_), channel_id=1, source_target_pairs={{16,0},{17,1},{18,2},{19,3},{20,4},{21,5},{22,6},{23,7},{24,8},{25... | collective-permute-start | bytes 3981320 | tf_op jit(solution)/shard_map/ppermute | solution.py:903
  310.3 29.3 %collective-permute-start.26 = (bf16[1024,512]{1,0:T(8,128)(2,1)}, bf16[1024,512]{1,0:T(8,128)(2,1)S(1)}, u32[]{:S(2)}, u32[]{:S(2)}) collective-permute-start(bf16[1024,512]{1,0:T(8,128)(2,1)} %get-tuple-element.253), channel_id=1, source_target_pairs={{16,19},{17,18},{18,17},{19,16},{20,23},{21,22},{22,21},{23,20},{2... | collective-permute-start | bytes 3145736 | tf_op jit(solution)/shard_map/ppermute | solution.py:767
  348.4 41.1 %all-to-all-start.9 = ((bf16[4,512,512]{2,1,0:T(8,128)(2,1)}), bf16[4,512,512]{2,1,0:T(8,128)(2,1)}, u32[]{:S(2)}, u32[]{:S(2)}) async-start(bf16[4,512,512]{2,1,0:T(8,128)(2,1)} %broadcast_in_dim.55), calls=%async_computation.9 | async-start | bytes 4194304 | tf_op jit(solution)/shard_map/all_to_all | solution.py:586
  352.9 27.0 %collective-permute-start.27 = (bf16[1024,512]{1,0:T(8,128)(2,1)S(1)}, bf16[1024,512]{1,0:T(8,128)(2,1)S(1)}, u32[]{:S(2)}, u32[]{:S(2)}) collective-permute-start(bf16[1024,512]{1,0:T(8,128)(2,1)S(1)} %get-tuple-element.264.refs_0_), channel_id=1, source_target_pairs={{16,0},{17,1},{18,2},{19,3},{20,4},{21,5},{22,6},{23,7},{24,8},{25... | collective-permute-start | bytes 3145736 | tf_op jit(solution)/shard_map/ppermute | solution.py:910
  354.3 25.6 %collective-permute-start.28 = (bf16[1024,512]{1,0:T(8,128)(2,1)}, bf16[1024,512]{1,0:T(8,128)(2,1)S(1)}, u32[]{:S(2)}, u32[]{:S(2)}) collective-permute-start(bf16[1024,512]{1,0:T(8,128)(2,1)} %collective-permute-done.24.refs_1_), channel_id=1, source_target_pairs={{16,0},{17,1},{18,2},{19,3},{20,4},{21,5},{22,6},{23,7},{24,8},{25... | collective-permute-start | bytes 3145736 | tf_op jit(solution)/shard_map/ppermute | solution.py:910
  421.6 46.7 %collective-permute-start.32 = (bf16[512,2048]{1,0:T(8,128)(2,1)}, bf16[512,2048]{1,0:T(8,128)(2,1)}, u32[]{:S(2)}, u32[]{:S(2)}) collective-permute-start(bf16[512,2048]{1,0:T(8,128)(2,1)} %add_convert_fusion.5.refs_0_), channel_id=1, source_target_pairs={{0,4},{12,8},{1,5},{13,9},{2,6},{14,10},{3,7},{15,11},{16,20},{28,... | collective-permute-start | bytes 6291464 | tf_op jit(solution)/shard_map/ppermute | solution.py:650
  427.9 29.4 %all-to-all-start.11 = ((bf16[4,128,2048]{2,1,0:T(8,128)(2,1)}), bf16[4,128,2048]{2,1,0:T(8,128)(2,1)}, u32[]{:S(2)}, u32[]{:S(2)}) async-start(bf16[4,128,2048]{2,1,0:T(8,128)(2,1)} %bitcast.302), calls=%async_computation.11 | async-start | bytes 4194304 | tf_op jit(solution)/shard_map/all_to_all | solution.py:586
  478.8 33.5 %collective-permute-start.33 = (bf16[2048,512]{1,0:T(8,128)(2,1)}, bf16[2048,512]{1,0:T(8,128)(2,1)}, u32[]{:S(2)}, u32[]{:S(2)}) collective-permute-start(bf16[2048,512]{1,0:T(8,128)(2,1)} %convolution_convert_fusion.5), channel_id=1, source_target_pairs={{0,16},{16,0},{1,17},{17,1},{2,18},{18,2},{3,19},{19,3},{4,20},{20... | collective-permute-start | bytes 6291464 | tf_op jit(solution)/shard_map/ppermute | solution.py:578
  479.4 37.7 %collective-permute-start.34 = (bf16[512,2048]{1,0:T(8,128)(2,1)}, bf16[512,2048]{1,0:T(8,128)(2,1)}, u32[]{:S(2)}, u32[]{:S(2)}) collective-permute-start(bf16[512,2048]{1,0:T(8,128)(2,1)} %combine.10.refs_0_), channel_id=1, source_target_pairs={{4,8},{8,4},{5,9},{9,5},{6,10},{10,6},{7,11},{11,7},{20,24},{24,20... | collective-permute-start | bytes 6291464 | tf_op jit(solution)/shard_map/ppermute | solution.py:650
  523.1 80.9 %all-to-all-start.13 = ((f32[4,128,2048]{2,1,0:T(8,128)}), f32[4,128,2048]{2,1,0:T(8,128)}, u32[]{:S(2)}, u32[]{:S(2)}) async-start(f32[4,128,2048]{2,1,0:T(8,128)} %bitcast.281), calls=%async_computation.13 | async-start | bytes 8388608 | tf_op jit(solution)/shard_map/all_to_all | solution.py:586
  528.2 60.9 %collective-permute-start.37 = (bf16[512,2048]{1,0:T(8,128)(2,1)}, bf16[512,2048]{1,0:T(8,128)(2,1)}, u32[]{:S(2)}, u32[]{:S(2)}) collective-permute-start(bf16[512,2048]{1,0:T(8,128)(2,1)} %copy-done.5), channel_id=1, source_target_pairs={{4,0},{8,12},{5,1},{9,13},{6,2},{10,14},{7,3},{11,15},{20,16},{24,... | collective-permute-start | bytes 6291464 | tf_op jit(solution)/shard_map/ppermute | solution.py:650
  529.6 61.7 %collective-permute-start.38 = (bf16[4,512,512]{2,1,0:T(8,128)(2,1)}, bf16[4,512,512]{2,1,0:T(8,128)(2,1)}, u32[]{:S(2)}, u32[]{:S(2)}) collective-permute-start(bf16[4,512,512]{2,1,0:T(8,128)(2,1)} %bitcast.307), channel_id=1, source_target_pairs={{0,4},{12,8},{1,5},{13,9},{2,6},{14,10},{3,7},{15,11},{16,20},{28,... | collective-permute-start | bytes 6291464 | tf_op jit(solution)/shard_map/ppermute | solution.py:650
  552.3 45.9 %collective-permute-start.35 = (bf16[2048,512]{1,0:T(8,128)(2,1)}, bf16[2048,512]{1,0:T(8,128)(2,1)}, u32[]{:S(2)}, u32[]{:S(2)}) collective-permute-start(bf16[2048,512]{1,0:T(8,128)(2,1)} %convolution_convert_fusion.4), channel_id=1, source_target_pairs={{0,16},{16,0},{1,17},{17,1},{2,18},{18,2},{3,19},{19,3},{4,20},{20... | collective-permute-start | bytes 6291464 | tf_op jit(solution)/shard_map/ppermute | solution.py:578
  607.7 26.0 %collective-permute-start.39 = (bf16[4,512,512]{2,1,0:T(8,128)(2,1)}, bf16[4,512,512]{2,1,0:T(8,128)(2,1)}, u32[]{:S(2)}, u32[]{:S(2)}) collective-permute-start(bf16[4,512,512]{2,1,0:T(8,128)(2,1)} %bitcast.273), channel_id=1, source_target_pairs={{4,8},{8,4},{5,9},{9,5},{6,10},{10,6},{7,11},{11,7},{20,24},{24,20... | collective-permute-start | bytes 6291464 | tf_op jit(solution)/shard_map/ppermute | solution.py:650
  609.8 53.3 %collective-permute-start.40 = (bf16[4,576,512]{2,1,0:T(8,128)(2,1)}, bf16[4,576,512]{2,1,0:T(8,128)(2,1)}, u32[]{:S(2)}, u32[]{:S(2)}) collective-permute-start(bf16[4,576,512]{2,1,0:T(8,128)(2,1)} %pad_maximum_fusion.4), channel_id=1, source_target_pairs={{0,4},{12,8},{1,5},{13,9},{2,6},{14,10},{3,7},{15,11},{16,20},{28,... | collective-permute-start | bytes 7077896 | tf_op jit(solution)/shard_map/ppermute | solution.py:650
  629.1 42.9 %all-to-all-start.14 = ((bf16[4,128,2048]{2,1,0:T(8,128)(2,1)}), bf16[4,128,2048]{2,1,0:T(8,128)(2,1)}, u32[]{:S(2)}, u32[]{:S(2)}) async-start(bf16[4,128,2048]{2,1,0:T(8,128)(2,1)} %broadcast_in_dim.59), calls=%async_computation.14 | async-start | bytes 4194304 | tf_op jit(solution)/shard_map/all_to_all | solution.py:586
  676.5 39.6 %collective-permute-start.41 = (bf16[512,2048]{1,0:T(8,128)(2,1)}, bf16[512,2048]{1,0:T(8,128)(2,1)}, u32[]{:S(2)}, u32[]{:S(2)}) collective-permute-start(bf16[512,2048]{1,0:T(8,128)(2,1)} %convolution_convert_fusion.3), channel_id=1, source_target_pairs={{0,16},{16,0},{1,17},{17,1},{2,18},{18,2},{3,19},{19,3},{4,20},{20... | collective-permute-start | bytes 6291464 | tf_op jit(solution)/shard_map/ppermute | solution.py:578
  679.4 52.6 %collective-permute-start.43 = (bf16[4,576,512]{2,1,0:T(8,128)(2,1)}, bf16[4,576,512]{2,1,0:T(8,128)(2,1)}, u32[]{:S(2)}, u32[]{:S(2)}) collective-permute-start(bf16[4,576,512]{2,1,0:T(8,128)(2,1)} %bitcast.73), channel_id=1, source_target_pairs={{4,8},{8,4},{5,9},{9,5},{6,10},{10,6},{7,11},{11,7},{20,24},{24,20... | collective-permute-start | bytes 7077896 | tf_op jit(solution)/shard_map/ppermute | solution.py:650
  681.4 50.5 %collective-permute-start.42 = (bf16[4,512,512]{2,1,0:T(8,128)(2,1)}, bf16[4,512,512]{2,1,0:T(8,128)(2,1)}, u32[]{:S(2)}, u32[]{:S(2)}) collective-permute-start(bf16[4,512,512]{2,1,0:T(8,128)(2,1)} %bitcast.72), channel_id=1, source_target_pairs={{4,0},{8,12},{5,1},{9,13},{6,2},{10,14},{7,3},{11,15},{20,16},{24,... | collective-permute-start | bytes 6291464 | tf_op jit(solution)/shard_map/ppermute | solution.py:650
  684.9 55.5 %all-to-all-start.16 = ((bf16[4,256,512]{2,1,0:T(8,128)(2,1)}), bf16[4,256,512]{2,1,0:T(8,128)(2,1)}, u32[]{:S(2)}, u32[]{:S(2)}) async-start(bf16[4,256,512]{2,1,0:T(8,128)(2,1)} %bitcast.263), calls=%async_computation.16 | async-start | bytes 2097152 | tf_op jit(solution)/shard_map/all_to_all | solution.py:586
  744.6 34.0 %collective-permute-start.45 = (bf16[2048,512]{1,0:T(8,128)(2,1)}, bf16[2048,512]{1,0:T(8,128)(2,1)}, u32[]{:S(2)}, u32[]{:S(2)}) collective-permute-start(bf16[2048,512]{1,0:T(8,128)(2,1)} %convolution_convert_fusion.1), channel_id=1, source_target_pairs={{0,16},{16,0},{1,17},{17,1},{2,18},{18,2},{3,19},{19,3},{4,20},{20... | collective-permute-start | bytes 6291464 | tf_op jit(solution)/shard_map/ppermute | solution.py:578
  748.0 35.1 %collective-permute-start.44 = (bf16[2048,512]{1,0:T(8,128)(2,1)}, bf16[2048,512]{1,0:T(8,128)(2,1)}, u32[]{:S(2)}, u32[]{:S(2)}) collective-permute-start(bf16[2048,512]{1,0:T(8,128)(2,1)} %convolution_convert_fusion.2), channel_id=1, source_target_pairs={{0,16},{16,0},{1,17},{17,1},{2,18},{18,2},{3,19},{19,3},{4,20},{20... | collective-permute-start | bytes 6291464 | tf_op jit(solution)/shard_map/ppermute | solution.py:578
  748.1 63.6 %collective-permute-start.47 = (bf16[4,576,512]{2,1,0:T(8,128)(2,1)}, bf16[4,576,512]{2,1,0:T(8,128)(2,1)}, u32[]{:S(2)}, u32[]{:S(2)}) collective-permute-start(bf16[4,576,512]{2,1,0:T(8,128)(2,1)} %bitcast.80), channel_id=1, source_target_pairs={{4,0},{8,12},{5,1},{9,13},{6,2},{10,14},{7,3},{11,15},{20,16},{24,... | collective-permute-start | bytes 7077896 | tf_op jit(solution)/shard_map/ppermute | solution.py:650
  755.1 52.8 %collective-permute-start.48 = (bf16[512,2048]{1,0:T(8,128)(2,1)}, bf16[512,2048]{1,0:T(8,128)(2,1)}, u32[]{:S(2)}, u32[]{:S(2)}) collective-permute-start(bf16[512,2048]{1,0:T(8,128)(2,1)} %add_convert_fusion.2.refs_2_), channel_id=1, source_target_pairs={{0,4},{12,8},{1,5},{13,9},{2,6},{14,10},{3,7},{15,11},{16,20},{28,... | collective-permute-start | bytes 6291464 | tf_op jit(solution)/shard_map/ppermute | solution.py:650
  766.4 58.4 %all-to-all-start.18 = ((bf16[4,256,512]{2,1,0:T(8,128)(2,1)}), bf16[4,256,512]{2,1,0:T(8,128)(2,1)}, u32[]{:S(2)}, u32[]{:S(2)}) async-start(bf16[4,256,512]{2,1,0:T(8,128)(2,1)} %all-to-all-done.16), calls=%async_computation.18 | async-start | bytes 2097152 | tf_op jit(solution)/shard_map/all_to_all | solution.py:607
  829.1 31.9 %collective-permute-start.49 = (bf16[512,2048]{1,0:T(8,128)(2,1)}, bf16[512,2048]{1,0:T(8,128)(2,1)}, u32[]{:S(2)}, u32[]{:S(2)}) collective-permute-start(bf16[512,2048]{1,0:T(8,128)(2,1)} %copy-done.29), channel_id=1, source_target_pairs={{4,8},{8,4},{5,9},{9,5},{6,10},{10,6},{7,11},{11,7},{20,24},{24,20... | collective-permute-start | bytes 6291464 | tf_op jit(solution)/shard_map/ppermute | solution.py:650
  831.2 48.7 %collective-permute-start.50 = (bf16[4,512,512]{2,1,0:T(8,128)(2,1)}, bf16[4,512,512]{2,1,0:T(8,128)(2,1)}, u32[]{:S(2)}, u32[]{:S(2)}) collective-permute-start(bf16[4,512,512]{2,1,0:T(8,128)(2,1)} %bitcast.308), channel_id=1, source_target_pairs={{0,4},{12,8},{1,5},{13,9},{2,6},{14,10},{3,7},{15,11},{16,20},{28,... | collective-permute-start | bytes 6291464 | tf_op jit(solution)/shard_map/ppermute | solution.py:650
  842.2 45.3 %all-to-all-start.19 = ((bf16[4,576,512]{2,1,0:T(8,128)(2,1)}), bf16[4,576,512]{2,1,0:T(8,128)(2,1)}, u32[]{:S(2)}, u32[]{:S(2)}) async-start(bf16[4,576,512]{2,1,0:T(8,128)(2,1)} %pad_maximum_fusion.5), calls=%async_computation.19 | async-start | bytes 4718592 | tf_op jit(solution)/shard_map/all_to_all | solution.py:586
  887.5 28.0 %all-to-all-start.21 = ((bf16[4,128,2048]{2,1,0:T(8,128)(2,1)}), bf16[4,128,2048]{2,1,0:T(8,128)(2,1)S(1)}, u32[]{:S(2)}, u32[]{:S(2)}) async-start(bf16[4,128,2048]{2,1,0:T(8,128)(2,1)} %bitcast.91), calls=%async_computation.21 | async-start | bytes 4194304 | tf_op jit(solution)/shard_map/all_to_all | solution.py:586
  891.1 52.0 %collective-permute-start.54 = (bf16[4,576,512]{2,1,0:T(8,128)(2,1)}, bf16[4,576,512]{2,1,0:T(8,128)(2,1)}, u32[]{:S(2)}, u32[]{:S(2)}) collective-permute-start(bf16[4,576,512]{2,1,0:T(8,128)(2,1)} %all-to-all-done.19), channel_id=1, source_target_pairs={{0,4},{12,8},{1,5},{13,9},{2,6},{14,10},{3,7},{15,11},{16,20},{28,... | collective-permute-start | bytes 7077896 | tf_op jit(solution)/shard_map/ppermute | solution.py:650
  896.7 46.1 %collective-permute-start.52 = (bf16[512,2048]{1,0:T(8,128)(2,1)}, bf16[512,2048]{1,0:T(8,128)(2,1)}, u32[]{:S(2)}, u32[]{:S(2)}) collective-permute-start(bf16[512,2048]{1,0:T(8,128)(2,1)} %get-tuple-element.335.refs_0_), channel_id=1, source_target_pairs={{4,0},{8,12},{5,1},{9,13},{6,2},{10,14},{7,3},{11,15},{20,16},{24,... | collective-permute-start | bytes 6291464 | tf_op jit(solution)/shard_map/ppermute | solution.py:650
  898.0 44.8 %collective-permute-start.53 = (bf16[4,512,512]{2,1,0:T(8,128)(2,1)}, bf16[4,512,512]{2,1,0:T(8,128)(2,1)}, u32[]{:S(2)}, u32[]{:S(2)}) collective-permute-start(bf16[4,512,512]{2,1,0:T(8,128)(2,1)} %bitcast.90), channel_id=1, source_target_pairs={{4,8},{8,4},{5,9},{9,5},{6,10},{10,6},{7,11},{11,7},{20,24},{24,20... | collective-permute-start | bytes 6291464 | tf_op jit(solution)/shard_map/ppermute | solution.py:650
  899.9 57.5 %collective-permute-start.51 = (bf16[512,2048]{1,0:T(8,128)(2,1)}, bf16[512,2048]{1,0:T(8,128)(2,1)}, u32[]{:S(2)}, u32[]{:S(2)}) collective-permute-start(bf16[512,2048]{1,0:T(8,128)(2,1)} %get-tuple-element.371), channel_id=1, source_target_pairs={{0,16},{1,17},{2,18},{3,19},{4,20},{5,21},{6,22},{7,23},{8,24},{9,... | collective-permute-start | bytes 6291464 | tf_op jit(solution)/shard_map/ppermute | solution.py:1071
  916.8 35.5 %all-to-all-start.22 = ((bf16[4,512,512]{2,1,0:T(8,128)(2,1)}), bf16[4,512,512]{2,1,0:T(8,128)(2,1)S(1)}, u32[]{:S(2)}, u32[]{:S(2)}) async-start(bf16[4,512,512]{2,1,0:T(8,128)(2,1)} %bitcast.274), calls=%async_computation.22 | async-start | bytes 4194304 | tf_op jit(solution)/shard_map/all_to_all | solution.py:586
  952.4 32.3 %all-to-all-start.24 = ((bf16[4,576,512]{2,1,0:T(8,128)(2,1)}), bf16[4,576,512]{2,1,0:T(8,128)(2,1)}, u32[]{:S(2)}, u32[]{:S(2)}) async-start(bf16[4,576,512]{2,1,0:T(8,128)(2,1)} %bitcast.299), calls=%async_computation.24 | async-start | bytes 4718592 | tf_op jit(solution)/shard_map/all_to_all | solution.py:586
  973.5 65.0 %collective-permute-start.56 = (bf16[4,512,512]{2,1,0:T(8,128)(2,1)S(1)}, bf16[4,512,512]{2,1,0:T(8,128)(2,1)}, u32[]{:S(2)}, u32[]{:S(2)}) collective-permute-start(bf16[4,512,512]{2,1,0:T(8,128)(2,1)S(1)} %all-to-all-done.22.refs_1_), channel_id=1, source_target_pairs={{0,16},{1,17},{2,18},{3,19},{4,20},{5,21},{6,22},{7,23},{8,24},{9,... | collective-permute-start | bytes 6291464 | tf_op jit(solution)/shard_map/ppermute | solution.py:1071
  974.7 63.7 %collective-permute-start.57 = (bf16[512,2048]{1,0:T(8,128)(2,1)}, bf16[512,2048]{1,0:T(8,128)(2,1)}, u32[]{:S(2)}, u32[]{:S(2)}) collective-permute-start(bf16[512,2048]{1,0:T(8,128)(2,1)} %get-tuple-element.370), channel_id=1, source_target_pairs={{16,0},{17,1},{18,2},{19,3},{20,4},{21,5},{22,6},{23,7},{24,8},{25... | collective-permute-start | bytes 6291464 | tf_op jit(solution)/shard_map/ppermute | solution.py:1071
  980.4 50.3 %collective-permute-start.58 = (bf16[4,512,512]{2,1,0:T(8,128)(2,1)}, bf16[4,512,512]{2,1,0:T(8,128)(2,1)}, u32[]{:S(2)}, u32[]{:S(2)}) collective-permute-start(bf16[4,512,512]{2,1,0:T(8,128)(2,1)} %bitcast.96), channel_id=1, source_target_pairs={{4,0},{8,12},{5,1},{9,13},{6,2},{10,14},{7,3},{11,15},{20,16},{24,... | collective-permute-start | bytes 6291464 | tf_op jit(solution)/shard_map/ppermute | solution.py:650
  981.7 49.1 %collective-permute-start.59 = (bf16[4,576,512]{2,1,0:T(8,128)(2,1)}, bf16[4,576,512]{2,1,0:T(8,128)(2,1)}, u32[]{:S(2)}, u32[]{:S(2)}) collective-permute-start(bf16[4,576,512]{2,1,0:T(8,128)(2,1)} %bitcast.97), channel_id=1, source_target_pairs={{4,8},{8,4},{5,9},{9,5},{6,10},{10,6},{7,11},{11,7},{20,24},{24,20... | collective-permute-start | bytes 7077896 | tf_op jit(solution)/shard_map/ppermute | solution.py:650
  984.6 53.8 %all-to-all-start.23 = ((bf16[4,256,512]{2,1,0:T(8,128)(2,1)}), bf16[4,256,512]{2,1,0:T(8,128)(2,1)}, u32[]{:S(2)}, u32[]{:S(2)}) async-start(bf16[4,256,512]{2,1,0:T(8,128)(2,1)} %bitcast.261), calls=%async_computation.23 | async-start | bytes 2097152 | tf_op jit(solution)/shard_map/all_to_all | solution.py:586
  1038.4 38.9 %all-to-all-start.25 = ((bf16[4,256,512]{2,1,0:T(8,128)(2,1)}), bf16[4,256,512]{2,1,0:T(8,128)(2,1)}, u32[]{:S(2)}, u32[]{:S(2)}) async-start(bf16[4,256,512]{2,1,0:T(8,128)(2,1)} %all-to-all-done.23), calls=%async_computation.25 | async-start | bytes 2097152 | tf_op jit(solution)/shard_map/all_to_all | solution.py:607
  1051.2 70.1 %collective-permute-start.63 = (bf16[4,576,512]{2,1,0:T(8,128)(2,1)}, bf16[4,576,512]{2,1,0:T(8,128)(2,1)S(1)}, u32[]{:S(2)}, u32[]{:S(2)}) collective-permute-start(bf16[4,576,512]{2,1,0:T(8,128)(2,1)} %bitcast.272), channel_id=1, source_target_pairs={{4,0},{8,12},{5,1},{9,13},{6,2},{10,14},{7,3},{11,15},{20,16},{24,... | collective-permute-start | bytes 7077896 | tf_op jit(solution)/shard_map/ppermute | solution.py:650
  1052.5 76.1 %collective-permute-start.62 = (bf16[4,576,512]{2,1,0:T(8,128)(2,1)}, bf16[4,576,512]{2,1,0:T(8,128)(2,1)}, u32[]{:S(2)}, u32[]{:S(2)}) collective-permute-start(bf16[4,576,512]{2,1,0:T(8,128)(2,1)} %all-to-all-done.24.refs_1_), channel_id=1, source_target_pairs={{0,16},{1,17},{2,18},{3,19},{4,20},{5,21},{6,22},{7,23},{8,24},{9,... | collective-permute-start | bytes 7077896 | tf_op jit(solution)/shard_map/ppermute | solution.py:1071
  1077.3 51.2 %all-to-all-start.26 = ((bf16[4,512,512]{2,1,0:T(8,128)(2,1)}), bf16[4,512,512]{2,1,0:T(8,128)(2,1)}, u32[]{:S(2)}, u32[]{:S(2)}) async-start(bf16[4,512,512]{2,1,0:T(8,128)(2,1)} %bitcast.110), calls=%async_computation.26 | async-start | bytes 4194304 | tf_op jit(solution)/shard_map/all_to_all | solution.py:586
  1081.8 30.2 %collective-permute-start.60 = (f32[2,28099]{1,0:T(2,128)S(1)}, f32[2,28099]{1,0:T(2,128)S(1)}, u32[]{:S(2)}, u32[]{:S(2)}) collective-permute-start(f32[2,28099]{1,0:T(2,128)S(1)} %fusion.107), channel_id=1, source_target_pairs={{0,1},{1,0},{2,3},{3,2},{4,5},{5,4},{6,7},{7,6},{8,9},{9,8},{10,11... | collective-permute-start | bytes 674384 | tf_op jit(solution)/shard_map/ppermute | solution.py:621
  1145.7 32.3 %collective-permute-start.68 = (bf16[4,512,512]{2,1,0:T(8,128)(2,1)}, bf16[4,512,512]{2,1,0:T(8,128)(2,1)}, u32[]{:S(2)}, u32[]{:S(2)}) collective-permute-start(bf16[4,512,512]{2,1,0:T(8,128)(2,1)} %all-to-all-done.26.refs_0_), channel_id=1, source_target_pairs={{16,0},{17,1},{18,2},{19,3},{20,4},{21,5},{22,6},{23,7},{24,8},{25... | collective-permute-start | bytes 6291464 | tf_op jit(solution)/shard_map/ppermute | solution.py:1071
  1150.2 26.5 %collective-permute-start.67 = (bf16[4,576,512]{2,1,0:T(8,128)(2,1)S(1)}, bf16[4,576,512]{2,1,0:T(8,128)(2,1)}, u32[]{:S(2)}, u32[]{:S(2)}) collective-permute-start(bf16[4,576,512]{2,1,0:T(8,128)(2,1)S(1)} %bitcast.269), channel_id=1, source_target_pairs={{16,0},{17,1},{18,2},{19,3},{20,4},{21,5},{22,6},{23,7},{24,8},{25... | collective-permute-start | bytes 7077896 | tf_op jit(solution)/shard_map/ppermute | solution.py:1071
  (120 other events, 1448.1 us)

commit v8 on v7

--- a/solution.py
+++ b/solution.py
@@ -547,33 +547,6 @@
     )(ids, *arrays, small, *before)
 
 
-def combine_kernel(flags, *refs, adds):
-    count = len(adds)
-    for k, add in enumerate(adds):
-        v, got, out = refs[2 * k], refs[2 * k + 1], refs[2 * count + k]
-        if add:
-            out[...] = (v[...].astype(F32) + got[...].astype(F32)).astype(BF16)
-        else:
-            out[...] = jnp.where(flags[k] == 1, got[...], v[...])
-
-
-def combine(items, flags):
-    steps = 8
-    shapes = [v.shape for v, _, _ in items]
-    flat = [(v.reshape(-1, v.shape[-1]), g.reshape(-1, g.shape[-1])) for v, g, _ in items]
-    spec = lambda v: pl.BlockSpec((v.shape[0] // steps, v.shape[1]), lambda i: (i, 0))
-    out = pl.pallas_call(
-        functools.partial(combine_kernel, adds=tuple(add for _, _, add in items)),
-        grid=(steps,),
-        in_specs=[pl.BlockSpec(memory_space=pltpu.SMEM)] + [spec(v) for p in flat for v in p],
-        out_specs=[spec(v) for v, _ in flat],
-        out_shape=[jax.ShapeDtypeStruct(v.shape, BF16) for v, _ in flat],
-        compiler_params=pltpu.CompilerParams(vmem_limit_bytes=VMEM_BYTES),
-        name="combine",
-    )(flags, *[v for p in flat for v in p])
-    return [v.reshape(shape) for v, shape in zip(out, shapes)]
-
-
 def swap_section(v):
     return lax.ppermute(v, "section", [(0, 1), (1, 0)])
 
@@ -628,52 +601,13 @@
 
 class SeqSums:
     def __init__(self):
-        s = lax.axis_size("seq")
-        half = s // 2
-        self.pairs = [[(j, j + 1), (s - 1 - j, s - 2 - j)] for j in range(half - 1)]
-        self.pairs.append([(half - 1, half), (half, half - 1)])
-        self.inward = half
-        self.pairs += [[(j + 1, j), (s - 2 - j, s - 1 - j)] for j in reversed(range(half - 1))]
-        self.values, self.phase, self.moving = [], [], []
-
-    def add(self, value):
-        self.values.append(value)
-        self.phase.append(0)
-        return len(self.values) - 1
-
-    def begin(self):
-        taken = set()
-        for k, step in enumerate(self.phase):
-            if step == len(self.pairs) or step in taken:
-                continue
-            taken.add(step)
-            self.moving.append((k, lax.ppermute(self.values[k], "seq", self.pairs[step])))
-
-    def end(self, work):
-        place = lax.axis_index("seq")
-        items, flags = [], []
-        for k, got in self.moving:
-            step = self.phase[k]
-            items.append((self.values[k], got, step < self.inward))
-            here = [place == to for _, to in self.pairs[step]]
-            flags.append(functools.reduce(jnp.logical_or, here))
-            self.phase[k] = step + 1
-        moved = combine(items, jnp.stack(flags).astype(jnp.int32)) if items else []
-        still = [k for k, p in enumerate(self.phase) if p == 0]
-        work, moved, rest = lax.optimization_barrier(
-            (work, moved, [self.values[k] for k in still])
-        )
-        for (k, _), v in zip(self.moving, moved):
-            self.values[k] = v
-        for k, v in zip(still, rest):
-            self.values[k] = v
-        self.moving = []
-        return work
-
-    def finish(self, chunks):
-        while any(self.phase[k] < len(self.pairs) for k in chunks):
-            self.begin()
-            self.end(())
+        self.last = None
+
+    def add(self, v):
+        if self.last is not None:
+            v, _ = lax.optimization_barrier((v, self.last))
+        self.last = lax.psum(v, "seq")
+        return self.last
 
 
 def relay(total, local, reverse):
@@ -1009,30 +943,27 @@
     sums = SeqSums()
     rc1 = scales(r1, (r1 * r1 * r1 / INNER) * stat1[1])
     away = away_out(normed1, dmixed1)
-    o1 = sums.add(own_out_piece(normed1, dmixed1, away))
-    rc1, normed1, dn1 = sums.end((rc1, normed1, dn1))
-
-    sums.begin()
+    go = own_out_piece(normed1, dmixed1, away)
+    rc1, normed1, dn1, go = tie((rc1, normed1, dn1, go))
+    o1 = sums.add(go)
+
     d1 = unscan(pz1, px1, fwd1, dn1, rc1, 1)
     mixed1 = scatter_sum(jnp.dot(normed1, wo[1], preferred_element_type=F32).astype(BF16))
-    d1, mixed1 = sums.end((d1, mixed1))
-
-    sums.begin()
+    d1, mixed1 = tie((d1, mixed1))
+
     away = away_in(normed_in1, d1[0])
     full1, xs1 = with_group(d1[1], d1[2])
     back1 = back_in(d1[0], full1, 1, F32)
     gz = own_in_piece(normed_in1, d1[0], away)
-    back1, xs1, full1, gz = sums.end((back1, xs1, full1, gz))
+    back1, xs1, gz = tie((back1, xs1, gz))
     z1 = sums.add(gz)
 
-    sums.begin()
     dnin1 = scatter_sum(back1)
     away = away_in(normed_in1, *xs1)
     gx = own_in_piece(normed_in1, xs1[0], away, xs1[1])
-    dnin1, gx = sums.end((dnin1, gx))
+    dnin1, gx, o1 = tie((dnin1, gx, o1))
     x1 = sums.add(gx)
 
-    sums.begin()
     grad1, dgin1 = back_norm(dout1, dnin1, h1, small[1][0])
     dout0 = grad1.astype(BF16).astype(F32)
     dmixed0_own = (valid * dout0).astype(BF16)
@@ -1040,78 +971,64 @@
     along0 = to_all(jnp.sum(dmixed0_own.astype(F32) * mixed0, axis=-1)).reshape(-1)
     rc0 = scales(r0, (r0 * r0 / INNER) * along0)
     out1 = valid * (h1.astype(F32) + mixed1)
-    grad1, dgin1, dmixed0, rc0, out1 = sums.end((grad1, dgin1, dmixed0, rc0, out1))
-
-    sums.begin()
+    grad1, dgin1, dmixed0, rc0, out1 = tie((grad1, dgin1, dmixed0, rc0, out1))
+
     back_h = exchange(quarters(jnp.concatenate([h1, out1.astype(BF16)])))
     dn0 = dot_cols(dmixed0, wo[0])
     d0 = unscan(pz0, px0, fwd0, dn0, rc0, 0)
     go = own_out_piece(normed0, dmixed0, away_out(normed0, dmixed0))
-    d0, go, back_h = sums.end((d0, go, back_h))
+    d0, go, back_h, z1 = tie((d0, go, back_h, z1))
     o0 = sums.add(go)
 
-    sums.begin()
-    back_h = in_group(back_h)
     away = away_in(normed_in0, d0[0])
     full0, xs0 = with_group(d0[1], d0[2])
     gz = own_in_piece(normed_in0, d0[0], away)
     away = away_in(normed_in0, *xs0)
     gx = own_in_piece(normed_in0, xs0[0], away, xs0[1])
-    full0, gz, gx, back_h = sums.end((full0, gz, gx, back_h))
+    full0, gz, gx, back_h = tie((full0, gz, gx, back_h))
     z0 = sums.add(gz)
-
-    sums.begin()
     gx = exchange(gx)
     back0 = back_in(d0[0], full0, 0, BF16)
-    back_h = joined(exchange(back_h))
-    gx, back0, back_h = sums.end((gx, back0, back_h))
+    gx, back0, x1 = tie((gx, back0, x1))
     x0 = sums.add(gx)
 
     def hand_over(v, layer):
         return lax.ppermute(v, "section", [(1 - layer, layer)])
 
-    sums.finish([o1, z1])
-    sums.begin()
     dnin0 = scatter_sum(back0)
-    own_z1 = exchange(sums.values[z1])
-    own_o1 = sums.values[o1]
+    back_h = joined(exchange(in_group(back_h)))
+    own_z1 = exchange(z1)
+    own_o1 = o1
     away_o1 = hand_over(own_o1, 1)
-    dnin0, own_z1, own_o1, away_o1 = sums.end((dnin0, own_z1, own_o1, away_o1))
-
-    sums.finish([x1, o0])
-    sums.begin()
-    own_x1 = exchange(sums.values[x1])
+    grad0, dgin0 = back_norm(dout0, dnin0, h0, small[0][0])
+    p = jnp.stack([packed(dgin0, d0, out0, mixed0), packed(dgin1, d1, out1, mixed1)])
+    p, grad0, back_h, own_z1, away_o1, o0 = tie((p, grad0, back_h, own_z1, away_o1, o0))
+
+    own_x1 = exchange(x1)
     away_z1 = hand_over(own_z1, 1)
-    own_o0 = sums.values[o0]
+    own_o0 = o0
     away_o0 = hand_over(own_o0, 0)
-    grad0, dgin0 = back_norm(dout0, dnin0, h0, small[0][0])
     back_g = exchange(quarters(jnp.concatenate([grad0.astype(BF16), grad1.astype(BF16)])))
-    p = jnp.stack([packed(dgin0, d0, out0, mixed0), packed(dgin1, d1, out1, mixed1)])
+    back_g = joined(exchange(in_group(back_g)))
+    away_x1 = hand_over(own_x1, 1)
     p = p + swap_section(p)
-    p, back_g, own_x1, own_z1, away_z1, own_o0, away_o0 = sums.end(
-        (p, back_g, own_x1, own_z1, away_z1, own_o0, away_o0)
-    )
-
-    sums.finish([z0])
-    sums.begin()
-    back_g = in_group(back_g)
-    own_z0 = exchange(sums.values[z0])
-    away_x1 = hand_over(own_x1, 1)
     m = 1
     while m < n:
         p = p + move_fsdp(p, m)
         m *= 2
-    p, back_g, own_z0, own_x1, away_x1 = sums.end((p, back_g, own_z0, own_x1, away_x1))
-    sums.finish([x0])
-    away_z0 = hand_over(own_z0, 0)
-    own_x0 = sums.values[x0]
-    away_x0 = hand_over(own_x0, 0)
-    back_g = joined(exchange(back_g))
     m = 1
     while m < nz:
         p = p + move_seq(p, m)
         m *= 2
     p = pick(p[0], p[1])
+    p, own_x1, away_x1, away_z1, away_o0, back_g, z0 = tie(
+        (p, own_x1, away_x1, away_z1, away_o0, back_g, z0)
+    )
+    own_z0 = exchange(z0)
+    away_z0 = hand_over(own_z0, 0)
+    own_z0, away_z0, x0 = tie((own_z0, away_z0, x0))
+    own_x0 = x0
+    away_x0 = hand_over(own_x0, 0)
     back = jnp.concatenate([back_h, back_g])
 
     used = 0

time: 1210 us -> 1320 us (1.091)
  waiting for transfers between devices: 422 us -> 635 us
  starting transfers between devices: 299 us -> 205 us
  Pallas kernels: 197 us -> 128 us
  blocking collectives: 6.54 us -> 52.7 us
  between operations: 3.74 us -> 17.1 us
    psum x0 -> x6, waiting for transfers between devices: none -> 288 us  [add(): self.last = lax.psum(v, 'seq')]
    ppermute x18 -> x0, waiting for transfers between devices: 182 us -> none  [begin(): lax.ppermute(self.values[k], 'seq', self.pairs[step])]
    all_to_all x23 -> x22, waiting for transfers between devices: 96.4 us -> 206 us  [exchange(): return lax.all_to_all(v, 'fsdp', 0, 0, tiled=True)]
    ppermute x18 -> x0, starting transfers between devices: 68.9 us -> none  [begin(): lax.ppermute(self.values[k], 'seq', self.pairs[step])]
    pallas_call x10 -> x0, Pallas kernels: 67.6 us -> none  [combine(): pl.pallas_call(functools.partial(combine_kernel, adds=tuple((add for _, _...]
    ppermute x2, waiting for transfers between devices: 4.37 us -> 38.5 us  [move_seq(): return lax.ppermute(v, 'seq', [(k, k ^ m) for k in range(s)])]
    all_to_all x0 -> x1, blocking collectives: none -> 29.9 us  [in_group(): return lax.all_to_all(v, 'seq', 0, 0, axis_index_groups=groups, tiled=True)]
    ppermute x2, waiting for transfers between devices: 33.5 us -> 6.2 us  [move_fsdp(): return lax.ppermute(v, 'fsdp', [(k, k ^ m) for k in range(n)])]
  transfers between devices with their start and end apart: 96 -> 82, of which waited for: 41 -> 38; matrix products, arithmetic and copies ran while one was open for 14% -> 11% of each run, Pallas kernels for 13% -> 8%
where the time goes in v8:
time: 1320 us; the launch traced here: 1300 us
  waiting for transfers between devices  635 us (48%)
  starting transfers between devices  205 us (16%)
  Pallas kernels  128 us (10%)
  local copies, waits for them, and re-layouts  105 us (8%)
  matrix products  82.2 us (6%)
  other arithmetic  78.1 us (6%)
  blocking collectives  52.7 us (4%)
  between operations  17.1 us (1%)
    psum x6, waiting for transfers between devices, add(): self.last = lax.psum(v, 'seq')  288 us
    all_to_all x22, waiting for transfers between devices, exchange(): return lax.all_to_all(v, 'fsdp', 0, 0, tiled=True)  206 us
    all_to_all x22, starting transfers between devices, exchange(): return lax.all_to_all(v, 'fsdp', 0, 0, tiled=True)  91.2 us
    dot_general x16, matrix products, dot_rows(): lax.dot_general(a, b, (((0,), (0,)), ((), ())), preferred_element_type=F32)  55.9 us
    unnamed x178, local copies, waits for them, and re-layouts  43.8 us
    pallas_call x2, Pallas kernels, run_backward(): pl.pallas_call(backward_kernel, grid=(count,), in_specs=[block(width), bl...  40.9 us
    ppermute x12, waiting for transfers between devices, fetch(): lax.ppermute(v, ('section', 'fsdp'), pairs(m))  39.5 us
    ppermute x2, waiting for transfers between devices, move_seq(): return lax.ppermute(v, 'seq', [(k, k ^ m) for k in range(s)])  38.5 us
  transfers between devices with their start and end apart: 82, of which 38 were waited for; matrix products, arithmetic and copies ran while one was open for 11% of the time, Pallas kernels for 8%

profile of v8, /device:TPU:1, one launch (start us, length us, event | category | flops | bytes accessed | tf_op | source)
XLA Modules:
  0.0 1303.0 jit_solution(13328411379085893125)
XLA Ops:
  20.1 6.5 dynamic-slice_bitcast_fusion
  49.6 4.6 all-to-all-start.2
  55.4 8.1 all-to-all-done.2
  67.0 4.5 all-to-all-start.3
  76.9 16.4 %all-to-all-done.3 = bf16[4,512,512]{2,1,0:T(8,128)(2,1)} async-done(((bf16[4,512,512]{2,1,0:T(8,128)(2,1)}), bf16[4,512,512]{2,1,0:T(8,128)(2,1)}, u32[]{:S(2)}, u32[]{:S(2)}) %all-to-all-start.3) | async-done | bytes 2097184 | tf_op jit(solution)/shard_map/all_to_all | solution.py:559
  109.3 8.7 project.4.proj
  118.0 9.6 collective-permute-start.19
  131.5 10.6 scan_forward.2
  151.9 8.1 collective-permute-done.11.refs_4_.refs_8_
  177.5 6.7 project.5.pz
  187.8 13.5 %collective-permute-done.17.refs_2_.refs_6_ = bf16[1296,512]{1,0:T(8,128)(2,1)} collective-permute-done((bf16[1296,512]{1,0:T(8,128)(2,1)}, bf16[1296,512]{1,0:T(8,128)(2,1)}, u32[]{:S(2)}, u32[]{:S(2)}) %collective-permute-start.17) | collective-permute-done | bytes 1327136 | tf_op jit(solution)/shard_map/ppermute | solution.py:701
  210.0 4.6 all-to-all-start.6
  217.5 5.8 broadcast_select_fusion
  225.8 6.9 fusion.115
  232.7 4.9 all-to-all-start.7
  240.7 6.7 collective-permute-start.24
  247.5 5.8 collective-permute-start.25
  253.2 29.5 %all-to-all-done.7 = f32[4,128,2048]{2,1,0:T(8,128)} async-done(((f32[4,128,2048]{2,1,0:T(8,128)}), f32[4,128,2048]{2,1,0:T(8,128)}, u32[]{:S(2)}, u32[]{:S(2)}) %all-to-all-start.7) | async-done | bytes 4194336 | tf_op jit(solution)/shard_map/all_to_all | solution.py:559
  302.3 4.5 collective-permute-start.26
  306.7 26.0 %collective-permute-done.26.refs_3_ = bf16[1024,512]{1,0:T(8,128)(2,1)S(1)} collective-permute-done((bf16[1024,512]{1,0:T(8,128)(2,1)}, bf16[1024,512]{1,0:T(8,128)(2,1)S(1)}, u32[]{:S(2)}, u32[]{:S(2)}) %collective-permute-start.26) | collective-permute-done | bytes 1048608 | tf_op jit(solution)/shard_map/ppermute | solution.py:701
  341.6 4.4 all-to-all-start.9
  351.8 7.7 project.6.proj
  359.5 10.7 scan_forward.3
  375.3 6.3 project.7.pz
  385.5 7.0 multiply_reduce_fusion.2
  410.1 5.1 add_convert_fusion.5
  415.2 5.9 convolution_convert_fusion
  421.0 4.5 all-to-all-start.11
  425.5 20.4 %scan_backward.2 = (bf16[512,1024]{1,0:T(8,128)(2,1)S(1)}, bf16[512,1296]{1,0:T(8,128)(2,1)S(1)}, f32[4,512,64]{2,1,0:T(8,128)S(1)}, f32[8,1024]{1,0:T(8,128)S(1...) custom-call(f32[512,1024]{1,0:T(8,128)} %project.7.pz, ...), custom_call_target="tpu_custom_call" | custom-call | tf_op jit(solution)/shard_map/scan_backward/pallas_call | solution.py:303
  467.0 6.4 all-to-all-done.12
  478.4 11.1 project_back.2
  489.6 4.8 add_convert_fusion.4
  494.4 5.0 all-to-all-start.13
  517.8 28.5 %all-to-all-done.13 = f32[4,128,2048]{2,1,0:T(8,128)} async-done(((f32[4,128,2048]{2,1,0:T(8,128)}), f32[4,128,2048]{2,1,0:T(8,128)}, u32[]{:S(2)}, u32[]{:S(2)}) %all-to-all-start.13) | async-done | bytes 4194336 | tf_op jit(solution)/shard_map/all_to_all | solution.py:559
  549.9 43.6 %all-reduce.9.cloned.1.call-done = bf16[512,2048]{1,0:T(8,128)(2,1)} async-done(((bf16[512,2048]{1,0:T(8,128)(2,1)}), bf16[512,2048]{1,0:T(8,128)(2,1)}) %all-reduce.9.cloned.1.call-update) | async-done | bytes 2097168 | tf_op jit(solution)/shard_map/psum | solution.py:609
  598.8 6.7 all_to_all.145
  607.1 4.6 all-to-all-start.14
  611.8 24.2 %all-to-all-done.14 = bf16[4,128,2048]{2,1,0:T(8,128)(2,1)} async-done(((bf16[4,128,2048]{2,1,0:T(8,128)(2,1)}), bf16[4,128,2048]{2,1,0:T(8,128)(2,1)}, u32[]{:S(2)}, u32[]{:S(2)}) %all-to-all-start.14) | async-done | bytes 2097184 | tf_op jit(solution)/shard_map/all_to_all | solution.py:559
  650.0 6.6 fusion.116.dn
  656.5 20.5 %scan_backward.3 = (bf16[512,1024]{1,0:T(8,128)(2,1)S(1)}, bf16[512,1296]{1,0:T(8,128)(2,1)S(1)}, f32[4,512,64]{2,1,0:T(8,128)S(1)}, f32[8,1024]{1,0:T(8,128)S(1...) custom-call(f32[512,1024]{1,0:T(8,128)} %project.5.pz, ...), custom_call_target="tpu_custom_call" | custom-call | tf_op jit(solution)/shard_map/scan_backward/pallas_call | solution.py:303
  679.0 4.9 add_convert_fusion.2
  683.9 42.3 %all-reduce.11.cloned.1.call-done = bf16[4,512,512]{2,1,0:T(8,128)(2,1)} async-done(((bf16[4,512,512]{2,1,0:T(8,128)(2,1)}), bf16[4,512,512]{2,1,0:T(8,128)(2,1)}) %all-reduce.11.cloned.1.call-update) | async-done | bytes 2097168 | tf_op jit(solution)/shard_map/psum | solution.py:609
  741.6 5.5 all-to-all-done.17
  763.7 29.9 %all_to_all.146 = bf16[4,256,512]{2,1,0:T(8,128)(2,1)} all-to-all(bf16[4,256,512]{2,1,0:T(8,128)(2,1)} %all-to-all-done.16), channel_id=1, replica_groups={{0,4,8,12},{1,5,9,13},{2,6,10,14},{3,7,11,15},{16,20,24,28},{17,21,25,2..., dimensions={0} | all-to-all | bytes 2097152 | tf_op jit(solution)/shard_map/all_to_all | solution.py:580
  793.6 4.5 all-to-all-start.18
  798.9 26.4 %all-to-all-done.18 = bf16[4,576,512]{2,1,0:T(8,128)(2,1)} async-done(((bf16[4,576,512]{2,1,0:T(8,128)(2,1)}), bf16[4,576,512]{2,1,0:T(8,128)(2,1)}, u32[]{:S(2)}, u32[]{:S(2)}) %all-to-all-start.18) | async-done | bytes 2359328 | tf_op jit(solution)/shard_map/all_to_all | solution.py:559
  830.9 10.7 project_back.3
  841.6 55.3 %all-reduce.13.cloned.1.call-done = bf16[4,576,512]{2,1,0:T(8,128)(2,1)} async-done(((bf16[4,576,512]{2,1,0:T(8,128)(2,1)}), bf16[4,576,512]{2,1,0:T(8,128)(2,1)}) %all-reduce.13.cloned.1.call-update) | async-done | bytes 2359312 | tf_op jit(solution)/shard_map/psum | solution.py:609
  900.5 24.3 %all-to-all-done.19 = bf16[4,128,2048]{2,1,0:T(8,128)(2,1)S(1)} async-done(((bf16[4,128,2048]{2,1,0:T(8,128)(2,1)}), bf16[4,128,2048]{2,1,0:T(8,128)(2,1)S(1)}, u32[]{:S(2)}, u32[]{:S(2)}) %all-to-all-start.19) | async-done | bytes 2097184 | tf_op jit(solution)/shard_map/all_to_all | solution.py:559
  945.3 8.9 all-to-all-done.22.refs_1_
  963.4 57.8 %all-reduce.15.cloned.1.call-done = bf16[512,2048]{1,0:T(8,128)(2,1)} async-done(((bf16[512,2048]{1,0:T(8,128)(2,1)}), bf16[512,2048]{1,0:T(8,128)(2,1)}) %all-reduce.15.cloned.1.call-update) | async-done | bytes 2097168 | tf_op jit(solution)/shard_map/psum | solution.py:609
  1022.6 16.2 %all_to_all.147 = bf16[4,256,512]{2,1,0:T(8,128)(2,1)} all-to-all(bf16[4,256,512]{2,1,0:T(8,128)(2,1)S(1)} %bitcast.250), channel_id=1, replica_groups=mesh['section'=2,'seq'=4,'fsdp'=4] {'fsdp'}, dimensions={0} | all-to-all | bytes 2097152 | tf_op jit(solution)/shard_map/all_to_all | solution.py:559
  1046.1 8.2 collective-permute-start.47
  1057.9 6.2 collective-permute-done.41
  1065.6 18.3 %all-to-all-done.25 = bf16[4,256,512]{2,1,0:T(8,128)(2,1)} async-done(((bf16[4,256,512]{2,1,0:T(8,128)(2,1)}), bf16[4,256,512]{2,1,0:T(8,128)(2,1)}, u32[]{:S(2)}, u32[]{:S(2)}) %all-to-all-start.25) | async-done | bytes 1048608 | tf_op jit(solution)/shard_map/all_to_all | solution.py:580
  1088.6 17.6 %collective-permute-done.43 = f32[2,28099]{1,0:T(2,128)S(1)} collective-permute-done((f32[2,28099]{1,0:T(2,128)S(1)}, f32[2,28099]{1,0:T(2,128)S(1)}, u32[]{:S(2)}, u32[]{:S(2)}) %collective-permute-start.43) | collective-permute-done | bytes 224824 | tf_op jit(solution)/shard_map/ppermute | solution.py:599
  1106.4 20.9 %collective-permute-done.44 = f32[2,28099]{1,0:T(2,128)S(1)} collective-permute-done((f32[2,28099]{1,0:T(2,128)S(1)}, f32[2,28099]{1,0:T(2,128)S(1)}, u32[]{:S(2)}, u32[]{:S(2)}) %collective-permute-start.44) | collective-permute-done | bytes 224824 | tf_op jit(solution)/shard_map/ppermute | solution.py:599
  1128.9 24.1 %all-reduce.17.cloned.1.call-done = bf16[4,512,512]{2,1,0:T(8,128)(2,1)} async-done(((bf16[4,512,512]{2,1,0:T(8,128)(2,1)}), bf16[4,512,512]{2,1,0:T(8,128)(2,1)}) %all-reduce.17.cloned.1.call-update) | async-done | bytes 2097168 | tf_op jit(solution)/shard_map/psum | solution.py:609
  1153.1 4.5 all-to-all-start.27
  1158.2 23.9 %all-to-all-done.27.refs_0_ = bf16[4,512,512]{2,1,0:T(8,128)(2,1)} async-done(((bf16[4,512,512]{2,1,0:T(8,128)(2,1)}), bf16[4,512,512]{2,1,0:T(8,128)(2,1)}, u32[]{:S(2)}, u32[]{:S(2)}) %all-to-all-start.27) | async-done | bytes 2097184 | tf_op jit(solution)/shard_map/all_to_all | solution.py:559
  1182.1 4.5 collective-permute-start.49
  1191.6 64.4 %all-reduce.19.cloned.1.call-done.refs_0_ = bf16[4,576,512]{2,1,0:T(8,128)(2,1)} async-done(((bf16[4,576,512]{2,1,0:T(8,128)(2,1)}), bf16[4,576,512]{2,1,0:T(8,128)(2,1)}) %all-reduce.19.cloned.1.call-update) | async-done | bytes 2359312 | tf_op jit(solution)/shard_map/psum | solution.py:609
  1281.4 7.0 place_in.2.refs_5_
  1288.4 7.3 place_in.3
  (518 shorter events, 366.3 us)
Async XLA Ops:
  44.5 19.0 %collective-permute-start = (bf16[1296,512]{1,0:T(8,128)(2,1)}, bf16[1296,512]{1,0:T(8,128)(2,1)}, u32[]{:S(2)}, u32[]{:S(2)}) collective-permute-start(bf16[1296,512]{1,0:T(8,128)(2,1)} %get-tuple-element.207), channel_id=1, source_target_pairs={{0,1},{1,0},{2,3},{3,2},{4,5},{5,4},{6,7},{7,6},{8,9},{9,8},{10,11... | collective-permute-start | bytes 3981320 | tf_op jit(solution)/shard_map/ppermute | solution.py:701
  46.2 17.3 %collective-permute-start.1 = (bf16[1296,512]{1,0:T(8,128)(2,1)}, bf16[1296,512]{1,0:T(8,128)(2,1)}, u32[]{:S(2)}, u32[]{:S(2)}) collective-permute-start(bf16[1296,512]{1,0:T(8,128)(2,1)} %get-tuple-element.208), channel_id=1, source_target_pairs={{0,2},{1,3},{2,0},{3,1},{4,6},{5,7},{6,4},{7,5},{8,10},{9,11},{10,... | collective-permute-start | bytes 3981320 | tf_op jit(solution)/shard_map/ppermute | solution.py:701
  47.9 15.6 %collective-permute-start.2 = (bf16[1296,512]{1,0:T(8,128)(2,1)}, bf16[1296,512]{1,0:T(8,128)(2,1)}, u32[]{:S(2)}, u32[]{:S(2)}) collective-permute-start(bf16[1296,512]{1,0:T(8,128)(2,1)} %get-tuple-element.209), channel_id=1, source_target_pairs={{0,3},{1,2},{2,1},{3,0},{4,7},{5,6},{6,5},{7,4},{8,11},{9,10},{10,... | collective-permute-start | bytes 3981320 | tf_op jit(solution)/shard_map/ppermute | solution.py:701
  67.0 26.3 %all-to-all-start.3 = ((bf16[4,512,512]{2,1,0:T(8,128)(2,1)}), bf16[4,512,512]{2,1,0:T(8,128)(2,1)}, u32[]{:S(2)}, u32[]{:S(2)}) async-start(bf16[4,512,512]{2,1,0:T(8,128)(2,1)} %broadcast_in_dim.54), calls=%async_computation.3 | async-start | bytes 4194304 | tf_op jit(solution)/shard_map/all_to_all | solution.py:559
  71.6 30.4 %collective-permute-start.4 = (bf16[1296,512]{1,0:T(8,128)(2,1)S(1)}, bf16[1296,512]{1,0:T(8,128)(2,1)}, u32[]{:S(2)}, u32[]{:S(2)}) collective-permute-start(bf16[1296,512]{1,0:T(8,128)(2,1)S(1)} %get-tuple-element.219.refs_0_.refs_4_), channel_id=1, source_target_pairs={{0,16},{1,17},{2,18},{3,19},{4,20},{5,21},{6,22},{7,23},{8,24},{9,... | collective-permute-start | bytes 3981320 | tf_op jit(solution)/shard_map/ppermute | solution.py:726
  72.9 31.7 %collective-permute-start.5 = (bf16[1296,512]{1,0:T(8,128)(2,1)}, bf16[1296,512]{1,0:T(8,128)(2,1)}, u32[]{:S(2)}, u32[]{:S(2)}) collective-permute-start(bf16[1296,512]{1,0:T(8,128)(2,1)} %collective-permute-done.refs_1_.refs_5_), channel_id=1, source_target_pairs={{0,16},{1,17},{2,18},{3,19},{4,20},{5,21},{6,22},{7,23},{8,24},{9,... | collective-permute-start | bytes 3981320 | tf_op jit(solution)/shard_map/ppermute | solution.py:726
  74.2 32.8 %collective-permute-start.6 = (bf16[1296,512]{1,0:T(8,128)(2,1)}, bf16[1296,512]{1,0:T(8,128)(2,1)}, u32[]{:S(2)}, u32[]{:S(2)}) collective-permute-start(bf16[1296,512]{1,0:T(8,128)(2,1)} %collective-permute-done.1.refs_2_.refs_6_), channel_id=1, source_target_pairs={{0,16},{1,17},{2,18},{3,19},{4,20},{5,21},{6,22},{7,23},{8,24},{9,... | collective-permute-start | bytes 3981320 | tf_op jit(solution)/shard_map/ppermute | solution.py:726
  75.5 33.8 %collective-permute-start.7 = (bf16[1296,512]{1,0:T(8,128)(2,1)}, bf16[1296,512]{1,0:T(8,128)(2,1)}, u32[]{:S(2)}, u32[]{:S(2)}) collective-permute-start(bf16[1296,512]{1,0:T(8,128)(2,1)} %collective-permute-done.2.refs_3_.refs_7_), channel_id=1, source_target_pairs={{0,16},{1,17},{2,18},{3,19},{4,20},{5,21},{6,22},{7,23},{8,24},{9,... | collective-permute-start | bytes 3981320 | tf_op jit(solution)/shard_map/ppermute | solution.py:726
  118.0 99.4 %collective-permute-start.19 = (bf16[1024,2048]{1,0:T(8,128)(2,1)}, bf16[1024,2048]{1,0:T(8,128)(2,1)}, u32[]{:S(2)}, u32[]{:S(2)}) collective-permute-start(bf16[1024,2048]{1,0:T(8,128)(2,1)} %bitcast.36), channel_id=1, source_target_pairs={{0,16},{16,0},{1,17},{17,1},{2,18},{18,2},{3,19},{19,3},{4,20},{20... | collective-permute-start | bytes 12582920 | tf_op jit(solution)/shard_map/ppermute | solution.py:551
  127.7 17.1 %collective-permute-start.10 = (bf16[1024,512]{1,0:T(8,128)(2,1)S(1)}, bf16[1024,512]{1,0:T(8,128)(2,1)}, u32[]{:S(2)}, u32[]{:S(2)}) collective-permute-start(bf16[1024,512]{1,0:T(8,128)(2,1)S(1)} %copy-done.64), channel_id=1, source_target_pairs={{0,3},{1,2},{2,1},{3,0},{4,7},{5,6},{6,5},{7,4},{8,11},{9,10},{10,... | collective-permute-start | bytes 3145736 | tf_op jit(solution)/shard_map/ppermute | solution.py:701
  146.1 17.9 %collective-permute-start.12 = (bf16[1024,512]{1,0:T(8,128)(2,1)S(1)}, bf16[1024,512]{1,0:T(8,128)(2,1)S(1)}, u32[]{:S(2)}, u32[]{:S(2)}) collective-permute-start(bf16[1024,512]{1,0:T(8,128)(2,1)S(1)} %collective-permute-done.8.refs_1_), channel_id=1, source_target_pairs={{0,16},{1,17},{2,18},{3,19},{4,20},{5,21},{6,22},{7,23},{8,24},{9,... | collective-permute-start | bytes 3145736 | tf_op jit(solution)/shard_map/ppermute | solution.py:826
  148.4 17.9 %collective-permute-start.13 = (bf16[1024,512]{1,0:T(8,128)(2,1)S(1)}, bf16[1024,512]{1,0:T(8,128)(2,1)S(1)}, u32[]{:S(2)}, u32[]{:S(2)}) collective-permute-start(bf16[1024,512]{1,0:T(8,128)(2,1)S(1)} %collective-permute-done.9.refs_2_), channel_id=1, source_target_pairs={{0,16},{1,17},{2,18},{3,19},{4,20},{5,21},{6,22},{7,23},{8,24},{9,... | collective-permute-start | bytes 3145736 | tf_op jit(solution)/shard_map/ppermute | solution.py:826
  150.6 23.0 %collective-permute-start.14 = (bf16[1024,512]{1,0:T(8,128)(2,1)}, bf16[1024,512]{1,0:T(8,128)(2,1)}, u32[]{:S(2)}, u32[]{:S(2)}) collective-permute-start(bf16[1024,512]{1,0:T(8,128)(2,1)} %collective-permute-done.10.refs_3_), channel_id=1, source_target_pairs={{0,16},{1,17},{2,18},{3,19},{4,20},{5,21},{6,22},{7,23},{8,24},{9,... | collective-permute-start | bytes 3145736 | tf_op jit(solution)/shard_map/ppermute | solution.py:826
  161.0 26.8 %collective-permute-start.16 = (bf16[1296,512]{1,0:T(8,128)(2,1)}, bf16[1296,512]{1,0:T(8,128)(2,1)}, u32[]{:S(2)}, u32[]{:S(2)}) collective-permute-start(bf16[1296,512]{1,0:T(8,128)(2,1)} %get-tuple-element.207), channel_id=1, source_target_pairs={{16,17},{17,16},{18,19},{19,18},{20,21},{21,20},{22,23},{23,22},{2... | collective-permute-start | bytes 3981320 | tf_op jit(solution)/shard_map/ppermute | solution.py:701
  164.0 37.3 %collective-permute-start.17 = (bf16[1296,512]{1,0:T(8,128)(2,1)}, bf16[1296,512]{1,0:T(8,128)(2,1)}, u32[]{:S(2)}, u32[]{:S(2)}) collective-permute-start(bf16[1296,512]{1,0:T(8,128)(2,1)} %get-tuple-element.208), channel_id=1, source_target_pairs={{16,18},{17,19},{18,16},{19,17},{20,22},{21,23},{22,20},{23,21},{2... | collective-permute-start | bytes 3981320 | tf_op jit(solution)/shard_map/ppermute | solution.py:701
  166.3 35.0 %collective-permute-start.18 = (bf16[1296,512]{1,0:T(8,128)(2,1)}, bf16[1296,512]{1,0:T(8,128)(2,1)}, u32[]{:S(2)}, u32[]{:S(2)}) collective-permute-start(bf16[1296,512]{1,0:T(8,128)(2,1)} %get-tuple-element.209), channel_id=1, source_target_pairs={{16,19},{17,18},{18,17},{19,16},{20,23},{21,22},{22,21},{23,20},{2... | collective-permute-start | bytes 3981320 | tf_op jit(solution)/shard_map/ppermute | solution.py:701
  169.5 33.2 %all-to-all-start.5 = ((bf16[4,128,512]{1,2,0:T(8,128)(2,1)}), bf16[4,128,512]{1,2,0:T(8,128)(2,1)}, u32[]{:S(2)}, u32[]{:S(2)}) async-start(bf16[4,128,512]{1,2,0:T(8,128)(2,1)} %bitcast.266), calls=%async_computation.5 | async-start | bytes 1048576 | tf_op jit(solution)/shard_map/all_to_all | solution.py:559
  210.0 15.8 %all-to-all-start.6 = ((bf16[4,128,512]{1,2,0:T(8,128)(2,1)}), bf16[4,128,512]{1,2,0:T(8,128)(2,1)}, u32[]{:S(2)}, u32[]{:S(2)}) async-start(bf16[4,128,512]{1,2,0:T(8,128)(2,1)} %all-to-all-done.5), calls=%async_computation.6 | async-start | bytes 1048576 | tf_op jit(solution)/shard_map/all_to_all | solution.py:580
  232.7 50.0 %all-to-all-start.7 = ((f32[4,128,2048]{2,1,0:T(8,128)}), f32[4,128,2048]{2,1,0:T(8,128)}, u32[]{:S(2)}, u32[]{:S(2)}) async-start(f32[4,128,2048]{2,1,0:T(8,128)} %bitcast.248), calls=%async_computation.7 | async-start | bytes 8388608 | tf_op jit(solution)/shard_map/all_to_all | solution.py:559
  240.7 59.2 %collective-permute-start.24 = (bf16[1024,512]{1,0:T(8,128)(2,1)}, bf16[1024,512]{1,0:T(8,128)(2,1)}, u32[]{:S(2)}, u32[]{:S(2)}) collective-permute-start(bf16[1024,512]{1,0:T(8,128)(2,1)} %get-tuple-element.225), channel_id=1, source_target_pairs={{16,17},{17,16},{18,19},{19,18},{20,21},{21,20},{22,23},{23,22},{2... | collective-permute-start | bytes 3145736 | tf_op jit(solution)/shard_map/ppermute | solution.py:701
  247.5 54.8 %collective-permute-start.25 = (bf16[1024,512]{1,0:T(8,128)(2,1)}, bf16[1024,512]{1,0:T(8,128)(2,1)}, u32[]{:S(2)}, u32[]{:S(2)}) collective-permute-start(bf16[1024,512]{1,0:T(8,128)(2,1)} %get-tuple-element.226), channel_id=1, source_target_pairs={{16,18},{17,19},{18,16},{19,17},{20,22},{21,23},{22,20},{23,21},{2... | collective-permute-start | bytes 3145736 | tf_op jit(solution)/shard_map/ppermute | solution.py:701
  291.1 45.9 %all-to-all-start.8 = ((bf16[4,128,2048]{2,1,0:T(8,128)(2,1)}), bf16[4,128,2048]{2,1,0:T(8,128)(2,1)}, u32[]{:S(2)}, u32[]{:S(2)}) async-start(bf16[4,128,2048]{2,1,0:T(8,128)(2,1)} %broadcast_in_dim.59), calls=%async_computation.8 | async-start | bytes 4194304 | tf_op jit(solution)/shard_map/all_to_all | solution.py:559
  295.5 37.2 %collective-permute-start.20 = (bf16[1296,512]{1,0:T(8,128)(2,1)S(1)}, bf16[1296,512]{1,0:T(8,128)(2,1)S(1)}, u32[]{:S(2)}, u32[]{:S(2)}) collective-permute-start(bf16[1296,512]{1,0:T(8,128)(2,1)S(1)} %get-tuple-element.219.refs_0_.refs_4_), channel_id=1, source_target_pairs={{16,0},{17,1},{18,2},{19,3},{20,4},{21,5},{22,6},{23,7},{24,8},{25... | collective-permute-start | bytes 3981320 | tf_op jit(solution)/shard_map/ppermute | solution.py:837
  297.1 36.7 %collective-permute-start.21 = (bf16[1296,512]{1,0:T(8,128)(2,1)}, bf16[1296,512]{1,0:T(8,128)(2,1)S(1)}, u32[]{:S(2)}, u32[]{:S(2)}) collective-permute-start(bf16[1296,512]{1,0:T(8,128)(2,1)} %collective-permute-done.16.refs_1_.refs_5_), channel_id=1, source_target_pairs={{16,0},{17,1},{18,2},{19,3},{20,4},{21,5},{22,6},{23,7},{24,8},{25... | collective-permute-start | bytes 3981320 | tf_op jit(solution)/shard_map/ppermute | solution.py:837
  298.5 36.3 %collective-permute-start.22 = (bf16[1296,512]{1,0:T(8,128)(2,1)}, bf16[1296,512]{1,0:T(8,128)(2,1)S(1)}, u32[]{:S(2)}, u32[]{:S(2)}) collective-permute-start(bf16[1296,512]{1,0:T(8,128)(2,1)} %collective-permute-done.17.refs_2_.refs_6_), channel_id=1, source_target_pairs={{16,0},{17,1},{18,2},{19,3},{20,4},{21,5},{22,6},{23,7},{24,8},{25... | collective-permute-start | bytes 3981320 | tf_op jit(solution)/shard_map/ppermute | solution.py:837
  299.9 37.1 %collective-permute-start.23 = (bf16[1296,512]{1,0:T(8,128)(2,1)}, bf16[1296,512]{1,0:T(8,128)(2,1)}, u32[]{:S(2)}, u32[]{:S(2)}) collective-permute-start(bf16[1296,512]{1,0:T(8,128)(2,1)} %collective-permute-done.18.refs_3_.refs_7_), channel_id=1, source_target_pairs={{16,0},{17,1},{18,2},{19,3},{20,4},{21,5},{22,6},{23,7},{24,8},{25... | collective-permute-start | bytes 3981320 | tf_op jit(solution)/shard_map/ppermute | solution.py:837
  302.3 30.5 %collective-permute-start.26 = (bf16[1024,512]{1,0:T(8,128)(2,1)}, bf16[1024,512]{1,0:T(8,128)(2,1)S(1)}, u32[]{:S(2)}, u32[]{:S(2)}) collective-permute-start(bf16[1024,512]{1,0:T(8,128)(2,1)} %get-tuple-element.227), channel_id=1, source_target_pairs={{16,19},{17,18},{18,17},{19,16},{20,23},{21,22},{22,21},{23,20},{2... | collective-permute-start | bytes 3145736 | tf_op jit(solution)/shard_map/ppermute | solution.py:701
  341.6 41.0 %all-to-all-start.9 = ((bf16[4,512,512]{2,1,0:T(8,128)(2,1)}), bf16[4,512,512]{2,1,0:T(8,128)(2,1)}, u32[]{:S(2)}, u32[]{:S(2)}) async-start(bf16[4,512,512]{2,1,0:T(8,128)(2,1)} %broadcast_in_dim.61), calls=%async_computation.9 | async-start | bytes 4194304 | tf_op jit(solution)/shard_map/all_to_all | solution.py:559
  346.1 26.9 %collective-permute-start.27 = (bf16[1024,512]{1,0:T(8,128)(2,1)S(1)}, bf16[1024,512]{1,0:T(8,128)(2,1)S(1)}, u32[]{:S(2)}, u32[]{:S(2)}) collective-permute-start(bf16[1024,512]{1,0:T(8,128)(2,1)S(1)} %get-tuple-element.238.refs_0_), channel_id=1, source_target_pairs={{16,0},{17,1},{18,2},{19,3},{20,4},{21,5},{22,6},{23,7},{24,8},{25... | collective-permute-start | bytes 3145736 | tf_op jit(solution)/shard_map/ppermute | solution.py:844
  347.4 25.5 %collective-permute-start.28 = (bf16[1024,512]{1,0:T(8,128)(2,1)}, bf16[1024,512]{1,0:T(8,128)(2,1)S(1)}, u32[]{:S(2)}, u32[]{:S(2)}) collective-permute-start(bf16[1024,512]{1,0:T(8,128)(2,1)} %collective-permute-done.24.refs_1_), channel_id=1, source_target_pairs={{16,0},{17,1},{18,2},{19,3},{20,4},{21,5},{22,6},{23,7},{24,8},{25... | collective-permute-start | bytes 3145736 | tf_op jit(solution)/shard_map/ppermute | solution.py:844
  348.8 24.2 %collective-permute-start.29 = (bf16[1024,512]{1,0:T(8,128)(2,1)}, bf16[1024,512]{1,0:T(8,128)(2,1)S(1)}, u32[]{:S(2)}, u32[]{:S(2)}) collective-permute-start(bf16[1024,512]{1,0:T(8,128)(2,1)} %collective-permute-done.25.refs_2_), channel_id=1, source_target_pairs={{16,0},{17,1},{18,2},{19,3},{20,4},{21,5},{22,6},{23,7},{24,8},{25... | collective-permute-start | bytes 3145736 | tf_op jit(solution)/shard_map/ppermute | solution.py:844
  350.3 22.7 %collective-permute-start.30 = (bf16[1024,512]{1,0:T(8,128)(2,1)}, bf16[1024,512]{1,0:T(8,128)(2,1)S(1)}, u32[]{:S(2)}, u32[]{:S(2)}) collective-permute-start(bf16[1024,512]{1,0:T(8,128)(2,1)} %copy-done.19), channel_id=1, source_target_pairs={{16,0},{17,1},{18,2},{19,3},{20,4},{21,5},{22,6},{23,7},{24,8},{25... | collective-permute-start | bytes 3145736 | tf_op jit(solution)/shard_map/ppermute | solution.py:844
  421.0 29.4 %all-to-all-start.11 = ((bf16[4,128,2048]{2,1,0:T(8,128)(2,1)}), bf16[4,128,2048]{2,1,0:T(8,128)(2,1)}, u32[]{:S(2)}, u32[]{:S(2)}) async-start(bf16[4,128,2048]{2,1,0:T(8,128)(2,1)} %bitcast.263), calls=%async_computation.11 | async-start | bytes 4194304 | tf_op jit(solution)/shard_map/all_to_all | solution.py:559
  457.7 31.8 %collective-permute-start.32 = (bf16[2048,512]{1,0:T(8,128)(2,1)}, bf16[2048,512]{1,0:T(8,128)(2,1)}, u32[]{:S(2)}, u32[]{:S(2)}) collective-permute-start(bf16[2048,512]{1,0:T(8,128)(2,1)} %convolution_convert_fusion.5), channel_id=1, source_target_pairs={{0,16},{16,0},{1,17},{17,1},{2,18},{18,2},{3,19},{19,3},{4,20},{20... | collective-permute-start | bytes 6291464 | tf_op jit(solution)/shard_map/ppermute | solution.py:551
  494.4 51.9 %all-to-all-start.13 = ((f32[4,128,2048]{2,1,0:T(8,128)}), f32[4,128,2048]{2,1,0:T(8,128)}, u32[]{:S(2)}, u32[]{:S(2)}) async-start(f32[4,128,2048]{2,1,0:T(8,128)} %bitcast.241), calls=%async_computation.13 | async-start | bytes 8388608 | tf_op jit(solution)/shard_map/all_to_all | solution.py:559
  499.4 94.1 %all-reduce.9.cloned.1.call-start = ((), (), s32[]{:S(2)}) async-start(), calls=%async_computation.28 | async-start | bytes 4194304 | tf_op jit(solution)/shard_map/psum | solution.py:609
  607.1 29.0 %all-to-all-start.14 = ((bf16[4,128,2048]{2,1,0:T(8,128)(2,1)}), bf16[4,128,2048]{2,1,0:T(8,128)(2,1)}, u32[]{:S(2)}, u32[]{:S(2)}) async-start(bf16[4,128,2048]{2,1,0:T(8,128)(2,1)} %broadcast_in_dim.65), calls=%async_computation.14 | async-start | bytes 4194304 | tf_op jit(solution)/shard_map/all_to_all | solution.py:559
  611.6 114.5 %all-reduce.11.cloned.1.call-start = ((), (), s32[]{:S(2)}) async-start(), calls=%async_computation.29 | async-start | bytes 4194304 | tf_op jit(solution)/shard_map/psum | solution.py:609
  640.2 38.8 %collective-permute-start.35 = (bf16[512,2048]{1,0:T(8,128)(2,1)}, bf16[512,2048]{1,0:T(8,128)(2,1)}, u32[]{:S(2)}, u32[]{:S(2)}) collective-permute-start(bf16[512,2048]{1,0:T(8,128)(2,1)} %convolution_convert_fusion.3), channel_id=1, source_target_pairs={{0,16},{16,0},{1,17},{17,1},{2,18},{18,2},{3,19},{19,3},{4,20},{20... | collective-permute-start | bytes 6291464 | tf_op jit(solution)/shard_map/ppermute | solution.py:551
  645.6 80.6 %all-to-all-start.16 = ((bf16[4,256,512]{2,1,0:T(8,128)(2,1)}), bf16[4,256,512]{2,1,0:T(8,128)(2,1)}, u32[]{:S(2)}, u32[]{:S(2)}) async-start(bf16[4,256,512]{2,1,0:T(8,128)(2,1)} %bitcast.229), calls=%async_computation.16 | async-start | bytes 2097152 | tf_op jit(solution)/shard_map/all_to_all | solution.py:559
  730.4 24.5 %collective-permute-start.37 = (bf16[2048,512]{1,0:T(8,128)(2,1)}, bf16[2048,512]{1,0:T(8,128)(2,1)}, u32[]{:S(2)}, u32[]{:S(2)}) collective-permute-start(bf16[2048,512]{1,0:T(8,128)(2,1)} %convolution_convert_fusion.1), channel_id=1, source_target_pairs={{0,16},{16,0},{1,17},{17,1},{2,18},{18,2},{3,19},{19,3},{4,20},{20... | collective-permute-start | bytes 6291464 | tf_op jit(solution)/shard_map/ppermute | solution.py:551
  733.7 25.8 %collective-permute-start.36 = (bf16[2048,512]{1,0:T(8,128)(2,1)}, bf16[2048,512]{1,0:T(8,128)(2,1)}, u32[]{:S(2)}, u32[]{:S(2)}) collective-permute-start(bf16[2048,512]{1,0:T(8,128)(2,1)} %convolution_convert_fusion.2), channel_id=1, source_target_pairs={{0,16},{16,0},{1,17},{17,1},{2,18},{18,2},{3,19},{19,3},{4,20},{20... | collective-permute-start | bytes 6291464 | tf_op jit(solution)/shard_map/ppermute | solution.py:551
  793.6 31.7 %all-to-all-start.18 = ((bf16[4,576,512]{2,1,0:T(8,128)(2,1)}), bf16[4,576,512]{2,1,0:T(8,128)(2,1)}, u32[]{:S(2)}, u32[]{:S(2)}) async-start(bf16[4,576,512]{2,1,0:T(8,128)(2,1)} %pad_maximum_fusion.5), calls=%async_computation.18 | async-start | bytes 4718592 | tf_op jit(solution)/shard_map/all_to_all | solution.py:559
  798.2 98.7 %all-reduce.13.cloned.1.call-start = ((), (), s32[]{:S(2)}) async-start(), calls=%async_computation.30 | async-start | bytes 4718592 | tf_op jit(solution)/shard_map/psum | solution.py:609
  825.3 71.6 %all-to-all-start.21 = ((bf16[4,256,512]{2,1,0:T(8,128)(2,1)}), bf16[4,256,512]{2,1,0:T(8,128)(2,1)}, u32[]{:S(2)}, u32[]{:S(2)}) async-start(bf16[4,256,512]{2,1,0:T(8,128)(2,1)} %all_to_all.146), calls=%async_computation.21 | async-start | bytes 2097152 | tf_op jit(solution)/shard_map/all_to_all | solution.py:559
  896.9 27.9 %all-to-all-start.19 = ((bf16[4,128,2048]{2,1,0:T(8,128)(2,1)}), bf16[4,128,2048]{2,1,0:T(8,128)(2,1)S(1)}, u32[]{:S(2)}, u32[]{:S(2)}) async-start(bf16[4,128,2048]{2,1,0:T(8,128)(2,1)} %bitcast.247), calls=%async_computation.19 | async-start | bytes 4194304 | tf_op jit(solution)/shard_map/all_to_all | solution.py:559
  926.2 28.0 %all-to-all-start.22 = ((bf16[4,512,512]{2,1,0:T(8,128)(2,1)}), bf16[4,512,512]{2,1,0:T(8,128)(2,1)S(1)}, u32[]{:S(2)}, u32[]{:S(2)}) async-start(bf16[4,512,512]{2,1,0:T(8,128)(2,1)} %all-reduce.11.cloned.1.call-done), calls=%async_computation.22 | async-start | bytes 4194304 | tf_op jit(solution)/shard_map/all_to_all | solution.py:559
  929.8 91.4 %all-reduce.15.cloned.1.call-start = ((), (), s32[]{:S(2)}) async-start(), calls=%async_computation.31 | async-start | bytes 4194304 | tf_op jit(solution)/shard_map/psum | solution.py:609
  931.5 31.9 %collective-permute-start.39 = (bf16[512,2048]{1,0:T(8,128)(2,1)}, bf16[512,2048]{1,0:T(8,128)(2,1)}, u32[]{:S(2)}, u32[]{:S(2)}) collective-permute-start(bf16[512,2048]{1,0:T(8,128)(2,1)} %all-reduce.9.cloned.1.call-done), channel_id=1, source_target_pairs={{0,16},{1,17},{2,18},{3,19},{4,20},{5,21},{6,22},{7,23},{8,24},{9,... | collective-permute-start | bytes 6291464 | tf_op jit(solution)/shard_map/ppermute | solution.py:996
  955.5 67.1 %all-to-all-start.23 = ((bf16[4,576,512]{2,1,0:T(8,128)(2,1)}), bf16[4,576,512]{2,1,0:T(8,128)(2,1)S(1)}, u32[]{:S(2)}, u32[]{:S(2)}) async-start(bf16[4,576,512]{2,1,0:T(8,128)(2,1)} %all-reduce.13.cloned.1.call-done), calls=%async_computation.23 | async-start | bytes 4718592 | tf_op jit(solution)/shard_map/all_to_all | solution.py:559
  1038.8 45.1 %all-to-all-start.25 = ((bf16[4,256,512]{2,1,0:T(8,128)(2,1)}), bf16[4,256,512]{2,1,0:T(8,128)(2,1)}, u32[]{:S(2)}, u32[]{:S(2)}) async-start(bf16[4,256,512]{2,1,0:T(8,128)(2,1)} %all_to_all.147), calls=%async_computation.25 | async-start | bytes 2097152 | tf_op jit(solution)/shard_map/all_to_all | solution.py:580
  1043.2 109.9 %all-reduce.17.cloned.1.call-start = ((), (), s32[]{:S(2)}) async-start(), calls=%async_computation.32 | async-start | bytes 4194304 | tf_op jit(solution)/shard_map/psum | solution.py:609
  1043.2 109.8 %collective-permute-start.45 = (bf16[4,576,512]{2,1,0:T(8,128)(2,1)S(1)}, bf16[4,576,512]{2,1,0:T(8,128)(2,1)}, u32[]{:S(2)}, u32[]{:S(2)}) collective-permute-start(bf16[4,576,512]{2,1,0:T(8,128)(2,1)S(1)} %all-to-all-done.23.refs_1_), channel_id=1, source_target_pairs={{0,16},{1,17},{2,18},{3,19},{4,20},{5,21},{6,22},{7,23},{8,24},{9,... | collective-permute-start | bytes 7077896 | tf_op jit(solution)/shard_map/ppermute | solution.py:996
  1044.8 108.3 %collective-permute-start.46 = (bf16[4,512,512]{2,1,0:T(8,128)(2,1)}, bf16[4,512,512]{2,1,0:T(8,128)(2,1)}, u32[]{:S(2)}, u32[]{:S(2)}) collective-permute-start(bf16[4,512,512]{2,1,0:T(8,128)(2,1)} %copy-done.3), channel_id=1, source_target_pairs={{0,16},{1,17},{2,18},{3,19},{4,20},{5,21},{6,22},{7,23},{8,24},{9,... | collective-permute-start | bytes 6291464 | tf_op jit(solution)/shard_map/ppermute | solution.py:996
  1046.1 107.0 %collective-permute-start.47 = (bf16[512,2048]{1,0:T(8,128)(2,1)}, bf16[512,2048]{1,0:T(8,128)(2,1)}, u32[]{:S(2)}, u32[]{:S(2)}) collective-permute-start(bf16[512,2048]{1,0:T(8,128)(2,1)} %all-reduce.15.cloned.1.call-done), channel_id=1, source_target_pairs={{16,0},{17,1},{18,2},{19,3},{20,4},{21,5},{22,6},{23,7},{24,8},{25... | collective-permute-start | bytes 6291464 | tf_op jit(solution)/shard_map/ppermute | solution.py:996
  1064.9 22.4 %collective-permute-start.42 = (f32[2,28099]{1,0:T(2,128)}, f32[2,28099]{1,0:T(2,128)}, u32[]{:S(2)}, u32[]{:S(2)}) collective-permute-start(f32[2,28099]{1,0:T(2,128)} %add.386), channel_id=1, source_target_pairs={{0,2},{1,3},{2,0},{3,1},{4,6},{5,7},{6,4},{7,5},{8,10},{9,11},{10,... | collective-permute-start | bytes 674384 | tf_op jit(solution)/shard_map/ppermute | solution.py:594
  1083.8 44.0 %all-to-all-start.26 = ((bf16[4,256,512]{2,1,0:T(8,128)(2,1)}), bf16[4,256,512]{2,1,0:T(8,128)(2,1)S(1)}, u32[]{:S(2)}, u32[]{:S(2)}) async-start(bf16[4,256,512]{2,1,0:T(8,128)(2,1)} %all-to-all-done.25), calls=%async_computation.26 | async-start | bytes 2097152 | tf_op jit(solution)/shard_map/all_to_all | solution.py:559
  1088.6 17.7 %collective-permute-start.43 = (f32[2,28099]{1,0:T(2,128)S(1)}, f32[2,28099]{1,0:T(2,128)S(1)}, u32[]{:S(2)}, u32[]{:S(2)}) collective-permute-start(f32[2,28099]{1,0:T(2,128)S(1)} %add.387), channel_id=1, source_target_pairs={{0,4},{4,0},{8,12},{12,8},{1,5},{5,1},{9,13},{13,9},{2,6},{6,2},{1... | collective-permute-start | bytes 674384 | tf_op jit(solution)/shard_map/ppermute | solution.py:599
  1106.4 21.0 %collective-permute-start.44 = (f32[2,28099]{1,0:T(2,128)S(1)}, f32[2,28099]{1,0:T(2,128)S(1)}, u32[]{:S(2)}, u32[]{:S(2)}) collective-permute-start(f32[2,28099]{1,0:T(2,128)S(1)} %add.388), channel_id=1, source_target_pairs={{0,8},{4,12},{8,0},{12,4},{1,9},{5,13},{9,1},{13,5},{2,10},{6,14},... | collective-permute-start | bytes 674384 | tf_op jit(solution)/shard_map/ppermute | solution.py:599
  1153.1 29.0 %all-to-all-start.27 = ((bf16[4,512,512]{2,1,0:T(8,128)(2,1)}), bf16[4,512,512]{2,1,0:T(8,128)(2,1)}, u32[]{:S(2)}, u32[]{:S(2)}) async-start(bf16[4,512,512]{2,1,0:T(8,128)(2,1)} %all-reduce.17.cloned.1.call-done), calls=%async_computation.27 | async-start | bytes 4194304 | tf_op jit(solution)/shard_map/all_to_all | solution.py:559
  1157.6 98.5 %all-reduce.19.cloned.1.call-start = ((), (), s32[]{:S(2)}) async-start(), calls=%async_computation.33 | async-start | bytes 4718592 | tf_op jit(solution)/shard_map/psum | solution.py:609
  1182.1 74.0 %collective-permute-start.49 = (bf16[4,512,512]{2,1,0:T(8,128)(2,1)}, bf16[4,512,512]{2,1,0:T(8,128)(2,1)}, u32[]{:S(2)}, u32[]{:S(2)}) collective-permute-start(bf16[4,512,512]{2,1,0:T(8,128)(2,1)} %all-to-all-done.27.refs_0_), channel_id=1, source_target_pairs={{16,0},{17,1},{18,2},{19,3},{20,4},{21,5},{22,6},{23,7},{24,8},{25... | collective-permute-start | bytes 6291464 | tf_op jit(solution)/shard_map/ppermute | solution.py:996
  1190.2 84.2 %collective-permute-start.48 = (bf16[2,128,2048]{2,1,0:T(8,128)(2,1)S(1)}, bf16[2,128,2048]{2,1,0:T(8,128)(2,1)}, u32[]{:S(2)}, u32[]{:S(2)}) collective-permute-start(bf16[2,128,2048]{2,1,0:T(8,128)(2,1)S(1)} %fusion.5), channel_id=1, source_target_pairs={{0,16},{16,0},{1,17},{17,1},{2,18},{18,2},{3,19},{19,3},{4,20},{20... | collective-permute-start | bytes 3145736 | tf_op jit(solution)/shard_map/ppermute | solution.py:551
  1256.1 21.7 %collective-permute-start.50 = (bf16[4,576,512]{2,1,0:T(8,128)(2,1)}, bf16[4,576,512]{2,1,0:T(8,128)(2,1)}, u32[]{:S(2)}, u32[]{:S(2)}) collective-permute-start(bf16[4,576,512]{2,1,0:T(8,128)(2,1)} %all-reduce.19.cloned.1.call-done.refs_0_), channel_id=1, source_target_pairs={{16,0},{17,1},{18,2},{19,3},{20,4},{21,5},{22,6},{23,7},{24,8},{25... | collective-permute-start | bytes 7077896 | tf_op jit(solution)/shard_map/ppermute | solution.py:996
  (103 other events, 1463.8 us)
Sparse Core Ops, SparseCore 0:
  505.3 88.1 all-reduce.8
  641.9 84.2 all-reduce.10
  801.4 95.4 all-reduce.12
  933.0 88.2 all-reduce.14
  1046.8 106.2 all-reduce.16
  1160.5 95.5 all-reduce.18

commit v9 on v7

--- a/solution.py
+++ b/solution.py
@@ -783,9 +783,13 @@
             conv_b[0],
         ]
     )
-    mine, part_h0, pieces_x = tie(
-        (to_all(pack), exchange(quarters(at(inputs, c)[0])), [piece_x(m) for m in range(n)])
-    )
+    more = -(-pack.shape[0] // (16 * share)) * 16
+    filled = jnp.concatenate([pack, jnp.zeros((more * share - pack.shape[0],), BF16)])
+    filled = jnp.broadcast_to(filled.reshape(1, more, share), (n, more, share))
+    first = exchange(jnp.concatenate([quarters(at(inputs, c)[0]), filled], axis=1))
+    first, pieces_x = tie((first, [piece_x(m) for m in range(n)]))
+    part_h0 = first[:, :rows]
+    mine = first[:, rows:].reshape(n, -1)[:, : pack.shape[0]]
     near_x0, far_x0 = fetch(pieces_x, 0)
     part_h0 = in_group(part_h0)
     near_x0, part_h0 = tie((near_x0, part_h0))
@@ -888,28 +892,31 @@
     own_rows = lambda v: lax.dynamic_slice_in_dim(v, f * rows, rows, 0)
     valid = own_rows(all_valid)
     h0 = own_rows(all_h0)
-    fwd0, near_z0 = tie((scan(px0, 0), near_z0))
+    fwd0, near_z0, wo = tie((scan(px0, 0), near_z0, wo))
     far_z0 = [lax.ppermute(v, "section", [(0, 1)]) for v in near_z0]
     win[0] = (near_z0, far_z0, near_x0, far_x0)
     pz0 = project_z(normed_in0, 0)
     g0 = gate(pz0, fwd0[0][0])
-    stat0, near_x1, pieces_z1 = tie((jnp.sum(g0 * g0, axis=1), near_x1, pieces_z1))
-    near_z1, far_z1 = fetch(pieces_z1, 1)
+    stat0 = jnp.sum(g0 * g0, axis=1)
     stat0 = sum_of_shares(stat0.reshape(n, rows)).reshape(-1)
     r0 = lax.rsqrt(stat0 / INNER + EPS)
     normed0 = gated(pz0, fwd0[0][0], r0, 0)
+    normed0, near_x1, own_ct = tie((normed0, near_x1, own_ct))
     part_ct = in_group(exchange(quarters(own_ct)))
-    normed0, wo, part_ct = tie((normed0, wo, part_ct))
     far_x1 = [lax.ppermute(v, "section", [(1, 0)]) for v in near_x1]
     mixed0 = scatter_sum(jnp.dot(normed0, wo[0], preferred_element_type=F32))
+    mixed0, part_ct, pieces_z1 = tie((mixed0, part_ct, pieces_z1))
+    near_z1, far_z1 = fetch(pieces_z1, 1)
     out0 = valid * (h0.astype(F32) + mixed0)
     h1 = out0.astype(BF16)
 
     normed_in1 = gather_rows(normalised(h1.astype(F32), small[1][0]).astype(BF16))
-    normed_in1, far_x1, part_ct, near_z1 = tie((normed_in1, far_x1, part_ct, near_z1))
+    normed_in1, far_x1 = tie((normed_in1, far_x1))
+    win[1] = (near_z1, far_z1, near_x1, far_x1)
+    px1 = project_x(normed_in1, 1)
+    px1, near_z1, part_ct = tie((px1, near_z1, part_ct))
     far_z1 = [lax.ppermute(v, "section", [(1, 0)]) for v in near_z1]
     win[1] = (near_z1, far_z1, near_x1, far_x1)
-    px1 = project_x(normed_in1, 1)
     all_ct = whole_slot(part_ct)
     fwd1 = scan(px1, 1)
     fwd1, all_ct = tie((fwd1, all_ct))
@@ -1022,14 +1029,17 @@
     full1, xs1 = with_group(d1[1], d1[2])
     back1 = back_in(d1[0], full1, 1, F32)
     gz = own_in_piece(normed_in1, d1[0], away)
-    back1, xs1, full1, gz = sums.end((back1, xs1, full1, gz))
+    out1 = valid * (h1.astype(F32) + mixed1)
+    back_h = exchange(quarters(jnp.concatenate([h1, out1.astype(BF16)])))
+    back1, xs1, full1, gz, out1, back_h = sums.end((back1, xs1, full1, gz, out1, back_h))
     z1 = sums.add(gz)
 
     sums.begin()
     dnin1 = scatter_sum(back1)
     away = away_in(normed_in1, *xs1)
     gx = own_in_piece(normed_in1, xs1[0], away, xs1[1])
-    dnin1, gx = sums.end((dnin1, gx))
+    back_h = in_group(back_h)
+    dnin1, gx, back_h = sums.end((dnin1, gx, back_h))
     x1 = sums.add(gx)
 
     sums.begin()
@@ -1039,32 +1049,29 @@
     dmixed0 = gather_rows(dmixed0_own)
     along0 = to_all(jnp.sum(dmixed0_own.astype(F32) * mixed0, axis=-1)).reshape(-1)
     rc0 = scales(r0, (r0 * r0 / INNER) * along0)
-    out1 = valid * (h1.astype(F32) + mixed1)
-    grad1, dgin1, dmixed0, rc0, out1 = sums.end((grad1, dgin1, dmixed0, rc0, out1))
+    back_h = joined(exchange(back_h))
+    grad1, dgin1, dmixed0, rc0, back_h = sums.end((grad1, dgin1, dmixed0, rc0, back_h))
 
     sums.begin()
-    back_h = exchange(quarters(jnp.concatenate([h1, out1.astype(BF16)])))
     dn0 = dot_cols(dmixed0, wo[0])
     d0 = unscan(pz0, px0, fwd0, dn0, rc0, 0)
     go = own_out_piece(normed0, dmixed0, away_out(normed0, dmixed0))
-    d0, go, back_h = sums.end((d0, go, back_h))
+    d0, go = sums.end((d0, go))
     o0 = sums.add(go)
 
     sums.begin()
-    back_h = in_group(back_h)
     away = away_in(normed_in0, d0[0])
     full0, xs0 = with_group(d0[1], d0[2])
     gz = own_in_piece(normed_in0, d0[0], away)
     away = away_in(normed_in0, *xs0)
     gx = own_in_piece(normed_in0, xs0[0], away, xs0[1])
-    full0, gz, gx, back_h = sums.end((full0, gz, gx, back_h))
+    full0, gz, gx = sums.end((full0, gz, gx))
     z0 = sums.add(gz)
 
     sums.begin()
     gx = exchange(gx)
     back0 = back_in(d0[0], full0, 0, BF16)
-    back_h = joined(exchange(back_h))
-    gx, back0, back_h = sums.end((gx, back0, back_h))
+    gx, back0 = sums.end((gx, back0))
     x0 = sums.add(gx)
 
     def hand_over(v, layer):
@@ -1101,16 +1108,16 @@
     while m < n:
         p = p + move_fsdp(p, m)
         m *= 2
+    m = 1
+    while m < nz:
+        p = p + move_seq(p, m)
+        m *= 2
     p, back_g, own_z0, own_x1, away_x1 = sums.end((p, back_g, own_z0, own_x1, away_x1))
     sums.finish([x0])
     away_z0 = hand_over(own_z0, 0)
     own_x0 = sums.values[x0]
     away_x0 = hand_over(own_x0, 0)
     back_g = joined(exchange(back_g))
-    m = 1
-    while m < nz:
-        p = p + move_seq(p, m)
-        m *= 2
     p = pick(p[0], p[1])
     back = jnp.concatenate([back_h, back_g])
 

time: 1210 us -> 1200 us (level)
  waiting for transfers between devices: 422 us -> 364 us
  blocking collectives: 6.54 us -> 48.5 us
  local copies, waits for them, and re-layouts: 110 us -> 91.8 us
  starting transfers between devices: 299 us -> 317 us
    all_to_all x1, blocking collectives: 6.54 us -> 48.5 us  [exchange(): return lax.all_to_all(v, 'fsdp', 0, 0, tiled=True)]
    ppermute x18, waiting for transfers between devices: 182 us -> 158 us  [begin(): lax.ppermute(self.values[k], 'seq', self.pairs[step])]
    ppermute x12, waiting for transfers between devices: 37.6 us -> 16.7 us  [fetch(): lax.ppermute(v, ('section', 'fsdp'), pairs(m))]
    ppermute x12, starting transfers between devices: 24.5 us -> 44.6 us  [swap_section(): return lax.ppermute(v, 'section', [(0, 1), (1, 0)])]
    unnamed x184 -> x177, local copies, waits for them, and re-layouts: 47.3 us -> 30.1 us
    ppermute x2, waiting for transfers between devices: 4.37 us -> 20.1 us  [move_seq(): return lax.ppermute(v, 'seq', [(k, k ^ m) for k in range(s)])]
    all_to_all x4, waiting for transfers between devices: 41 us -> 25.7 us  [in_group(): return lax.all_to_all(v, 'seq', 0, 0, axis_index_groups=groups, tiled=True)]
    all_to_all x23 -> x22, waiting for transfers between devices: 96.4 us -> 101 us  [exchange(): return lax.all_to_all(v, 'fsdp', 0, 0, tiled=True)]
  transfers between devices with their start and end apart: 96 -> 95, of which waited for: 41 -> 34; matrix products, arithmetic and copies ran while one was open for 14% -> 15% of each run, Pallas kernels for 13% -> 13%
where the time goes in v9:
time: 1200 us; the launch traced here: 1180 us
  waiting for transfers between devices  364 us (30%)
  starting transfers between devices  317 us (26%)
  Pallas kernels  197 us (16%)
  local copies, waits for them, and re-layouts  91.8 us (8%)
  other arithmetic  79.5 us (7%)
  matrix products  79.3 us (7%)
  blocking collectives  48.5 us (4%)
    ppermute x18, waiting for transfers between devices, begin(): lax.ppermute(self.values[k], 'seq', self.pairs[step])  158 us
    all_to_all x22, waiting for transfers between devices, exchange(): return lax.all_to_all(v, 'fsdp', 0, 0, tiled=True)  101 us
    all_to_all x22, starting transfers between devices, exchange(): return lax.all_to_all(v, 'fsdp', 0, 0, tiled=True)  98.1 us
    pallas_call x10, Pallas kernels, combine(): pl.pallas_call(functools.partial(combine_kernel, adds=tuple((add for _, _...  67.5 us
    ppermute x18, starting transfers between devices, begin(): lax.ppermute(self.values[k], 'seq', self.pairs[step])  65.1 us
    dot_general x16, matrix products, dot_rows(): lax.dot_general(a, b, (((0,), (0,)), ((), ())), preferred_element_type=F32)  55.3 us
    all_to_all x1, blocking collectives, exchange(): return lax.all_to_all(v, 'fsdp', 0, 0, tiled=True)  48.5 us
    ppermute x12, starting transfers between devices, swap_section(): return lax.ppermute(v, 'section', [(0, 1), (1, 0)])  44.6 us
  transfers between devices with their start and end apart: 95, of which 34 were waited for; matrix products, arithmetic and copies ran while one was open for 15% of the time, Pallas kernels for 13%

profile of v9, /device:TPU:1, one launch (start us, length us, event | category | flops | bytes accessed | tf_op | source)
XLA Modules:
  0.0 1181.7 jit_solution(14553407050623846970)
XLA Ops:
  15.6 5.7 dynamic-slice_bitcast_fusion
  29.4 4.7 all-to-all-start.1
  34.2 5.2 collective-permute-start.3
  55.8 17.2 %all-to-all-done.2 = bf16[4,512,512]{2,1,0:T(8,128)(2,1)} async-done(((bf16[4,512,512]{2,1,0:T(8,128)(2,1)}), bf16[4,512,512]{2,1,0:T(8,128)(2,1)}, u32[]{:S(2)}, u32[]{:S(2)}) %all-to-all-start.2) | async-done | bytes 2097184 | tf_op jit(solution)/shard_map/all_to_all | solution.py:586
  82.1 8.7 project.4.proj
  90.9 26.4 %collective-permute-start.12 = (bf16[1024,2048]{1,0:T(8,128)(2,1)}, bf16[1024,2048]{1,0:T(8,128)(2,1)}, u32[]{:S(2)}, u32[]{:S(2)}) collective-permute-start(bf16[1024,2048]{1,0:T(8,128)(2,1)} %bitcast.36), channel_id=1, source_target_pairs={{0,16},{16,0},{1,17},{17,1},{2,18},{18,2},{3,19},{19,3},{4,20},{20... | collective-permute-start | bytes 12582920 | tf_op jit(solution)/shard_map/ppermute | solution.py:578
  121.8 10.6 scan_forward.2
  132.4 7.3 broadcast_select_fusion
  148.1 5.8 collective-permute-done.13.refs_4_.refs_8_
  161.3 6.8 project.5.pz
  175.6 11.4 all-to-all-done.3
  194.0 6.9 fusion.115
  200.9 48.5 %all_to_all.136 = f32[4,128,2048]{2,1,0:T(8,128)} all-to-all(f32[4,128,2048]{2,1,0:T(8,128)} %bitcast.289), channel_id=1, replica_groups=mesh['section'=2,'seq'=4,'fsdp'=4] {'fsdp'}, dimensions={0} | all-to-all | bytes 8388608 | tf_op jit(solution)/shard_map/all_to_all | solution.py:586
  270.5 11.2 all-to-all-start.7
  296.5 6.6 all-to-all-done.7
  303.1 7.7 project.6.proj
  314.2 13.4 %collective-permute-done.26.refs_3_ = bf16[1024,512]{1,0:T(8,128)(2,1)} collective-permute-done((bf16[1024,512]{1,0:T(8,128)(2,1)}, bf16[1024,512]{1,0:T(8,128)(2,1)}, u32[]{:S(2)}, u32[]{:S(2)}) %collective-permute-start.26) | collective-permute-done | bytes 1048608 | tf_op jit(solution)/shard_map/ppermute | solution.py:767
  340.3 10.6 scan_forward.3
  356.0 6.6 project.7.pz
  366.5 6.9 multiply_reduce_fusion.2
  390.8 4.9 add_convert_fusion.5.refs_0_
  395.7 5.3 collective-permute-start.32
  409.2 20.4 %scan_backward.2 = (bf16[512,1024]{1,0:T(8,128)(2,1)S(1)}, bf16[512,1296]{1,0:T(8,128)(2,1)S(1)}, f32[4,512,64]{2,1,0:T(8,128)S(1)}, f32[8,1024]{1,0:T(8,128)S(1...) custom-call(f32[512,1024]{1,0:T(8,128)} %project.7.pz, ...), custom_call_target="tpu_custom_call" | custom-call | tf_op jit(solution)/shard_map/scan_backward/pallas_call | solution.py:303
  436.8 8.0 collective-permute-done.32.refs_1_
  444.8 6.2 combine.10.refs_0_
  481.4 11.0 project_back.2
  492.5 4.8 combine.11.refs_0_
  498.6 4.8 add_convert_fusion.4
  503.5 5.0 all-to-all-start.13
  509.8 16.6 %collective-permute-start.38 = (bf16[4,512,512]{2,1,0:T(8,128)(2,1)}, bf16[4,512,512]{2,1,0:T(8,128)(2,1)}, u32[]{:S(2)}, u32[]{:S(2)}) collective-permute-start(bf16[4,512,512]{2,1,0:T(8,128)(2,1)} %bitcast.313), channel_id=1, source_target_pairs={{0,4},{12,8},{1,5},{13,9},{2,6},{14,10},{3,7},{15,11},{16,20},{28,... | collective-permute-start | bytes 6291464 | tf_op jit(solution)/shard_map/ppermute | solution.py:650
  532.3 23.0 %all-to-all-done.13 = f32[4,128,2048]{2,1,0:T(8,128)} async-done(((f32[4,128,2048]{2,1,0:T(8,128)}), f32[4,128,2048]{2,1,0:T(8,128)}, u32[]{:S(2)}, u32[]{:S(2)}) %all-to-all-start.13) | async-done | bytes 4194336 | tf_op jit(solution)/shard_map/all_to_all | solution.py:586
  555.4 14.1 %all-to-all-start.14 = ((bf16[4,256,512]{2,1,0:T(8,128)(2,1)}), bf16[4,256,512]{2,1,0:T(8,128)(2,1)}, u32[]{:S(2)}, u32[]{:S(2)}) async-start(bf16[4,256,512]{2,1,0:T(8,128)(2,1)} %all-to-all-done.12), calls=%async_computation.14 | async-start | bytes 2097152 | tf_op jit(solution)/shard_map/all_to_all | solution.py:607
  578.0 6.9 combine.12
  614.1 11.1 all-to-all-done.17
  633.8 23.9 %collective-permute-done.40 = bf16[4,576,512]{2,1,0:T(8,128)(2,1)} collective-permute-done((bf16[4,576,512]{2,1,0:T(8,128)(2,1)}, bf16[4,576,512]{2,1,0:T(8,128)(2,1)}, u32[]{:S(2)}, u32[]{:S(2)}) %collective-permute-start.40) | collective-permute-done | bytes 2359328 | tf_op jit(solution)/shard_map/ppermute | solution.py:650
  657.6 6.8 combine.13
  673.5 6.5 fusion.116.dn
  680.0 20.5 %scan_backward.3 = (bf16[512,1024]{1,0:T(8,128)(2,1)S(1)}, bf16[512,1296]{1,0:T(8,128)(2,1)S(1)}, f32[4,512,64]{2,1,0:T(8,128)S(1)}, f32[8,1024]{1,0:T(8,128)S(1...) custom-call(f32[512,1024]{1,0:T(8,128)} %project.5.pz, ...), custom_call_target="tpu_custom_call" | custom-call | tf_op jit(solution)/shard_map/scan_backward/pallas_call | solution.py:303
  700.5 5.6 add_convert_fusion.2.refs_2_
  706.1 18.9 %collective-permute-done.42 = bf16[4,512,512]{2,1,0:T(8,128)(2,1)S(1)} collective-permute-done((bf16[4,512,512]{2,1,0:T(8,128)(2,1)S(1)}, bf16[4,512,512]{2,1,0:T(8,128)(2,1)S(1)}, u32[]{:S(2)}, u32[]{:S(2)}) %collective-permute-start.42) | collective-permute-done | bytes 2097184 | tf_op jit(solution)/shard_map/ppermute | solution.py:650
  727.1 6.8 combine.14
  749.6 8.8 collective-permute-start.48
  774.8 26.6 %collective-permute-done.48.refs_3_ = bf16[512,2048]{1,0:T(8,128)(2,1)} collective-permute-done((bf16[512,2048]{1,0:T(8,128)(2,1)}, bf16[512,2048]{1,0:T(8,128)(2,1)}, u32[]{:S(2)}, u32[]{:S(2)}) %collective-permute-start.48) | collective-permute-done | bytes 2097184 | tf_op jit(solution)/shard_map/ppermute | solution.py:650
  801.4 7.2 combine.15
  810.8 6.5 collective-permute-start.50
  824.2 10.7 project_back.3
  834.9 24.3 %collective-permute-done.50 = bf16[4,512,512]{2,1,0:T(8,128)(2,1)} collective-permute-done((bf16[4,512,512]{2,1,0:T(8,128)(2,1)}, bf16[4,512,512]{2,1,0:T(8,128)(2,1)}, u32[]{:S(2)}, u32[]{:S(2)}) %collective-permute-start.50) | collective-permute-done | bytes 2097184 | tf_op jit(solution)/shard_map/ppermute | solution.py:650
  859.2 7.6 combine.16
  870.4 5.6 collective-permute-start.54
  880.6 14.2 %all-to-all-done.20 = bf16[4,128,2048]{2,1,0:T(8,128)(2,1)S(1)} async-done(((bf16[4,128,2048]{2,1,0:T(8,128)(2,1)}), bf16[4,128,2048]{2,1,0:T(8,128)(2,1)S(1)}, u32[]{:S(2)}, u32[]{:S(2)}) %all-to-all-start.20) | async-done | bytes 2097184 | tf_op jit(solution)/shard_map/all_to_all | solution.py:586
  906.6 15.6 %collective-permute-done.52.refs_1_ = bf16[512,2048]{1,0:T(8,128)(2,1)} collective-permute-done((bf16[512,2048]{1,0:T(8,128)(2,1)}, bf16[512,2048]{1,0:T(8,128)(2,1)}, u32[]{:S(2)}, u32[]{:S(2)}) %collective-permute-start.52) | collective-permute-done | bytes 2097184 | tf_op jit(solution)/shard_map/ppermute | solution.py:650
  922.5 9.2 combine.17
  931.8 5.0 all-to-all-start.23
  954.1 5.8 collective-permute-start.57
  969.5 40.7 %collective-permute-done.58 = bf16[4,512,512]{2,1,0:T(8,128)(2,1)} collective-permute-done((bf16[4,512,512]{2,1,0:T(8,128)(2,1)}, bf16[4,512,512]{2,1,0:T(8,128)(2,1)}, u32[]{:S(2)}, u32[]{:S(2)}) %collective-permute-start.58) | collective-permute-done | bytes 2097184 | tf_op jit(solution)/shard_map/ppermute | solution.py:650
  1010.2 7.8 combine.18
  1018.0 11.9 %all-to-all-start.24 = ((bf16[4,256,512]{2,1,0:T(8,128)(2,1)}), bf16[4,256,512]{2,1,0:T(8,128)(2,1)}, u32[]{:S(2)}, u32[]{:S(2)}) async-start(bf16[4,256,512]{2,1,0:T(8,128)(2,1)} %all-to-all-done.22), calls=%async_computation.24 | async-start | bytes 2097152 | tf_op jit(solution)/shard_map/all_to_all | solution.py:607
  1034.2 21.7 %all-to-all-done.24 = bf16[4,256,512]{2,1,0:T(8,128)(2,1)} async-done(((bf16[4,256,512]{2,1,0:T(8,128)(2,1)}), bf16[4,256,512]{2,1,0:T(8,128)(2,1)}, u32[]{:S(2)}, u32[]{:S(2)}) %all-to-all-start.24) | async-done | bytes 1048608 | tf_op jit(solution)/shard_map/all_to_all | solution.py:607
  1062.2 28.4 %collective-permute-done.61 = f32[2,28099]{1,0:T(2,128)S(1)} collective-permute-done((f32[2,28099]{1,0:T(2,128)S(1)}, f32[2,28099]{1,0:T(2,128)S(1)}, u32[]{:S(2)}, u32[]{:S(2)}) %collective-permute-start.61) | collective-permute-done | bytes 224824 | tf_op jit(solution)/shard_map/ppermute | solution.py:621
  1093.5 11.9 %collective-permute-done.62 = f32[2,28099]{1,0:T(2,128)S(1)} collective-permute-done((f32[2,28099]{1,0:T(2,128)S(1)}, f32[2,28099]{1,0:T(2,128)S(1)}, u32[]{:S(2)}, u32[]{:S(2)}) %collective-permute-start.62) | collective-permute-done | bytes 224824 | tf_op jit(solution)/shard_map/ppermute | solution.py:626
  1109.9 8.2 collective-permute-done.63
  1133.8 7.7 all-to-all-done.26
  1165.5 7.0 place_in.2.refs_5_
  1172.4 8.8 place_in.3
  (553 shorter events, 417.2 us)
Async XLA Ops:
  23.4 20.1 %collective-permute-start = (bf16[1296,512]{1,0:T(8,128)(2,1)}, bf16[1296,512]{1,0:T(8,128)(2,1)}, u32[]{:S(2)}, u32[]{:S(2)}) collective-permute-start(bf16[1296,512]{1,0:T(8,128)(2,1)} %get-tuple-element.233), channel_id=1, source_target_pairs={{0,1},{1,0},{2,3},{3,2},{4,5},{5,4},{6,7},{7,6},{8,9},{9,8},{10,11... | collective-permute-start | bytes 3981320 | tf_op jit(solution)/shard_map/ppermute | solution.py:767
  34.2 21.5 %collective-permute-start.3 = (bf16[4,7024]{1,0:T(4,128)(2,1)S(1)}, bf16[4,7024]{1,0:T(4,128)(2,1)S(1)}, u32[]{:S(2)}, u32[]{:S(2)}) collective-permute-start(bf16[4,7024]{1,0:T(4,128)(2,1)S(1)} %slice.277), channel_id=1, source_target_pairs={{0,16},{16,0},{1,17},{17,1},{2,18},{18,2},{3,19},{19,3},{4,20},{20... | collective-permute-start | bytes 168584 | tf_op jit(solution)/shard_map/ppermute | solution.py:578
  43.5 36.1 %collective-permute-start.4 = (bf16[1296,512]{1,0:T(8,128)(2,1)S(1)}, bf16[1296,512]{1,0:T(8,128)(2,1)}, u32[]{:S(2)}, u32[]{:S(2)}) collective-permute-start(bf16[1296,512]{1,0:T(8,128)(2,1)S(1)} %get-tuple-element.245.refs_0_.refs_4_), channel_id=1, source_target_pairs={{0,16},{1,17},{2,18},{3,19},{4,20},{5,21},{6,22},{7,23},{8,24},{9,... | collective-permute-start | bytes 3981320 | tf_op jit(solution)/shard_map/ppermute | solution.py:796
  44.8 34.8 %collective-permute-start.5 = (bf16[1296,512]{1,0:T(8,128)(2,1)}, bf16[1296,512]{1,0:T(8,128)(2,1)}, u32[]{:S(2)}, u32[]{:S(2)}) collective-permute-start(bf16[1296,512]{1,0:T(8,128)(2,1)} %collective-permute-done.refs_1_.refs_5_), channel_id=1, source_target_pairs={{0,16},{1,17},{2,18},{3,19},{4,20},{5,21},{6,22},{7,23},{8,24},{9,... | collective-permute-start | bytes 3981320 | tf_op jit(solution)/shard_map/ppermute | solution.py:796
  46.1 33.6 %collective-permute-start.6 = (bf16[1296,512]{1,0:T(8,128)(2,1)}, bf16[1296,512]{1,0:T(8,128)(2,1)}, u32[]{:S(2)}, u32[]{:S(2)}) collective-permute-start(bf16[1296,512]{1,0:T(8,128)(2,1)} %collective-permute-done.1.refs_2_.refs_6_), channel_id=1, source_target_pairs={{0,16},{1,17},{2,18},{3,19},{4,20},{5,21},{6,22},{7,23},{8,24},{9,... | collective-permute-start | bytes 3981320 | tf_op jit(solution)/shard_map/ppermute | solution.py:796
  47.4 34.7 %collective-permute-start.7 = (bf16[1296,512]{1,0:T(8,128)(2,1)}, bf16[1296,512]{1,0:T(8,128)(2,1)}, u32[]{:S(2)}, u32[]{:S(2)}) collective-permute-start(bf16[1296,512]{1,0:T(8,128)(2,1)} %collective-permute-done.2.refs_3_.refs_7_), channel_id=1, source_target_pairs={{0,16},{1,17},{2,18},{3,19},{4,20},{5,21},{6,22},{7,23},{8,24},{9,... | collective-permute-start | bytes 3981320 | tf_op jit(solution)/shard_map/ppermute | solution.py:796
  51.2 21.8 %all-to-all-start.2 = ((bf16[4,512,512]{2,1,0:T(8,128)(2,1)}), bf16[4,512,512]{2,1,0:T(8,128)(2,1)}, u32[]{:S(2)}, u32[]{:S(2)}) async-start(bf16[4,512,512]{2,1,0:T(8,128)(2,1)} %broadcast_in_dim.54), calls=%async_computation.2 | async-start | bytes 4194304 | tf_op jit(solution)/shard_map/all_to_all | solution.py:586
  90.9 41.5 %collective-permute-start.12 = (bf16[1024,2048]{1,0:T(8,128)(2,1)}, bf16[1024,2048]{1,0:T(8,128)(2,1)}, u32[]{:S(2)}, u32[]{:S(2)}) collective-permute-start(bf16[1024,2048]{1,0:T(8,128)(2,1)} %bitcast.36), channel_id=1, source_target_pairs={{0,16},{16,0},{1,17},{17,1},{2,18},{18,2},{3,19},{19,3},{4,20},{20... | collective-permute-start | bytes 12582920 | tf_op jit(solution)/shard_map/ppermute | solution.py:578
  119.0 20.8 %collective-permute-start.9 = (bf16[1024,512]{1,0:T(8,128)(2,1)}, bf16[1024,512]{1,0:T(8,128)(2,1)S(1)}, u32[]{:S(2)}, u32[]{:S(2)}) collective-permute-start(bf16[1024,512]{1,0:T(8,128)(2,1)} %get-tuple-element.255), channel_id=1, source_target_pairs={{0,1},{1,0},{2,3},{3,2},{4,5},{5,4},{6,7},{7,6},{8,9},{9,8},{10,11... | collective-permute-start | bytes 3145736 | tf_op jit(solution)/shard_map/ppermute | solution.py:767
  119.7 20.1 %collective-permute-start.10 = (bf16[1024,512]{1,0:T(8,128)(2,1)}, bf16[1024,512]{1,0:T(8,128)(2,1)S(1)}, u32[]{:S(2)}, u32[]{:S(2)}) collective-permute-start(bf16[1024,512]{1,0:T(8,128)(2,1)} %get-tuple-element.256), channel_id=1, source_target_pairs={{0,2},{1,3},{2,0},{3,1},{4,6},{5,7},{6,4},{7,5},{8,10},{9,11},{10,... | collective-permute-start | bytes 3145736 | tf_op jit(solution)/shard_map/ppermute | solution.py:767
  120.4 19.4 %collective-permute-start.11 = (bf16[1024,512]{1,0:T(8,128)(2,1)}, bf16[1024,512]{1,0:T(8,128)(2,1)S(1)}, u32[]{:S(2)}, u32[]{:S(2)}) collective-permute-start(bf16[1024,512]{1,0:T(8,128)(2,1)} %get-tuple-element.257), channel_id=1, source_target_pairs={{0,3},{1,2},{2,1},{3,0},{4,7},{5,6},{6,5},{7,4},{8,11},{9,10},{10,... | collective-permute-start | bytes 3145736 | tf_op jit(solution)/shard_map/ppermute | solution.py:767
  145.0 44.9 %collective-permute-start.17 = (bf16[1296,512]{1,0:T(8,128)(2,1)}, bf16[1296,512]{1,0:T(8,128)(2,1)}, u32[]{:S(2)}, u32[]{:S(2)}) collective-permute-start(bf16[1296,512]{1,0:T(8,128)(2,1)} %get-tuple-element.233), channel_id=1, source_target_pairs={{16,17},{17,16},{18,19},{19,18},{20,21},{21,20},{22,23},{23,22},{2... | collective-permute-start | bytes 3981320 | tf_op jit(solution)/shard_map/ppermute | solution.py:767
  153.9 36.0 %collective-permute-start.18 = (bf16[1296,512]{1,0:T(8,128)(2,1)}, bf16[1296,512]{1,0:T(8,128)(2,1)}, u32[]{:S(2)}, u32[]{:S(2)}) collective-permute-start(bf16[1296,512]{1,0:T(8,128)(2,1)} %get-tuple-element.234), channel_id=1, source_target_pairs={{16,18},{17,19},{18,16},{19,17},{20,22},{21,23},{22,20},{23,21},{2... | collective-permute-start | bytes 3981320 | tf_op jit(solution)/shard_map/ppermute | solution.py:767
  155.9 34.0 %collective-permute-start.19 = (bf16[1296,512]{1,0:T(8,128)(2,1)}, bf16[1296,512]{1,0:T(8,128)(2,1)}, u32[]{:S(2)}, u32[]{:S(2)}) collective-permute-start(bf16[1296,512]{1,0:T(8,128)(2,1)} %get-tuple-element.235), channel_id=1, source_target_pairs={{16,19},{17,18},{18,17},{19,16},{20,23},{21,22},{22,21},{23,20},{2... | collective-permute-start | bytes 3981320 | tf_op jit(solution)/shard_map/ppermute | solution.py:767
  257.3 32.4 %collective-permute-start.20 = (bf16[1296,512]{1,0:T(8,128)(2,1)S(1)}, bf16[1296,512]{1,0:T(8,128)(2,1)}, u32[]{:S(2)}, u32[]{:S(2)}) collective-permute-start(bf16[1296,512]{1,0:T(8,128)(2,1)S(1)} %get-tuple-element.245.refs_0_.refs_4_), channel_id=1, source_target_pairs={{16,0},{17,1},{18,2},{19,3},{20,4},{21,5},{22,6},{23,7},{24,8},{25... | collective-permute-start | bytes 3981320 | tf_op jit(solution)/shard_map/ppermute | solution.py:906
  259.7 33.7 %collective-permute-start.21 = (bf16[1296,512]{1,0:T(8,128)(2,1)}, bf16[1296,512]{1,0:T(8,128)(2,1)}, u32[]{:S(2)}, u32[]{:S(2)}) collective-permute-start(bf16[1296,512]{1,0:T(8,128)(2,1)} %collective-permute-done.17.refs_1_.refs_5_), channel_id=1, source_target_pairs={{16,0},{17,1},{18,2},{19,3},{20,4},{21,5},{22,6},{23,7},{24,8},{25... | collective-permute-start | bytes 3981320 | tf_op jit(solution)/shard_map/ppermute | solution.py:906
  270.5 32.6 %all-to-all-start.7 = ((bf16[4,128,2048]{2,1,0:T(8,128)(2,1)}), bf16[4,128,2048]{2,1,0:T(8,128)(2,1)}, u32[]{:S(2)}, u32[]{:S(2)}) async-start(bf16[4,128,2048]{2,1,0:T(8,128)(2,1)} %broadcast_in_dim.59), calls=%async_computation.7 | async-start | bytes 4194304 | tf_op jit(solution)/shard_map/all_to_all | solution.py:586
  286.4 27.0 %collective-permute-start.24 = (bf16[1024,512]{1,0:T(8,128)(2,1)}, bf16[1024,512]{1,0:T(8,128)(2,1)}, u32[]{:S(2)}, u32[]{:S(2)}) collective-permute-start(bf16[1024,512]{1,0:T(8,128)(2,1)} %get-tuple-element.255), channel_id=1, source_target_pairs={{16,17},{17,16},{18,19},{19,18},{20,21},{21,20},{22,23},{23,22},{2... | collective-permute-start | bytes 3145736 | tf_op jit(solution)/shard_map/ppermute | solution.py:767
  289.7 24.4 %collective-permute-start.25 = (bf16[1024,512]{1,0:T(8,128)(2,1)}, bf16[1024,512]{1,0:T(8,128)(2,1)}, u32[]{:S(2)}, u32[]{:S(2)}) collective-permute-start(bf16[1024,512]{1,0:T(8,128)(2,1)} %get-tuple-element.256), channel_id=1, source_target_pairs={{16,18},{17,19},{18,16},{19,17},{20,22},{21,23},{22,20},{23,21},{2... | collective-permute-start | bytes 3145736 | tf_op jit(solution)/shard_map/ppermute | solution.py:767
  293.4 34.1 %collective-permute-start.26 = (bf16[1024,512]{1,0:T(8,128)(2,1)}, bf16[1024,512]{1,0:T(8,128)(2,1)}, u32[]{:S(2)}, u32[]{:S(2)}) collective-permute-start(bf16[1024,512]{1,0:T(8,128)(2,1)} %get-tuple-element.257), channel_id=1, source_target_pairs={{16,19},{17,18},{18,17},{19,16},{20,23},{21,22},{22,21},{23,20},{2... | collective-permute-start | bytes 3145736 | tf_op jit(solution)/shard_map/ppermute | solution.py:767
  330.3 33.4 %all-to-all-start.8 = ((bf16[4,512,512]{2,1,0:T(8,128)(2,1)}), bf16[4,512,512]{2,1,0:T(8,128)(2,1)}, u32[]{:S(2)}, u32[]{:S(2)}) async-start(bf16[4,512,512]{2,1,0:T(8,128)(2,1)} %broadcast_in_dim.61), calls=%async_computation.8 | async-start | bytes 4194304 | tf_op jit(solution)/shard_map/all_to_all | solution.py:586
  395.7 49.1 %collective-permute-start.32 = (bf16[512,2048]{1,0:T(8,128)(2,1)}, bf16[512,2048]{1,0:T(8,128)(2,1)}, u32[]{:S(2)}, u32[]{:S(2)}) collective-permute-start(bf16[512,2048]{1,0:T(8,128)(2,1)} %add_convert_fusion.5.refs_0_), channel_id=1, source_target_pairs={{0,4},{12,8},{1,5},{13,9},{2,6},{14,10},{3,7},{15,11},{16,20},{28,... | collective-permute-start | bytes 6291464 | tf_op jit(solution)/shard_map/ppermute | solution.py:650
  404.7 29.1 %all-to-all-start.10 = ((bf16[4,128,2048]{2,1,0:T(8,128)(2,1)}), bf16[4,128,2048]{2,1,0:T(8,128)(2,1)}, u32[]{:S(2)}, u32[]{:S(2)}) async-start(bf16[4,128,2048]{2,1,0:T(8,128)(2,1)} %bitcast.307), calls=%async_computation.10 | async-start | bytes 4194304 | tf_op jit(solution)/shard_map/all_to_all | solution.py:586
  451.0 41.5 %collective-permute-start.34 = (bf16[512,2048]{1,0:T(8,128)(2,1)}, bf16[512,2048]{1,0:T(8,128)(2,1)}, u32[]{:S(2)}, u32[]{:S(2)}) collective-permute-start(bf16[512,2048]{1,0:T(8,128)(2,1)} %combine.10.refs_0_), channel_id=1, source_target_pairs={{4,8},{8,4},{5,9},{9,5},{6,10},{10,6},{7,11},{11,7},{20,24},{24,20... | collective-permute-start | bytes 6291464 | tf_op jit(solution)/shard_map/ppermute | solution.py:650
  457.3 41.3 %collective-permute-start.33 = (bf16[2048,512]{1,0:T(8,128)(2,1)}, bf16[2048,512]{1,0:T(8,128)(2,1)}, u32[]{:S(2)}, u32[]{:S(2)}) collective-permute-start(bf16[2048,512]{1,0:T(8,128)(2,1)} %convolution_convert_fusion.5), channel_id=1, source_target_pairs={{0,16},{16,0},{1,17},{17,1},{2,18},{18,2},{3,19},{19,3},{4,20},{20... | collective-permute-start | bytes 6291464 | tf_op jit(solution)/shard_map/ppermute | solution.py:578
  473.0 30.5 %all-to-all-start.12 = ((bf16[4,256,512]{2,1,0:T(8,128)(2,1)}), bf16[4,256,512]{2,1,0:T(8,128)(2,1)}, u32[]{:S(2)}, u32[]{:S(2)}) async-start(bf16[4,256,512]{2,1,0:T(8,128)(2,1)} %bitcast.290), calls=%async_computation.12 | async-start | bytes 2097152 | tf_op jit(solution)/shard_map/all_to_all | solution.py:586
  503.5 51.9 %all-to-all-start.13 = ((f32[4,128,2048]{2,1,0:T(8,128)}), f32[4,128,2048]{2,1,0:T(8,128)}, u32[]{:S(2)}, u32[]{:S(2)}) async-start(f32[4,128,2048]{2,1,0:T(8,128)} %bitcast.282), calls=%async_computation.13 | async-start | bytes 8388608 | tf_op jit(solution)/shard_map/all_to_all | solution.py:586
  508.5 69.5 %collective-permute-start.37 = (bf16[512,2048]{1,0:T(8,128)(2,1)}, bf16[512,2048]{1,0:T(8,128)(2,1)}, u32[]{:S(2)}, u32[]{:S(2)}) collective-permute-start(bf16[512,2048]{1,0:T(8,128)(2,1)} %copy-done.5), channel_id=1, source_target_pairs={{4,0},{8,12},{5,1},{9,13},{6,2},{10,14},{7,3},{11,15},{20,16},{24,... | collective-permute-start | bytes 6291464 | tf_op jit(solution)/shard_map/ppermute | solution.py:650
  509.8 68.2 %collective-permute-start.38 = (bf16[4,512,512]{2,1,0:T(8,128)(2,1)}, bf16[4,512,512]{2,1,0:T(8,128)(2,1)}, u32[]{:S(2)}, u32[]{:S(2)}) collective-permute-start(bf16[4,512,512]{2,1,0:T(8,128)(2,1)} %bitcast.313), channel_id=1, source_target_pairs={{0,4},{12,8},{1,5},{13,9},{2,6},{14,10},{3,7},{15,11},{16,20},{28,... | collective-permute-start | bytes 6291464 | tf_op jit(solution)/shard_map/ppermute | solution.py:650
  530.5 54.4 %collective-permute-start.35 = (bf16[2048,512]{1,0:T(8,128)(2,1)}, bf16[2048,512]{1,0:T(8,128)(2,1)}, u32[]{:S(2)}, u32[]{:S(2)}) collective-permute-start(bf16[2048,512]{1,0:T(8,128)(2,1)} %convolution_convert_fusion.4), channel_id=1, source_target_pairs={{0,16},{16,0},{1,17},{17,1},{2,18},{18,2},{3,19},{19,3},{4,20},{20... | collective-permute-start | bytes 6291464 | tf_op jit(solution)/shard_map/ppermute | solution.py:578
  555.4 40.6 %all-to-all-start.14 = ((bf16[4,256,512]{2,1,0:T(8,128)(2,1)}), bf16[4,256,512]{2,1,0:T(8,128)(2,1)}, u32[]{:S(2)}, u32[]{:S(2)}) async-start(bf16[4,256,512]{2,1,0:T(8,128)(2,1)} %all-to-all-done.12), calls=%async_computation.14 | async-start | bytes 2097152 | tf_op jit(solution)/shard_map/all_to_all | solution.py:607
  604.9 52.7 %collective-permute-start.40 = (bf16[4,576,512]{2,1,0:T(8,128)(2,1)}, bf16[4,576,512]{2,1,0:T(8,128)(2,1)}, u32[]{:S(2)}, u32[]{:S(2)}) collective-permute-start(bf16[4,576,512]{2,1,0:T(8,128)(2,1)} %pad_maximum_fusion.4), channel_id=1, source_target_pairs={{0,4},{12,8},{1,5},{13,9},{2,6},{14,10},{3,7},{15,11},{16,20},{28,... | collective-permute-start | bytes 7077896 | tf_op jit(solution)/shard_map/ppermute | solution.py:650
  612.1 21.6 %collective-permute-start.39 = (bf16[4,512,512]{2,1,0:T(8,128)(2,1)}, bf16[4,512,512]{2,1,0:T(8,128)(2,1)}, u32[]{:S(2)}, u32[]{:S(2)}) collective-permute-start(bf16[4,512,512]{2,1,0:T(8,128)(2,1)} %bitcast.273), channel_id=1, source_target_pairs={{4,8},{8,4},{5,9},{9,5},{6,10},{10,6},{7,11},{11,7},{20,24},{24,20... | collective-permute-start | bytes 6291464 | tf_op jit(solution)/shard_map/ppermute | solution.py:650
  627.8 38.0 %all-to-all-start.15 = ((bf16[4,128,2048]{2,1,0:T(8,128)(2,1)}), bf16[4,128,2048]{2,1,0:T(8,128)(2,1)}, u32[]{:S(2)}, u32[]{:S(2)}) async-start(bf16[4,128,2048]{2,1,0:T(8,128)(2,1)} %broadcast_in_dim.65), calls=%async_computation.15 | async-start | bytes 4194304 | tf_op jit(solution)/shard_map/all_to_all | solution.py:586
  670.2 30.3 %collective-permute-start.41 = (bf16[512,2048]{1,0:T(8,128)(2,1)}, bf16[512,2048]{1,0:T(8,128)(2,1)}, u32[]{:S(2)}, u32[]{:S(2)}) collective-permute-start(bf16[512,2048]{1,0:T(8,128)(2,1)} %convolution_convert_fusion.3), channel_id=1, source_target_pairs={{0,16},{16,0},{1,17},{17,1},{2,18},{18,2},{3,19},{19,3},{4,20},{20... | collective-permute-start | bytes 6291464 | tf_op jit(solution)/shard_map/ppermute | solution.py:578
  671.4 53.6 %collective-permute-start.43 = (bf16[4,576,512]{2,1,0:T(8,128)(2,1)S(1)}, bf16[4,576,512]{2,1,0:T(8,128)(2,1)S(1)}, u32[]{:S(2)}, u32[]{:S(2)}) collective-permute-start(bf16[4,576,512]{2,1,0:T(8,128)(2,1)S(1)} %bitcast.302), channel_id=1, source_target_pairs={{4,8},{8,4},{5,9},{9,5},{6,10},{10,6},{7,11},{11,7},{20,24},{24,20... | collective-permute-start | bytes 7077896 | tf_op jit(solution)/shard_map/ppermute | solution.py:650
  672.2 52.8 %collective-permute-start.42 = (bf16[4,512,512]{2,1,0:T(8,128)(2,1)S(1)}, bf16[4,512,512]{2,1,0:T(8,128)(2,1)S(1)}, u32[]{:S(2)}, u32[]{:S(2)}) collective-permute-start(bf16[4,512,512]{2,1,0:T(8,128)(2,1)S(1)} %bitcast.274), channel_id=1, source_target_pairs={{4,0},{8,12},{5,1},{9,13},{6,2},{10,14},{7,3},{11,15},{20,16},{24,... | collective-permute-start | bytes 6291464 | tf_op jit(solution)/shard_map/ppermute | solution.py:650
  739.0 26.8 %collective-permute-start.45 = (bf16[2048,512]{1,0:T(8,128)(2,1)}, bf16[2048,512]{1,0:T(8,128)(2,1)}, u32[]{:S(2)}, u32[]{:S(2)}) collective-permute-start(bf16[2048,512]{1,0:T(8,128)(2,1)} %convolution_convert_fusion.1), channel_id=1, source_target_pairs={{0,16},{16,0},{1,17},{17,1},{2,18},{18,2},{3,19},{19,3},{4,20},{20... | collective-permute-start | bytes 6291464 | tf_op jit(solution)/shard_map/ppermute | solution.py:578
  742.4 28.0 %collective-permute-start.44 = (bf16[2048,512]{1,0:T(8,128)(2,1)}, bf16[2048,512]{1,0:T(8,128)(2,1)}, u32[]{:S(2)}, u32[]{:S(2)}) collective-permute-start(bf16[2048,512]{1,0:T(8,128)(2,1)} %convolution_convert_fusion.2), channel_id=1, source_target_pairs={{0,16},{16,0},{1,17},{17,1},{2,18},{18,2},{3,19},{19,3},{4,20},{20... | collective-permute-start | bytes 6291464 | tf_op jit(solution)/shard_map/ppermute | solution.py:578
  742.4 59.0 %collective-permute-start.47 = (bf16[4,576,512]{2,1,0:T(8,128)(2,1)}, bf16[4,576,512]{2,1,0:T(8,128)(2,1)}, u32[]{:S(2)}, u32[]{:S(2)}) collective-permute-start(bf16[4,576,512]{2,1,0:T(8,128)(2,1)} %bitcast.81), channel_id=1, source_target_pairs={{4,0},{8,12},{5,1},{9,13},{6,2},{10,14},{7,3},{11,15},{20,16},{24,... | collective-permute-start | bytes 7077896 | tf_op jit(solution)/shard_map/ppermute | solution.py:650
  749.6 51.7 %collective-permute-start.48 = (bf16[512,2048]{1,0:T(8,128)(2,1)}, bf16[512,2048]{1,0:T(8,128)(2,1)}, u32[]{:S(2)}, u32[]{:S(2)}) collective-permute-start(bf16[512,2048]{1,0:T(8,128)(2,1)} %add_convert_fusion.2.refs_2_), channel_id=1, source_target_pairs={{0,4},{12,8},{1,5},{13,9},{2,6},{14,10},{3,7},{15,11},{16,20},{28,... | collective-permute-start | bytes 6291464 | tf_op jit(solution)/shard_map/ppermute | solution.py:650
  808.6 26.3 %collective-permute-start.49 = (bf16[512,2048]{1,0:T(8,128)(2,1)}, bf16[512,2048]{1,0:T(8,128)(2,1)}, u32[]{:S(2)}, u32[]{:S(2)}) collective-permute-start(bf16[512,2048]{1,0:T(8,128)(2,1)} %get-tuple-element.329.refs_0_), channel_id=1, source_target_pairs={{4,8},{8,4},{5,9},{9,5},{6,10},{10,6},{7,11},{11,7},{20,24},{24,20... | collective-permute-start | bytes 6291464 | tf_op jit(solution)/shard_map/ppermute | solution.py:650
  810.8 48.4 %collective-permute-start.50 = (bf16[4,512,512]{2,1,0:T(8,128)(2,1)}, bf16[4,512,512]{2,1,0:T(8,128)(2,1)}, u32[]{:S(2)}, u32[]{:S(2)}) collective-permute-start(bf16[4,512,512]{2,1,0:T(8,128)(2,1)} %bitcast.82), channel_id=1, source_target_pairs={{0,4},{12,8},{1,5},{13,9},{2,6},{14,10},{3,7},{15,11},{16,20},{28,... | collective-permute-start | bytes 6291464 | tf_op jit(solution)/shard_map/ppermute | solution.py:650
  817.2 49.6 %all-to-all-start.19 = ((bf16[4,576,512]{2,1,0:T(8,128)(2,1)}), bf16[4,576,512]{2,1,0:T(8,128)(2,1)}, u32[]{:S(2)}, u32[]{:S(2)}) async-start(bf16[4,576,512]{2,1,0:T(8,128)(2,1)} %pad_maximum_fusion.5), calls=%async_computation.19 | async-start | bytes 4718592 | tf_op jit(solution)/shard_map/all_to_all | solution.py:586
  866.8 28.0 %all-to-all-start.20 = ((bf16[4,128,2048]{2,1,0:T(8,128)(2,1)}), bf16[4,128,2048]{2,1,0:T(8,128)(2,1)S(1)}, u32[]{:S(2)}, u32[]{:S(2)}) async-start(bf16[4,128,2048]{2,1,0:T(8,128)(2,1)} %bitcast.91), calls=%async_computation.20 | async-start | bytes 4194304 | tf_op jit(solution)/shard_map/all_to_all | solution.py:586
  870.4 52.1 %collective-permute-start.54 = (bf16[4,576,512]{2,1,0:T(8,128)(2,1)}, bf16[4,576,512]{2,1,0:T(8,128)(2,1)}, u32[]{:S(2)}, u32[]{:S(2)}) collective-permute-start(bf16[4,576,512]{2,1,0:T(8,128)(2,1)} %all-to-all-done.19), channel_id=1, source_target_pairs={{0,4},{12,8},{1,5},{13,9},{2,6},{14,10},{3,7},{15,11},{16,20},{28,... | collective-permute-start | bytes 7077896 | tf_op jit(solution)/shard_map/ppermute | solution.py:650
  876.0 46.2 %collective-permute-start.52 = (bf16[512,2048]{1,0:T(8,128)(2,1)}, bf16[512,2048]{1,0:T(8,128)(2,1)}, u32[]{:S(2)}, u32[]{:S(2)}) collective-permute-start(bf16[512,2048]{1,0:T(8,128)(2,1)} %get-tuple-element.336.refs_0_), channel_id=1, source_target_pairs={{4,0},{8,12},{5,1},{9,13},{6,2},{10,14},{7,3},{11,15},{20,16},{24,... | collective-permute-start | bytes 6291464 | tf_op jit(solution)/shard_map/ppermute | solution.py:650
  877.3 44.9 %collective-permute-start.53 = (bf16[4,512,512]{2,1,0:T(8,128)(2,1)}, bf16[4,512,512]{2,1,0:T(8,128)(2,1)}, u32[]{:S(2)}, u32[]{:S(2)}) collective-permute-start(bf16[4,512,512]{2,1,0:T(8,128)(2,1)} %bitcast.90), channel_id=1, source_target_pairs={{4,8},{8,4},{5,9},{9,5},{6,10},{10,6},{7,11},{11,7},{20,24},{24,20... | collective-permute-start | bytes 6291464 | tf_op jit(solution)/shard_map/ppermute | solution.py:650
  879.3 57.6 %collective-permute-start.51 = (bf16[512,2048]{1,0:T(8,128)(2,1)}, bf16[512,2048]{1,0:T(8,128)(2,1)}, u32[]{:S(2)}, u32[]{:S(2)}) collective-permute-start(bf16[512,2048]{1,0:T(8,128)(2,1)} %get-tuple-element.373), channel_id=1, source_target_pairs={{0,16},{1,17},{2,18},{3,19},{4,20},{5,21},{6,22},{7,23},{8,24},{9,... | collective-permute-start | bytes 6291464 | tf_op jit(solution)/shard_map/ppermute | solution.py:1078
  896.1 35.6 %all-to-all-start.21 = ((bf16[4,512,512]{2,1,0:T(8,128)(2,1)}), bf16[4,512,512]{2,1,0:T(8,128)(2,1)S(1)}, u32[]{:S(2)}, u32[]{:S(2)}) async-start(bf16[4,512,512]{2,1,0:T(8,128)(2,1)} %bitcast.275), calls=%async_computation.21 | async-start | bytes 4194304 | tf_op jit(solution)/shard_map/all_to_all | solution.py:586
  931.8 32.3 %all-to-all-start.23 = ((bf16[4,576,512]{2,1,0:T(8,128)(2,1)}), bf16[4,576,512]{2,1,0:T(8,128)(2,1)}, u32[]{:S(2)}, u32[]{:S(2)}) async-start(bf16[4,576,512]{2,1,0:T(8,128)(2,1)} %bitcast.304), calls=%async_computation.23 | async-start | bytes 4718592 | tf_op jit(solution)/shard_map/all_to_all | solution.py:586
  946.2 22.1 %collective-permute-start.55 = (f32[2,28099]{1,0:T(2,128)}, f32[2,28099]{1,0:T(2,128)}, u32[]{:S(2)}, u32[]{:S(2)}) collective-permute-start(f32[2,28099]{1,0:T(2,128)} %pad_maximum_fusion.12), channel_id=1, source_target_pairs={{0,16},{16,0},{1,17},{17,1},{2,18},{18,2},{3,19},{19,3},{4,20},{20... | collective-permute-start | bytes 674384 | tf_op jit(solution)/shard_map/ppermute | solution.py:578
  952.8 65.2 %collective-permute-start.56 = (bf16[4,512,512]{2,1,0:T(8,128)(2,1)S(1)}, bf16[4,512,512]{2,1,0:T(8,128)(2,1)}, u32[]{:S(2)}, u32[]{:S(2)}) collective-permute-start(bf16[4,512,512]{2,1,0:T(8,128)(2,1)S(1)} %all-to-all-done.21.refs_1_), channel_id=1, source_target_pairs={{0,16},{1,17},{2,18},{3,19},{4,20},{5,21},{6,22},{7,23},{8,24},{9,... | collective-permute-start | bytes 6291464 | tf_op jit(solution)/shard_map/ppermute | solution.py:1078
  954.1 63.9 %collective-permute-start.57 = (bf16[512,2048]{1,0:T(8,128)(2,1)}, bf16[512,2048]{1,0:T(8,128)(2,1)}, u32[]{:S(2)}, u32[]{:S(2)}) collective-permute-start(bf16[512,2048]{1,0:T(8,128)(2,1)} %get-tuple-element.372), channel_id=1, source_target_pairs={{16,0},{17,1},{18,2},{19,3},{20,4},{21,5},{22,6},{23,7},{24,8},{25... | collective-permute-start | bytes 6291464 | tf_op jit(solution)/shard_map/ppermute | solution.py:1078
  959.9 50.3 %collective-permute-start.58 = (bf16[4,512,512]{2,1,0:T(8,128)(2,1)}, bf16[4,512,512]{2,1,0:T(8,128)(2,1)}, u32[]{:S(2)}, u32[]{:S(2)}) collective-permute-start(bf16[4,512,512]{2,1,0:T(8,128)(2,1)} %bitcast.96), channel_id=1, source_target_pairs={{4,0},{8,12},{5,1},{9,13},{6,2},{10,14},{7,3},{11,15},{20,16},{24,... | collective-permute-start | bytes 6291464 | tf_op jit(solution)/shard_map/ppermute | solution.py:650
  961.2 49.0 %collective-permute-start.59 = (bf16[4,576,512]{2,1,0:T(8,128)(2,1)}, bf16[4,576,512]{2,1,0:T(8,128)(2,1)}, u32[]{:S(2)}, u32[]{:S(2)}) collective-permute-start(bf16[4,576,512]{2,1,0:T(8,128)(2,1)} %bitcast.97), channel_id=1, source_target_pairs={{4,8},{8,4},{5,9},{9,5},{6,10},{10,6},{7,11},{11,7},{20,24},{24,20... | collective-permute-start | bytes 7077896 | tf_op jit(solution)/shard_map/ppermute | solution.py:650
  964.0 53.9 %all-to-all-start.22 = ((bf16[4,256,512]{2,1,0:T(8,128)(2,1)}), bf16[4,256,512]{2,1,0:T(8,128)(2,1)}, u32[]{:S(2)}, u32[]{:S(2)}) async-start(bf16[4,256,512]{2,1,0:T(8,128)(2,1)} %bitcast.262), calls=%async_computation.22 | async-start | bytes 2097152 | tf_op jit(solution)/shard_map/all_to_all | solution.py:586
  1018.0 37.9 %all-to-all-start.24 = ((bf16[4,256,512]{2,1,0:T(8,128)(2,1)}), bf16[4,256,512]{2,1,0:T(8,128)(2,1)}, u32[]{:S(2)}, u32[]{:S(2)}) async-start(bf16[4,256,512]{2,1,0:T(8,128)(2,1)} %all-to-all-done.22), calls=%async_computation.24 | async-start | bytes 2097152 | tf_op jit(solution)/shard_map/all_to_all | solution.py:607
  1029.8 89.0 %collective-permute-start.65 = (bf16[4,576,512]{2,1,0:T(8,128)(2,1)}, bf16[4,576,512]{2,1,0:T(8,128)(2,1)S(1)}, u32[]{:S(2)}, u32[]{:S(2)}) collective-permute-start(bf16[4,576,512]{2,1,0:T(8,128)(2,1)} %bitcast.272), channel_id=1, source_target_pairs={{4,0},{8,12},{5,1},{9,13},{6,2},{10,14},{7,3},{11,15},{20,16},{24,... | collective-permute-start | bytes 7077896 | tf_op jit(solution)/shard_map/ppermute | solution.py:650
  1031.1 93.4 %collective-permute-start.64 = (bf16[4,576,512]{2,1,0:T(8,128)(2,1)}, bf16[4,576,512]{2,1,0:T(8,128)(2,1)}, u32[]{:S(2)}, u32[]{:S(2)}) collective-permute-start(bf16[4,576,512]{2,1,0:T(8,128)(2,1)} %all-to-all-done.23.refs_1_), channel_id=1, source_target_pairs={{0,16},{1,17},{2,18},{3,19},{4,20},{5,21},{6,22},{7,23},{8,24},{9,... | collective-permute-start | bytes 7077896 | tf_op jit(solution)/shard_map/ppermute | solution.py:1078
  1032.4 27.9 %collective-permute-start.60 = (f32[2,28099]{1,0:T(2,128)S(1)}, f32[2,28099]{1,0:T(2,128)S(1)}, u32[]{:S(2)}, u32[]{:S(2)}) collective-permute-start(f32[2,28099]{1,0:T(2,128)S(1)} %fusion.104), channel_id=1, source_target_pairs={{0,1},{1,0},{2,3},{3,2},{4,5},{5,4},{6,7},{7,6},{8,9},{9,8},{10,11... | collective-permute-start | bytes 674384 | tf_op jit(solution)/shard_map/ppermute | solution.py:621
  1055.9 68.7 %all-to-all-start.25 = ((bf16[4,512,512]{2,1,0:T(8,128)(2,1)}), bf16[4,512,512]{2,1,0:T(8,128)(2,1)}, u32[]{:S(2)}, u32[]{:S(2)}) async-start(bf16[4,512,512]{2,1,0:T(8,128)(2,1)} %bitcast.110), calls=%async_computation.25 | async-start | bytes 4194304 | tf_op jit(solution)/shard_map/all_to_all | solution.py:586
  1060.5 30.1 %collective-permute-start.61 = (f32[2,28099]{1,0:T(2,128)S(1)}, f32[2,28099]{1,0:T(2,128)S(1)}, u32[]{:S(2)}, u32[]{:S(2)}) collective-permute-start(f32[2,28099]{1,0:T(2,128)S(1)} %add.374), channel_id=1, source_target_pairs={{0,2},{1,3},{2,0},{3,1},{4,6},{5,7},{6,4},{7,5},{8,10},{9,11},{10,... | collective-permute-start | bytes 674384 | tf_op jit(solution)/shard_map/ppermute | solution.py:621
  1129.8 32.9 %collective-permute-start.67 = (bf16[4,576,512]{2,1,0:T(8,128)(2,1)S(1)}, bf16[4,576,512]{2,1,0:T(8,128)(2,1)}, u32[]{:S(2)}, u32[]{:S(2)}) collective-permute-start(bf16[4,576,512]{2,1,0:T(8,128)(2,1)S(1)} %bitcast.269), channel_id=1, source_target_pairs={{16,0},{17,1},{18,2},{19,3},{20,4},{21,5},{22,6},{23,7},{24,8},{25... | collective-permute-start | bytes 7077896 | tf_op jit(solution)/shard_map/ppermute | solution.py:1078
  (116 other events, 1664.6 us)

commit v10 on v9

--- a/solution.py
+++ b/solution.py
@@ -1056,16 +1056,19 @@
     dn0 = dot_cols(dmixed0, wo[0])
     d0 = unscan(pz0, px0, fwd0, dn0, rc0, 0)
     go = own_out_piece(normed0, dmixed0, away_out(normed0, dmixed0))
-    d0, go = sums.end((d0, go))
+    p1 = packed(dgin1, d1, out1, mixed1)
+    d0, go, p1 = sums.end((d0, go, p1))
     o0 = sums.add(go)
 
+    sums.finish([o1, z1])
     sums.begin()
     away = away_in(normed_in0, d0[0])
     full0, xs0 = with_group(d0[1], d0[2])
     gz = own_in_piece(normed_in0, d0[0], away)
     away = away_in(normed_in0, *xs0)
     gx = own_in_piece(normed_in0, xs0[0], away, xs0[1])
-    full0, gz, gx = sums.end((full0, gz, gx))
+    own_z1 = exchange(sums.values[z1])
+    full0, gz, gx, own_z1 = sums.end((full0, gz, gx, own_z1))
     z0 = sums.add(gz)
 
     sums.begin()
@@ -1077,31 +1080,28 @@
     def hand_over(v, layer):
         return lax.ppermute(v, "section", [(1 - layer, layer)])
 
-    sums.finish([o1, z1])
     sums.begin()
     dnin0 = scatter_sum(back0)
-    own_z1 = exchange(sums.values[z1])
     own_o1 = sums.values[o1]
     away_o1 = hand_over(own_o1, 1)
-    dnin0, own_z1, own_o1, away_o1 = sums.end((dnin0, own_z1, own_o1, away_o1))
+    away_z1 = hand_over(own_z1, 1)
+    dnin0, own_z1, away_z1, own_o1, away_o1 = sums.end(
+        (dnin0, own_z1, away_z1, own_o1, away_o1)
+    )
 
     sums.finish([x1, o0])
     sums.begin()
     own_x1 = exchange(sums.values[x1])
-    away_z1 = hand_over(own_z1, 1)
     own_o0 = sums.values[o0]
     away_o0 = hand_over(own_o0, 0)
     grad0, dgin0 = back_norm(dout0, dnin0, h0, small[0][0])
     back_g = exchange(quarters(jnp.concatenate([grad0.astype(BF16), grad1.astype(BF16)])))
-    p = jnp.stack([packed(dgin0, d0, out0, mixed0), packed(dgin1, d1, out1, mixed1)])
+    p = jnp.stack([packed(dgin0, d0, out0, mixed0), p1])
     p = p + swap_section(p)
-    p, back_g, own_x1, own_z1, away_z1, own_o0, away_o0 = sums.end(
-        (p, back_g, own_x1, own_z1, away_z1, own_o0, away_o0)
-    )
+    p, back_g, own_x1, own_o0, away_o0 = sums.end((p, back_g, own_x1, own_o0, away_o0))
 
     sums.finish([z0])
     sums.begin()
-    back_g = in_group(back_g)
     own_z0 = exchange(sums.values[z0])
     away_x1 = hand_over(own_x1, 1)
     m = 1
@@ -1112,12 +1112,14 @@
     while m < nz:
         p = p + move_seq(p, m)
         m *= 2
-    p, back_g, own_z0, own_x1, away_x1 = sums.end((p, back_g, own_z0, own_x1, away_x1))
+    away_z0 = hand_over(own_z0, 0)
+    p, back_g, own_z0, away_z0, own_x1, away_x1 = sums.end(
+        (p, back_g, own_z0, away_z0, own_x1, away_x1)
+    )
     sums.finish([x0])
-    away_z0 = hand_over(own_z0, 0)
     own_x0 = sums.values[x0]
     away_x0 = hand_over(own_x0, 0)
-    back_g = joined(exchange(back_g))
+    back_g = joined(exchange(in_group(back_g)))
     p = pick(p[0], p[1])
     back = jnp.concatenate([back_h, back_g])
 

time: 1200 us -> 1180 us (0.983)
    all_to_all x22, waiting for transfers between devices: 101 us -> 128 us  [exchange(): return lax.all_to_all(v, 'fsdp', 0, 0, tiled=True)]
    ppermute x18, waiting for transfers between devices: 158 us -> 137 us  [begin(): lax.ppermute(self.values[k], 'seq', self.pairs[step])]
    ppermute x2, waiting for transfers between devices: 28.4 us -> 10.9 us  [move_fsdp(): return lax.ppermute(v, 'fsdp', [(k, k ^ m) for k in range(n)])]
    unnamed x177 -> x167, local copies, waits for them, and re-layouts: 30.1 us -> 30.7 us
  transfers between devices with their start and end apart: 95 -> 95, of which waited for: 34 -> 36; matrix products, arithmetic and copies ran while one was open for 15% -> 15% of each run, Pallas kernels for 13% -> 15%
where the time goes in v10:
time: 1180 us; the launch traced here: 1170 us
  waiting for transfers between devices  353 us (30%)
  starting transfers between devices  320 us (27%)
  Pallas kernels  195 us (17%)
  local copies, waits for them, and re-layouts  90.2 us (8%)
  matrix products  81 us (7%)
  other arithmetic  73.7 us (6%)
  blocking collectives  48.5 us (4%)
    ppermute x18, waiting for transfers between devices, begin(): lax.ppermute(self.values[k], 'seq', self.pairs[step])  137 us
    all_to_all x22, waiting for transfers between devices, exchange(): return lax.all_to_all(v, 'fsdp', 0, 0, tiled=True)  128 us
    all_to_all x22, starting transfers between devices, exchange(): return lax.all_to_all(v, 'fsdp', 0, 0, tiled=True)  99.5 us
    ppermute x18, starting transfers between devices, begin(): lax.ppermute(self.values[k], 'seq', self.pairs[step])  66.7 us
    pallas_call x10, Pallas kernels, combine(): pl.pallas_call(functools.partial(combine_kernel, adds=tuple((add for _, _...  63.9 us
    dot_general x16, matrix products, dot_rows(): lax.dot_general(a, b, (((0,), (0,)), ((), ())), preferred_element_type=F32)  57 us
    all_to_all x1, blocking collectives, exchange(): return lax.all_to_all(v, 'fsdp', 0, 0, tiled=True)  48.5 us
    ppermute x12, starting transfers between devices, swap_section(): return lax.ppermute(v, 'section', [(0, 1), (1, 0)])  44.8 us
  transfers between devices with their start and end apart: 95, of which 36 were waited for; matrix products, arithmetic and copies ran while one was open for 15% of the time, Pallas kernels for 15%

profile of v10, /device:TPU:1, one launch (start us, length us, event | category | flops | bytes accessed | tf_op | source)
XLA Modules:
  0.0 1165.5 jit_solution(14851814764879561782)
XLA Ops:
  15.6 5.7 dynamic-slice_bitcast_fusion
  29.4 4.7 all-to-all-start.1
  34.2 5.2 collective-permute-start.3
  55.8 17.2 %all-to-all-done.2 = bf16[4,512,512]{2,1,0:T(8,128)(2,1)} async-done(((bf16[4,512,512]{2,1,0:T(8,128)(2,1)}), bf16[4,512,512]{2,1,0:T(8,128)(2,1)}, u32[]{:S(2)}, u32[]{:S(2)}) %all-to-all-start.2) | async-done | bytes 2097184 | tf_op jit(solution)/shard_map/all_to_all | solution.py:586
  82.1 8.8 project.4.proj
  90.9 26.5 %collective-permute-start.12 = (bf16[1024,2048]{1,0:T(8,128)(2,1)}, bf16[1024,2048]{1,0:T(8,128)(2,1)}, u32[]{:S(2)}, u32[]{:S(2)}) collective-permute-start(bf16[1024,2048]{1,0:T(8,128)(2,1)} %bitcast.36), channel_id=1, source_target_pairs={{0,16},{16,0},{1,17},{17,1},{2,18},{18,2},{3,19},{19,3},{4,20},{20... | collective-permute-start | bytes 12582920 | tf_op jit(solution)/shard_map/ppermute | solution.py:578
  121.5 10.6 scan_forward.2
  132.2 7.3 broadcast_select_fusion
  147.9 6.1 collective-permute-done.13.refs_4_.refs_8_
  161.3 6.8 project.5.pz
  175.6 11.4 all-to-all-done.3
  194.1 6.9 fusion.115
  201.0 48.5 %all_to_all.136 = f32[4,128,2048]{2,1,0:T(8,128)} all-to-all(f32[4,128,2048]{2,1,0:T(8,128)} %bitcast.291), channel_id=1, replica_groups=mesh['section'=2,'seq'=4,'fsdp'=4] {'fsdp'}, dimensions={0} | all-to-all | bytes 8388608 | tf_op jit(solution)/shard_map/all_to_all | solution.py:586
  270.3 11.0 all-to-all-start.7
  296.3 6.8 all-to-all-done.7
  303.1 7.9 project.6.proj
  314.2 13.1 %collective-permute-done.26.refs_3_ = bf16[1024,512]{1,0:T(8,128)(2,1)} collective-permute-done((bf16[1024,512]{1,0:T(8,128)(2,1)}, bf16[1024,512]{1,0:T(8,128)(2,1)}, u32[]{:S(2)}, u32[]{:S(2)}) %collective-permute-start.26) | collective-permute-done | bytes 1048608 | tf_op jit(solution)/shard_map/ppermute | solution.py:767
  340.1 10.6 scan_forward.3
  355.8 6.6 project.7.pz
  366.3 6.9 multiply_reduce_fusion.2
  390.6 4.9 add_convert_fusion.5.refs_0_
  408.1 20.4 %scan_backward.2 = (bf16[512,1024]{1,0:T(8,128)(2,1)S(1)}, bf16[512,1296]{1,0:T(8,128)(2,1)S(1)}, f32[4,512,64]{2,1,0:T(8,128)S(1)}, f32[8,1024]{1,0:T(8,128)S(1...) custom-call(f32[512,1024]{1,0:T(8,128)} %project.7.pz, ...), custom_call_target="tpu_custom_call" | custom-call | tf_op jit(solution)/shard_map/scan_backward/pallas_call | solution.py:303
  435.8 8.0 collective-permute-done.32.refs_1_
  443.8 6.2 combine.10.refs_0_
  480.4 11.0 project_back.2
  491.5 4.8 combine.11.refs_0_
  497.6 4.8 add_convert_fusion.4
  502.4 5.0 all-to-all-start.13
  508.7 17.3 %collective-permute-start.38 = (bf16[4,512,512]{2,1,0:T(8,128)(2,1)}, bf16[4,512,512]{2,1,0:T(8,128)(2,1)}, u32[]{:S(2)}, u32[]{:S(2)}) collective-permute-start(bf16[4,512,512]{2,1,0:T(8,128)(2,1)} %bitcast.311), channel_id=1, source_target_pairs={{0,4},{12,8},{1,5},{13,9},{2,6},{14,10},{3,7},{15,11},{16,20},{28,... | collective-permute-start | bytes 6291464 | tf_op jit(solution)/shard_map/ppermute | solution.py:650
  532.2 22.1 %all-to-all-done.13 = f32[4,128,2048]{2,1,0:T(8,128)} async-done(((f32[4,128,2048]{2,1,0:T(8,128)}), f32[4,128,2048]{2,1,0:T(8,128)}, u32[]{:S(2)}, u32[]{:S(2)}) %all-to-all-start.13) | async-done | bytes 4194336 | tf_op jit(solution)/shard_map/all_to_all | solution.py:586
  554.3 14.9 %all-to-all-start.14 = ((bf16[4,256,512]{2,1,0:T(8,128)(2,1)}), bf16[4,256,512]{2,1,0:T(8,128)(2,1)}, u32[]{:S(2)}, u32[]{:S(2)}) async-start(bf16[4,256,512]{2,1,0:T(8,128)(2,1)} %all-to-all-done.12), calls=%async_computation.14 | async-start | bytes 2097152 | tf_op jit(solution)/shard_map/all_to_all | solution.py:607
  577.7 5.8 combine.12
  583.5 5.0 add_convert_fusion.3
  612.9 11.1 all-to-all-done.17
  632.3 24.0 %collective-permute-done.40 = bf16[4,576,512]{2,1,0:T(8,128)(2,1)} collective-permute-done((bf16[4,576,512]{2,1,0:T(8,128)(2,1)}, bf16[4,576,512]{2,1,0:T(8,128)(2,1)}, u32[]{:S(2)}, u32[]{:S(2)}) %collective-permute-start.40) | collective-permute-done | bytes 2359328 | tf_op jit(solution)/shard_map/ppermute | solution.py:650
  656.4 7.3 combine.13
  674.4 6.5 fusion.116.dn
  680.9 20.3 %scan_backward.3 = (bf16[512,1024]{1,0:T(8,128)(2,1)S(1)}, bf16[512,1296]{1,0:T(8,128)(2,1)S(1)}, f32[4,512,64]{2,1,0:T(8,128)S(1)}, f32[8,1024]{1,0:T(8,128)S(1...) custom-call(f32[512,1024]{1,0:T(8,128)} %project.5.pz, ...), custom_call_target="tpu_custom_call" | custom-call | tf_op jit(solution)/shard_map/scan_backward/pallas_call | solution.py:303
  705.8 5.0 add_convert_fusion.2.refs_2_
  710.8 12.5 %collective-permute-done.42 = bf16[4,512,512]{2,1,0:T(8,128)(2,1)} collective-permute-done((bf16[4,512,512]{2,1,0:T(8,128)(2,1)}, bf16[4,512,512]{2,1,0:T(8,128)(2,1)}, u32[]{:S(2)}, u32[]{:S(2)}) %collective-permute-start.42) | collective-permute-done | bytes 2097184 | tf_op jit(solution)/shard_map/ppermute | solution.py:650
  723.3 7.2 combine.14
  746.2 9.3 collective-permute-start.48
  755.8 4.7 all-to-all-start.19
  776.3 22.3 %collective-permute-done.48.refs_3_ = bf16[512,2048]{1,0:T(8,128)(2,1)} collective-permute-done((bf16[512,2048]{1,0:T(8,128)(2,1)}, bf16[512,2048]{1,0:T(8,128)(2,1)}, u32[]{:S(2)}, u32[]{:S(2)}) %collective-permute-start.48) | collective-permute-done | bytes 2097184 | tf_op jit(solution)/shard_map/ppermute | solution.py:650
  798.7 6.6 combine.15
  808.7 6.6 collective-permute-start.50
  822.3 10.7 project_back.3
  833.0 24.2 %collective-permute-done.50 = bf16[4,512,512]{2,1,0:T(8,128)(2,1)} collective-permute-done((bf16[4,512,512]{2,1,0:T(8,128)(2,1)}, bf16[4,512,512]{2,1,0:T(8,128)(2,1)}, u32[]{:S(2)}, u32[]{:S(2)}) %collective-permute-start.50) | collective-permute-done | bytes 2097184 | tf_op jit(solution)/shard_map/ppermute | solution.py:650
  857.2 6.0 combine.16
  866.0 5.6 collective-permute-start.55
  882.9 23.6 %all-to-all-done.21 = bf16[4,128,2048]{2,1,0:T(8,128)(2,1)} async-done(((bf16[4,128,2048]{2,1,0:T(8,128)(2,1)}), bf16[4,128,2048]{2,1,0:T(8,128)(2,1)}, u32[]{:S(2)}, u32[]{:S(2)}) %all-to-all-start.21) | async-done | bytes 2097184 | tf_op jit(solution)/shard_map/all_to_all | solution.py:586
  918.1 8.7 combine.17
  953.4 41.3 %collective-permute-done.58 = bf16[4,512,512]{2,1,0:T(8,128)(2,1)} collective-permute-done((bf16[4,512,512]{2,1,0:T(8,128)(2,1)}, bf16[4,512,512]{2,1,0:T(8,128)(2,1)}, u32[]{:S(2)}, u32[]{:S(2)}) %collective-permute-start.58) | collective-permute-done | bytes 2097184 | tf_op jit(solution)/shard_map/ppermute | solution.py:650
  994.7 7.2 combine.18
  1010.4 22.2 %all-to-all-done.24.refs_0_ = bf16[4,512,512]{2,1,0:T(8,128)(2,1)} async-done(((bf16[4,512,512]{2,1,0:T(8,128)(2,1)}), bf16[4,512,512]{2,1,0:T(8,128)(2,1)}, u32[]{:S(2)}, u32[]{:S(2)}) %all-to-all-start.24) | async-done | bytes 2097184 | tf_op jit(solution)/shard_map/all_to_all | solution.py:586
  1036.8 5.1 collective-permute-done.60
  1043.3 5.8 collective-permute-done.61
  1049.2 11.0 collective-permute-start.62
  1062.8 12.7 %collective-permute-done.62 = f32[2,28099]{1,0:T(2,128)S(1)} collective-permute-done((f32[2,28099]{1,0:T(2,128)S(1)}, f32[2,28099]{1,0:T(2,128)S(1)}, u32[]{:S(2)}, u32[]{:S(2)}) %collective-permute-start.62) | collective-permute-done | bytes 224824 | tf_op jit(solution)/shard_map/ppermute | solution.py:626
  1080.0 8.2 collective-permute-done.63
  1101.5 20.8 %all-to-all-done.25 = bf16[4,256,512]{2,1,0:T(8,128)(2,1)} async-done(((bf16[4,256,512]{2,1,0:T(8,128)(2,1)}), bf16[4,256,512]{2,1,0:T(8,128)(2,1)}, u32[]{:S(2)}, u32[]{:S(2)}) %all-to-all-start.25) | async-done | bytes 1048608 | tf_op jit(solution)/shard_map/all_to_all | solution.py:607
  1133.7 5.4 all-to-all-done.26
  1145.8 8.4 place_in.2.refs_5_
  1154.1 8.8 place_in.3
  (543 shorter events, 423.7 us)
Async XLA Ops:
  23.3 20.1 %collective-permute-start = (bf16[1296,512]{1,0:T(8,128)(2,1)}, bf16[1296,512]{1,0:T(8,128)(2,1)}, u32[]{:S(2)}, u32[]{:S(2)}) collective-permute-start(bf16[1296,512]{1,0:T(8,128)(2,1)} %get-tuple-element.235), channel_id=1, source_target_pairs={{0,1},{1,0},{2,3},{3,2},{4,5},{5,4},{6,7},{7,6},{8,9},{9,8},{10,11... | collective-permute-start | bytes 3981320 | tf_op jit(solution)/shard_map/ppermute | solution.py:767
  34.2 21.5 %collective-permute-start.3 = (bf16[4,7024]{1,0:T(4,128)(2,1)S(1)}, bf16[4,7024]{1,0:T(4,128)(2,1)S(1)}, u32[]{:S(2)}, u32[]{:S(2)}) collective-permute-start(bf16[4,7024]{1,0:T(4,128)(2,1)S(1)} %slice.277), channel_id=1, source_target_pairs={{0,16},{16,0},{1,17},{17,1},{2,18},{18,2},{3,19},{19,3},{4,20},{20... | collective-permute-start | bytes 168584 | tf_op jit(solution)/shard_map/ppermute | solution.py:578
  43.5 36.1 %collective-permute-start.4 = (bf16[1296,512]{1,0:T(8,128)(2,1)S(1)}, bf16[1296,512]{1,0:T(8,128)(2,1)}, u32[]{:S(2)}, u32[]{:S(2)}) collective-permute-start(bf16[1296,512]{1,0:T(8,128)(2,1)S(1)} %get-tuple-element.247.refs_0_.refs_4_), channel_id=1, source_target_pairs={{0,16},{1,17},{2,18},{3,19},{4,20},{5,21},{6,22},{7,23},{8,24},{9,... | collective-permute-start | bytes 3981320 | tf_op jit(solution)/shard_map/ppermute | solution.py:796
  44.8 34.8 %collective-permute-start.5 = (bf16[1296,512]{1,0:T(8,128)(2,1)}, bf16[1296,512]{1,0:T(8,128)(2,1)}, u32[]{:S(2)}, u32[]{:S(2)}) collective-permute-start(bf16[1296,512]{1,0:T(8,128)(2,1)} %collective-permute-done.refs_1_.refs_5_), channel_id=1, source_target_pairs={{0,16},{1,17},{2,18},{3,19},{4,20},{5,21},{6,22},{7,23},{8,24},{9,... | collective-permute-start | bytes 3981320 | tf_op jit(solution)/shard_map/ppermute | solution.py:796
  46.1 33.6 %collective-permute-start.6 = (bf16[1296,512]{1,0:T(8,128)(2,1)}, bf16[1296,512]{1,0:T(8,128)(2,1)}, u32[]{:S(2)}, u32[]{:S(2)}) collective-permute-start(bf16[1296,512]{1,0:T(8,128)(2,1)} %collective-permute-done.1.refs_2_.refs_6_), channel_id=1, source_target_pairs={{0,16},{1,17},{2,18},{3,19},{4,20},{5,21},{6,22},{7,23},{8,24},{9,... | collective-permute-start | bytes 3981320 | tf_op jit(solution)/shard_map/ppermute | solution.py:796
  47.4 34.8 %collective-permute-start.7 = (bf16[1296,512]{1,0:T(8,128)(2,1)}, bf16[1296,512]{1,0:T(8,128)(2,1)}, u32[]{:S(2)}, u32[]{:S(2)}) collective-permute-start(bf16[1296,512]{1,0:T(8,128)(2,1)} %collective-permute-done.2.refs_3_.refs_7_), channel_id=1, source_target_pairs={{0,16},{1,17},{2,18},{3,19},{4,20},{5,21},{6,22},{7,23},{8,24},{9,... | collective-permute-start | bytes 3981320 | tf_op jit(solution)/shard_map/ppermute | solution.py:796
  51.2 21.8 %all-to-all-start.2 = ((bf16[4,512,512]{2,1,0:T(8,128)(2,1)}), bf16[4,512,512]{2,1,0:T(8,128)(2,1)}, u32[]{:S(2)}, u32[]{:S(2)}) async-start(bf16[4,512,512]{2,1,0:T(8,128)(2,1)} %broadcast_in_dim.54), calls=%async_computation.2 | async-start | bytes 4194304 | tf_op jit(solution)/shard_map/all_to_all | solution.py:586
  90.9 41.3 %collective-permute-start.12 = (bf16[1024,2048]{1,0:T(8,128)(2,1)}, bf16[1024,2048]{1,0:T(8,128)(2,1)}, u32[]{:S(2)}, u32[]{:S(2)}) collective-permute-start(bf16[1024,2048]{1,0:T(8,128)(2,1)} %bitcast.36), channel_id=1, source_target_pairs={{0,16},{16,0},{1,17},{17,1},{2,18},{18,2},{3,19},{19,3},{4,20},{20... | collective-permute-start | bytes 12582920 | tf_op jit(solution)/shard_map/ppermute | solution.py:578
  119.0 20.6 %collective-permute-start.9 = (bf16[1024,512]{1,0:T(8,128)(2,1)}, bf16[1024,512]{1,0:T(8,128)(2,1)S(1)}, u32[]{:S(2)}, u32[]{:S(2)}) collective-permute-start(bf16[1024,512]{1,0:T(8,128)(2,1)} %get-tuple-element.257), channel_id=1, source_target_pairs={{0,1},{1,0},{2,3},{3,2},{4,5},{5,4},{6,7},{7,6},{8,9},{9,8},{10,11... | collective-permute-start | bytes 3145736 | tf_op jit(solution)/shard_map/ppermute | solution.py:767
  119.7 19.8 %collective-permute-start.10 = (bf16[1024,512]{1,0:T(8,128)(2,1)}, bf16[1024,512]{1,0:T(8,128)(2,1)S(1)}, u32[]{:S(2)}, u32[]{:S(2)}) collective-permute-start(bf16[1024,512]{1,0:T(8,128)(2,1)} %get-tuple-element.258), channel_id=1, source_target_pairs={{0,2},{1,3},{2,0},{3,1},{4,6},{5,7},{6,4},{7,5},{8,10},{9,11},{10,... | collective-permute-start | bytes 3145736 | tf_op jit(solution)/shard_map/ppermute | solution.py:767
  120.5 19.1 %collective-permute-start.11 = (bf16[1024,512]{1,0:T(8,128)(2,1)}, bf16[1024,512]{1,0:T(8,128)(2,1)S(1)}, u32[]{:S(2)}, u32[]{:S(2)}) collective-permute-start(bf16[1024,512]{1,0:T(8,128)(2,1)} %get-tuple-element.259), channel_id=1, source_target_pairs={{0,3},{1,2},{2,1},{3,0},{4,7},{5,6},{6,5},{7,4},{8,11},{9,10},{10,... | collective-permute-start | bytes 3145736 | tf_op jit(solution)/shard_map/ppermute | solution.py:767
  144.8 45.1 %collective-permute-start.17 = (bf16[1296,512]{1,0:T(8,128)(2,1)}, bf16[1296,512]{1,0:T(8,128)(2,1)}, u32[]{:S(2)}, u32[]{:S(2)}) collective-permute-start(bf16[1296,512]{1,0:T(8,128)(2,1)} %get-tuple-element.235), channel_id=1, source_target_pairs={{16,17},{17,16},{18,19},{19,18},{20,21},{21,20},{22,23},{23,22},{2... | collective-permute-start | bytes 3981320 | tf_op jit(solution)/shard_map/ppermute | solution.py:767
  153.9 36.0 %collective-permute-start.18 = (bf16[1296,512]{1,0:T(8,128)(2,1)}, bf16[1296,512]{1,0:T(8,128)(2,1)}, u32[]{:S(2)}, u32[]{:S(2)}) collective-permute-start(bf16[1296,512]{1,0:T(8,128)(2,1)} %get-tuple-element.236), channel_id=1, source_target_pairs={{16,18},{17,19},{18,16},{19,17},{20,22},{21,23},{22,20},{23,21},{2... | collective-permute-start | bytes 3981320 | tf_op jit(solution)/shard_map/ppermute | solution.py:767
  155.9 34.0 %collective-permute-start.19 = (bf16[1296,512]{1,0:T(8,128)(2,1)}, bf16[1296,512]{1,0:T(8,128)(2,1)}, u32[]{:S(2)}, u32[]{:S(2)}) collective-permute-start(bf16[1296,512]{1,0:T(8,128)(2,1)} %get-tuple-element.237), channel_id=1, source_target_pairs={{16,19},{17,18},{18,17},{19,16},{20,23},{21,22},{22,21},{23,20},{2... | collective-permute-start | bytes 3981320 | tf_op jit(solution)/shard_map/ppermute | solution.py:767
  257.2 32.3 %collective-permute-start.20 = (bf16[1296,512]{1,0:T(8,128)(2,1)S(1)}, bf16[1296,512]{1,0:T(8,128)(2,1)}, u32[]{:S(2)}, u32[]{:S(2)}) collective-permute-start(bf16[1296,512]{1,0:T(8,128)(2,1)S(1)} %get-tuple-element.247.refs_0_.refs_4_), channel_id=1, source_target_pairs={{16,0},{17,1},{18,2},{19,3},{20,4},{21,5},{22,6},{23,7},{24,8},{25... | collective-permute-start | bytes 3981320 | tf_op jit(solution)/shard_map/ppermute | solution.py:906
  259.6 33.6 %collective-permute-start.21 = (bf16[1296,512]{1,0:T(8,128)(2,1)}, bf16[1296,512]{1,0:T(8,128)(2,1)}, u32[]{:S(2)}, u32[]{:S(2)}) collective-permute-start(bf16[1296,512]{1,0:T(8,128)(2,1)} %collective-permute-done.17.refs_1_.refs_5_), channel_id=1, source_target_pairs={{16,0},{17,1},{18,2},{19,3},{20,4},{21,5},{22,6},{23,7},{24,8},{25... | collective-permute-start | bytes 3981320 | tf_op jit(solution)/shard_map/ppermute | solution.py:906
  270.3 32.8 %all-to-all-start.7 = ((bf16[4,128,2048]{2,1,0:T(8,128)(2,1)}), bf16[4,128,2048]{2,1,0:T(8,128)(2,1)}, u32[]{:S(2)}, u32[]{:S(2)}) async-start(bf16[4,128,2048]{2,1,0:T(8,128)(2,1)} %broadcast_in_dim.59), calls=%async_computation.7 | async-start | bytes 4194304 | tf_op jit(solution)/shard_map/all_to_all | solution.py:586
  286.1 27.2 %collective-permute-start.24 = (bf16[1024,512]{1,0:T(8,128)(2,1)}, bf16[1024,512]{1,0:T(8,128)(2,1)}, u32[]{:S(2)}, u32[]{:S(2)}) collective-permute-start(bf16[1024,512]{1,0:T(8,128)(2,1)} %get-tuple-element.257), channel_id=1, source_target_pairs={{16,17},{17,16},{18,19},{19,18},{20,21},{21,20},{22,23},{23,22},{2... | collective-permute-start | bytes 3145736 | tf_op jit(solution)/shard_map/ppermute | solution.py:767
  289.5 24.7 %collective-permute-start.25 = (bf16[1024,512]{1,0:T(8,128)(2,1)}, bf16[1024,512]{1,0:T(8,128)(2,1)}, u32[]{:S(2)}, u32[]{:S(2)}) collective-permute-start(bf16[1024,512]{1,0:T(8,128)(2,1)} %get-tuple-element.258), channel_id=1, source_target_pairs={{16,18},{17,19},{18,16},{19,17},{20,22},{21,23},{22,20},{23,21},{2... | collective-permute-start | bytes 3145736 | tf_op jit(solution)/shard_map/ppermute | solution.py:767
  293.2 34.1 %collective-permute-start.26 = (bf16[1024,512]{1,0:T(8,128)(2,1)}, bf16[1024,512]{1,0:T(8,128)(2,1)}, u32[]{:S(2)}, u32[]{:S(2)}) collective-permute-start(bf16[1024,512]{1,0:T(8,128)(2,1)} %get-tuple-element.259), channel_id=1, source_target_pairs={{16,19},{17,18},{18,17},{19,16},{20,23},{21,22},{22,21},{23,20},{2... | collective-permute-start | bytes 3145736 | tf_op jit(solution)/shard_map/ppermute | solution.py:767
  330.0 33.4 %all-to-all-start.8 = ((bf16[4,512,512]{2,1,0:T(8,128)(2,1)}), bf16[4,512,512]{2,1,0:T(8,128)(2,1)}, u32[]{:S(2)}, u32[]{:S(2)}) async-start(bf16[4,512,512]{2,1,0:T(8,128)(2,1)} %broadcast_in_dim.61), calls=%async_computation.8 | async-start | bytes 4194304 | tf_op jit(solution)/shard_map/all_to_all | solution.py:586
  395.5 48.3 %collective-permute-start.32 = (bf16[512,2048]{1,0:T(8,128)(2,1)}, bf16[512,2048]{1,0:T(8,128)(2,1)}, u32[]{:S(2)}, u32[]{:S(2)}) collective-permute-start(bf16[512,2048]{1,0:T(8,128)(2,1)} %add_convert_fusion.5.refs_0_), channel_id=1, source_target_pairs={{0,4},{12,8},{1,5},{13,9},{2,6},{14,10},{3,7},{15,11},{16,20},{28,... | collective-permute-start | bytes 6291464 | tf_op jit(solution)/shard_map/ppermute | solution.py:650
  403.7 29.1 %all-to-all-start.10 = ((bf16[4,128,2048]{2,1,0:T(8,128)(2,1)}), bf16[4,128,2048]{2,1,0:T(8,128)(2,1)}, u32[]{:S(2)}, u32[]{:S(2)}) async-start(bf16[4,128,2048]{2,1,0:T(8,128)(2,1)} %bitcast.305), calls=%async_computation.10 | async-start | bytes 4194304 | tf_op jit(solution)/shard_map/all_to_all | solution.py:586
  450.0 41.5 %collective-permute-start.34 = (bf16[512,2048]{1,0:T(8,128)(2,1)}, bf16[512,2048]{1,0:T(8,128)(2,1)}, u32[]{:S(2)}, u32[]{:S(2)}) collective-permute-start(bf16[512,2048]{1,0:T(8,128)(2,1)} %combine.10.refs_0_), channel_id=1, source_target_pairs={{4,8},{8,4},{5,9},{9,5},{6,10},{10,6},{7,11},{11,7},{20,24},{24,20... | collective-permute-start | bytes 6291464 | tf_op jit(solution)/shard_map/ppermute | solution.py:650
  456.3 41.3 %collective-permute-start.33 = (bf16[2048,512]{1,0:T(8,128)(2,1)}, bf16[2048,512]{1,0:T(8,128)(2,1)}, u32[]{:S(2)}, u32[]{:S(2)}) collective-permute-start(bf16[2048,512]{1,0:T(8,128)(2,1)} %convolution_convert_fusion.5), channel_id=1, source_target_pairs={{0,16},{16,0},{1,17},{17,1},{2,18},{18,2},{3,19},{19,3},{4,20},{20... | collective-permute-start | bytes 6291464 | tf_op jit(solution)/shard_map/ppermute | solution.py:578
  472.0 30.5 %all-to-all-start.12 = ((bf16[4,256,512]{2,1,0:T(8,128)(2,1)}), bf16[4,256,512]{2,1,0:T(8,128)(2,1)}, u32[]{:S(2)}, u32[]{:S(2)}) async-start(bf16[4,256,512]{2,1,0:T(8,128)(2,1)} %bitcast.292), calls=%async_computation.12 | async-start | bytes 2097152 | tf_op jit(solution)/shard_map/all_to_all | solution.py:586
  502.4 51.9 %all-to-all-start.13 = ((f32[4,128,2048]{2,1,0:T(8,128)}), f32[4,128,2048]{2,1,0:T(8,128)}, u32[]{:S(2)}, u32[]{:S(2)}) async-start(f32[4,128,2048]{2,1,0:T(8,128)} %bitcast.283), calls=%async_computation.13 | async-start | bytes 8388608 | tf_op jit(solution)/shard_map/all_to_all | solution.py:586
  507.4 70.2 %collective-permute-start.37 = (bf16[512,2048]{1,0:T(8,128)(2,1)}, bf16[512,2048]{1,0:T(8,128)(2,1)}, u32[]{:S(2)}, u32[]{:S(2)}) collective-permute-start(bf16[512,2048]{1,0:T(8,128)(2,1)} %copy-done.3), channel_id=1, source_target_pairs={{4,0},{8,12},{5,1},{9,13},{6,2},{10,14},{7,3},{11,15},{20,16},{24,... | collective-permute-start | bytes 6291464 | tf_op jit(solution)/shard_map/ppermute | solution.py:650
  508.7 68.9 %collective-permute-start.38 = (bf16[4,512,512]{2,1,0:T(8,128)(2,1)}, bf16[4,512,512]{2,1,0:T(8,128)(2,1)}, u32[]{:S(2)}, u32[]{:S(2)}) collective-permute-start(bf16[4,512,512]{2,1,0:T(8,128)(2,1)} %bitcast.311), channel_id=1, source_target_pairs={{0,4},{12,8},{1,5},{13,9},{2,6},{14,10},{3,7},{15,11},{16,20},{28,... | collective-permute-start | bytes 6291464 | tf_op jit(solution)/shard_map/ppermute | solution.py:650
  530.3 53.2 %collective-permute-start.35 = (bf16[2048,512]{1,0:T(8,128)(2,1)}, bf16[2048,512]{1,0:T(8,128)(2,1)}, u32[]{:S(2)}, u32[]{:S(2)}) collective-permute-start(bf16[2048,512]{1,0:T(8,128)(2,1)} %convolution_convert_fusion.4), channel_id=1, source_target_pairs={{0,16},{16,0},{1,17},{17,1},{2,18},{18,2},{3,19},{19,3},{4,20},{20... | collective-permute-start | bytes 6291464 | tf_op jit(solution)/shard_map/ppermute | solution.py:578
  554.3 41.4 %all-to-all-start.14 = ((bf16[4,256,512]{2,1,0:T(8,128)(2,1)}), bf16[4,256,512]{2,1,0:T(8,128)(2,1)}, u32[]{:S(2)}, u32[]{:S(2)}) async-start(bf16[4,256,512]{2,1,0:T(8,128)(2,1)} %all-to-all-done.12), calls=%async_computation.14 | async-start | bytes 2097152 | tf_op jit(solution)/shard_map/all_to_all | solution.py:607
  604.0 52.3 %collective-permute-start.40 = (bf16[4,576,512]{2,1,0:T(8,128)(2,1)}, bf16[4,576,512]{2,1,0:T(8,128)(2,1)}, u32[]{:S(2)}, u32[]{:S(2)}) collective-permute-start(bf16[4,576,512]{2,1,0:T(8,128)(2,1)} %pad_maximum_fusion.4), channel_id=1, source_target_pairs={{0,4},{12,8},{1,5},{13,9},{2,6},{14,10},{3,7},{15,11},{16,20},{28,... | collective-permute-start | bytes 7077896 | tf_op jit(solution)/shard_map/ppermute | solution.py:650
  610.9 21.4 %collective-permute-start.39 = (bf16[4,512,512]{2,1,0:T(8,128)(2,1)}, bf16[4,512,512]{2,1,0:T(8,128)(2,1)}, u32[]{:S(2)}, u32[]{:S(2)}) collective-permute-start(bf16[4,512,512]{2,1,0:T(8,128)(2,1)} %bitcast.273), channel_id=1, source_target_pairs={{4,8},{8,4},{5,9},{9,5},{6,10},{10,6},{7,11},{11,7},{20,24},{24,20... | collective-permute-start | bytes 6291464 | tf_op jit(solution)/shard_map/ppermute | solution.py:650
  626.6 37.1 %all-to-all-start.15 = ((bf16[4,128,2048]{2,1,0:T(8,128)(2,1)}), bf16[4,128,2048]{2,1,0:T(8,128)(2,1)}, u32[]{:S(2)}, u32[]{:S(2)}) async-start(bf16[4,128,2048]{2,1,0:T(8,128)(2,1)} %broadcast_in_dim.65), calls=%async_computation.15 | async-start | bytes 4194304 | tf_op jit(solution)/shard_map/all_to_all | solution.py:586
  668.1 37.7 %collective-permute-start.41 = (bf16[512,2048]{1,0:T(8,128)(2,1)}, bf16[512,2048]{1,0:T(8,128)(2,1)}, u32[]{:S(2)}, u32[]{:S(2)}) collective-permute-start(bf16[512,2048]{1,0:T(8,128)(2,1)} %convolution_convert_fusion.3), channel_id=1, source_target_pairs={{0,16},{16,0},{1,17},{17,1},{2,18},{18,2},{3,19},{19,3},{4,20},{20... | collective-permute-start | bytes 6291464 | tf_op jit(solution)/shard_map/ppermute | solution.py:578
  669.4 53.9 %collective-permute-start.43 = (bf16[4,576,512]{2,1,0:T(8,128)(2,1)}, bf16[4,576,512]{2,1,0:T(8,128)(2,1)}, u32[]{:S(2)}, u32[]{:S(2)}) collective-permute-start(bf16[4,576,512]{2,1,0:T(8,128)(2,1)} %bitcast.75), channel_id=1, source_target_pairs={{4,8},{8,4},{5,9},{9,5},{6,10},{10,6},{7,11},{11,7},{20,24},{24,20... | collective-permute-start | bytes 7077896 | tf_op jit(solution)/shard_map/ppermute | solution.py:650
  671.5 51.8 %collective-permute-start.42 = (bf16[4,512,512]{2,1,0:T(8,128)(2,1)}, bf16[4,512,512]{2,1,0:T(8,128)(2,1)}, u32[]{:S(2)}, u32[]{:S(2)}) collective-permute-start(bf16[4,512,512]{2,1,0:T(8,128)(2,1)} %bitcast.74), channel_id=1, source_target_pairs={{4,0},{8,12},{5,1},{9,13},{6,2},{10,14},{7,3},{11,15},{20,16},{24,... | collective-permute-start | bytes 6291464 | tf_op jit(solution)/shard_map/ppermute | solution.py:650
  735.6 31.8 %collective-permute-start.45 = (bf16[2048,512]{1,0:T(8,128)(2,1)}, bf16[2048,512]{1,0:T(8,128)(2,1)}, u32[]{:S(2)}, u32[]{:S(2)}) collective-permute-start(bf16[2048,512]{1,0:T(8,128)(2,1)} %convolution_convert_fusion.1), channel_id=1, source_target_pairs={{0,16},{16,0},{1,17},{17,1},{2,18},{18,2},{3,19},{19,3},{4,20},{20... | collective-permute-start | bytes 6291464 | tf_op jit(solution)/shard_map/ppermute | solution.py:578
  739.0 32.9 %collective-permute-start.44 = (bf16[2048,512]{1,0:T(8,128)(2,1)}, bf16[2048,512]{1,0:T(8,128)(2,1)}, u32[]{:S(2)}, u32[]{:S(2)}) collective-permute-start(bf16[2048,512]{1,0:T(8,128)(2,1)} %convolution_convert_fusion.2), channel_id=1, source_target_pairs={{0,16},{16,0},{1,17},{17,1},{2,18},{18,2},{3,19},{19,3},{4,20},{20... | collective-permute-start | bytes 6291464 | tf_op jit(solution)/shard_map/ppermute | solution.py:578
  739.0 59.7 %collective-permute-start.47 = (bf16[4,576,512]{2,1,0:T(8,128)(2,1)}, bf16[4,576,512]{2,1,0:T(8,128)(2,1)}, u32[]{:S(2)}, u32[]{:S(2)}) collective-permute-start(bf16[4,576,512]{2,1,0:T(8,128)(2,1)} %bitcast.85), channel_id=1, source_target_pairs={{4,0},{8,12},{5,1},{9,13},{6,2},{10,14},{7,3},{11,15},{20,16},{24,... | collective-permute-start | bytes 7077896 | tf_op jit(solution)/shard_map/ppermute | solution.py:650
  746.2 52.4 %collective-permute-start.48 = (bf16[512,2048]{1,0:T(8,128)(2,1)}, bf16[512,2048]{1,0:T(8,128)(2,1)}, u32[]{:S(2)}, u32[]{:S(2)}) collective-permute-start(bf16[512,2048]{1,0:T(8,128)(2,1)} %add_convert_fusion.2.refs_2_), channel_id=1, source_target_pairs={{0,4},{12,8},{1,5},{13,9},{2,6},{14,10},{3,7},{15,11},{16,20},{28,... | collective-permute-start | bytes 6291464 | tf_op jit(solution)/shard_map/ppermute | solution.py:650
  755.8 50.8 %all-to-all-start.19 = ((bf16[4,512,512]{2,1,0:T(8,128)(2,1)}), bf16[4,512,512]{2,1,0:T(8,128)(2,1)}, u32[]{:S(2)}, u32[]{:S(2)}) async-start(bf16[4,512,512]{2,1,0:T(8,128)(2,1)} %bitcast.275), calls=%async_computation.19 | async-start | bytes 4194304 | tf_op jit(solution)/shard_map/all_to_all | solution.py:586
  806.6 26.4 %collective-permute-start.49 = (bf16[512,2048]{1,0:T(8,128)(2,1)}, bf16[512,2048]{1,0:T(8,128)(2,1)}, u32[]{:S(2)}, u32[]{:S(2)}) collective-permute-start(bf16[512,2048]{1,0:T(8,128)(2,1)} %copy-done.30), channel_id=1, source_target_pairs={{4,8},{8,4},{5,9},{9,5},{6,10},{10,6},{7,11},{11,7},{20,24},{24,20... | collective-permute-start | bytes 6291464 | tf_op jit(solution)/shard_map/ppermute | solution.py:650
  808.7 48.5 %collective-permute-start.50 = (bf16[4,512,512]{2,1,0:T(8,128)(2,1)}, bf16[4,512,512]{2,1,0:T(8,128)(2,1)}, u32[]{:S(2)}, u32[]{:S(2)}) collective-permute-start(bf16[4,512,512]{2,1,0:T(8,128)(2,1)} %bitcast.312), channel_id=1, source_target_pairs={{0,4},{12,8},{1,5},{13,9},{2,6},{14,10},{3,7},{15,11},{16,20},{28,... | collective-permute-start | bytes 6291464 | tf_op jit(solution)/shard_map/ppermute | solution.py:650
  815.3 50.7 %all-to-all-start.20 = ((bf16[4,576,512]{2,1,0:T(8,128)(2,1)}), bf16[4,576,512]{2,1,0:T(8,128)(2,1)}, u32[]{:S(2)}, u32[]{:S(2)}) async-start(bf16[4,576,512]{2,1,0:T(8,128)(2,1)} %pad_maximum_fusion.5), calls=%async_computation.20 | async-start | bytes 4718592 | tf_op jit(solution)/shard_map/all_to_all | solution.py:586
  866.0 52.1 %collective-permute-start.55 = (bf16[4,576,512]{2,1,0:T(8,128)(2,1)}, bf16[4,576,512]{2,1,0:T(8,128)(2,1)}, u32[]{:S(2)}, u32[]{:S(2)}) collective-permute-start(bf16[4,576,512]{2,1,0:T(8,128)(2,1)} %all-to-all-done.20), channel_id=1, source_target_pairs={{0,4},{12,8},{1,5},{13,9},{2,6},{14,10},{3,7},{15,11},{16,20},{28,... | collective-permute-start | bytes 7077896 | tf_op jit(solution)/shard_map/ppermute | solution.py:650
  871.6 46.2 %collective-permute-start.53 = (bf16[512,2048]{1,0:T(8,128)(2,1)}, bf16[512,2048]{1,0:T(8,128)(2,1)}, u32[]{:S(2)}, u32[]{:S(2)}) collective-permute-start(bf16[512,2048]{1,0:T(8,128)(2,1)} %copy-done.26), channel_id=1, source_target_pairs={{4,0},{8,12},{5,1},{9,13},{6,2},{10,14},{7,3},{11,15},{20,16},{24,... | collective-permute-start | bytes 6291464 | tf_op jit(solution)/shard_map/ppermute | solution.py:650
  872.8 44.9 %collective-permute-start.54 = (bf16[4,512,512]{2,1,0:T(8,128)(2,1)}, bf16[4,512,512]{2,1,0:T(8,128)(2,1)}, u32[]{:S(2)}, u32[]{:S(2)}) collective-permute-start(bf16[4,512,512]{2,1,0:T(8,128)(2,1)} %bitcast.274), channel_id=1, source_target_pairs={{4,8},{8,4},{5,9},{9,5},{6,10},{10,6},{7,11},{11,7},{20,24},{24,20... | collective-permute-start | bytes 6291464 | tf_op jit(solution)/shard_map/ppermute | solution.py:650
  874.8 53.2 %collective-permute-start.52 = (bf16[512,2048]{1,0:T(8,128)(2,1)S(1)}, bf16[512,2048]{1,0:T(8,128)(2,1)}, u32[]{:S(2)}, u32[]{:S(2)}) collective-permute-start(bf16[512,2048]{1,0:T(8,128)(2,1)S(1)} %copy-done.20), channel_id=1, source_target_pairs={{0,16},{1,17},{2,18},{3,19},{4,20},{5,21},{6,22},{7,23},{8,24},{9,... | collective-permute-start | bytes 6291464 | tf_op jit(solution)/shard_map/ppermute | solution.py:1081
  876.1 51.9 %collective-permute-start.51 = (bf16[4,512,512]{2,1,0:T(8,128)(2,1)}, bf16[4,512,512]{2,1,0:T(8,128)(2,1)}, u32[]{:S(2)}, u32[]{:S(2)}) collective-permute-start(bf16[4,512,512]{2,1,0:T(8,128)(2,1)} %all-to-all-done.19.refs_1_), channel_id=1, source_target_pairs={{0,16},{1,17},{2,18},{3,19},{4,20},{5,21},{6,22},{7,23},{8,24},{9,... | collective-permute-start | bytes 6291464 | tf_op jit(solution)/shard_map/ppermute | solution.py:1081
  877.5 29.0 %all-to-all-start.21 = ((bf16[4,128,2048]{2,1,0:T(8,128)(2,1)}), bf16[4,128,2048]{2,1,0:T(8,128)(2,1)}, u32[]{:S(2)}, u32[]{:S(2)}) async-start(bf16[4,128,2048]{2,1,0:T(8,128)(2,1)} %bitcast.290), calls=%async_computation.21 | async-start | bytes 4194304 | tf_op jit(solution)/shard_map/all_to_all | solution.py:586
  906.4 41.3 %all-to-all-start.23 = ((bf16[4,576,512]{2,1,0:T(8,128)(2,1)}), bf16[4,576,512]{2,1,0:T(8,128)(2,1)}, u32[]{:S(2)}, u32[]{:S(2)}) async-start(bf16[4,576,512]{2,1,0:T(8,128)(2,1)} %bitcast.303), calls=%async_computation.23 | async-start | bytes 4718592 | tf_op jit(solution)/shard_map/all_to_all | solution.py:586
  941.1 62.1 %collective-permute-start.57 = (bf16[512,2048]{1,0:T(8,128)(2,1)S(1)}, bf16[512,2048]{1,0:T(8,128)(2,1)}, u32[]{:S(2)}, u32[]{:S(2)}) collective-permute-start(bf16[512,2048]{1,0:T(8,128)(2,1)S(1)} %copy-done.22), channel_id=1, source_target_pairs={{16,0},{17,1},{18,2},{19,3},{20,4},{21,5},{22,6},{23,7},{24,8},{25... | collective-permute-start | bytes 6291464 | tf_op jit(solution)/shard_map/ppermute | solution.py:1081
  944.3 50.4 %collective-permute-start.58 = (bf16[4,512,512]{2,1,0:T(8,128)(2,1)}, bf16[4,512,512]{2,1,0:T(8,128)(2,1)}, u32[]{:S(2)}, u32[]{:S(2)}) collective-permute-start(bf16[4,512,512]{2,1,0:T(8,128)(2,1)} %bitcast.100), channel_id=1, source_target_pairs={{4,0},{8,12},{5,1},{9,13},{6,2},{10,14},{7,3},{11,15},{20,16},{24,... | collective-permute-start | bytes 6291464 | tf_op jit(solution)/shard_map/ppermute | solution.py:650
  945.6 49.1 %collective-permute-start.59 = (bf16[4,576,512]{2,1,0:T(8,128)(2,1)}, bf16[4,576,512]{2,1,0:T(8,128)(2,1)}, u32[]{:S(2)}, u32[]{:S(2)}) collective-permute-start(bf16[4,576,512]{2,1,0:T(8,128)(2,1)} %bitcast.101), channel_id=1, source_target_pairs={{4,8},{8,4},{5,9},{9,5},{6,10},{10,6},{7,11},{11,7},{20,24},{24,20... | collective-permute-start | bytes 7077896 | tf_op jit(solution)/shard_map/ppermute | solution.py:650
  947.7 55.5 %all-to-all-start.22 = ((bf16[4,256,512]{2,1,0:T(8,128)(2,1)}), bf16[4,256,512]{2,1,0:T(8,128)(2,1)}, u32[]{:S(2)}, u32[]{:S(2)}) async-start(bf16[4,256,512]{2,1,0:T(8,128)(2,1)} %bitcast.262), calls=%async_computation.22 | async-start | bytes 2097152 | tf_op jit(solution)/shard_map/all_to_all | solution.py:586
  1003.2 29.4 %all-to-all-start.24 = ((bf16[4,512,512]{2,1,0:T(8,128)(2,1)}), bf16[4,512,512]{2,1,0:T(8,128)(2,1)}, u32[]{:S(2)}, u32[]{:S(2)}) async-start(bf16[4,512,512]{2,1,0:T(8,128)(2,1)} %bitcast.276), calls=%async_computation.24 | async-start | bytes 4194304 | tf_op jit(solution)/shard_map/all_to_all | solution.py:586
  1007.8 80.5 %collective-permute-start.66 = (bf16[4,576,512]{2,1,0:T(8,128)(2,1)S(1)}, bf16[4,576,512]{2,1,0:T(8,128)(2,1)}, u32[]{:S(2)}, u32[]{:S(2)}) collective-permute-start(bf16[4,576,512]{2,1,0:T(8,128)(2,1)S(1)} %bitcast.272), channel_id=1, source_target_pairs={{4,0},{8,12},{5,1},{9,13},{6,2},{10,14},{7,3},{11,15},{20,16},{24,... | collective-permute-start | bytes 7077896 | tf_op jit(solution)/shard_map/ppermute | solution.py:650
  1009.1 83.4 %collective-permute-start.65 = (bf16[4,576,512]{2,1,0:T(8,128)(2,1)}, bf16[4,576,512]{2,1,0:T(8,128)(2,1)}, u32[]{:S(2)}, u32[]{:S(2)}) collective-permute-start(bf16[4,576,512]{2,1,0:T(8,128)(2,1)} %all-to-all-done.23.refs_1_), channel_id=1, source_target_pairs={{0,16},{1,17},{2,18},{3,19},{4,20},{5,21},{6,22},{7,23},{8,24},{9,... | collective-permute-start | bytes 7077896 | tf_op jit(solution)/shard_map/ppermute | solution.py:1081
  1032.7 59.9 %collective-permute-start.64 = (bf16[4,512,512]{2,1,0:T(8,128)(2,1)}, bf16[4,512,512]{2,1,0:T(8,128)(2,1)}, u32[]{:S(2)}, u32[]{:S(2)}) collective-permute-start(bf16[4,512,512]{2,1,0:T(8,128)(2,1)} %all-to-all-done.24.refs_0_), channel_id=1, source_target_pairs={{16,0},{17,1},{18,2},{19,3},{20,4},{21,5},{22,6},{23,7},{24,8},{25... | collective-permute-start | bytes 6291464 | tf_op jit(solution)/shard_map/ppermute | solution.py:1081
  1049.2 26.3 %collective-permute-start.62 = (f32[2,28099]{1,0:T(2,128)S(1)}, f32[2,28099]{1,0:T(2,128)S(1)}, u32[]{:S(2)}, u32[]{:S(2)}) collective-permute-start(f32[2,28099]{1,0:T(2,128)S(1)} %add.375), channel_id=1, source_target_pairs={{0,4},{4,0},{8,12},{12,8},{1,5},{5,1},{9,13},{13,9},{2,6},{6,2},{1... | collective-permute-start | bytes 674384 | tf_op jit(solution)/shard_map/ppermute | solution.py:626
  1092.6 29.7 %all-to-all-start.25 = ((bf16[4,256,512]{2,1,0:T(8,128)(2,1)}), bf16[4,256,512]{2,1,0:T(8,128)(2,1)}, u32[]{:S(2)}, u32[]{:S(2)}) async-start(bf16[4,256,512]{2,1,0:T(8,128)(2,1)} %all-to-all-done.22), calls=%async_computation.25 | async-start | bytes 2097152 | tf_op jit(solution)/shard_map/all_to_all | solution.py:607
  1096.9 47.5 %collective-permute-start.68 = (bf16[4,576,512]{2,1,0:T(8,128)(2,1)S(1)}, bf16[4,576,512]{2,1,0:T(8,128)(2,1)}, u32[]{:S(2)}, u32[]{:S(2)}) collective-permute-start(bf16[4,576,512]{2,1,0:T(8,128)(2,1)S(1)} %bitcast.269), channel_id=1, source_target_pairs={{16,0},{17,1},{18,2},{19,3},{20,4},{21,5},{22,6},{23,7},{24,8},{25... | collective-permute-start | bytes 7077896 | tf_op jit(solution)/shard_map/ppermute | solution.py:1081
  1140.8 22.2 %collective-permute-start.67 = (bf16[2,128,2048]{2,1,0:T(8,128)(2,1)S(1)}, bf16[2,128,2048]{2,1,0:T(8,128)(2,1)S(1)}, u32[]{:S(2)}, u32[]{:S(2)}) collective-permute-start(bf16[2,128,2048]{2,1,0:T(8,128)(2,1)S(1)} %fusion.5), channel_id=1, source_target_pairs={{0,16},{16,0},{1,17},{17,1},{2,18},{18,2},{3,19},{19,3},{4,20},{20... | collective-permute-start | bytes 3145736 | tf_op jit(solution)/shard_map/ppermute | solution.py:578
  (111 other events, 1638.4 us)

commit v11 on v10

--- a/solution.py
+++ b/solution.py
@@ -1039,18 +1039,21 @@
     away = away_in(normed_in1, *xs1)
     gx = own_in_piece(normed_in1, xs1[0], away, xs1[1])
     back_h = in_group(back_h)
-    dnin1, gx, back_h = sums.end((dnin1, gx, back_h))
-    x1 = sums.add(gx)
-
-    sums.begin()
     grad1, dgin1 = back_norm(dout1, dnin1, h1, small[1][0])
     dout0 = grad1.astype(BF16).astype(F32)
     dmixed0_own = (valid * dout0).astype(BF16)
+    along0 = jnp.sum(dmixed0_own.astype(F32) * mixed0, axis=-1)
+    grad1, dgin1, dout0, dmixed0_own, along0, gx, back_h = sums.end(
+        (grad1, dgin1, dout0, dmixed0_own, along0, gx, back_h)
+    )
+    x1 = sums.add(gx)
+
+    sums.begin()
     dmixed0 = gather_rows(dmixed0_own)
-    along0 = to_all(jnp.sum(dmixed0_own.astype(F32) * mixed0, axis=-1)).reshape(-1)
+    along0 = to_all(along0).reshape(-1)
     rc0 = scales(r0, (r0 * r0 / INNER) * along0)
     back_h = joined(exchange(back_h))
-    grad1, dgin1, dmixed0, rc0, back_h = sums.end((grad1, dgin1, dmixed0, rc0, back_h))
+    dmixed0, rc0, back_h = sums.end((dmixed0, rc0, back_h))
 
     sums.begin()
     dn0 = dot_cols(dmixed0, wo[0])
@@ -1085,8 +1088,9 @@
     own_o1 = sums.values[o1]
     away_o1 = hand_over(own_o1, 1)
     away_z1 = hand_over(own_z1, 1)
-    dnin0, own_z1, away_z1, own_o1, away_o1 = sums.end(
-        (dnin0, own_z1, away_z1, own_o1, away_o1)
+    grad0, dgin0 = back_norm(dout0, dnin0, h0, small[0][0])
+    grad0, dgin0, own_z1, away_z1, own_o1, away_o1 = sums.end(
+        (grad0, dgin0, own_z1, away_z1, own_o1, away_o1)
     )
 
     sums.finish([x1, o0])
@@ -1094,7 +1098,6 @@
     own_x1 = exchange(sums.values[x1])
     own_o0 = sums.values[o0]
     away_o0 = hand_over(own_o0, 0)
-    grad0, dgin0 = back_norm(dout0, dnin0, h0, small[0][0])
     back_g = exchange(quarters(jnp.concatenate([grad0.astype(BF16), grad1.astype(BF16)])))
     p = jnp.stack([packed(dgin0, d0, out0, mixed0), p1])
     p = p + swap_section(p)
@@ -1108,10 +1111,6 @@
     while m < n:
         p = p + move_fsdp(p, m)
         m *= 2
-    m = 1
-    while m < nz:
-        p = p + move_seq(p, m)
-        m *= 2
     away_z0 = hand_over(own_z0, 0)
     p, back_g, own_z0, away_z0, own_x1, away_x1 = sums.end(
         (p, back_g, own_z0, away_z0, own_x1, away_x1)
@@ -1119,9 +1118,12 @@
     sums.finish([x0])
     own_x0 = sums.values[x0]
     away_x0 = hand_over(own_x0, 0)
-    back_g = joined(exchange(in_group(back_g)))
+    back_g = in_group(back_g)
+    m = 1
+    while m < nz:
+        p = p + move_seq(p, m)
+        m *= 2
     p = pick(p[0], p[1])
-    back = jnp.concatenate([back_h, back_g])
 
     used = 0
 
@@ -1158,6 +1160,9 @@
     g_w_in = []
     shape_in = (2 * INNER + GROUP + HEADS, share)
     for k, rows_of_small in ((0, None), (1, (2 * INNER, GROUP + HEADS))):
+        if g_w_in:
+            back_g, g_w_in = tie((back_g, g_w_in))
+            back_g = exchange(back_g)
         arrays, plan = [], []
         for s in range(2):
             arrays += [held[s][0][k], held[s][1][k]]
@@ -1168,6 +1173,8 @@
                 ids, arrays, tuple(plan), small_in, rows_of_small, g_w_in, shape_in, part_width
             )
         ]
+    g_w_in, back_g = tie((g_w_in, back_g))
+    back = jnp.concatenate([back_h, joined(back_g)])
     halves_out = [pick(side[0][2], side[1][2]) for side in held]
     g_w_out = jnp.concatenate([pick(*halves_out), pick(*halves_out[::-1])]).astype(F32)
 

time: 1180 us -> 1170 us (level)
    ppermute x18, waiting for transfers between devices: 137 us -> 171 us  [begin(): lax.ppermute(self.values[k], 'seq', self.pairs[step])]
    all_to_all x4, waiting for transfers between devices: 25.2 us -> 4.2 us  [in_group(): return lax.all_to_all(v, 'seq', 0, 0, axis_index_groups=groups, tiled=True)]
    all_to_all x22, waiting for transfers between devices: 128 us -> 113 us  [exchange(): return lax.all_to_all(v, 'fsdp', 0, 0, tiled=True)]
    unnamed x167 -> x175, local copies, waits for them, and re-layouts: 30.7 us -> 30.1 us
  transfers between devices with their start and end apart: 95 -> 95, of which waited for: 36 -> 34; matrix products, arithmetic and copies ran while one was open for 15% -> 15% of each run, Pallas kernels for 15% -> 15%
where the time goes in v11:
time: 1170 us; the launch traced here: 1160 us
  waiting for transfers between devices  352 us (30%)
  starting transfers between devices  315 us (27%)
  Pallas kernels  195 us (17%)
  local copies, waits for them, and re-layouts  86.8 us (7%)
  matrix products  81.6 us (7%)
  other arithmetic  73.8 us (6%)
  blocking collectives  48.5 us (4%)
    ppermute x18, waiting for transfers between devices, begin(): lax.ppermute(self.values[k], 'seq', self.pairs[step])  171 us
    all_to_all x22, waiting for transfers between devices, exchange(): return lax.all_to_all(v, 'fsdp', 0, 0, tiled=True)  113 us
    all_to_all x22, starting transfers between devices, exchange(): return lax.all_to_all(v, 'fsdp', 0, 0, tiled=True)  101 us
    ppermute x18, starting transfers between devices, begin(): lax.ppermute(self.values[k], 'seq', self.pairs[step])  67.3 us
    pallas_call x10, Pallas kernels, combine(): pl.pallas_call(functools.partial(combine_kernel, adds=tuple((add for _, _...  63.7 us
    dot_general x16, matrix products, dot_rows(): lax.dot_general(a, b, (((0,), (0,)), ((), ())), preferred_element_type=F32)  57.6 us
    all_to_all x1, blocking collectives, exchange(): return lax.all_to_all(v, 'fsdp', 0, 0, tiled=True)  48.5 us
    ppermute x12, starting transfers between devices, swap_section(): return lax.ppermute(v, 'section', [(0, 1), (1, 0)])  44.8 us
  transfers between devices with their start and end apart: 95, of which 34 were waited for; matrix products, arithmetic and copies ran while one was open for 15% of the time, Pallas kernels for 15%

profile of v11, /device:TPU:1, one launch (start us, length us, event | category | flops | bytes accessed | tf_op | source)
XLA Modules:
  0.0 1157.0 jit_solution(11535670872546740020)
XLA Ops:
  15.6 5.7 dynamic-slice_bitcast_fusion
  29.4 4.7 all-to-all-start.1
  34.2 5.2 collective-permute-start.3
  55.8 17.2 %all-to-all-done.2 = bf16[4,512,512]{2,1,0:T(8,128)(2,1)} async-done(((bf16[4,512,512]{2,1,0:T(8,128)(2,1)}), bf16[4,512,512]{2,1,0:T(8,128)(2,1)}, u32[]{:S(2)}, u32[]{:S(2)}) %all-to-all-start.2) | async-done | bytes 2097184 | tf_op jit(solution)/shard_map/all_to_all | solution.py:586
  82.1 8.8 project.4.proj
  90.9 26.5 %collective-permute-start.12 = (bf16[1024,2048]{1,0:T(8,128)(2,1)}, bf16[1024,2048]{1,0:T(8,128)(2,1)}, u32[]{:S(2)}, u32[]{:S(2)}) collective-permute-start(bf16[1024,2048]{1,0:T(8,128)(2,1)} %bitcast.36), channel_id=1, source_target_pairs={{0,16},{16,0},{1,17},{17,1},{2,18},{18,2},{3,19},{19,3},{4,20},{20... | collective-permute-start | bytes 12582920 | tf_op jit(solution)/shard_map/ppermute | solution.py:578
  121.5 10.6 scan_forward.2
  132.2 7.3 broadcast_select_fusion
  147.9 6.1 collective-permute-done.13.refs_4_.refs_8_
  161.3 6.8 project.5.pz
  175.7 11.4 all-to-all-done.3
  194.1 6.9 fusion.112
  201.0 48.5 %all_to_all.136 = f32[4,128,2048]{2,1,0:T(8,128)} all-to-all(f32[4,128,2048]{2,1,0:T(8,128)} %bitcast.291), channel_id=1, replica_groups=mesh['section'=2,'seq'=4,'fsdp'=4] {'fsdp'}, dimensions={0} | all-to-all | bytes 8388608 | tf_op jit(solution)/shard_map/all_to_all | solution.py:586
  270.5 11.1 all-to-all-start.7
  296.4 6.9 all-to-all-done.7
  303.3 7.9 project.6.proj
  314.3 13.1 %collective-permute-done.26.refs_3_ = bf16[1024,512]{1,0:T(8,128)(2,1)} collective-permute-done((bf16[1024,512]{1,0:T(8,128)(2,1)}, bf16[1024,512]{1,0:T(8,128)(2,1)}, u32[]{:S(2)}, u32[]{:S(2)}) %collective-permute-start.26) | collective-permute-done | bytes 1048608 | tf_op jit(solution)/shard_map/ppermute | solution.py:767
  340.2 10.6 scan_forward.3
  356.0 6.6 project.7.pz
  366.4 6.9 multiply_reduce_fusion.2
  390.7 4.9 add_convert_fusion.5.refs_0_
  395.6 4.7 collective-permute-start.32
  408.5 20.4 %scan_backward.2 = (bf16[512,1024]{1,0:T(8,128)(2,1)S(1)}, bf16[512,1296]{1,0:T(8,128)(2,1)S(1)}, f32[4,512,64]{2,1,0:T(8,128)S(1)}, f32[8,1024]{1,0:T(8,128)S(1...) custom-call(f32[512,1024]{1,0:T(8,128)} %project.7.pz, ...), custom_call_target="tpu_custom_call" | custom-call | tf_op jit(solution)/shard_map/scan_backward/pallas_call | solution.py:303
  436.1 8.1 collective-permute-done.32.refs_1_
  444.2 6.2 combine.10.refs_0_
  480.8 11.0 project_back.2
  491.8 4.8 combine.11.refs_0_
  498.0 4.8 add_convert_fusion.4
  502.8 5.0 all-to-all-start.13
  509.2 17.1 %collective-permute-start.38 = (bf16[4,512,512]{2,1,0:T(8,128)(2,1)}, bf16[4,512,512]{2,1,0:T(8,128)(2,1)}, u32[]{:S(2)}, u32[]{:S(2)}) collective-permute-start(bf16[4,512,512]{2,1,0:T(8,128)(2,1)} %bitcast.309), channel_id=1, source_target_pairs={{0,4},{12,8},{1,5},{13,9},{2,6},{14,10},{3,7},{15,11},{16,20},{28,... | collective-permute-start | bytes 6291464 | tf_op jit(solution)/shard_map/ppermute | solution.py:650
  535.9 18.8 %all-to-all-done.13 = f32[4,128,2048]{2,1,0:T(8,128)} async-done(((f32[4,128,2048]{2,1,0:T(8,128)}), f32[4,128,2048]{2,1,0:T(8,128)}, u32[]{:S(2)}, u32[]{:S(2)}) %all-to-all-start.13) | async-done | bytes 4194336 | tf_op jit(solution)/shard_map/all_to_all | solution.py:586
  554.7 14.6 %all-to-all-start.14 = ((bf16[4,256,512]{2,1,0:T(8,128)(2,1)}), bf16[4,256,512]{2,1,0:T(8,128)(2,1)}, u32[]{:S(2)}, u32[]{:S(2)}) async-start(bf16[4,256,512]{2,1,0:T(8,128)(2,1)} %all-to-all-done.12), calls=%async_computation.14 | async-start | bytes 2097152 | tf_op jit(solution)/shard_map/all_to_all | solution.py:607
  571.5 5.8 combine.12
  577.3 5.0 add_convert_fusion.3
  609.5 11.2 all-to-all-done.17
  629.3 20.6 %collective-permute-done.40 = bf16[4,576,512]{2,1,0:T(8,128)(2,1)} collective-permute-done((bf16[4,576,512]{2,1,0:T(8,128)(2,1)}, bf16[4,576,512]{2,1,0:T(8,128)(2,1)}, u32[]{:S(2)}, u32[]{:S(2)}) %collective-permute-start.40) | collective-permute-done | bytes 2359328 | tf_op jit(solution)/shard_map/ppermute | solution.py:650
  649.9 7.3 combine.13
  673.0 6.5 fusion.113.dn
  679.5 20.4 %scan_backward.3 = (bf16[512,1024]{1,0:T(8,128)(2,1)S(1)}, bf16[512,1296]{1,0:T(8,128)(2,1)S(1)}, f32[4,512,64]{2,1,0:T(8,128)S(1)}, f32[8,1024]{1,0:T(8,128)S(1...) custom-call(f32[512,1024]{1,0:T(8,128)} %project.5.pz, ...), custom_call_target="tpu_custom_call" | custom-call | tf_op jit(solution)/shard_map/scan_backward/pallas_call | solution.py:303
  700.0 5.6 add_convert_fusion.2.refs_2_
  705.6 14.4 %collective-permute-done.42 = bf16[4,512,512]{2,1,0:T(8,128)(2,1)} collective-permute-done((bf16[4,512,512]{2,1,0:T(8,128)(2,1)}, bf16[4,512,512]{2,1,0:T(8,128)(2,1)}, u32[]{:S(2)}, u32[]{:S(2)}) %collective-permute-start.42) | collective-permute-done | bytes 2097184 | tf_op jit(solution)/shard_map/ppermute | solution.py:650
  720.0 7.2 combine.14
  742.9 9.3 collective-permute-start.48
  752.5 4.7 all-to-all-start.19
  773.1 22.3 %collective-permute-done.48.refs_3_ = bf16[512,2048]{1,0:T(8,128)(2,1)} collective-permute-done((bf16[512,2048]{1,0:T(8,128)(2,1)}, bf16[512,2048]{1,0:T(8,128)(2,1)}, u32[]{:S(2)}, u32[]{:S(2)}) %collective-permute-start.48) | collective-permute-done | bytes 2097184 | tf_op jit(solution)/shard_map/ppermute | solution.py:650
  795.4 6.6 combine.15
  805.4 6.6 collective-permute-start.50
  819.0 10.7 project_back.3
  829.7 24.2 %collective-permute-done.50 = bf16[4,512,512]{2,1,0:T(8,128)(2,1)} collective-permute-done((bf16[4,512,512]{2,1,0:T(8,128)(2,1)}, bf16[4,512,512]{2,1,0:T(8,128)(2,1)}, u32[]{:S(2)}, u32[]{:S(2)}) %collective-permute-start.50) | collective-permute-done | bytes 2097184 | tf_op jit(solution)/shard_map/ppermute | solution.py:650
  853.9 5.9 combine.16
  867.2 5.6 collective-permute-start.55
  879.4 12.1 %all-to-all-done.21 = bf16[4,128,2048]{2,1,0:T(8,128)(2,1)} async-done(((bf16[4,128,2048]{2,1,0:T(8,128)(2,1)}), bf16[4,128,2048]{2,1,0:T(8,128)(2,1)}, u32[]{:S(2)}, u32[]{:S(2)}) %all-to-all-start.21) | async-done | bytes 2097184 | tf_op jit(solution)/shard_map/all_to_all | solution.py:586
  900.1 18.8 %collective-permute-done.53.refs_1_ = bf16[512,2048]{1,0:T(8,128)(2,1)} collective-permute-done((bf16[512,2048]{1,0:T(8,128)(2,1)}, bf16[512,2048]{1,0:T(8,128)(2,1)}, u32[]{:S(2)}, u32[]{:S(2)}) %collective-permute-start.53) | collective-permute-done | bytes 2097184 | tf_op jit(solution)/shard_map/ppermute | solution.py:650
  919.3 8.6 combine.17
  950.4 41.1 %collective-permute-done.58 = bf16[4,512,512]{2,1,0:T(8,128)(2,1)} collective-permute-done((bf16[4,512,512]{2,1,0:T(8,128)(2,1)}, bf16[4,512,512]{2,1,0:T(8,128)(2,1)}, u32[]{:S(2)}, u32[]{:S(2)}) %collective-permute-start.58) | collective-permute-done | bytes 2097184 | tf_op jit(solution)/shard_map/ppermute | solution.py:650
  991.6 7.2 combine.18
  1007.3 22.1 %all-to-all-done.24.refs_0_ = bf16[4,512,512]{2,1,0:T(8,128)(2,1)} async-done(((bf16[4,512,512]{2,1,0:T(8,128)(2,1)}), bf16[4,512,512]{2,1,0:T(8,128)(2,1)}, u32[]{:S(2)}, u32[]{:S(2)}) %all-to-all-start.24) | async-done | bytes 2097184 | tf_op jit(solution)/shard_map/all_to_all | solution.py:586
  1032.2 6.2 collective-permute-done.60
  1039.8 6.1 collective-permute-done.61
  1046.0 21.4 %collective-permute-done.64 = bf16[4,576,512]{2,1,0:T(8,128)(2,1)} collective-permute-done((bf16[4,576,512]{2,1,0:T(8,128)(2,1)S(1)}, bf16[4,576,512]{2,1,0:T(8,128)(2,1)}, u32[]{:S(2)}, u32[]{:S(2)}) %collective-permute-start.64) | collective-permute-done | bytes 2359328 | tf_op jit(solution)/shard_map/ppermute | solution.py:650
  1086.3 16.4 %collective-permute-done.67 = f32[2,28099]{1,0:T(2,128)S(1)} collective-permute-done((f32[2,28099]{1,0:T(2,128)S(1)}, f32[2,28099]{1,0:T(2,128)S(1)}, u32[]{:S(2)}, u32[]{:S(2)}) %collective-permute-start.67) | collective-permute-done | bytes 224824 | tf_op jit(solution)/shard_map/ppermute | solution.py:626
  1111.5 5.4 collective-permute-done.68
  1118.4 8.4 place_in.2.refs_5_
  1132.1 8.8 place_in.3
  (552 shorter events, 421.5 us)
Async XLA Ops:
  23.4 20.1 %collective-permute-start = (bf16[1296,512]{1,0:T(8,128)(2,1)}, bf16[1296,512]{1,0:T(8,128)(2,1)}, u32[]{:S(2)}, u32[]{:S(2)}) collective-permute-start(bf16[1296,512]{1,0:T(8,128)(2,1)} %get-tuple-element.242), channel_id=1, source_target_pairs={{0,1},{1,0},{2,3},{3,2},{4,5},{5,4},{6,7},{7,6},{8,9},{9,8},{10,11... | collective-permute-start | bytes 3981320 | tf_op jit(solution)/shard_map/ppermute | solution.py:767
  34.2 21.5 %collective-permute-start.3 = (bf16[4,7024]{1,0:T(4,128)(2,1)S(1)}, bf16[4,7024]{1,0:T(4,128)(2,1)S(1)}, u32[]{:S(2)}, u32[]{:S(2)}) collective-permute-start(bf16[4,7024]{1,0:T(4,128)(2,1)S(1)} %slice.277), channel_id=1, source_target_pairs={{0,16},{16,0},{1,17},{17,1},{2,18},{18,2},{3,19},{19,3},{4,20},{20... | collective-permute-start | bytes 168584 | tf_op jit(solution)/shard_map/ppermute | solution.py:578
  43.5 36.1 %collective-permute-start.4 = (bf16[1296,512]{1,0:T(8,128)(2,1)S(1)}, bf16[1296,512]{1,0:T(8,128)(2,1)}, u32[]{:S(2)}, u32[]{:S(2)}) collective-permute-start(bf16[1296,512]{1,0:T(8,128)(2,1)S(1)} %get-tuple-element.254.refs_0_.refs_4_), channel_id=1, source_target_pairs={{0,16},{1,17},{2,18},{3,19},{4,20},{5,21},{6,22},{7,23},{8,24},{9,... | collective-permute-start | bytes 3981320 | tf_op jit(solution)/shard_map/ppermute | solution.py:796
  44.8 34.8 %collective-permute-start.5 = (bf16[1296,512]{1,0:T(8,128)(2,1)}, bf16[1296,512]{1,0:T(8,128)(2,1)}, u32[]{:S(2)}, u32[]{:S(2)}) collective-permute-start(bf16[1296,512]{1,0:T(8,128)(2,1)} %collective-permute-done.refs_1_.refs_5_), channel_id=1, source_target_pairs={{0,16},{1,17},{2,18},{3,19},{4,20},{5,21},{6,22},{7,23},{8,24},{9,... | collective-permute-start | bytes 3981320 | tf_op jit(solution)/shard_map/ppermute | solution.py:796
  46.1 33.7 %collective-permute-start.6 = (bf16[1296,512]{1,0:T(8,128)(2,1)}, bf16[1296,512]{1,0:T(8,128)(2,1)}, u32[]{:S(2)}, u32[]{:S(2)}) collective-permute-start(bf16[1296,512]{1,0:T(8,128)(2,1)} %collective-permute-done.1.refs_2_.refs_6_), channel_id=1, source_target_pairs={{0,16},{1,17},{2,18},{3,19},{4,20},{5,21},{6,22},{7,23},{8,24},{9,... | collective-permute-start | bytes 3981320 | tf_op jit(solution)/shard_map/ppermute | solution.py:796
  47.4 34.8 %collective-permute-start.7 = (bf16[1296,512]{1,0:T(8,128)(2,1)}, bf16[1296,512]{1,0:T(8,128)(2,1)}, u32[]{:S(2)}, u32[]{:S(2)}) collective-permute-start(bf16[1296,512]{1,0:T(8,128)(2,1)} %collective-permute-done.2.refs_3_.refs_7_), channel_id=1, source_target_pairs={{0,16},{1,17},{2,18},{3,19},{4,20},{5,21},{6,22},{7,23},{8,24},{9,... | collective-permute-start | bytes 3981320 | tf_op jit(solution)/shard_map/ppermute | solution.py:796
  51.2 21.8 %all-to-all-start.2 = ((bf16[4,512,512]{2,1,0:T(8,128)(2,1)}), bf16[4,512,512]{2,1,0:T(8,128)(2,1)}, u32[]{:S(2)}, u32[]{:S(2)}) async-start(bf16[4,512,512]{2,1,0:T(8,128)(2,1)} %broadcast_in_dim.54), calls=%async_computation.2 | async-start | bytes 4194304 | tf_op jit(solution)/shard_map/all_to_all | solution.py:586
  90.9 41.3 %collective-permute-start.12 = (bf16[1024,2048]{1,0:T(8,128)(2,1)}, bf16[1024,2048]{1,0:T(8,128)(2,1)}, u32[]{:S(2)}, u32[]{:S(2)}) collective-permute-start(bf16[1024,2048]{1,0:T(8,128)(2,1)} %bitcast.36), channel_id=1, source_target_pairs={{0,16},{16,0},{1,17},{17,1},{2,18},{18,2},{3,19},{19,3},{4,20},{20... | collective-permute-start | bytes 12582920 | tf_op jit(solution)/shard_map/ppermute | solution.py:578
  119.0 20.5 %collective-permute-start.9 = (bf16[1024,512]{1,0:T(8,128)(2,1)}, bf16[1024,512]{1,0:T(8,128)(2,1)S(1)}, u32[]{:S(2)}, u32[]{:S(2)}) collective-permute-start(bf16[1024,512]{1,0:T(8,128)(2,1)} %get-tuple-element.264), channel_id=1, source_target_pairs={{0,1},{1,0},{2,3},{3,2},{4,5},{5,4},{6,7},{7,6},{8,9},{9,8},{10,11... | collective-permute-start | bytes 3145736 | tf_op jit(solution)/shard_map/ppermute | solution.py:767
  119.7 19.8 %collective-permute-start.10 = (bf16[1024,512]{1,0:T(8,128)(2,1)}, bf16[1024,512]{1,0:T(8,128)(2,1)S(1)}, u32[]{:S(2)}, u32[]{:S(2)}) collective-permute-start(bf16[1024,512]{1,0:T(8,128)(2,1)} %get-tuple-element.265), channel_id=1, source_target_pairs={{0,2},{1,3},{2,0},{3,1},{4,6},{5,7},{6,4},{7,5},{8,10},{9,11},{10,... | collective-permute-start | bytes 3145736 | tf_op jit(solution)/shard_map/ppermute | solution.py:767
  120.5 19.1 %collective-permute-start.11 = (bf16[1024,512]{1,0:T(8,128)(2,1)}, bf16[1024,512]{1,0:T(8,128)(2,1)S(1)}, u32[]{:S(2)}, u32[]{:S(2)}) collective-permute-start(bf16[1024,512]{1,0:T(8,128)(2,1)} %get-tuple-element.266), channel_id=1, source_target_pairs={{0,3},{1,2},{2,1},{3,0},{4,7},{5,6},{6,5},{7,4},{8,11},{9,10},{10,... | collective-permute-start | bytes 3145736 | tf_op jit(solution)/shard_map/ppermute | solution.py:767
  144.8 45.1 %collective-permute-start.17 = (bf16[1296,512]{1,0:T(8,128)(2,1)}, bf16[1296,512]{1,0:T(8,128)(2,1)}, u32[]{:S(2)}, u32[]{:S(2)}) collective-permute-start(bf16[1296,512]{1,0:T(8,128)(2,1)} %get-tuple-element.242), channel_id=1, source_target_pairs={{16,17},{17,16},{18,19},{19,18},{20,21},{21,20},{22,23},{23,22},{2... | collective-permute-start | bytes 3981320 | tf_op jit(solution)/shard_map/ppermute | solution.py:767
  154.0 35.9 %collective-permute-start.18 = (bf16[1296,512]{1,0:T(8,128)(2,1)}, bf16[1296,512]{1,0:T(8,128)(2,1)}, u32[]{:S(2)}, u32[]{:S(2)}) collective-permute-start(bf16[1296,512]{1,0:T(8,128)(2,1)} %get-tuple-element.243), channel_id=1, source_target_pairs={{16,18},{17,19},{18,16},{19,17},{20,22},{21,23},{22,20},{23,21},{2... | collective-permute-start | bytes 3981320 | tf_op jit(solution)/shard_map/ppermute | solution.py:767
  155.9 34.0 %collective-permute-start.19 = (bf16[1296,512]{1,0:T(8,128)(2,1)}, bf16[1296,512]{1,0:T(8,128)(2,1)}, u32[]{:S(2)}, u32[]{:S(2)}) collective-permute-start(bf16[1296,512]{1,0:T(8,128)(2,1)} %get-tuple-element.244), channel_id=1, source_target_pairs={{16,19},{17,18},{18,17},{19,16},{20,23},{21,22},{22,21},{23,20},{2... | collective-permute-start | bytes 3981320 | tf_op jit(solution)/shard_map/ppermute | solution.py:767
  257.3 32.3 %collective-permute-start.20 = (bf16[1296,512]{1,0:T(8,128)(2,1)S(1)}, bf16[1296,512]{1,0:T(8,128)(2,1)}, u32[]{:S(2)}, u32[]{:S(2)}) collective-permute-start(bf16[1296,512]{1,0:T(8,128)(2,1)S(1)} %get-tuple-element.254.refs_0_.refs_4_), channel_id=1, source_target_pairs={{16,0},{17,1},{18,2},{19,3},{20,4},{21,5},{22,6},{23,7},{24,8},{25... | collective-permute-start | bytes 3981320 | tf_op jit(solution)/shard_map/ppermute | solution.py:906
  259.7 33.6 %collective-permute-start.21 = (bf16[1296,512]{1,0:T(8,128)(2,1)}, bf16[1296,512]{1,0:T(8,128)(2,1)}, u32[]{:S(2)}, u32[]{:S(2)}) collective-permute-start(bf16[1296,512]{1,0:T(8,128)(2,1)} %collective-permute-done.17.refs_1_.refs_5_), channel_id=1, source_target_pairs={{16,0},{17,1},{18,2},{19,3},{20,4},{21,5},{22,6},{23,7},{24,8},{25... | collective-permute-start | bytes 3981320 | tf_op jit(solution)/shard_map/ppermute | solution.py:906
  270.5 32.8 %all-to-all-start.7 = ((bf16[4,128,2048]{2,1,0:T(8,128)(2,1)}), bf16[4,128,2048]{2,1,0:T(8,128)(2,1)}, u32[]{:S(2)}, u32[]{:S(2)}) async-start(bf16[4,128,2048]{2,1,0:T(8,128)(2,1)} %broadcast_in_dim.59), calls=%async_computation.7 | async-start | bytes 4194304 | tf_op jit(solution)/shard_map/all_to_all | solution.py:586
  286.2 27.2 %collective-permute-start.24 = (bf16[1024,512]{1,0:T(8,128)(2,1)}, bf16[1024,512]{1,0:T(8,128)(2,1)}, u32[]{:S(2)}, u32[]{:S(2)}) collective-permute-start(bf16[1024,512]{1,0:T(8,128)(2,1)} %get-tuple-element.264), channel_id=1, source_target_pairs={{16,17},{17,16},{18,19},{19,18},{20,21},{21,20},{22,23},{23,22},{2... | collective-permute-start | bytes 3145736 | tf_op jit(solution)/shard_map/ppermute | solution.py:767
  289.6 24.7 %collective-permute-start.25 = (bf16[1024,512]{1,0:T(8,128)(2,1)}, bf16[1024,512]{1,0:T(8,128)(2,1)}, u32[]{:S(2)}, u32[]{:S(2)}) collective-permute-start(bf16[1024,512]{1,0:T(8,128)(2,1)} %get-tuple-element.265), channel_id=1, source_target_pairs={{16,18},{17,19},{18,16},{19,17},{20,22},{21,23},{22,20},{23,21},{2... | collective-permute-start | bytes 3145736 | tf_op jit(solution)/shard_map/ppermute | solution.py:767
  293.3 34.2 %collective-permute-start.26 = (bf16[1024,512]{1,0:T(8,128)(2,1)}, bf16[1024,512]{1,0:T(8,128)(2,1)}, u32[]{:S(2)}, u32[]{:S(2)}) collective-permute-start(bf16[1024,512]{1,0:T(8,128)(2,1)} %get-tuple-element.266), channel_id=1, source_target_pairs={{16,19},{17,18},{18,17},{19,16},{20,23},{21,22},{22,21},{23,20},{2... | collective-permute-start | bytes 3145736 | tf_op jit(solution)/shard_map/ppermute | solution.py:767
  330.2 33.4 %all-to-all-start.8 = ((bf16[4,512,512]{2,1,0:T(8,128)(2,1)}), bf16[4,512,512]{2,1,0:T(8,128)(2,1)}, u32[]{:S(2)}, u32[]{:S(2)}) async-start(bf16[4,512,512]{2,1,0:T(8,128)(2,1)} %broadcast_in_dim.61), calls=%async_computation.8 | async-start | bytes 4194304 | tf_op jit(solution)/shard_map/all_to_all | solution.py:586
  395.6 48.6 %collective-permute-start.32 = (bf16[512,2048]{1,0:T(8,128)(2,1)}, bf16[512,2048]{1,0:T(8,128)(2,1)}, u32[]{:S(2)}, u32[]{:S(2)}) collective-permute-start(bf16[512,2048]{1,0:T(8,128)(2,1)} %add_convert_fusion.5.refs_0_), channel_id=1, source_target_pairs={{0,4},{12,8},{1,5},{13,9},{2,6},{14,10},{3,7},{15,11},{16,20},{28,... | collective-permute-start | bytes 6291464 | tf_op jit(solution)/shard_map/ppermute | solution.py:650
  404.0 29.1 %all-to-all-start.10 = ((bf16[4,128,2048]{2,1,0:T(8,128)(2,1)}), bf16[4,128,2048]{2,1,0:T(8,128)(2,1)}, u32[]{:S(2)}, u32[]{:S(2)}) async-start(bf16[4,128,2048]{2,1,0:T(8,128)(2,1)} %bitcast.303), calls=%async_computation.10 | async-start | bytes 4194304 | tf_op jit(solution)/shard_map/all_to_all | solution.py:586
  450.4 41.5 %collective-permute-start.34 = (bf16[512,2048]{1,0:T(8,128)(2,1)}, bf16[512,2048]{1,0:T(8,128)(2,1)}, u32[]{:S(2)}, u32[]{:S(2)}) collective-permute-start(bf16[512,2048]{1,0:T(8,128)(2,1)} %combine.10.refs_0_), channel_id=1, source_target_pairs={{4,8},{8,4},{5,9},{9,5},{6,10},{10,6},{7,11},{11,7},{20,24},{24,20... | collective-permute-start | bytes 6291464 | tf_op jit(solution)/shard_map/ppermute | solution.py:650
  456.7 41.3 %collective-permute-start.33 = (bf16[2048,512]{1,0:T(8,128)(2,1)}, bf16[2048,512]{1,0:T(8,128)(2,1)}, u32[]{:S(2)}, u32[]{:S(2)}) collective-permute-start(bf16[2048,512]{1,0:T(8,128)(2,1)} %convolution_convert_fusion.5), channel_id=1, source_target_pairs={{0,16},{16,0},{1,17},{17,1},{2,18},{18,2},{3,19},{19,3},{4,20},{20... | collective-permute-start | bytes 6291464 | tf_op jit(solution)/shard_map/ppermute | solution.py:578
  472.4 30.5 %all-to-all-start.12 = ((bf16[4,256,512]{2,1,0:T(8,128)(2,1)}), bf16[4,256,512]{2,1,0:T(8,128)(2,1)}, u32[]{:S(2)}, u32[]{:S(2)}) async-start(bf16[4,256,512]{2,1,0:T(8,128)(2,1)} %bitcast.292), calls=%async_computation.12 | async-start | bytes 2097152 | tf_op jit(solution)/shard_map/all_to_all | solution.py:586
  502.8 51.9 %all-to-all-start.13 = ((f32[4,128,2048]{2,1,0:T(8,128)}), f32[4,128,2048]{2,1,0:T(8,128)}, u32[]{:S(2)}, u32[]{:S(2)}) async-start(f32[4,128,2048]{2,1,0:T(8,128)} %bitcast.283), calls=%async_computation.13 | async-start | bytes 8388608 | tf_op jit(solution)/shard_map/all_to_all | solution.py:586
  507.8 63.6 %collective-permute-start.37 = (bf16[512,2048]{1,0:T(8,128)(2,1)}, bf16[512,2048]{1,0:T(8,128)(2,1)}, u32[]{:S(2)}, u32[]{:S(2)}) collective-permute-start(bf16[512,2048]{1,0:T(8,128)(2,1)} %copy-done.3), channel_id=1, source_target_pairs={{4,0},{8,12},{5,1},{9,13},{6,2},{10,14},{7,3},{11,15},{20,16},{24,... | collective-permute-start | bytes 6291464 | tf_op jit(solution)/shard_map/ppermute | solution.py:650
  509.2 62.2 %collective-permute-start.38 = (bf16[4,512,512]{2,1,0:T(8,128)(2,1)}, bf16[4,512,512]{2,1,0:T(8,128)(2,1)}, u32[]{:S(2)}, u32[]{:S(2)}) collective-permute-start(bf16[4,512,512]{2,1,0:T(8,128)(2,1)} %bitcast.309), channel_id=1, source_target_pairs={{0,4},{12,8},{1,5},{13,9},{2,6},{14,10},{3,7},{15,11},{16,20},{28,... | collective-permute-start | bytes 6291464 | tf_op jit(solution)/shard_map/ppermute | solution.py:650
  530.6 46.7 %collective-permute-start.35 = (bf16[2048,512]{1,0:T(8,128)(2,1)}, bf16[2048,512]{1,0:T(8,128)(2,1)}, u32[]{:S(2)}, u32[]{:S(2)}) collective-permute-start(bf16[2048,512]{1,0:T(8,128)(2,1)} %convolution_convert_fusion.4), channel_id=1, source_target_pairs={{0,16},{16,0},{1,17},{17,1},{2,18},{18,2},{3,19},{19,3},{4,20},{20... | collective-permute-start | bytes 6291464 | tf_op jit(solution)/shard_map/ppermute | solution.py:578
  535.6 33.7 %collective-permute-start.36 = (bf16[40,2048]{1,0:T(8,128)(2,1)}, bf16[40,2048]{1,0:T(8,128)(2,1)}, u32[]{:S(2)}, u32[]{:S(2)}) collective-permute-start(bf16[40,2048]{1,0:T(8,128)(2,1)} %convolution_convert_fusion.8), channel_id=1, source_target_pairs={{0,16},{16,0},{1,17},{17,1},{2,18},{18,2},{3,19},{19,3},{4,20},{20... | collective-permute-start | bytes 491528 | tf_op jit(solution)/shard_map/ppermute | solution.py:578
  554.7 41.1 %all-to-all-start.14 = ((bf16[4,256,512]{2,1,0:T(8,128)(2,1)}), bf16[4,256,512]{2,1,0:T(8,128)(2,1)}, u32[]{:S(2)}, u32[]{:S(2)}) async-start(bf16[4,256,512]{2,1,0:T(8,128)(2,1)} %all-to-all-done.12), calls=%async_computation.14 | async-start | bytes 2097152 | tf_op jit(solution)/shard_map/all_to_all | solution.py:607
  599.6 50.3 %collective-permute-start.40 = (bf16[4,576,512]{2,1,0:T(8,128)(2,1)}, bf16[4,576,512]{2,1,0:T(8,128)(2,1)}, u32[]{:S(2)}, u32[]{:S(2)}) collective-permute-start(bf16[4,576,512]{2,1,0:T(8,128)(2,1)} %pad_maximum_fusion.4), channel_id=1, source_target_pairs={{0,4},{12,8},{1,5},{13,9},{2,6},{14,10},{3,7},{15,11},{16,20},{28,... | collective-permute-start | bytes 7077896 | tf_op jit(solution)/shard_map/ppermute | solution.py:650
  607.6 21.8 %collective-permute-start.39 = (bf16[4,512,512]{2,1,0:T(8,128)(2,1)}, bf16[4,512,512]{2,1,0:T(8,128)(2,1)}, u32[]{:S(2)}, u32[]{:S(2)}) collective-permute-start(bf16[4,512,512]{2,1,0:T(8,128)(2,1)} %bitcast.274), channel_id=1, source_target_pairs={{4,8},{8,4},{5,9},{9,5},{6,10},{10,6},{7,11},{11,7},{20,24},{24,20... | collective-permute-start | bytes 6291464 | tf_op jit(solution)/shard_map/ppermute | solution.py:650
  622.3 34.9 %all-to-all-start.15 = ((bf16[4,128,2048]{2,1,0:T(8,128)(2,1)}), bf16[4,128,2048]{2,1,0:T(8,128)(2,1)}, u32[]{:S(2)}, u32[]{:S(2)}) async-start(bf16[4,128,2048]{2,1,0:T(8,128)(2,1)} %broadcast_in_dim.65), calls=%async_computation.15 | async-start | bytes 4194304 | tf_op jit(solution)/shard_map/all_to_all | solution.py:586
  661.6 38.4 %collective-permute-start.41 = (bf16[512,2048]{1,0:T(8,128)(2,1)}, bf16[512,2048]{1,0:T(8,128)(2,1)}, u32[]{:S(2)}, u32[]{:S(2)}) collective-permute-start(bf16[512,2048]{1,0:T(8,128)(2,1)} %convolution_convert_fusion.3), channel_id=1, source_target_pairs={{0,16},{16,0},{1,17},{17,1},{2,18},{18,2},{3,19},{19,3},{4,20},{20... | collective-permute-start | bytes 6291464 | tf_op jit(solution)/shard_map/ppermute | solution.py:578
  665.3 54.7 %collective-permute-start.43 = (bf16[4,576,512]{2,1,0:T(8,128)(2,1)}, bf16[4,576,512]{2,1,0:T(8,128)(2,1)}, u32[]{:S(2)}, u32[]{:S(2)}) collective-permute-start(bf16[4,576,512]{2,1,0:T(8,128)(2,1)} %bitcast.75), channel_id=1, source_target_pairs={{4,8},{8,4},{5,9},{9,5},{6,10},{10,6},{7,11},{11,7},{20,24},{24,20... | collective-permute-start | bytes 7077896 | tf_op jit(solution)/shard_map/ppermute | solution.py:650
  667.4 52.6 %collective-permute-start.42 = (bf16[4,512,512]{2,1,0:T(8,128)(2,1)}, bf16[4,512,512]{2,1,0:T(8,128)(2,1)}, u32[]{:S(2)}, u32[]{:S(2)}) collective-permute-start(bf16[4,512,512]{2,1,0:T(8,128)(2,1)} %bitcast.74), channel_id=1, source_target_pairs={{4,0},{8,12},{5,1},{9,13},{6,2},{10,14},{7,3},{11,15},{20,16},{24,... | collective-permute-start | bytes 6291464 | tf_op jit(solution)/shard_map/ppermute | solution.py:650
  732.2 31.9 %collective-permute-start.45 = (bf16[2048,512]{1,0:T(8,128)(2,1)}, bf16[2048,512]{1,0:T(8,128)(2,1)}, u32[]{:S(2)}, u32[]{:S(2)}) collective-permute-start(bf16[2048,512]{1,0:T(8,128)(2,1)} %convolution_convert_fusion.1), channel_id=1, source_target_pairs={{0,16},{16,0},{1,17},{17,1},{2,18},{18,2},{3,19},{19,3},{4,20},{20... | collective-permute-start | bytes 6291464 | tf_op jit(solution)/shard_map/ppermute | solution.py:578
  735.7 33.0 %collective-permute-start.44 = (bf16[2048,512]{1,0:T(8,128)(2,1)}, bf16[2048,512]{1,0:T(8,128)(2,1)}, u32[]{:S(2)}, u32[]{:S(2)}) collective-permute-start(bf16[2048,512]{1,0:T(8,128)(2,1)} %convolution_convert_fusion.2), channel_id=1, source_target_pairs={{0,16},{16,0},{1,17},{17,1},{2,18},{18,2},{3,19},{19,3},{4,20},{20... | collective-permute-start | bytes 6291464 | tf_op jit(solution)/shard_map/ppermute | solution.py:578
  735.7 59.7 %collective-permute-start.47 = (bf16[4,576,512]{2,1,0:T(8,128)(2,1)}, bf16[4,576,512]{2,1,0:T(8,128)(2,1)}, u32[]{:S(2)}, u32[]{:S(2)}) collective-permute-start(bf16[4,576,512]{2,1,0:T(8,128)(2,1)} %bitcast.85), channel_id=1, source_target_pairs={{4,0},{8,12},{5,1},{9,13},{6,2},{10,14},{7,3},{11,15},{20,16},{24,... | collective-permute-start | bytes 7077896 | tf_op jit(solution)/shard_map/ppermute | solution.py:650
  742.9 52.4 %collective-permute-start.48 = (bf16[512,2048]{1,0:T(8,128)(2,1)}, bf16[512,2048]{1,0:T(8,128)(2,1)}, u32[]{:S(2)}, u32[]{:S(2)}) collective-permute-start(bf16[512,2048]{1,0:T(8,128)(2,1)} %add_convert_fusion.2.refs_2_), channel_id=1, source_target_pairs={{0,4},{12,8},{1,5},{13,9},{2,6},{14,10},{3,7},{15,11},{16,20},{28,... | collective-permute-start | bytes 6291464 | tf_op jit(solution)/shard_map/ppermute | solution.py:650
  752.5 50.8 %all-to-all-start.19 = ((bf16[4,512,512]{2,1,0:T(8,128)(2,1)}), bf16[4,512,512]{2,1,0:T(8,128)(2,1)}, u32[]{:S(2)}, u32[]{:S(2)}) async-start(bf16[4,512,512]{2,1,0:T(8,128)(2,1)} %bitcast.275), calls=%async_computation.19 | async-start | bytes 4194304 | tf_op jit(solution)/shard_map/all_to_all | solution.py:586
  803.3 26.4 %collective-permute-start.49 = (bf16[512,2048]{1,0:T(8,128)(2,1)}, bf16[512,2048]{1,0:T(8,128)(2,1)}, u32[]{:S(2)}, u32[]{:S(2)}) collective-permute-start(bf16[512,2048]{1,0:T(8,128)(2,1)} %copy-done.30), channel_id=1, source_target_pairs={{4,8},{8,4},{5,9},{9,5},{6,10},{10,6},{7,11},{11,7},{20,24},{24,20... | collective-permute-start | bytes 6291464 | tf_op jit(solution)/shard_map/ppermute | solution.py:650
  805.4 48.5 %collective-permute-start.50 = (bf16[4,512,512]{2,1,0:T(8,128)(2,1)}, bf16[4,512,512]{2,1,0:T(8,128)(2,1)}, u32[]{:S(2)}, u32[]{:S(2)}) collective-permute-start(bf16[4,512,512]{2,1,0:T(8,128)(2,1)} %bitcast.310), channel_id=1, source_target_pairs={{0,4},{12,8},{1,5},{13,9},{2,6},{14,10},{3,7},{15,11},{16,20},{28,... | collective-permute-start | bytes 6291464 | tf_op jit(solution)/shard_map/ppermute | solution.py:650
  812.0 50.5 %all-to-all-start.20 = ((bf16[4,576,512]{2,1,0:T(8,128)(2,1)}), bf16[4,576,512]{2,1,0:T(8,128)(2,1)}, u32[]{:S(2)}, u32[]{:S(2)}) async-start(bf16[4,576,512]{2,1,0:T(8,128)(2,1)} %pad_maximum_fusion.5), calls=%async_computation.20 | async-start | bytes 4718592 | tf_op jit(solution)/shard_map/all_to_all | solution.py:586
  862.6 29.0 %all-to-all-start.21 = ((bf16[4,128,2048]{2,1,0:T(8,128)(2,1)}), bf16[4,128,2048]{2,1,0:T(8,128)(2,1)}, u32[]{:S(2)}, u32[]{:S(2)}) async-start(bf16[4,128,2048]{2,1,0:T(8,128)(2,1)} %bitcast.290), calls=%async_computation.21 | async-start | bytes 4194304 | tf_op jit(solution)/shard_map/all_to_all | solution.py:586
  867.2 52.1 %collective-permute-start.55 = (bf16[4,576,512]{2,1,0:T(8,128)(2,1)}, bf16[4,576,512]{2,1,0:T(8,128)(2,1)}, u32[]{:S(2)}, u32[]{:S(2)}) collective-permute-start(bf16[4,576,512]{2,1,0:T(8,128)(2,1)} %all-to-all-done.20), channel_id=1, source_target_pairs={{0,4},{12,8},{1,5},{13,9},{2,6},{14,10},{3,7},{15,11},{16,20},{28,... | collective-permute-start | bytes 7077896 | tf_op jit(solution)/shard_map/ppermute | solution.py:650
  872.8 46.2 %collective-permute-start.53 = (bf16[512,2048]{1,0:T(8,128)(2,1)}, bf16[512,2048]{1,0:T(8,128)(2,1)}, u32[]{:S(2)}, u32[]{:S(2)}) collective-permute-start(bf16[512,2048]{1,0:T(8,128)(2,1)} %copy-done.24), channel_id=1, source_target_pairs={{4,0},{8,12},{5,1},{9,13},{6,2},{10,14},{7,3},{11,15},{20,16},{24,... | collective-permute-start | bytes 6291464 | tf_op jit(solution)/shard_map/ppermute | solution.py:650
  874.0 44.9 %collective-permute-start.54 = (bf16[4,512,512]{2,1,0:T(8,128)(2,1)}, bf16[4,512,512]{2,1,0:T(8,128)(2,1)}, u32[]{:S(2)}, u32[]{:S(2)}) collective-permute-start(bf16[4,512,512]{2,1,0:T(8,128)(2,1)} %bitcast.273), channel_id=1, source_target_pairs={{4,8},{8,4},{5,9},{9,5},{6,10},{10,6},{7,11},{11,7},{20,24},{24,20... | collective-permute-start | bytes 6291464 | tf_op jit(solution)/shard_map/ppermute | solution.py:650
  876.0 53.2 %collective-permute-start.52 = (bf16[512,2048]{1,0:T(8,128)(2,1)S(1)}, bf16[512,2048]{1,0:T(8,128)(2,1)}, u32[]{:S(2)}, u32[]{:S(2)}) collective-permute-start(bf16[512,2048]{1,0:T(8,128)(2,1)S(1)} %copy-done.20), channel_id=1, source_target_pairs={{0,16},{1,17},{2,18},{3,19},{4,20},{5,21},{6,22},{7,23},{8,24},{9,... | collective-permute-start | bytes 6291464 | tf_op jit(solution)/shard_map/ppermute | solution.py:1084
  877.3 51.9 %collective-permute-start.51 = (bf16[4,512,512]{2,1,0:T(8,128)(2,1)}, bf16[4,512,512]{2,1,0:T(8,128)(2,1)}, u32[]{:S(2)}, u32[]{:S(2)}) collective-permute-start(bf16[4,512,512]{2,1,0:T(8,128)(2,1)} %all-to-all-done.19.refs_1_), channel_id=1, source_target_pairs={{0,16},{1,17},{2,18},{3,19},{4,20},{5,21},{6,22},{7,23},{8,24},{9,... | collective-permute-start | bytes 6291464 | tf_op jit(solution)/shard_map/ppermute | solution.py:1084
  891.5 53.2 %all-to-all-start.23 = ((bf16[4,576,512]{2,1,0:T(8,128)(2,1)}), bf16[4,576,512]{2,1,0:T(8,128)(2,1)}, u32[]{:S(2)}, u32[]{:S(2)}) async-start(bf16[4,576,512]{2,1,0:T(8,128)(2,1)} %bitcast.301), calls=%async_computation.23 | async-start | bytes 4718592 | tf_op jit(solution)/shard_map/all_to_all | solution.py:586
  937.2 62.9 %collective-permute-start.57 = (bf16[512,2048]{1,0:T(8,128)(2,1)S(1)}, bf16[512,2048]{1,0:T(8,128)(2,1)}, u32[]{:S(2)}, u32[]{:S(2)}) collective-permute-start(bf16[512,2048]{1,0:T(8,128)(2,1)S(1)} %copy-done.22), channel_id=1, source_target_pairs={{16,0},{17,1},{18,2},{19,3},{20,4},{21,5},{22,6},{23,7},{24,8},{25... | collective-permute-start | bytes 6291464 | tf_op jit(solution)/shard_map/ppermute | solution.py:1084
  941.3 50.2 %collective-permute-start.58 = (bf16[4,512,512]{2,1,0:T(8,128)(2,1)}, bf16[4,512,512]{2,1,0:T(8,128)(2,1)}, u32[]{:S(2)}, u32[]{:S(2)}) collective-permute-start(bf16[4,512,512]{2,1,0:T(8,128)(2,1)} %bitcast.100), channel_id=1, source_target_pairs={{4,0},{8,12},{5,1},{9,13},{6,2},{10,14},{7,3},{11,15},{20,16},{24,... | collective-permute-start | bytes 6291464 | tf_op jit(solution)/shard_map/ppermute | solution.py:650
  942.6 49.0 %collective-permute-start.59 = (bf16[4,576,512]{2,1,0:T(8,128)(2,1)}, bf16[4,576,512]{2,1,0:T(8,128)(2,1)}, u32[]{:S(2)}, u32[]{:S(2)}) collective-permute-start(bf16[4,576,512]{2,1,0:T(8,128)(2,1)} %bitcast.101), channel_id=1, source_target_pairs={{4,8},{8,4},{5,9},{9,5},{6,10},{10,6},{7,11},{11,7},{20,24},{24,20... | collective-permute-start | bytes 7077896 | tf_op jit(solution)/shard_map/ppermute | solution.py:650
  944.7 55.3 %all-to-all-start.22 = ((bf16[4,256,512]{2,1,0:T(8,128)(2,1)}), bf16[4,256,512]{2,1,0:T(8,128)(2,1)}, u32[]{:S(2)}, u32[]{:S(2)}) async-start(bf16[4,256,512]{2,1,0:T(8,128)(2,1)} %bitcast.262), calls=%async_computation.22 | async-start | bytes 2097152 | tf_op jit(solution)/shard_map/all_to_all | solution.py:586
  1000.1 29.3 %all-to-all-start.24 = ((bf16[4,512,512]{2,1,0:T(8,128)(2,1)}), bf16[4,512,512]{2,1,0:T(8,128)(2,1)}, u32[]{:S(2)}, u32[]{:S(2)}) async-start(bf16[4,512,512]{2,1,0:T(8,128)(2,1)} %bitcast.276), calls=%async_computation.24 | async-start | bytes 4194304 | tf_op jit(solution)/shard_map/all_to_all | solution.py:586
  1004.7 62.7 %collective-permute-start.64 = (bf16[4,576,512]{2,1,0:T(8,128)(2,1)S(1)}, bf16[4,576,512]{2,1,0:T(8,128)(2,1)}, u32[]{:S(2)}, u32[]{:S(2)}) collective-permute-start(bf16[4,576,512]{2,1,0:T(8,128)(2,1)S(1)} %bitcast.272), channel_id=1, source_target_pairs={{4,0},{8,12},{5,1},{9,13},{6,2},{10,14},{7,3},{11,15},{20,16},{24,... | collective-permute-start | bytes 7077896 | tf_op jit(solution)/shard_map/ppermute | solution.py:650
  1006.0 67.3 %collective-permute-start.63 = (bf16[4,576,512]{2,1,0:T(8,128)(2,1)}, bf16[4,576,512]{2,1,0:T(8,128)(2,1)}, u32[]{:S(2)}, u32[]{:S(2)}) collective-permute-start(bf16[4,576,512]{2,1,0:T(8,128)(2,1)} %all-to-all-done.23.refs_1_), channel_id=1, source_target_pairs={{0,16},{1,17},{2,18},{3,19},{4,20},{5,21},{6,22},{7,23},{8,24},{9,... | collective-permute-start | bytes 7077896 | tf_op jit(solution)/shard_map/ppermute | solution.py:1084
  1029.4 43.9 %collective-permute-start.62 = (bf16[4,512,512]{2,1,0:T(8,128)(2,1)}, bf16[4,512,512]{2,1,0:T(8,128)(2,1)S(1)}, u32[]{:S(2)}, u32[]{:S(2)}) collective-permute-start(bf16[4,512,512]{2,1,0:T(8,128)(2,1)} %all-to-all-done.24.refs_0_), channel_id=1, source_target_pairs={{16,0},{17,1},{18,2},{19,3},{20,4},{21,5},{22,6},{23,7},{24,8},{25... | collective-permute-start | bytes 6291464 | tf_op jit(solution)/shard_map/ppermute | solution.py:1084
  1074.6 42.4 %collective-permute-start.65 = (bf16[4,576,512]{2,1,0:T(8,128)(2,1)S(1)}, bf16[4,576,512]{2,1,0:T(8,128)(2,1)}, u32[]{:S(2)}, u32[]{:S(2)}) collective-permute-start(bf16[4,576,512]{2,1,0:T(8,128)(2,1)S(1)} %bitcast.269), channel_id=1, source_target_pairs={{16,0},{17,1},{18,2},{19,3},{20,4},{21,5},{22,6},{23,7},{24,8},{25... | collective-permute-start | bytes 7077896 | tf_op jit(solution)/shard_map/ppermute | solution.py:1084
  1077.9 48.8 %all-to-all-start.25 = ((bf16[4,256,512]{2,1,0:T(8,128)(2,1)}), bf16[4,256,512]{2,1,0:T(8,128)(2,1)}, u32[]{:S(2)}, u32[]{:S(2)}) async-start(bf16[4,256,512]{2,1,0:T(8,128)(2,1)} %all-to-all-done.22), calls=%async_computation.25 | async-start | bytes 2097152 | tf_op jit(solution)/shard_map/all_to_all | solution.py:607
  1082.2 20.5 %collective-permute-start.67 = (f32[2,28099]{1,0:T(2,128)S(1)}, f32[2,28099]{1,0:T(2,128)S(1)}, u32[]{:S(2)}, u32[]{:S(2)}) collective-permute-start(f32[2,28099]{1,0:T(2,128)S(1)} %add.375), channel_id=1, source_target_pairs={{0,4},{4,0},{8,12},{12,8},{1,5},{5,1},{9,13},{13,9},{2,6},{6,2},{1... | collective-permute-start | bytes 674384 | tf_op jit(solution)/shard_map/ppermute | solution.py:626
  (115 other events, 1729.2 us)

commit v12 on v11

--- a/solution.py
+++ b/solution.py
@@ -1119,26 +1119,7 @@
     own_x0 = sums.values[x0]
     away_x0 = hand_over(own_x0, 0)
     back_g = in_group(back_g)
-    m = 1
-    while m < nz:
-        p = p + move_seq(p, m)
-        m *= 2
-    p = pick(p[0], p[1])
-
-    used = 0
-
-    def part(size):
-        nonlocal used
-        used += size
-        return p[used - size : used]
-
-    mine_of = lambda v, size: lax.dynamic_slice_in_dim(v, f * size, size, v.ndim - 1)
-    o_gain_in = mine_of(part(D), share)
-    o_conv = mine_of(part(5 * CHANNELS).reshape(5, CHANNELS), CHANNELS // n)
-    o_heads = mine_of(part(3 * HEADS).reshape(3, HEADS), heads)
-    o_gain_out = mine_of(part(INNER), width)
-    totals = part(3)
-    act_rms = jnp.sqrt(totals[:2] / (totals[2] * D))[None]
+    p = p + move_seq(p, 1)
 
     held = [
         [(own_z0, own_x0, own_o0), (own_z1, own_x1, own_o1)],
@@ -1161,7 +1142,7 @@
     shape_in = (2 * INNER + GROUP + HEADS, share)
     for k, rows_of_small in ((0, None), (1, (2 * INNER, GROUP + HEADS))):
         if g_w_in:
-            back_g, g_w_in = tie((back_g, g_w_in))
+            back_g, g_w_in, p = tie((back_g, g_w_in, p))
             back_g = exchange(back_g)
         arrays, plan = [], []
         for s in range(2):
@@ -1173,7 +1154,28 @@
                 ids, arrays, tuple(plan), small_in, rows_of_small, g_w_in, shape_in, part_width
             )
         ]
-    g_w_in, back_g = tie((g_w_in, back_g))
+    m = 2
+    while m < nz:
+        p = p + move_seq(p, m)
+        m *= 2
+    p = pick(p[0], p[1])
+    g_w_in, back_g, p = tie((g_w_in, back_g, p))
+
+    used = 0
+
+    def part(size):
+        nonlocal used
+        used += size
+        return p[used - size : used]
+
+    mine_of = lambda v, size: lax.dynamic_slice_in_dim(v, f * size, size, v.ndim - 1)
+    o_gain_in = mine_of(part(D), share)
+    o_conv = mine_of(part(5 * CHANNELS).reshape(5, CHANNELS), CHANNELS // n)
+    o_heads = mine_of(part(3 * HEADS).reshape(3, HEADS), heads)
+    o_gain_out = mine_of(part(INNER), width)
+    totals = part(3)
+    act_rms = jnp.sqrt(totals[:2] / (totals[2] * D))[None]
+
     back = jnp.concatenate([back_h, joined(back_g)])
     halves_out = [pick(side[0][2], side[1][2]) for side in held]
     g_w_out = jnp.concatenate([pick(*halves_out), pick(*halves_out[::-1])]).astype(F32)

time: 1170 us -> 1170 us (level)
    unnamed x175 -> x177, local copies, waits for them, and re-layouts: 30.1 us -> 32 us
  transfers between devices with their start and end apart: 95 -> 95, of which waited for: 34 -> 32; matrix products, arithmetic and copies ran while one was open for 15% -> 15% of each run, Pallas kernels for 15% -> 15%
where the time goes in v12:
time: 1170 us; the launch traced here: 1150 us
  waiting for transfers between devices  345 us (29%)
  starting transfers between devices  315 us (27%)
  Pallas kernels  195 us (17%)
  local copies, waits for them, and re-layouts  87.9 us (8%)
  matrix products  81.8 us (7%)
  other arithmetic  77.9 us (7%)
  blocking collectives  48.5 us (4%)
    ppermute x18, waiting for transfers between devices, begin(): lax.ppermute(self.values[k], 'seq', self.pairs[step])  171 us
    all_to_all x22, waiting for transfers between devices, exchange(): return lax.all_to_all(v, 'fsdp', 0, 0, tiled=True)  108 us
    all_to_all x22, starting transfers between devices, exchange(): return lax.all_to_all(v, 'fsdp', 0, 0, tiled=True)  101 us
    ppermute x18, starting transfers between devices, begin(): lax.ppermute(self.values[k], 'seq', self.pairs[step])  67.2 us
    pallas_call x10, Pallas kernels, combine(): pl.pallas_call(functools.partial(combine_kernel, adds=tuple((add for _, _...  63.8 us
    dot_general x16, matrix products, dot_rows(): lax.dot_general(a, b, (((0,), (0,)), ((), ())), preferred_element_type=F32)  57.7 us
    all_to_all x1, blocking collectives, exchange(): return lax.all_to_all(v, 'fsdp', 0, 0, tiled=True)  48.5 us
    ppermute x12, starting transfers between devices, swap_section(): return lax.ppermute(v, 'section', [(0, 1), (1, 0)])  44 us
  transfers between devices with their start and end apart: 95, of which 32 were waited for; matrix products, arithmetic and copies ran while one was open for 15% of the time, Pallas kernels for 15%

profile of v12, /device:TPU:1, one launch (start us, length us, event | category | flops | bytes accessed | tf_op | source)
XLA Modules:
  0.0 1154.1 jit_solution(2864951621451075210)
XLA Ops:
  15.6 5.7 dynamic-slice_bitcast_fusion
  29.3 4.7 all-to-all-start.1
  34.1 5.2 collective-permute-start.3
  55.7 17.3 %all-to-all-done.2 = bf16[4,512,512]{2,1,0:T(8,128)(2,1)} async-done(((bf16[4,512,512]{2,1,0:T(8,128)(2,1)}), bf16[4,512,512]{2,1,0:T(8,128)(2,1)}, u32[]{:S(2)}, u32[]{:S(2)}) %all-to-all-start.2) | async-done | bytes 2097184 | tf_op jit(solution)/shard_map/all_to_all | solution.py:586
  82.1 8.8 project.4.proj
  90.9 26.5 %collective-permute-start.12 = (bf16[1024,2048]{1,0:T(8,128)(2,1)}, bf16[1024,2048]{1,0:T(8,128)(2,1)}, u32[]{:S(2)}, u32[]{:S(2)}) collective-permute-start(bf16[1024,2048]{1,0:T(8,128)(2,1)} %bitcast.36), channel_id=1, source_target_pairs={{0,16},{16,0},{1,17},{17,1},{2,18},{18,2},{3,19},{19,3},{4,20},{20... | collective-permute-start | bytes 12582920 | tf_op jit(solution)/shard_map/ppermute | solution.py:578
  121.5 10.6 scan_forward.2
  132.1 7.3 broadcast_select_fusion
  147.8 6.1 collective-permute-done.13.refs_4_.refs_8_
  161.3 6.8 project.5.pz
  175.6 11.4 all-to-all-done.3
  194.0 6.9 fusion.112
  201.0 48.5 %all_to_all.136 = f32[4,128,2048]{2,1,0:T(8,128)} all-to-all(f32[4,128,2048]{2,1,0:T(8,128)} %bitcast.295), channel_id=1, replica_groups=mesh['section'=2,'seq'=4,'fsdp'=4] {'fsdp'}, dimensions={0} | all-to-all | bytes 8388608 | tf_op jit(solution)/shard_map/all_to_all | solution.py:586
  270.6 11.1 all-to-all-start.7
  296.6 6.5 all-to-all-done.7
  303.2 7.9 project.6.proj
  314.2 13.1 %collective-permute-done.26.refs_3_ = bf16[1024,512]{1,0:T(8,128)(2,1)} collective-permute-done((bf16[1024,512]{1,0:T(8,128)(2,1)}, bf16[1024,512]{1,0:T(8,128)(2,1)}, u32[]{:S(2)}, u32[]{:S(2)}) %collective-permute-start.26) | collective-permute-done | bytes 1048608 | tf_op jit(solution)/shard_map/ppermute | solution.py:767
  340.1 10.6 scan_forward.3
  355.8 6.6 project.7.pz
  366.3 6.9 multiply_reduce_fusion.2
  390.6 4.9 add_convert_fusion.5.refs_0_
  408.4 20.4 %scan_backward.2 = (bf16[512,1024]{1,0:T(8,128)(2,1)S(1)}, bf16[512,1296]{1,0:T(8,128)(2,1)S(1)}, f32[4,512,64]{2,1,0:T(8,128)S(1)}, f32[8,1024]{1,0:T(8,128)S(1...) custom-call(f32[512,1024]{1,0:T(8,128)} %project.7.pz, ...), custom_call_target="tpu_custom_call" | custom-call | tf_op jit(solution)/shard_map/scan_backward/pallas_call | solution.py:303
  436.0 8.0 collective-permute-done.32.refs_1_
  444.0 6.2 combine.10.refs_0_
  472.2 4.7 all-to-all-start.12
  480.7 11.0 project_back.2
  491.7 4.8 combine.11.refs_0_
  497.9 4.8 add_convert_fusion.4
  502.7 5.0 all-to-all-start.13
  509.1 17.2 %collective-permute-start.38 = (bf16[4,512,512]{2,1,0:T(8,128)(2,1)}, bf16[4,512,512]{2,1,0:T(8,128)(2,1)}, u32[]{:S(2)}, u32[]{:S(2)}) collective-permute-start(bf16[4,512,512]{2,1,0:T(8,128)(2,1)} %bitcast.313), channel_id=1, source_target_pairs={{0,4},{12,8},{1,5},{13,9},{2,6},{14,10},{3,7},{15,11},{16,20},{28,... | collective-permute-start | bytes 6291464 | tf_op jit(solution)/shard_map/ppermute | solution.py:650
  535.9 18.8 %all-to-all-done.13 = f32[4,128,2048]{2,1,0:T(8,128)} async-done(((f32[4,128,2048]{2,1,0:T(8,128)}), f32[4,128,2048]{2,1,0:T(8,128)}, u32[]{:S(2)}, u32[]{:S(2)}) %all-to-all-start.13) | async-done | bytes 4194336 | tf_op jit(solution)/shard_map/all_to_all | solution.py:586
  554.6 14.6 %all-to-all-start.14 = ((bf16[4,256,512]{2,1,0:T(8,128)(2,1)}), bf16[4,256,512]{2,1,0:T(8,128)(2,1)}, u32[]{:S(2)}, u32[]{:S(2)}) async-start(bf16[4,256,512]{2,1,0:T(8,128)(2,1)} %all-to-all-done.12), calls=%async_computation.14 | async-start | bytes 2097152 | tf_op jit(solution)/shard_map/all_to_all | solution.py:607
  571.4 5.8 combine.12
  577.2 5.0 add_convert_fusion.3
  609.5 11.2 all-to-all-done.17
  629.3 20.5 %collective-permute-done.40 = bf16[4,576,512]{2,1,0:T(8,128)(2,1)} collective-permute-done((bf16[4,576,512]{2,1,0:T(8,128)(2,1)}, bf16[4,576,512]{2,1,0:T(8,128)(2,1)}, u32[]{:S(2)}, u32[]{:S(2)}) %collective-permute-start.40) | collective-permute-done | bytes 2359328 | tf_op jit(solution)/shard_map/ppermute | solution.py:650
  649.8 7.4 combine.13
  673.1 6.5 fusion.113.dn
  679.6 20.4 %scan_backward.3 = (bf16[512,1024]{1,0:T(8,128)(2,1)S(1)}, bf16[512,1296]{1,0:T(8,128)(2,1)S(1)}, f32[4,512,64]{2,1,0:T(8,128)S(1)}, f32[8,1024]{1,0:T(8,128)S(1...) custom-call(f32[512,1024]{1,0:T(8,128)} %project.5.pz, ...), custom_call_target="tpu_custom_call" | custom-call | tf_op jit(solution)/shard_map/scan_backward/pallas_call | solution.py:303
  700.1 5.6 add_convert_fusion.2.refs_2_
  705.7 14.4 %collective-permute-done.42 = bf16[4,512,512]{2,1,0:T(8,128)(2,1)} collective-permute-done((bf16[4,512,512]{2,1,0:T(8,128)(2,1)}, bf16[4,512,512]{2,1,0:T(8,128)(2,1)}, u32[]{:S(2)}, u32[]{:S(2)}) %collective-permute-start.42) | collective-permute-done | bytes 2097184 | tf_op jit(solution)/shard_map/ppermute | solution.py:650
  720.1 7.2 combine.14
  743.0 9.3 collective-permute-start.48
  752.6 4.7 all-to-all-start.19
  773.2 22.3 %collective-permute-done.48.refs_3_ = bf16[512,2048]{1,0:T(8,128)(2,1)} collective-permute-done((bf16[512,2048]{1,0:T(8,128)(2,1)}, bf16[512,2048]{1,0:T(8,128)(2,1)}, u32[]{:S(2)}, u32[]{:S(2)}) %collective-permute-start.48) | collective-permute-done | bytes 2097184 | tf_op jit(solution)/shard_map/ppermute | solution.py:650
  795.5 6.6 combine.15
  805.5 6.6 collective-permute-start.50
  819.2 10.7 project_back.3
  829.9 24.2 %collective-permute-done.50 = bf16[4,512,512]{2,1,0:T(8,128)(2,1)} collective-permute-done((bf16[4,512,512]{2,1,0:T(8,128)(2,1)}, bf16[4,512,512]{2,1,0:T(8,128)(2,1)}, u32[]{:S(2)}, u32[]{:S(2)}) %collective-permute-start.50) | collective-permute-done | bytes 2097184 | tf_op jit(solution)/shard_map/ppermute | solution.py:650
  854.0 5.9 combine.16
  867.3 5.6 collective-permute-start.55
  879.6 12.1 %all-to-all-done.21 = bf16[4,128,2048]{2,1,0:T(8,128)(2,1)} async-done(((bf16[4,128,2048]{2,1,0:T(8,128)(2,1)}), bf16[4,128,2048]{2,1,0:T(8,128)(2,1)}, u32[]{:S(2)}, u32[]{:S(2)}) %all-to-all-start.21) | async-done | bytes 2097184 | tf_op jit(solution)/shard_map/all_to_all | solution.py:586
  900.3 18.8 %collective-permute-done.53.refs_1_ = bf16[512,2048]{1,0:T(8,128)(2,1)} collective-permute-done((bf16[512,2048]{1,0:T(8,128)(2,1)}, bf16[512,2048]{1,0:T(8,128)(2,1)}, u32[]{:S(2)}, u32[]{:S(2)}) %collective-permute-start.53) | collective-permute-done | bytes 2097184 | tf_op jit(solution)/shard_map/ppermute | solution.py:650
  919.4 8.6 combine.17
  950.5 41.2 %collective-permute-done.58 = bf16[4,512,512]{2,1,0:T(8,128)(2,1)} collective-permute-done((bf16[4,512,512]{2,1,0:T(8,128)(2,1)}, bf16[4,512,512]{2,1,0:T(8,128)(2,1)}, u32[]{:S(2)}, u32[]{:S(2)}) %collective-permute-start.58) | collective-permute-done | bytes 2097184 | tf_op jit(solution)/shard_map/ppermute | solution.py:650
  991.7 7.2 combine.18
  1007.4 22.1 %all-to-all-done.24.refs_0_ = bf16[4,512,512]{2,1,0:T(8,128)(2,1)} async-done(((bf16[4,512,512]{2,1,0:T(8,128)(2,1)}), bf16[4,512,512]{2,1,0:T(8,128)(2,1)}, u32[]{:S(2)}, u32[]{:S(2)}) %all-to-all-start.24) | async-done | bytes 2097184 | tf_op jit(solution)/shard_map/all_to_all | solution.py:586
  1032.4 6.2 collective-permute-done.60
  1040.0 6.1 collective-permute-done.61
  1046.2 21.4 %collective-permute-done.64 = bf16[4,576,512]{2,1,0:T(8,128)(2,1)} collective-permute-done((bf16[4,576,512]{2,1,0:T(8,128)(2,1)S(1)}, bf16[4,576,512]{2,1,0:T(8,128)(2,1)}, u32[]{:S(2)}, u32[]{:S(2)}) %collective-permute-start.64) | collective-permute-done | bytes 2359328 | tf_op jit(solution)/shard_map/ppermute | solution.py:650
  1083.8 19.1 %collective-permute-done.66 = f32[2,28099]{1,0:T(2,128)S(1)} collective-permute-done((f32[2,28099]{1,0:T(2,128)S(1)}, f32[2,28099]{1,0:T(2,128)S(1)}, u32[]{:S(2)}, u32[]{:S(2)}) %collective-permute-start.66) | collective-permute-done | bytes 224824 | tf_op jit(solution)/shard_map/ppermute | solution.py:626
  1105.1 8.4 place_in.2.refs_5_
  1122.1 4.7 select_bitcast_fusion.1
  1126.8 8.8 place_in.3
  (554 shorter events, 417.0 us)
Async XLA Ops:
  23.3 20.1 %collective-permute-start = (bf16[1296,512]{1,0:T(8,128)(2,1)}, bf16[1296,512]{1,0:T(8,128)(2,1)}, u32[]{:S(2)}, u32[]{:S(2)}) collective-permute-start(bf16[1296,512]{1,0:T(8,128)(2,1)} %get-tuple-element.244), channel_id=1, source_target_pairs={{0,1},{1,0},{2,3},{3,2},{4,5},{5,4},{6,7},{7,6},{8,9},{9,8},{10,11... | collective-permute-start | bytes 3981320 | tf_op jit(solution)/shard_map/ppermute | solution.py:767
  34.1 21.5 %collective-permute-start.3 = (bf16[4,7024]{1,0:T(4,128)(2,1)S(1)}, bf16[4,7024]{1,0:T(4,128)(2,1)S(1)}, u32[]{:S(2)}, u32[]{:S(2)}) collective-permute-start(bf16[4,7024]{1,0:T(4,128)(2,1)S(1)} %slice.271), channel_id=1, source_target_pairs={{0,16},{16,0},{1,17},{17,1},{2,18},{18,2},{3,19},{19,3},{4,20},{20... | collective-permute-start | bytes 168584 | tf_op jit(solution)/shard_map/ppermute | solution.py:578
  43.4 36.1 %collective-permute-start.4 = (bf16[1296,512]{1,0:T(8,128)(2,1)S(1)}, bf16[1296,512]{1,0:T(8,128)(2,1)}, u32[]{:S(2)}, u32[]{:S(2)}) collective-permute-start(bf16[1296,512]{1,0:T(8,128)(2,1)S(1)} %get-tuple-element.256.refs_0_.refs_4_), channel_id=1, source_target_pairs={{0,16},{1,17},{2,18},{3,19},{4,20},{5,21},{6,22},{7,23},{8,24},{9,... | collective-permute-start | bytes 3981320 | tf_op jit(solution)/shard_map/ppermute | solution.py:796
  44.7 34.8 %collective-permute-start.5 = (bf16[1296,512]{1,0:T(8,128)(2,1)}, bf16[1296,512]{1,0:T(8,128)(2,1)}, u32[]{:S(2)}, u32[]{:S(2)}) collective-permute-start(bf16[1296,512]{1,0:T(8,128)(2,1)} %collective-permute-done.refs_1_.refs_5_), channel_id=1, source_target_pairs={{0,16},{1,17},{2,18},{3,19},{4,20},{5,21},{6,22},{7,23},{8,24},{9,... | collective-permute-start | bytes 3981320 | tf_op jit(solution)/shard_map/ppermute | solution.py:796
  46.0 33.7 %collective-permute-start.6 = (bf16[1296,512]{1,0:T(8,128)(2,1)}, bf16[1296,512]{1,0:T(8,128)(2,1)}, u32[]{:S(2)}, u32[]{:S(2)}) collective-permute-start(bf16[1296,512]{1,0:T(8,128)(2,1)} %collective-permute-done.1.refs_2_.refs_6_), channel_id=1, source_target_pairs={{0,16},{1,17},{2,18},{3,19},{4,20},{5,21},{6,22},{7,23},{8,24},{9,... | collective-permute-start | bytes 3981320 | tf_op jit(solution)/shard_map/ppermute | solution.py:796
  47.3 34.8 %collective-permute-start.7 = (bf16[1296,512]{1,0:T(8,128)(2,1)}, bf16[1296,512]{1,0:T(8,128)(2,1)}, u32[]{:S(2)}, u32[]{:S(2)}) collective-permute-start(bf16[1296,512]{1,0:T(8,128)(2,1)} %collective-permute-done.2.refs_3_.refs_7_), channel_id=1, source_target_pairs={{0,16},{1,17},{2,18},{3,19},{4,20},{5,21},{6,22},{7,23},{8,24},{9,... | collective-permute-start | bytes 3981320 | tf_op jit(solution)/shard_map/ppermute | solution.py:796
  51.1 21.8 %all-to-all-start.2 = ((bf16[4,512,512]{2,1,0:T(8,128)(2,1)}), bf16[4,512,512]{2,1,0:T(8,128)(2,1)}, u32[]{:S(2)}, u32[]{:S(2)}) async-start(bf16[4,512,512]{2,1,0:T(8,128)(2,1)} %broadcast_in_dim.60), calls=%async_computation.2 | async-start | bytes 4194304 | tf_op jit(solution)/shard_map/all_to_all | solution.py:586
  90.9 41.3 %collective-permute-start.12 = (bf16[1024,2048]{1,0:T(8,128)(2,1)}, bf16[1024,2048]{1,0:T(8,128)(2,1)}, u32[]{:S(2)}, u32[]{:S(2)}) collective-permute-start(bf16[1024,2048]{1,0:T(8,128)(2,1)} %bitcast.36), channel_id=1, source_target_pairs={{0,16},{16,0},{1,17},{17,1},{2,18},{18,2},{3,19},{19,3},{4,20},{20... | collective-permute-start | bytes 12582920 | tf_op jit(solution)/shard_map/ppermute | solution.py:578
  119.0 20.5 %collective-permute-start.9 = (bf16[1024,512]{1,0:T(8,128)(2,1)}, bf16[1024,512]{1,0:T(8,128)(2,1)S(1)}, u32[]{:S(2)}, u32[]{:S(2)}) collective-permute-start(bf16[1024,512]{1,0:T(8,128)(2,1)} %get-tuple-element.266), channel_id=1, source_target_pairs={{0,1},{1,0},{2,3},{3,2},{4,5},{5,4},{6,7},{7,6},{8,9},{9,8},{10,11... | collective-permute-start | bytes 3145736 | tf_op jit(solution)/shard_map/ppermute | solution.py:767
  119.7 19.8 %collective-permute-start.10 = (bf16[1024,512]{1,0:T(8,128)(2,1)}, bf16[1024,512]{1,0:T(8,128)(2,1)S(1)}, u32[]{:S(2)}, u32[]{:S(2)}) collective-permute-start(bf16[1024,512]{1,0:T(8,128)(2,1)} %get-tuple-element.267), channel_id=1, source_target_pairs={{0,2},{1,3},{2,0},{3,1},{4,6},{5,7},{6,4},{7,5},{8,10},{9,11},{10,... | collective-permute-start | bytes 3145736 | tf_op jit(solution)/shard_map/ppermute | solution.py:767
  144.7 45.1 %collective-permute-start.17 = (bf16[1296,512]{1,0:T(8,128)(2,1)}, bf16[1296,512]{1,0:T(8,128)(2,1)}, u32[]{:S(2)}, u32[]{:S(2)}) collective-permute-start(bf16[1296,512]{1,0:T(8,128)(2,1)} %get-tuple-element.244), channel_id=1, source_target_pairs={{16,17},{17,16},{18,19},{19,18},{20,21},{21,20},{22,23},{23,22},{2... | collective-permute-start | bytes 3981320 | tf_op jit(solution)/shard_map/ppermute | solution.py:767
  153.9 36.0 %collective-permute-start.18 = (bf16[1296,512]{1,0:T(8,128)(2,1)}, bf16[1296,512]{1,0:T(8,128)(2,1)}, u32[]{:S(2)}, u32[]{:S(2)}) collective-permute-start(bf16[1296,512]{1,0:T(8,128)(2,1)} %get-tuple-element.245), channel_id=1, source_target_pairs={{16,18},{17,19},{18,16},{19,17},{20,22},{21,23},{22,20},{23,21},{2... | collective-permute-start | bytes 3981320 | tf_op jit(solution)/shard_map/ppermute | solution.py:767
  155.8 34.0 %collective-permute-start.19 = (bf16[1296,512]{1,0:T(8,128)(2,1)}, bf16[1296,512]{1,0:T(8,128)(2,1)}, u32[]{:S(2)}, u32[]{:S(2)}) collective-permute-start(bf16[1296,512]{1,0:T(8,128)(2,1)} %get-tuple-element.246), channel_id=1, source_target_pairs={{16,19},{17,18},{18,17},{19,16},{20,23},{21,22},{22,21},{23,20},{2... | collective-permute-start | bytes 3981320 | tf_op jit(solution)/shard_map/ppermute | solution.py:767
  257.3 32.4 %collective-permute-start.20 = (bf16[1296,512]{1,0:T(8,128)(2,1)S(1)}, bf16[1296,512]{1,0:T(8,128)(2,1)}, u32[]{:S(2)}, u32[]{:S(2)}) collective-permute-start(bf16[1296,512]{1,0:T(8,128)(2,1)S(1)} %get-tuple-element.256.refs_0_.refs_4_), channel_id=1, source_target_pairs={{16,0},{17,1},{18,2},{19,3},{20,4},{21,5},{22,6},{23,7},{24,8},{25... | collective-permute-start | bytes 3981320 | tf_op jit(solution)/shard_map/ppermute | solution.py:906
  259.7 33.7 %collective-permute-start.21 = (bf16[1296,512]{1,0:T(8,128)(2,1)}, bf16[1296,512]{1,0:T(8,128)(2,1)}, u32[]{:S(2)}, u32[]{:S(2)}) collective-permute-start(bf16[1296,512]{1,0:T(8,128)(2,1)} %collective-permute-done.17.refs_1_.refs_5_), channel_id=1, source_target_pairs={{16,0},{17,1},{18,2},{19,3},{20,4},{21,5},{22,6},{23,7},{24,8},{25... | collective-permute-start | bytes 3981320 | tf_op jit(solution)/shard_map/ppermute | solution.py:906
  270.6 32.6 %all-to-all-start.7 = ((bf16[4,128,2048]{2,1,0:T(8,128)(2,1)}), bf16[4,128,2048]{2,1,0:T(8,128)(2,1)}, u32[]{:S(2)}, u32[]{:S(2)}) async-start(bf16[4,128,2048]{2,1,0:T(8,128)(2,1)} %broadcast_in_dim.65), calls=%async_computation.7 | async-start | bytes 4194304 | tf_op jit(solution)/shard_map/all_to_all | solution.py:586
  286.4 26.9 %collective-permute-start.24 = (bf16[1024,512]{1,0:T(8,128)(2,1)}, bf16[1024,512]{1,0:T(8,128)(2,1)}, u32[]{:S(2)}, u32[]{:S(2)}) collective-permute-start(bf16[1024,512]{1,0:T(8,128)(2,1)} %get-tuple-element.266), channel_id=1, source_target_pairs={{16,17},{17,16},{18,19},{19,18},{20,21},{21,20},{22,23},{23,22},{2... | collective-permute-start | bytes 3145736 | tf_op jit(solution)/shard_map/ppermute | solution.py:767
  289.8 24.4 %collective-permute-start.25 = (bf16[1024,512]{1,0:T(8,128)(2,1)}, bf16[1024,512]{1,0:T(8,128)(2,1)}, u32[]{:S(2)}, u32[]{:S(2)}) collective-permute-start(bf16[1024,512]{1,0:T(8,128)(2,1)} %get-tuple-element.267), channel_id=1, source_target_pairs={{16,18},{17,19},{18,16},{19,17},{20,22},{21,23},{22,20},{23,21},{2... | collective-permute-start | bytes 3145736 | tf_op jit(solution)/shard_map/ppermute | solution.py:767
  293.5 33.8 %collective-permute-start.26 = (bf16[1024,512]{1,0:T(8,128)(2,1)}, bf16[1024,512]{1,0:T(8,128)(2,1)}, u32[]{:S(2)}, u32[]{:S(2)}) collective-permute-start(bf16[1024,512]{1,0:T(8,128)(2,1)} %get-tuple-element.268), channel_id=1, source_target_pairs={{16,19},{17,18},{18,17},{19,16},{20,23},{21,22},{22,21},{23,20},{2... | collective-permute-start | bytes 3145736 | tf_op jit(solution)/shard_map/ppermute | solution.py:767
  330.0 33.4 %all-to-all-start.8 = ((bf16[4,512,512]{2,1,0:T(8,128)(2,1)}), bf16[4,512,512]{2,1,0:T(8,128)(2,1)}, u32[]{:S(2)}, u32[]{:S(2)}) async-start(bf16[4,512,512]{2,1,0:T(8,128)(2,1)} %broadcast_in_dim.126), calls=%async_computation.8 | async-start | bytes 4194304 | tf_op jit(solution)/shard_map/all_to_all | solution.py:586
  395.5 48.5 %collective-permute-start.32 = (bf16[512,2048]{1,0:T(8,128)(2,1)}, bf16[512,2048]{1,0:T(8,128)(2,1)}, u32[]{:S(2)}, u32[]{:S(2)}) collective-permute-start(bf16[512,2048]{1,0:T(8,128)(2,1)} %add_convert_fusion.5.refs_0_), channel_id=1, source_target_pairs={{0,4},{12,8},{1,5},{13,9},{2,6},{14,10},{3,7},{15,11},{16,20},{28,... | collective-permute-start | bytes 6291464 | tf_op jit(solution)/shard_map/ppermute | solution.py:650
  403.9 29.1 %all-to-all-start.10 = ((bf16[4,128,2048]{2,1,0:T(8,128)(2,1)}), bf16[4,128,2048]{2,1,0:T(8,128)(2,1)}, u32[]{:S(2)}, u32[]{:S(2)}) async-start(bf16[4,128,2048]{2,1,0:T(8,128)(2,1)} %bitcast.307), calls=%async_computation.10 | async-start | bytes 4194304 | tf_op jit(solution)/shard_map/all_to_all | solution.py:586
  450.2 41.5 %collective-permute-start.34 = (bf16[512,2048]{1,0:T(8,128)(2,1)}, bf16[512,2048]{1,0:T(8,128)(2,1)}, u32[]{:S(2)}, u32[]{:S(2)}) collective-permute-start(bf16[512,2048]{1,0:T(8,128)(2,1)} %combine.10.refs_0_), channel_id=1, source_target_pairs={{4,8},{8,4},{5,9},{9,5},{6,10},{10,6},{7,11},{11,7},{20,24},{24,20... | collective-permute-start | bytes 6291464 | tf_op jit(solution)/shard_map/ppermute | solution.py:650
  456.5 41.3 %collective-permute-start.33 = (bf16[2048,512]{1,0:T(8,128)(2,1)}, bf16[2048,512]{1,0:T(8,128)(2,1)}, u32[]{:S(2)}, u32[]{:S(2)}) collective-permute-start(bf16[2048,512]{1,0:T(8,128)(2,1)} %convolution_convert_fusion.5), channel_id=1, source_target_pairs={{0,16},{16,0},{1,17},{17,1},{2,18},{18,2},{3,19},{19,3},{4,20},{20... | collective-permute-start | bytes 6291464 | tf_op jit(solution)/shard_map/ppermute | solution.py:578
  472.2 30.5 %all-to-all-start.12 = ((bf16[4,256,512]{2,1,0:T(8,128)(2,1)}), bf16[4,256,512]{2,1,0:T(8,128)(2,1)}, u32[]{:S(2)}, u32[]{:S(2)}) async-start(bf16[4,256,512]{2,1,0:T(8,128)(2,1)} %bitcast.296), calls=%async_computation.12 | async-start | bytes 2097152 | tf_op jit(solution)/shard_map/all_to_all | solution.py:586
  502.7 51.9 %all-to-all-start.13 = ((f32[4,128,2048]{2,1,0:T(8,128)}), f32[4,128,2048]{2,1,0:T(8,128)}, u32[]{:S(2)}, u32[]{:S(2)}) async-start(f32[4,128,2048]{2,1,0:T(8,128)} %bitcast.287), calls=%async_computation.13 | async-start | bytes 8388608 | tf_op jit(solution)/shard_map/all_to_all | solution.py:586
  507.7 63.7 %collective-permute-start.37 = (bf16[512,2048]{1,0:T(8,128)(2,1)}, bf16[512,2048]{1,0:T(8,128)(2,1)}, u32[]{:S(2)}, u32[]{:S(2)}) collective-permute-start(bf16[512,2048]{1,0:T(8,128)(2,1)} %copy-done.3), channel_id=1, source_target_pairs={{4,0},{8,12},{5,1},{9,13},{6,2},{10,14},{7,3},{11,15},{20,16},{24,... | collective-permute-start | bytes 6291464 | tf_op jit(solution)/shard_map/ppermute | solution.py:650
  509.1 62.3 %collective-permute-start.38 = (bf16[4,512,512]{2,1,0:T(8,128)(2,1)}, bf16[4,512,512]{2,1,0:T(8,128)(2,1)}, u32[]{:S(2)}, u32[]{:S(2)}) collective-permute-start(bf16[4,512,512]{2,1,0:T(8,128)(2,1)} %bitcast.313), channel_id=1, source_target_pairs={{0,4},{12,8},{1,5},{13,9},{2,6},{14,10},{3,7},{15,11},{16,20},{28,... | collective-permute-start | bytes 6291464 | tf_op jit(solution)/shard_map/ppermute | solution.py:650
  530.6 46.6 %collective-permute-start.35 = (bf16[2048,512]{1,0:T(8,128)(2,1)}, bf16[2048,512]{1,0:T(8,128)(2,1)}, u32[]{:S(2)}, u32[]{:S(2)}) collective-permute-start(bf16[2048,512]{1,0:T(8,128)(2,1)} %convolution_convert_fusion.4), channel_id=1, source_target_pairs={{0,16},{16,0},{1,17},{17,1},{2,18},{18,2},{3,19},{19,3},{4,20},{20... | collective-permute-start | bytes 6291464 | tf_op jit(solution)/shard_map/ppermute | solution.py:578
  535.6 33.6 %collective-permute-start.36 = (bf16[40,2048]{1,0:T(8,128)(2,1)}, bf16[40,2048]{1,0:T(8,128)(2,1)}, u32[]{:S(2)}, u32[]{:S(2)}) collective-permute-start(bf16[40,2048]{1,0:T(8,128)(2,1)} %convolution_convert_fusion.8), channel_id=1, source_target_pairs={{0,16},{16,0},{1,17},{17,1},{2,18},{18,2},{3,19},{19,3},{4,20},{20... | collective-permute-start | bytes 491528 | tf_op jit(solution)/shard_map/ppermute | solution.py:578
  554.6 41.2 %all-to-all-start.14 = ((bf16[4,256,512]{2,1,0:T(8,128)(2,1)}), bf16[4,256,512]{2,1,0:T(8,128)(2,1)}, u32[]{:S(2)}, u32[]{:S(2)}) async-start(bf16[4,256,512]{2,1,0:T(8,128)(2,1)} %all-to-all-done.12), calls=%async_computation.14 | async-start | bytes 2097152 | tf_op jit(solution)/shard_map/all_to_all | solution.py:607
  599.6 50.2 %collective-permute-start.40 = (bf16[4,576,512]{2,1,0:T(8,128)(2,1)}, bf16[4,576,512]{2,1,0:T(8,128)(2,1)}, u32[]{:S(2)}, u32[]{:S(2)}) collective-permute-start(bf16[4,576,512]{2,1,0:T(8,128)(2,1)} %pad_maximum_fusion.4), channel_id=1, source_target_pairs={{0,4},{12,8},{1,5},{13,9},{2,6},{14,10},{3,7},{15,11},{16,20},{28,... | collective-permute-start | bytes 7077896 | tf_op jit(solution)/shard_map/ppermute | solution.py:650
  607.5 21.8 %collective-permute-start.39 = (bf16[4,512,512]{2,1,0:T(8,128)(2,1)}, bf16[4,512,512]{2,1,0:T(8,128)(2,1)}, u32[]{:S(2)}, u32[]{:S(2)}) collective-permute-start(bf16[4,512,512]{2,1,0:T(8,128)(2,1)} %bitcast.278), channel_id=1, source_target_pairs={{4,8},{8,4},{5,9},{9,5},{6,10},{10,6},{7,11},{11,7},{20,24},{24,20... | collective-permute-start | bytes 6291464 | tf_op jit(solution)/shard_map/ppermute | solution.py:650
  622.3 35.0 %all-to-all-start.15 = ((bf16[4,128,2048]{2,1,0:T(8,128)(2,1)}), bf16[4,128,2048]{2,1,0:T(8,128)(2,1)}, u32[]{:S(2)}, u32[]{:S(2)}) async-start(bf16[4,128,2048]{2,1,0:T(8,128)(2,1)} %broadcast_in_dim.130), calls=%async_computation.15 | async-start | bytes 4194304 | tf_op jit(solution)/shard_map/all_to_all | solution.py:586
  661.7 38.4 %collective-permute-start.41 = (bf16[512,2048]{1,0:T(8,128)(2,1)}, bf16[512,2048]{1,0:T(8,128)(2,1)}, u32[]{:S(2)}, u32[]{:S(2)}) collective-permute-start(bf16[512,2048]{1,0:T(8,128)(2,1)} %convolution_convert_fusion.3), channel_id=1, source_target_pairs={{0,16},{16,0},{1,17},{17,1},{2,18},{18,2},{3,19},{19,3},{4,20},{20... | collective-permute-start | bytes 6291464 | tf_op jit(solution)/shard_map/ppermute | solution.py:578
  665.4 54.7 %collective-permute-start.43 = (bf16[4,576,512]{2,1,0:T(8,128)(2,1)}, bf16[4,576,512]{2,1,0:T(8,128)(2,1)}, u32[]{:S(2)}, u32[]{:S(2)}) collective-permute-start(bf16[4,576,512]{2,1,0:T(8,128)(2,1)} %bitcast.75), channel_id=1, source_target_pairs={{4,8},{8,4},{5,9},{9,5},{6,10},{10,6},{7,11},{11,7},{20,24},{24,20... | collective-permute-start | bytes 7077896 | tf_op jit(solution)/shard_map/ppermute | solution.py:650
  667.5 52.6 %collective-permute-start.42 = (bf16[4,512,512]{2,1,0:T(8,128)(2,1)}, bf16[4,512,512]{2,1,0:T(8,128)(2,1)}, u32[]{:S(2)}, u32[]{:S(2)}) collective-permute-start(bf16[4,512,512]{2,1,0:T(8,128)(2,1)} %bitcast.74), channel_id=1, source_target_pairs={{4,0},{8,12},{5,1},{9,13},{6,2},{10,14},{7,3},{11,15},{20,16},{24,... | collective-permute-start | bytes 6291464 | tf_op jit(solution)/shard_map/ppermute | solution.py:650
  732.4 31.9 %collective-permute-start.45 = (bf16[2048,512]{1,0:T(8,128)(2,1)}, bf16[2048,512]{1,0:T(8,128)(2,1)}, u32[]{:S(2)}, u32[]{:S(2)}) collective-permute-start(bf16[2048,512]{1,0:T(8,128)(2,1)} %convolution_convert_fusion.1), channel_id=1, source_target_pairs={{0,16},{16,0},{1,17},{17,1},{2,18},{18,2},{3,19},{19,3},{4,20},{20... | collective-permute-start | bytes 6291464 | tf_op jit(solution)/shard_map/ppermute | solution.py:578
  735.8 33.0 %collective-permute-start.44 = (bf16[2048,512]{1,0:T(8,128)(2,1)}, bf16[2048,512]{1,0:T(8,128)(2,1)}, u32[]{:S(2)}, u32[]{:S(2)}) collective-permute-start(bf16[2048,512]{1,0:T(8,128)(2,1)} %convolution_convert_fusion.2), channel_id=1, source_target_pairs={{0,16},{16,0},{1,17},{17,1},{2,18},{18,2},{3,19},{19,3},{4,20},{20... | collective-permute-start | bytes 6291464 | tf_op jit(solution)/shard_map/ppermute | solution.py:578
  735.8 59.6 %collective-permute-start.47 = (bf16[4,576,512]{2,1,0:T(8,128)(2,1)}, bf16[4,576,512]{2,1,0:T(8,128)(2,1)}, u32[]{:S(2)}, u32[]{:S(2)}) collective-permute-start(bf16[4,576,512]{2,1,0:T(8,128)(2,1)} %bitcast.85), channel_id=1, source_target_pairs={{4,0},{8,12},{5,1},{9,13},{6,2},{10,14},{7,3},{11,15},{20,16},{24,... | collective-permute-start | bytes 7077896 | tf_op jit(solution)/shard_map/ppermute | solution.py:650
  743.0 52.4 %collective-permute-start.48 = (bf16[512,2048]{1,0:T(8,128)(2,1)}, bf16[512,2048]{1,0:T(8,128)(2,1)}, u32[]{:S(2)}, u32[]{:S(2)}) collective-permute-start(bf16[512,2048]{1,0:T(8,128)(2,1)} %add_convert_fusion.2.refs_2_), channel_id=1, source_target_pairs={{0,4},{12,8},{1,5},{13,9},{2,6},{14,10},{3,7},{15,11},{16,20},{28,... | collective-permute-start | bytes 6291464 | tf_op jit(solution)/shard_map/ppermute | solution.py:650
  752.6 50.8 %all-to-all-start.19 = ((bf16[4,512,512]{2,1,0:T(8,128)(2,1)}), bf16[4,512,512]{2,1,0:T(8,128)(2,1)}, u32[]{:S(2)}, u32[]{:S(2)}) async-start(bf16[4,512,512]{2,1,0:T(8,128)(2,1)} %bitcast.279), calls=%async_computation.19 | async-start | bytes 4194304 | tf_op jit(solution)/shard_map/all_to_all | solution.py:586
  803.4 26.4 %collective-permute-start.49 = (bf16[512,2048]{1,0:T(8,128)(2,1)}, bf16[512,2048]{1,0:T(8,128)(2,1)}, u32[]{:S(2)}, u32[]{:S(2)}) collective-permute-start(bf16[512,2048]{1,0:T(8,128)(2,1)} %copy-done.30), channel_id=1, source_target_pairs={{4,8},{8,4},{5,9},{9,5},{6,10},{10,6},{7,11},{11,7},{20,24},{24,20... | collective-permute-start | bytes 6291464 | tf_op jit(solution)/shard_map/ppermute | solution.py:650
  805.5 48.5 %collective-permute-start.50 = (bf16[4,512,512]{2,1,0:T(8,128)(2,1)}, bf16[4,512,512]{2,1,0:T(8,128)(2,1)}, u32[]{:S(2)}, u32[]{:S(2)}) collective-permute-start(bf16[4,512,512]{2,1,0:T(8,128)(2,1)} %bitcast.314), channel_id=1, source_target_pairs={{0,4},{12,8},{1,5},{13,9},{2,6},{14,10},{3,7},{15,11},{16,20},{28,... | collective-permute-start | bytes 6291464 | tf_op jit(solution)/shard_map/ppermute | solution.py:650
  812.1 50.5 %all-to-all-start.20 = ((bf16[4,576,512]{2,1,0:T(8,128)(2,1)}), bf16[4,576,512]{2,1,0:T(8,128)(2,1)}, u32[]{:S(2)}, u32[]{:S(2)}) async-start(bf16[4,576,512]{2,1,0:T(8,128)(2,1)} %pad_maximum_fusion.5), calls=%async_computation.20 | async-start | bytes 4718592 | tf_op jit(solution)/shard_map/all_to_all | solution.py:586
  862.7 29.0 %all-to-all-start.21 = ((bf16[4,128,2048]{2,1,0:T(8,128)(2,1)}), bf16[4,128,2048]{2,1,0:T(8,128)(2,1)}, u32[]{:S(2)}, u32[]{:S(2)}) async-start(bf16[4,128,2048]{2,1,0:T(8,128)(2,1)} %bitcast.294), calls=%async_computation.21 | async-start | bytes 4194304 | tf_op jit(solution)/shard_map/all_to_all | solution.py:586
  867.3 52.1 %collective-permute-start.55 = (bf16[4,576,512]{2,1,0:T(8,128)(2,1)}, bf16[4,576,512]{2,1,0:T(8,128)(2,1)}, u32[]{:S(2)}, u32[]{:S(2)}) collective-permute-start(bf16[4,576,512]{2,1,0:T(8,128)(2,1)} %all-to-all-done.20), channel_id=1, source_target_pairs={{0,4},{12,8},{1,5},{13,9},{2,6},{14,10},{3,7},{15,11},{16,20},{28,... | collective-permute-start | bytes 7077896 | tf_op jit(solution)/shard_map/ppermute | solution.py:650
  872.9 46.2 %collective-permute-start.53 = (bf16[512,2048]{1,0:T(8,128)(2,1)}, bf16[512,2048]{1,0:T(8,128)(2,1)}, u32[]{:S(2)}, u32[]{:S(2)}) collective-permute-start(bf16[512,2048]{1,0:T(8,128)(2,1)} %copy-done.24), channel_id=1, source_target_pairs={{4,0},{8,12},{5,1},{9,13},{6,2},{10,14},{7,3},{11,15},{20,16},{24,... | collective-permute-start | bytes 6291464 | tf_op jit(solution)/shard_map/ppermute | solution.py:650
  874.2 44.9 %collective-permute-start.54 = (bf16[4,512,512]{2,1,0:T(8,128)(2,1)}, bf16[4,512,512]{2,1,0:T(8,128)(2,1)}, u32[]{:S(2)}, u32[]{:S(2)}) collective-permute-start(bf16[4,512,512]{2,1,0:T(8,128)(2,1)} %bitcast.277), channel_id=1, source_target_pairs={{4,8},{8,4},{5,9},{9,5},{6,10},{10,6},{7,11},{11,7},{20,24},{24,20... | collective-permute-start | bytes 6291464 | tf_op jit(solution)/shard_map/ppermute | solution.py:650
  876.1 53.2 %collective-permute-start.52 = (bf16[512,2048]{1,0:T(8,128)(2,1)S(1)}, bf16[512,2048]{1,0:T(8,128)(2,1)}, u32[]{:S(2)}, u32[]{:S(2)}) collective-permute-start(bf16[512,2048]{1,0:T(8,128)(2,1)S(1)} %copy-done.20), channel_id=1, source_target_pairs={{0,16},{1,17},{2,18},{3,19},{4,20},{5,21},{6,22},{7,23},{8,24},{9,... | collective-permute-start | bytes 6291464 | tf_op jit(solution)/shard_map/ppermute | solution.py:1084
  877.4 51.9 %collective-permute-start.51 = (bf16[4,512,512]{2,1,0:T(8,128)(2,1)}, bf16[4,512,512]{2,1,0:T(8,128)(2,1)}, u32[]{:S(2)}, u32[]{:S(2)}) collective-permute-start(bf16[4,512,512]{2,1,0:T(8,128)(2,1)} %all-to-all-done.19.refs_1_), channel_id=1, source_target_pairs={{0,16},{1,17},{2,18},{3,19},{4,20},{5,21},{6,22},{7,23},{8,24},{9,... | collective-permute-start | bytes 6291464 | tf_op jit(solution)/shard_map/ppermute | solution.py:1084
  891.7 53.2 %all-to-all-start.23 = ((bf16[4,576,512]{2,1,0:T(8,128)(2,1)}), bf16[4,576,512]{2,1,0:T(8,128)(2,1)}, u32[]{:S(2)}, u32[]{:S(2)}) async-start(bf16[4,576,512]{2,1,0:T(8,128)(2,1)} %bitcast.305), calls=%async_computation.23 | async-start | bytes 4718592 | tf_op jit(solution)/shard_map/all_to_all | solution.py:586
  937.3 62.9 %collective-permute-start.57 = (bf16[512,2048]{1,0:T(8,128)(2,1)S(1)}, bf16[512,2048]{1,0:T(8,128)(2,1)}, u32[]{:S(2)}, u32[]{:S(2)}) collective-permute-start(bf16[512,2048]{1,0:T(8,128)(2,1)S(1)} %copy-done.22), channel_id=1, source_target_pairs={{16,0},{17,1},{18,2},{19,3},{20,4},{21,5},{22,6},{23,7},{24,8},{25... | collective-permute-start | bytes 6291464 | tf_op jit(solution)/shard_map/ppermute | solution.py:1084
  941.4 50.3 %collective-permute-start.58 = (bf16[4,512,512]{2,1,0:T(8,128)(2,1)}, bf16[4,512,512]{2,1,0:T(8,128)(2,1)}, u32[]{:S(2)}, u32[]{:S(2)}) collective-permute-start(bf16[4,512,512]{2,1,0:T(8,128)(2,1)} %bitcast.100), channel_id=1, source_target_pairs={{4,0},{8,12},{5,1},{9,13},{6,2},{10,14},{7,3},{11,15},{20,16},{24,... | collective-permute-start | bytes 6291464 | tf_op jit(solution)/shard_map/ppermute | solution.py:650
  942.7 49.0 %collective-permute-start.59 = (bf16[4,576,512]{2,1,0:T(8,128)(2,1)}, bf16[4,576,512]{2,1,0:T(8,128)(2,1)}, u32[]{:S(2)}, u32[]{:S(2)}) collective-permute-start(bf16[4,576,512]{2,1,0:T(8,128)(2,1)} %bitcast.101), channel_id=1, source_target_pairs={{4,8},{8,4},{5,9},{9,5},{6,10},{10,6},{7,11},{11,7},{20,24},{24,20... | collective-permute-start | bytes 7077896 | tf_op jit(solution)/shard_map/ppermute | solution.py:650
  944.8 55.4 %all-to-all-start.22 = ((bf16[4,256,512]{2,1,0:T(8,128)(2,1)}), bf16[4,256,512]{2,1,0:T(8,128)(2,1)}, u32[]{:S(2)}, u32[]{:S(2)}) async-start(bf16[4,256,512]{2,1,0:T(8,128)(2,1)} %bitcast.266), calls=%async_computation.22 | async-start | bytes 2097152 | tf_op jit(solution)/shard_map/all_to_all | solution.py:586
  1000.2 29.3 %all-to-all-start.24 = ((bf16[4,512,512]{2,1,0:T(8,128)(2,1)}), bf16[4,512,512]{2,1,0:T(8,128)(2,1)}, u32[]{:S(2)}, u32[]{:S(2)}) async-start(bf16[4,512,512]{2,1,0:T(8,128)(2,1)} %bitcast.280), calls=%async_computation.24 | async-start | bytes 4194304 | tf_op jit(solution)/shard_map/all_to_all | solution.py:586
  1004.8 62.7 %collective-permute-start.64 = (bf16[4,576,512]{2,1,0:T(8,128)(2,1)S(1)}, bf16[4,576,512]{2,1,0:T(8,128)(2,1)}, u32[]{:S(2)}, u32[]{:S(2)}) collective-permute-start(bf16[4,576,512]{2,1,0:T(8,128)(2,1)S(1)} %bitcast.276), channel_id=1, source_target_pairs={{4,0},{8,12},{5,1},{9,13},{6,2},{10,14},{7,3},{11,15},{20,16},{24,... | collective-permute-start | bytes 7077896 | tf_op jit(solution)/shard_map/ppermute | solution.py:650
  1006.1 67.3 %collective-permute-start.63 = (bf16[4,576,512]{2,1,0:T(8,128)(2,1)}, bf16[4,576,512]{2,1,0:T(8,128)(2,1)}, u32[]{:S(2)}, u32[]{:S(2)}) collective-permute-start(bf16[4,576,512]{2,1,0:T(8,128)(2,1)} %all-to-all-done.23.refs_1_), channel_id=1, source_target_pairs={{0,16},{1,17},{2,18},{3,19},{4,20},{5,21},{6,22},{7,23},{8,24},{9,... | collective-permute-start | bytes 7077896 | tf_op jit(solution)/shard_map/ppermute | solution.py:1084
  1029.5 43.9 %collective-permute-start.62 = (bf16[4,512,512]{2,1,0:T(8,128)(2,1)}, bf16[4,512,512]{2,1,0:T(8,128)(2,1)S(1)}, u32[]{:S(2)}, u32[]{:S(2)}) collective-permute-start(bf16[4,512,512]{2,1,0:T(8,128)(2,1)} %all-to-all-done.24.refs_0_), channel_id=1, source_target_pairs={{16,0},{17,1},{18,2},{19,3},{20,4},{21,5},{22,6},{23,7},{24,8},{25... | collective-permute-start | bytes 6291464 | tf_op jit(solution)/shard_map/ppermute | solution.py:1084
  1074.8 28.9 %collective-permute-start.65 = (bf16[4,576,512]{2,1,0:T(8,128)(2,1)S(1)}, bf16[4,576,512]{2,1,0:T(8,128)(2,1)}, u32[]{:S(2)}, u32[]{:S(2)}) collective-permute-start(bf16[4,576,512]{2,1,0:T(8,128)(2,1)S(1)} %bitcast.273), channel_id=1, source_target_pairs={{16,0},{17,1},{18,2},{19,3},{20,4},{21,5},{22,6},{23,7},{24,8},{25... | collective-permute-start | bytes 7077896 | tf_op jit(solution)/shard_map/ppermute | solution.py:1084
  1078.1 35.3 %all-to-all-start.25 = ((bf16[4,256,512]{2,1,0:T(8,128)(2,1)}), bf16[4,256,512]{2,1,0:T(8,128)(2,1)}, u32[]{:S(2)}, u32[]{:S(2)}) async-start(bf16[4,256,512]{2,1,0:T(8,128)(2,1)} %all-to-all-done.22), calls=%async_computation.25 | async-start | bytes 2097152 | tf_op jit(solution)/shard_map/all_to_all | solution.py:607
  1082.4 20.5 %collective-permute-start.66 = (f32[2,28099]{1,0:T(2,128)S(1)}, f32[2,28099]{1,0:T(2,128)S(1)}, u32[]{:S(2)}, u32[]{:S(2)}) collective-permute-start(f32[2,28099]{1,0:T(2,128)S(1)} %add.375), channel_id=1, source_target_pairs={{0,4},{4,0},{8,12},{12,8},{1,5},{5,1},{9,13},{13,9},{2,6},{6,2},{1... | collective-permute-start | bytes 674384 | tf_op jit(solution)/shard_map/ppermute | solution.py:626
  1113.4 23.7 %all-to-all-start.26 = ((bf16[4,256,512]{2,1,0:T(8,128)(2,1)}), bf16[4,256,512]{2,1,0:T(8,128)(2,1)}, u32[]{:S(2)}, u32[]{:S(2)}) async-start(bf16[4,256,512]{2,1,0:T(8,128)(2,1)} %all-to-all-done.25), calls=%async_computation.26 | async-start | bytes 2097152 | tf_op jit(solution)/shard_map/all_to_all | solution.py:586
  (116 other events, 1738.4 us)
